TPU v7x, 32 devices: a whole 2x2x4 slice. The times are simulated.
32 devices in a mesh: ctx: 16 (over z, y, x), head: 2 (over core).
Axes of the slice: x: 2, y: 2, z: 4, core: 2. Of those that a mesh axis runs over, the one named last changes fastest.
Arguments:
- hidden: bfloat16 [2048, 2048], P(('ctx', 'head')), may hold values from -6 to 6
- w_query: bfloat16 [2048, 2048], P(None, 'head'), may hold values from -0.125 to 0.125
- w_key: bfloat16 [2048, 256], P(None, 'head'), may hold values from -0.125 to 0.125
- w_value: bfloat16 [2048, 256], P(None, 'head'), may hold values from -0.125 to 0.125
- w_dir: bfloat16 [2048, 256], P(None, 'head'), may hold values from -0.125 to 0.125
- u_rate: bfloat16 [2, 2048], P('head'), may hold values from -0.125 to 0.125
- rate_bias: float32 [2], P('head'), may hold values from 5 to 7
- q_gain: float32 [128], replicated, may hold values from 0.8 to 12
- k_gain: float32 [128], replicated, may hold values from 0.8 to 12
- w_out: bfloat16 [2048, 2048], P('head'), may hold values from -0.1875 to 0.1875
- block_mask: int32 [16, 16], P('ctx'), may hold values from 0 to 1, as said below
Outputs:
- layer_out: bfloat16 [2048, 2048], P(('ctx', 'head'))
Inputs may be any that keep to these rules, and one draw needn't show every extreme that they name: block_mask[I, J] is 1 only where J < I; each row holds at most 4 ones, and row 15 holds exactly 4.
All inputs are finite; a program needn't handle non-finite values.
Results may differ from a plain program's by a relative error of at most 0.01045.
Values may be sent and summed in bfloat16 or wider, within the bound.
No kernel may reach another device: no remote copies, remote signals or barrier semaphores. Data moves between devices by JAX's collectives and lax.ppermute only.
A program may use at most 128 MiB of HBM per device.

v0:
```python
import math

import jax
import jax.numpy as jnp
from jax import lax
from jax.sharding import PartitionSpec as P

HD = 128
SEG = 128


HIGHEST = lax.Precision.HIGHEST
EPSILON = 1e-06
NEGATIVE = -1e30


def shifted(value, axis, steps):
    count = lax.axis_size(axis)
    leading, last = (max(0, -steps), min(count, count - steps))
    return lax.ppermute(value, axis, [(source, source + steps) for source in range(leading, last)])


def rms_scaled(values_in, gain):
    return (
        values_in
        * lax.rsqrt(jnp.mean(values_in * values_in, axis=-1, keepdims=True) + EPSILON)
        * gain
    )


def segment_terms(
    seg_rows, query_cols, key_cols, value_cols, dir_cols, rate_vector, rate_offset, q_gain, k_gain
):
    tokens_here = seg_rows.shape[0]
    head_size = key_cols.shape[1]
    groups = query_cols.shape[1] // head_size
    scaling = 1.0 / math.sqrt(head_size)
    queries = jnp.dot(seg_rows, query_cols, preferred_element_type=jnp.float32)
    queries = (
        queries.reshape(tokens_here, groups, head_size)
        .transpose(1, 0, 2)
        .reshape(groups * tokens_here, head_size)
    )
    queries = rms_scaled(queries, q_gain)
    key_rows = rms_scaled(jnp.dot(seg_rows, key_cols, preferred_element_type=jnp.float32), k_gain)
    value_rows = jnp.dot(seg_rows, value_cols, preferred_element_type=jnp.float32).astype(
        jnp.bfloat16
    )
    raw_dirs = jnp.dot(seg_rows, dir_cols, preferred_element_type=jnp.float32)
    directions = raw_dirs * lax.rsqrt(
        jnp.sum(raw_dirs * raw_dirs, axis=-1, keepdims=True) + EPSILON
    )
    rate_values = 2.0 * jax.nn.sigmoid(
        jnp.dot(seg_rows, rate_vector, preferred_element_type=jnp.float32) + rate_offset
    )
    positions = jnp.arange(tokens_here, dtype=jnp.int32)
    strictly_below = positions[:, None] > positions[None, :]
    up_to = jnp.tile(positions[:, None] >= positions[None, :], (groups, 1))
    gram_matrix = jnp.dot(directions, directions.T, precision=HIGHEST)
    lower_unit = jnp.eye(tokens_here, dtype=directions.dtype) + jnp.where(
        strictly_below, rate_values[:, None] * gram_matrix, 0.0
    )
    solved = lax.linalg.triangular_solve(
        lower_unit,
        rate_values[:, None] * directions,
        left_side=True,
        lower=True,
        unit_diagonal=True,
    )
    crossing = jnp.where(strictly_below, jnp.dot(directions, key_rows.T, precision=HIGHEST), 0.0)
    coefficients = lax.linalg.triangular_solve(
        lower_unit, rate_values[:, None] * crossing, left_side=True, lower=True, unit_diagonal=True
    )
    exit_keys = key_rows - jnp.dot(coefficients.T, directions, precision=HIGHEST)
    product = jnp.eye(head_size, dtype=directions.dtype) - jnp.dot(
        directions.T, solved, precision=HIGHEST
    )
    reach_terms = jnp.where(up_to, jnp.dot(queries, directions.T, precision=HIGHEST), 0.0)
    moved_queries = (queries - jnp.dot(reach_terms, solved, precision=HIGHEST)).astype(jnp.bfloat16)
    own_scores = (
        jnp.dot(queries, key_rows.T, precision=HIGHEST)
        - jnp.dot(reach_terms, coefficients, precision=HIGHEST)
    ) * scaling
    own_scores = jnp.where(up_to, own_scores, NEGATIVE)
    return (moved_queries, own_scores, exit_keys, value_rows, product)


def attend_blocks(moved_queries, key_blocks, value_blocks, usable, running):
    block_total, tokens_here, head_size = key_blocks.shape
    scaling = 1.0 / math.sqrt(head_size)
    per_step = math.gcd(block_total, max(1, 1024 // tokens_here))
    steps_total = block_total // per_step
    key_groups = key_blocks.reshape(steps_total, per_step * tokens_here, head_size)
    value_groups = value_blocks.reshape(steps_total, per_step * tokens_here, head_size)
    keep_groups = jnp.repeat(usable, tokens_here).reshape(steps_total, per_step * tokens_here)

    def advance(carried, pieces):
        peak_score, total_weight, weighted = carried
        group_keys, group_values, group_keep = pieces
        scores = (
            lax.dot_general(
                moved_queries,
                group_keys,
                (((1,), (1,)), ((), ())),
                preferred_element_type=jnp.float32,
            )
            * scaling
        )
        scores = jnp.where(group_keep[None, :], scores, NEGATIVE)
        new_peak = jnp.maximum(peak_score, jnp.max(scores, axis=1))
        fading = jnp.exp(peak_score - new_peak)
        expo_weights = jnp.exp(scores - new_peak[:, None])
        total_weight = total_weight * fading + jnp.sum(expo_weights, axis=1)
        weighted = weighted * fading[:, None] + jnp.dot(
            expo_weights.astype(jnp.bfloat16), group_values, preferred_element_type=jnp.float32
        )
        return ((new_peak, total_weight, weighted), None)

    running, _ = lax.scan(advance, running, (key_groups, value_groups, keep_groups))
    return running


def body(
    hidden, w_query, w_key, w_value, w_dir, u_rate, rate_bias, q_gain, k_gain, w_out, block_mask
):
    seg_rows = lax.all_gather(hidden, "head", axis=0, tiled=True)
    moved_queries, own_scores, exit_keys, value_rows, product = segment_terms(
        seg_rows, w_query, w_key, w_value, w_dir, u_rate[0], rate_bias[0], q_gain, k_gain
    )
    segments = lax.axis_size("ctx")
    position = lax.axis_index("ctx")
    mask_row = block_mask[0]
    slots = jnp.arange(segments, dtype=jnp.int32)
    key_buffer = jnp.concatenate([product, exit_keys], axis=0)
    value_buffer = value_rows
    for section_index in range(segments.bit_length()):
        distance = 1 if section_index == 0 else 2 ** (section_index - 1)
        arrived = shifted(key_buffer, "ctx", distance)
        arrived_values = shifted(value_buffer, "ctx", distance)
        if section_index == 0:
            key_buffer = arrived
            value_buffer = arrived_values
        else:
            own_product = key_buffer[:HD]
            older_keys = jnp.dot(arrived[HD:], own_product.T, precision=HIGHEST)
            combined = jnp.dot(own_product, arrived[:HD], precision=HIGHEST)
            key_buffer = jnp.concatenate([combined, older_keys, key_buffer[HD:]], axis=0)
            value_buffer = jnp.concatenate([arrived_values, value_buffer], axis=0)
    key_all = key_buffer[HD:].astype(jnp.bfloat16)
    allowed = (jnp.roll(mask_row, segments - position) > 0) & (slots >= segments - position)
    local_peak = jnp.max(own_scores, axis=1)
    near_exp = jnp.exp(own_scores - local_peak[:, None])
    running = (
        local_peak,
        jnp.sum(near_exp, axis=1),
        jnp.dot(near_exp.astype(jnp.bfloat16), value_rows, preferred_element_type=jnp.float32),
    )
    key_blocks = key_all.reshape(segments, SEG, HD)
    value_blocks = value_buffer.reshape(segments, SEG, HD)
    most_blocks = segments // 4
    ranking = jnp.where(allowed, 0, 1) * segments + slots
    chosen_slots = jnp.argsort(ranking)[:most_blocks]
    key_blocks = key_blocks[chosen_slots]
    value_blocks = value_blocks[chosen_slots]
    allowed = allowed[chosen_slots]
    running = attend_blocks(moved_queries, key_blocks, value_blocks, allowed, running)
    attended = (running[2] / running[1][:, None]).astype(jnp.bfloat16)
    groups = attended.shape[0] // SEG
    attended = attended.reshape(groups, SEG, HD).transpose(1, 0, 2).reshape(SEG, groups * HD)
    return lax.psum_scatter(
        jnp.dot(attended, w_out, preferred_element_type=jnp.float32).astype(jnp.bfloat16),
        "head",
        scatter_dimension=0,
        tiled=True,
    )


def solution(mesh):
    in_specs = (
        P(("ctx", "head"), None),
        P(None, "head"),
        P(None, "head"),
        P(None, "head"),
        P(None, "head"),
        P("head", None),
        P("head"),
        P(),
        P(),
        P("head", None),
        P("ctx", None),
    )
    out_specs = P(("ctx", "head"), None)
    return jax.shard_map(body, mesh=mesh, in_specs=in_specs, out_specs=out_specs, check_vma=False)
```

profile of v0, /device:TPU:0, one launch (start us, length us, event | category | flops | bytes accessed | tf_op | source)
XLA Modules:
  0.0 129.9 jit_solution(8927209365442570039)
XLA Ops:
  6.5 2.6 %all_gather.3 = bf16[128,2048]{1,0:T(8,128)(2,1)S(1)} all-gather(bf16[64,2048]{1,0:T(8,128)(2,1)} %param.13), channel_id=1, replica_groups=mesh['ctx'=16,'head'=2] {'head'}, dimensions={0}, use_global_device_ids=true | all-gather | bytes 786432 | tf_op jit(solution)/shard_map/all_gather | solution.py:126
  9.2 1.3 %convolution_convert_fusion.2 = bf16[128,128]{1,0:T(8,128)(2,1)S(1)} fusion(bf16[128,2048]{1,0:T(8,128)(2,1)S(1)} %all_gather.3, bf16[2048,128]{1,0:T(8,128)(2,1)} %param.16), kind=kOutput, calls=%fused_computation.32 | convolution fusion | flops 67125248 | bytes 1081344 | tf_op jit(solution)/shard_map/dot_general | solution.py:46
  10.5 4.8 %collective-permute-start.5 = (bf16[128,128]{1,0:T(8,128)(2,1)S(1)}, bf16[128,128]{1,0:T(8,128)(2,1)S(1)}, u32[]{:S(2)}, u32[]{:S(2)}) collective-permute-start(bf16[128,128]{1,0:T(8,128)(2,1)S(1)} %convolution_convert_fusion.2), channel_id=1, source_target_pairs={{0,2},{2,4},{4,6},{6,8},{8,10},{10,12},{12,14},{14,16},{16,18},{18... | collective-permute-start | bytes 98312 | tf_op jit(solution)/shard_map/ppermute | solution.py:20
  17.4 9.8 %custom-call.4 = f32[1,128,128]{1,2,0:T(8,128)S(1)} custom-call(f32[1,128,128]{2,1,0:T(8,128)S(1)} %fusion.14), custom_call_target="InvertDiagBlocksLowerTriangular" | custom-call | tf_op jit(solution)/shard_map/triangular_solve/custom-call.1 | solution.py:71
  28.9 3.4 %collective-permute-start = (f32[256,128]{1,0:T(8,128)S(1)}, f32[256,128]{1,0:T(8,128)S(1)}, u32[]{:S(2)}, u32[]{:S(2)}) collective-permute-start(f32[256,128]{1,0:T(8,128)S(1)} %pad_maximum_fusion.3), channel_id=1, source_target_pairs={{0,2},{2,4},{4,6},{6,8},{8,10},{10,12},{12,14},{14,16},{16,18},{18... | collective-permute-start | bytes 393224 | tf_op jit(solution)/shard_map/ppermute | solution.py:20
  32.4 2.9 %convolution_bitcast_fusion = f32[16,8,8,128]{3,2,1,0:T(8,128)S(1)} fusion(bf16[128,2048]{1,0:T(8,128)(2,1)S(1)} %all_gather.3, bf16[2048,1024]{1,0:T(8,128)(2,1)} %param.14), kind=kOutput, calls=%fused_computation.17 | convolution fusion | flops 536870912 | bytes 5242880 | tf_op jit(solution)/shard_map/dot_general | solution.py:38
  37.2 1.0 fusion.8
  38.2 0.7 fusion.73
  39.1 1.2 sort.17
  40.3 3.4 %collective-permute-start.6 = (bf16[128,128]{1,0:T(8,128)(2,1)S(1)}, bf16[128,128]{1,0:T(8,128)(2,1)S(1)}, u32[]{:S(2)}, u32[]{:S(2)}) collective-permute-start(bf16[128,128]{1,0:T(8,128)(2,1)S(1)} %collective-permute-done.5), channel_id=1, source_target_pairs={{0,2},{2,4},{4,6},{6,8},{8,10},{10,12},{12,14},{14,16},{16,18},{18... | collective-permute-start | bytes 98312 | tf_op jit(solution)/shard_map/ppermute | solution.py:20
  43.7 3.4 %collective-permute-start.1 = (f32[256,128]{1,0:T(8,128)S(1)}, f32[256,128]{1,0:T(8,128)S(1)}, u32[]{:S(2)}, u32[]{:S(2)}) collective-permute-start(f32[256,128]{1,0:T(8,128)S(1)} %collective-permute-done), channel_id=1, source_target_pairs={{0,2},{2,4},{4,6},{6,8},{8,10},{10,12},{12,14},{14,16},{16,18},{18... | collective-permute-start | bytes 393224 | tf_op jit(solution)/shard_map/ppermute | solution.py:20
  47.2 3.4 %collective-permute-start.7 = (bf16[256,128]{1,0:T(8,128)(2,1)S(1)}, bf16[256,128]{1,0:T(8,128)(2,1)S(1)}, u32[]{:S(2)}, u32[]{:S(2)}) collective-permute-start(bf16[256,128]{1,0:T(8,128)(2,1)S(1)} %pad_maximum_fusion.5), channel_id=1, source_target_pairs={{0,4},{2,6},{4,8},{6,10},{8,12},{10,14},{12,16},{14,18},{16,20},{1... | collective-permute-start | bytes 196616 | tf_op jit(solution)/shard_map/ppermute | solution.py:20
  51.1 4.4 %collective-permute-start.2 = (f32[384,128]{1,0:T(8,128)S(1)}, f32[384,128]{1,0:T(8,128)S(1)}, u32[]{:S(2)}, u32[]{:S(2)}) collective-permute-start(f32[384,128]{1,0:T(8,128)S(1)} %pad_maximum_fusion.2), channel_id=1, source_target_pairs={{0,4},{2,6},{4,8},{6,10},{8,12},{10,14},{12,16},{14,18},{16,20},{1... | collective-permute-start | bytes 589832 | tf_op jit(solution)/shard_map/ppermute | solution.py:20
  56.2 3.5 %collective-permute-start.8 = (bf16[512,128]{1,0:T(8,128)(2,1)S(1)}, bf16[512,128]{1,0:T(8,128)(2,1)S(1)}, u32[]{:S(2)}, u32[]{:S(2)}) collective-permute-start(bf16[512,128]{1,0:T(8,128)(2,1)S(1)} %pad_maximum_fusion.4), channel_id=1, source_target_pairs={{0,8},{2,10},{4,12},{6,14},{8,16},{10,18},{12,20},{14,22},{16,24},... | collective-permute-start | bytes 393224 | tf_op jit(solution)/shard_map/ppermute | solution.py:20
  60.2 7.2 %collective-permute-start.3 = (f32[640,128]{1,0:T(8,128)S(1)}, f32[640,128]{1,0:T(8,128)S(1)}, u32[]{:S(2)}, u32[]{:S(2)}) collective-permute-start(f32[640,128]{1,0:T(8,128)S(1)} %pad_maximum_fusion), channel_id=1, source_target_pairs={{0,8},{2,10},{4,12},{6,14},{8,16},{10,18},{12,20},{14,22},{16,24},... | collective-permute-start | bytes 983048 | tf_op jit(solution)/shard_map/ppermute | solution.py:20
  67.5 3.9 %collective-permute-start.9 = (bf16[1024,128]{1,0:T(8,128)(2,1)S(1)}, bf16[1024,128]{1,0:T(8,128)(2,1)S(1)}, u32[]{:S(2)}, u32[]{:S(2)}) collective-permute-start(bf16[1024,128]{1,0:T(8,128)(2,1)S(1)} %pad_maximum_fusion.1), channel_id=1, source_target_pairs={{0,16},{2,18},{4,20},{6,22},{8,24},{10,26},{12,28},{14,30},{1,17},... | collective-permute-start | bytes 786440 | tf_op jit(solution)/shard_map/ppermute | solution.py:20
  71.4 1.7 %collective-permute-done.3 = f32[640,128]{1,0:T(8,128)S(1)} collective-permute-done((f32[640,128]{1,0:T(8,128)S(1)}, f32[640,128]{1,0:T(8,128)S(1)}, u32[]{:S(2)}, u32[]{:S(2)}) %collective-permute-start.3) | collective-permute-done | bytes 327712 | tf_op jit(solution)/shard_map/ppermute | solution.py:20
  73.1 0.8 constant_dynamic-update-slice_fusion.4
  73.9 1.1 constant_dynamic-update-slice_fusion.3
  76.9 18.4 %collective-permute-start.4 = (f32[1152,128]{1,0:T(8,128)}, f32[1152,128]{1,0:T(8,128)S(1)}, u32[]{:S(2)}, u32[]{:S(2)}) collective-permute-start(f32[1152,128]{1,0:T(8,128)} %constant_dynamic-update-slice_fusion), channel_id=1, source_target_pairs={{0,16},{2,18},{4,20},{6,22},{8,24},{10,26},{12,28},{14,30},{1,17},... | collective-permute-start | bytes 1769480 | tf_op jit(solution)/shard_map/ppermute | solution.py:20
  96.1 6.7 %collective-permute-done.4 = f32[1152,128]{1,0:T(8,128)S(1)} collective-permute-done((f32[1152,128]{1,0:T(8,128)}, f32[1152,128]{1,0:T(8,128)S(1)}, u32[]{:S(2)}, u32[]{:S(2)}) %collective-permute-start.4) | collective-permute-done | bytes 589856 | tf_op jit(solution)/shard_map/ppermute | solution.py:20
  105.4 0.8 fusion.6
  106.4 3.7 %convolution_convert_fusion = bf16[128,2048]{1,0:T(8,128)(2,1)} fusion(bf16[128,1024]{0,1:T(8,128)(2,1)S(1)} %bitcast.95, bf16[1024,2048]{1,0:T(8,128)(2,1)} %param.22), kind=kOutput, calls=%fused_computation.3 | convolution fusion | flops 537133056 | bytes 4980736 | tf_op jit(solution)/shard_map/dot_general | solution.py:171
  110.2 12.8 %reduce-scatter.2.cloned.1.call-done = bf16[64,2048]{1,0:T(8,128)(2,1)} async-done(((bf16[128,2048]{1,0:T(8,128)(2,1)}), bf16[64,2048]{1,0:T(8,128)(2,1)}) %reduce-scatter.2.cloned.1.call-update) | async-done | bytes 262160 | tf_op jit(solution)/shard_map/reduce_scatter | solution.py:170
  (82 shorter events, 12.2 us)
Async XLA Ops:
  6.5 9.4 %copy-start = (bf16[2048,128]{1,0:T(8,128)(2,1)S(1)}, bf16[2048,128]{1,0:T(8,128)(2,1)}, u32[]{:S(2)}) copy-start(bf16[2048,128]{1,0:T(8,128)(2,1)} %param.17) | copy-start | bytes 1572868
  6.5 9.9 %copy-start.1 = (bf16[2048,128]{1,0:T(8,128)(2,1)S(1)}, bf16[2048,128]{1,0:T(8,128)(2,1)}, u32[]{:S(2)}) copy-start(bf16[2048,128]{1,0:T(8,128)(2,1)} %param.15) | copy-start | bytes 1572868
  6.5 10.2 %copy-start.2 = (bf16[1,2048]{1,0:T(2,128)(2,1)S(1)}, bf16[1,2048]{1,0:T(2,128)(2,1)}, u32[]{:S(2)}) copy-start(bf16[1,2048]{1,0:T(2,128)(2,1)} %param.18) | copy-start | bytes 12292
  6.5 116.5 %reduce-scatter.2.cloned.1.call-start = ((), (), s32[]{:S(2)}) async-start(), calls=%async_computation.1 | async-start | bytes 786432 | tf_op jit(solution)/shard_map/reduce_scatter | solution.py:170
  9.2 18.4 %copy-start.3 = (f32[128]{0:T(128)S(1)}, f32[128]{0:T(128)}, u32[]{:S(2)}) copy-start(f32[128]{0:T(128)} %param.21) | copy-start | bytes 1540
  10.5 29.8 %collective-permute-start.5 = (bf16[128,128]{1,0:T(8,128)(2,1)S(1)}, bf16[128,128]{1,0:T(8,128)(2,1)S(1)}, u32[]{:S(2)}, u32[]{:S(2)}) collective-permute-start(bf16[128,128]{1,0:T(8,128)(2,1)S(1)} %convolution_convert_fusion.2), channel_id=1, source_target_pairs={{0,2},{2,4},{4,6},{6,8},{8,10},{10,12},{12,14},{14,16},{16,18},{18... | collective-permute-start | bytes 98312 | tf_op jit(solution)/shard_map/ppermute | solution.py:20
  28.9 14.8 %collective-permute-start = (f32[256,128]{1,0:T(8,128)S(1)}, f32[256,128]{1,0:T(8,128)S(1)}, u32[]{:S(2)}, u32[]{:S(2)}) collective-permute-start(f32[256,128]{1,0:T(8,128)S(1)} %pad_maximum_fusion.3), channel_id=1, source_target_pairs={{0,2},{2,4},{4,6},{6,8},{8,10},{10,12},{12,14},{14,16},{16,18},{18... | collective-permute-start | bytes 393224 | tf_op jit(solution)/shard_map/ppermute | solution.py:20
  32.4 3.2 %copy-start.4 = (f32[128]{0:T(128)S(1)}, f32[128]{0:T(128)}, u32[]{:S(2)}) copy-start(f32[128]{0:T(128)} %param.20) | copy-start | bytes 1540
  36.5 2.4 %copy-start.5 = (s32[1,16]{1,0:T(1,128)S(1)}, s32[1,16]{1,0:T(1,128)}, u32[]{:S(2)}) copy-start(s32[1,16]{1,0:T(1,128)} %param.23) | copy-start | bytes 196
  40.3 6.8 %collective-permute-start.6 = (bf16[128,128]{1,0:T(8,128)(2,1)S(1)}, bf16[128,128]{1,0:T(8,128)(2,1)S(1)}, u32[]{:S(2)}, u32[]{:S(2)}) collective-permute-start(bf16[128,128]{1,0:T(8,128)(2,1)S(1)} %collective-permute-done.5), channel_id=1, source_target_pairs={{0,2},{2,4},{4,6},{6,8},{8,10},{10,12},{12,14},{14,16},{16,18},{18... | collective-permute-start | bytes 98312 | tf_op jit(solution)/shard_map/ppermute | solution.py:20
  43.7 6.9 %collective-permute-start.1 = (f32[256,128]{1,0:T(8,128)S(1)}, f32[256,128]{1,0:T(8,128)S(1)}, u32[]{:S(2)}, u32[]{:S(2)}) collective-permute-start(f32[256,128]{1,0:T(8,128)S(1)} %collective-permute-done), channel_id=1, source_target_pairs={{0,2},{2,4},{4,6},{6,8},{8,10},{10,12},{12,14},{14,16},{16,18},{18... | collective-permute-start | bytes 393224 | tf_op jit(solution)/shard_map/ppermute | solution.py:20
  47.2 9.0 %collective-permute-start.7 = (bf16[256,128]{1,0:T(8,128)(2,1)S(1)}, bf16[256,128]{1,0:T(8,128)(2,1)S(1)}, u32[]{:S(2)}, u32[]{:S(2)}) collective-permute-start(bf16[256,128]{1,0:T(8,128)(2,1)S(1)} %pad_maximum_fusion.5), channel_id=1, source_target_pairs={{0,4},{2,6},{4,8},{6,10},{8,12},{10,14},{12,16},{14,18},{16,20},{1... | collective-permute-start | bytes 196616 | tf_op jit(solution)/shard_map/ppermute | solution.py:20
  51.1 8.6 %collective-permute-start.2 = (f32[384,128]{1,0:T(8,128)S(1)}, f32[384,128]{1,0:T(8,128)S(1)}, u32[]{:S(2)}, u32[]{:S(2)}) collective-permute-start(f32[384,128]{1,0:T(8,128)S(1)} %pad_maximum_fusion.2), channel_id=1, source_target_pairs={{0,4},{2,6},{4,8},{6,10},{8,12},{10,14},{12,16},{14,18},{16,20},{1... | collective-permute-start | bytes 589832 | tf_op jit(solution)/shard_map/ppermute | solution.py:20
  56.2 11.3 %collective-permute-start.8 = (bf16[512,128]{1,0:T(8,128)(2,1)S(1)}, bf16[512,128]{1,0:T(8,128)(2,1)S(1)}, u32[]{:S(2)}, u32[]{:S(2)}) collective-permute-start(bf16[512,128]{1,0:T(8,128)(2,1)S(1)} %pad_maximum_fusion.4), channel_id=1, source_target_pairs={{0,8},{2,10},{4,12},{6,14},{8,16},{10,18},{12,20},{14,22},{16,24},... | collective-permute-start | bytes 393224 | tf_op jit(solution)/shard_map/ppermute | solution.py:20
  60.2 12.9 %collective-permute-start.3 = (f32[640,128]{1,0:T(8,128)S(1)}, f32[640,128]{1,0:T(8,128)S(1)}, u32[]{:S(2)}, u32[]{:S(2)}) collective-permute-start(f32[640,128]{1,0:T(8,128)S(1)} %pad_maximum_fusion), channel_id=1, source_target_pairs={{0,8},{2,10},{4,12},{6,14},{8,16},{10,18},{12,20},{14,22},{16,24},... | collective-permute-start | bytes 983048 | tf_op jit(solution)/shard_map/ppermute | solution.py:20
  67.5 27.9 %collective-permute-start.9 = (bf16[1024,128]{1,0:T(8,128)(2,1)S(1)}, bf16[1024,128]{1,0:T(8,128)(2,1)S(1)}, u32[]{:S(2)}, u32[]{:S(2)}) collective-permute-start(bf16[1024,128]{1,0:T(8,128)(2,1)S(1)} %pad_maximum_fusion.1), channel_id=1, source_target_pairs={{0,16},{2,18},{4,20},{6,22},{8,24},{10,26},{12,28},{14,30},{1,17},... | collective-permute-start | bytes 786440 | tf_op jit(solution)/shard_map/ppermute | solution.py:20
  76.9 25.9 %collective-permute-start.4 = (f32[1152,128]{1,0:T(8,128)}, f32[1152,128]{1,0:T(8,128)S(1)}, u32[]{:S(2)}, u32[]{:S(2)}) collective-permute-start(f32[1152,128]{1,0:T(8,128)} %constant_dynamic-update-slice_fusion), channel_id=1, source_target_pairs={{0,16},{2,18},{4,20},{6,22},{8,24},{10,26},{12,28},{14,30},{1,17},... | collective-permute-start | bytes 1769480 | tf_op jit(solution)/shard_map/ppermute | solution.py:20
Sparse Core Ops, SparseCore 0:
  110.3 12.6 reduce-scatter.1
where the time goes:
time: 130 us
  starting transfers between devices  55.7 us (43%)
  waiting for transfers between devices  21.3 us (16%)
  matrix products  18.9 us (15%)
  between operations  14.6 us (11%)
  other arithmetic  12.4 us (10%)
  local copies, waits for them, and re-layouts  4.28 us (3%)
  blocking collectives  2.6 us (2%)
    ppermute x10, starting transfers between devices, shifted(): lax.ppermute(value, axis, [(source, source + steps) for source in range(l...  55.7 us
    reduce_scatter x1, waiting for transfers between devices, body(): lax.psum_scatter(jnp.dot(attended, w_out, preferred_element_type=jnp.floa...  12.8 us
    another operation x2, other arithmetic, segment_terms(): lax.linalg.triangular_solve(lower_unit, rate_values[:, None] * crossing,...  9.81 us
    ppermute x10, waiting for transfers between devices, shifted(): lax.ppermute(value, axis, [(source, source + steps) for source in range(l...  8.46 us
    dot_general x1, matrix products, body(): jnp.dot(attended, w_out, preferred_element_type=jnp.float32)  3.73 us
    dot_general x1, matrix products, segment_terms(): queries = jnp.dot(seg_rows, query_cols, preferred_element_type=jnp.float32)  2.9 us
    all_gather x1, blocking collectives, body(): seg_rows = lax.all_gather(hidden, 'head', axis=0, tiled=True)  2.6 us
  transfers between devices with their start and end apart: 11, of which 3 were waited for; matrix products, arithmetic and copies ran while one was open for 21% of the time, Pallas kernels for 0%

commit v1 on v0

--- a/solution.py
+++ b/solution.py
@@ -12,12 +12,6 @@
 HIGHEST = lax.Precision.HIGHEST
 EPSILON = 1e-06
 NEGATIVE = -1e30
-
-
-def shifted(value, axis, steps):
-    count = lax.axis_size(axis)
-    leading, last = (max(0, -steps), min(count, count - steps))
-    return lax.ppermute(value, axis, [(source, source + steps) for source in range(leading, last)])
 
 
 def rms_scaled(values_in, gain):
@@ -130,24 +124,28 @@
     segments = lax.axis_size("ctx")
     position = lax.axis_index("ctx")
     mask_row = block_mask[0]
+    most_blocks = segments // 4
     slots = jnp.arange(segments, dtype=jnp.int32)
-    key_buffer = jnp.concatenate([product, exit_keys], axis=0)
-    value_buffer = value_rows
-    for section_index in range(segments.bit_length()):
-        distance = 1 if section_index == 0 else 2 ** (section_index - 1)
-        arrived = shifted(key_buffer, "ctx", distance)
-        arrived_values = shifted(value_buffer, "ctx", distance)
-        if section_index == 0:
-            key_buffer = arrived
-            value_buffer = arrived_values
-        else:
-            own_product = key_buffer[:HD]
-            older_keys = jnp.dot(arrived[HD:], own_product.T, precision=HIGHEST)
-            combined = jnp.dot(own_product, arrived[:HD], precision=HIGHEST)
-            key_buffer = jnp.concatenate([combined, older_keys, key_buffer[HD:]], axis=0)
-            value_buffer = jnp.concatenate([arrived_values, value_buffer], axis=0)
-    key_all = key_buffer[HD:].astype(jnp.bfloat16)
-    allowed = (jnp.roll(mask_row, segments - position) > 0) & (slots >= segments - position)
+    value_blocks = lax.all_gather(value_rows, "ctx")
+    products = lax.all_gather(product, "ctx")
+    key_blocks = lax.all_gather(exit_keys, "ctx")
+    allowed = (mask_row > 0) & (slots < position)
+    ranking = jnp.where(allowed, 0, 1) * segments + slots
+    chosen = jnp.argsort(ranking)[:most_blocks]
+    allowed = allowed[chosen]
+
+    def extend(crossed, step):
+        segment = jnp.maximum(position - 1 - step, 0)
+        return jnp.dot(crossed, products[segment], precision=HIGHEST), crossed
+
+    _, crossings = lax.scan(
+        extend, jnp.eye(HD, dtype=jnp.float32), jnp.arange(segments - 1, dtype=jnp.int32)
+    )
+    crossings = crossings[jnp.clip(position - 1 - chosen, 0, segments - 2)]
+    key_blocks = jnp.einsum(
+        "bij,btj->bti", crossings, key_blocks[chosen], precision=HIGHEST
+    ).astype(jnp.bfloat16)
+    value_blocks = value_blocks[chosen]
     local_peak = jnp.max(own_scores, axis=1)
     near_exp = jnp.exp(own_scores - local_peak[:, None])
     running = (
@@ -155,24 +153,16 @@
         jnp.sum(near_exp, axis=1),
         jnp.dot(near_exp.astype(jnp.bfloat16), value_rows, preferred_element_type=jnp.float32),
     )
-    key_blocks = key_all.reshape(segments, SEG, HD)
-    value_blocks = value_buffer.reshape(segments, SEG, HD)
-    most_blocks = segments // 4
-    ranking = jnp.where(allowed, 0, 1) * segments + slots
-    chosen_slots = jnp.argsort(ranking)[:most_blocks]
-    key_blocks = key_blocks[chosen_slots]
-    value_blocks = value_blocks[chosen_slots]
-    allowed = allowed[chosen_slots]
     running = attend_blocks(moved_queries, key_blocks, value_blocks, allowed, running)
     attended = (running[2] / running[1][:, None]).astype(jnp.bfloat16)
     groups = attended.shape[0] // SEG
     attended = attended.reshape(groups, SEG, HD).transpose(1, 0, 2).reshape(SEG, groups * HD)
-    return lax.psum_scatter(
-        jnp.dot(attended, w_out, preferred_element_type=jnp.float32).astype(jnp.bfloat16),
-        "head",
-        scatter_dimension=0,
-        tiled=True,
-    )
+    partial = jnp.dot(attended, w_out, preferred_element_type=jnp.float32).astype(jnp.bfloat16)
+    core = lax.axis_index("head")
+    half = SEG // lax.axis_size("head")
+    away = lax.dynamic_slice_in_dim(partial, (1 - core) * half, half)
+    kept = lax.dynamic_slice_in_dim(partial, core * half, half)
+    return kept + lax.ppermute(away, "head", [(0, 1), (1, 0)])
 
 
 def solution(mesh):

time: 130 us -> 203 us (1.56)
  starting transfers between devices: 55.7 us -> 0.12 us
  blocking collectives: 2.6 us -> 49.7 us
  waiting for transfers between devices: 21.3 us -> 57.3 us
  local copies, waits for them, and re-layouts: 4.28 us -> 23.9 us
  matrix products: 18.9 us -> 33.3 us
  loops' own time: 0 us -> 10.3 us
    all_gather x0 -> x2, waiting for transfers between devices: none -> 55.7 us  [the longest x1 54.4 us: body(): products = lax.all_gather(product, 'ctx')]
    ppermute x10 -> x1, starting transfers between devices: 55.7 us -> 0.07 us  [body(): return kept + lax.ppermute(away, 'head', [(0, 1), (1, 0)])]
    all_gather x0 -> x1, blocking collectives: none -> 47.1 us  [body(): value_blocks = lax.all_gather(value_rows, 'ctx')]
    dot_general x7 -> x16, matrix products: 3.43 us -> 17.3 us  [the longest x15 16.9 us: extend(): return (jnp.dot(crossed, products[segment], precision=HIGHEST), crossed)]
    reduce_scatter x1 -> x0, waiting for transfers between devices: 12.8 us -> none  [body(): lax.psum_scatter(jnp.dot(attended, w_out, preferred_element_type=jnp.floa...]
    another operation x0 -> x1, loops' own time: none -> 10.3 us  [body(): lax.scan(extend, jnp.eye(HD, dtype=jnp.float32), jnp.arange(segments - 1,...]
    dynamic_update_slice x0 -> x15, local copies, waits for them, and re-layouts: none -> 9.41 us  [body(): lax.scan(extend, jnp.eye(HD, dtype=jnp.float32), jnp.arange(segments - 1,...]
    dynamic_slice x0 -> x16, local copies, waits for them, and re-layouts: none -> 8.76 us  [the longest x15 8.73 us: body(): lax.scan(extend, jnp.eye(HD, dtype=jnp.float32), jnp.arange(segments - 1,...]
  transfers between devices with their start and end apart: 11 -> 3, of which waited for: 3 -> 3; matrix products, arithmetic and copies ran while one was open for 21% -> 6% of each run, Pallas kernels for 0% -> 0%
where the time goes in v1:
time: 203 us; the launch traced here: 202 us
  waiting for transfers between devices  57.3 us (28%)
  blocking collectives  49.7 us (24%)
  matrix products  33.3 us (16%)
  local copies, waits for them, and re-layouts  23.9 us (12%)
  between operations  14.4 us (7%)
  other arithmetic  12.9 us (6%)
  loops' own time  10.3 us (5%)
    all_gather x1, waiting for transfers between devices, body(): products = lax.all_gather(product, 'ctx')  54.4 us
    all_gather x1, blocking collectives, body(): value_blocks = lax.all_gather(value_rows, 'ctx')  47.1 us
    dot_general x15, matrix products, extend(): return (jnp.dot(crossed, products[segment], precision=HIGHEST), crossed)  16.9 us
    another operation x1, loops' own time, body(): lax.scan(extend, jnp.eye(HD, dtype=jnp.float32), jnp.arange(segments - 1,...  10.3 us
    another operation x2, other arithmetic, segment_terms(): lax.linalg.triangular_solve(lower_unit, rate_values[:, None] * crossing,...  9.81 us
    dynamic_update_slice x15, local copies, waits for them, and re-layouts, body(): lax.scan(extend, jnp.eye(HD, dtype=jnp.float32), jnp.arange(segments - 1,...  9.41 us
    dynamic_slice x15, local copies, waits for them, and re-layouts, body(): lax.scan(extend, jnp.eye(HD, dtype=jnp.float32), jnp.arange(segments - 1,...  8.73 us
  transfers between devices with their start and end apart: 3, of which 3 were waited for; matrix products, arithmetic and copies ran while one was open for 6% of the time, Pallas kernels for 0%

profile of v1, /device:TPU:0, one launch (start us, length us, event | category | flops | bytes accessed | tf_op | source)
XLA Modules:
  0.0 201.9 jit_solution(14812693193883655751)
XLA Ops:
  6.6 2.6 %all_gather.21 = bf16[128,2048]{1,0:T(8,128)(2,1)S(1)} all-gather(bf16[64,2048]{1,0:T(8,128)(2,1)} %param.15), channel_id=1, replica_groups=mesh['ctx'=16,'head'=2] {'head'}, dimensions={0}, use_global_device_ids=true | all-gather | bytes 786432 | tf_op jit(solution)/shard_map/all_gather | solution.py:120
  9.5 1.4 multiply_reduce_fusion
  12.3 9.8 %custom-call.4 = f32[1,128,128]{1,2,0:T(8,128)S(1)} custom-call(f32[1,128,128]{2,1,0:T(8,128)S(1)} %fusion.16), custom_call_target="InvertDiagBlocksLowerTriangular" | custom-call | tf_op jit(solution)/shard_map/triangular_solve/custom-call.1 | solution.py:65
  25.2 3.0 %convolution_bitcast_fusion.1 = f32[16,8,8,128]{3,2,1,0:T(8,128)S(1)} fusion(bf16[128,2048]{1,0:T(8,128)(2,1)S(1)} %all_gather.21, bf16[2048,1024]{1,0:T(8,128)(2,1)} %param.16), kind=kOutput, calls=%fused_computation.23 | convolution fusion | flops 536870912 | bytes 5242880 | tf_op jit(solution)/shard_map/dot_general | solution.py:32
  28.8 1.3 sort.17
  30.2 47.1 %all-gather.2 = bf16[2048,128]{1,0:T(8,128)(2,1)S(1)} all-gather(bf16[128,128]{1,0:T(8,128)(2,1)S(1)} %convolution_convert_fusion.2), channel_id=4, replica_groups=mesh['ctx'=16,'head'=2] {'ctx'}, dimensions={0}, use_global_device_ids=true | all-gather | bytes 557056 | tf_op jit(solution)/shard_map/all_gather | solution.py:129
  82.0 1.3 all-gather.6.cloned.1.call-done
  83.3 1.5 copy.28
  85.5 54.4 %all-gather.8.cloned.1.call-done = f32[2048,128]{1,0:T(8,128)} async-done(((f32[128,128]{1,0:T(8,128)}), f32[2048,128]{1,0:T(8,128)}) %all-gather.8.cloned.1.call-update) | async-done | bytes 1048592 | tf_op jit(solution)/shard_map/all_gather | solution.py:130
  139.9 45.4 %while.4 = (s32[]{:T(128)}, f32[128,128]{0,1:T(8,128)S(1)}, f32[15,128,128]{1,2,0:T(8,128)}, s32[15]{0:T(128)S(1)}, s32[]{:T(128)}, /*index=5*/f32[16,128,128]{2,1,0:T(8,128)}, s32[]{:T(128)}, s32[]{:T(128)}) while((s32[]{:T(128)}, f32[128,128]{0,1:T(8,128)S(1)}, f32[15,128,128]{1,2,0:T(8,128)}, s32[15]{0:T(128)S(1)}, s32[]{:T(128)}, ...), condition=%wide.region_6.8_spmd, body=%wide.region_5.7_spmd.sunk | while | flops 25165828 | bytes 458889 | solution.py:141
  141.7 1.1 convolution_bitcast_fusion.4
  144.7 1.1 convolution_bitcast_fusion.4
  147.8 1.1 convolution_bitcast_fusion.4
  150.8 1.1 convolution_bitcast_fusion.4
  153.8 1.1 convolution_bitcast_fusion.4
  156.8 1.1 convolution_bitcast_fusion.4
  159.9 1.1 convolution_bitcast_fusion.4
  162.9 1.1 convolution_bitcast_fusion.4
  172.0 1.1 convolution_bitcast_fusion.4
  178.0 1.1 convolution_bitcast_fusion.4
  181.1 1.1 convolution_bitcast_fusion.4
  185.2 1.8 gather_fusion.2
  189.7 2.9 %convolution_convert_fusion = bf16[128,2048]{1,0:T(8,128)(2,1)S(1)} fusion(bf16[128,1024]{0,1:T(8,128)(2,1)S(1)} %bitcast.115, bf16[1024,2048]{1,0:T(8,128)(2,1)} %param.24), kind=kOutput, calls=%fused_computation.9 | convolution fusion | flops 537133056 | bytes 4980736 | tf_op jit(solution)/shard_map/dot_general | solution.py:160
  192.8 1.5 collective-permute-done
  (112 shorter events, 36.3 us)
Async XLA Ops:
  6.5 2.6 %copy-start = (bf16[2048,128]{1,0:T(8,128)(2,1)S(1)}, bf16[2048,128]{1,0:T(8,128)(2,1)}, u32[]{:S(2)}) copy-start(bf16[2048,128]{1,0:T(8,128)(2,1)} %param.17) | copy-start | bytes 1572868
  6.5 5.2 %copy-start.2 = (bf16[1,2048]{1,0:T(2,128)(2,1)S(1)}, bf16[1,2048]{1,0:T(2,128)(2,1)}, u32[]{:S(2)}) copy-start(bf16[1,2048]{1,0:T(2,128)(2,1)} %param.20) | copy-start | bytes 12292
  6.5 15.6 %copy-start.3 = (f32[128]{0:T(128)S(1)}, f32[128]{0:T(128)}, u32[]{:S(2)}) copy-start(f32[128]{0:T(128)} %param.23) | copy-start | bytes 1540
  6.5 76.8 %all-gather.6.cloned.1.call-start = ((), (), s32[]{:S(2)}) async-start(), calls=%async_computation | async-start | bytes 1114112 | tf_op jit(solution)/shard_map/all_gather | solution.py:131
  23.7 116.1 %all-gather.8.cloned.1.call-start = ((), (), s32[]{:S(2)}) async-start(), calls=%async_computation.1 | async-start | bytes 1114112 | tf_op jit(solution)/shard_map/all_gather | solution.py:130
  25.1 3.3 %copy-start.1 = (bf16[2048,128]{1,0:T(8,128)(2,1)S(1)}, bf16[2048,128]{1,0:T(8,128)(2,1)}, u32[]{:S(2)}) copy-start(bf16[2048,128]{1,0:T(8,128)(2,1)} %param.18) | copy-start | bytes 1572868
  28.1 0.7 copy-start.5
  28.1 50.3 %copy-start.4 = (f32[128]{0:T(128)S(1)}, f32[128]{0:T(128)}, u32[]{:S(2)}) copy-start(f32[128]{0:T(128)} %param.22) | copy-start | bytes 1540
  192.7 1.6 collective-permute-start
Sparse Core Ops, SparseCore 0:
  23.9 59.4 all-gather.5
  86.1 53.7 all-gather.7

commit v2 on v1

v2 whole, which is shorter than its diff:
```python
import functools
import math

import jax
import jax.numpy as jnp
from jax import lax
from jax.experimental import pallas as pl
from jax.experimental.pallas import tpu as pltpu
from jax.sharding import PartitionSpec as P

EPSILON = 1e-06
NEGATIVE = -1e30
F32 = jnp.float32
BF16 = jnp.bfloat16
VMEM_LIMIT = 48 * 1024 * 1024


def call(kernel, out_shape, args, in_specs=None, scratch=(), flops=0, moved=0):
    vmem = pl.BlockSpec(memory_space=pltpu.VMEM)
    return pl.pallas_call(
        kernel,
        out_shape=out_shape,
        in_specs=in_specs or [vmem] * len(args),
        out_specs=jax.tree.map(lambda _: vmem, out_shape),
        scratch_shapes=list(scratch),
        compiler_params=pltpu.CompilerParams(vmem_limit_bytes=VMEM_LIMIT),
        cost_estimate=pl.CostEstimate(flops=flops, bytes_accessed=moved, transcendentals=0),
    )(*args)


def shaped(shape, dtype):
    return jax.ShapeDtypeStruct(shape, dtype)


def split(value):
    high = value.astype(BF16)
    return high, (value - high.astype(F32)).astype(BF16)


def dot3(left, right, left_dim=1, right_dim=0):
    left_high, left_low = split(left)
    right_high, right_low = split(right)
    return lax.dot_general(
        jnp.concatenate([left_high, left_high, left_low], axis=left_dim),
        jnp.concatenate([right_high, right_low, right_high], axis=right_dim),
        (((left_dim,), (right_dim,)), ((), ())),
        preferred_element_type=F32,
    )


def iota2(shape):
    return lax.broadcasted_iota(jnp.int32, shape, 0), lax.broadcasted_iota(jnp.int32, shape, 1)


def project_kernel(rows_ref, key_ref, value_ref, dir_ref, rate_ref, bias_ref, gain_ref,
                   kn_ref, val_ref, dirs_ref, rates_ref):
    rows = rows_ref[...]
    keys = jnp.dot(rows, key_ref[...], preferred_element_type=F32)
    kn_ref[...] = (
        keys * lax.rsqrt(jnp.mean(keys * keys, axis=-1, keepdims=True) + EPSILON) * gain_ref[...]
    )
    raw = jnp.dot(rows, dir_ref[...], preferred_element_type=F32)
    dirs_ref[...] = raw * lax.rsqrt(jnp.sum(raw * raw, axis=-1, keepdims=True) + EPSILON)
    vector = jnp.broadcast_to(rate_ref[...], (16, rows.shape[1]))
    logits = lax.dot_general(rows, vector, (((1,), (1,)), ((), ())), preferred_element_type=F32)
    rates_ref[...] = 2.0 * jax.nn.sigmoid(logits[:, :1] + bias_ref[0])
    val_ref[...] = jnp.dot(rows, value_ref[...], preferred_element_type=F32).astype(BF16)


def solve_kernel(kn_ref, dirs_ref, rates_ref, exit_ref, turn_ref, coeff_ref, solved_ref):
    kn, dirs, rates = kn_ref[...], dirs_ref[...], rates_ref[...]
    tokens, size = dirs.shape
    rows, cols = iota2((tokens, tokens))
    below = rows > cols
    grams = dot3(dirs, jnp.concatenate([dirs, kn], axis=0), 1, 1)
    lower = jnp.where(below, rates * grams[:, :tokens], 0.0)
    crossing = jnp.where(below, rates * grams[:, tokens:], 0.0)
    block = 8
    inverse = jnp.where(rows == cols, 1.0, 0.0).astype(F32)
    first = rows - rows % block
    for step in range(block - 1):
        column = jnp.sum(jnp.where(cols == first + step, lower, 0.0), axis=1, keepdims=True)
        pivot = inverse.reshape(tokens // block, block, tokens)[:, step : step + 1, :]
        pivot = jnp.broadcast_to(pivot, (tokens // block, block, tokens)).reshape(tokens, tokens)
        inverse = inverse - column * pivot
    while block < tokens:
        corner = (
            (rows // (2 * block) == cols // (2 * block))
            & (rows % (2 * block) >= block)
            & (cols % (2 * block) < block)
        )
        inverse = inverse - dot3(dot3(inverse, jnp.where(corner, lower, 0.0)), inverse)
        block *= 2
    both = dot3(inverse, jnp.concatenate([crossing, rates * dirs], axis=1))
    coeff_ref[...] = both[:, :tokens]
    solved_ref[...] = both[:, tokens:]
    crossed = dot3(both, dirs, 0, 0)
    exit_ref[...] = kn - crossed[:tokens]
    heads, lanes = iota2((size, size))
    turn_ref[...] = jnp.where(heads == lanes, 1.0, 0.0) - crossed[tokens:]


def query_kernel(rows_ref, weight_ref, gain_ref, kn_ref, dirs_ref, coeff_ref, solved_ref, val_ref,
                 moved_ref, weighted_ref, peak_ref, total_ref):
    tokens, size = kn_ref.shape
    heads = moved_ref.shape[0]
    raw = jnp.dot(rows_ref[...], weight_ref[...], preferred_element_type=F32)
    raw = jnp.concatenate([raw[:, h * size : (h + 1) * size] for h in range(heads)], axis=0)
    queries = raw * lax.rsqrt(jnp.mean(raw * raw, axis=-1, keepdims=True) + EPSILON) * gain_ref[...]
    seen = dot3(queries, jnp.concatenate([kn_ref[...], dirs_ref[...]], axis=0), 1, 1)
    rows, cols = iota2((heads * tokens, tokens))
    up_to = rows % tokens >= cols
    reach = jnp.where(up_to, seen[:, tokens:], 0.0)
    taken = dot3(reach, jnp.concatenate([coeff_ref[...], solved_ref[...]], axis=1))
    scores = (seen[:, :tokens] - taken[:, :tokens]) * (1.0 / math.sqrt(size))
    scores = jnp.where(up_to, scores, NEGATIVE)
    moved = (queries - taken[:, tokens:]).astype(BF16)
    peak = jnp.max(scores, axis=1, keepdims=True)
    weights = jnp.exp(scores - peak)
    total = jnp.sum(weights, axis=1, keepdims=True)
    weighted = jnp.dot(weights.astype(BF16), val_ref[...], preferred_element_type=F32)
    for h in range(heads):
        part = slice(h * tokens, (h + 1) * tokens)
        moved_ref[h] = moved[part]
        weighted_ref[h] = weighted[part]
        peak_ref[h] = peak[part]
        total_ref[h] = total[part]


def leave_kernel(member_ref, exit_ref, turns_ref, near_ref, last_ref, whole_ref, starts_ref):
    member = member_ref[0]
    size = exit_ref.shape[1]
    group = turns_ref.shape[0]
    own = exit_ref[...]
    heads, lanes = iota2((size, size))
    product = jnp.where(heads == lanes, 1.0, 0.0).astype(F32)
    keys = own
    for index in range(group):
        near_ref[index] = keys.astype(BF16)
        starts_ref[:, index * size : (index + 1) * size] = product
        turn = turns_ref[index]
        product = dot3(product, turn) if index else turn
        keys = jnp.where(index > member, dot3(keys, turn), own)
    last_ref[...] = keys
    whole_ref[...] = product


def arrive_kernel(count, *refs):
    lasts, wholes = refs[:count], refs[count : 2 * count - 1]
    starts_ref, far_ref = refs[2 * count - 1 :]
    tokens, size = lasts[0].shape
    brought = [lasts[0][...]]
    product = None
    for index in range(1, count):
        whole = wholes[index - 1][...]
        product = whole if product is None else dot3(whole, product)
        brought.append(dot3(lasts[index][...], product))
    keys = jnp.concatenate(brought, axis=0)
    for member in range(far_ref.shape[0]):
        start = starts_ref[:, member * size : (member + 1) * size]
        far_ref[member] = (dot3(keys, start) if member else keys).astype(BF16)


def attend_kernel(most, position_ref, mask_ref, near_ref, far_ref, val_ref, moved_ref, weighted_ref,
                  peak_ref, total_ref, out_hbm, away_ref, kept_ref,
                  chosen_ref, keys_ref, vals_ref, attended_ref, run_w, run_p, run_t, out_ref, out_sem):
    out_copy = pltpu.make_async_copy(out_hbm, out_ref, out_sem)
    out_copy.start()
    place, core = position_ref[0], position_ref[1]
    group = near_ref.shape[0]
    heads, tokens, size = moved_ref.shape
    segments = mask_ref.shape[0]
    scaling = 1.0 / math.sqrt(size)
    mine, member = place // group, place % group

    def pick(segment, count):
        @pl.when((mask_ref[segment] > 0) & (segment < place) & (count < most))
        def _():
            chosen_ref[count] = segment

        return count + ((mask_ref[segment] > 0) & (segment < place)).astype(jnp.int32)

    for slot in range(most):
        chosen_ref[slot] = 0
    found = lax.fori_loop(0, segments, pick, jnp.int32(0))
    chunk = keys_ref.shape[0] // tokens
    run_w[...] = weighted_ref[...]
    run_p[...] = peak_ref[...]
    run_t[...] = total_ref[...]
    lanes = lax.broadcasted_iota(jnp.int32, (tokens, chunk * tokens), 1)

    @pl.loop(0, most // chunk)
    def _(turn):
        for slot in range(chunk):
            segment = chosen_ref[turn * chunk + slot]
            whose, distance = segment % group, mine - segment // group
            before = pl.multiple_of(jnp.maximum(distance - 1, 0) * tokens, tokens)
            far = far_ref[whose, pl.ds(before, tokens), :]
            keys_ref[slot * tokens : (slot + 1) * tokens, :] = jnp.where(
                distance > 0, far, near_ref[whose]
            )
            vals_ref[slot * tokens : (slot + 1) * tokens, :] = val_ref[
                whose, pl.ds(pl.multiple_of(distance * tokens, tokens), tokens), :
            ]
        keep = lanes < (found - turn * chunk) * tokens
        keys, vals = keys_ref[...], vals_ref[...]
        for head in range(heads):
            scores = lax.dot_general(
                moved_ref[head], keys, (((1,), (1,)), ((), ())), preferred_element_type=F32
            )
            scores = jnp.where(keep, scores * scaling, NEGATIVE)
            peak = run_p[head]
            new_peak = jnp.maximum(peak, jnp.max(scores, axis=1, keepdims=True))
            fading = jnp.exp(peak - new_peak)
            weights = jnp.exp(scores - new_peak)
            run_p[head] = new_peak
            run_t[head] = run_t[head] * fading + jnp.sum(weights, axis=1, keepdims=True)
            run_w[head] = run_w[head] * fading + jnp.dot(
                weights.astype(BF16), vals, preferred_element_type=F32
            )

    for head in range(heads):
        attended_ref[:, head * size : (head + 1) * size] = (run_w[head] / run_t[head]).astype(BF16)
    out_copy.wait()
    half = kept_ref.shape[0]
    weight = out_ref[...]
    for ref, which in ((away_ref, 1 - core), (kept_ref, core)):
        rows = attended_ref[pl.ds(pl.multiple_of(which * half, half), half), :]
        ref[...] = jnp.dot(rows, weight, preferred_element_type=F32).astype(BF16)


def body(
    hidden, w_query, w_key, w_value, w_dir, u_rate, rate_bias, q_gain, k_gain, w_out, block_mask
):
    segments = lax.axis_size("ctx")
    position = lax.axis_index("ctx")
    core = lax.axis_index("head")
    group = max(d for d in range(1, math.isqrt(segments) + 1) if segments % d == 0)
    groups = segments // group
    members = [[g * group + m for m in range(group)] for g in range(groups)]
    seg_rows = lax.all_gather(hidden, "head", axis=0, tiled=True)
    tokens, width = seg_rows.shape
    size = w_key.shape[1]
    heads = w_query.shape[1] // size
    smem = pl.BlockSpec(memory_space=pltpu.SMEM)
    vmem = pl.BlockSpec(memory_space=pltpu.VMEM)
    square = shaped((tokens, size), F32)

    def within_group(parts):
        return lax.all_to_all(parts, "ctx", 0, 0, axis_index_groups=members)

    def to_later_group(value, distance):
        step = distance * group
        return lax.ppermute(value, "ctx", [(s, s + step) for s in range(segments - step)])

    kn, val, dirs, rates = call(
        project_kernel,
        (square, shaped((tokens, size), BF16), square, shaped((tokens, 1), F32)),
        (seg_rows, w_key, w_value, w_dir, u_rate, rate_bias, k_gain.reshape(1, size)),
        in_specs=[vmem] * 5 + [smem, vmem],
        flops=6 * tokens * width * size,
        moved=8 * width * size,
    )
    vals = jnp.concatenate([val] + [to_later_group(val, d) for d in range(1, groups)], axis=0)
    vals = within_group(jnp.broadcast_to(vals[None], (group,) + vals.shape))
    exit_keys, turn, coeff, solved = call(
        solve_kernel, (square, shaped((size, size), F32), square, square), (kn, dirs, rates),
        flops=40 * tokens**3 * 3, moved=10**6,
    )
    turns = within_group(jnp.broadcast_to(turn[None], (group, size, size)))
    pair = math.gcd(heads, 2)
    blocks = pl.BlockSpec((pair, tokens, size), lambda i: (i, 0, 0))
    thin = pl.BlockSpec((pair, tokens, 1), lambda i: (i, 0, 0))
    moved, weighted, peak, total = pl.pallas_call(
        query_kernel,
        grid=(heads // pair,),
        in_specs=[vmem, pl.BlockSpec((width, pair * size), lambda i: (0, i))] + [vmem] * 6,
        out_specs=(blocks, blocks, thin, thin),
        out_shape=(
            shaped((heads, tokens, size), BF16),
            shaped((heads, tokens, size), F32),
            shaped((heads, tokens, 1), F32),
            shaped((heads, tokens, 1), F32),
        ),
        compiler_params=pltpu.CompilerParams(vmem_limit_bytes=VMEM_LIMIT),
        cost_estimate=pl.CostEstimate(
            flops=4 * tokens * width * heads * size, bytes_accessed=8 * width * heads * size,
            transcendentals=0,
        ),
    )(seg_rows, w_query, q_gain.reshape(1, size), kn, dirs, coeff, solved, val)
    near, last, whole, starts = call(
        leave_kernel,
        (
            shaped((group, tokens, size), BF16),
            square,
            shaped((size, size), F32),
            shaped((size, group * size), F32),
        ),
        ((position % group).reshape(1).astype(jnp.int32), exit_keys, turns),
        in_specs=[smem, vmem, vmem],
        flops=12 * group * size**3,
        moved=10**6,
    )
    wholes = [to_later_group(whole, d) for d in range(1, groups - 1)]
    lasts = [to_later_group(last, d) for d in range(1, groups)]
    near = within_group(near)
    far = call(
        functools.partial(arrive_kernel, groups - 1),
        shaped((group, (groups - 1) * tokens, size), BF16),
        tuple(lasts + wholes + [starts]),
        flops=6 * groups * group * size**3,
        moved=10**6,
    )
    far = within_group(far)
    most = segments // 4
    chunk = math.gcd(most, 4)
    width_out = w_out.shape[1]
    half = tokens // lax.axis_size("head")
    away, kept = call(
        functools.partial(attend_kernel, most),
        (shaped((half, width_out), BF16), shaped((half, width_out), BF16)),
        (
            jnp.stack([position, core]).astype(jnp.int32),
            block_mask[0], near, far, vals, moved, weighted, peak, total, w_out,
        ),
        in_specs=[smem] * 2 + [vmem] * 7 + [pl.BlockSpec(memory_space=pl.ANY)],
        scratch=(
            pltpu.SMEM((most,), jnp.int32),
            pltpu.VMEM((chunk * tokens, size), BF16),
            pltpu.VMEM((chunk * tokens, size), BF16),
            pltpu.VMEM((tokens, heads * size), BF16),
            pltpu.VMEM((heads, tokens, size), F32),
            pltpu.VMEM((heads, tokens, 1), F32),
            pltpu.VMEM((heads, tokens, 1), F32),
            pltpu.VMEM(w_out.shape, BF16),
            pltpu.SemaphoreType.DMA,
        ),
        flops=2 * tokens * width_out * heads * size,
        moved=4 * 10**6,
    )
    return kept + lax.ppermute(away, "head", [(0, 1), (1, 0)])


def solution(mesh):
    in_specs = (
        P(("ctx", "head"), None),
        P(None, "head"),
        P(None, "head"),
        P(None, "head"),
        P(None, "head"),
        P("head", None),
        P("head"),
        P(),
        P(),
        P("head", None),
        P("ctx", None),
    )
    out_specs = P(("ctx", "head"), None)
    return jax.shard_map(body, mesh=mesh, in_specs=in_specs, out_specs=out_specs, check_vma=False)
```

time: 203 us -> 74 us (0.36)
  waiting for transfers between devices: 57.3 us -> 8.37 us
  blocking collectives: 49.7 us -> 2.46 us
  starting transfers between devices: 0.12 us -> 33.5 us
  matrix products: 33.3 us -> 0 us
  Pallas kernels: 0 us -> 16.4 us
  between operations: 14.4 us -> 0.88 us
  local copies, waits for them, and re-layouts: 23.9 us -> 10.4 us
  other arithmetic: 12.9 us -> 0.86 us
  loops' own time: 10.3 us -> 0 us
    all_gather x2 -> x0, waiting for transfers between devices: 55.7 us -> none  [the longest x1 54.4 us: body(): products = lax.all_gather(product, 'ctx')]
    all_gather x1 -> x0, blocking collectives: 47.1 us -> none  [body(): value_blocks = lax.all_gather(value_rows, 'ctx')]
    dot_general x33 -> x0, matrix products: 32.7 us -> none  [the longest x15 16.9 us: extend(): return (jnp.dot(crossed, products[segment], precision=HIGHEST), crossed)]
    all_to_all x0 -> x4, starting transfers between devices: none -> 16.9 us  [within_group(): return lax.all_to_all(parts, 'ctx', 0, 0, axis_index_groups=members)]
    ppermute x0 -> x8, starting transfers between devices: none -> 16.6 us  [to_later_group(): lax.ppermute(value, 'ctx', [(s, s + step) for s in range(segments - step)])]
    pallas_call x0 -> x6, Pallas kernels: none -> 16.4 us  [the longest x5 10.5 us: call(): pl.pallas_call(kernel, out_shape=out_shape, in_specs=in_specs or [vmem] *...]
    another operation x1 -> x0, loops' own time: 10.3 us -> none  [body(): lax.scan(extend, jnp.eye(HD, dtype=jnp.float32), jnp.arange(segments - 1,...]
    another operation x2 -> x1, other arithmetic: 9.81 us -> 0.08 us  [body(): jnp.stack([position, core]).astype(jnp.int32)]
  transfers between devices with their start and end apart: 3 -> 13, of which waited for: 3 -> 4; matrix products, arithmetic and copies ran while one was open for 6% -> 0% of each run, Pallas kernels for 0% -> 12%
where the time goes in v2:
time: 74 us; the launch traced here: 72.9 us
  starting transfers between devices  33.5 us (45%)
  Pallas kernels  16.4 us (22%)
  local copies, waits for them, and re-layouts  10.4 us (14%)
  waiting for transfers between devices  8.37 us (11%)
  blocking collectives  2.46 us (3%)
  between operations  0.88 us (1%)
  other arithmetic  0.86 us (1%)
    all_to_all x4, starting transfers between devices, within_group(): return lax.all_to_all(parts, 'ctx', 0, 0, axis_index_groups=members)  16.9 us
    ppermute x8, starting transfers between devices, to_later_group(): lax.ppermute(value, 'ctx', [(s, s + step) for s in range(segments - step)])  16.6 us
    pallas_call x5, Pallas kernels, call(): pl.pallas_call(kernel, out_shape=out_shape, in_specs=in_specs or [vmem] *...  10.5 us
    unnamed x26, local copies, waits for them, and re-layouts  8.86 us
    pallas_call x1, Pallas kernels, body(): pl.pallas_call(query_kernel, grid=(heads // pair,), in_specs=[vmem, pl.Bl...  5.82 us
    all_to_all x4, waiting for transfers between devices, within_group(): return lax.all_to_all(parts, 'ctx', 0, 0, axis_index_groups=members)  4.98 us
    all_gather x1, blocking collectives, body(): seg_rows = lax.all_gather(hidden, 'head', axis=0, tiled=True)  2.46 us
    ppermute x8, waiting for transfers between devices, to_later_group(): lax.ppermute(value, 'ctx', [(s, s + step) for s in range(segments - step)])  1.87 us
  transfers between devices with their start and end apart: 13, of which 4 were waited for; matrix products, arithmetic and copies ran while one was open for 0% of the time, Pallas kernels for 12%

profile of v2, /device:TPU:0, one launch (start us, length us, event | category | flops | bytes accessed | tf_op | source)
XLA Modules:
  0.0 72.9 jit_solution(9716305610491315613)
XLA Ops:
  0.0 2.5 %all_gather.3.rows_ref = bf16[128,2048]{1,0:T(8,128)(2,1)S(1)} all-gather(bf16[64,2048]{1,0:T(8,128)(2,1)} %param.11), channel_id=1, replica_groups=mesh['ctx'=16,'head'=2] {'head'}, dimensions={0}, use_global_device_ids=true | all-gather | bytes 786432 | tf_op jit(solution)/shard_map/all_gather | solution.py:241
  3.1 1.0 %copy-done = bf16[2048,128]{1,0:T(8,128)(2,1)S(1)} copy-done((bf16[2048,128]{1,0:T(8,128)(2,1)S(1)}, bf16[2048,128]{1,0:T(8,128)(2,1)}, u32[]{:S(2)}) %copy-start) | copy-done | bytes 524312
  4.2 1.0 %copy-done.1 = bf16[2048,128]{1,0:T(8,128)(2,1)S(1)} copy-done((bf16[2048,128]{1,0:T(8,128)(2,1)S(1)}, bf16[2048,128]{1,0:T(8,128)(2,1)}, u32[]{:S(2)}) %copy-start.1) | copy-done | bytes 524312
  5.2 1.0 %copy-done.2 = bf16[2048,128]{1,0:T(8,128)(2,1)S(1)} copy-done((bf16[2048,128]{1,0:T(8,128)(2,1)S(1)}, bf16[2048,128]{1,0:T(8,128)(2,1)}, u32[]{:S(2)}) %copy-start.2) | copy-done | bytes 524312
  8.3 1.9 %shard_map.110 = (f32[128,128]{1,0:T(8,128)S(1)}, f32[128,128]{1,0:T(8,128)S(1)}, f32[128,128]{1,0:T(8,128)S(1)}, f32[128,128]{1,0:T(8,128)S(1)}) custom-call(f32[128,128]{1,0:T(8,128)S(1)} %get-tuple-element.23.kn_ref, f32[128,128]{1,0:T(8,128)S(1)} %get-tuple-element.24.dirs_ref, f32[128,1]{1,0:T(8,128)S(1)} %get-tuple-element.25.rates_ref), custom_call_target="tpu_custom_call" | custom-call | flops 251658240 | bytes 1000000 | tf_op jit(solution)/shard_map/pallas_call | solution.py:20
  12.8 5.1 %all-to-all-start = ((f32[4,128,128]{2,1,0:T(8,128)}), f32[4,128,128]{2,1,0:T(8,128)S(1)}, u32[]{:S(2)}, u32[]{:S(2)}) async-start(f32[4,128,128]{2,1,0:T(8,128)} %broadcast_in_dim.4), calls=%async_computation | async-start | bytes 524288 | tf_op jit(solution)/shard_map/all_to_all | solution.py:250
  17.9 3.5 %collective-permute-start.5 = (bf16[128,128]{1,0:T(8,128)(2,1)S(1)}, bf16[128,128]{1,0:T(8,128)(2,1)S(1)}, u32[]{:S(2)}, u32[]{:S(2)}) collective-permute-start(bf16[128,128]{1,0:T(8,128)(2,1)S(1)} %get-tuple-element.32.val_ref), channel_id=1, source_target_pairs={{0,8},{2,10},{4,12},{6,14},{8,16},{10,18},{12,20},{14,22},{16,24},... | collective-permute-start | bytes 98312 | tf_op jit(solution)/shard_map/ppermute | solution.py:254
  21.4 4.5 %collective-permute-start.6 = (bf16[128,128]{1,0:T(8,128)(2,1)S(1)}, bf16[128,128]{1,0:T(8,128)(2,1)S(1)}, u32[]{:S(2)}, u32[]{:S(2)}) collective-permute-start(bf16[128,128]{1,0:T(8,128)(2,1)S(1)} %get-tuple-element.32.val_ref), channel_id=1, source_target_pairs={{0,16},{2,18},{4,20},{6,22},{8,24},{10,26},{12,28},{14,30},{1,17},... | collective-permute-start | bytes 98312 | tf_op jit(solution)/shard_map/ppermute | solution.py:254
  25.9 1.3 %collective-permute-start.7 = (bf16[128,128]{1,0:T(8,128)(2,1)S(1)}, bf16[128,128]{1,0:T(8,128)(2,1)S(1)}, u32[]{:S(2)}, u32[]{:S(2)}) collective-permute-start(bf16[128,128]{1,0:T(8,128)(2,1)S(1)} %get-tuple-element.32.val_ref), channel_id=1, source_target_pairs={{0,24},{2,26},{4,28},{6,30},{1,25},{3,27},{5,29},{7,31}} | collective-permute-start | bytes 98312 | tf_op jit(solution)/shard_map/ppermute | solution.py:254
  27.2 1.1 %shard_map.111 = (bf16[4,128,128]{2,1,0:T(8,128)(2,1)}, f32[128,128]{1,0:T(8,128)S(1)}, f32[128,128]{1,0:T(8,128)S(1)}, f32[128,512]{1,0:T(8,128)S(1)}) custom-call(s32[1]{0:T(128)} %bitcast.3.member_ref, f32[128,128]{1,0:T(8,128)S(1)} %get-tuple-element.26.exit_ref, f32[4,128,128]{2,1,0:T(8,128)S(1)} %all-to-all-done.turns_ref), custom_call_target="tpu_custom_call" | custom-call | flops 100663296 | bytes 1000000 | tf_op jit(solution)/shard_map/pallas_call | solution.py:20
  28.3 4.2 %all-to-all-start.1 = ((bf16[4,128,128]{2,1,0:T(8,128)(2,1)}), bf16[4,128,128]{2,1,0:T(8,128)(2,1)S(1)}, u32[]{:S(2)}, u32[]{:S(2)}) async-start(bf16[4,128,128]{2,1,0:T(8,128)(2,1)} %get-tuple-element.28), calls=%async_computation.1 | async-start | bytes 262144 | tf_op jit(solution)/shard_map/all_to_all | solution.py:250
  32.6 5.0 %all-to-all-done.1.near_ref = bf16[4,128,128]{2,1,0:T(8,128)(2,1)S(1)} async-done(((bf16[4,128,128]{2,1,0:T(8,128)(2,1)}), bf16[4,128,128]{2,1,0:T(8,128)(2,1)S(1)}, u32[]{:S(2)}, u32[]{:S(2)}) %all-to-all-start.1) | async-done | bytes 131104 | tf_op jit(solution)/shard_map/all_to_all | solution.py:250
  38.4 3.5 %all-to-all-start.3 = ((bf16[4,512,128]{2,1,0:T(8,128)(2,1)}), bf16[4,512,128]{2,1,0:T(8,128)(2,1)S(1)}, u32[]{:S(2)}, u32[]{:S(2)}) async-start(bf16[4,512,128]{2,1,0:T(8,128)(2,1)} %broadcast_in_dim.5), calls=%async_computation.3 | async-start | bytes 1048576 | tf_op jit(solution)/shard_map/all_to_all | solution.py:250
  41.9 1.3 %collective-permute-start = (f32[128,128]{1,0:T(8,128)S(1)}, f32[128,128]{1,0:T(8,128)S(1)}, u32[]{:S(2)}, u32[]{:S(2)}) collective-permute-start(f32[128,128]{1,0:T(8,128)S(1)} %get-tuple-element.29), channel_id=1, source_target_pairs={{0,8},{2,10},{4,12},{6,14},{8,16},{10,18},{12,20},{14,22},{16,24},... | collective-permute-start | bytes 196616 | tf_op jit(solution)/shard_map/ppermute | solution.py:254
  43.2 2.1 %collective-permute-start.1 = (f32[128,128]{1,0:T(8,128)S(1)}, f32[128,128]{1,0:T(8,128)S(1)}, u32[]{:S(2)}, u32[]{:S(2)}) collective-permute-start(f32[128,128]{1,0:T(8,128)S(1)} %get-tuple-element.29), channel_id=1, source_target_pairs={{0,16},{2,18},{4,20},{6,22},{8,24},{10,26},{12,28},{14,30},{1,17},... | collective-permute-start | bytes 196616 | tf_op jit(solution)/shard_map/ppermute | solution.py:254
  45.4 1.3 %collective-permute-start.2 = (f32[128,128]{1,0:T(8,128)S(1)}, f32[128,128]{1,0:T(8,128)S(1)}, u32[]{:S(2)}, u32[]{:S(2)}) collective-permute-start(f32[128,128]{1,0:T(8,128)S(1)} %get-tuple-element.29), channel_id=1, source_target_pairs={{0,24},{2,26},{4,28},{6,30},{1,25},{3,27},{5,29},{7,31}} | collective-permute-start | bytes 196616 | tf_op jit(solution)/shard_map/ppermute | solution.py:254
  46.7 1.3 %collective-permute-start.3 = (f32[128,128]{1,0:T(8,128)S(1)}, f32[128,128]{1,0:T(8,128)S(1)}, u32[]{:S(2)}, u32[]{:S(2)}) collective-permute-start(f32[128,128]{1,0:T(8,128)S(1)} %get-tuple-element.30), channel_id=1, source_target_pairs={{0,8},{2,10},{4,12},{6,14},{8,16},{10,18},{12,20},{14,22},{16,24},... | collective-permute-start | bytes 196616 | tf_op jit(solution)/shard_map/ppermute | solution.py:254
  48.0 1.3 %collective-permute-start.4 = (f32[128,128]{1,0:T(8,128)S(1)}, f32[128,128]{1,0:T(8,128)S(1)}, u32[]{:S(2)}, u32[]{:S(2)}) collective-permute-start(f32[128,128]{1,0:T(8,128)S(1)} %get-tuple-element.30), channel_id=1, source_target_pairs={{0,16},{2,18},{4,20},{6,22},{8,24},{10,26},{12,28},{14,30},{1,17},... | collective-permute-start | bytes 196616 | tf_op jit(solution)/shard_map/ppermute | solution.py:254
  49.8 1.3 %collective-permute-done.4.refs_4_ = f32[128,128]{1,0:T(8,128)S(1)} collective-permute-done((f32[128,128]{1,0:T(8,128)S(1)}, f32[128,128]{1,0:T(8,128)S(1)}, u32[]{:S(2)}, u32[]{:S(2)}) %collective-permute-start.4) | collective-permute-done | bytes 65568 | tf_op jit(solution)/shard_map/ppermute | solution.py:254
  51.1 1.5 %shard_map.112 = bf16[4,384,128]{2,1,0:T(8,128)(2,1)} custom-call(f32[128,128]{1,0:T(8,128)S(1)} %collective-permute-done.refs_0_, f32[128,128]{1,0:T(8,128)S(1)} %collective-permute-done.1.refs_1_, f32[128,128]{1,0:T(8,128)S(1)} %collective-permute-done.2.refs_2_, f32[128,128]{1,0:T(8,128)S(1)} %collective-permute-done.3.refs_3_, ...), custom_call_target="tpu_custom_call" | custom-call | flops 201326592 | bytes 1000000 | tf_op jit(solution)/shard_map/pallas_call | solution.py:20
  52.6 4.1 %all-to-all-start.2 = ((bf16[4,384,128]{2,1,0:T(8,128)(2,1)}), bf16[4,384,128]{2,1,0:T(8,128)(2,1)S(1)}, u32[]{:S(2)}, u32[]{:S(2)}) async-start(bf16[4,384,128]{2,1,0:T(8,128)(2,1)} %shard_map.112), calls=%async_computation.2 | async-start | bytes 786432 | tf_op jit(solution)/shard_map/all_to_all | solution.py:250
  59.3 5.8 %shard_map.113 = (bf16[8,128,128]{2,1,0:T(8,128)(2,1)S(1)}, f32[8,128,128]{2,1,0:T(8,128)S(1)}, f32[8,128,1]{2,1,0:T(8,128)S(1)}, f32[8,128,1]{2,1,0:T(8,128)S(1)}) custom-call(bf16[128,2048]{1,0:T(8,128)(2,1)S(1)} %all_gather.3.rows_ref, bf16[2048,1024]{1,0:T(8,128)(2,1)} %weight_ref.1, f32[1,128]{1,0:T(1,128)S(1)} %bitcast.7, ...), custom_call_target="tpu_custom_call" | custom-call | flops 1073741824 | bytes 16777216 | tf_op jit(solution)/shard_map/pallas_call | solution.py:274
  65.2 5.3 %shard_map.114 = (bf16[64,2048]{1,0:T(8,128)(2,1)S(1)}, bf16[64,2048]{1,0:T(8,128)(2,1)S(1)}) custom-call(s32[2]{0:T(128)S(1)} %pad_add_fusion.position_ref, s32[16]{0:T(128)S(1)} %bitcast.8, bf16[4,128,128]{2,1,0:T(8,128)(2,1)S(1)} %all-to-all-done.1.near_ref, bf16[4,384,128]{2,1,0:T(8,128)(2,1)S(1)} %all-to-all-done.2.far_ref, ...), custom_call_target="tpu_custom_call" | custom-call | flops 536870912 | bytes 4000000 | tf_op jit(solution)/shard_map/pallas_call | solution.py:20
  70.6 1.5 %collective-permute-done.8 = bf16[64,2048]{1,0:T(8,128)(2,1)S(1)} collective-permute-done((bf16[64,2048]{1,0:T(8,128)(2,1)S(1)}, bf16[64,2048]{1,0:T(8,128)(2,1)S(1)}, u32[]{:S(2)}, u32[]{:S(2)}) %collective-permute-start.8) | collective-permute-done | bytes 262176 | tf_op jit(solution)/shard_map/ppermute | solution.py:341
  (40 shorter events, 9.5 us)
Async XLA Ops:
  2.5 54.3 %copy-start.11 = (f32[128]{0:T(128)S(1)}, f32[128]{0:T(128)}, u32[]{:S(2)}) copy-start(f32[128]{0:T(128)} %param.18) | copy-start | bytes 1540
  3.1 1.0 %copy-start = (bf16[2048,128]{1,0:T(8,128)(2,1)S(1)}, bf16[2048,128]{1,0:T(8,128)(2,1)}, u32[]{:S(2)}) copy-start(bf16[2048,128]{1,0:T(8,128)(2,1)} %key_ref.1) | copy-start | bytes 1572868
  4.2 1.0 %copy-start.1 = (bf16[2048,128]{1,0:T(8,128)(2,1)S(1)}, bf16[2048,128]{1,0:T(8,128)(2,1)}, u32[]{:S(2)}) copy-start(bf16[2048,128]{1,0:T(8,128)(2,1)} %value_ref.1) | copy-start | bytes 1572868
  5.2 1.0 %copy-start.2 = (bf16[2048,128]{1,0:T(8,128)(2,1)S(1)}, bf16[2048,128]{1,0:T(8,128)(2,1)}, u32[]{:S(2)}) copy-start(bf16[2048,128]{1,0:T(8,128)(2,1)} %dir_ref.1) | copy-start | bytes 1572868
  6.3 0.7 copy-start.9
  7.0 0.7 copy-start.10
  10.2 0.6 copy-start.3
  12.8 14.4 %all-to-all-start = ((f32[4,128,128]{2,1,0:T(8,128)}), f32[4,128,128]{2,1,0:T(8,128)S(1)}, u32[]{:S(2)}, u32[]{:S(2)}) async-start(f32[4,128,128]{2,1,0:T(8,128)} %broadcast_in_dim.4), calls=%async_computation | async-start | bytes 524288 | tf_op jit(solution)/shard_map/all_to_all | solution.py:250
  17.9 14.6 %collective-permute-start.5 = (bf16[128,128]{1,0:T(8,128)(2,1)S(1)}, bf16[128,128]{1,0:T(8,128)(2,1)S(1)}, u32[]{:S(2)}, u32[]{:S(2)}) collective-permute-start(bf16[128,128]{1,0:T(8,128)(2,1)S(1)} %get-tuple-element.32.val_ref), channel_id=1, source_target_pairs={{0,8},{2,10},{4,12},{6,14},{8,16},{10,18},{12,20},{14,22},{16,24},... | collective-permute-start | bytes 98312 | tf_op jit(solution)/shard_map/ppermute | solution.py:254
  21.4 11.1 %collective-permute-start.6 = (bf16[128,128]{1,0:T(8,128)(2,1)S(1)}, bf16[128,128]{1,0:T(8,128)(2,1)S(1)}, u32[]{:S(2)}, u32[]{:S(2)}) collective-permute-start(bf16[128,128]{1,0:T(8,128)(2,1)S(1)} %get-tuple-element.32.val_ref), channel_id=1, source_target_pairs={{0,16},{2,18},{4,20},{6,22},{8,24},{10,26},{12,28},{14,30},{1,17},... | collective-permute-start | bytes 98312 | tf_op jit(solution)/shard_map/ppermute | solution.py:254
  25.9 6.6 %collective-permute-start.7 = (bf16[128,128]{1,0:T(8,128)(2,1)S(1)}, bf16[128,128]{1,0:T(8,128)(2,1)S(1)}, u32[]{:S(2)}, u32[]{:S(2)}) collective-permute-start(bf16[128,128]{1,0:T(8,128)(2,1)S(1)} %get-tuple-element.32.val_ref), channel_id=1, source_target_pairs={{0,24},{2,26},{4,28},{6,30},{1,25},{3,27},{5,29},{7,31}} | collective-permute-start | bytes 98312 | tf_op jit(solution)/shard_map/ppermute | solution.py:254
  28.3 9.2 %all-to-all-start.1 = ((bf16[4,128,128]{2,1,0:T(8,128)(2,1)}), bf16[4,128,128]{2,1,0:T(8,128)(2,1)S(1)}, u32[]{:S(2)}, u32[]{:S(2)}) async-start(bf16[4,128,128]{2,1,0:T(8,128)(2,1)} %get-tuple-element.28), calls=%async_computation.1 | async-start | bytes 262144 | tf_op jit(solution)/shard_map/all_to_all | solution.py:250
  32.6 32.6 %copy-start.12 = (s32[1,16]{1,0:T(1,128)S(1)}, s32[1,16]{1,0:T(1,128)}, u32[]{:S(2)}) copy-start(s32[1,16]{1,0:T(1,128)} %param.21) | copy-start | bytes 196
  38.4 14.2 %all-to-all-start.3 = ((bf16[4,512,128]{2,1,0:T(8,128)(2,1)}), bf16[4,512,128]{2,1,0:T(8,128)(2,1)S(1)}, u32[]{:S(2)}, u32[]{:S(2)}) async-start(bf16[4,512,128]{2,1,0:T(8,128)(2,1)} %broadcast_in_dim.5), calls=%async_computation.3 | async-start | bytes 1048576 | tf_op jit(solution)/shard_map/all_to_all | solution.py:250
  41.9 7.4 %collective-permute-start = (f32[128,128]{1,0:T(8,128)S(1)}, f32[128,128]{1,0:T(8,128)S(1)}, u32[]{:S(2)}, u32[]{:S(2)}) collective-permute-start(f32[128,128]{1,0:T(8,128)S(1)} %get-tuple-element.29), channel_id=1, source_target_pairs={{0,8},{2,10},{4,12},{6,14},{8,16},{10,18},{12,20},{14,22},{16,24},... | collective-permute-start | bytes 196616 | tf_op jit(solution)/shard_map/ppermute | solution.py:254
  43.2 6.1 %collective-permute-start.1 = (f32[128,128]{1,0:T(8,128)S(1)}, f32[128,128]{1,0:T(8,128)S(1)}, u32[]{:S(2)}, u32[]{:S(2)}) collective-permute-start(f32[128,128]{1,0:T(8,128)S(1)} %get-tuple-element.29), channel_id=1, source_target_pairs={{0,16},{2,18},{4,20},{6,22},{8,24},{10,26},{12,28},{14,30},{1,17},... | collective-permute-start | bytes 196616 | tf_op jit(solution)/shard_map/ppermute | solution.py:254
  45.4 3.9 %collective-permute-start.2 = (f32[128,128]{1,0:T(8,128)S(1)}, f32[128,128]{1,0:T(8,128)S(1)}, u32[]{:S(2)}, u32[]{:S(2)}) collective-permute-start(f32[128,128]{1,0:T(8,128)S(1)} %get-tuple-element.29), channel_id=1, source_target_pairs={{0,24},{2,26},{4,28},{6,30},{1,25},{3,27},{5,29},{7,31}} | collective-permute-start | bytes 196616 | tf_op jit(solution)/shard_map/ppermute | solution.py:254
  46.7 3.2 %collective-permute-start.3 = (f32[128,128]{1,0:T(8,128)S(1)}, f32[128,128]{1,0:T(8,128)S(1)}, u32[]{:S(2)}, u32[]{:S(2)}) collective-permute-start(f32[128,128]{1,0:T(8,128)S(1)} %get-tuple-element.30), channel_id=1, source_target_pairs={{0,8},{2,10},{4,12},{6,14},{8,16},{10,18},{12,20},{14,22},{16,24},... | collective-permute-start | bytes 196616 | tf_op jit(solution)/shard_map/ppermute | solution.py:254
  48.0 3.2 %collective-permute-start.4 = (f32[128,128]{1,0:T(8,128)S(1)}, f32[128,128]{1,0:T(8,128)S(1)}, u32[]{:S(2)}, u32[]{:S(2)}) collective-permute-start(f32[128,128]{1,0:T(8,128)S(1)} %get-tuple-element.30), channel_id=1, source_target_pairs={{0,16},{2,18},{4,20},{6,22},{8,24},{10,26},{12,28},{14,30},{1,17},... | collective-permute-start | bytes 196616 | tf_op jit(solution)/shard_map/ppermute | solution.py:254
  52.6 12.6 %all-to-all-start.2 = ((bf16[4,384,128]{2,1,0:T(8,128)(2,1)}), bf16[4,384,128]{2,1,0:T(8,128)(2,1)S(1)}, u32[]{:S(2)}, u32[]{:S(2)}) async-start(bf16[4,384,128]{2,1,0:T(8,128)(2,1)} %shard_map.112), calls=%async_computation.2 | async-start | bytes 786432 | tf_op jit(solution)/shard_map/all_to_all | solution.py:250
  56.8 0.8 %copy-start.4 = (f32[128,128]{1,0:T(8,128)S(1)}, f32[128,128]{1,0:T(8,128)}, u32[]{:S(2)}) copy-start(f32[128,128]{1,0:T(8,128)} %copy-done.3) | copy-start | bytes 196612
  57.6 0.8 %copy-start.6 = (f32[128,128]{1,0:T(8,128)S(1)}, f32[128,128]{1,0:T(8,128)}, u32[]{:S(2)}) copy-start(f32[128,128]{1,0:T(8,128)} %copy-done.5) | copy-start | bytes 196612
  58.5 0.8 %copy-start.8 = (f32[128,128]{1,0:T(8,128)S(1)}, f32[128,128]{1,0:T(8,128)}, u32[]{:S(2)}) copy-start(f32[128,128]{1,0:T(8,128)} %copy-done.7) | copy-start | bytes 196612
  70.5 1.6 %collective-permute-start.8 = (bf16[64,2048]{1,0:T(8,128)(2,1)S(1)}, bf16[64,2048]{1,0:T(8,128)(2,1)S(1)}, u32[]{:S(2)}, u32[]{:S(2)}) collective-permute-start(bf16[64,2048]{1,0:T(8,128)(2,1)S(1)} %get-tuple-element.40), channel_id=1, source_target_pairs={{0,1},{1,0},{2,3},{3,2},{4,5},{5,4},{6,7},{7,6},{8,9},{9,8},{10,11... | collective-permute-start | bytes 786440 | tf_op jit(solution)/shard_map/ppermute | solution.py:341
  (2 other events, 1.2 us)

commit v3 on v2

v3 whole, which is shorter than its diff:
```python
import functools
import math

import jax
import jax.numpy as jnp
from jax import lax
from jax.experimental import pallas as pl
from jax.experimental.pallas import tpu as pltpu
from jax.sharding import PartitionSpec as P

EPSILON = 1e-06
NEGATIVE = -1e30
F32 = jnp.float32
BF16 = jnp.bfloat16
MIB = 1024 * 1024


def call(kernel, out_shape, args, in_specs=None, scratch=(), flops=0, moved=0, limit=6):
    vmem = pl.BlockSpec(memory_space=pltpu.VMEM)
    return pl.pallas_call(
        kernel,
        out_shape=out_shape,
        in_specs=in_specs or [vmem] * len(args),
        out_specs=jax.tree.map(lambda _: vmem, out_shape),
        scratch_shapes=list(scratch),
        compiler_params=pltpu.CompilerParams(vmem_limit_bytes=limit * MIB),
        cost_estimate=pl.CostEstimate(flops=flops, bytes_accessed=moved, transcendentals=0),
    )(*args)


def shaped(shape, dtype):
    return jax.ShapeDtypeStruct(shape, dtype)


def split(value):
    high = value.astype(BF16)
    return high, (value - high.astype(F32)).astype(BF16)


def dot3(left, right, left_dim=1, right_dim=0):
    left_high, left_low = split(left)
    right_high, right_low = split(right)
    return lax.dot_general(
        jnp.concatenate([left_high, left_high, left_low], axis=left_dim),
        jnp.concatenate([right_high, right_low, right_high], axis=right_dim),
        (((left_dim,), (right_dim,)), ((), ())),
        preferred_element_type=F32,
    )


def iota2(shape):
    return lax.broadcasted_iota(jnp.int32, shape, 0), lax.broadcasted_iota(jnp.int32, shape, 1)


def merge_inverse(lower, rows, cols):
    tokens = lower.shape[0]
    block = 8
    inverse = jnp.where(rows == cols, 1.0, 0.0).astype(F32)
    first = rows - rows % block
    for step in range(block - 1):
        column = jnp.sum(jnp.where(cols == first + step, lower, 0.0), axis=1, keepdims=True)
        pivot = inverse.reshape(tokens // block, block, tokens)[:, step : step + 1, :]
        pivot = jnp.broadcast_to(pivot, (tokens // block, block, tokens)).reshape(tokens, tokens)
        inverse = inverse - column * pivot
    while block < tokens:
        corner = (
            (rows // (2 * block) == cols // (2 * block))
            & (rows % (2 * block) >= block)
            & (cols % (2 * block) < block)
        )
        inverse = inverse - dot3(dot3(inverse, jnp.where(corner, lower, 0.0)), inverse)
        block *= 2
    return inverse


def prepare_kernel(core_ref, mine_ref, other_ref, key_ref, value_ref, dir_ref, rate_ref, bias_ref,
                   gain_ref, rows_ref, kn_ref, val_ref, dirs_ref, coeff_ref, solved_ref, exit_ref,
                   turns_ref):
    core = core_ref[0]
    half = mine_ref.shape[0]
    rows_ref[pl.ds(pl.multiple_of(core * half, half), half), :] = mine_ref[...]
    rows_ref[pl.ds(pl.multiple_of((1 - core) * half, half), half), :] = other_ref[...]
    seg = rows_ref[...]
    keys = jnp.dot(seg, key_ref[...], preferred_element_type=F32)
    kn = keys * lax.rsqrt(jnp.mean(keys * keys, axis=-1, keepdims=True) + EPSILON) * gain_ref[...]
    raw = jnp.dot(seg, dir_ref[...], preferred_element_type=F32)
    dirs = raw * lax.rsqrt(jnp.sum(raw * raw, axis=-1, keepdims=True) + EPSILON)
    vector = jnp.broadcast_to(rate_ref[...], (16, seg.shape[1]))
    logits = lax.dot_general(seg, vector, (((1,), (1,)), ((), ())), preferred_element_type=F32)
    rates = 2.0 * jax.nn.sigmoid(logits[:, :1] + bias_ref[0])
    val_ref[...] = jnp.dot(seg, value_ref[...], preferred_element_type=F32).astype(BF16)
    kn_ref[...] = kn
    dirs_ref[...] = dirs
    tokens, size = dirs.shape
    rows, cols = iota2((tokens, tokens))
    below = rows > cols
    grams = dot3(dirs, jnp.concatenate([dirs, kn], axis=0), 1, 1)
    lower = jnp.where(below, rates * grams[:, :tokens], 0.0)
    crossing = jnp.where(below, rates * grams[:, tokens:], 0.0)
    inverse = merge_inverse(lower, rows, cols)
    both = dot3(inverse, jnp.concatenate([crossing, rates * dirs], axis=1))
    coeff_ref[...] = both[:, :tokens]
    solved_ref[...] = both[:, tokens:]
    crossed = dot3(both, dirs, 0, 0)
    exit_ref[...] = kn - crossed[:tokens]
    heads, lanes = iota2((size, size))
    turn = jnp.where(heads == lanes, 1.0, 0.0) - crossed[tokens:]
    for member in range(turns_ref.shape[0]):
        turns_ref[member] = turn


def leave_kernel(member_ref, exit_ref, val_ref, turns_ref, long_ref, short_ref, starts_ref):
    member = member_ref[0]
    tokens, size = exit_ref.shape
    group = turns_ref.shape[0]
    own = exit_ref[...]
    keys = own
    product = None
    heads, lanes = iota2((size, size))
    starts_ref[:, :size] = jnp.where(heads == lanes, 1.0, 0.0)
    for index in range(group):
        turn = turns_ref[index]
        product = turn if product is None else dot3(product, turn)
        if index:
            keys = jnp.where(index > member, dot3(keys, turn), own)
        if index < group - 1:
            starts_ref[:, (index + 1) * size : (index + 2) * size] = product
    high, low = split(keys)
    for ref in (long_ref, short_ref):
        ref[:tokens] = high
        ref[tokens : 2 * tokens] = low
        ref[2 * tokens : 3 * tokens] = val_ref[...]
    high, low = split(product)
    long_ref[3 * tokens : 3 * tokens + size] = high
    long_ref[3 * tokens + size :] = low


def query_kernel(member_ref, rows_ref, weight_ref, gain_ref, kn_ref, dirs_ref, coeff_ref,
                 solved_ref, val_ref, exit_ref, turns_ref, after_ref,
                 moved_ref, weighted_ref, peak_ref, total_ref, near_ref):
    tokens, size = kn_ref.shape
    heads = moved_ref.shape[0]

    @pl.when(pl.program_id(0) == 0)
    def _():
        member = member_ref[0]
        keys = exit_ref[...]
        for index in range(near_ref.shape[0]):
            if index > 1:
                keys = jnp.where(index - 1 > member, dot3(keys, turns_ref[index - 1]), exit_ref[...])
            near_ref[index, :tokens] = keys.astype(BF16)
            near_ref[index, tokens:] = val_ref[...]

    raw = jnp.dot(rows_ref[...], weight_ref[...], preferred_element_type=F32)
    raw = jnp.concatenate([raw[:, h * size : (h + 1) * size] for h in range(heads)], axis=0)
    queries = raw * lax.rsqrt(jnp.mean(raw * raw, axis=-1, keepdims=True) + EPSILON) * gain_ref[...]
    seen = dot3(queries, jnp.concatenate([kn_ref[...], dirs_ref[...]], axis=0), 1, 1)
    rows, cols = iota2((heads * tokens, tokens))
    up_to = rows % tokens >= cols
    reach = jnp.where(up_to, seen[:, tokens:], 0.0)
    taken = dot3(reach, jnp.concatenate([coeff_ref[...], solved_ref[...]], axis=1))
    scores = (seen[:, :tokens] - taken[:, :tokens]) * (1.0 / math.sqrt(size))
    scores = jnp.where(up_to, scores, NEGATIVE)
    moved = (queries - taken[:, tokens:]).astype(BF16)
    peak = jnp.max(scores, axis=1, keepdims=True)
    weights = jnp.exp(scores - peak)
    total = jnp.sum(weights, axis=1, keepdims=True)
    weighted = jnp.dot(weights.astype(BF16), val_ref[...], preferred_element_type=F32)
    for h in range(heads):
        part = slice(h * tokens, (h + 1) * tokens)
        moved_ref[h] = moved[part]
        weighted_ref[h] = weighted[part]
        peak_ref[h] = peak[part]
        total_ref[h] = total[part]


def arrive_kernel(count, tokens, *refs):
    arrived, starts_ref, far_ref = refs[:count], refs[count], refs[-1]
    size = starts_ref.shape[0]
    product = None
    brought = []
    for index in range(count):
        ref = arrived[index]
        keys = ref[:tokens].astype(F32) + ref[tokens : 2 * tokens].astype(F32)
        if index:
            before = arrived[index - 1]
            whole = before[3 * tokens : 3 * tokens + size].astype(F32)
            whole = whole + before[3 * tokens + size :].astype(F32)
            product = whole if product is None else dot3(whole, product)
            keys = dot3(keys, product)
        brought.append(keys)
    keys = jnp.concatenate(brought, axis=0)
    split_at = count * tokens
    for member in range(far_ref.shape[0]):
        start = starts_ref[:, member * size : (member + 1) * size]
        far_ref[member, :split_at] = (dot3(keys, start) if member else keys).astype(BF16)
        for index in range(count):
            far_ref[member, split_at + index * tokens : split_at + (index + 1) * tokens] = arrived[
                index
            ][2 * tokens : 3 * tokens]


def attend_kernel(most, position_ref, mask_ref, near_ref, far_ref, moved_ref, weighted_ref, peak_ref,
                  total_ref, out_hbm, away_ref, kept_ref,
                  chosen_ref, keys_ref, vals_ref, attended_ref, run_w, run_p, run_t, out_ref, out_sem):
    out_copy = pltpu.make_async_copy(out_hbm, out_ref, out_sem)
    out_copy.start()
    place, core = position_ref[0], position_ref[1]
    group = near_ref.shape[0]
    heads, tokens, size = moved_ref.shape
    segments = mask_ref.shape[0]
    scaling = 1.0 / math.sqrt(size)
    mine, member = place // group, place % group

    def pick(segment, count):
        @pl.when((mask_ref[segment] > 0) & (segment < place) & (count < most))
        def _():
            chosen_ref[count] = segment

        return count + ((mask_ref[segment] > 0) & (segment < place)).astype(jnp.int32)

    for slot in range(most):
        chosen_ref[slot] = 0
    found = lax.fori_loop(0, segments, pick, jnp.int32(0))
    chunk = keys_ref.shape[0] // tokens
    run_w[...] = weighted_ref[...]
    run_p[...] = peak_ref[...]
    run_t[...] = total_ref[...]
    lanes = lax.broadcasted_iota(jnp.int32, (tokens, chunk * tokens), 1)

    @pl.loop(0, most // chunk)
    def _(turn):
        for slot in range(chunk):
            segment = chosen_ref[turn * chunk + slot]
            whose, distance = segment % group, mine - segment // group
            before = jnp.maximum(distance - 1, 0) * tokens
            part = slice(slot * tokens, (slot + 1) * tokens)
            for ref, at, offset in ((keys_ref, 0, 0), (vals_ref, tokens, far_ref.shape[1] // 2)):
                far = far_ref[whose, pl.ds(pl.multiple_of(offset + before, tokens), tokens), :]
                ref[part, :] = jnp.where(distance > 0, far, near_ref[whose, at : at + tokens, :])
        keep = lanes < (found - turn * chunk) * tokens
        keys, vals = keys_ref[...], vals_ref[...]
        for head in range(heads):
            scores = lax.dot_general(
                moved_ref[head], keys, (((1,), (1,)), ((), ())), preferred_element_type=F32
            )
            scores = jnp.where(keep, scores * scaling, NEGATIVE)
            peak = run_p[head]
            new_peak = jnp.maximum(peak, jnp.max(scores, axis=1, keepdims=True))
            fading = jnp.exp(peak - new_peak)
            weights = jnp.exp(scores - new_peak)
            run_p[head] = new_peak
            run_t[head] = run_t[head] * fading + jnp.sum(weights, axis=1, keepdims=True)
            run_w[head] = run_w[head] * fading + jnp.dot(
                weights.astype(BF16), vals, preferred_element_type=F32
            )

    half = kept_ref.shape[0]
    for head in range(heads):
        done = (run_w[head] / run_t[head]).astype(BF16)
        for index in range(tokens // half):
            at = jnp.where(index == core, half, 0)
            attended_ref[pl.ds(pl.multiple_of(at, half), half), head * size : (head + 1) * size] = (
                done[index * half : (index + 1) * half]
            )
    out_copy.wait()
    result = jnp.dot(attended_ref[...], out_ref[...], preferred_element_type=F32).astype(BF16)
    away_ref[...] = result[:half]
    kept_ref[...] = result[half:]


def body(
    hidden, w_query, w_key, w_value, w_dir, u_rate, rate_bias, q_gain, k_gain, w_out, block_mask
):
    segments = lax.axis_size("ctx")
    position = lax.axis_index("ctx")
    core = lax.axis_index("head")
    group = max(d for d in range(1, math.isqrt(segments) + 1) if segments % d == 0)
    groups = segments // group
    members = [[g * group + m for m in range(group)] for g in range(groups)]
    other = lax.ppermute(hidden, "head", [(0, 1), (1, 0)])
    half, width = hidden.shape
    tokens = half * lax.axis_size("head")
    size = w_key.shape[1]
    heads = w_query.shape[1] // size
    smem = pl.BlockSpec(memory_space=pltpu.SMEM)
    vmem = pl.BlockSpec(memory_space=pltpu.VMEM)
    anywhere = pl.BlockSpec(memory_space=pl.ANY)
    square = shaped((tokens, size), F32)
    member = (position % group).reshape(1).astype(jnp.int32)

    def within_group(parts):
        return lax.all_to_all(parts, "ctx", 0, 0, axis_index_groups=members)

    def to_later_group(value, distance):
        step = distance * group
        return lax.ppermute(value, "ctx", [(s, s + step) for s in range(segments - step)])

    rows, kn, val, dirs, coeff, solved, exit_keys, turns = call(
        prepare_kernel,
        (
            shaped((tokens, width), BF16), square, shaped((tokens, size), BF16), square, square,
            square, square, shaped((group, size, size), F32),
        ),
        (
            core.reshape(1).astype(jnp.int32), hidden, other, w_key, w_value, w_dir, u_rate,
            rate_bias, k_gain.reshape(1, size),
        ),
        in_specs=[smem] + [vmem] * 6 + [smem, vmem],
        flops=6 * tokens * width * size,
        moved=8 * width * size,
    )
    turns = within_group(turns)
    long, short, starts = call(
        leave_kernel,
        (
            shaped((3 * tokens + 2 * size, size), BF16),
            shaped((3 * tokens, size), BF16),
            shaped((size, group * size), F32),
        ),
        (member, exit_keys, val, turns),
        in_specs=[smem, vmem, vmem, vmem],
        flops=12 * group * size**3,
        moved=10**6,
    )
    arrived = [
        to_later_group(long if d < groups - 1 else short, d) for d in range(1, groups)
    ]
    pair = math.gcd(heads, 2)
    blocks = pl.BlockSpec((pair, tokens, size), lambda i: (i, 0, 0))
    thin = pl.BlockSpec((pair, tokens, 1), lambda i: (i, 0, 0))
    moved, weighted, peak, total, near = pl.pallas_call(
        query_kernel,
        grid=(heads // pair,),
        in_specs=[smem, vmem, pl.BlockSpec((width, pair * size), lambda i: (0, i))]
        + [vmem] * 8
        + [anywhere],
        out_specs=(
            blocks, blocks, thin, thin,
            pl.BlockSpec((group, 2 * tokens, size), lambda i: (0, 0, 0)),
        ),
        out_shape=(
            shaped((heads, tokens, size), BF16),
            shaped((heads, tokens, size), F32),
            shaped((heads, tokens, 1), F32),
            shaped((heads, tokens, 1), F32),
            shaped((group, 2 * tokens, size), BF16),
        ),
        compiler_params=pltpu.CompilerParams(vmem_limit_bytes=12 * MIB),
        cost_estimate=pl.CostEstimate(
            flops=4 * tokens * width * heads * size, bytes_accessed=8 * width * heads * size,
            transcendentals=0,
        ),
    )(
        member, rows, w_query, q_gain.reshape(1, size), kn, dirs, coeff, solved, val, exit_keys,
        turns, starts,
    )
    near = within_group(near)
    far = call(
        functools.partial(arrive_kernel, groups - 1, tokens),
        shaped((group, 2 * (groups - 1) * tokens, size), BF16),
        tuple(arrived + [starts, peak]),
        in_specs=[vmem] * groups + [anywhere],
        flops=6 * groups * group * size**3,
        moved=10**6,
        limit=8 + group * groups // 4,
    )
    far = within_group(far)
    most = segments // 4
    chunk = math.gcd(most, 4)
    width_out = w_out.shape[1]
    away, kept = call(
        functools.partial(attend_kernel, most),
        (shaped((half, width_out), BF16), shaped((half, width_out), BF16)),
        (
            jnp.stack([position, core]).astype(jnp.int32),
            block_mask[0], near, far, moved, weighted, peak, total, w_out,
        ),
        in_specs=[smem] * 2 + [vmem] * 6 + [anywhere],
        scratch=(
            pltpu.SMEM((most,), jnp.int32),
            pltpu.VMEM((chunk * tokens, size), BF16),
            pltpu.VMEM((chunk * tokens, size), BF16),
            pltpu.VMEM((tokens, heads * size), BF16),
            pltpu.VMEM((heads, tokens, size), F32),
            pltpu.VMEM((heads, tokens, 1), F32),
            pltpu.VMEM((heads, tokens, 1), F32),
            pltpu.VMEM(w_out.shape, BF16),
            pltpu.SemaphoreType.DMA,
        ),
        flops=2 * tokens * width_out * heads * size,
        moved=4 * 10**6,
        limit=14 + group * groups // 4,
    )
    return kept + lax.ppermute(away, "head", [(0, 1), (1, 0)])


def solution(mesh):
    in_specs = (
        P(("ctx", "head"), None),
        P(None, "head"),
        P(None, "head"),
        P(None, "head"),
        P(None, "head"),
        P("head", None),
        P("head"),
        P(),
        P(),
        P("head", None),
        P("ctx", None),
    )
    out_specs = P(("ctx", "head"), None)
    return jax.shard_map(body, mesh=mesh, in_specs=in_specs, out_specs=out_specs, check_vma=False)
```

time: 74 us -> 73.9 us (level)
  the two profiles are of different devices: /device:TPU:0 before, /device:TPU:25 now
where the time goes in v3:
time: 73.9 us; the launch traced here: 73.2 us
  waiting for transfers between devices  27.8 us (38%)
  starting transfers between devices  17.4 us (24%)
  Pallas kernels  16 us (22%)
  local copies, waits for them, and re-layouts  10.5 us (14%)
  other arithmetic  0.85 us (1%)
    all_to_all x3, waiting for transfers between devices, within_group(): return lax.all_to_all(parts, 'ctx', 0, 0, axis_index_groups=members)  13.8 us
    ppermute x3, waiting for transfers between devices, to_later_group(): lax.ppermute(value, 'ctx', [(s, s + step) for s in range(segments - step)])  12 us
    unnamed x20, local copies, waits for them, and re-layouts  10.5 us
    all_to_all x3, starting transfers between devices, within_group(): return lax.all_to_all(parts, 'ctx', 0, 0, axis_index_groups=members)  10.3 us
    pallas_call x4, Pallas kernels, call(): pl.pallas_call(kernel, out_shape=out_shape, in_specs=in_specs or [vmem] *...  10.1 us
    pallas_call x1, Pallas kernels, body(): pl.pallas_call(query_kernel, grid=(heads // pair,), in_specs=[smem, vmem,...  5.93 us
    ppermute x3, starting transfers between devices, to_later_group(): lax.ppermute(value, 'ctx', [(s, s + step) for s in range(segments - step)])  3.88 us
    ppermute x1, starting transfers between devices, body(): return kept + lax.ppermute(away, 'head', [(0, 1), (1, 0)])  2.49 us
  transfers between devices with their start and end apart: 8, of which 6 were waited for; matrix products, arithmetic and copies ran while one was open for 0% of the time, Pallas kernels for 2%

profile of v3, /device:TPU:25, one launch (start us, length us, event | category | flops | bytes accessed | tf_op | source)
XLA Modules:
  0.0 73.2 jit_solution(11369229783074626616)
XLA Ops:
  1.3 0.7 collective-permute-done.other_ref
  2.1 1.0 %copy-done.2 = bf16[2048,128]{1,0:T(8,128)(2,1)S(1)} copy-done((bf16[2048,128]{1,0:T(8,128)(2,1)S(1)}, bf16[2048,128]{1,0:T(8,128)(2,1)}, u32[]{:S(2)}) %copy-start.2) | copy-done | bytes 524312
  3.1 1.0 %copy-done.3 = bf16[2048,128]{1,0:T(8,128)(2,1)S(1)} copy-done((bf16[2048,128]{1,0:T(8,128)(2,1)S(1)}, bf16[2048,128]{1,0:T(8,128)(2,1)}, u32[]{:S(2)}) %copy-start.3) | copy-done | bytes 524312
  4.1 1.0 %copy-done.4 = bf16[2048,128]{1,0:T(8,128)(2,1)S(1)} copy-done((bf16[2048,128]{1,0:T(8,128)(2,1)S(1)}, bf16[2048,128]{1,0:T(8,128)(2,1)}, u32[]{:S(2)}) %copy-start.4) | copy-done | bytes 524312
  5.2 0.9 %copy-done.5 = bf16[64,2048]{1,0:T(8,128)(2,1)S(1)} copy-done((bf16[64,2048]{1,0:T(8,128)(2,1)S(1)}, bf16[64,2048]{1,0:T(8,128)(2,1)}, u32[]{:S(2)}) %copy-start.5) | copy-done | bytes 262168
  7.5 3.2 %shard_map.109 = (bf16[128,2048]{1,0:T(8,128)(2,1)S(1)}, f32[128,128]{1,0:T(8,128)S(1)}, bf16[128,128]{1,0:T(8,128)(2,1)S(1)}, f32[128,128]{1,0:T(8,128)S(1)}, f...) custom-call(s32[1]{0:T(128)} %bitcast.1.core_ref, ...), custom_call_target="tpu_custom_call" | custom-call | flops 201326592 | bytes 2097152 | tf_op jit(solution)/shard_map/pallas_call | solution.py:20
  10.7 3.4 %all-to-all-start = ((f32[4,128,128]{2,1,0:T(8,128)}), f32[4,128,128]{2,1,0:T(8,128)S(1)}, u32[]{:S(2)}, u32[]{:S(2)}) async-start(f32[4,128,128]{2,1,0:T(8,128)} %get-tuple-element.30), calls=%async_computation | async-start | bytes 524288 | tf_op jit(solution)/shard_map/all_to_all | solution.py:293
  14.1 4.6 %all-to-all-done.turns_ref = f32[4,128,128]{2,1,0:T(8,128)S(1)} async-done(((f32[4,128,128]{2,1,0:T(8,128)}), f32[4,128,128]{2,1,0:T(8,128)S(1)}, u32[]{:S(2)}, u32[]{:S(2)}) %all-to-all-start) | async-done | bytes 262176 | tf_op jit(solution)/shard_map/all_to_all | solution.py:293
  19.2 2.2 %copy-done = bf16[2048,1024]{1,0:T(8,128)(2,1)S(1)} copy-done((bf16[2048,1024]{1,0:T(8,128)(2,1)S(1)}, bf16[2048,1024]{1,0:T(8,128)(2,1)}, u32[]{:S(2)}) %copy-start) | copy-done | bytes 4194328
  22.1 5.9 %shard_map.111 = (bf16[8,128,128]{2,1,0:T(8,128)(2,1)S(1)}, f32[8,128,128]{2,1,0:T(8,128)S(1)}, f32[8,128,1]{2,1,0:T(8,128)S(1)}, f32[8,128,1]{2,1,0:T(8,128)S(1)}, bf16[4,256,128]{2,1,0:T(8,128)(2,1)}) custom-call(s32[1]{0:T(128)} %bitcast.3.member_ref, bf16[128,2048]{1,0:T(8,128)(2,1)S(1)} %get-tuple-element.23.rows_ref, bf16[2048,1024]{1,0:T(8,128)(2,1)S(1)} %copy-done, ...), custom_call_target="tpu_custom_call" | custom-call | flops 1073741824 | bytes 16777216 | tf_op jit(solution)/shard_map/pallas_call | solution.py:332
  28.0 3.4 %all-to-all-start.1 = ((bf16[4,256,128]{2,1,0:T(8,128)(2,1)}), bf16[4,256,128]{2,1,0:T(8,128)(2,1)S(1)}, u32[]{:S(2)}, u32[]{:S(2)}) async-start(bf16[4,256,128]{2,1,0:T(8,128)(2,1)} %get-tuple-element.32), calls=%async_computation.1 | async-start | bytes 524288 | tf_op jit(solution)/shard_map/all_to_all | solution.py:293
  31.4 1.3 %collective-permute-start.1 = (bf16[640,128]{1,0:T(8,128)(2,1)S(1)}, bf16[640,128]{1,0:T(8,128)(2,1)S(1)}, u32[]{:S(2)}, u32[]{:S(2)}) collective-permute-start(bf16[640,128]{1,0:T(8,128)(2,1)S(1)} %get-tuple-element.33), channel_id=1, source_target_pairs={{0,8},{2,10},{4,12},{6,14},{8,16},{10,18},{12,20},{14,22},{16,24},... | collective-permute-start | bytes 491528 | tf_op jit(solution)/shard_map/ppermute | solution.py:297
  32.7 1.3 %collective-permute-start.2 = (bf16[640,128]{1,0:T(8,128)(2,1)S(1)}, bf16[640,128]{1,0:T(8,128)(2,1)S(1)}, u32[]{:S(2)}, u32[]{:S(2)}) collective-permute-start(bf16[640,128]{1,0:T(8,128)(2,1)S(1)} %get-tuple-element.33), channel_id=1, source_target_pairs={{0,16},{2,18},{4,20},{6,22},{8,24},{10,26},{12,28},{14,30},{1,17},... | collective-permute-start | bytes 491528 | tf_op jit(solution)/shard_map/ppermute | solution.py:297
  34.0 1.3 %collective-permute-start.3 = (bf16[384,128]{1,0:T(8,128)(2,1)S(1)}, bf16[384,128]{1,0:T(8,128)(2,1)S(1)}, u32[]{:S(2)}, u32[]{:S(2)}) collective-permute-start(bf16[384,128]{1,0:T(8,128)(2,1)S(1)} %get-tuple-element.34), channel_id=1, source_target_pairs={{0,24},{2,26},{4,28},{6,30},{1,25},{3,27},{5,29},{7,31}} | collective-permute-start | bytes 294920 | tf_op jit(solution)/shard_map/ppermute | solution.py:297
  35.3 7.6 %collective-permute-done.3.refs_2_ = bf16[384,128]{1,0:T(8,128)(2,1)S(1)} collective-permute-done((bf16[384,128]{1,0:T(8,128)(2,1)S(1)}, bf16[384,128]{1,0:T(8,128)(2,1)S(1)}, u32[]{:S(2)}, u32[]{:S(2)}) %collective-permute-start.3) | collective-permute-done | bytes 98336 | tf_op jit(solution)/shard_map/ppermute | solution.py:297
  42.9 4.4 %collective-permute-done.2.refs_1_ = bf16[640,128]{1,0:T(8,128)(2,1)S(1)} collective-permute-done((bf16[640,128]{1,0:T(8,128)(2,1)S(1)}, bf16[640,128]{1,0:T(8,128)(2,1)S(1)}, u32[]{:S(2)}, u32[]{:S(2)}) %collective-permute-start.2) | collective-permute-done | bytes 163872 | tf_op jit(solution)/shard_map/ppermute | solution.py:297
  47.3 1.6 %shard_map.112 = bf16[4,768,128]{2,1,0:T(8,128)(2,1)} custom-call(bf16[640,128]{1,0:T(8,128)(2,1)S(1)} %collective-permute-done.1.refs_0_, bf16[640,128]{1,0:T(8,128)(2,1)S(1)} %collective-permute-done.2.refs_1_, bf16[384,128]{1,0:T(8,128)(2,1)S(1)} %collective-permute-done.3.refs_2_, f32[128,512]{1,0:T(8,128)S(1)} %get-tuple-element.31.after_ref.refs_3_, ...), custom_call_target="tpu_custom_call" | custom-call | flops 201326592 | bytes 1000000 | tf_op jit(solution)/shard_map/pallas_call | solution.py:20
  48.9 3.5 %all-to-all-start.2 = ((bf16[4,768,128]{2,1,0:T(8,128)(2,1)}), bf16[4,768,128]{2,1,0:T(8,128)(2,1)S(1)}, u32[]{:S(2)}, u32[]{:S(2)}) async-start(bf16[4,768,128]{2,1,0:T(8,128)(2,1)} %shard_map.112), calls=%async_computation.2 | async-start | bytes 1572864 | tf_op jit(solution)/shard_map/all_to_all | solution.py:293
  52.5 9.2 %all-to-all-done.2.far_ref = bf16[4,768,128]{2,1,0:T(8,128)(2,1)S(1)} async-done(((bf16[4,768,128]{2,1,0:T(8,128)(2,1)}), bf16[4,768,128]{2,1,0:T(8,128)(2,1)S(1)}, u32[]{:S(2)}, u32[]{:S(2)}) %all-to-all-start.2) | async-done | bytes 786464 | tf_op jit(solution)/shard_map/all_to_all | solution.py:293
  61.8 2.2 %copy-done.1 = bf16[1024,2048]{1,0:T(8,128)(2,1)S(1)} copy-done((bf16[1024,2048]{1,0:T(8,128)(2,1)S(1)}, bf16[1024,2048]{1,0:T(8,128)(2,1)}, u32[]{:S(2)}) %copy-start.1) | copy-done | bytes 4194328
  64.0 4.8 %shard_map.113 = (bf16[64,2048]{1,0:T(8,128)(2,1)S(1)}, bf16[64,2048]{1,0:T(8,128)(2,1)S(1)}) custom-call(s32[2]{0:T(128)S(1)} %pad_add_fusion.position_ref, s32[16]{0:T(128)S(1)} %bitcast.8, bf16[4,256,128]{2,1,0:T(8,128)(2,1)S(1)} %all-to-all-done.1.near_ref, bf16[4,768,128]{2,1,0:T(8,128)(2,1)S(1)} %all-to-all-done.2.far_ref, ...), custom_call_target="tpu_custom_call" | custom-call | flops 536870912 | bytes 4000000 | tf_op jit(solution)/shard_map/pallas_call | solution.py:20
  68.7 2.5 %collective-permute-start.4 = (bf16[64,2048]{1,0:T(8,128)(2,1)S(1)}, bf16[64,2048]{1,0:T(8,128)(2,1)S(1)}, u32[]{:S(2)}, u32[]{:S(2)}) collective-permute-start(bf16[64,2048]{1,0:T(8,128)(2,1)S(1)} %get-tuple-element.40), channel_id=1, source_target_pairs={{0,1},{1,0},{2,3},{3,2},{4,5},{5,4},{6,7},{7,6},{8,9},{9,8},{10,11... | collective-permute-start | bytes 786440 | tf_op jit(solution)/shard_map/ppermute | solution.py:395
  71.2 1.2 %collective-permute-done.4 = bf16[64,2048]{1,0:T(8,128)(2,1)S(1)} collective-permute-done((bf16[64,2048]{1,0:T(8,128)(2,1)S(1)}, bf16[64,2048]{1,0:T(8,128)(2,1)S(1)}, u32[]{:S(2)}, u32[]{:S(2)}) %collective-permute-start.4) | collective-permute-done | bytes 262176 | tf_op jit(solution)/shard_map/ppermute | solution.py:395
  72.4 0.8 %add.8 = bf16[64,2048]{1,0:T(8,128)(2,1)} add(bf16[64,2048]{1,0:T(8,128)(2,1)S(1)} %get-tuple-element.39, bf16[64,2048]{1,0:T(8,128)(2,1)S(1)} %collective-permute-done.4) | non-fusion elementwise | flops 131072 | bytes 786432 | tf_op jit(solution)/shard_map/add | solution.py:395
  (19 shorter events, 3.3 us)
Async XLA Ops:
  0.0 2.0 %collective-permute-start = (bf16[64,2048]{1,0:T(8,128)(2,1)}, bf16[64,2048]{1,0:T(8,128)(2,1)S(1)}, u32[]{:S(2)}, u32[]{:S(2)}) collective-permute-start(bf16[64,2048]{1,0:T(8,128)(2,1)} %mine_ref.1), channel_id=1, source_target_pairs={{0,1},{1,0},{2,3},{3,2},{4,5},{5,4},{6,7},{7,6},{8,9},{9,8},{10,11... | collective-permute-start | bytes 786440 | tf_op jit(solution)/shard_map/ppermute | solution.py:281
  2.0 1.0 %copy-start.2 = (bf16[2048,128]{1,0:T(8,128)(2,1)S(1)}, bf16[2048,128]{1,0:T(8,128)(2,1)}, u32[]{:S(2)}) copy-start(bf16[2048,128]{1,0:T(8,128)(2,1)} %key_ref.1) | copy-start | bytes 1572868
  3.1 1.0 %copy-start.3 = (bf16[2048,128]{1,0:T(8,128)(2,1)S(1)}, bf16[2048,128]{1,0:T(8,128)(2,1)}, u32[]{:S(2)}) copy-start(bf16[2048,128]{1,0:T(8,128)(2,1)} %value_ref.1) | copy-start | bytes 1572868
  4.1 1.0 %copy-start.4 = (bf16[2048,128]{1,0:T(8,128)(2,1)S(1)}, bf16[2048,128]{1,0:T(8,128)(2,1)}, u32[]{:S(2)}) copy-start(bf16[2048,128]{1,0:T(8,128)(2,1)} %dir_ref.1) | copy-start | bytes 1572868
  5.2 0.9 %copy-start.5 = (bf16[64,2048]{1,0:T(8,128)(2,1)S(1)}, bf16[64,2048]{1,0:T(8,128)(2,1)}, u32[]{:S(2)}) copy-start(bf16[64,2048]{1,0:T(8,128)(2,1)} %mine_ref.1) | copy-start | bytes 786436
  6.1 0.7 copy-start.6
  6.8 0.7 copy-start.7
  10.7 8.0 %all-to-all-start = ((f32[4,128,128]{2,1,0:T(8,128)}), f32[4,128,128]{2,1,0:T(8,128)S(1)}, u32[]{:S(2)}, u32[]{:S(2)}) async-start(f32[4,128,128]{2,1,0:T(8,128)} %get-tuple-element.30), calls=%async_computation | async-start | bytes 524288 | tf_op jit(solution)/shard_map/all_to_all | solution.py:293
  19.2 2.2 %copy-start = (bf16[2048,1024]{1,0:T(8,128)(2,1)S(1)}, bf16[2048,1024]{1,0:T(8,128)(2,1)}, u32[]{:S(2)}) copy-start(bf16[2048,1024]{1,0:T(8,128)(2,1)} %weight_ref.1) | copy-start | bytes 12582916
  21.4 0.7 copy-start.8
  22.1 39.7 %copy-start.9 = (s32[1,16]{1,0:T(1,128)S(1)}, s32[1,16]{1,0:T(1,128)}, u32[]{:S(2)}) copy-start(s32[1,16]{1,0:T(1,128)} %param.21) | copy-start | bytes 196
  28.0 21.0 %all-to-all-start.1 = ((bf16[4,256,128]{2,1,0:T(8,128)(2,1)}), bf16[4,256,128]{2,1,0:T(8,128)(2,1)S(1)}, u32[]{:S(2)}, u32[]{:S(2)}) async-start(bf16[4,256,128]{2,1,0:T(8,128)(2,1)} %get-tuple-element.32), calls=%async_computation.1 | async-start | bytes 524288 | tf_op jit(solution)/shard_map/all_to_all | solution.py:293
  31.4 11.5 %collective-permute-start.1 = (bf16[640,128]{1,0:T(8,128)(2,1)S(1)}, bf16[640,128]{1,0:T(8,128)(2,1)S(1)}, u32[]{:S(2)}, u32[]{:S(2)}) collective-permute-start(bf16[640,128]{1,0:T(8,128)(2,1)S(1)} %get-tuple-element.33), channel_id=1, source_target_pairs={{0,8},{2,10},{4,12},{6,14},{8,16},{10,18},{12,20},{14,22},{16,24},... | collective-permute-start | bytes 491528 | tf_op jit(solution)/shard_map/ppermute | solution.py:297
  32.7 14.6 %collective-permute-start.2 = (bf16[640,128]{1,0:T(8,128)(2,1)S(1)}, bf16[640,128]{1,0:T(8,128)(2,1)S(1)}, u32[]{:S(2)}, u32[]{:S(2)}) collective-permute-start(bf16[640,128]{1,0:T(8,128)(2,1)S(1)} %get-tuple-element.33), channel_id=1, source_target_pairs={{0,16},{2,18},{4,20},{6,22},{8,24},{10,26},{12,28},{14,30},{1,17},... | collective-permute-start | bytes 491528 | tf_op jit(solution)/shard_map/ppermute | solution.py:297
  34.0 8.9 %collective-permute-start.3 = (bf16[384,128]{1,0:T(8,128)(2,1)S(1)}, bf16[384,128]{1,0:T(8,128)(2,1)S(1)}, u32[]{:S(2)}, u32[]{:S(2)}) collective-permute-start(bf16[384,128]{1,0:T(8,128)(2,1)S(1)} %get-tuple-element.34), channel_id=1, source_target_pairs={{0,24},{2,26},{4,28},{6,30},{1,25},{3,27},{5,29},{7,31}} | collective-permute-start | bytes 294920 | tf_op jit(solution)/shard_map/ppermute | solution.py:297
  48.9 12.8 %all-to-all-start.2 = ((bf16[4,768,128]{2,1,0:T(8,128)(2,1)}), bf16[4,768,128]{2,1,0:T(8,128)(2,1)S(1)}, u32[]{:S(2)}, u32[]{:S(2)}) async-start(bf16[4,768,128]{2,1,0:T(8,128)(2,1)} %shard_map.112), calls=%async_computation.2 | async-start | bytes 1572864 | tf_op jit(solution)/shard_map/all_to_all | solution.py:293
  61.8 2.2 %copy-start.1 = (bf16[1024,2048]{1,0:T(8,128)(2,1)S(1)}, bf16[1024,2048]{1,0:T(8,128)(2,1)}, u32[]{:S(2)}) copy-start(bf16[1024,2048]{1,0:T(8,128)(2,1)} %out_hbm.1) | copy-start | bytes 12582916
  68.7 3.7 %collective-permute-start.4 = (bf16[64,2048]{1,0:T(8,128)(2,1)S(1)}, bf16[64,2048]{1,0:T(8,128)(2,1)S(1)}, u32[]{:S(2)}, u32[]{:S(2)}) collective-permute-start(bf16[64,2048]{1,0:T(8,128)(2,1)S(1)} %get-tuple-element.40), channel_id=1, source_target_pairs={{0,1},{1,0},{2,3},{3,2},{4,5},{5,4},{6,7},{7,6},{8,9},{9,8},{10,11... | collective-permute-start | bytes 786440 | tf_op jit(solution)/shard_map/ppermute | solution.py:395

commit v4 on v3

v4 whole, which is shorter than its diff:
```python
import functools
import math

import jax
import jax.numpy as jnp
from jax import lax
from jax.experimental import pallas as pl
from jax.experimental.pallas import tpu as pltpu
from jax.sharding import PartitionSpec as P

EPSILON = 1e-06
NEGATIVE = -1e30
F32 = jnp.float32
BF16 = jnp.bfloat16
MIB = 1024 * 1024


def call(kernel, out_shape, args, in_specs=None, scratch=(), flops=0, moved=0, limit=6):
    vmem = pl.BlockSpec(memory_space=pltpu.VMEM)
    return pl.pallas_call(
        kernel,
        out_shape=out_shape,
        in_specs=in_specs or [vmem] * len(args),
        out_specs=jax.tree.map(lambda _: vmem, out_shape),
        scratch_shapes=list(scratch),
        compiler_params=pltpu.CompilerParams(vmem_limit_bytes=limit * MIB),
        cost_estimate=pl.CostEstimate(flops=flops, bytes_accessed=moved, transcendentals=0),
    )(*args)


def target_of(member, step, group):
    return member ^ step if group & (group - 1) == 0 else (member + step) % group


def source_of(member, step, group):
    return member ^ step if group & (group - 1) == 0 else (member + group - step) % group


def in_hbm(array):
    return pltpu.with_memory_space_constraint(array, pltpu.HBM)


def shaped(shape, dtype):
    return jax.ShapeDtypeStruct(shape, dtype)


def split(value):
    high = value.astype(BF16)
    return high, (value - high.astype(F32)).astype(BF16)


def dot3(left, right, left_dim=1, right_dim=0):
    left_high, left_low = split(left)
    right_high, right_low = split(right)
    return lax.dot_general(
        jnp.concatenate([left_high, left_high, left_low], axis=left_dim),
        jnp.concatenate([right_high, right_low, right_high], axis=right_dim),
        (((left_dim,), (right_dim,)), ((), ())),
        preferred_element_type=F32,
    )


def iota2(shape):
    return lax.broadcasted_iota(jnp.int32, shape, 0), lax.broadcasted_iota(jnp.int32, shape, 1)


def merge_inverse(lower, rows, cols):
    tokens = lower.shape[0]
    block = 8
    inverse = jnp.where(rows == cols, 1.0, 0.0).astype(F32)
    first = rows - rows % block
    for step in range(block - 1):
        column = jnp.sum(jnp.where(cols == first + step, lower, 0.0), axis=1, keepdims=True)
        pivot = inverse.reshape(tokens // block, block, tokens)[:, step : step + 1, :]
        pivot = jnp.broadcast_to(pivot, (tokens // block, block, tokens)).reshape(tokens, tokens)
        inverse = inverse - column * pivot
    while block < tokens:
        corner = (
            (rows // (2 * block) == cols // (2 * block))
            & (rows % (2 * block) >= block)
            & (cols % (2 * block) < block)
        )
        inverse = inverse - dot3(dot3(inverse, jnp.where(corner, lower, 0.0)), inverse)
        block *= 2
    return inverse


def load_kernel(size, key_hbm, dir_hbm, value_hbm, rate_hbm, key_gain_hbm,
                query_gain_hbm, mine_hbm, weight_ref, rate_ref, key_gain_ref, query_gain_ref,
                mine_ref, sems):
    pairs = [
        (hbm, weight_ref.at[:, index * size : (index + 1) * size])
        for index, hbm in enumerate((key_hbm, dir_hbm, value_hbm))
    ]
    pairs += [(rate_hbm, rate_ref), (key_gain_hbm, key_gain_ref)]
    pairs += [(query_gain_hbm, query_gain_ref), (mine_hbm, mine_ref)]
    copies = [pltpu.make_async_copy(*pair, sems.at[n]) for n, pair in enumerate(pairs)]
    for copy in copies:
        copy.start()
    for copy in copies:
        copy.wait()


def prepare_kernel(place_ref, mine_ref, other_ref, weight_ref, rate_ref, bias_ref, gain_ref,
                   rows_ref, kn_ref, val_ref, dirs_ref, coeff_ref, solved_ref, exit_ref, turn_ref):
    core = place_ref[1]
    half = mine_ref.shape[0]
    rows_ref[pl.ds(pl.multiple_of(core * half, half), half), :] = mine_ref[...]
    rows_ref[pl.ds(pl.multiple_of((1 - core) * half, half), half), :] = other_ref[...]
    seg = rows_ref[...]
    size = turn_ref.shape[0]
    raw = jnp.dot(seg, weight_ref[...], preferred_element_type=F32)
    keys, raw, vals = raw[:, :size], raw[:, size : 2 * size], raw[:, 2 * size :]
    kn = keys * lax.rsqrt(jnp.mean(keys * keys, axis=-1, keepdims=True) + EPSILON) * gain_ref[...]
    dirs = raw * lax.rsqrt(jnp.sum(raw * raw, axis=-1, keepdims=True) + EPSILON)
    vector = jnp.broadcast_to(rate_ref[...], (16, seg.shape[1]))
    logits = lax.dot_general(seg, vector, (((1,), (1,)), ((), ())), preferred_element_type=F32)
    rates = 2.0 * jax.nn.sigmoid(logits[:, :1] + bias_ref[0])
    val_ref[...] = vals.astype(BF16)
    kn_ref[...] = kn
    dirs_ref[...] = dirs
    tokens, size = dirs.shape
    rows, cols = iota2((tokens, tokens))
    below = rows > cols
    grams = dot3(dirs, jnp.concatenate([dirs, kn], axis=0), 1, 1)
    lower = jnp.where(below, rates * grams[:, :tokens], 0.0)
    crossing = jnp.where(below, rates * grams[:, tokens:], 0.0)
    inverse = merge_inverse(lower, rows, cols)
    both = dot3(inverse, jnp.concatenate([crossing, rates * dirs], axis=1))
    coeff_ref[...] = both[:, :tokens]
    solved_ref[...] = both[:, tokens:]
    crossed = dot3(both, dirs, 0, 0)
    exit_ref[...] = kn - crossed[:tokens]
    heads, lanes = iota2((size, size))
    turn_ref[...] = jnp.where(heads == lanes, 1.0, 0.0) - crossed[tokens:]


def leave_kernel(group, place_ref, exit_ref, val_ref, *refs):
    turn_refs, (long_ref, short_ref, starts_ref) = refs[:group], refs[group : group + 3]
    near_refs, (turns_ref, seen_ref) = refs[group + 3 : -2], refs[-2:]
    member = place_ref[0] % group
    tokens, size = exit_ref.shape
    for step in range(group):
        turns_ref[source_of(member, step, group)] = turn_refs[step][...]
    own = exit_ref[...]
    keys = own
    product = None
    heads, lanes = iota2((size, size))
    starts_ref[0] = jnp.where(heads == lanes, 1.0, 0.0)
    for index in range(group):
        seen_ref[index] = keys.astype(BF16)
        turn = turns_ref[index]
        product = turn if product is None else dot3(product, turn)
        if index:
            keys = jnp.where(index > member, dot3(keys, turn), own)
        if index < group - 1:
            starts_ref[index + 1] = product
    high, low = split(keys)
    for ref in (long_ref, short_ref):
        ref[:tokens] = high
        ref[tokens : 2 * tokens] = low
        ref[2 * tokens : 3 * tokens] = val_ref[...]
    high, low = split(product)
    long_ref[3 * tokens : 3 * tokens + size] = high
    long_ref[3 * tokens + size :] = low
    for step in range(1, group):
        near_refs[step - 1][:tokens] = seen_ref[target_of(member, step, group)]
        near_refs[step - 1][tokens:] = val_ref[...]


def query_kernel(rows_ref, weight_hbm, gain_ref, kn_ref, dirs_ref, coeff_ref, solved_ref, val_ref,
                 moved_ref, weighted_ref, peak_ref, total_ref, weight_ref, sems):
    tokens, size = kn_ref.shape
    heads = moved_ref.shape[0]
    pieces = weight_ref.shape[0]
    wide = weight_ref.shape[2]
    copies = [
        pltpu.make_async_copy(
            weight_hbm.at[:, n * wide : (n + 1) * wide], weight_ref.at[n], sems.at[n]
        )
        for n in range(pieces)
    ]
    for copy in copies:
        copy.start()
    across = jnp.concatenate([kn_ref[...], dirs_ref[...]], axis=0)
    into = jnp.concatenate([coeff_ref[...], solved_ref[...]], axis=1)
    together = math.gcd(pieces, 2)
    for turn in range(pieces // together):
        parts = []
        for n in range(turn * together, (turn + 1) * together):
            copies[n].wait()
            raw = jnp.dot(rows_ref[...], weight_ref[n], preferred_element_type=F32)
            parts += [raw[:, at : at + size] for at in range(0, wide, size)]
        count = len(parts)
        raw = jnp.concatenate(parts, axis=0)
        queries = (
            raw * lax.rsqrt(jnp.mean(raw * raw, axis=-1, keepdims=True) + EPSILON) * gain_ref[...]
        )
        seen = dot3(queries, across, 1, 1)
        rows, cols = iota2((count * tokens, tokens))
        up_to = rows % tokens >= cols
        reach = jnp.where(up_to, seen[:, tokens:], 0.0)
        taken = dot3(reach, into)
        scores = (seen[:, :tokens] - taken[:, :tokens]) * (1.0 / math.sqrt(size))
        scores = jnp.where(up_to, scores, NEGATIVE)
        moved = (queries - taken[:, tokens:]).astype(BF16)
        peak = jnp.max(scores, axis=1, keepdims=True)
        weights = jnp.exp(scores - peak)
        total = jnp.sum(weights, axis=1, keepdims=True)
        weighted = jnp.dot(weights.astype(BF16), val_ref[...], preferred_element_type=F32)
        for h in range(count):
            part = slice(h * tokens, (h + 1) * tokens)
            head = turn * count + h
            moved_ref[head] = moved[part]
            weighted_ref[head] = weighted[part]
            peak_ref[head] = peak[part]
            total_ref[head] = total[part]


def arrive_kernel(count, group, tokens, place_ref, *refs):
    arrived, starts_ref = refs[:count], refs[count]
    far_refs = refs[-group:]
    member = place_ref[0] % group
    size = starts_ref.shape[1]
    product = None
    brought = []
    for index in range(count):
        ref = arrived[index]
        keys = ref[:tokens].astype(F32) + ref[tokens : 2 * tokens].astype(F32)
        if index:
            before = arrived[index - 1]
            whole = before[3 * tokens : 3 * tokens + size].astype(F32)
            whole = whole + before[3 * tokens + size :].astype(F32)
            product = whole if product is None else dot3(whole, product)
            keys = dot3(keys, product)
        brought.append(keys)
    keys = jnp.concatenate(brought, axis=0)
    split_at = count * tokens
    for step in range(group):
        start = starts_ref[target_of(member, step, group)]
        far_refs[step][:split_at] = dot3(keys, start).astype(BF16)
        for index in range(count):
            far_refs[step][split_at + index * tokens : split_at + (index + 1) * tokens] = arrived[
                index
            ][2 * tokens : 3 * tokens]


def attend_kernel(most, group, place_ref, mask_ref, *refs):
    near_refs, far_refs = refs[: group - 1], refs[group - 1 : 2 * group - 1]
    (moved_ref, weighted_ref, peak_ref, total_ref, out_hbm, away_ref, kept_ref, chosen_ref,
     keys_ref, vals_ref, attended_ref, out_ref, sems, *state) = refs[2 * group - 1 :]
    pieces, _, wide = out_ref.shape
    copies = [
        pltpu.make_async_copy(
            out_hbm.at[:, n * wide : (n + 1) * wide], out_ref.at[n], sems.at[n]
        )
        for n in range(pieces)
    ]
    for copy in copies:
        copy.start()
    place, core = place_ref[0], place_ref[1]
    heads, tokens, size = moved_ref.shape
    segments = mask_ref.shape[0]
    scaling = 1.0 / math.sqrt(size)
    mine, member = place // group, place % group

    def pick(segment, count):
        wanted = (mask_ref[segment] > 0) & (segment < place)

        @pl.when(wanted & (count < most))
        def _():
            chosen_ref[count] = segment

        return count + wanted.astype(jnp.int32)

    found = lax.fori_loop(0, segments, pick, jnp.int32(0))
    chunk = keys_ref.shape[0] // tokens
    lanes = lax.broadcasted_iota(jnp.int32, (tokens, chunk * tokens), 1)

    def collect(turn):
        for slot in range(chunk):
            part = slice(slot * tokens, (slot + 1) * tokens)
            index = turn * chunk + slot
            used = index < found
            segment = jnp.where(used, chosen_ref[index], 0)
            whose, distance = segment % group, mine - segment // group
            before = jnp.maximum(distance - 1, 0) * tokens

            @pl.when(jnp.logical_not(used))
            def _():
                keys_ref[part, :] = jnp.zeros((tokens, size), BF16)
                vals_ref[part, :] = jnp.zeros((tokens, size), BF16)

            for step in range(group):
                here = used & (whose == source_of(member, step, group))

                @pl.when(here & (distance > 0))
                def _():
                    far = far_refs[step]
                    middle = far.shape[0] // 2
                    keys_ref[part, :] = far[pl.ds(pl.multiple_of(before, tokens), tokens), :]
                    vals_ref[part, :] = far[
                        pl.ds(pl.multiple_of(middle + before, tokens), tokens), :
                    ]

                if step:

                    @pl.when(here & (distance == 0))
                    def _():
                        keys_ref[part, :] = near_refs[step - 1][:tokens]
                        vals_ref[part, :] = near_refs[step - 1][tokens:]

    def advance(head, turn, peak, total, weighted):
        scores = lax.dot_general(
            moved_ref[head], keys_ref[...], (((1,), (1,)), ((), ())), preferred_element_type=F32
        )
        scores = jnp.where(lanes < (found - turn * chunk) * tokens, scores * scaling, NEGATIVE)
        new_peak = jnp.maximum(peak, jnp.max(scores, axis=1, keepdims=True))
        fading = jnp.exp(peak - new_peak)
        weights = jnp.exp(scores - new_peak)
        total = total * fading + jnp.sum(weights, axis=1, keepdims=True)
        weighted = weighted * fading + jnp.dot(
            weights.astype(BF16), vals_ref[...], preferred_element_type=F32
        )
        return new_peak, total, weighted

    half = kept_ref.shape[0]

    def finish(head, total, weighted):
        done = (weighted / total).astype(BF16)
        for index in range(tokens // half):
            at = pl.multiple_of(jnp.where(index == core, half, 0), half)
            attended_ref[pl.ds(at, half), head * size : (head + 1) * size] = done[
                index * half : (index + 1) * half
            ]

    turns = most // chunk
    if turns == 1:
        collect(0)
        for head in range(heads):
            _, total, weighted = advance(
                head, 0, peak_ref[head], total_ref[head], weighted_ref[head]
            )
            finish(head, total, weighted)
    else:
        run_p, run_t, run_w = state
        run_p[...], run_t[...], run_w[...] = peak_ref[...], total_ref[...], weighted_ref[...]

        @pl.loop(0, turns)
        def _(turn):
            collect(turn)
            for head in range(heads):
                run_p[head], run_t[head], run_w[head] = advance(
                    head, turn, run_p[head], run_t[head], run_w[head]
                )

        for head in range(heads):
            finish(head, run_t[head], run_w[head])
    for n in range(pieces):
        copies[n].wait()
        result = jnp.dot(attended_ref[...], out_ref[n], preferred_element_type=F32).astype(BF16)
        away_ref[:, n * wide : (n + 1) * wide] = result[:half]
        kept_ref[:, n * wide : (n + 1) * wide] = result[half:]


def body(
    hidden, w_query, w_key, w_value, w_dir, u_rate, rate_bias, q_gain, k_gain, w_out, block_mask
):
    segments = lax.axis_size("ctx")
    position = lax.axis_index("ctx")
    core = lax.axis_index("head")
    group = max(d for d in range(1, math.isqrt(segments) + 1) if segments % d == 0)
    groups = segments // group
    other = lax.ppermute(hidden, "head", [(0, 1), (1, 0)])
    half, width = hidden.shape
    tokens = half * lax.axis_size("head")
    size = w_key.shape[1]
    heads = w_query.shape[1] // size
    smem = pl.BlockSpec(memory_space=pltpu.SMEM)
    vmem = pl.BlockSpec(memory_space=pltpu.VMEM)
    hbm = pl.BlockSpec(memory_space=pltpu.HBM)
    anywhere = pl.BlockSpec(memory_space=pl.ANY)
    square = shaped((tokens, size), F32)
    place = jnp.stack([position, core]).astype(jnp.int32)

    def to_member(value, step):
        pairs = [
            (s, s - s % group + target_of(s % group, step, group)) for s in range(segments)
        ]
        return lax.ppermute(value, "ctx", pairs)

    def to_later_group(value, distance):
        step = distance * group
        return lax.ppermute(value, "ctx", [(s, s + step) for s in range(segments - step)])

    weights, rate_row, key_gain, query_gain, mine = call(
        functools.partial(load_kernel, size),
        (
            shaped((width, 3 * size), BF16), shaped((1, width), BF16), shaped((1, size), F32),
            shaped((1, size), F32), shaped((half, width), BF16),
        ),
        tuple(
            in_hbm(array)
            for array in (
                w_key, w_dir, w_value, u_rate, k_gain.reshape(1, size), q_gain.reshape(1, size),
                hidden,
            )
        ),
        in_specs=[hbm] * 7,
        scratch=(pltpu.SemaphoreType.DMA((7,)),),
        moved=12 * width * size,
    )
    rows, kn, val, dirs, coeff, solved, exit_keys, turn = call(
        prepare_kernel,
        (
            shaped((tokens, width), BF16), square, shaped((tokens, size), BF16), square, square,
            square, square, shaped((size, size), F32),
        ),
        (place, mine, other, weights, rate_row, rate_bias, key_gain),
        in_specs=[smem] + [vmem] * 4 + [smem, vmem],
        flops=6 * tokens * width * size,
        moved=8 * width * size,
    )
    turns = [turn] + [to_member(turn, step) for step in range(1, group)]
    long, short, starts, *near = call(
        functools.partial(leave_kernel, group),
        [
            shaped((3 * tokens + 2 * size, size), BF16),
            shaped((3 * tokens, size), BF16),
            shaped((group, size, size), F32),
        ]
        + [shaped((2 * tokens, size), BF16)] * (group - 1),
        (place, exit_keys, val, *turns),
        in_specs=[smem] + [vmem] * (2 + group),
        scratch=(
            pltpu.VMEM((group, size, size), F32),
            pltpu.VMEM((group, tokens, size), BF16),
        ),
        flops=12 * group * size**3,
        moved=10**6,
    )
    arrived = [
        to_later_group(long if d < groups - 1 else short, d) for d in range(1, groups)
    ]
    near = [to_member(near[step - 1], step) for step in range(1, group)]
    pieces = math.gcd(heads, 4)
    moved, weighted, peak, total = call(
        query_kernel,
        (
            shaped((heads, tokens, size), BF16),
            shaped((heads, tokens, size), F32),
            shaped((heads, tokens, 1), F32),
            shaped((heads, tokens, 1), F32),
        ),
        (rows, in_hbm(w_query), query_gain, kn, dirs, coeff, solved, val),
        in_specs=[vmem, hbm] + [vmem] * 6,
        scratch=(
            pltpu.VMEM((pieces, width, w_query.shape[1] // pieces), BF16),
            pltpu.SemaphoreType.DMA((pieces,)),
        ),
        flops=4 * tokens * width * heads * size,
        moved=8 * width * heads * size,
        limit=16,
    )
    far = call(
        functools.partial(arrive_kernel, groups - 1, group, tokens),
        [shaped((2 * (groups - 1) * tokens, size), BF16)] * group,
        (place, *arrived, starts, *near),
        in_specs=[smem] + [vmem] * groups + [anywhere] * (group - 1),
        flops=6 * groups * group * size**3,
        moved=10**6,
        limit=8 + group * groups // 4,
    )
    far = [far[0]] + [to_member(far[step], step) for step in range(1, group)]
    most = segments // 4
    chunk = math.gcd(most, 4)
    width_out = w_out.shape[1]
    pieces = math.gcd(width_out // size, 4)
    scratch = [
        pltpu.SMEM((most,), jnp.int32),
        pltpu.VMEM((chunk * tokens, size), BF16),
        pltpu.VMEM((chunk * tokens, size), BF16),
        pltpu.VMEM((tokens, heads * size), BF16),
        pltpu.VMEM((pieces, heads * size, width_out // pieces), BF16),
        pltpu.SemaphoreType.DMA((pieces,)),
    ]
    if most > chunk:
        scratch += [pltpu.VMEM((heads, tokens, 1), F32)] * 2
        scratch += [pltpu.VMEM((heads, tokens, size), F32)]
    away, kept = call(
        functools.partial(attend_kernel, most, group),
        [shaped((half, width_out), BF16)] * 2,
        (place, block_mask[0], *near, *far, moved, weighted, peak, total, in_hbm(w_out)),
        in_specs=[smem] * 2 + [vmem] * (2 * group - 1 + 4) + [hbm],
        scratch=scratch,
        flops=2 * tokens * width_out * heads * size,
        moved=4 * 10**6,
        limit=16 + group * groups // 4,
    )
    return kept + lax.ppermute(away, "head", [(0, 1), (1, 0)])


def solution(mesh):
    in_specs = (
        P(("ctx", "head"), None),
        P(None, "head"),
        P(None, "head"),
        P(None, "head"),
        P(None, "head"),
        P("head", None),
        P("head"),
        P(),
        P(),
        P("head", None),
        P("ctx", None),
    )
    out_specs = P(("ctx", "head"), None)
    return jax.shard_map(body, mesh=mesh, in_specs=in_specs, out_specs=out_specs, check_vma=False)
```

time: 73.9 us -> 51.2 us (0.69)
  the two profiles are of different devices: /device:TPU:25 before, /device:TPU:0 now
where the time goes in v4:
time: 51.2 us; the launch traced here: 51 us
  starting transfers between devices  18.9 us (37%)
  Pallas kernels  16.7 us (33%)
  waiting for transfers between devices  13.8 us (27%)
  other arithmetic  0.85 us (2%)
  between operations  0.78 us (2%)
    pallas_call x6, Pallas kernels, call(): pl.pallas_call(kernel, out_shape=out_shape, in_specs=in_specs or [vmem] *...  16.7 us
    ppermute x9, waiting for transfers between devices, to_member(): return lax.ppermute(value, 'ctx', pairs)  12.3 us
    ppermute x3, starting transfers between devices, to_later_group(): lax.ppermute(value, 'ctx', [(s, s + step) for s in range(segments - step)])  9.27 us
    ppermute x9, starting transfers between devices, to_member(): return lax.ppermute(value, 'ctx', pairs)  9.07 us
    ppermute x1, waiting for transfers between devices, body(): return kept + lax.ppermute(away, 'head', [(0, 1), (1, 0)])  1.52 us
  transfers between devices with their start and end apart: 14, of which 7 were waited for; matrix products, arithmetic and copies ran while one was open for 0% of the time, Pallas kernels for 12%

profile of v4, /device:TPU:0, one launch (start us, length us, event | category | flops | bytes accessed | tf_op | source)
XLA Modules:
  0.0 51.0 jit_solution(17253003412784263676)
XLA Ops:
  0.0 0.5 collective-permute-start
  1.1 1.5 %shard_map.109 = (bf16[2048,384]{1,0:T(8,128)(2,1)S(1)}, bf16[1,2048]{1,0:T(2,128)(2,1)S(1)}, f32[1,128]{1,0:T(1,128)S(1)}, f32[1,128]{1,0:T(1,128)S(1)}, bf16[64,2048]{1,0:T(8,128)(2,1)S(1)}) custom-call(bf16[2048,128]{1,0:T(8,128)(2,1)} %key_hbm.1, bf16[2048,128]{1,0:T(8,128)(2,1)} %dir_hbm.1, bf16[2048,128]{1,0:T(8,128)(2,1)} %value_hbm.1, ...), custom_call_target="tpu_custom_call" | custom-call | bytes 3145728 | tf_op jit(solution)/shard_map/pallas_call | solution.py:20
  2.7 3.0 %shard_map.110 = (bf16[128,2048]{1,0:T(8,128)(2,1)S(1)}, f32[128,128]{1,0:T(8,128)S(1)}, bf16[128,128]{1,0:T(8,128)(2,1)S(1)}, f32[128,128]{1,0:T(8,128)S(1)}, f...) custom-call(s32[2]{0:T(128)S(1)} %pad_add_fusion.place_ref, ...), custom_call_target="tpu_custom_call" | custom-call | flops 201326592 | bytes 2097152 | tf_op jit(solution)/shard_map/pallas_call | solution.py:20
  5.7 2.6 %collective-permute-start.1 = (f32[128,128]{1,0:T(8,128)S(1)}, f32[128,128]{1,0:T(8,128)S(1)}, u32[]{:S(2)}, u32[]{:S(2)}) collective-permute-start(f32[128,128]{1,0:T(8,128)S(1)} %get-tuple-element.40.refs_0_), channel_id=1, source_target_pairs={{0,2},{2,0},{4,6},{6,4},{8,10},{10,8},{12,14},{14,12},{16,18},{18,... | collective-permute-start | bytes 196616 | tf_op jit(solution)/shard_map/ppermute | solution.py:390
  8.3 1.5 %collective-permute-start.2 = (f32[128,128]{1,0:T(8,128)S(1)}, f32[128,128]{1,0:T(8,128)S(1)}, u32[]{:S(2)}, u32[]{:S(2)}) collective-permute-start(f32[128,128]{1,0:T(8,128)S(1)} %get-tuple-element.40.refs_0_), channel_id=1, source_target_pairs={{0,4},{2,6},{4,0},{6,2},{8,12},{10,14},{12,8},{14,10},{16,20},{18,... | collective-permute-start | bytes 196616 | tf_op jit(solution)/shard_map/ppermute | solution.py:390
  9.8 1.2 %collective-permute-done.1.refs_1_ = f32[128,128]{1,0:T(8,128)S(1)} collective-permute-done((f32[128,128]{1,0:T(8,128)S(1)}, f32[128,128]{1,0:T(8,128)S(1)}, u32[]{:S(2)}, u32[]{:S(2)}) %collective-permute-start.1) | collective-permute-done | bytes 65568 | tf_op jit(solution)/shard_map/ppermute | solution.py:390
  11.0 1.5 %collective-permute-done.2.refs_2_ = f32[128,128]{1,0:T(8,128)S(1)} collective-permute-done((f32[128,128]{1,0:T(8,128)S(1)}, f32[128,128]{1,0:T(8,128)S(1)}, u32[]{:S(2)}, u32[]{:S(2)}) %collective-permute-start.2) | collective-permute-done | bytes 65568 | tf_op jit(solution)/shard_map/ppermute | solution.py:390
  12.5 2.4 %collective-permute-done.3.refs_3_ = f32[128,128]{1,0:T(8,128)S(1)} collective-permute-done((f32[128,128]{1,0:T(8,128)S(1)}, f32[128,128]{1,0:T(8,128)S(1)}, u32[]{:S(2)}, u32[]{:S(2)}) %collective-permute-start.3) | collective-permute-done | bytes 65568 | tf_op jit(solution)/shard_map/ppermute | solution.py:390
  15.0 1.0 %shard_map.111 = (bf16[640,128]{1,0:T(8,128)(2,1)S(1)}, bf16[384,128]{1,0:T(8,128)(2,1)S(1)}, f32[4,128,128]{2,1,0:T(8,128)S(1)}, bf16[256,128]{1,0:T(8,128)(2,1...) custom-call(s32[2]{0:T(128)S(1)} %pad_add_fusion.place_ref, ...), custom_call_target="tpu_custom_call" | custom-call | flops 100663296 | bytes 1000000 | tf_op jit(solution)/shard_map/pallas_call | solution.py:20
  16.0 3.5 %collective-permute-start.7 = (bf16[640,128]{1,0:T(8,128)(2,1)S(1)}, bf16[640,128]{1,0:T(8,128)(2,1)S(1)}, u32[]{:S(2)}, u32[]{:S(2)}) collective-permute-start(bf16[640,128]{1,0:T(8,128)(2,1)S(1)} %get-tuple-element.44), channel_id=1, source_target_pairs={{0,8},{2,10},{4,12},{6,14},{8,16},{10,18},{12,20},{14,22},{16,24},... | collective-permute-start | bytes 491528 | tf_op jit(solution)/shard_map/ppermute | solution.py:394
  19.5 4.5 %collective-permute-start.8 = (bf16[640,128]{1,0:T(8,128)(2,1)S(1)}, bf16[640,128]{1,0:T(8,128)(2,1)S(1)}, u32[]{:S(2)}, u32[]{:S(2)}) collective-permute-start(bf16[640,128]{1,0:T(8,128)(2,1)S(1)} %get-tuple-element.44), channel_id=1, source_target_pairs={{0,16},{2,18},{4,20},{6,22},{8,24},{10,26},{12,28},{14,30},{1,17},... | collective-permute-start | bytes 491528 | tf_op jit(solution)/shard_map/ppermute | solution.py:394
  24.0 0.6 %collective-permute-start.4 = (bf16[256,128]{1,0:T(8,128)(2,1)S(1)}, bf16[256,128]{1,0:T(8,128)(2,1)S(1)}, u32[]{:S(2)}, u32[]{:S(2)}) collective-permute-start(bf16[256,128]{1,0:T(8,128)(2,1)S(1)} %get-tuple-element.41), channel_id=1, source_target_pairs={{0,2},{2,0},{4,6},{6,4},{8,10},{10,8},{12,14},{14,12},{16,18},{18,... | collective-permute-start | bytes 196616 | tf_op jit(solution)/shard_map/ppermute | solution.py:390
  24.6 1.3 %collective-permute-start.9 = (bf16[384,128]{1,0:T(8,128)(2,1)S(1)}, bf16[384,128]{1,0:T(8,128)(2,1)S(1)}, u32[]{:S(2)}, u32[]{:S(2)}) collective-permute-start(bf16[384,128]{1,0:T(8,128)(2,1)S(1)} %get-tuple-element.45), channel_id=1, source_target_pairs={{0,24},{2,26},{4,28},{6,30},{1,25},{3,27},{5,29},{7,31}} | collective-permute-start | bytes 294920 | tf_op jit(solution)/shard_map/ppermute | solution.py:394
  25.9 0.6 %collective-permute-start.5 = (bf16[256,128]{1,0:T(8,128)(2,1)S(1)}, bf16[256,128]{1,0:T(8,128)(2,1)S(1)}, u32[]{:S(2)}, u32[]{:S(2)}) collective-permute-start(bf16[256,128]{1,0:T(8,128)(2,1)S(1)} %get-tuple-element.42), channel_id=1, source_target_pairs={{0,4},{2,6},{4,0},{6,2},{8,12},{10,14},{12,8},{14,10},{16,20},{18,... | collective-permute-start | bytes 196616 | tf_op jit(solution)/shard_map/ppermute | solution.py:390
  26.5 2.2 %collective-permute-done.4.refs_4_.refs_0_ = bf16[256,128]{1,0:T(8,128)(2,1)S(1)} collective-permute-done((bf16[256,128]{1,0:T(8,128)(2,1)S(1)}, bf16[256,128]{1,0:T(8,128)(2,1)S(1)}, u32[]{:S(2)}, u32[]{:S(2)}) %collective-permute-start.4) | collective-permute-done | bytes 65568 | tf_op jit(solution)/shard_map/ppermute | solution.py:390
  28.9 1.4 %collective-permute-done.5.refs_5_.refs_1_ = bf16[256,128]{1,0:T(8,128)(2,1)S(1)} collective-permute-done((bf16[256,128]{1,0:T(8,128)(2,1)S(1)}, bf16[256,128]{1,0:T(8,128)(2,1)S(1)}, u32[]{:S(2)}, u32[]{:S(2)}) %collective-permute-start.5) | collective-permute-done | bytes 65568 | tf_op jit(solution)/shard_map/ppermute | solution.py:390
  30.3 3.5 %collective-permute-done.6.refs_6_.refs_2_ = bf16[256,128]{1,0:T(8,128)(2,1)S(1)} collective-permute-done((bf16[256,128]{1,0:T(8,128)(2,1)S(1)}, bf16[256,128]{1,0:T(8,128)(2,1)S(1)}, u32[]{:S(2)}, u32[]{:S(2)}) %collective-permute-start.6) | collective-permute-done | bytes 65568 | tf_op jit(solution)/shard_map/ppermute | solution.py:390
  33.9 1.3 %shard_map.112 = (bf16[768,128]{1,0:T(8,128)(2,1)S(1)}, bf16[768,128]{1,0:T(8,128)(2,1)S(1)}, bf16[768,128]{1,0:T(8,128)(2,1)S(1)}, bf16[768,128]{1,0:T(8,128)(2,1)S(1)}) custom-call(s32[2]{0:T(128)S(1)} %pad_add_fusion.place_ref, bf16[640,128]{1,0:T(8,128)(2,1)S(1)} %collective-permute-done.7.refs_0_, bf16[640,128]{1,0:T(8,128)(2,1)S(1)} %collective-permute-done.8.refs_1_, ...), custom_call_target="tpu_custom_call" | custom-call | flops 201326592 | bytes 1000000 | tf_op jit(solution)/shard_map/pallas_call | solution.py:20
  35.4 0.6 %collective-permute-start.11 = (bf16[768,128]{1,0:T(8,128)(2,1)S(1)}, bf16[768,128]{1,0:T(8,128)(2,1)S(1)}, u32[]{:S(2)}, u32[]{:S(2)}) collective-permute-start(bf16[768,128]{1,0:T(8,128)(2,1)S(1)} %get-tuple-element.49), channel_id=1, source_target_pairs={{0,4},{2,6},{4,0},{6,2},{8,12},{10,14},{12,8},{14,10},{16,20},{18,... | collective-permute-start | bytes 589832 | tf_op jit(solution)/shard_map/ppermute | solution.py:390
  36.0 2.7 %collective-permute-start.12 = (bf16[768,128]{1,0:T(8,128)(2,1)S(1)}, bf16[768,128]{1,0:T(8,128)(2,1)S(1)}, u32[]{:S(2)}, u32[]{:S(2)}) collective-permute-start(bf16[768,128]{1,0:T(8,128)(2,1)S(1)} %get-tuple-element.50), channel_id=1, source_target_pairs={{0,6},{2,4},{4,2},{6,0},{8,14},{10,12},{12,10},{14,8},{16,22},{18,... | collective-permute-start | bytes 589832 | tf_op jit(solution)/shard_map/ppermute | solution.py:390
  38.7 4.6 %shard_map.113 = (bf16[8,128,128]{2,1,0:T(8,128)(2,1)S(1)}, f32[8,128,128]{2,1,0:T(8,128)S(1)}, f32[8,128,1]{2,1,0:T(8,128)S(1)}, f32[8,128,1]{2,1,0:T(8,128)S(1)}) custom-call(bf16[128,2048]{1,0:T(8,128)(2,1)S(1)} %get-tuple-element.51.rows_ref, bf16[2048,1024]{1,0:T(8,128)(2,1)} %weight_hbm.1, f32[1,128]{1,0:T(1,128)S(1)} %get-tuple-element.52.gain_ref, ...), custom_call_target="tpu_custom_call" | custom-call | flops 1073741824 | bytes 16777216 | tf_op jit(solution)/shard_map/pallas_call | solution.py:20
  43.4 5.2 %shard_map.114 = (bf16[64,2048]{1,0:T(8,128)(2,1)S(1)}, bf16[64,2048]{1,0:T(8,128)(2,1)S(1)}) custom-call(s32[2]{0:T(128)S(1)} %pad_add_fusion.place_ref, s32[16]{0:T(128)S(1)} %bitcast.5, bf16[256,128]{1,0:T(8,128)(2,1)S(1)} %collective-permute-done.4.refs_4_.refs_0_, bf16[256,128]{1,0:T(8,128)(2,1)S(1)} %collective-permute-done.5.refs_5_.refs_1_, ...), custom_call_target="tpu_custom_call" | custom-call | flops 536870912 | bytes 4000000 | tf_op jit(solution)/shard_map/pallas_call | solution.py:20
  48.7 1.5 %collective-permute-done.13 = bf16[64,2048]{1,0:T(8,128)(2,1)S(1)} collective-permute-done((bf16[64,2048]{1,0:T(8,128)(2,1)S(1)}, bf16[64,2048]{1,0:T(8,128)(2,1)S(1)}, u32[]{:S(2)}, u32[]{:S(2)}) %collective-permute-start.13) | collective-permute-done | bytes 262176 | tf_op jit(solution)/shard_map/ppermute | solution.py:500
  50.2 0.8 %add.3 = bf16[64,2048]{1,0:T(8,128)(2,1)} add(bf16[64,2048]{1,0:T(8,128)(2,1)S(1)} %get-tuple-element.61, bf16[64,2048]{1,0:T(8,128)(2,1)S(1)} %collective-permute-done.13) | non-fusion elementwise | flops 131072 | bytes 786432 | tf_op jit(solution)/shard_map/add | solution.py:500
  (14 shorter events, 0.7 us)
Async XLA Ops:
  0.0 2.7 %collective-permute-start = (bf16[64,2048]{1,0:T(8,128)(2,1)}, bf16[64,2048]{1,0:T(8,128)(2,1)S(1)}, u32[]{:S(2)}, u32[]{:S(2)}) collective-permute-start(bf16[64,2048]{1,0:T(8,128)(2,1)} %mine_hbm.1), channel_id=1, source_target_pairs={{0,1},{1,0},{2,3},{3,2},{4,5},{5,4},{6,7},{7,6},{8,9},{9,8},{10,11... | collective-permute-start | bytes 786440 | tf_op jit(solution)/shard_map/ppermute | solution.py:374
  2.7 40.6 %copy-start = (s32[1,16]{1,0:T(1,128)S(1)}, s32[1,16]{1,0:T(1,128)}, u32[]{:S(2)}) copy-start(s32[1,16]{1,0:T(1,128)} %param.21) | copy-start | bytes 196
  5.7 5.3 %collective-permute-start.1 = (f32[128,128]{1,0:T(8,128)S(1)}, f32[128,128]{1,0:T(8,128)S(1)}, u32[]{:S(2)}, u32[]{:S(2)}) collective-permute-start(f32[128,128]{1,0:T(8,128)S(1)} %get-tuple-element.40.refs_0_), channel_id=1, source_target_pairs={{0,2},{2,0},{4,6},{6,4},{8,10},{10,8},{12,14},{14,12},{16,18},{18,... | collective-permute-start | bytes 196616 | tf_op jit(solution)/shard_map/ppermute | solution.py:390
  8.3 4.3 %collective-permute-start.2 = (f32[128,128]{1,0:T(8,128)S(1)}, f32[128,128]{1,0:T(8,128)S(1)}, u32[]{:S(2)}, u32[]{:S(2)}) collective-permute-start(f32[128,128]{1,0:T(8,128)S(1)} %get-tuple-element.40.refs_0_), channel_id=1, source_target_pairs={{0,4},{2,6},{4,0},{6,2},{8,12},{10,14},{12,8},{14,10},{16,20},{18,... | collective-permute-start | bytes 196616 | tf_op jit(solution)/shard_map/ppermute | solution.py:390
  9.8 5.2 %collective-permute-start.3 = (f32[128,128]{1,0:T(8,128)S(1)}, f32[128,128]{1,0:T(8,128)S(1)}, u32[]{:S(2)}, u32[]{:S(2)}) collective-permute-start(f32[128,128]{1,0:T(8,128)S(1)} %get-tuple-element.40.refs_0_), channel_id=1, source_target_pairs={{0,6},{2,4},{4,2},{6,0},{8,14},{10,12},{12,10},{14,8},{16,22},{18,... | collective-permute-start | bytes 196616 | tf_op jit(solution)/shard_map/ppermute | solution.py:390
  16.0 17.9 %collective-permute-start.7 = (bf16[640,128]{1,0:T(8,128)(2,1)S(1)}, bf16[640,128]{1,0:T(8,128)(2,1)S(1)}, u32[]{:S(2)}, u32[]{:S(2)}) collective-permute-start(bf16[640,128]{1,0:T(8,128)(2,1)S(1)} %get-tuple-element.44), channel_id=1, source_target_pairs={{0,8},{2,10},{4,12},{6,14},{8,16},{10,18},{12,20},{14,22},{16,24},... | collective-permute-start | bytes 491528 | tf_op jit(solution)/shard_map/ppermute | solution.py:394
  19.5 14.4 %collective-permute-start.8 = (bf16[640,128]{1,0:T(8,128)(2,1)S(1)}, bf16[640,128]{1,0:T(8,128)(2,1)S(1)}, u32[]{:S(2)}, u32[]{:S(2)}) collective-permute-start(bf16[640,128]{1,0:T(8,128)(2,1)S(1)} %get-tuple-element.44), channel_id=1, source_target_pairs={{0,16},{2,18},{4,20},{6,22},{8,24},{10,26},{12,28},{14,30},{1,17},... | collective-permute-start | bytes 491528 | tf_op jit(solution)/shard_map/ppermute | solution.py:394
  24.0 4.7 %collective-permute-start.4 = (bf16[256,128]{1,0:T(8,128)(2,1)S(1)}, bf16[256,128]{1,0:T(8,128)(2,1)S(1)}, u32[]{:S(2)}, u32[]{:S(2)}) collective-permute-start(bf16[256,128]{1,0:T(8,128)(2,1)S(1)} %get-tuple-element.41), channel_id=1, source_target_pairs={{0,2},{2,0},{4,6},{6,4},{8,10},{10,8},{12,14},{14,12},{16,18},{18,... | collective-permute-start | bytes 196616 | tf_op jit(solution)/shard_map/ppermute | solution.py:390
  24.6 9.3 %collective-permute-start.9 = (bf16[384,128]{1,0:T(8,128)(2,1)S(1)}, bf16[384,128]{1,0:T(8,128)(2,1)S(1)}, u32[]{:S(2)}, u32[]{:S(2)}) collective-permute-start(bf16[384,128]{1,0:T(8,128)(2,1)S(1)} %get-tuple-element.45), channel_id=1, source_target_pairs={{0,24},{2,26},{4,28},{6,30},{1,25},{3,27},{5,29},{7,31}} | collective-permute-start | bytes 294920 | tf_op jit(solution)/shard_map/ppermute | solution.py:394
  25.9 4.4 %collective-permute-start.5 = (bf16[256,128]{1,0:T(8,128)(2,1)S(1)}, bf16[256,128]{1,0:T(8,128)(2,1)S(1)}, u32[]{:S(2)}, u32[]{:S(2)}) collective-permute-start(bf16[256,128]{1,0:T(8,128)(2,1)S(1)} %get-tuple-element.42), channel_id=1, source_target_pairs={{0,4},{2,6},{4,0},{6,2},{8,12},{10,14},{12,8},{14,10},{16,20},{18,... | collective-permute-start | bytes 196616 | tf_op jit(solution)/shard_map/ppermute | solution.py:390
  28.7 5.2 %collective-permute-start.6 = (bf16[256,128]{1,0:T(8,128)(2,1)S(1)}, bf16[256,128]{1,0:T(8,128)(2,1)S(1)}, u32[]{:S(2)}, u32[]{:S(2)}) collective-permute-start(bf16[256,128]{1,0:T(8,128)(2,1)S(1)} %get-tuple-element.43), channel_id=1, source_target_pairs={{0,6},{2,4},{4,2},{6,0},{8,14},{10,12},{12,10},{14,8},{16,22},{18,... | collective-permute-start | bytes 196616 | tf_op jit(solution)/shard_map/ppermute | solution.py:390
  35.2 8.1 %collective-permute-start.10 = (bf16[768,128]{1,0:T(8,128)(2,1)S(1)}, bf16[768,128]{1,0:T(8,128)(2,1)S(1)}, u32[]{:S(2)}, u32[]{:S(2)}) collective-permute-start(bf16[768,128]{1,0:T(8,128)(2,1)S(1)} %get-tuple-element.48), channel_id=1, source_target_pairs={{0,2},{2,0},{4,6},{6,4},{8,10},{10,8},{12,14},{14,12},{16,18},{18,... | collective-permute-start | bytes 589832 | tf_op jit(solution)/shard_map/ppermute | solution.py:390
  35.4 7.9 %collective-permute-start.11 = (bf16[768,128]{1,0:T(8,128)(2,1)S(1)}, bf16[768,128]{1,0:T(8,128)(2,1)S(1)}, u32[]{:S(2)}, u32[]{:S(2)}) collective-permute-start(bf16[768,128]{1,0:T(8,128)(2,1)S(1)} %get-tuple-element.49), channel_id=1, source_target_pairs={{0,4},{2,6},{4,0},{6,2},{8,12},{10,14},{12,8},{14,10},{16,20},{18,... | collective-permute-start | bytes 589832 | tf_op jit(solution)/shard_map/ppermute | solution.py:390
  36.0 7.3 %collective-permute-start.12 = (bf16[768,128]{1,0:T(8,128)(2,1)S(1)}, bf16[768,128]{1,0:T(8,128)(2,1)S(1)}, u32[]{:S(2)}, u32[]{:S(2)}) collective-permute-start(bf16[768,128]{1,0:T(8,128)(2,1)S(1)} %get-tuple-element.50), channel_id=1, source_target_pairs={{0,6},{2,4},{4,2},{6,0},{8,14},{10,12},{12,10},{14,8},{16,22},{18,... | collective-permute-start | bytes 589832 | tf_op jit(solution)/shard_map/ppermute | solution.py:390
  48.6 1.6 %collective-permute-start.13 = (bf16[64,2048]{1,0:T(8,128)(2,1)S(1)}, bf16[64,2048]{1,0:T(8,128)(2,1)S(1)}, u32[]{:S(2)}, u32[]{:S(2)}) collective-permute-start(bf16[64,2048]{1,0:T(8,128)(2,1)S(1)} %get-tuple-element.62), channel_id=1, source_target_pairs={{0,1},{1,0},{2,3},{3,2},{4,5},{5,4},{6,7},{7,6},{8,9},{9,8},{10,11... | collective-permute-start | bytes 786440 | tf_op jit(solution)/shard_map/ppermute | solution.py:500

commit v5 on v4

--- a/solution.py
+++ b/solution.py
@@ -135,20 +135,24 @@
     turn_ref[...] = jnp.where(heads == lanes, 1.0, 0.0) - crossed[tokens:]
 
 
-def leave_kernel(group, place_ref, exit_ref, val_ref, *refs):
-    turn_refs, (long_ref, short_ref, starts_ref) = refs[:group], refs[group : group + 3]
-    near_refs, (turns_ref, seen_ref) = refs[group + 3 : -2], refs[-2:]
+def in_order(place_ref, turn_refs, turns_ref):
+    group = len(turn_refs)
     member = place_ref[0] % group
-    tokens, size = exit_ref.shape
     for step in range(group):
         turns_ref[source_of(member, step, group)] = turn_refs[step][...]
+    return member
+
+
+def leave_kernel(group, place_ref, exit_ref, *refs):
+    turn_refs, (long_ref, short_ref, starts_ref, turns_ref) = refs[:group], refs[group:]
+    member = in_order(place_ref, turn_refs, turns_ref)
+    tokens, size = exit_ref.shape
     own = exit_ref[...]
     keys = own
     product = None
     heads, lanes = iota2((size, size))
     starts_ref[0] = jnp.where(heads == lanes, 1.0, 0.0)
     for index in range(group):
-        seen_ref[index] = keys.astype(BF16)
         turn = turns_ref[index]
         product = turn if product is None else dot3(product, turn)
         if index:
@@ -159,16 +163,28 @@
     for ref in (long_ref, short_ref):
         ref[:tokens] = high
         ref[tokens : 2 * tokens] = low
-        ref[2 * tokens : 3 * tokens] = val_ref[...]
     high, low = split(product)
-    long_ref[3 * tokens : 3 * tokens + size] = high
-    long_ref[3 * tokens + size :] = low
-    for step in range(1, group):
-        near_refs[step - 1][:tokens] = seen_ref[target_of(member, step, group)]
-        near_refs[step - 1][tokens:] = val_ref[...]
-
-
-def query_kernel(rows_ref, weight_hbm, gain_ref, kn_ref, dirs_ref, coeff_ref, solved_ref, val_ref,
+    long_ref[2 * tokens : 2 * tokens + size] = high
+    long_ref[2 * tokens + size :] = low
+
+
+def bundle_kernel(group, place_ref, exit_ref, after_ref, *refs):
+    turn_refs, val_refs = refs[:group], refs[group : -group - 2]
+    bundle_refs, (turns_ref, seen_ref) = refs[-group - 2 : -2], refs[-2:]
+    member = in_order(place_ref, turn_refs, turns_ref)
+    tokens, size = exit_ref.shape
+    keys = exit_ref[...]
+    for index in range(group):
+        if index > 1:
+            keys = jnp.where(index - 1 > member, dot3(keys, turns_ref[index - 1]), exit_ref[...])
+        seen_ref[index] = keys.astype(BF16)
+    for step in range(group):
+        bundle_refs[step][:tokens] = seen_ref[target_of(member, step, group)]
+        for index, ref in enumerate(val_refs):
+            bundle_refs[step][(index + 1) * tokens : (index + 2) * tokens] = ref[...]
+
+
+def query_kernel(first, rows_ref, weight_hbm, gain_ref, kn_ref, dirs_ref, coeff_ref, solved_ref, val_ref,
                  moved_ref, weighted_ref, peak_ref, total_ref, weight_ref, sems):
     tokens, size = kn_ref.shape
     heads = moved_ref.shape[0]
@@ -176,7 +192,7 @@
     wide = weight_ref.shape[2]
     copies = [
         pltpu.make_async_copy(
-            weight_hbm.at[:, n * wide : (n + 1) * wide], weight_ref.at[n], sems.at[n]
+            weight_hbm.at[:, first + n * wide : first + (n + 1) * wide], weight_ref.at[n], sems.at[n]
         )
         for n in range(pieces)
     ]
@@ -229,26 +245,25 @@
         keys = ref[:tokens].astype(F32) + ref[tokens : 2 * tokens].astype(F32)
         if index:
             before = arrived[index - 1]
-            whole = before[3 * tokens : 3 * tokens + size].astype(F32)
-            whole = whole + before[3 * tokens + size :].astype(F32)
+            whole = before[2 * tokens : 2 * tokens + size].astype(F32)
+            whole = whole + before[2 * tokens + size :].astype(F32)
             product = whole if product is None else dot3(whole, product)
             keys = dot3(keys, product)
         brought.append(keys)
     keys = jnp.concatenate(brought, axis=0)
-    split_at = count * tokens
     for step in range(group):
         start = starts_ref[target_of(member, step, group)]
-        far_refs[step][:split_at] = dot3(keys, start).astype(BF16)
-        for index in range(count):
-            far_refs[step][split_at + index * tokens : split_at + (index + 1) * tokens] = arrived[
-                index
-            ][2 * tokens : 3 * tokens]
+        far_refs[step][...] = dot3(keys, start).astype(BF16)
 
 
 def attend_kernel(most, group, place_ref, mask_ref, *refs):
-    near_refs, far_refs = refs[: group - 1], refs[group - 1 : 2 * group - 1]
-    (moved_ref, weighted_ref, peak_ref, total_ref, out_hbm, away_ref, kept_ref, chosen_ref,
-     keys_ref, vals_ref, attended_ref, out_ref, sems, *state) = refs[2 * group - 1 :]
+    bundle_refs, far_refs = refs[:group], refs[group : 2 * group]
+    parts = (len(refs) - 2 * group - 9) // 4
+    owns, refs = [refs[2 * group + 4 * n : 2 * group + 4 * n + 4] for n in range(parts)], refs[
+        2 * group + 4 * parts :
+    ]
+    (out_hbm, away_ref, kept_ref, chosen_ref, keys_ref, vals_ref, attended_ref, out_ref,
+     sems) = refs
     pieces, _, wide = out_ref.shape
     copies = [
         pltpu.make_async_copy(
@@ -259,7 +274,7 @@
     for copy in copies:
         copy.start()
     place, core = place_ref[0], place_ref[1]
-    heads, tokens, size = moved_ref.shape
+    heads, tokens, size = owns[0][0].shape
     segments = mask_ref.shape[0]
     scaling = 1.0 / math.sqrt(size)
     mine, member = place // group, place % group
@@ -275,7 +290,7 @@
 
     found = lax.fori_loop(0, segments, pick, jnp.int32(0))
     chunk = keys_ref.shape[0] // tokens
-    lanes = lax.broadcasted_iota(jnp.int32, (tokens, chunk * tokens), 1)
+    lanes = lax.broadcasted_iota(jnp.int32, (heads * tokens, chunk * tokens), 1)
 
     def collect(turn):
         for slot in range(chunk):
@@ -284,7 +299,7 @@
             used = index < found
             segment = jnp.where(used, chosen_ref[index], 0)
             whose, distance = segment % group, mine - segment // group
-            before = jnp.maximum(distance - 1, 0) * tokens
+            before = pl.multiple_of(jnp.maximum(distance - 1, 0) * tokens, tokens)
 
             @pl.when(jnp.logical_not(used))
             def _():
@@ -294,25 +309,22 @@
             for step in range(group):
                 here = used & (whose == source_of(member, step, group))
 
+                @pl.when(here)
+                def _():
+                    after = pl.multiple_of((distance + 1) * tokens, tokens)
+                    vals_ref[part, :] = bundle_refs[step][pl.ds(after, tokens), :]
+
                 @pl.when(here & (distance > 0))
                 def _():
-                    far = far_refs[step]
-                    middle = far.shape[0] // 2
-                    keys_ref[part, :] = far[pl.ds(pl.multiple_of(before, tokens), tokens), :]
-                    vals_ref[part, :] = far[
-                        pl.ds(pl.multiple_of(middle + before, tokens), tokens), :
-                    ]
-
-                if step:
-
-                    @pl.when(here & (distance == 0))
-                    def _():
-                        keys_ref[part, :] = near_refs[step - 1][:tokens]
-                        vals_ref[part, :] = near_refs[step - 1][tokens:]
-
-    def advance(head, turn, peak, total, weighted):
+                    keys_ref[part, :] = far_refs[step][pl.ds(before, tokens), :]
+
+                @pl.when(here & (distance == 0))
+                def _():
+                    keys_ref[part, :] = bundle_refs[step][:tokens]
+
+    def advance(moved, turn, peak, total, weighted):
         scores = lax.dot_general(
-            moved_ref[head], keys_ref[...], (((1,), (1,)), ((), ())), preferred_element_type=F32
+            moved, keys_ref[...], (((1,), (1,)), ((), ())), preferred_element_type=F32
         )
         scores = jnp.where(lanes < (found - turn * chunk) * tokens, scores * scaling, NEGATIVE)
         new_peak = jnp.maximum(peak, jnp.max(scores, axis=1, keepdims=True))
@@ -325,37 +337,33 @@
         return new_peak, total, weighted
 
     half = kept_ref.shape[0]
-
-    def finish(head, total, weighted):
-        done = (weighted / total).astype(BF16)
-        for index in range(tokens // half):
-            at = pl.multiple_of(jnp.where(index == core, half, 0), half)
-            attended_ref[pl.ds(at, half), head * size : (head + 1) * size] = done[
-                index * half : (index + 1) * half
-            ]
-
     turns = most // chunk
     if turns == 1:
         collect(0)
-        for head in range(heads):
-            _, total, weighted = advance(
-                head, 0, peak_ref[head], total_ref[head], weighted_ref[head]
-            )
-            finish(head, total, weighted)
-    else:
-        run_p, run_t, run_w = state
-        run_p[...], run_t[...], run_w[...] = peak_ref[...], total_ref[...], weighted_ref[...]
-
-        @pl.loop(0, turns)
-        def _(turn):
-            collect(turn)
-            for head in range(heads):
-                run_p[head], run_t[head], run_w[head] = advance(
-                    head, turn, run_p[head], run_t[head], run_w[head]
-                )
-
-        for head in range(heads):
-            finish(head, run_t[head], run_w[head])
+    for number, (moved_ref, weighted_ref, peak_ref, total_ref) in enumerate(owns):
+        moved = moved_ref[...].reshape(heads * tokens, size)
+        state = (
+            peak_ref[...].reshape(heads * tokens, 1),
+            total_ref[...].reshape(heads * tokens, 1),
+            weighted_ref[...].reshape(heads * tokens, size),
+        )
+        if turns == 1:
+            _, total, weighted = advance(moved, 0, *state)
+        else:
+
+            def step_of(turn, state, moved=moved):
+                collect(turn)
+                return advance(moved, turn, *state)
+
+            _, total, weighted = lax.fori_loop(0, turns, step_of, state)
+        done = (weighted * (1.0 / total)).astype(BF16)
+        for h in range(heads):
+            columns = slice((number * heads + h) * size, (number * heads + h + 1) * size)
+            for index in range(tokens // half):
+                at = pl.multiple_of(jnp.where(index == core, half, 0), half)
+                attended_ref[pl.ds(at, half), columns] = done[
+                    h * tokens + index * half : h * tokens + (index + 1) * half
+                ]
     for n in range(pieces):
         copies[n].wait()
         result = jnp.dot(attended_ref[...], out_ref[n], preferred_element_type=F32).astype(BF16)
@@ -422,51 +430,66 @@
         moved=8 * width * size,
     )
     turns = [turn] + [to_member(turn, step) for step in range(1, group)]
-    long, short, starts, *near = call(
+    line = [val] + [to_later_group(val, d) for d in range(1, groups)]
+    long, short, starts = call(
         functools.partial(leave_kernel, group),
         [
-            shaped((3 * tokens + 2 * size, size), BF16),
-            shaped((3 * tokens, size), BF16),
+            shaped((2 * tokens + 2 * size, size), BF16),
+            shaped((2 * tokens, size), BF16),
             shaped((group, size, size), F32),
-        ]
-        + [shaped((2 * tokens, size), BF16)] * (group - 1),
-        (place, exit_keys, val, *turns),
-        in_specs=[smem] + [vmem] * (2 + group),
+        ],
+        (place, exit_keys, *turns),
+        in_specs=[smem] + [vmem] * (1 + group),
+        scratch=(pltpu.VMEM((group, size, size), F32),),
+        flops=12 * group * size**3,
+        moved=10**6,
+    )
+    arrived = [
+        to_later_group(long if d < groups - 1 else short, d) for d in range(1, groups)
+    ]
+    bundle = call(
+        functools.partial(bundle_kernel, group),
+        [shaped(((1 + groups) * tokens, size), BF16)] * group,
+        (place, exit_keys, starts, *turns, *line),
+        in_specs=[smem, vmem, anywhere] + [vmem] * (group + groups),
         scratch=(
             pltpu.VMEM((group, size, size), F32),
             pltpu.VMEM((group, tokens, size), BF16),
         ),
         flops=12 * group * size**3,
         moved=10**6,
-    )
-    arrived = [
-        to_later_group(long if d < groups - 1 else short, d) for d in range(1, groups)
-    ]
-    near = [to_member(near[step - 1], step) for step in range(1, group)]
-    pieces = math.gcd(heads, 4)
-    moved, weighted, peak, total = call(
-        query_kernel,
-        (
-            shaped((heads, tokens, size), BF16),
-            shaped((heads, tokens, size), F32),
-            shaped((heads, tokens, 1), F32),
-            shaped((heads, tokens, 1), F32),
-        ),
-        (rows, in_hbm(w_query), query_gain, kn, dirs, coeff, solved, val),
-        in_specs=[vmem, hbm] + [vmem] * 6,
-        scratch=(
-            pltpu.VMEM((pieces, width, w_query.shape[1] // pieces), BF16),
-            pltpu.SemaphoreType.DMA((pieces,)),
-        ),
-        flops=4 * tokens * width * heads * size,
-        moved=8 * width * heads * size,
-        limit=16,
-    )
+        limit=8 + group * groups // 4,
+    )
+    bundle = [bundle[0]] + [to_member(bundle[step], step) for step in range(1, group)]
+    calls = math.gcd(heads, 2)
+    each = heads // calls
+    pieces = math.gcd(each, 2)
+    owns = [
+        call(
+            functools.partial(query_kernel, number * each * size),
+            (
+                shaped((each, tokens, size), BF16),
+                shaped((each, tokens, size), F32),
+                shaped((each, tokens, 1), F32),
+                shaped((each, tokens, 1), F32),
+            ),
+            (rows, in_hbm(w_query), query_gain, kn, dirs, coeff, solved, val),
+            in_specs=[vmem, hbm] + [vmem] * 6,
+            scratch=(
+                pltpu.VMEM((pieces, width, each * size // pieces), BF16),
+                pltpu.SemaphoreType.DMA((pieces,)),
+            ),
+            flops=4 * tokens * width * each * size,
+            moved=8 * width * each * size,
+            limit=12,
+        )
+        for number in range(calls)
+    ]
     far = call(
         functools.partial(arrive_kernel, groups - 1, group, tokens),
-        [shaped((2 * (groups - 1) * tokens, size), BF16)] * group,
-        (place, *arrived, starts, *near),
-        in_specs=[smem] + [vmem] * groups + [anywhere] * (group - 1),
+        [shaped(((groups - 1) * tokens, size), BF16)] * group,
+        (place, *arrived, starts, owns[0][2]),
+        in_specs=[smem] + [vmem] * groups + [anywhere],
         flops=6 * groups * group * size**3,
         moved=10**6,
         limit=8 + group * groups // 4,
@@ -484,18 +507,18 @@
         pltpu.VMEM((pieces, heads * size, width_out // pieces), BF16),
         pltpu.SemaphoreType.DMA((pieces,)),
     ]
-    if most > chunk:
-        scratch += [pltpu.VMEM((heads, tokens, 1), F32)] * 2
-        scratch += [pltpu.VMEM((heads, tokens, size), F32)]
     away, kept = call(
         functools.partial(attend_kernel, most, group),
         [shaped((half, width_out), BF16)] * 2,
-        (place, block_mask[0], *near, *far, moved, weighted, peak, total, in_hbm(w_out)),
-        in_specs=[smem] * 2 + [vmem] * (2 * group - 1 + 4) + [hbm],
+        (
+            place, block_mask[0], *bundle, *far, *(array for own in owns for array in own),
+            in_hbm(w_out),
+        ),
+        in_specs=[smem] * 2 + [vmem] * (2 * group + 4 * calls) + [hbm],
         scratch=scratch,
         flops=2 * tokens * width_out * heads * size,
         moved=4 * 10**6,
-        limit=16 + group * groups // 4,
+        limit=20 + group * groups // 4,
     )
     return kept + lax.ppermute(away, "head", [(0, 1), (1, 0)])
 

time: 51.2 us -> 56.9 us (1.11)
  starting transfers between devices: 18.9 us -> 32.3 us
  waiting for transfers between devices: 13.8 us -> 3.42 us
  Pallas kernels: 16.7 us -> 19.1 us
    ppermute x9, waiting for transfers between devices: 12.3 us -> 1.08 us  [to_member(): return lax.ppermute(value, 'ctx', pairs)]
    ppermute x3 -> x6, starting transfers between devices: 9.27 us -> 19.5 us  [to_later_group(): lax.ppermute(value, 'ctx', [(s, s + step) for s in range(segments - step)])]
    ppermute x9, starting transfers between devices: 9.07 us -> 12.3 us  [to_member(): return lax.ppermute(value, 'ctx', pairs)]
    pallas_call x6 -> x8, Pallas kernels: 16.7 us -> 19.1 us  [call(): pl.pallas_call(kernel, out_shape=out_shape, in_specs=in_specs or [vmem] *...]
    ppermute x3 -> x6, waiting for transfers between devices: 0.01 us -> 0.82 us  [to_later_group(): lax.ppermute(value, 'ctx', [(s, s + step) for s in range(segments - step)])]
  transfers between devices with their start and end apart: 14 -> 17, of which waited for: 7 -> 4; matrix products, arithmetic and copies ran while one was open for 0% -> 0% of each run, Pallas kernels for 12% -> 17%
where the time goes in v5:
time: 56.9 us; the launch traced here: 56.6 us
  starting transfers between devices  32.3 us (57%)
  Pallas kernels  19.1 us (34%)
  waiting for transfers between devices  3.42 us (6%)
  between operations  0.87 us (2%)
  other arithmetic  0.84 us (1%)
    ppermute x6, starting transfers between devices, to_later_group(): lax.ppermute(value, 'ctx', [(s, s + step) for s in range(segments - step)])  19.5 us
    pallas_call x8, Pallas kernels, call(): pl.pallas_call(kernel, out_shape=out_shape, in_specs=in_specs or [vmem] *...  19.1 us
    ppermute x9, starting transfers between devices, to_member(): return lax.ppermute(value, 'ctx', pairs)  12.3 us
    ppermute x1, waiting for transfers between devices, body(): return kept + lax.ppermute(away, 'head', [(0, 1), (1, 0)])  1.52 us
  transfers between devices with their start and end apart: 17, of which 4 were waited for; matrix products, arithmetic and copies ran while one was open for 0% of the time, Pallas kernels for 17%

profile of v5, /device:TPU:0, one launch (start us, length us, event | category | flops | bytes accessed | tf_op | source)
XLA Modules:
  0.0 56.6 jit_solution(12365531163200640697)
XLA Ops:
  1.1 1.5 %shard_map.109 = (bf16[2048,384]{1,0:T(8,128)(2,1)S(1)}, bf16[1,2048]{1,0:T(2,128)(2,1)S(1)}, f32[1,128]{1,0:T(1,128)S(1)}, f32[1,128]{1,0:T(1,128)S(1)}, bf16[64,2048]{1,0:T(8,128)(2,1)S(1)}) custom-call(bf16[2048,128]{1,0:T(8,128)(2,1)} %key_hbm.1, bf16[2048,128]{1,0:T(8,128)(2,1)} %dir_hbm.1, bf16[2048,128]{1,0:T(8,128)(2,1)} %value_hbm.1, ...), custom_call_target="tpu_custom_call" | custom-call | bytes 3145728 | tf_op jit(solution)/shard_map/pallas_call | solution.py:20
  2.7 3.0 %shard_map.110 = (bf16[128,2048]{1,0:T(8,128)(2,1)S(1)}, f32[128,128]{1,0:T(8,128)S(1)}, bf16[128,128]{1,0:T(8,128)(2,1)S(1)}, f32[128,128]{1,0:T(8,128)S(1)}, f...) custom-call(s32[2]{0:T(128)S(1)} %pad_add_fusion.place_ref, ...), custom_call_target="tpu_custom_call" | custom-call | flops 201326592 | bytes 2097152 | tf_op jit(solution)/shard_map/pallas_call | solution.py:20
  5.7 2.6 %collective-permute-start.1 = (f32[128,128]{1,0:T(8,128)S(1)}, f32[128,128]{1,0:T(8,128)S(1)}, u32[]{:S(2)}, u32[]{:S(2)}) collective-permute-start(f32[128,128]{1,0:T(8,128)S(1)} %get-tuple-element.44.refs_0_), channel_id=1, source_target_pairs={{0,2},{2,0},{4,6},{6,4},{8,10},{10,8},{12,14},{14,12},{16,18},{18,... | collective-permute-start | bytes 196616 | tf_op jit(solution)/shard_map/ppermute | solution.py:398
  8.3 1.5 %collective-permute-start.2 = (f32[128,128]{1,0:T(8,128)S(1)}, f32[128,128]{1,0:T(8,128)S(1)}, u32[]{:S(2)}, u32[]{:S(2)}) collective-permute-start(f32[128,128]{1,0:T(8,128)S(1)} %get-tuple-element.44.refs_0_), channel_id=1, source_target_pairs={{0,4},{2,6},{4,0},{6,2},{8,12},{10,14},{12,8},{14,10},{16,20},{18,... | collective-permute-start | bytes 196616 | tf_op jit(solution)/shard_map/ppermute | solution.py:398
  9.8 3.9 %collective-permute-start.4 = (bf16[128,128]{1,0:T(8,128)(2,1)S(1)}, bf16[128,128]{1,0:T(8,128)(2,1)S(1)}, u32[]{:S(2)}, u32[]{:S(2)}) collective-permute-start(bf16[128,128]{1,0:T(8,128)(2,1)S(1)} %get-tuple-element.46.refs_4_.val_ref), channel_id=1, source_target_pairs={{0,8},{2,10},{4,12},{6,14},{8,16},{10,18},{12,20},{14,22},{16,24},... | collective-permute-start | bytes 98312 | tf_op jit(solution)/shard_map/ppermute | solution.py:402
  13.7 4.5 %collective-permute-start.5 = (bf16[128,128]{1,0:T(8,128)(2,1)S(1)}, bf16[128,128]{1,0:T(8,128)(2,1)S(1)}, u32[]{:S(2)}, u32[]{:S(2)}) collective-permute-start(bf16[128,128]{1,0:T(8,128)(2,1)S(1)} %get-tuple-element.46.refs_4_.val_ref), channel_id=1, source_target_pairs={{0,16},{2,18},{4,20},{6,22},{8,24},{10,26},{12,28},{14,30},{1,17},... | collective-permute-start | bytes 98312 | tf_op jit(solution)/shard_map/ppermute | solution.py:402
  18.3 1.3 %collective-permute-start.6 = (bf16[128,128]{1,0:T(8,128)(2,1)S(1)}, bf16[128,128]{1,0:T(8,128)(2,1)S(1)}, u32[]{:S(2)}, u32[]{:S(2)}) collective-permute-start(bf16[128,128]{1,0:T(8,128)(2,1)S(1)} %get-tuple-element.46.refs_4_.val_ref), channel_id=1, source_target_pairs={{0,24},{2,26},{4,28},{6,30},{1,25},{3,27},{5,29},{7,31}} | collective-permute-start | bytes 98312 | tf_op jit(solution)/shard_map/ppermute | solution.py:402
  19.6 1.0 %shard_map.111 = (bf16[512,128]{1,0:T(8,128)(2,1)S(1)}, bf16[256,128]{1,0:T(8,128)(2,1)S(1)}, f32[4,128,128]{2,1,0:T(8,128)S(1)}) custom-call(s32[2]{0:T(128)S(1)} %pad_add_fusion.place_ref, f32[128,128]{1,0:T(8,128)S(1)} %get-tuple-element.43.exit_ref, f32[128,128]{1,0:T(8,128)S(1)} %get-tuple-element.44.refs_0_, ...), custom_call_target="tpu_custom_call" | custom-call | flops 100663296 | bytes 1000000 | tf_op jit(solution)/shard_map/pallas_call | solution.py:20
  21.1 0.9 %shard_map.112 = (bf16[640,128]{1,0:T(8,128)(2,1)S(1)}, bf16[640,128]{1,0:T(8,128)(2,1)S(1)}, bf16[640,128]{1,0:T(8,128)(2,1)S(1)}, bf16[640,128]{1,0:T(8,128)(2,1)S(1)}) custom-call(s32[2]{0:T(128)S(1)} %pad_add_fusion.place_ref, f32[128,128]{1,0:T(8,128)S(1)} %get-tuple-element.43.exit_ref, f32[4,128,128]{2,1,0:T(8,128)S(1)} %get-tuple-element.45.after_ref.refs_3_, ...), custom_call_target="tpu_custom_call" | custom-call | flops 100663296 | bytes 1000000 | tf_op jit(solution)/shard_map/pallas_call | solution.py:20
  22.0 1.6 %collective-permute-start.7 = (bf16[640,128]{1,0:T(8,128)(2,1)S(1)}, bf16[640,128]{1,0:T(8,128)(2,1)S(1)}, u32[]{:S(2)}, u32[]{:S(2)}) collective-permute-start(bf16[640,128]{1,0:T(8,128)(2,1)S(1)} %get-tuple-element.48), channel_id=1, source_target_pairs={{0,2},{2,0},{4,6},{6,4},{8,10},{10,8},{12,14},{14,12},{16,18},{18,... | collective-permute-start | bytes 491528 | tf_op jit(solution)/shard_map/ppermute | solution.py:398
  23.6 1.3 %collective-permute-start.10 = (bf16[512,128]{1,0:T(8,128)(2,1)S(1)}, bf16[512,128]{1,0:T(8,128)(2,1)S(1)}, u32[]{:S(2)}, u32[]{:S(2)}) collective-permute-start(bf16[512,128]{1,0:T(8,128)(2,1)S(1)} %get-tuple-element.51), channel_id=1, source_target_pairs={{0,8},{2,10},{4,12},{6,14},{8,16},{10,18},{12,20},{14,22},{16,24},... | collective-permute-start | bytes 393224 | tf_op jit(solution)/shard_map/ppermute | solution.py:402
  24.9 7.2 %collective-permute-start.11 = (bf16[512,128]{1,0:T(8,128)(2,1)S(1)}, bf16[512,128]{1,0:T(8,128)(2,1)S(1)}, u32[]{:S(2)}, u32[]{:S(2)}) collective-permute-start(bf16[512,128]{1,0:T(8,128)(2,1)S(1)} %get-tuple-element.51), channel_id=1, source_target_pairs={{0,16},{2,18},{4,20},{6,22},{8,24},{10,26},{12,28},{14,30},{1,17},... | collective-permute-start | bytes 393224 | tf_op jit(solution)/shard_map/ppermute | solution.py:402
  32.1 1.3 %collective-permute-start.12 = (bf16[256,128]{1,0:T(8,128)(2,1)S(1)}, bf16[256,128]{1,0:T(8,128)(2,1)S(1)}, u32[]{:S(2)}, u32[]{:S(2)}) collective-permute-start(bf16[256,128]{1,0:T(8,128)(2,1)S(1)} %get-tuple-element.52), channel_id=1, source_target_pairs={{0,24},{2,26},{4,28},{6,30},{1,25},{3,27},{5,29},{7,31}} | collective-permute-start | bytes 196616 | tf_op jit(solution)/shard_map/ppermute | solution.py:402
  33.4 1.6 %collective-permute-start.8 = (bf16[640,128]{1,0:T(8,128)(2,1)S(1)}, bf16[640,128]{1,0:T(8,128)(2,1)S(1)}, u32[]{:S(2)}, u32[]{:S(2)}) collective-permute-start(bf16[640,128]{1,0:T(8,128)(2,1)S(1)} %get-tuple-element.49), channel_id=1, source_target_pairs={{0,4},{2,6},{4,0},{6,2},{8,12},{10,14},{12,8},{14,10},{16,20},{18,... | collective-permute-start | bytes 491528 | tf_op jit(solution)/shard_map/ppermute | solution.py:398
  35.3 1.5 %collective-permute-start.9 = (bf16[640,128]{1,0:T(8,128)(2,1)S(1)}, bf16[640,128]{1,0:T(8,128)(2,1)S(1)}, u32[]{:S(2)}, u32[]{:S(2)}) collective-permute-start(bf16[640,128]{1,0:T(8,128)(2,1)S(1)} %get-tuple-element.50), channel_id=1, source_target_pairs={{0,6},{2,4},{4,2},{6,0},{8,14},{10,12},{12,10},{14,8},{16,22},{18,... | collective-permute-start | bytes 491528 | tf_op jit(solution)/shard_map/ppermute | solution.py:398
  36.8 2.9 %shard_map.113 = (bf16[4,128,128]{2,1,0:T(8,128)(2,1)S(1)}, f32[4,128,128]{2,1,0:T(8,128)S(1)}, f32[4,128,1]{2,1,0:T(8,128)S(1)}, f32[4,128,1]{2,1,0:T(8,128)S(1)}) custom-call(bf16[128,2048]{1,0:T(8,128)(2,1)S(1)} %get-tuple-element.53.rows_ref, bf16[2048,1024]{1,0:T(8,128)(2,1)} %weight_hbm.3, f32[1,128]{1,0:T(1,128)S(1)} %get-tuple-element.54.gain_ref, ...), custom_call_target="tpu_custom_call" | custom-call | flops 536870912 | bytes 8388608 | tf_op jit(solution)/shard_map/pallas_call | solution.py:20
  39.7 1.3 %shard_map.114 = (bf16[384,128]{1,0:T(8,128)(2,1)S(1)}, bf16[384,128]{1,0:T(8,128)(2,1)S(1)}, bf16[384,128]{1,0:T(8,128)(2,1)S(1)}, bf16[384,128]{1,0:T(8,128)(2,1)S(1)}) custom-call(s32[2]{0:T(128)S(1)} %pad_add_fusion.place_ref, bf16[512,128]{1,0:T(8,128)(2,1)S(1)} %collective-permute-done.10.refs_0_, ...), custom_call_target="tpu_custom_call" | custom-call | flops 201326592 | bytes 1000000 | tf_op jit(solution)/shard_map/pallas_call | solution.py:20
  41.1 1.6 %collective-permute-start.13 = (bf16[384,128]{1,0:T(8,128)(2,1)S(1)}, bf16[384,128]{1,0:T(8,128)(2,1)S(1)}, u32[]{:S(2)}, u32[]{:S(2)}) collective-permute-start(bf16[384,128]{1,0:T(8,128)(2,1)S(1)} %get-tuple-element.61), channel_id=1, source_target_pairs={{0,2},{2,0},{4,6},{6,4},{8,10},{10,8},{12,14},{14,12},{16,18},{18,... | collective-permute-start | bytes 294920 | tf_op jit(solution)/shard_map/ppermute | solution.py:398
  43.1 1.5 %collective-permute-start.15 = (bf16[384,128]{1,0:T(8,128)(2,1)S(1)}, bf16[384,128]{1,0:T(8,128)(2,1)S(1)}, u32[]{:S(2)}, u32[]{:S(2)}) collective-permute-start(bf16[384,128]{1,0:T(8,128)(2,1)S(1)} %get-tuple-element.63), channel_id=1, source_target_pairs={{0,6},{2,4},{4,2},{6,0},{8,14},{10,12},{12,10},{14,8},{16,22},{18,... | collective-permute-start | bytes 294920 | tf_op jit(solution)/shard_map/ppermute | solution.py:398
  44.6 2.9 %shard_map.115 = (bf16[4,128,128]{2,1,0:T(8,128)(2,1)S(1)}, f32[4,128,128]{2,1,0:T(8,128)S(1)}, f32[4,128,1]{2,1,0:T(8,128)S(1)}, f32[4,128,1]{2,1,0:T(8,128)S(1)}) custom-call(bf16[128,2048]{1,0:T(8,128)(2,1)S(1)} %get-tuple-element.53.rows_ref, bf16[2048,1024]{1,0:T(8,128)(2,1)} %weight_hbm.3, f32[1,128]{1,0:T(1,128)S(1)} %get-tuple-element.54.gain_ref, ...), custom_call_target="tpu_custom_call" | custom-call | flops 536870912 | bytes 8388608 | tf_op jit(solution)/shard_map/pallas_call | solution.py:20
  47.6 1.1 %collective-permute-done.15.refs_7_ = bf16[384,128]{1,0:T(8,128)(2,1)S(1)} collective-permute-done((bf16[384,128]{1,0:T(8,128)(2,1)S(1)}, bf16[384,128]{1,0:T(8,128)(2,1)S(1)}, u32[]{:S(2)}, u32[]{:S(2)}) %collective-permute-start.15) | collective-permute-done | bytes 98336 | tf_op jit(solution)/shard_map/ppermute | solution.py:398
  48.6 5.6 %shard_map.116 = (bf16[64,2048]{1,0:T(8,128)(2,1)S(1)}, bf16[64,2048]{1,0:T(8,128)(2,1)S(1)}) custom-call(s32[2]{0:T(128)S(1)} %pad_add_fusion.place_ref, s32[16]{0:T(128)S(1)} %bitcast.5, bf16[640,128]{1,0:T(8,128)(2,1)S(1)} %get-tuple-element.47.refs_0_, bf16[640,128]{1,0:T(8,128)(2,1)S(1)} %collective-permute-done.7.refs_1_, ...), custom_call_target="tpu_custom_call" | custom-call | flops 536870912 | bytes 4000000 | tf_op jit(solution)/shard_map/pallas_call | solution.py:20
  54.3 1.5 %collective-permute-done.16 = bf16[64,2048]{1,0:T(8,128)(2,1)S(1)} collective-permute-done((bf16[64,2048]{1,0:T(8,128)(2,1)S(1)}, bf16[64,2048]{1,0:T(8,128)(2,1)S(1)}, u32[]{:S(2)}, u32[]{:S(2)}) %collective-permute-start.16) | collective-permute-done | bytes 262176 | tf_op jit(solution)/shard_map/ppermute | solution.py:523
  55.8 0.8 %add.3 = bf16[64,2048]{1,0:T(8,128)(2,1)} add(bf16[64,2048]{1,0:T(8,128)(2,1)S(1)} %get-tuple-element.71, bf16[64,2048]{1,0:T(8,128)(2,1)S(1)} %collective-permute-done.16) | non-fusion elementwise | flops 131072 | bytes 786432 | tf_op jit(solution)/shard_map/add | solution.py:523
  (22 shorter events, 2.0 us)
Async XLA Ops:
  0.0 2.7 %collective-permute-start = (bf16[64,2048]{1,0:T(8,128)(2,1)}, bf16[64,2048]{1,0:T(8,128)(2,1)S(1)}, u32[]{:S(2)}, u32[]{:S(2)}) collective-permute-start(bf16[64,2048]{1,0:T(8,128)(2,1)} %mine_hbm.1), channel_id=1, source_target_pairs={{0,1},{1,0},{2,3},{3,2},{4,5},{5,4},{6,7},{7,6},{8,9},{9,8},{10,11... | collective-permute-start | bytes 786440 | tf_op jit(solution)/shard_map/ppermute | solution.py:382
  5.7 12.5 %collective-permute-start.1 = (f32[128,128]{1,0:T(8,128)S(1)}, f32[128,128]{1,0:T(8,128)S(1)}, u32[]{:S(2)}, u32[]{:S(2)}) collective-permute-start(f32[128,128]{1,0:T(8,128)S(1)} %get-tuple-element.44.refs_0_), channel_id=1, source_target_pairs={{0,2},{2,0},{4,6},{6,4},{8,10},{10,8},{12,14},{14,12},{16,18},{18,... | collective-permute-start | bytes 196616 | tf_op jit(solution)/shard_map/ppermute | solution.py:398
  8.3 11.3 %collective-permute-start.2 = (f32[128,128]{1,0:T(8,128)S(1)}, f32[128,128]{1,0:T(8,128)S(1)}, u32[]{:S(2)}, u32[]{:S(2)}) collective-permute-start(f32[128,128]{1,0:T(8,128)S(1)} %get-tuple-element.44.refs_0_), channel_id=1, source_target_pairs={{0,4},{2,6},{4,0},{6,2},{8,12},{10,14},{12,8},{14,10},{16,20},{18,... | collective-permute-start | bytes 196616 | tf_op jit(solution)/shard_map/ppermute | solution.py:398
  9.8 9.8 %collective-permute-start.3 = (f32[128,128]{1,0:T(8,128)S(1)}, f32[128,128]{1,0:T(8,128)S(1)}, u32[]{:S(2)}, u32[]{:S(2)}) collective-permute-start(f32[128,128]{1,0:T(8,128)S(1)} %get-tuple-element.44.refs_0_), channel_id=1, source_target_pairs={{0,6},{2,4},{4,2},{6,0},{8,14},{10,12},{12,10},{14,8},{16,22},{18,... | collective-permute-start | bytes 196616 | tf_op jit(solution)/shard_map/ppermute | solution.py:398
  9.8 10.8 %collective-permute-start.4 = (bf16[128,128]{1,0:T(8,128)(2,1)S(1)}, bf16[128,128]{1,0:T(8,128)(2,1)S(1)}, u32[]{:S(2)}, u32[]{:S(2)}) collective-permute-start(bf16[128,128]{1,0:T(8,128)(2,1)S(1)} %get-tuple-element.46.refs_4_.val_ref), channel_id=1, source_target_pairs={{0,8},{2,10},{4,12},{6,14},{8,16},{10,18},{12,20},{14,22},{16,24},... | collective-permute-start | bytes 98312 | tf_op jit(solution)/shard_map/ppermute | solution.py:402
  13.7 6.9 %collective-permute-start.5 = (bf16[128,128]{1,0:T(8,128)(2,1)S(1)}, bf16[128,128]{1,0:T(8,128)(2,1)S(1)}, u32[]{:S(2)}, u32[]{:S(2)}) collective-permute-start(bf16[128,128]{1,0:T(8,128)(2,1)S(1)} %get-tuple-element.46.refs_4_.val_ref), channel_id=1, source_target_pairs={{0,16},{2,18},{4,20},{6,22},{8,24},{10,26},{12,28},{14,30},{1,17},... | collective-permute-start | bytes 98312 | tf_op jit(solution)/shard_map/ppermute | solution.py:402
  18.3 2.9 %collective-permute-start.6 = (bf16[128,128]{1,0:T(8,128)(2,1)S(1)}, bf16[128,128]{1,0:T(8,128)(2,1)S(1)}, u32[]{:S(2)}, u32[]{:S(2)}) collective-permute-start(bf16[128,128]{1,0:T(8,128)(2,1)S(1)} %get-tuple-element.46.refs_4_.val_ref), channel_id=1, source_target_pairs={{0,24},{2,26},{4,28},{6,30},{1,25},{3,27},{5,29},{7,31}} | collective-permute-start | bytes 98312 | tf_op jit(solution)/shard_map/ppermute | solution.py:402
  22.0 21.1 %collective-permute-start.7 = (bf16[640,128]{1,0:T(8,128)(2,1)S(1)}, bf16[640,128]{1,0:T(8,128)(2,1)S(1)}, u32[]{:S(2)}, u32[]{:S(2)}) collective-permute-start(bf16[640,128]{1,0:T(8,128)(2,1)S(1)} %get-tuple-element.48), channel_id=1, source_target_pairs={{0,2},{2,0},{4,6},{6,4},{8,10},{10,8},{12,14},{14,12},{16,18},{18,... | collective-permute-start | bytes 491528 | tf_op jit(solution)/shard_map/ppermute | solution.py:398
  23.6 16.1 %collective-permute-start.10 = (bf16[512,128]{1,0:T(8,128)(2,1)S(1)}, bf16[512,128]{1,0:T(8,128)(2,1)S(1)}, u32[]{:S(2)}, u32[]{:S(2)}) collective-permute-start(bf16[512,128]{1,0:T(8,128)(2,1)S(1)} %get-tuple-element.51), channel_id=1, source_target_pairs={{0,8},{2,10},{4,12},{6,14},{8,16},{10,18},{12,20},{14,22},{16,24},... | collective-permute-start | bytes 393224 | tf_op jit(solution)/shard_map/ppermute | solution.py:402
  24.9 14.9 %collective-permute-start.11 = (bf16[512,128]{1,0:T(8,128)(2,1)S(1)}, bf16[512,128]{1,0:T(8,128)(2,1)S(1)}, u32[]{:S(2)}, u32[]{:S(2)}) collective-permute-start(bf16[512,128]{1,0:T(8,128)(2,1)S(1)} %get-tuple-element.51), channel_id=1, source_target_pairs={{0,16},{2,18},{4,20},{6,22},{8,24},{10,26},{12,28},{14,30},{1,17},... | collective-permute-start | bytes 393224 | tf_op jit(solution)/shard_map/ppermute | solution.py:402
  32.1 3.2 %collective-permute-start.12 = (bf16[256,128]{1,0:T(8,128)(2,1)S(1)}, bf16[256,128]{1,0:T(8,128)(2,1)S(1)}, u32[]{:S(2)}, u32[]{:S(2)}) collective-permute-start(bf16[256,128]{1,0:T(8,128)(2,1)S(1)} %get-tuple-element.52), channel_id=1, source_target_pairs={{0,24},{2,26},{4,28},{6,30},{1,25},{3,27},{5,29},{7,31}} | collective-permute-start | bytes 196616 | tf_op jit(solution)/shard_map/ppermute | solution.py:402
  33.4 14.2 %collective-permute-start.8 = (bf16[640,128]{1,0:T(8,128)(2,1)S(1)}, bf16[640,128]{1,0:T(8,128)(2,1)S(1)}, u32[]{:S(2)}, u32[]{:S(2)}) collective-permute-start(bf16[640,128]{1,0:T(8,128)(2,1)S(1)} %get-tuple-element.49), channel_id=1, source_target_pairs={{0,4},{2,6},{4,0},{6,2},{8,12},{10,14},{12,8},{14,10},{16,20},{18,... | collective-permute-start | bytes 491528 | tf_op jit(solution)/shard_map/ppermute | solution.py:398
  35.3 12.3 %collective-permute-start.9 = (bf16[640,128]{1,0:T(8,128)(2,1)S(1)}, bf16[640,128]{1,0:T(8,128)(2,1)S(1)}, u32[]{:S(2)}, u32[]{:S(2)}) collective-permute-start(bf16[640,128]{1,0:T(8,128)(2,1)S(1)} %get-tuple-element.50), channel_id=1, source_target_pairs={{0,6},{2,4},{4,2},{6,0},{8,14},{10,12},{12,10},{14,8},{16,22},{18,... | collective-permute-start | bytes 491528 | tf_op jit(solution)/shard_map/ppermute | solution.py:398
  39.7 8.9 %copy-start = (s32[1,16]{1,0:T(1,128)S(1)}, s32[1,16]{1,0:T(1,128)}, u32[]{:S(2)}) copy-start(s32[1,16]{1,0:T(1,128)} %param.21) | copy-start | bytes 196
  41.1 6.5 %collective-permute-start.13 = (bf16[384,128]{1,0:T(8,128)(2,1)S(1)}, bf16[384,128]{1,0:T(8,128)(2,1)S(1)}, u32[]{:S(2)}, u32[]{:S(2)}) collective-permute-start(bf16[384,128]{1,0:T(8,128)(2,1)S(1)} %get-tuple-element.61), channel_id=1, source_target_pairs={{0,2},{2,0},{4,6},{6,4},{8,10},{10,8},{12,14},{14,12},{16,18},{18,... | collective-permute-start | bytes 294920 | tf_op jit(solution)/shard_map/ppermute | solution.py:398
  42.6 4.9 %collective-permute-start.14 = (bf16[384,128]{1,0:T(8,128)(2,1)S(1)}, bf16[384,128]{1,0:T(8,128)(2,1)S(1)}, u32[]{:S(2)}, u32[]{:S(2)}) collective-permute-start(bf16[384,128]{1,0:T(8,128)(2,1)S(1)} %get-tuple-element.62), channel_id=1, source_target_pairs={{0,4},{2,6},{4,0},{6,2},{8,12},{10,14},{12,8},{14,10},{16,20},{18,... | collective-permute-start | bytes 294920 | tf_op jit(solution)/shard_map/ppermute | solution.py:398
  43.1 5.5 %collective-permute-start.15 = (bf16[384,128]{1,0:T(8,128)(2,1)S(1)}, bf16[384,128]{1,0:T(8,128)(2,1)S(1)}, u32[]{:S(2)}, u32[]{:S(2)}) collective-permute-start(bf16[384,128]{1,0:T(8,128)(2,1)S(1)} %get-tuple-element.63), channel_id=1, source_target_pairs={{0,6},{2,4},{4,2},{6,0},{8,14},{10,12},{12,10},{14,8},{16,22},{18,... | collective-permute-start | bytes 294920 | tf_op jit(solution)/shard_map/ppermute | solution.py:398
  54.2 1.6 %collective-permute-start.16 = (bf16[64,2048]{1,0:T(8,128)(2,1)S(1)}, bf16[64,2048]{1,0:T(8,128)(2,1)S(1)}, u32[]{:S(2)}, u32[]{:S(2)}) collective-permute-start(bf16[64,2048]{1,0:T(8,128)(2,1)S(1)} %get-tuple-element.72), channel_id=1, source_target_pairs={{0,1},{1,0},{2,3},{3,2},{4,5},{5,4},{6,7},{7,6},{8,9},{9,8},{10,11... | collective-permute-start | bytes 786440 | tf_op jit(solution)/shard_map/ppermute | solution.py:523

commit v6 on v5

--- a/solution.py
+++ b/solution.py
@@ -15,13 +15,13 @@
 MIB = 1024 * 1024
 
 
-def call(kernel, out_shape, args, in_specs=None, scratch=(), flops=0, moved=0, limit=6):
+def call(kernel, out_shape, args, in_specs=None, out_specs=None, scratch=(), flops=0, moved=0, limit=6):
     vmem = pl.BlockSpec(memory_space=pltpu.VMEM)
     return pl.pallas_call(
         kernel,
         out_shape=out_shape,
         in_specs=in_specs or [vmem] * len(args),
-        out_specs=jax.tree.map(lambda _: vmem, out_shape),
+        out_specs=out_specs or jax.tree.map(lambda _: vmem, out_shape),
         scratch_shapes=list(scratch),
         compiler_params=pltpu.CompilerParams(vmem_limit_bytes=limit * MIB),
         cost_estimate=pl.CostEstimate(flops=flops, bytes_accessed=moved, transcendentals=0),
@@ -144,7 +144,7 @@
 
 
 def leave_kernel(group, place_ref, exit_ref, *refs):
-    turn_refs, (long_ref, short_ref, starts_ref, turns_ref) = refs[:group], refs[group:]
+    turn_refs, (leave_ref, starts_ref, turns_ref) = refs[:group], refs[group:]
     member = in_order(place_ref, turn_refs, turns_ref)
     tokens, size = exit_ref.shape
     own = exit_ref[...]
@@ -160,18 +160,39 @@
         if index < group - 1:
             starts_ref[index + 1] = product
     high, low = split(keys)
-    for ref in (long_ref, short_ref):
-        ref[:tokens] = high
-        ref[tokens : 2 * tokens] = low
+    leave_ref[:tokens] = high
+    leave_ref[tokens : 2 * tokens] = low
     high, low = split(product)
-    long_ref[2 * tokens : 2 * tokens + size] = high
-    long_ref[2 * tokens + size :] = low
-
-
-def bundle_kernel(group, place_ref, exit_ref, after_ref, *refs):
-    turn_refs, val_refs = refs[:group], refs[group : -group - 2]
-    bundle_refs, (turns_ref, seen_ref) = refs[-group - 2 : -2], refs[-2:]
+    leave_ref[2 * tokens : 2 * tokens + size] = high
+    leave_ref[2 * tokens + size :] = low
+
+
+def bundle_kernel(group, place_ref, mask_ref, exit_ref, after_ref, *refs):
+    groups = len(refs) - 2 * group - 3
+    turn_refs, val_refs = refs[:group], refs[group : group + groups]
+    bundle_refs, (table_ref, turns_ref, seen_ref) = refs[-group - 3 : -3], refs[-3:]
     member = in_order(place_ref, turn_refs, turns_ref)
+    place = place_ref[0]
+    mine = place // group
+    most = (table_ref.shape[0] - 1) // 2
+    for slot in range(most):
+        table_ref[2 * slot] = 0
+        table_ref[2 * slot + 1] = mine
+    segments = mask_ref.shape[0]
+
+    def pick(segment, count):
+        wanted = (mask_ref[segment] > 0) & (segment < place) & (count < most)
+
+        @pl.when(wanted)
+        def _():
+            table_ref[2 * count] = target_of(segment % group, member, group) if (
+                group & (group - 1) == 0
+            ) else (member + group - segment % group) % group
+            table_ref[2 * count + 1] = segment // group
+
+        return count + wanted.astype(jnp.int32)
+
+    table_ref[2 * most] = lax.fori_loop(0, segments, pick, jnp.int32(0))
     tokens, size = exit_ref.shape
     keys = exit_ref[...]
     for index in range(group):
@@ -180,8 +201,9 @@
         seen_ref[index] = keys.astype(BF16)
     for step in range(group):
         bundle_refs[step][:tokens] = seen_ref[target_of(member, step, group)]
-        for index, ref in enumerate(val_refs):
-            bundle_refs[step][(index + 1) * tokens : (index + 2) * tokens] = ref[...]
+        for way in range(groups):
+            at = (source_of(mine, way, groups) + 1) * tokens
+            bundle_refs[step][pl.ds(pl.multiple_of(at, tokens), tokens), :] = val_refs[way][...]
 
 
 def query_kernel(first, rows_ref, weight_hbm, gain_ref, kn_ref, dirs_ref, coeff_ref, solved_ref, val_ref,
@@ -233,37 +255,38 @@
             total_ref[head] = total[part]
 
 
-def arrive_kernel(count, group, tokens, place_ref, *refs):
-    arrived, starts_ref = refs[:count], refs[count]
-    far_refs = refs[-group:]
-    member = place_ref[0] % group
+def arrive_kernel(groups, group, tokens, place_ref, *refs):
+    arrived, starts_ref = refs[:groups], refs[groups]
+    far_refs, (keys_ref, whole_ref) = refs[-group - 2 : -2], refs[-2:]
+    mine, member = place_ref[0] // group, place_ref[0] % group
     size = starts_ref.shape[1]
+    for step in range(groups):
+        index = source_of(mine, step, groups)
+        ref = arrived[step]
+        keys_ref[index] = ref[:tokens].astype(F32) + ref[tokens : 2 * tokens].astype(F32)
+        whole = ref[2 * tokens : 2 * tokens + size].astype(F32)
+        whole_ref[index] = whole + ref[2 * tokens + size :].astype(F32)
+    brought = [keys_ref[groups - 2]]
     product = None
-    brought = []
-    for index in range(count):
-        ref = arrived[index]
-        keys = ref[:tokens].astype(F32) + ref[tokens : 2 * tokens].astype(F32)
-        if index:
-            before = arrived[index - 1]
-            whole = before[2 * tokens : 2 * tokens + size].astype(F32)
-            whole = whole + before[2 * tokens + size :].astype(F32)
-            product = whole if product is None else dot3(whole, product)
-            keys = dot3(keys, product)
-        brought.append(keys)
-    keys = jnp.concatenate(brought, axis=0)
+    for index in range(groups - 3, -1, -1):
+        keys, whole = keys_ref[index], whole_ref[index + 1]
+        if product is not None:
+            whole = jnp.where(index + 2 < mine, dot3(whole, product), whole)
+        product = whole
+        brought.append(jnp.where(index + 1 < mine, dot3(keys, product), keys))
+    keys = jnp.concatenate(brought[::-1], axis=0)
     for step in range(group):
         start = starts_ref[target_of(member, step, group)]
         far_refs[step][...] = dot3(keys, start).astype(BF16)
 
 
-def attend_kernel(most, group, place_ref, mask_ref, *refs):
+def attend_kernel(group, place_ref, table_ref, *refs):
     bundle_refs, far_refs = refs[:group], refs[group : 2 * group]
-    parts = (len(refs) - 2 * group - 9) // 4
+    parts = (len(refs) - 2 * group - 8) // 4
     owns, refs = [refs[2 * group + 4 * n : 2 * group + 4 * n + 4] for n in range(parts)], refs[
         2 * group + 4 * parts :
     ]
-    (out_hbm, away_ref, kept_ref, chosen_ref, keys_ref, vals_ref, attended_ref, out_ref,
-     sems) = refs
+    out_hbm, away_ref, kept_ref, keys_ref, vals_ref, attended_ref, out_ref, sems = refs
     pieces, _, wide = out_ref.shape
     copies = [
         pltpu.make_async_copy(
@@ -273,54 +296,32 @@
     ]
     for copy in copies:
         copy.start()
-    place, core = place_ref[0], place_ref[1]
+    core = place_ref[1]
+    mine = place_ref[0] // group
+    most = (table_ref.shape[0] - 1) // 2
+    found = table_ref[2 * most]
     heads, tokens, size = owns[0][0].shape
-    segments = mask_ref.shape[0]
+    earlier = far_refs[0].shape[0] // tokens
     scaling = 1.0 / math.sqrt(size)
-    mine, member = place // group, place % group
-
-    def pick(segment, count):
-        wanted = (mask_ref[segment] > 0) & (segment < place)
-
-        @pl.when(wanted & (count < most))
-        def _():
-            chosen_ref[count] = segment
-
-        return count + wanted.astype(jnp.int32)
-
-    found = lax.fori_loop(0, segments, pick, jnp.int32(0))
     chunk = keys_ref.shape[0] // tokens
-    lanes = lax.broadcasted_iota(jnp.int32, (heads * tokens, chunk * tokens), 1)
+    lanes = lax.broadcasted_iota(jnp.int32, (tokens, chunk * tokens), 1)
 
     def collect(turn):
         for slot in range(chunk):
             part = slice(slot * tokens, (slot + 1) * tokens)
-            index = turn * chunk + slot
-            used = index < found
-            segment = jnp.where(used, chosen_ref[index], 0)
-            whose, distance = segment % group, mine - segment // group
-            before = pl.multiple_of(jnp.maximum(distance - 1, 0) * tokens, tokens)
-
-            @pl.when(jnp.logical_not(used))
-            def _():
-                keys_ref[part, :] = jnp.zeros((tokens, size), BF16)
-                vals_ref[part, :] = jnp.zeros((tokens, size), BF16)
-
-            for step in range(group):
-                here = used & (whose == source_of(member, step, group))
-
-                @pl.when(here)
+            step, source = table_ref[2 * (turn * chunk + slot)], table_ref[2 * (turn * chunk + slot) + 1]
+            before = pl.multiple_of(jnp.minimum(source, earlier - 1) * tokens, tokens)
+            after = pl.multiple_of((source + 1) * tokens, tokens)
+            for number in range(group):
+
+                @pl.when(step == number)
                 def _():
-                    after = pl.multiple_of((distance + 1) * tokens, tokens)
-                    vals_ref[part, :] = bundle_refs[step][pl.ds(after, tokens), :]
-
-                @pl.when(here & (distance > 0))
-                def _():
-                    keys_ref[part, :] = far_refs[step][pl.ds(before, tokens), :]
-
-                @pl.when(here & (distance == 0))
-                def _():
-                    keys_ref[part, :] = bundle_refs[step][:tokens]
+                    vals_ref[part, :] = bundle_refs[number][pl.ds(after, tokens), :]
+                    keys_ref[part, :] = jnp.where(
+                        source < mine,
+                        far_refs[number][pl.ds(before, tokens), :],
+                        bundle_refs[number][:tokens],
+                    )
 
     def advance(moved, turn, peak, total, weighted):
         scores = lax.dot_general(
@@ -340,30 +341,25 @@
     turns = most // chunk
     if turns == 1:
         collect(0)
-    for number, (moved_ref, weighted_ref, peak_ref, total_ref) in enumerate(owns):
-        moved = moved_ref[...].reshape(heads * tokens, size)
-        state = (
-            peak_ref[...].reshape(heads * tokens, 1),
-            total_ref[...].reshape(heads * tokens, 1),
-            weighted_ref[...].reshape(heads * tokens, size),
-        )
+    for number in range(parts * heads):
+        moved_ref, weighted_ref, peak_ref, total_ref = owns[number // heads]
+        h = number % heads
+        state = (peak_ref[h], total_ref[h], weighted_ref[h])
         if turns == 1:
-            _, total, weighted = advance(moved, 0, *state)
+            _, total, weighted = advance(moved_ref[h], 0, *state)
         else:
 
-            def step_of(turn, state, moved=moved):
+            def step_of(turn, state, moved_ref=moved_ref, h=h):
                 collect(turn)
-                return advance(moved, turn, *state)
+                return advance(moved_ref[h], turn, *state)
 
             _, total, weighted = lax.fori_loop(0, turns, step_of, state)
         done = (weighted * (1.0 / total)).astype(BF16)
-        for h in range(heads):
-            columns = slice((number * heads + h) * size, (number * heads + h + 1) * size)
-            for index in range(tokens // half):
-                at = pl.multiple_of(jnp.where(index == core, half, 0), half)
-                attended_ref[pl.ds(at, half), columns] = done[
-                    h * tokens + index * half : h * tokens + (index + 1) * half
-                ]
+        for index in range(tokens // half):
+            at = pl.multiple_of(jnp.where(index == core, half, 0), half)
+            attended_ref[pl.ds(at, half), number * size : (number + 1) * size] = done[
+                index * half : (index + 1) * half
+            ]
     for n in range(pieces):
         copies[n].wait()
         result = jnp.dot(attended_ref[...], out_ref[n], preferred_element_type=F32).astype(BF16)
@@ -391,15 +387,21 @@
     square = shaped((tokens, size), F32)
     place = jnp.stack([position, core]).astype(jnp.int32)
 
-    def to_member(value, step):
-        pairs = [
+    def swapped(values, count, pairs_of):
+        out = [values[0]] * count
+        for step in range(count - 1, 0, -1):
+            out[step] = lax.ppermute(values[step], "ctx", pairs_of(step))
+        return out
+
+    def within_group(values):
+        return swapped(values, group, lambda step: [
             (s, s - s % group + target_of(s % group, step, group)) for s in range(segments)
-        ]
-        return lax.ppermute(value, "ctx", pairs)
-
-    def to_later_group(value, distance):
-        step = distance * group
-        return lax.ppermute(value, "ctx", [(s, s + step) for s in range(segments - step)])
+        ])
+
+    def along_line(values):
+        return swapped(values, groups, lambda step: [
+            (s, s % group + group * target_of(s // group, step, groups)) for s in range(segments)
+        ])
 
     weights, rate_row, key_gain, query_gain, mine = call(
         functools.partial(load_kernel, size),
@@ -429,13 +431,12 @@
         flops=6 * tokens * width * size,
         moved=8 * width * size,
     )
-    turns = [turn] + [to_member(turn, step) for step in range(1, group)]
-    line = [val] + [to_later_group(val, d) for d in range(1, groups)]
-    long, short, starts = call(
+    turns = within_group([turn] * group)
+    line = along_line([val] * groups)
+    leaving, starts = call(
         functools.partial(leave_kernel, group),
         [
             shaped((2 * tokens + 2 * size, size), BF16),
-            shaped((2 * tokens, size), BF16),
             shaped((group, size, size), F32),
         ],
         (place, exit_keys, *turns),
@@ -444,14 +445,14 @@
         flops=12 * group * size**3,
         moved=10**6,
     )
-    arrived = [
-        to_later_group(long if d < groups - 1 else short, d) for d in range(1, groups)
-    ]
-    bundle = call(
+    arrived = along_line([leaving] * groups)
+    *bundle, table = call(
         functools.partial(bundle_kernel, group),
-        [shaped(((1 + groups) * tokens, size), BF16)] * group,
-        (place, exit_keys, starts, *turns, *line),
-        in_specs=[smem, vmem, anywhere] + [vmem] * (group + groups),
+        [shaped(((1 + groups) * tokens, size), BF16)] * group
+        + [shaped((2 * (segments // 4) + 1,), jnp.int32)],
+        (place, block_mask[0], exit_keys, starts, *turns, *line),
+        in_specs=[smem, smem, vmem, anywhere] + [vmem] * (group + groups),
+        out_specs=[vmem] * group + [smem],
         scratch=(
             pltpu.VMEM((group, size, size), F32),
             pltpu.VMEM((group, tokens, size), BF16),
@@ -460,7 +461,7 @@
         moved=10**6,
         limit=8 + group * groups // 4,
     )
-    bundle = [bundle[0]] + [to_member(bundle[step], step) for step in range(1, group)]
+    bundle = within_group(bundle)
     calls = math.gcd(heads, 2)
     each = heads // calls
     pieces = math.gcd(each, 2)
@@ -486,21 +487,24 @@
         for number in range(calls)
     ]
     far = call(
-        functools.partial(arrive_kernel, groups - 1, group, tokens),
+        functools.partial(arrive_kernel, groups, group, tokens),
         [shaped(((groups - 1) * tokens, size), BF16)] * group,
         (place, *arrived, starts, owns[0][2]),
-        in_specs=[smem] + [vmem] * groups + [anywhere],
+        in_specs=[smem] + [vmem] * (groups + 1) + [anywhere],
+        scratch=(
+            pltpu.VMEM((groups, tokens, size), F32),
+            pltpu.VMEM((groups, size, size), F32),
+        ),
         flops=6 * groups * group * size**3,
         moved=10**6,
         limit=8 + group * groups // 4,
     )
-    far = [far[0]] + [to_member(far[step], step) for step in range(1, group)]
+    far = within_group(far)
     most = segments // 4
     chunk = math.gcd(most, 4)
     width_out = w_out.shape[1]
     pieces = math.gcd(width_out // size, 4)
     scratch = [
-        pltpu.SMEM((most,), jnp.int32),
         pltpu.VMEM((chunk * tokens, size), BF16),
         pltpu.VMEM((chunk * tokens, size), BF16),
         pltpu.VMEM((tokens, heads * size), BF16),
@@ -508,10 +512,10 @@
         pltpu.SemaphoreType.DMA((pieces,)),
     ]
     away, kept = call(
-        functools.partial(attend_kernel, most, group),
+        functools.partial(attend_kernel, group),
         [shaped((half, width_out), BF16)] * 2,
         (
-            place, block_mask[0], *bundle, *far, *(array for own in owns for array in own),
+            place, table, *bundle, *far, *(array for own in owns for array in own),
             in_hbm(w_out),
         ),
         in_specs=[smem] * 2 + [vmem] * (2 * group + 4 * calls) + [hbm],

time: 56.9 us -> 49.1 us (0.86)
  starting transfers between devices: 32.3 us -> 19.5 us
  waiting for transfers between devices: 3.42 us -> 8.76 us
    ppermute x15, starting transfers between devices: 31.8 us -> 18.9 us  [swapped(): out[step] = lax.ppermute(values[step], 'ctx', pairs_of(step))]
    ppermute x15, waiting for transfers between devices: 1.9 us -> 7.24 us  [swapped(): out[step] = lax.ppermute(values[step], 'ctx', pairs_of(step))]
  transfers between devices with their start and end apart: 17 -> 17, of which waited for: 4 -> 5; matrix products, arithmetic and copies ran while one was open for 0% -> 0% of each run, Pallas kernels for 17% -> 23%
where the time goes in v6:
time: 49.1 us; the launch traced here: 48.9 us
  starting transfers between devices  19.5 us (40%)
  Pallas kernels  19.1 us (39%)
  waiting for transfers between devices  8.76 us (18%)
  other arithmetic  0.84 us (2%)
  between operations  0.77 us (2%)
    pallas_call x8, Pallas kernels, call(): pl.pallas_call(kernel, out_shape=out_shape, in_specs=in_specs or [vmem] *...  19.1 us
    ppermute x15, starting transfers between devices, swapped(): out[step] = lax.ppermute(values[step], 'ctx', pairs_of(step))  18.9 us
    ppermute x15, waiting for transfers between devices, swapped(): out[step] = lax.ppermute(values[step], 'ctx', pairs_of(step))  7.24 us
    ppermute x1, waiting for transfers between devices, body(): return kept + lax.ppermute(away, 'head', [(0, 1), (1, 0)])  1.52 us
  transfers between devices with their start and end apart: 17, of which 5 were waited for; matrix products, arithmetic and copies ran while one was open for 0% of the time, Pallas kernels for 23%

profile of v6, /device:TPU:0, one launch (start us, length us, event | category | flops | bytes accessed | tf_op | source)
XLA Modules:
  0.0 48.9 jit_solution(4814750187199404464)
XLA Ops:
  1.1 1.5 %shard_map.109 = (bf16[2048,384]{1,0:T(8,128)(2,1)S(1)}, bf16[1,2048]{1,0:T(2,128)(2,1)S(1)}, f32[1,128]{1,0:T(1,128)S(1)}, f32[1,128]{1,0:T(1,128)S(1)}, bf16[64,2048]{1,0:T(8,128)(2,1)S(1)}) custom-call(bf16[2048,128]{1,0:T(8,128)(2,1)} %key_hbm.1, bf16[2048,128]{1,0:T(8,128)(2,1)} %dir_hbm.1, bf16[2048,128]{1,0:T(8,128)(2,1)} %value_hbm.1, ...), custom_call_target="tpu_custom_call" | custom-call | bytes 3145728 | tf_op jit(solution)/shard_map/pallas_call | solution.py:20
  2.7 3.0 %shard_map.110 = (bf16[128,2048]{1,0:T(8,128)(2,1)S(1)}, f32[128,128]{1,0:T(8,128)S(1)}, bf16[128,128]{1,0:T(8,128)(2,1)S(1)}, f32[128,128]{1,0:T(8,128)S(1)}, f...) custom-call(s32[2]{0:T(128)S(1)} %pad_add_fusion.place_ref, ...), custom_call_target="tpu_custom_call" | custom-call | flops 201326592 | bytes 2097152 | tf_op jit(solution)/shard_map/pallas_call | solution.py:20
  5.7 2.6 %collective-permute-start.1 = (f32[128,128]{1,0:T(8,128)S(1)}, f32[128,128]{1,0:T(8,128)S(1)}, u32[]{:S(2)}, u32[]{:S(2)}) collective-permute-start(f32[128,128]{1,0:T(8,128)S(1)} %get-tuple-element.44.refs_0_), channel_id=1, source_target_pairs={{0,2},{2,0},{4,6},{6,4},{8,10},{10,8},{12,14},{14,12},{16,18},{18,... | collective-permute-start | bytes 196616 | tf_op jit(solution)/shard_map/ppermute | solution.py:393
  8.3 1.5 %collective-permute-start.2 = (f32[128,128]{1,0:T(8,128)S(1)}, f32[128,128]{1,0:T(8,128)S(1)}, u32[]{:S(2)}, u32[]{:S(2)}) collective-permute-start(f32[128,128]{1,0:T(8,128)S(1)} %get-tuple-element.44.refs_0_), channel_id=1, source_target_pairs={{0,4},{2,6},{4,0},{6,2},{8,12},{10,14},{12,8},{14,10},{16,20},{18,... | collective-permute-start | bytes 196616 | tf_op jit(solution)/shard_map/ppermute | solution.py:393
  9.8 2.0 %collective-permute-start.4 = (bf16[128,128]{1,0:T(8,128)(2,1)S(1)}, bf16[128,128]{1,0:T(8,128)(2,1)S(1)}, u32[]{:S(2)}, u32[]{:S(2)}) collective-permute-start(bf16[128,128]{1,0:T(8,128)(2,1)S(1)} %get-tuple-element.46.refs_4_.val_ref), channel_id=1, source_target_pairs={{0,8},{2,10},{4,12},{6,14},{8,0},{10,2},{12,4},{14,6},{16,24},{18,... | collective-permute-start | bytes 98312 | tf_op jit(solution)/shard_map/ppermute | solution.py:393
  11.9 2.6 %collective-permute-start.5 = (bf16[128,128]{1,0:T(8,128)(2,1)S(1)}, bf16[128,128]{1,0:T(8,128)(2,1)S(1)}, u32[]{:S(2)}, u32[]{:S(2)}) collective-permute-start(bf16[128,128]{1,0:T(8,128)(2,1)S(1)} %get-tuple-element.46.refs_4_.val_ref), channel_id=1, source_target_pairs={{0,16},{2,18},{4,20},{6,22},{8,24},{10,26},{12,28},{14,30},{16,0},... | collective-permute-start | bytes 98312 | tf_op jit(solution)/shard_map/ppermute | solution.py:393
  15.0 1.0 %shard_map.111 = (bf16[512,128]{1,0:T(8,128)(2,1)S(1)}, f32[4,128,128]{2,1,0:T(8,128)S(1)}) custom-call(s32[2]{0:T(128)S(1)} %pad_add_fusion.place_ref, f32[128,128]{1,0:T(8,128)S(1)} %get-tuple-element.43.exit_ref, f32[128,128]{1,0:T(8,128)S(1)} %get-tuple-element.44.refs_0_, f32[128,128]{1,0:T(8,128)S(1)} %collective-permute-done.1.refs_1_, ...), custom_call_target="tpu_custom_call" | custom-call | flops 100663296 | bytes 1000000 | tf_op jit(solution)/shard_map/pallas_call | solution.py:20
  16.0 1.6 %collective-permute-start.10 = (bf16[512,128]{1,0:T(8,128)(2,1)S(1)}, bf16[512,128]{1,0:T(8,128)(2,1)S(1)}, u32[]{:S(2)}, u32[]{:S(2)}) collective-permute-start(bf16[512,128]{1,0:T(8,128)(2,1)S(1)} %get-tuple-element.52.refs_0_), channel_id=1, source_target_pairs={{0,8},{2,10},{4,12},{6,14},{8,0},{10,2},{12,4},{14,6},{16,24},{18,... | collective-permute-start | bytes 393224 | tf_op jit(solution)/shard_map/ppermute | solution.py:393
  17.7 2.9 %collective-permute-done.6.refs_7_ = bf16[128,128]{1,0:T(8,128)(2,1)S(1)} collective-permute-done((bf16[128,128]{1,0:T(8,128)(2,1)S(1)}, bf16[128,128]{1,0:T(8,128)(2,1)S(1)}, u32[]{:S(2)}, u32[]{:S(2)}) %collective-permute-start.6) | collective-permute-done | bytes 32800 | tf_op jit(solution)/shard_map/ppermute | solution.py:393
  20.5 1.4 %shard_map.112 = (bf16[640,128]{1,0:T(8,128)(2,1)S(1)}, bf16[640,128]{1,0:T(8,128)(2,1)S(1)}, bf16[640,128]{1,0:T(8,128)(2,1)S(1)}, bf16[640,128]{1,0:T(8,128)(2,1)S(1)}, s32[9]{0:T(128)S(1)}) custom-call(s32[2]{0:T(128)S(1)} %pad_add_fusion.place_ref, s32[16]{0:T(128)S(1)} %bitcast.5, f32[128,128]{1,0:T(8,128)S(1)} %get-tuple-element.43.exit_ref, ...), custom_call_target="tpu_custom_call" | custom-call | flops 100663296 | bytes 1000000 | tf_op jit(solution)/shard_map/pallas_call | solution.py:20
  21.9 1.5 %collective-permute-start.7 = (bf16[640,128]{1,0:T(8,128)(2,1)S(1)}, bf16[640,128]{1,0:T(8,128)(2,1)S(1)}, u32[]{:S(2)}, u32[]{:S(2)}) collective-permute-start(bf16[640,128]{1,0:T(8,128)(2,1)S(1)} %get-tuple-element.49), channel_id=1, source_target_pairs={{0,2},{2,0},{4,6},{6,4},{8,10},{10,8},{12,14},{14,12},{16,18},{18,... | collective-permute-start | bytes 491528 | tf_op jit(solution)/shard_map/ppermute | solution.py:393
  23.4 1.1 %collective-permute-start.12 = (bf16[512,128]{1,0:T(8,128)(2,1)S(1)}, bf16[512,128]{1,0:T(8,128)(2,1)S(1)}, u32[]{:S(2)}, u32[]{:S(2)}) collective-permute-start(bf16[512,128]{1,0:T(8,128)(2,1)S(1)} %get-tuple-element.52.refs_0_), channel_id=1, source_target_pairs={{0,24},{2,26},{4,28},{6,30},{8,16},{10,18},{12,20},{14,22},{16,8},... | collective-permute-start | bytes 393224 | tf_op jit(solution)/shard_map/ppermute | solution.py:393
  24.5 1.5 %collective-permute-start.8 = (bf16[640,128]{1,0:T(8,128)(2,1)S(1)}, bf16[640,128]{1,0:T(8,128)(2,1)S(1)}, u32[]{:S(2)}, u32[]{:S(2)}) collective-permute-start(bf16[640,128]{1,0:T(8,128)(2,1)S(1)} %get-tuple-element.50), channel_id=1, source_target_pairs={{0,4},{2,6},{4,0},{6,2},{8,12},{10,14},{12,8},{14,10},{16,20},{18,... | collective-permute-start | bytes 491528 | tf_op jit(solution)/shard_map/ppermute | solution.py:393
  26.5 2.9 %shard_map.113 = (bf16[4,128,128]{2,1,0:T(8,128)(2,1)S(1)}, f32[4,128,128]{2,1,0:T(8,128)S(1)}, f32[4,128,1]{2,1,0:T(8,128)S(1)}, f32[4,128,1]{2,1,0:T(8,128)S(1)}) custom-call(bf16[128,2048]{1,0:T(8,128)(2,1)S(1)} %get-tuple-element.53.rows_ref, bf16[2048,1024]{1,0:T(8,128)(2,1)} %weight_hbm.3, f32[1,128]{1,0:T(1,128)S(1)} %get-tuple-element.54.gain_ref, ...), custom_call_target="tpu_custom_call" | custom-call | flops 536870912 | bytes 8388608 | tf_op jit(solution)/shard_map/pallas_call | solution.py:20
  29.4 3.2 %collective-permute-done.11.refs_2_ = bf16[512,128]{1,0:T(8,128)(2,1)S(1)} collective-permute-done((bf16[512,128]{1,0:T(8,128)(2,1)S(1)}, bf16[512,128]{1,0:T(8,128)(2,1)S(1)}, u32[]{:S(2)}, u32[]{:S(2)}) %collective-permute-start.11) | collective-permute-done | bytes 131104 | tf_op jit(solution)/shard_map/ppermute | solution.py:393
  32.6 1.4 %shard_map.114 = (bf16[384,128]{1,0:T(8,128)(2,1)S(1)}, bf16[384,128]{1,0:T(8,128)(2,1)S(1)}, bf16[384,128]{1,0:T(8,128)(2,1)S(1)}, bf16[384,128]{1,0:T(8,128)(2,1)S(1)}) custom-call(s32[2]{0:T(128)S(1)} %pad_add_fusion.place_ref, bf16[512,128]{1,0:T(8,128)(2,1)S(1)} %get-tuple-element.52.refs_0_, bf16[512,128]{1,0:T(8,128)(2,1)S(1)} %collective-permute-done.10.refs_1_, ...), custom_call_target="tpu_custom_call" | custom-call | flops 201326592 | bytes 1000000 | tf_op jit(solution)/shard_map/pallas_call | solution.py:20
  34.0 0.8 %collective-permute-start.13 = (bf16[384,128]{1,0:T(8,128)(2,1)S(1)}, bf16[384,128]{1,0:T(8,128)(2,1)S(1)}, u32[]{:S(2)}, u32[]{:S(2)}) collective-permute-start(bf16[384,128]{1,0:T(8,128)(2,1)S(1)} %get-tuple-element.61), channel_id=1, source_target_pairs={{0,2},{2,0},{4,6},{6,4},{8,10},{10,8},{12,14},{14,12},{16,18},{18,... | collective-permute-start | bytes 294920 | tf_op jit(solution)/shard_map/ppermute | solution.py:393
  34.7 1.3 %collective-permute-start.14 = (bf16[384,128]{1,0:T(8,128)(2,1)S(1)}, bf16[384,128]{1,0:T(8,128)(2,1)S(1)}, u32[]{:S(2)}, u32[]{:S(2)}) collective-permute-start(bf16[384,128]{1,0:T(8,128)(2,1)S(1)} %get-tuple-element.62), channel_id=1, source_target_pairs={{0,4},{2,6},{4,0},{6,2},{8,12},{10,14},{12,8},{14,10},{16,20},{18,... | collective-permute-start | bytes 294920 | tf_op jit(solution)/shard_map/ppermute | solution.py:393
  36.1 1.4 %collective-permute-start.15 = (bf16[384,128]{1,0:T(8,128)(2,1)S(1)}, bf16[384,128]{1,0:T(8,128)(2,1)S(1)}, u32[]{:S(2)}, u32[]{:S(2)}) collective-permute-start(bf16[384,128]{1,0:T(8,128)(2,1)S(1)} %get-tuple-element.63), channel_id=1, source_target_pairs={{0,6},{2,4},{4,2},{6,0},{8,14},{10,12},{12,10},{14,8},{16,22},{18,... | collective-permute-start | bytes 294920 | tf_op jit(solution)/shard_map/ppermute | solution.py:393
  37.5 2.9 %shard_map.115 = (bf16[4,128,128]{2,1,0:T(8,128)(2,1)S(1)}, f32[4,128,128]{2,1,0:T(8,128)S(1)}, f32[4,128,1]{2,1,0:T(8,128)S(1)}, f32[4,128,1]{2,1,0:T(8,128)S(1)}) custom-call(bf16[128,2048]{1,0:T(8,128)(2,1)S(1)} %get-tuple-element.53.rows_ref, bf16[2048,1024]{1,0:T(8,128)(2,1)} %weight_hbm.3, f32[1,128]{1,0:T(1,128)S(1)} %get-tuple-element.54.gain_ref, ...), custom_call_target="tpu_custom_call" | custom-call | flops 536870912 | bytes 8388608 | tf_op jit(solution)/shard_map/pallas_call | solution.py:20
  40.5 1.1 %collective-permute-done.15.refs_7_ = bf16[384,128]{1,0:T(8,128)(2,1)S(1)} collective-permute-done((bf16[384,128]{1,0:T(8,128)(2,1)S(1)}, bf16[384,128]{1,0:T(8,128)(2,1)S(1)}, u32[]{:S(2)}, u32[]{:S(2)}) %collective-permute-start.15) | collective-permute-done | bytes 98336 | tf_op jit(solution)/shard_map/ppermute | solution.py:393
  41.6 4.9 %shard_map.116 = (bf16[64,2048]{1,0:T(8,128)(2,1)S(1)}, bf16[64,2048]{1,0:T(8,128)(2,1)S(1)}) custom-call(s32[2]{0:T(128)S(1)} %pad_add_fusion.place_ref, s32[9]{0:T(128)S(1)} %get-tuple-element.47.table_ref, bf16[640,128]{1,0:T(8,128)(2,1)S(1)} %get-tuple-element.48.refs_0_, bf16[640,128]{1,0:T(8,128)(2,1)S(1)} %collective-permute-done.7.refs_1_, ...), custom_call_target="tpu_custom_call" | custom-call | flops 536870912 | bytes 4000000 | tf_op jit(solution)/shard_map/pallas_call | solution.py:20
  46.6 1.5 %collective-permute-done.16 = bf16[64,2048]{1,0:T(8,128)(2,1)S(1)} collective-permute-done((bf16[64,2048]{1,0:T(8,128)(2,1)S(1)}, bf16[64,2048]{1,0:T(8,128)(2,1)S(1)}, u32[]{:S(2)}, u32[]{:S(2)}) %collective-permute-start.16) | collective-permute-done | bytes 262176 | tf_op jit(solution)/shard_map/ppermute | solution.py:527
  48.1 0.8 %add.3 = bf16[64,2048]{1,0:T(8,128)(2,1)} add(bf16[64,2048]{1,0:T(8,128)(2,1)S(1)} %get-tuple-element.71, bf16[64,2048]{1,0:T(8,128)(2,1)S(1)} %collective-permute-done.16) | non-fusion elementwise | flops 131072 | bytes 786432 | tf_op jit(solution)/shard_map/add | solution.py:527
  (22 shorter events, 1.6 us)
Async XLA Ops:
  0.0 20.5 %copy-start = (s32[1,16]{1,0:T(1,128)S(1)}, s32[1,16]{1,0:T(1,128)}, u32[]{:S(2)}) copy-start(s32[1,16]{1,0:T(1,128)} %param.21) | copy-start | bytes 196
  0.0 2.7 %collective-permute-start = (bf16[64,2048]{1,0:T(8,128)(2,1)}, bf16[64,2048]{1,0:T(8,128)(2,1)S(1)}, u32[]{:S(2)}, u32[]{:S(2)}) collective-permute-start(bf16[64,2048]{1,0:T(8,128)(2,1)} %mine_hbm.1), channel_id=1, source_target_pairs={{0,1},{1,0},{2,3},{3,2},{4,5},{5,4},{6,7},{7,6},{8,9},{9,8},{10,11... | collective-permute-start | bytes 786440 | tf_op jit(solution)/shard_map/ppermute | solution.py:378
  5.7 8.7 %collective-permute-start.1 = (f32[128,128]{1,0:T(8,128)S(1)}, f32[128,128]{1,0:T(8,128)S(1)}, u32[]{:S(2)}, u32[]{:S(2)}) collective-permute-start(f32[128,128]{1,0:T(8,128)S(1)} %get-tuple-element.44.refs_0_), channel_id=1, source_target_pairs={{0,2},{2,0},{4,6},{6,4},{8,10},{10,8},{12,14},{14,12},{16,18},{18,... | collective-permute-start | bytes 196616 | tf_op jit(solution)/shard_map/ppermute | solution.py:393
  8.3 6.6 %collective-permute-start.2 = (f32[128,128]{1,0:T(8,128)S(1)}, f32[128,128]{1,0:T(8,128)S(1)}, u32[]{:S(2)}, u32[]{:S(2)}) collective-permute-start(f32[128,128]{1,0:T(8,128)S(1)} %get-tuple-element.44.refs_0_), channel_id=1, source_target_pairs={{0,4},{2,6},{4,0},{6,2},{8,12},{10,14},{12,8},{14,10},{16,20},{18,... | collective-permute-start | bytes 196616 | tf_op jit(solution)/shard_map/ppermute | solution.py:393
  9.8 5.2 %collective-permute-start.3 = (f32[128,128]{1,0:T(8,128)S(1)}, f32[128,128]{1,0:T(8,128)S(1)}, u32[]{:S(2)}, u32[]{:S(2)}) collective-permute-start(f32[128,128]{1,0:T(8,128)S(1)} %get-tuple-element.44.refs_0_), channel_id=1, source_target_pairs={{0,6},{2,4},{4,2},{6,0},{8,14},{10,12},{12,10},{14,8},{16,22},{18,... | collective-permute-start | bytes 196616 | tf_op jit(solution)/shard_map/ppermute | solution.py:393
  9.8 7.8 %collective-permute-start.4 = (bf16[128,128]{1,0:T(8,128)(2,1)S(1)}, bf16[128,128]{1,0:T(8,128)(2,1)S(1)}, u32[]{:S(2)}, u32[]{:S(2)}) collective-permute-start(bf16[128,128]{1,0:T(8,128)(2,1)S(1)} %get-tuple-element.46.refs_4_.val_ref), channel_id=1, source_target_pairs={{0,8},{2,10},{4,12},{6,14},{8,0},{10,2},{12,4},{14,6},{16,24},{18,... | collective-permute-start | bytes 98312 | tf_op jit(solution)/shard_map/ppermute | solution.py:393
  11.9 5.8 %collective-permute-start.5 = (bf16[128,128]{1,0:T(8,128)(2,1)S(1)}, bf16[128,128]{1,0:T(8,128)(2,1)S(1)}, u32[]{:S(2)}, u32[]{:S(2)}) collective-permute-start(bf16[128,128]{1,0:T(8,128)(2,1)S(1)} %get-tuple-element.46.refs_4_.val_ref), channel_id=1, source_target_pairs={{0,16},{2,18},{4,20},{6,22},{8,24},{10,26},{12,28},{14,30},{16,0},... | collective-permute-start | bytes 98312 | tf_op jit(solution)/shard_map/ppermute | solution.py:393
  14.4 6.1 %collective-permute-start.6 = (bf16[128,128]{1,0:T(8,128)(2,1)S(1)}, bf16[128,128]{1,0:T(8,128)(2,1)S(1)}, u32[]{:S(2)}, u32[]{:S(2)}) collective-permute-start(bf16[128,128]{1,0:T(8,128)(2,1)S(1)} %get-tuple-element.46.refs_4_.val_ref), channel_id=1, source_target_pairs={{0,24},{2,26},{4,28},{6,30},{8,16},{10,18},{12,20},{14,22},{16,8},... | collective-permute-start | bytes 98312 | tf_op jit(solution)/shard_map/ppermute | solution.py:393
  16.0 10.0 %collective-permute-start.10 = (bf16[512,128]{1,0:T(8,128)(2,1)S(1)}, bf16[512,128]{1,0:T(8,128)(2,1)S(1)}, u32[]{:S(2)}, u32[]{:S(2)}) collective-permute-start(bf16[512,128]{1,0:T(8,128)(2,1)S(1)} %get-tuple-element.52.refs_0_), channel_id=1, source_target_pairs={{0,8},{2,10},{4,12},{6,14},{8,0},{10,2},{12,4},{14,6},{16,24},{18,... | collective-permute-start | bytes 393224 | tf_op jit(solution)/shard_map/ppermute | solution.py:393
  21.9 14.2 %collective-permute-start.7 = (bf16[640,128]{1,0:T(8,128)(2,1)S(1)}, bf16[640,128]{1,0:T(8,128)(2,1)S(1)}, u32[]{:S(2)}, u32[]{:S(2)}) collective-permute-start(bf16[640,128]{1,0:T(8,128)(2,1)S(1)} %get-tuple-element.49), channel_id=1, source_target_pairs={{0,2},{2,0},{4,6},{6,4},{8,10},{10,8},{12,14},{14,12},{16,18},{18,... | collective-permute-start | bytes 491528 | tf_op jit(solution)/shard_map/ppermute | solution.py:393
  23.4 9.1 %collective-permute-start.11 = (bf16[512,128]{1,0:T(8,128)(2,1)S(1)}, bf16[512,128]{1,0:T(8,128)(2,1)S(1)}, u32[]{:S(2)}, u32[]{:S(2)}) collective-permute-start(bf16[512,128]{1,0:T(8,128)(2,1)S(1)} %get-tuple-element.52.refs_0_), channel_id=1, source_target_pairs={{0,16},{2,18},{4,20},{6,22},{8,24},{10,26},{12,28},{14,30},{16,0},... | collective-permute-start | bytes 393224 | tf_op jit(solution)/shard_map/ppermute | solution.py:393
  23.4 9.1 %collective-permute-start.12 = (bf16[512,128]{1,0:T(8,128)(2,1)S(1)}, bf16[512,128]{1,0:T(8,128)(2,1)S(1)}, u32[]{:S(2)}, u32[]{:S(2)}) collective-permute-start(bf16[512,128]{1,0:T(8,128)(2,1)S(1)} %get-tuple-element.52.refs_0_), channel_id=1, source_target_pairs={{0,24},{2,26},{4,28},{6,30},{8,16},{10,18},{12,20},{14,22},{16,8},... | collective-permute-start | bytes 393224 | tf_op jit(solution)/shard_map/ppermute | solution.py:393
  24.5 16.0 %collective-permute-start.8 = (bf16[640,128]{1,0:T(8,128)(2,1)S(1)}, bf16[640,128]{1,0:T(8,128)(2,1)S(1)}, u32[]{:S(2)}, u32[]{:S(2)}) collective-permute-start(bf16[640,128]{1,0:T(8,128)(2,1)S(1)} %get-tuple-element.50), channel_id=1, source_target_pairs={{0,4},{2,6},{4,0},{6,2},{8,12},{10,14},{12,8},{14,10},{16,20},{18,... | collective-permute-start | bytes 491528 | tf_op jit(solution)/shard_map/ppermute | solution.py:393
  26.0 14.4 %collective-permute-start.9 = (bf16[640,128]{1,0:T(8,128)(2,1)S(1)}, bf16[640,128]{1,0:T(8,128)(2,1)S(1)}, u32[]{:S(2)}, u32[]{:S(2)}) collective-permute-start(bf16[640,128]{1,0:T(8,128)(2,1)S(1)} %get-tuple-element.51), channel_id=1, source_target_pairs={{0,6},{2,4},{4,2},{6,0},{8,14},{10,12},{12,10},{14,8},{16,22},{18,... | collective-permute-start | bytes 491528 | tf_op jit(solution)/shard_map/ppermute | solution.py:393
  34.0 6.5 %collective-permute-start.13 = (bf16[384,128]{1,0:T(8,128)(2,1)S(1)}, bf16[384,128]{1,0:T(8,128)(2,1)S(1)}, u32[]{:S(2)}, u32[]{:S(2)}) collective-permute-start(bf16[384,128]{1,0:T(8,128)(2,1)S(1)} %get-tuple-element.61), channel_id=1, source_target_pairs={{0,2},{2,0},{4,6},{6,4},{8,10},{10,8},{12,14},{14,12},{16,18},{18,... | collective-permute-start | bytes 294920 | tf_op jit(solution)/shard_map/ppermute | solution.py:393
  34.7 5.7 %collective-permute-start.14 = (bf16[384,128]{1,0:T(8,128)(2,1)S(1)}, bf16[384,128]{1,0:T(8,128)(2,1)S(1)}, u32[]{:S(2)}, u32[]{:S(2)}) collective-permute-start(bf16[384,128]{1,0:T(8,128)(2,1)S(1)} %get-tuple-element.62), channel_id=1, source_target_pairs={{0,4},{2,6},{4,0},{6,2},{8,12},{10,14},{12,8},{14,10},{16,20},{18,... | collective-permute-start | bytes 294920 | tf_op jit(solution)/shard_map/ppermute | solution.py:393
  36.1 5.5 %collective-permute-start.15 = (bf16[384,128]{1,0:T(8,128)(2,1)S(1)}, bf16[384,128]{1,0:T(8,128)(2,1)S(1)}, u32[]{:S(2)}, u32[]{:S(2)}) collective-permute-start(bf16[384,128]{1,0:T(8,128)(2,1)S(1)} %get-tuple-element.63), channel_id=1, source_target_pairs={{0,6},{2,4},{4,2},{6,0},{8,14},{10,12},{12,10},{14,8},{16,22},{18,... | collective-permute-start | bytes 294920 | tf_op jit(solution)/shard_map/ppermute | solution.py:393
  46.5 1.6 %collective-permute-start.16 = (bf16[64,2048]{1,0:T(8,128)(2,1)S(1)}, bf16[64,2048]{1,0:T(8,128)(2,1)S(1)}, u32[]{:S(2)}, u32[]{:S(2)}) collective-permute-start(bf16[64,2048]{1,0:T(8,128)(2,1)S(1)} %get-tuple-element.72), channel_id=1, source_target_pairs={{0,1},{1,0},{2,3},{3,2},{4,5},{5,4},{6,7},{7,6},{8,9},{9,8},{10,11... | collective-permute-start | bytes 786440 | tf_op jit(solution)/shard_map/ppermute | solution.py:527

commit v7 on v6

--- a/solution.py
+++ b/solution.py
@@ -139,7 +139,7 @@
     group = len(turn_refs)
     member = place_ref[0] % group
     for step in range(group):
-        turns_ref[source_of(member, step, group)] = turn_refs[step][...]
+        turns_ref[source_of(member, step, group)] = turn_refs[group - 1 - step][...]
     return member
 
 
@@ -168,9 +168,9 @@
 
 
 def bundle_kernel(group, place_ref, mask_ref, exit_ref, after_ref, *refs):
-    groups = len(refs) - 2 * group - 3
-    turn_refs, val_refs = refs[:group], refs[group : group + groups]
-    bundle_refs, (table_ref, turns_ref, seen_ref) = refs[-group - 3 : -3], refs[-3:]
+    groups = len(refs) - 2 * group - 4
+    turn_refs, val_refs, line_ref = refs[:group], refs[group : group + groups], refs[group + groups]
+    near_refs, (table_ref, turns_ref, seen_ref) = refs[-group - 3 : -3], refs[-3:]
     member = in_order(place_ref, turn_refs, turns_ref)
     place = place_ref[0]
     mine = place // group
@@ -200,10 +200,10 @@
             keys = jnp.where(index - 1 > member, dot3(keys, turns_ref[index - 1]), exit_ref[...])
         seen_ref[index] = keys.astype(BF16)
     for step in range(group):
-        bundle_refs[step][:tokens] = seen_ref[target_of(member, step, group)]
-        for way in range(groups):
-            at = (source_of(mine, way, groups) + 1) * tokens
-            bundle_refs[step][pl.ds(pl.multiple_of(at, tokens), tokens), :] = val_refs[way][...]
+        near_refs[step][...] = seen_ref[target_of(member, step, group)]
+    for way in range(groups):
+        at = pl.multiple_of(source_of(mine, way, groups) * tokens, tokens)
+        line_ref[pl.ds(at, tokens), :] = val_refs[groups - 1 - way][...]
 
 
 def query_kernel(first, rows_ref, weight_hbm, gain_ref, kn_ref, dirs_ref, coeff_ref, solved_ref, val_ref,
@@ -256,13 +256,13 @@
 
 
 def arrive_kernel(groups, group, tokens, place_ref, *refs):
-    arrived, starts_ref = refs[:groups], refs[groups]
+    arrived, starts_ref, near_refs = refs[:groups], refs[groups], refs[groups + 1 :]
     far_refs, (keys_ref, whole_ref) = refs[-group - 2 : -2], refs[-2:]
     mine, member = place_ref[0] // group, place_ref[0] % group
     size = starts_ref.shape[1]
     for step in range(groups):
         index = source_of(mine, step, groups)
-        ref = arrived[step]
+        ref = arrived[groups - 1 - step]
         keys_ref[index] = ref[:tokens].astype(F32) + ref[tokens : 2 * tokens].astype(F32)
         whole = ref[2 * tokens : 2 * tokens + size].astype(F32)
         whole_ref[index] = whole + ref[2 * tokens + size :].astype(F32)
@@ -277,11 +277,12 @@
     keys = jnp.concatenate(brought[::-1], axis=0)
     for step in range(group):
         start = starts_ref[target_of(member, step, group)]
-        far_refs[step][...] = dot3(keys, start).astype(BF16)
+        far_refs[step][: (groups - 1) * tokens] = dot3(keys, start).astype(BF16)
+        far_refs[step][(groups - 1) * tokens :] = near_refs[step][...]
 
 
 def attend_kernel(group, place_ref, table_ref, *refs):
-    bundle_refs, far_refs = refs[:group], refs[group : 2 * group]
+    far_refs, line_refs = refs[:group][::-1], refs[group : 2 * group][::-1]
     parts = (len(refs) - 2 * group - 8) // 4
     owns, refs = [refs[2 * group + 4 * n : 2 * group + 4 * n + 4] for n in range(parts)], refs[
         2 * group + 4 * parts :
@@ -301,7 +302,7 @@
     most = (table_ref.shape[0] - 1) // 2
     found = table_ref[2 * most]
     heads, tokens, size = owns[0][0].shape
-    earlier = far_refs[0].shape[0] // tokens
+    groups = far_refs[0].shape[0] // tokens
     scaling = 1.0 / math.sqrt(size)
     chunk = keys_ref.shape[0] // tokens
     lanes = lax.broadcasted_iota(jnp.int32, (tokens, chunk * tokens), 1)
@@ -310,18 +311,15 @@
         for slot in range(chunk):
             part = slice(slot * tokens, (slot + 1) * tokens)
             step, source = table_ref[2 * (turn * chunk + slot)], table_ref[2 * (turn * chunk + slot) + 1]
-            before = pl.multiple_of(jnp.minimum(source, earlier - 1) * tokens, tokens)
-            after = pl.multiple_of((source + 1) * tokens, tokens)
+            before = jnp.where(source < mine, source, groups - 1)
+            before = pl.multiple_of(before * tokens, tokens)
+            after = pl.multiple_of(source * tokens, tokens)
             for number in range(group):
 
                 @pl.when(step == number)
                 def _():
-                    vals_ref[part, :] = bundle_refs[number][pl.ds(after, tokens), :]
-                    keys_ref[part, :] = jnp.where(
-                        source < mine,
-                        far_refs[number][pl.ds(before, tokens), :],
-                        bundle_refs[number][:tokens],
-                    )
+                    vals_ref[part, :] = line_refs[number][pl.ds(after, tokens), :]
+                    keys_ref[part, :] = far_refs[number][pl.ds(before, tokens), :]
 
     def advance(moved, turn, peak, total, weighted):
         scores = lax.dot_general(
@@ -439,20 +437,21 @@
             shaped((2 * tokens + 2 * size, size), BF16),
             shaped((group, size, size), F32),
         ],
-        (place, exit_keys, *turns),
+        (place, exit_keys, *turns[::-1]),
         in_specs=[smem] + [vmem] * (1 + group),
         scratch=(pltpu.VMEM((group, size, size), F32),),
         flops=12 * group * size**3,
         moved=10**6,
     )
     arrived = along_line([leaving] * groups)
-    *bundle, table = call(
+    values, *near, table = call(
         functools.partial(bundle_kernel, group),
-        [shaped(((1 + groups) * tokens, size), BF16)] * group
+        [shaped((groups * tokens, size), BF16)]
+        + [shaped((tokens, size), BF16)] * group
         + [shaped((2 * (segments // 4) + 1,), jnp.int32)],
-        (place, block_mask[0], exit_keys, starts, *turns, *line),
+        (place, block_mask[0], exit_keys, starts, *turns[::-1], *line[::-1]),
         in_specs=[smem, smem, vmem, anywhere] + [vmem] * (group + groups),
-        out_specs=[vmem] * group + [smem],
+        out_specs=[vmem] * (1 + group) + [smem],
         scratch=(
             pltpu.VMEM((group, size, size), F32),
             pltpu.VMEM((group, tokens, size), BF16),
@@ -461,7 +460,7 @@
         moved=10**6,
         limit=8 + group * groups // 4,
     )
-    bundle = within_group(bundle)
+    values = within_group([values] * group)
     calls = math.gcd(heads, 2)
     each = heads // calls
     pieces = math.gcd(each, 2)
@@ -488,9 +487,9 @@
     ]
     far = call(
         functools.partial(arrive_kernel, groups, group, tokens),
-        [shaped(((groups - 1) * tokens, size), BF16)] * group,
-        (place, *arrived, starts, owns[0][2]),
-        in_specs=[smem] + [vmem] * (groups + 1) + [anywhere],
+        [shaped((groups * tokens, size), BF16)] * group,
+        (place, *arrived[::-1], starts, *near, owns[0][2]),
+        in_specs=[smem] + [vmem] * (groups + 1 + group) + [anywhere],
         scratch=(
             pltpu.VMEM((groups, tokens, size), F32),
             pltpu.VMEM((groups, size, size), F32),
@@ -515,7 +514,7 @@
         functools.partial(attend_kernel, group),
         [shaped((half, width_out), BF16)] * 2,
         (
-            place, table, *bundle, *far, *(array for own in owns for array in own),
+            place, table, *far[::-1], *values[::-1], *(array for own in owns for array in own),
             in_hbm(w_out),
         ),
         in_specs=[smem] * 2 + [vmem] * (2 * group + 4 * calls) + [hbm],

time: 49.1 us -> 47.4 us (0.965)
  waiting for transfers between devices: 8.76 us -> 5.46 us
  starting transfers between devices: 19.5 us -> 21 us
    ppermute x15, waiting for transfers between devices: 7.24 us -> 3.93 us  [swapped(): out[step] = lax.ppermute(values[step], 'ctx', pairs_of(step))]
    ppermute x15, starting transfers between devices: 18.9 us -> 20.4 us  [swapped(): out[step] = lax.ppermute(values[step], 'ctx', pairs_of(step))]
  transfers between devices with their start and end apart: 17 -> 17, of which waited for: 5 -> 4; matrix products, arithmetic and copies ran while one was open for 0% -> 0% of each run, Pallas kernels for 23% -> 24%
where the time goes in v7:
time: 47.4 us; the launch traced here: 47.2 us
  starting transfers between devices  21 us (44%)
  Pallas kernels  19.2 us (41%)
  waiting for transfers between devices  5.46 us (12%)
  other arithmetic  0.84 us (2%)
  between operations  0.76 us (2%)
    ppermute x15, starting transfers between devices, swapped(): out[step] = lax.ppermute(values[step], 'ctx', pairs_of(step))  20.4 us
    pallas_call x8, Pallas kernels, call(): pl.pallas_call(kernel, out_shape=out_shape, in_specs=in_specs or [vmem] *...  19.2 us
    ppermute x15, waiting for transfers between devices, swapped(): out[step] = lax.ppermute(values[step], 'ctx', pairs_of(step))  3.93 us
    ppermute x1, waiting for transfers between devices, body(): return kept + lax.ppermute(away, 'head', [(0, 1), (1, 0)])  1.52 us
  transfers between devices with their start and end apart: 17, of which 4 were waited for; matrix products, arithmetic and copies ran while one was open for 0% of the time, Pallas kernels for 24%

profile of v7, /device:TPU:0, one launch (start us, length us, event | category | flops | bytes accessed | tf_op | source)
XLA Modules:
  0.0 47.2 jit_solution(8484928318926902515)
XLA Ops:
  0.0 0.5 collective-permute-start
  1.1 1.5 %shard_map.109 = (bf16[2048,384]{1,0:T(8,128)(2,1)S(1)}, bf16[1,2048]{1,0:T(2,128)(2,1)S(1)}, f32[1,128]{1,0:T(1,128)S(1)}, f32[1,128]{1,0:T(1,128)S(1)}, bf16[64,2048]{1,0:T(8,128)(2,1)S(1)}) custom-call(bf16[2048,128]{1,0:T(8,128)(2,1)} %key_hbm.1, bf16[2048,128]{1,0:T(8,128)(2,1)} %dir_hbm.1, bf16[2048,128]{1,0:T(8,128)(2,1)} %value_hbm.1, ...), custom_call_target="tpu_custom_call" | custom-call | bytes 3145728 | tf_op jit(solution)/shard_map/pallas_call | solution.py:20
  2.7 3.0 %shard_map.110 = (bf16[128,2048]{1,0:T(8,128)(2,1)S(1)}, f32[128,128]{1,0:T(8,128)S(1)}, bf16[128,128]{1,0:T(8,128)(2,1)S(1)}, f32[128,128]{1,0:T(8,128)S(1)}, f...) custom-call(s32[2]{0:T(128)S(1)} %pad_add_fusion.place_ref, ...), custom_call_target="tpu_custom_call" | custom-call | flops 201326592 | bytes 2097152 | tf_op jit(solution)/shard_map/pallas_call | solution.py:20
  5.7 3.5 %collective-permute-start.1 = (f32[128,128]{1,0:T(8,128)S(1)}, f32[128,128]{1,0:T(8,128)S(1)}, u32[]{:S(2)}, u32[]{:S(2)}) collective-permute-start(f32[128,128]{1,0:T(8,128)S(1)} %get-tuple-element.45.refs_3_), channel_id=1, source_target_pairs={{0,6},{2,4},{4,2},{6,0},{8,14},{10,12},{12,10},{14,8},{16,22},{18,... | collective-permute-start | bytes 196616 | tf_op jit(solution)/shard_map/ppermute | solution.py:391
  9.2 0.5 %collective-permute-start.2 = (f32[128,128]{1,0:T(8,128)S(1)}, f32[128,128]{1,0:T(8,128)S(1)}, u32[]{:S(2)}, u32[]{:S(2)}) collective-permute-start(f32[128,128]{1,0:T(8,128)S(1)} %get-tuple-element.45.refs_3_), channel_id=1, source_target_pairs={{0,4},{2,6},{4,0},{6,2},{8,12},{10,14},{12,8},{14,10},{16,20},{18,... | collective-permute-start | bytes 196616 | tf_op jit(solution)/shard_map/ppermute | solution.py:391
  9.9 4.0 %collective-permute-start.4 = (bf16[128,128]{1,0:T(8,128)(2,1)S(1)}, bf16[128,128]{1,0:T(8,128)(2,1)S(1)}, u32[]{:S(2)}, u32[]{:S(2)}) collective-permute-start(bf16[128,128]{1,0:T(8,128)(2,1)S(1)} %get-tuple-element.47.refs_7_.val_ref), channel_id=1, source_target_pairs={{0,24},{2,26},{4,28},{6,30},{8,16},{10,18},{12,20},{14,22},{16,8},... | collective-permute-start | bytes 98312 | tf_op jit(solution)/shard_map/ppermute | solution.py:391
  13.9 0.6 %collective-permute-start.6 = (bf16[128,128]{1,0:T(8,128)(2,1)S(1)}, bf16[128,128]{1,0:T(8,128)(2,1)S(1)}, u32[]{:S(2)}, u32[]{:S(2)}) collective-permute-start(bf16[128,128]{1,0:T(8,128)(2,1)S(1)} %get-tuple-element.47.refs_7_.val_ref), channel_id=1, source_target_pairs={{0,8},{2,10},{4,12},{6,14},{8,0},{10,2},{12,4},{14,6},{16,24},{18,... | collective-permute-start | bytes 98312 | tf_op jit(solution)/shard_map/ppermute | solution.py:391
  14.5 1.0 %shard_map.111 = (bf16[512,128]{1,0:T(8,128)(2,1)S(1)}, f32[4,128,128]{2,1,0:T(8,128)S(1)}) custom-call(s32[2]{0:T(128)S(1)} %pad_add_fusion.place_ref, f32[128,128]{1,0:T(8,128)S(1)} %get-tuple-element.44.exit_ref, f32[128,128]{1,0:T(8,128)S(1)} %collective-permute-done.1.refs_0_, f32[128,128]{1,0:T(8,128)S(1)} %collective-permute-done.2.refs_1_, ...), custom_call_target="tpu_custom_call" | custom-call | flops 100663296 | bytes 1000000 | tf_op jit(solution)/shard_map/pallas_call | solution.py:20
  15.5 3.9 %collective-permute-start.7 = (bf16[512,128]{1,0:T(8,128)(2,1)S(1)}, bf16[512,128]{1,0:T(8,128)(2,1)S(1)}, u32[]{:S(2)}, u32[]{:S(2)}) collective-permute-start(bf16[512,128]{1,0:T(8,128)(2,1)S(1)} %get-tuple-element.49.refs_3_), channel_id=1, source_target_pairs={{0,24},{2,26},{4,28},{6,30},{8,16},{10,18},{12,20},{14,22},{16,8},... | collective-permute-start | bytes 393224 | tf_op jit(solution)/shard_map/ppermute | solution.py:391
  19.4 0.6 %collective-permute-start.9 = (bf16[512,128]{1,0:T(8,128)(2,1)S(1)}, bf16[512,128]{1,0:T(8,128)(2,1)S(1)}, u32[]{:S(2)}, u32[]{:S(2)}) collective-permute-start(bf16[512,128]{1,0:T(8,128)(2,1)S(1)} %get-tuple-element.49.refs_3_), channel_id=1, source_target_pairs={{0,8},{2,10},{4,12},{6,14},{8,0},{10,2},{12,4},{14,6},{16,24},{18,... | collective-permute-start | bytes 393224 | tf_op jit(solution)/shard_map/ppermute | solution.py:391
  20.1 1.6 %shard_map.112 = (bf16[512,128]{1,0:T(8,128)(2,1)S(1)}, bf16[128,128]{1,0:T(8,128)(2,1)S(1)}, bf16[128,128]{1,0:T(8,128)(2,1)S(1)}, bf16[128,128]{1,0:T(8,128)(2...) custom-call(s32[2]{0:T(128)S(1)} %pad_add_fusion.place_ref, s32[16]{0:T(128)S(1)} %bitcast.5, ...), custom_call_target="tpu_custom_call" | custom-call | flops 100663296 | bytes 1000000 | tf_op jit(solution)/shard_map/pallas_call | solution.py:20
  21.6 2.7 %collective-permute-start.13 = (bf16[512,128]{1,0:T(8,128)(2,1)S(1)}, bf16[512,128]{1,0:T(8,128)(2,1)S(1)}, u32[]{:S(2)}, u32[]{:S(2)}) collective-permute-start(bf16[512,128]{1,0:T(8,128)(2,1)S(1)} %get-tuple-element.65.refs_7_), channel_id=1, source_target_pairs={{0,6},{2,4},{4,2},{6,0},{8,14},{10,12},{12,10},{14,8},{16,22},{18,... | collective-permute-start | bytes 393224 | tf_op jit(solution)/shard_map/ppermute | solution.py:391
  24.3 2.9 %shard_map.113 = (bf16[4,128,128]{2,1,0:T(8,128)(2,1)S(1)}, f32[4,128,128]{2,1,0:T(8,128)S(1)}, f32[4,128,1]{2,1,0:T(8,128)S(1)}, f32[4,128,1]{2,1,0:T(8,128)S(1)}) custom-call(bf16[128,2048]{1,0:T(8,128)(2,1)S(1)} %get-tuple-element.54.rows_ref, bf16[2048,1024]{1,0:T(8,128)(2,1)} %weight_hbm.3, f32[1,128]{1,0:T(1,128)S(1)} %get-tuple-element.55.gain_ref, ...), custom_call_target="tpu_custom_call" | custom-call | flops 536870912 | bytes 8388608 | tf_op jit(solution)/shard_map/pallas_call | solution.py:20
  27.2 0.6 %collective-permute-start.14 = (bf16[512,128]{1,0:T(8,128)(2,1)S(1)}, bf16[512,128]{1,0:T(8,128)(2,1)S(1)}, u32[]{:S(2)}, u32[]{:S(2)}) collective-permute-start(bf16[512,128]{1,0:T(8,128)(2,1)S(1)} %get-tuple-element.65.refs_7_), channel_id=1, source_target_pairs={{0,4},{2,6},{4,0},{6,2},{8,12},{10,14},{12,8},{14,10},{16,20},{18,... | collective-permute-start | bytes 393224 | tf_op jit(solution)/shard_map/ppermute | solution.py:391
  27.8 0.4 collective-permute-start.15
  28.2 1.6 %collective-permute-done.8.refs_1_ = bf16[512,128]{1,0:T(8,128)(2,1)S(1)} collective-permute-done((bf16[512,128]{1,0:T(8,128)(2,1)S(1)}, bf16[512,128]{1,0:T(8,128)(2,1)S(1)}, u32[]{:S(2)}, u32[]{:S(2)}) %collective-permute-start.8) | collective-permute-done | bytes 131104 | tf_op jit(solution)/shard_map/ppermute | solution.py:391
  29.8 1.4 %shard_map.114 = (bf16[512,128]{1,0:T(8,128)(2,1)S(1)}, bf16[512,128]{1,0:T(8,128)(2,1)S(1)}, bf16[512,128]{1,0:T(8,128)(2,1)S(1)}, bf16[512,128]{1,0:T(8,128)(2,1)S(1)}) custom-call(s32[2]{0:T(128)S(1)} %pad_add_fusion.place_ref, bf16[512,128]{1,0:T(8,128)(2,1)S(1)} %collective-permute-done.7.refs_0_, bf16[512,128]{1,0:T(8,128)(2,1)S(1)} %collective-permute-done.8.refs_1_, ...), custom_call_target="tpu_custom_call" | custom-call | flops 201326592 | bytes 1000000 | tf_op jit(solution)/shard_map/pallas_call | solution.py:20
  31.1 2.5 %collective-permute-start.10 = (bf16[512,128]{1,0:T(8,128)(2,1)S(1)}, bf16[512,128]{1,0:T(8,128)(2,1)S(1)}, u32[]{:S(2)}, u32[]{:S(2)}) collective-permute-start(bf16[512,128]{1,0:T(8,128)(2,1)S(1)} %get-tuple-element.61), channel_id=1, source_target_pairs={{0,6},{2,4},{4,2},{6,0},{8,14},{10,12},{12,10},{14,8},{16,22},{18,... | collective-permute-start | bytes 393224 | tf_op jit(solution)/shard_map/ppermute | solution.py:391
  33.7 0.7 %collective-permute-start.11 = (bf16[512,128]{1,0:T(8,128)(2,1)S(1)}, bf16[512,128]{1,0:T(8,128)(2,1)S(1)}, u32[]{:S(2)}, u32[]{:S(2)}) collective-permute-start(bf16[512,128]{1,0:T(8,128)(2,1)S(1)} %get-tuple-element.62), channel_id=1, source_target_pairs={{0,4},{2,6},{4,0},{6,2},{8,12},{10,14},{12,8},{14,10},{16,20},{18,... | collective-permute-start | bytes 393224 | tf_op jit(solution)/shard_map/ppermute | solution.py:391
  34.7 2.9 %shard_map.115 = (bf16[4,128,128]{2,1,0:T(8,128)(2,1)S(1)}, f32[4,128,128]{2,1,0:T(8,128)S(1)}, f32[4,128,1]{2,1,0:T(8,128)S(1)}, f32[4,128,1]{2,1,0:T(8,128)S(1)}) custom-call(bf16[128,2048]{1,0:T(8,128)(2,1)S(1)} %get-tuple-element.54.rows_ref, bf16[2048,1024]{1,0:T(8,128)(2,1)} %weight_hbm.3, f32[1,128]{1,0:T(1,128)S(1)} %get-tuple-element.55.gain_ref, ...), custom_call_target="tpu_custom_call" | custom-call | flops 536870912 | bytes 8388608 | tf_op jit(solution)/shard_map/pallas_call | solution.py:20
  37.7 2.0 %collective-permute-done.11.refs_1_ = bf16[512,128]{1,0:T(8,128)(2,1)S(1)} collective-permute-done((bf16[512,128]{1,0:T(8,128)(2,1)S(1)}, bf16[512,128]{1,0:T(8,128)(2,1)S(1)}, u32[]{:S(2)}, u32[]{:S(2)}) %collective-permute-start.11) | collective-permute-done | bytes 131104 | tf_op jit(solution)/shard_map/ppermute | solution.py:391
  40.0 4.9 %shard_map.116 = (bf16[64,2048]{1,0:T(8,128)(2,1)S(1)}, bf16[64,2048]{1,0:T(8,128)(2,1)S(1)}) custom-call(s32[2]{0:T(128)S(1)} %pad_add_fusion.place_ref, s32[9]{0:T(128)S(1)} %get-tuple-element.48.table_ref, bf16[512,128]{1,0:T(8,128)(2,1)S(1)} %collective-permute-done.10.refs_0_, bf16[512,128]{1,0:T(8,128)(2,1)S(1)} %collective-permute-done.11.refs_1_, ...), custom_call_target="tpu_custom_call" | custom-call | flops 536870912 | bytes 4000000 | tf_op jit(solution)/shard_map/pallas_call | solution.py:20
  45.0 1.5 %collective-permute-done.16 = bf16[64,2048]{1,0:T(8,128)(2,1)S(1)} collective-permute-done((bf16[64,2048]{1,0:T(8,128)(2,1)S(1)}, bf16[64,2048]{1,0:T(8,128)(2,1)S(1)}, u32[]{:S(2)}, u32[]{:S(2)}) %collective-permute-start.16) | collective-permute-done | bytes 262176 | tf_op jit(solution)/shard_map/ppermute | solution.py:526
  46.5 0.8 %add.3 = bf16[64,2048]{1,0:T(8,128)(2,1)} add(bf16[64,2048]{1,0:T(8,128)(2,1)S(1)} %get-tuple-element.73, bf16[64,2048]{1,0:T(8,128)(2,1)S(1)} %collective-permute-done.16) | non-fusion elementwise | flops 131072 | bytes 786432 | tf_op jit(solution)/shard_map/add | solution.py:526
  (22 shorter events, 1.0 us)
Async XLA Ops:
  0.0 20.0 %copy-start = (s32[1,16]{1,0:T(1,128)S(1)}, s32[1,16]{1,0:T(1,128)}, u32[]{:S(2)}) copy-start(s32[1,16]{1,0:T(1,128)} %param.21) | copy-start | bytes 196
  0.0 2.7 %collective-permute-start = (bf16[64,2048]{1,0:T(8,128)(2,1)}, bf16[64,2048]{1,0:T(8,128)(2,1)S(1)}, u32[]{:S(2)}, u32[]{:S(2)}) collective-permute-start(bf16[64,2048]{1,0:T(8,128)(2,1)} %mine_hbm.1), channel_id=1, source_target_pairs={{0,1},{1,0},{2,3},{3,2},{4,5},{5,4},{6,7},{7,6},{8,9},{9,8},{10,11... | collective-permute-start | bytes 786440 | tf_op jit(solution)/shard_map/ppermute | solution.py:376
  5.7 8.2 %collective-permute-start.1 = (f32[128,128]{1,0:T(8,128)S(1)}, f32[128,128]{1,0:T(8,128)S(1)}, u32[]{:S(2)}, u32[]{:S(2)}) collective-permute-start(f32[128,128]{1,0:T(8,128)S(1)} %get-tuple-element.45.refs_3_), channel_id=1, source_target_pairs={{0,6},{2,4},{4,2},{6,0},{8,14},{10,12},{12,10},{14,8},{16,22},{18,... | collective-permute-start | bytes 196616 | tf_op jit(solution)/shard_map/ppermute | solution.py:391
  9.2 5.2 %collective-permute-start.2 = (f32[128,128]{1,0:T(8,128)S(1)}, f32[128,128]{1,0:T(8,128)S(1)}, u32[]{:S(2)}, u32[]{:S(2)}) collective-permute-start(f32[128,128]{1,0:T(8,128)S(1)} %get-tuple-element.45.refs_3_), channel_id=1, source_target_pairs={{0,4},{2,6},{4,0},{6,2},{8,12},{10,14},{12,8},{14,10},{16,20},{18,... | collective-permute-start | bytes 196616 | tf_op jit(solution)/shard_map/ppermute | solution.py:391
  9.7 4.7 %collective-permute-start.3 = (f32[128,128]{1,0:T(8,128)S(1)}, f32[128,128]{1,0:T(8,128)S(1)}, u32[]{:S(2)}, u32[]{:S(2)}) collective-permute-start(f32[128,128]{1,0:T(8,128)S(1)} %get-tuple-element.45.refs_3_), channel_id=1, source_target_pairs={{0,2},{2,0},{4,6},{6,4},{8,10},{10,8},{12,14},{14,12},{16,18},{18,... | collective-permute-start | bytes 196616 | tf_op jit(solution)/shard_map/ppermute | solution.py:391
  9.9 9.5 %collective-permute-start.4 = (bf16[128,128]{1,0:T(8,128)(2,1)S(1)}, bf16[128,128]{1,0:T(8,128)(2,1)S(1)}, u32[]{:S(2)}, u32[]{:S(2)}) collective-permute-start(bf16[128,128]{1,0:T(8,128)(2,1)S(1)} %get-tuple-element.47.refs_7_.val_ref), channel_id=1, source_target_pairs={{0,24},{2,26},{4,28},{6,30},{8,16},{10,18},{12,20},{14,22},{16,8},... | collective-permute-start | bytes 98312 | tf_op jit(solution)/shard_map/ppermute | solution.py:391
  13.9 6.2 %collective-permute-start.5 = (bf16[128,128]{1,0:T(8,128)(2,1)S(1)}, bf16[128,128]{1,0:T(8,128)(2,1)S(1)}, u32[]{:S(2)}, u32[]{:S(2)}) collective-permute-start(bf16[128,128]{1,0:T(8,128)(2,1)S(1)} %get-tuple-element.47.refs_7_.val_ref), channel_id=1, source_target_pairs={{0,16},{2,18},{4,20},{6,22},{8,24},{10,26},{12,28},{14,30},{16,0},... | collective-permute-start | bytes 98312 | tf_op jit(solution)/shard_map/ppermute | solution.py:391
  13.9 6.2 %collective-permute-start.6 = (bf16[128,128]{1,0:T(8,128)(2,1)S(1)}, bf16[128,128]{1,0:T(8,128)(2,1)S(1)}, u32[]{:S(2)}, u32[]{:S(2)}) collective-permute-start(bf16[128,128]{1,0:T(8,128)(2,1)S(1)} %get-tuple-element.47.refs_7_.val_ref), channel_id=1, source_target_pairs={{0,8},{2,10},{4,12},{6,14},{8,0},{10,2},{12,4},{14,6},{16,24},{18,... | collective-permute-start | bytes 98312 | tf_op jit(solution)/shard_map/ppermute | solution.py:391
  15.5 12.3 %collective-permute-start.7 = (bf16[512,128]{1,0:T(8,128)(2,1)S(1)}, bf16[512,128]{1,0:T(8,128)(2,1)S(1)}, u32[]{:S(2)}, u32[]{:S(2)}) collective-permute-start(bf16[512,128]{1,0:T(8,128)(2,1)S(1)} %get-tuple-element.49.refs_3_), channel_id=1, source_target_pairs={{0,24},{2,26},{4,28},{6,30},{8,16},{10,18},{12,20},{14,22},{16,8},... | collective-permute-start | bytes 393224 | tf_op jit(solution)/shard_map/ppermute | solution.py:391
  19.4 10.4 %collective-permute-start.8 = (bf16[512,128]{1,0:T(8,128)(2,1)S(1)}, bf16[512,128]{1,0:T(8,128)(2,1)S(1)}, u32[]{:S(2)}, u32[]{:S(2)}) collective-permute-start(bf16[512,128]{1,0:T(8,128)(2,1)S(1)} %get-tuple-element.49.refs_3_), channel_id=1, source_target_pairs={{0,16},{2,18},{4,20},{6,22},{8,24},{10,26},{12,28},{14,30},{16,0},... | collective-permute-start | bytes 393224 | tf_op jit(solution)/shard_map/ppermute | solution.py:391
  19.4 10.4 %collective-permute-start.9 = (bf16[512,128]{1,0:T(8,128)(2,1)S(1)}, bf16[512,128]{1,0:T(8,128)(2,1)S(1)}, u32[]{:S(2)}, u32[]{:S(2)}) collective-permute-start(bf16[512,128]{1,0:T(8,128)(2,1)S(1)} %get-tuple-element.49.refs_3_), channel_id=1, source_target_pairs={{0,8},{2,10},{4,12},{6,14},{8,0},{10,2},{12,4},{14,6},{16,24},{18,... | collective-permute-start | bytes 393224 | tf_op jit(solution)/shard_map/ppermute | solution.py:391
  21.6 12.7 %collective-permute-start.13 = (bf16[512,128]{1,0:T(8,128)(2,1)S(1)}, bf16[512,128]{1,0:T(8,128)(2,1)S(1)}, u32[]{:S(2)}, u32[]{:S(2)}) collective-permute-start(bf16[512,128]{1,0:T(8,128)(2,1)S(1)} %get-tuple-element.65.refs_7_), channel_id=1, source_target_pairs={{0,6},{2,4},{4,2},{6,0},{8,14},{10,12},{12,10},{14,8},{16,22},{18,... | collective-permute-start | bytes 393224 | tf_op jit(solution)/shard_map/ppermute | solution.py:391
  27.2 10.4 %collective-permute-start.14 = (bf16[512,128]{1,0:T(8,128)(2,1)S(1)}, bf16[512,128]{1,0:T(8,128)(2,1)S(1)}, u32[]{:S(2)}, u32[]{:S(2)}) collective-permute-start(bf16[512,128]{1,0:T(8,128)(2,1)S(1)} %get-tuple-element.65.refs_7_), channel_id=1, source_target_pairs={{0,4},{2,6},{4,0},{6,2},{8,12},{10,14},{12,8},{14,10},{16,20},{18,... | collective-permute-start | bytes 393224 | tf_op jit(solution)/shard_map/ppermute | solution.py:391
  27.8 9.8 %collective-permute-start.15 = (bf16[512,128]{1,0:T(8,128)(2,1)S(1)}, bf16[512,128]{1,0:T(8,128)(2,1)S(1)}, u32[]{:S(2)}, u32[]{:S(2)}) collective-permute-start(bf16[512,128]{1,0:T(8,128)(2,1)S(1)} %get-tuple-element.65.refs_7_), channel_id=1, source_target_pairs={{0,2},{2,0},{4,6},{6,4},{8,10},{10,8},{12,14},{14,12},{16,18},{18,... | collective-permute-start | bytes 393224 | tf_op jit(solution)/shard_map/ppermute | solution.py:391
  31.1 6.5 %collective-permute-start.10 = (bf16[512,128]{1,0:T(8,128)(2,1)S(1)}, bf16[512,128]{1,0:T(8,128)(2,1)S(1)}, u32[]{:S(2)}, u32[]{:S(2)}) collective-permute-start(bf16[512,128]{1,0:T(8,128)(2,1)S(1)} %get-tuple-element.61), channel_id=1, source_target_pairs={{0,6},{2,4},{4,2},{6,0},{8,14},{10,12},{12,10},{14,8},{16,22},{18,... | collective-permute-start | bytes 393224 | tf_op jit(solution)/shard_map/ppermute | solution.py:391
  33.7 6.0 %collective-permute-start.11 = (bf16[512,128]{1,0:T(8,128)(2,1)S(1)}, bf16[512,128]{1,0:T(8,128)(2,1)S(1)}, u32[]{:S(2)}, u32[]{:S(2)}) collective-permute-start(bf16[512,128]{1,0:T(8,128)(2,1)S(1)} %get-tuple-element.62), channel_id=1, source_target_pairs={{0,4},{2,6},{4,0},{6,2},{8,12},{10,14},{12,8},{14,10},{16,20},{18,... | collective-permute-start | bytes 393224 | tf_op jit(solution)/shard_map/ppermute | solution.py:391
  34.3 5.6 %collective-permute-start.12 = (bf16[512,128]{1,0:T(8,128)(2,1)S(1)}, bf16[512,128]{1,0:T(8,128)(2,1)S(1)}, u32[]{:S(2)}, u32[]{:S(2)}) collective-permute-start(bf16[512,128]{1,0:T(8,128)(2,1)S(1)} %get-tuple-element.63), channel_id=1, source_target_pairs={{0,2},{2,0},{4,6},{6,4},{8,10},{10,8},{12,14},{14,12},{16,18},{18,... | collective-permute-start | bytes 393224 | tf_op jit(solution)/shard_map/ppermute | solution.py:391
  44.9 1.6 %collective-permute-start.16 = (bf16[64,2048]{1,0:T(8,128)(2,1)S(1)}, bf16[64,2048]{1,0:T(8,128)(2,1)S(1)}, u32[]{:S(2)}, u32[]{:S(2)}) collective-permute-start(bf16[64,2048]{1,0:T(8,128)(2,1)S(1)} %get-tuple-element.74), channel_id=1, source_target_pairs={{0,1},{1,0},{2,3},{3,2},{4,5},{5,4},{6,7},{7,6},{8,9},{9,8},{10,11... | collective-permute-start | bytes 786440 | tf_op jit(solution)/shard_map/ppermute | solution.py:526

commit v8 on v7

--- a/solution.py
+++ b/solution.py
@@ -101,9 +101,9 @@
         copy.wait()
 
 
-def prepare_kernel(place_ref, mine_ref, other_ref, weight_ref, rate_ref, bias_ref, gain_ref,
+def prepare_kernel(core_ref, mine_ref, other_ref, weight_ref, rate_ref, bias_ref, gain_ref,
                    rows_ref, kn_ref, val_ref, dirs_ref, coeff_ref, solved_ref, exit_ref, turn_ref):
-    core = place_ref[1]
+    core = core_ref[0]
     half = mine_ref.shape[0]
     rows_ref[pl.ds(pl.multiple_of(core * half, half), half), :] = mine_ref[...]
     rows_ref[pl.ds(pl.multiple_of((1 - core) * half, half), half), :] = other_ref[...]
@@ -135,24 +135,20 @@
     turn_ref[...] = jnp.where(heads == lanes, 1.0, 0.0) - crossed[tokens:]
 
 
-def in_order(place_ref, turn_refs, turns_ref):
-    group = len(turn_refs)
+def leave_kernel(group, place_ref, exit_ref, *refs):
+    turn_refs, (leave_ref, starts_ref) = refs[:group], refs[group : group + 2]
+    near_refs, (turns_ref, seen_ref) = refs[group + 2 : -2], refs[-2:]
     member = place_ref[0] % group
+    tokens, size = exit_ref.shape
     for step in range(group):
         turns_ref[source_of(member, step, group)] = turn_refs[group - 1 - step][...]
-    return member
-
-
-def leave_kernel(group, place_ref, exit_ref, *refs):
-    turn_refs, (leave_ref, starts_ref, turns_ref) = refs[:group], refs[group:]
-    member = in_order(place_ref, turn_refs, turns_ref)
-    tokens, size = exit_ref.shape
     own = exit_ref[...]
     keys = own
     product = None
     heads, lanes = iota2((size, size))
     starts_ref[0] = jnp.where(heads == lanes, 1.0, 0.0)
     for index in range(group):
+        seen_ref[index] = keys.astype(BF16)
         turn = turns_ref[index]
         product = turn if product is None else dot3(product, turn)
         if index:
@@ -165,42 +161,36 @@
     high, low = split(product)
     leave_ref[2 * tokens : 2 * tokens + size] = high
     leave_ref[2 * tokens + size :] = low
-
-
-def bundle_kernel(group, place_ref, mask_ref, exit_ref, after_ref, *refs):
-    groups = len(refs) - 2 * group - 4
-    turn_refs, val_refs, line_ref = refs[:group], refs[group : group + groups], refs[group + groups]
-    near_refs, (table_ref, turns_ref, seen_ref) = refs[-group - 3 : -3], refs[-3:]
-    member = in_order(place_ref, turn_refs, turns_ref)
+    for step in range(group):
+        near_refs[step][...] = seen_ref[target_of(member, step, group)]
+
+
+def word_of(slot, segments):
+    bits = segments.bit_length()
+    per_word = 31 // bits
+    return slot // per_word, bits * (slot % per_word), (1 << bits) - 1
+
+
+def bundle_kernel(group, groups, most, place_ref, mask_ref, after_ref, *refs):
+    val_refs, (line_ref, table_ref) = refs[:groups], refs[groups:]
     place = place_ref[0]
     mine = place // group
-    most = (table_ref.shape[0] - 1) // 2
-    for slot in range(most):
-        table_ref[2 * slot] = 0
-        table_ref[2 * slot + 1] = mine
     segments = mask_ref.shape[0]
+    for word in range(table_ref.shape[0]):
+        table_ref[word] = 0
 
     def pick(segment, count):
         wanted = (mask_ref[segment] > 0) & (segment < place) & (count < most)
+        word, shift, _ = word_of(count, segments)
 
         @pl.when(wanted)
         def _():
-            table_ref[2 * count] = target_of(segment % group, member, group) if (
-                group & (group - 1) == 0
-            ) else (member + group - segment % group) % group
-            table_ref[2 * count + 1] = segment // group
+            table_ref[word] = table_ref[word] | ((segment + 1) << shift)
 
         return count + wanted.astype(jnp.int32)
 
-    table_ref[2 * most] = lax.fori_loop(0, segments, pick, jnp.int32(0))
-    tokens, size = exit_ref.shape
-    keys = exit_ref[...]
-    for index in range(group):
-        if index > 1:
-            keys = jnp.where(index - 1 > member, dot3(keys, turns_ref[index - 1]), exit_ref[...])
-        seen_ref[index] = keys.astype(BF16)
-    for step in range(group):
-        near_refs[step][...] = seen_ref[target_of(member, step, group)]
+    lax.fori_loop(0, segments, pick, jnp.int32(0))
+    tokens = val_refs[0].shape[0]
     for way in range(groups):
         at = pl.multiple_of(source_of(mine, way, groups) * tokens, tokens)
         line_ref[pl.ds(at, tokens), :] = val_refs[groups - 1 - way][...]
@@ -281,7 +271,7 @@
         far_refs[step][(groups - 1) * tokens :] = near_refs[step][...]
 
 
-def attend_kernel(group, place_ref, table_ref, *refs):
+def attend_kernel(group, segments, most, place_ref, core_ref, table_ref, *refs):
     far_refs, line_refs = refs[:group][::-1], refs[group : 2 * group][::-1]
     parts = (len(refs) - 2 * group - 8) // 4
     owns, refs = [refs[2 * group + 4 * n : 2 * group + 4 * n + 4] for n in range(parts)], refs[
@@ -297,10 +287,8 @@
     ]
     for copy in copies:
         copy.start()
-    core = place_ref[1]
-    mine = place_ref[0] // group
-    most = (table_ref.shape[0] - 1) // 2
-    found = table_ref[2 * most]
+    core = core_ref[0]
+    mine, member = place_ref[0] // group, place_ref[0] % group
     heads, tokens, size = owns[0][0].shape
     groups = far_refs[0].shape[0] // tokens
     scaling = 1.0 / math.sqrt(size)
@@ -308,24 +296,31 @@
     lanes = lax.broadcasted_iota(jnp.int32, (tokens, chunk * tokens), 1)
 
     def collect(turn):
+        found = jnp.int32(0)
         for slot in range(chunk):
             part = slice(slot * tokens, (slot + 1) * tokens)
-            step, source = table_ref[2 * (turn * chunk + slot)], table_ref[2 * (turn * chunk + slot) + 1]
+            word, shift, ones = word_of(turn * chunk + slot, segments)
+            code = (table_ref[word] >> shift) & ones
+            found = found + (code > 0).astype(jnp.int32)
+            segment = jnp.maximum(code - 1, 0)
+            whose, source = segment % group, segment // group
             before = jnp.where(source < mine, source, groups - 1)
             before = pl.multiple_of(before * tokens, tokens)
             after = pl.multiple_of(source * tokens, tokens)
             for number in range(group):
 
-                @pl.when(step == number)
+                @pl.when(whose == source_of(member, number, group))
                 def _():
                     vals_ref[part, :] = line_refs[number][pl.ds(after, tokens), :]
                     keys_ref[part, :] = far_refs[number][pl.ds(before, tokens), :]
 
-    def advance(moved, turn, peak, total, weighted):
+        return found * tokens
+
+    def advance(moved, kept, peak, total, weighted):
         scores = lax.dot_general(
             moved, keys_ref[...], (((1,), (1,)), ((), ())), preferred_element_type=F32
         )
-        scores = jnp.where(lanes < (found - turn * chunk) * tokens, scores * scaling, NEGATIVE)
+        scores = jnp.where(lanes < kept, scores * scaling, NEGATIVE)
         new_peak = jnp.maximum(peak, jnp.max(scores, axis=1, keepdims=True))
         fading = jnp.exp(peak - new_peak)
         weights = jnp.exp(scores - new_peak)
@@ -338,18 +333,17 @@
     half = kept_ref.shape[0]
     turns = most // chunk
     if turns == 1:
-        collect(0)
+        kept = collect(0)
     for number in range(parts * heads):
         moved_ref, weighted_ref, peak_ref, total_ref = owns[number // heads]
         h = number % heads
         state = (peak_ref[h], total_ref[h], weighted_ref[h])
         if turns == 1:
-            _, total, weighted = advance(moved_ref[h], 0, *state)
+            _, total, weighted = advance(moved_ref[h], kept, *state)
         else:
 
             def step_of(turn, state, moved_ref=moved_ref, h=h):
-                collect(turn)
-                return advance(moved_ref[h], turn, *state)
+                return advance(moved_ref[h], collect(turn), *state)
 
             _, total, weighted = lax.fori_loop(0, turns, step_of, state)
         done = (weighted * (1.0 / total)).astype(BF16)
@@ -369,8 +363,8 @@
     hidden, w_query, w_key, w_value, w_dir, u_rate, rate_bias, q_gain, k_gain, w_out, block_mask
 ):
     segments = lax.axis_size("ctx")
-    position = lax.axis_index("ctx")
-    core = lax.axis_index("head")
+    place = lax.axis_index("ctx").astype(jnp.int32).reshape(1)
+    core = lax.axis_index("head").astype(jnp.int32).reshape(1)
     group = max(d for d in range(1, math.isqrt(segments) + 1) if segments % d == 0)
     groups = segments // group
     other = lax.ppermute(hidden, "head", [(0, 1), (1, 0)])
@@ -383,7 +377,6 @@
     hbm = pl.BlockSpec(memory_space=pltpu.HBM)
     anywhere = pl.BlockSpec(memory_space=pl.ANY)
     square = shaped((tokens, size), F32)
-    place = jnp.stack([position, core]).astype(jnp.int32)
 
     def swapped(values, count, pairs_of):
         out = [values[0]] * count
@@ -424,46 +417,47 @@
             shaped((tokens, width), BF16), square, shaped((tokens, size), BF16), square, square,
             square, square, shaped((size, size), F32),
         ),
-        (place, mine, other, weights, rate_row, rate_bias, key_gain),
+        (core, mine, other, weights, rate_row, rate_bias, key_gain),
         in_specs=[smem] + [vmem] * 4 + [smem, vmem],
         flops=6 * tokens * width * size,
         moved=8 * width * size,
     )
     turns = within_group([turn] * group)
     line = along_line([val] * groups)
-    leaving, starts = call(
+    leaving, starts, *near = call(
         functools.partial(leave_kernel, group),
         [
             shaped((2 * tokens + 2 * size, size), BF16),
             shaped((group, size, size), F32),
-        ],
+        ]
+        + [shaped((tokens, size), BF16)] * group,
         (place, exit_keys, *turns[::-1]),
         in_specs=[smem] + [vmem] * (1 + group),
-        scratch=(pltpu.VMEM((group, size, size), F32),),
-        flops=12 * group * size**3,
-        moved=10**6,
-    )
-    arrived = along_line([leaving] * groups)
-    values, *near, table = call(
-        functools.partial(bundle_kernel, group),
-        [shaped((groups * tokens, size), BF16)]
-        + [shaped((tokens, size), BF16)] * group
-        + [shaped((2 * (segments // 4) + 1,), jnp.int32)],
-        (place, block_mask[0], exit_keys, starts, *turns[::-1], *line[::-1]),
-        in_specs=[smem, smem, vmem, anywhere] + [vmem] * (group + groups),
-        out_specs=[vmem] * (1 + group) + [smem],
         scratch=(
             pltpu.VMEM((group, size, size), F32),
             pltpu.VMEM((group, tokens, size), BF16),
         ),
         flops=12 * group * size**3,
         moved=10**6,
+    )
+    arrived = along_line([leaving] * groups)
+    most = segments // 4
+    values, table = call(
+        functools.partial(bundle_kernel, group, groups, most),
+        [
+            shaped((groups * tokens, size), BF16),
+            shaped((word_of(most - 1, segments)[0] + 1,), jnp.int32),
+        ],
+        (place, block_mask[0], starts, *line[::-1]),
+        in_specs=[smem, smem, anywhere] + [vmem] * groups,
+        out_specs=[vmem, smem],
+        moved=10**6,
         limit=8 + group * groups // 4,
     )
     values = within_group([values] * group)
-    calls = math.gcd(heads, 2)
+    calls = 1
     each = heads // calls
-    pieces = math.gcd(each, 2)
+    pieces = math.gcd(each, 4)
     owns = [
         call(
             functools.partial(query_kernel, number * each * size),
@@ -481,15 +475,15 @@
             ),
             flops=4 * tokens * width * each * size,
             moved=8 * width * each * size,
-            limit=12,
+            limit=16,
         )
         for number in range(calls)
     ]
     far = call(
         functools.partial(arrive_kernel, groups, group, tokens),
         [shaped((groups * tokens, size), BF16)] * group,
-        (place, *arrived[::-1], starts, *near, owns[0][2]),
-        in_specs=[smem] + [vmem] * (groups + 1 + group) + [anywhere],
+        (place, *arrived[::-1], starts, *near),
+        in_specs=[smem] + [vmem] * (groups + 1 + group),
         scratch=(
             pltpu.VMEM((groups, tokens, size), F32),
             pltpu.VMEM((groups, size, size), F32),
@@ -499,7 +493,6 @@
         limit=8 + group * groups // 4,
     )
     far = within_group(far)
-    most = segments // 4
     chunk = math.gcd(most, 4)
     width_out = w_out.shape[1]
     pieces = math.gcd(width_out // size, 4)
@@ -511,13 +504,13 @@
         pltpu.SemaphoreType.DMA((pieces,)),
     ]
     away, kept = call(
-        functools.partial(attend_kernel, group),
+        functools.partial(attend_kernel, group, segments, most),
         [shaped((half, width_out), BF16)] * 2,
         (
-            place, table, *far[::-1], *values[::-1], *(array for own in owns for array in own),
+            place, core, table, *far[::-1], *values[::-1], *(array for own in owns for array in own),
             in_hbm(w_out),
         ),
-        in_specs=[smem] * 2 + [vmem] * (2 * group + 4 * calls) + [hbm],
+        in_specs=[smem] * 3 + [vmem] * (2 * group + 4 * calls) + [hbm],
         scratch=scratch,
         flops=2 * tokens * width_out * heads * size,
         moved=4 * 10**6,

time: 47.4 us -> 45.8 us (0.966)
  Pallas kernels: 19.2 us -> 16.3 us
  waiting for transfers between devices: 5.46 us -> 6.97 us
    pallas_call x8 -> x7, Pallas kernels: 19.2 us -> 16.3 us  [call(): pl.pallas_call(kernel, out_shape=out_shape, in_specs=in_specs or [vmem] *...]
    ppermute x15, waiting for transfers between devices: 3.93 us -> 5.45 us  [swapped(): out[step] = lax.ppermute(values[step], 'ctx', pairs_of(step))]
  transfers between devices with their start and end apart: 17 -> 17, of which waited for: 4 -> 4; matrix products, arithmetic and copies ran while one was open for 0% -> 0% of each run, Pallas kernels for 24% -> 19%
where the time goes in v8:
time: 45.8 us; the launch traced here: 45.7 us
  starting transfers between devices  20.9 us (46%)
  Pallas kernels  16.3 us (36%)
  waiting for transfers between devices  6.97 us (15%)
  other arithmetic  0.77 us (2%)
  between operations  0.76 us (2%)
    ppermute x15, starting transfers between devices, swapped(): out[step] = lax.ppermute(values[step], 'ctx', pairs_of(step))  20.4 us
    pallas_call x7, Pallas kernels, call(): pl.pallas_call(kernel, out_shape=out_shape, in_specs=in_specs or [vmem] *...  16.3 us
    ppermute x15, waiting for transfers between devices, swapped(): out[step] = lax.ppermute(values[step], 'ctx', pairs_of(step))  5.45 us
    ppermute x1, waiting for transfers between devices, body(): return kept + lax.ppermute(away, 'head', [(0, 1), (1, 0)])  1.52 us
  transfers between devices with their start and end apart: 17, of which 4 were waited for; matrix products, arithmetic and copies ran while one was open for 0% of the time, Pallas kernels for 19%

profile of v8, /device:TPU:0, one launch (start us, length us, event | category | flops | bytes accessed | tf_op | source)
XLA Modules:
  0.0 45.7 jit_solution(8787007980760048461)
XLA Ops:
  0.0 0.5 collective-permute-start
  1.1 1.5 %shard_map.109 = (bf16[2048,384]{1,0:T(8,128)(2,1)S(1)}, bf16[1,2048]{1,0:T(2,128)(2,1)S(1)}, f32[1,128]{1,0:T(1,128)S(1)}, f32[1,128]{1,0:T(1,128)S(1)}, bf16[64,2048]{1,0:T(8,128)(2,1)S(1)}) custom-call(bf16[2048,128]{1,0:T(8,128)(2,1)} %key_hbm.1, bf16[2048,128]{1,0:T(8,128)(2,1)} %dir_hbm.1, bf16[2048,128]{1,0:T(8,128)(2,1)} %value_hbm.1, ...), custom_call_target="tpu_custom_call" | custom-call | bytes 3145728 | tf_op jit(solution)/shard_map/pallas_call | solution.py:20
  2.7 2.4 %shard_map.110 = (bf16[128,2048]{1,0:T(8,128)(2,1)S(1)}, f32[128,128]{1,0:T(8,128)S(1)}, bf16[128,128]{1,0:T(8,128)(2,1)S(1)}, f32[128,128]{1,0:T(8,128)S(1)}, f...) custom-call(s32[1]{0:T(128)} %bitcast.1.core_ref, ...), custom_call_target="tpu_custom_call" | custom-call | flops 201326592 | bytes 2097152 | tf_op jit(solution)/shard_map/pallas_call | solution.py:20
  5.1 3.5 %collective-permute-start.1 = (f32[128,128]{1,0:T(8,128)S(1)}, f32[128,128]{1,0:T(8,128)S(1)}, u32[]{:S(2)}, u32[]{:S(2)}) collective-permute-start(f32[128,128]{1,0:T(8,128)S(1)} %get-tuple-element.41.refs_3_), channel_id=1, source_target_pairs={{0,6},{2,4},{4,2},{6,0},{8,14},{10,12},{12,10},{14,8},{16,22},{18,... | collective-permute-start | bytes 196616 | tf_op jit(solution)/shard_map/ppermute | solution.py:384
  8.6 0.5 %collective-permute-start.2 = (f32[128,128]{1,0:T(8,128)S(1)}, f32[128,128]{1,0:T(8,128)S(1)}, u32[]{:S(2)}, u32[]{:S(2)}) collective-permute-start(f32[128,128]{1,0:T(8,128)S(1)} %get-tuple-element.41.refs_3_), channel_id=1, source_target_pairs={{0,4},{2,6},{4,0},{6,2},{8,12},{10,14},{12,8},{14,10},{16,20},{18,... | collective-permute-start | bytes 196616 | tf_op jit(solution)/shard_map/ppermute | solution.py:384
  9.3 4.0 %collective-permute-start.4 = (bf16[128,128]{1,0:T(8,128)(2,1)S(1)}, bf16[128,128]{1,0:T(8,128)(2,1)S(1)}, u32[]{:S(2)}, u32[]{:S(2)}) collective-permute-start(bf16[128,128]{1,0:T(8,128)(2,1)S(1)} %get-tuple-element.43.refs_3_.val_ref), channel_id=1, source_target_pairs={{0,24},{2,26},{4,28},{6,30},{8,16},{10,18},{12,20},{14,22},{16,8},... | collective-permute-start | bytes 98312 | tf_op jit(solution)/shard_map/ppermute | solution.py:384
  13.3 0.6 %collective-permute-start.6 = (bf16[128,128]{1,0:T(8,128)(2,1)S(1)}, bf16[128,128]{1,0:T(8,128)(2,1)S(1)}, u32[]{:S(2)}, u32[]{:S(2)}) collective-permute-start(bf16[128,128]{1,0:T(8,128)(2,1)S(1)} %get-tuple-element.43.refs_3_.val_ref), channel_id=1, source_target_pairs={{0,8},{2,10},{4,12},{6,14},{8,0},{10,2},{12,4},{14,6},{16,24},{18,... | collective-permute-start | bytes 98312 | tf_op jit(solution)/shard_map/ppermute | solution.py:384
  13.9 0.5 %shard_map.111 = (bf16[512,128]{1,0:T(8,128)(2,1)S(1)}, f32[4,128,128]{2,1,0:T(8,128)S(1)}, bf16[128,128]{1,0:T(8,128)(2,1)S(1)}, bf16[128,128]{1,0:T(8,128)(2,1...) custom-call(s32[1]{0:T(128)} %bitcast.place_ref, f32[128,128]{1,0:T(8,128)S(1)} %get-tuple-element.40.exit_ref, ...), custom_call_target="tpu_custom_call" | custom-call | flops 100663296 | bytes 1000000 | tf_op jit(solution)/shard_map/pallas_call | solution.py:20
  14.4 3.9 %collective-permute-start.7 = (bf16[512,128]{1,0:T(8,128)(2,1)S(1)}, bf16[512,128]{1,0:T(8,128)(2,1)S(1)}, u32[]{:S(2)}, u32[]{:S(2)}) collective-permute-start(bf16[512,128]{1,0:T(8,128)(2,1)S(1)} %get-tuple-element.45.refs_3_), channel_id=1, source_target_pairs={{0,24},{2,26},{4,28},{6,30},{8,16},{10,18},{12,20},{14,22},{16,8},... | collective-permute-start | bytes 393224 | tf_op jit(solution)/shard_map/ppermute | solution.py:384
  18.3 0.6 %collective-permute-start.9 = (bf16[512,128]{1,0:T(8,128)(2,1)S(1)}, bf16[512,128]{1,0:T(8,128)(2,1)S(1)}, u32[]{:S(2)}, u32[]{:S(2)}) collective-permute-start(bf16[512,128]{1,0:T(8,128)(2,1)S(1)} %get-tuple-element.45.refs_3_), channel_id=1, source_target_pairs={{0,8},{2,10},{4,12},{6,14},{8,0},{10,2},{12,4},{14,6},{16,24},{18,... | collective-permute-start | bytes 393224 | tf_op jit(solution)/shard_map/ppermute | solution.py:384
  18.9 3.6 %collective-permute-done.5.refs_1_ = bf16[128,128]{1,0:T(8,128)(2,1)S(1)} collective-permute-done((bf16[128,128]{1,0:T(8,128)(2,1)S(1)}, bf16[128,128]{1,0:T(8,128)(2,1)S(1)}, u32[]{:S(2)}, u32[]{:S(2)}) %collective-permute-start.5) | collective-permute-done | bytes 32800 | tf_op jit(solution)/shard_map/ppermute | solution.py:384
  22.5 1.3 %shard_map.112 = (bf16[512,128]{1,0:T(8,128)(2,1)S(1)}, s32[1]{0:T(128)}) custom-call(s32[1]{0:T(128)} %bitcast.place_ref, s32[16]{0:T(128)S(1)} %bitcast.5, f32[4,128,128]{2,1,0:T(8,128)S(1)} %get-tuple-element.42.after_ref.refs_4_, bf16[128,128]{1,0:T(8,128)(2,1)S(1)} %collective-permute-done.4.refs_0_, ...), custom_call_target="tpu_custom_call" | custom-call | bytes 1000000 | tf_op jit(solution)/shard_map/pallas_call | solution.py:20
  23.8 2.4 %collective-permute-start.13 = (bf16[512,128]{1,0:T(8,128)(2,1)S(1)}, bf16[512,128]{1,0:T(8,128)(2,1)S(1)}, u32[]{:S(2)}, u32[]{:S(2)}) collective-permute-start(bf16[512,128]{1,0:T(8,128)(2,1)S(1)} %get-tuple-element.54.refs_7_), channel_id=1, source_target_pairs={{0,6},{2,4},{4,2},{6,0},{8,14},{10,12},{12,10},{14,8},{16,22},{18,... | collective-permute-start | bytes 393224 | tf_op jit(solution)/shard_map/ppermute | solution.py:384
  26.2 1.2 %collective-permute-start.15 = (bf16[512,128]{1,0:T(8,128)(2,1)S(1)}, bf16[512,128]{1,0:T(8,128)(2,1)S(1)}, u32[]{:S(2)}, u32[]{:S(2)}) collective-permute-start(bf16[512,128]{1,0:T(8,128)(2,1)S(1)} %get-tuple-element.54.refs_7_), channel_id=1, source_target_pairs={{0,2},{2,0},{4,6},{6,4},{8,10},{10,8},{12,14},{14,12},{16,18},{18,... | collective-permute-start | bytes 393224 | tf_op jit(solution)/shard_map/ppermute | solution.py:384
  27.4 1.3 %collective-permute-done.8.refs_1_ = bf16[512,128]{1,0:T(8,128)(2,1)S(1)} collective-permute-done((bf16[512,128]{1,0:T(8,128)(2,1)S(1)}, bf16[512,128]{1,0:T(8,128)(2,1)S(1)}, u32[]{:S(2)}, u32[]{:S(2)}) %collective-permute-start.8) | collective-permute-done | bytes 131104 | tf_op jit(solution)/shard_map/ppermute | solution.py:384
  28.7 0.8 %shard_map.113 = (bf16[512,128]{1,0:T(8,128)(2,1)S(1)}, bf16[512,128]{1,0:T(8,128)(2,1)S(1)}, bf16[512,128]{1,0:T(8,128)(2,1)S(1)}, bf16[512,128]{1,0:T(8,128)(2,1)S(1)}) custom-call(s32[1]{0:T(128)} %bitcast.place_ref, bf16[512,128]{1,0:T(8,128)(2,1)S(1)} %collective-permute-done.7.refs_0_, bf16[512,128]{1,0:T(8,128)(2,1)S(1)} %collective-permute-done.8.refs_1_, ...), custom_call_target="tpu_custom_call" | custom-call | flops 201326592 | bytes 1000000 | tf_op jit(solution)/shard_map/pallas_call | solution.py:20
  29.5 2.5 %collective-permute-start.10 = (bf16[512,128]{1,0:T(8,128)(2,1)S(1)}, bf16[512,128]{1,0:T(8,128)(2,1)S(1)}, u32[]{:S(2)}, u32[]{:S(2)}) collective-permute-start(bf16[512,128]{1,0:T(8,128)(2,1)S(1)} %get-tuple-element.50), channel_id=1, source_target_pairs={{0,6},{2,4},{4,2},{6,0},{8,14},{10,12},{12,10},{14,8},{16,22},{18,... | collective-permute-start | bytes 393224 | tf_op jit(solution)/shard_map/ppermute | solution.py:384
  32.0 0.6 %collective-permute-start.11 = (bf16[512,128]{1,0:T(8,128)(2,1)S(1)}, bf16[512,128]{1,0:T(8,128)(2,1)S(1)}, u32[]{:S(2)}, u32[]{:S(2)}) collective-permute-start(bf16[512,128]{1,0:T(8,128)(2,1)S(1)} %get-tuple-element.51), channel_id=1, source_target_pairs={{0,4},{2,6},{4,0},{6,2},{8,12},{10,14},{12,8},{14,10},{16,20},{18,... | collective-permute-start | bytes 393224 | tf_op jit(solution)/shard_map/ppermute | solution.py:384
  32.7 0.4 collective-permute-start.12
  33.1 4.6 %shard_map.114 = (bf16[8,128,128]{2,1,0:T(8,128)(2,1)S(1)}, f32[8,128,128]{2,1,0:T(8,128)S(1)}, f32[8,128,1]{2,1,0:T(8,128)S(1)}, f32[8,128,1]{2,1,0:T(8,128)S(1)}) custom-call(bf16[128,2048]{1,0:T(8,128)(2,1)S(1)} %get-tuple-element.55.rows_ref, bf16[2048,1024]{1,0:T(8,128)(2,1)} %weight_hbm.1, f32[1,128]{1,0:T(1,128)S(1)} %get-tuple-element.56.gain_ref, ...), custom_call_target="tpu_custom_call" | custom-call | flops 1073741824 | bytes 16777216 | tf_op jit(solution)/shard_map/pallas_call | solution.py:20
  37.7 0.6 %collective-permute-done.11.refs_1_ = bf16[512,128]{1,0:T(8,128)(2,1)S(1)} collective-permute-done((bf16[512,128]{1,0:T(8,128)(2,1)S(1)}, bf16[512,128]{1,0:T(8,128)(2,1)S(1)}, u32[]{:S(2)}, u32[]{:S(2)}) %collective-permute-start.11) | collective-permute-done | bytes 131104 | tf_op jit(solution)/shard_map/ppermute | solution.py:384
  38.3 5.0 %shard_map.115 = (bf16[64,2048]{1,0:T(8,128)(2,1)S(1)}, bf16[64,2048]{1,0:T(8,128)(2,1)S(1)}) custom-call(s32[1]{0:T(128)} %bitcast.place_ref, s32[1]{0:T(128)} %bitcast.1.core_ref, s32[1]{0:T(128)} %get-tuple-element.44.table_ref, bf16[512,128]{1,0:T(8,128)(2,1)S(1)} %collective-permute-done.10.refs_0_, ...), custom_call_target="tpu_custom_call" | custom-call | flops 536870912 | bytes 4000000 | tf_op jit(solution)/shard_map/pallas_call | solution.py:20
  43.4 1.5 %collective-permute-done.16 = bf16[64,2048]{1,0:T(8,128)(2,1)S(1)} collective-permute-done((bf16[64,2048]{1,0:T(8,128)(2,1)S(1)}, bf16[64,2048]{1,0:T(8,128)(2,1)S(1)}, u32[]{:S(2)}, u32[]{:S(2)}) %collective-permute-start.16) | collective-permute-done | bytes 262176 | tf_op jit(solution)/shard_map/ppermute | solution.py:519
  44.9 0.8 %add.3 = bf16[64,2048]{1,0:T(8,128)(2,1)} add(bf16[64,2048]{1,0:T(8,128)(2,1)S(1)} %get-tuple-element.65, bf16[64,2048]{1,0:T(8,128)(2,1)S(1)} %collective-permute-done.16) | non-fusion elementwise | flops 131072 | bytes 786432 | tf_op jit(solution)/shard_map/add | solution.py:519
  (20 shorter events, 0.3 us)
Async XLA Ops:
  0.0 22.5 %copy-start = (s32[1,16]{1,0:T(1,128)S(1)}, s32[1,16]{1,0:T(1,128)}, u32[]{:S(2)}) copy-start(s32[1,16]{1,0:T(1,128)} %param.21) | copy-start | bytes 196
  0.0 2.6 %collective-permute-start = (bf16[64,2048]{1,0:T(8,128)(2,1)}, bf16[64,2048]{1,0:T(8,128)(2,1)S(1)}, u32[]{:S(2)}, u32[]{:S(2)}) collective-permute-start(bf16[64,2048]{1,0:T(8,128)(2,1)} %mine_hbm.1), channel_id=1, source_target_pairs={{0,1},{1,0},{2,3},{3,2},{4,5},{5,4},{6,7},{7,6},{8,9},{9,8},{10,11... | collective-permute-start | bytes 786440 | tf_op jit(solution)/shard_map/ppermute | solution.py:370
  5.1 8.2 %collective-permute-start.1 = (f32[128,128]{1,0:T(8,128)S(1)}, f32[128,128]{1,0:T(8,128)S(1)}, u32[]{:S(2)}, u32[]{:S(2)}) collective-permute-start(f32[128,128]{1,0:T(8,128)S(1)} %get-tuple-element.41.refs_3_), channel_id=1, source_target_pairs={{0,6},{2,4},{4,2},{6,0},{8,14},{10,12},{12,10},{14,8},{16,22},{18,... | collective-permute-start | bytes 196616 | tf_op jit(solution)/shard_map/ppermute | solution.py:384
  8.6 5.2 %collective-permute-start.2 = (f32[128,128]{1,0:T(8,128)S(1)}, f32[128,128]{1,0:T(8,128)S(1)}, u32[]{:S(2)}, u32[]{:S(2)}) collective-permute-start(f32[128,128]{1,0:T(8,128)S(1)} %get-tuple-element.41.refs_3_), channel_id=1, source_target_pairs={{0,4},{2,6},{4,0},{6,2},{8,12},{10,14},{12,8},{14,10},{16,20},{18,... | collective-permute-start | bytes 196616 | tf_op jit(solution)/shard_map/ppermute | solution.py:384
  9.1 4.7 %collective-permute-start.3 = (f32[128,128]{1,0:T(8,128)S(1)}, f32[128,128]{1,0:T(8,128)S(1)}, u32[]{:S(2)}, u32[]{:S(2)}) collective-permute-start(f32[128,128]{1,0:T(8,128)S(1)} %get-tuple-element.41.refs_3_), channel_id=1, source_target_pairs={{0,2},{2,0},{4,6},{6,4},{8,10},{10,8},{12,14},{14,12},{16,18},{18,... | collective-permute-start | bytes 196616 | tf_op jit(solution)/shard_map/ppermute | solution.py:384
  9.3 9.0 %collective-permute-start.4 = (bf16[128,128]{1,0:T(8,128)(2,1)S(1)}, bf16[128,128]{1,0:T(8,128)(2,1)S(1)}, u32[]{:S(2)}, u32[]{:S(2)}) collective-permute-start(bf16[128,128]{1,0:T(8,128)(2,1)S(1)} %get-tuple-element.43.refs_3_.val_ref), channel_id=1, source_target_pairs={{0,24},{2,26},{4,28},{6,30},{8,16},{10,18},{12,20},{14,22},{16,8},... | collective-permute-start | bytes 98312 | tf_op jit(solution)/shard_map/ppermute | solution.py:384
  13.3 9.2 %collective-permute-start.5 = (bf16[128,128]{1,0:T(8,128)(2,1)S(1)}, bf16[128,128]{1,0:T(8,128)(2,1)S(1)}, u32[]{:S(2)}, u32[]{:S(2)}) collective-permute-start(bf16[128,128]{1,0:T(8,128)(2,1)S(1)} %get-tuple-element.43.refs_3_.val_ref), channel_id=1, source_target_pairs={{0,16},{2,18},{4,20},{6,22},{8,24},{10,26},{12,28},{14,30},{16,0},... | collective-permute-start | bytes 98312 | tf_op jit(solution)/shard_map/ppermute | solution.py:384
  13.3 9.2 %collective-permute-start.6 = (bf16[128,128]{1,0:T(8,128)(2,1)S(1)}, bf16[128,128]{1,0:T(8,128)(2,1)S(1)}, u32[]{:S(2)}, u32[]{:S(2)}) collective-permute-start(bf16[128,128]{1,0:T(8,128)(2,1)S(1)} %get-tuple-element.43.refs_3_.val_ref), channel_id=1, source_target_pairs={{0,8},{2,10},{4,12},{6,14},{8,0},{10,2},{12,4},{14,6},{16,24},{18,... | collective-permute-start | bytes 98312 | tf_op jit(solution)/shard_map/ppermute | solution.py:384
  14.4 11.8 %collective-permute-start.7 = (bf16[512,128]{1,0:T(8,128)(2,1)S(1)}, bf16[512,128]{1,0:T(8,128)(2,1)S(1)}, u32[]{:S(2)}, u32[]{:S(2)}) collective-permute-start(bf16[512,128]{1,0:T(8,128)(2,1)S(1)} %get-tuple-element.45.refs_3_), channel_id=1, source_target_pairs={{0,24},{2,26},{4,28},{6,30},{8,16},{10,18},{12,20},{14,22},{16,8},... | collective-permute-start | bytes 393224 | tf_op jit(solution)/shard_map/ppermute | solution.py:384
  18.3 10.4 %collective-permute-start.8 = (bf16[512,128]{1,0:T(8,128)(2,1)S(1)}, bf16[512,128]{1,0:T(8,128)(2,1)S(1)}, u32[]{:S(2)}, u32[]{:S(2)}) collective-permute-start(bf16[512,128]{1,0:T(8,128)(2,1)S(1)} %get-tuple-element.45.refs_3_), channel_id=1, source_target_pairs={{0,16},{2,18},{4,20},{6,22},{8,24},{10,26},{12,28},{14,30},{16,0},... | collective-permute-start | bytes 393224 | tf_op jit(solution)/shard_map/ppermute | solution.py:384
  18.3 10.4 %collective-permute-start.9 = (bf16[512,128]{1,0:T(8,128)(2,1)S(1)}, bf16[512,128]{1,0:T(8,128)(2,1)S(1)}, u32[]{:S(2)}, u32[]{:S(2)}) collective-permute-start(bf16[512,128]{1,0:T(8,128)(2,1)S(1)} %get-tuple-element.45.refs_3_), channel_id=1, source_target_pairs={{0,8},{2,10},{4,12},{6,14},{8,0},{10,2},{12,4},{14,6},{16,24},{18,... | collective-permute-start | bytes 393224 | tf_op jit(solution)/shard_map/ppermute | solution.py:384
  23.8 8.8 %collective-permute-start.13 = (bf16[512,128]{1,0:T(8,128)(2,1)S(1)}, bf16[512,128]{1,0:T(8,128)(2,1)S(1)}, u32[]{:S(2)}, u32[]{:S(2)}) collective-permute-start(bf16[512,128]{1,0:T(8,128)(2,1)S(1)} %get-tuple-element.54.refs_7_), channel_id=1, source_target_pairs={{0,6},{2,4},{4,2},{6,0},{8,14},{10,12},{12,10},{14,8},{16,22},{18,... | collective-permute-start | bytes 393224 | tf_op jit(solution)/shard_map/ppermute | solution.py:384
  26.2 11.5 %collective-permute-start.14 = (bf16[512,128]{1,0:T(8,128)(2,1)S(1)}, bf16[512,128]{1,0:T(8,128)(2,1)S(1)}, u32[]{:S(2)}, u32[]{:S(2)}) collective-permute-start(bf16[512,128]{1,0:T(8,128)(2,1)S(1)} %get-tuple-element.54.refs_7_), channel_id=1, source_target_pairs={{0,4},{2,6},{4,0},{6,2},{8,12},{10,14},{12,8},{14,10},{16,20},{18,... | collective-permute-start | bytes 393224 | tf_op jit(solution)/shard_map/ppermute | solution.py:384
  26.2 11.5 %collective-permute-start.15 = (bf16[512,128]{1,0:T(8,128)(2,1)S(1)}, bf16[512,128]{1,0:T(8,128)(2,1)S(1)}, u32[]{:S(2)}, u32[]{:S(2)}) collective-permute-start(bf16[512,128]{1,0:T(8,128)(2,1)S(1)} %get-tuple-element.54.refs_7_), channel_id=1, source_target_pairs={{0,2},{2,0},{4,6},{6,4},{8,10},{10,8},{12,14},{14,12},{16,18},{18,... | collective-permute-start | bytes 393224 | tf_op jit(solution)/shard_map/ppermute | solution.py:384
  29.5 8.2 %collective-permute-start.10 = (bf16[512,128]{1,0:T(8,128)(2,1)S(1)}, bf16[512,128]{1,0:T(8,128)(2,1)S(1)}, u32[]{:S(2)}, u32[]{:S(2)}) collective-permute-start(bf16[512,128]{1,0:T(8,128)(2,1)S(1)} %get-tuple-element.50), channel_id=1, source_target_pairs={{0,6},{2,4},{4,2},{6,0},{8,14},{10,12},{12,10},{14,8},{16,22},{18,... | collective-permute-start | bytes 393224 | tf_op jit(solution)/shard_map/ppermute | solution.py:384
  32.0 6.2 %collective-permute-start.11 = (bf16[512,128]{1,0:T(8,128)(2,1)S(1)}, bf16[512,128]{1,0:T(8,128)(2,1)S(1)}, u32[]{:S(2)}, u32[]{:S(2)}) collective-permute-start(bf16[512,128]{1,0:T(8,128)(2,1)S(1)} %get-tuple-element.51), channel_id=1, source_target_pairs={{0,4},{2,6},{4,0},{6,2},{8,12},{10,14},{12,8},{14,10},{16,20},{18,... | collective-permute-start | bytes 393224 | tf_op jit(solution)/shard_map/ppermute | solution.py:384
  32.7 5.6 %collective-permute-start.12 = (bf16[512,128]{1,0:T(8,128)(2,1)S(1)}, bf16[512,128]{1,0:T(8,128)(2,1)S(1)}, u32[]{:S(2)}, u32[]{:S(2)}) collective-permute-start(bf16[512,128]{1,0:T(8,128)(2,1)S(1)} %get-tuple-element.52), channel_id=1, source_target_pairs={{0,2},{2,0},{4,6},{6,4},{8,10},{10,8},{12,14},{14,12},{16,18},{18,... | collective-permute-start | bytes 393224 | tf_op jit(solution)/shard_map/ppermute | solution.py:384
  43.3 1.6 %collective-permute-start.16 = (bf16[64,2048]{1,0:T(8,128)(2,1)S(1)}, bf16[64,2048]{1,0:T(8,128)(2,1)S(1)}, u32[]{:S(2)}, u32[]{:S(2)}) collective-permute-start(bf16[64,2048]{1,0:T(8,128)(2,1)S(1)} %get-tuple-element.66), channel_id=1, source_target_pairs={{0,1},{1,0},{2,3},{3,2},{4,5},{5,4},{6,7},{7,6},{8,9},{9,8},{10,11... | collective-permute-start | bytes 786440 | tf_op jit(solution)/shard_map/ppermute | solution.py:519

commit v9 on v8

--- a/solution.py
+++ b/solution.py
@@ -10,6 +10,7 @@
 
 EPSILON = 1e-06
 NEGATIVE = -1e30
+LOG2E = math.log2(math.e)
 F32 = jnp.float32
 BF16 = jnp.bfloat16
 MIB = 1024 * 1024
@@ -38,6 +39,10 @@
 
 def in_hbm(array):
     return pltpu.with_memory_space_constraint(array, pltpu.HBM)
+
+
+def step_between(member, source, group):
+    return member ^ source if group & (group - 1) == 0 else (member + group - source) % group
 
 
 def shaped(shape, dtype):
@@ -108,7 +113,7 @@
     rows_ref[pl.ds(pl.multiple_of(core * half, half), half), :] = mine_ref[...]
     rows_ref[pl.ds(pl.multiple_of((1 - core) * half, half), half), :] = other_ref[...]
     seg = rows_ref[...]
-    size = turn_ref.shape[0]
+    size = turn_ref.shape[1]
     raw = jnp.dot(seg, weight_ref[...], preferred_element_type=F32)
     keys, raw, vals = raw[:, :size], raw[:, size : 2 * size], raw[:, 2 * size :]
     kn = keys * lax.rsqrt(jnp.mean(keys * keys, axis=-1, keepdims=True) + EPSILON) * gain_ref[...]
@@ -132,7 +137,10 @@
     crossed = dot3(both, dirs, 0, 0)
     exit_ref[...] = kn - crossed[:tokens]
     heads, lanes = iota2((size, size))
-    turn_ref[...] = jnp.where(heads == lanes, 1.0, 0.0) - crossed[tokens:]
+    high, low = split(jnp.where(heads == lanes, 1.0, 0.0) - crossed[tokens:])
+    turn_ref[:size] = high
+    turn_ref[size : 2 * size] = low
+    turn_ref[2 * size :] = vals.astype(BF16)
 
 
 def leave_kernel(group, place_ref, exit_ref, *refs):
@@ -141,7 +149,10 @@
     member = place_ref[0] % group
     tokens, size = exit_ref.shape
     for step in range(group):
-        turns_ref[source_of(member, step, group)] = turn_refs[group - 1 - step][...]
+        ref = turn_refs[group - 1 - step]
+        turns_ref[source_of(member, step, group)] = ref[:size].astype(F32) + ref[
+            size : 2 * size
+        ].astype(F32)
     own = exit_ref[...]
     keys = own
     product = None
@@ -158,9 +169,7 @@
     high, low = split(keys)
     leave_ref[:tokens] = high
     leave_ref[tokens : 2 * tokens] = low
-    high, low = split(product)
-    leave_ref[2 * tokens : 2 * tokens + size] = high
-    leave_ref[2 * tokens + size :] = low
+    leave_ref[2 * tokens :] = product.astype(BF16)
     for step in range(group):
         near_refs[step][...] = seen_ref[target_of(member, step, group)]
 
@@ -172,9 +181,8 @@
 
 
 def bundle_kernel(group, groups, most, place_ref, mask_ref, after_ref, *refs):
-    val_refs, (line_ref, table_ref) = refs[:groups], refs[groups:]
+    val_refs, (line_ref, table_ref) = refs[: groups - 1], refs[groups - 1 :]
     place = place_ref[0]
-    mine = place // group
     segments = mask_ref.shape[0]
     for word in range(table_ref.shape[0]):
         table_ref[word] = 0
@@ -191,35 +199,21 @@
 
     lax.fori_loop(0, segments, pick, jnp.int32(0))
     tokens = val_refs[0].shape[0]
-    for way in range(groups):
-        at = pl.multiple_of(source_of(mine, way, groups) * tokens, tokens)
-        line_ref[pl.ds(at, tokens), :] = val_refs[groups - 1 - way][...]
-
-
-def query_kernel(first, rows_ref, weight_hbm, gain_ref, kn_ref, dirs_ref, coeff_ref, solved_ref, val_ref,
-                 moved_ref, weighted_ref, peak_ref, total_ref, weight_ref, sems):
+    for way in range(1, groups):
+        line_ref[(way - 1) * tokens : way * tokens] = val_refs[groups - 1 - way][...]
+
+
+def query_kernel(rows_ref, weight_ref, gain_ref, kn_ref, dirs_ref, coeff_ref, solved_ref, val_ref,
+                 moved_ref, weighted_ref, peak_ref, total_ref):
     tokens, size = kn_ref.shape
     heads = moved_ref.shape[0]
-    pieces = weight_ref.shape[0]
-    wide = weight_ref.shape[2]
-    copies = [
-        pltpu.make_async_copy(
-            weight_hbm.at[:, first + n * wide : first + (n + 1) * wide], weight_ref.at[n], sems.at[n]
-        )
-        for n in range(pieces)
-    ]
-    for copy in copies:
-        copy.start()
     across = jnp.concatenate([kn_ref[...], dirs_ref[...]], axis=0)
     into = jnp.concatenate([coeff_ref[...], solved_ref[...]], axis=1)
-    together = math.gcd(pieces, 2)
-    for turn in range(pieces // together):
-        parts = []
-        for n in range(turn * together, (turn + 1) * together):
-            copies[n].wait()
-            raw = jnp.dot(rows_ref[...], weight_ref[n], preferred_element_type=F32)
-            parts += [raw[:, at : at + size] for at in range(0, wide, size)]
-        count = len(parts)
+    count = math.gcd(heads, 4)
+    for turn in range(heads // count):
+        wide = slice(turn * count * size, (turn + 1) * count * size)
+        raw = jnp.dot(rows_ref[...], weight_ref[:, wide], preferred_element_type=F32)
+        parts = [raw[:, at : at + size] for at in range(0, count * size, size)]
         raw = jnp.concatenate(parts, axis=0)
         queries = (
             raw * lax.rsqrt(jnp.mean(raw * raw, axis=-1, keepdims=True) + EPSILON) * gain_ref[...]
@@ -229,11 +223,11 @@
         up_to = rows % tokens >= cols
         reach = jnp.where(up_to, seen[:, tokens:], 0.0)
         taken = dot3(reach, into)
-        scores = (seen[:, :tokens] - taken[:, :tokens]) * (1.0 / math.sqrt(size))
+        scores = (seen[:, :tokens] - taken[:, :tokens]) * (LOG2E / math.sqrt(size))
         scores = jnp.where(up_to, scores, NEGATIVE)
         moved = (queries - taken[:, tokens:]).astype(BF16)
         peak = jnp.max(scores, axis=1, keepdims=True)
-        weights = jnp.exp(scores - peak)
+        weights = jnp.exp2(scores - peak)
         total = jnp.sum(weights, axis=1, keepdims=True)
         weighted = jnp.dot(weights.astype(BF16), val_ref[...], preferred_element_type=F32)
         for h in range(count):
@@ -254,8 +248,7 @@
         index = source_of(mine, step, groups)
         ref = arrived[groups - 1 - step]
         keys_ref[index] = ref[:tokens].astype(F32) + ref[tokens : 2 * tokens].astype(F32)
-        whole = ref[2 * tokens : 2 * tokens + size].astype(F32)
-        whole_ref[index] = whole + ref[2 * tokens + size :].astype(F32)
+        whole_ref[index] = ref[2 * tokens :].astype(F32)
     brought = [keys_ref[groups - 2]]
     product = None
     for index in range(groups - 3, -1, -1):
@@ -273,27 +266,16 @@
 
 def attend_kernel(group, segments, most, place_ref, core_ref, table_ref, *refs):
     far_refs, line_refs = refs[:group][::-1], refs[group : 2 * group][::-1]
-    parts = (len(refs) - 2 * group - 8) // 4
-    owns, refs = [refs[2 * group + 4 * n : 2 * group + 4 * n + 4] for n in range(parts)], refs[
-        2 * group + 4 * parts :
-    ]
-    out_hbm, away_ref, kept_ref, keys_ref, vals_ref, attended_ref, out_ref, sems = refs
-    pieces, _, wide = out_ref.shape
-    copies = [
-        pltpu.make_async_copy(
-            out_hbm.at[:, n * wide : (n + 1) * wide], out_ref.at[n], sems.at[n]
-        )
-        for n in range(pieces)
-    ]
-    for copy in copies:
-        copy.start()
+    turn_refs = refs[2 * group : 3 * group][::-1]
+    (moved_ref, weighted_ref, peak_ref, total_ref, out_ref, away_ref, kept_ref, keys_ref, vals_ref,
+     attended_ref) = refs[3 * group :]
     core = core_ref[0]
     mine, member = place_ref[0] // group, place_ref[0] % group
-    heads, tokens, size = owns[0][0].shape
+    heads, tokens, size = moved_ref.shape
     groups = far_refs[0].shape[0] // tokens
-    scaling = 1.0 / math.sqrt(size)
+    scaling = LOG2E / math.sqrt(size)
     chunk = keys_ref.shape[0] // tokens
-    lanes = lax.broadcasted_iota(jnp.int32, (tokens, chunk * tokens), 1)
+    lanes = lax.broadcasted_iota(jnp.int32, (1, chunk * tokens), 1)
 
     def collect(turn):
         found = jnp.int32(0)
@@ -306,24 +288,29 @@
             whose, source = segment % group, segment // group
             before = jnp.where(source < mine, source, groups - 1)
             before = pl.multiple_of(before * tokens, tokens)
-            after = pl.multiple_of(source * tokens, tokens)
+            after = jnp.maximum(step_between(mine, source, groups) - 1, 0)
+            after = pl.multiple_of(after * tokens, tokens)
             for number in range(group):
 
                 @pl.when(whose == source_of(member, number, group))
                 def _():
-                    vals_ref[part, :] = line_refs[number][pl.ds(after, tokens), :]
+                    vals_ref[part, :] = jnp.where(
+                        source < mine,
+                        line_refs[number][pl.ds(after, tokens), :],
+                        turn_refs[number][2 * size :],
+                    )
                     keys_ref[part, :] = far_refs[number][pl.ds(before, tokens), :]
 
-        return found * tokens
-
-    def advance(moved, kept, peak, total, weighted):
+        return jnp.where(lanes < found * tokens, 0.0, NEGATIVE)
+
+    def advance(moved, bias, peak, total, weighted):
         scores = lax.dot_general(
             moved, keys_ref[...], (((1,), (1,)), ((), ())), preferred_element_type=F32
         )
-        scores = jnp.where(lanes < kept, scores * scaling, NEGATIVE)
+        scores = scores * scaling + bias
         new_peak = jnp.maximum(peak, jnp.max(scores, axis=1, keepdims=True))
-        fading = jnp.exp(peak - new_peak)
-        weights = jnp.exp(scores - new_peak)
+        fading = jnp.exp2(peak - new_peak)
+        weights = jnp.exp2(scores - new_peak)
         total = total * fading + jnp.sum(weights, axis=1, keepdims=True)
         weighted = weighted * fading + jnp.dot(
             weights.astype(BF16), vals_ref[...], preferred_element_type=F32
@@ -333,30 +320,30 @@
     half = kept_ref.shape[0]
     turns = most // chunk
     if turns == 1:
-        kept = collect(0)
-    for number in range(parts * heads):
-        moved_ref, weighted_ref, peak_ref, total_ref = owns[number // heads]
-        h = number % heads
-        state = (peak_ref[h], total_ref[h], weighted_ref[h])
+        bias = collect(0)
+    for head in range(heads):
+        state = (peak_ref[head], total_ref[head], weighted_ref[head])
         if turns == 1:
-            _, total, weighted = advance(moved_ref[h], kept, *state)
+            _, total, weighted = advance(moved_ref[head], bias, *state)
         else:
 
-            def step_of(turn, state, moved_ref=moved_ref, h=h):
-                return advance(moved_ref[h], collect(turn), *state)
+            def step_of(turn, state, head=head):
+                return advance(moved_ref[head], collect(turn), *state)
 
             _, total, weighted = lax.fori_loop(0, turns, step_of, state)
         done = (weighted * (1.0 / total)).astype(BF16)
         for index in range(tokens // half):
             at = pl.multiple_of(jnp.where(index == core, half, 0), half)
-            attended_ref[pl.ds(at, half), number * size : (number + 1) * size] = done[
+            attended_ref[pl.ds(at, half), head * size : (head + 1) * size] = done[
                 index * half : (index + 1) * half
             ]
-    for n in range(pieces):
-        copies[n].wait()
-        result = jnp.dot(attended_ref[...], out_ref[n], preferred_element_type=F32).astype(BF16)
-        away_ref[:, n * wide : (n + 1) * wide] = result[:half]
-        kept_ref[:, n * wide : (n + 1) * wide] = result[half:]
+    wide = math.gcd(out_ref.shape[1], 4 * size)
+    for at in range(0, out_ref.shape[1], wide):
+        part = slice(at, at + wide)
+        result = jnp.dot(attended_ref[...], out_ref[:, part], preferred_element_type=F32)
+        result = result.astype(BF16)
+        away_ref[:, part] = result[:half]
+        kept_ref[:, part] = result[half:]
 
 
 def body(
@@ -415,7 +402,7 @@
         prepare_kernel,
         (
             shaped((tokens, width), BF16), square, shaped((tokens, size), BF16), square, square,
-            square, square, shaped((size, size), F32),
+            square, square, shaped((2 * size + tokens, size), BF16),
         ),
         (core, mine, other, weights, rate_row, rate_bias, key_gain),
         in_specs=[smem] + [vmem] * 4 + [smem, vmem],
@@ -427,7 +414,7 @@
     leaving, starts, *near = call(
         functools.partial(leave_kernel, group),
         [
-            shaped((2 * tokens + 2 * size, size), BF16),
+            shaped((2 * tokens + size, size), BF16),
             shaped((group, size, size), F32),
         ]
         + [shaped((tokens, size), BF16)] * group,
@@ -445,40 +432,43 @@
     values, table = call(
         functools.partial(bundle_kernel, group, groups, most),
         [
-            shaped((groups * tokens, size), BF16),
+            shaped(((groups - 1) * tokens, size), BF16),
             shaped((word_of(most - 1, segments)[0] + 1,), jnp.int32),
         ],
-        (place, block_mask[0], starts, *line[::-1]),
-        in_specs=[smem, smem, anywhere] + [vmem] * groups,
+        (place, block_mask[0], starts, *line[:0:-1]),
+        in_specs=[smem, smem, anywhere] + [vmem] * (groups - 1),
         out_specs=[vmem, smem],
         moved=10**6,
         limit=8 + group * groups // 4,
     )
     values = within_group([values] * group)
-    calls = 1
-    each = heads // calls
-    pieces = math.gcd(each, 4)
-    owns = [
-        call(
-            functools.partial(query_kernel, number * each * size),
-            (
-                shaped((each, tokens, size), BF16),
-                shaped((each, tokens, size), F32),
-                shaped((each, tokens, 1), F32),
-                shaped((each, tokens, 1), F32),
-            ),
-            (rows, in_hbm(w_query), query_gain, kn, dirs, coeff, solved, val),
-            in_specs=[vmem, hbm] + [vmem] * 6,
-            scratch=(
-                pltpu.VMEM((pieces, width, each * size // pieces), BF16),
-                pltpu.SemaphoreType.DMA((pieces,)),
-            ),
-            flops=4 * tokens * width * each * size,
-            moved=8 * width * each * size,
-            limit=16,
-        )
-        for number in range(calls)
-    ]
+    own = call(
+        query_kernel,
+        (
+            shaped((heads, tokens, size), BF16),
+            shaped((heads, tokens, size), F32),
+            shaped((heads, tokens, 1), F32),
+            shaped((heads, tokens, 1), F32),
+        ),
+        (rows, w_query, query_gain, kn, dirs, coeff, solved, val),
+        flops=4 * tokens * width * heads * size,
+        moved=8 * width * heads * size,
+        limit=14,
+    )
+    most = segments // 4
+    values, table = call(
+        functools.partial(bundle_kernel, group, groups, most),
+        [
+            shaped(((groups - 1) * tokens, size), BF16),
+            shaped((word_of(most - 1, segments)[0] + 1,), jnp.int32),
+        ],
+        (place, block_mask[0], starts, *line[:0:-1]),
+        in_specs=[smem, smem, anywhere] + [vmem] * (groups - 1),
+        out_specs=[vmem, smem],
+        moved=10**6,
+        limit=8 + group * groups // 4,
+    )
+    values = within_group([values] * group)
     far = call(
         functools.partial(arrive_kernel, groups, group, tokens),
         [shaped((groups * tokens, size), BF16)] * group,
@@ -495,26 +485,20 @@
     far = within_group(far)
     chunk = math.gcd(most, 4)
     width_out = w_out.shape[1]
-    pieces = math.gcd(width_out // size, 4)
     scratch = [
         pltpu.VMEM((chunk * tokens, size), BF16),
         pltpu.VMEM((chunk * tokens, size), BF16),
         pltpu.VMEM((tokens, heads * size), BF16),
-        pltpu.VMEM((pieces, heads * size, width_out // pieces), BF16),
-        pltpu.SemaphoreType.DMA((pieces,)),
     ]
     away, kept = call(
         functools.partial(attend_kernel, group, segments, most),
         [shaped((half, width_out), BF16)] * 2,
-        (
-            place, core, table, *far[::-1], *values[::-1], *(array for own in owns for array in own),
-            in_hbm(w_out),
-        ),
-        in_specs=[smem] * 3 + [vmem] * (2 * group + 4 * calls) + [hbm],
+        (place, core, table, *far[::-1], *values[::-1], *turns[::-1], *own, w_out),
+        in_specs=[smem] * 3 + [vmem] * (3 * group + 5),
         scratch=scratch,
         flops=2 * tokens * width_out * heads * size,
         moved=4 * 10**6,
-        limit=20 + group * groups // 4,
+        limit=14 + group * groups // 4,
     )
     return kept + lax.ppermute(away, "head", [(0, 1), (1, 0)])
 

time: 45.8 us -> 50.2 us (1.096)
  starting transfers between devices: 20.9 us -> 24.4 us
  Pallas kernels: 16.3 us -> 13.5 us
  local copies, waits for them, and re-layouts: 0.01 us -> 2.19 us
  waiting for transfers between devices: 6.97 us -> 8.38 us
    ppermute x15, starting transfers between devices: 20.4 us -> 23.9 us  [swapped(): out[step] = lax.ppermute(values[step], 'ctx', pairs_of(step))]
    pallas_call x7, Pallas kernels: 16.3 us -> 13.5 us  [call(): pl.pallas_call(kernel, out_shape=out_shape, in_specs=in_specs or [vmem] *...]
    unnamed x2 -> x6, local copies, waits for them, and re-layouts: 0.01 us -> 2.19 us
    ppermute x15, waiting for transfers between devices: 5.45 us -> 6.86 us  [swapped(): out[step] = lax.ppermute(values[step], 'ctx', pairs_of(step))]
  transfers between devices with their start and end apart: 17 -> 17, of which waited for: 4 -> 6; matrix products, arithmetic and copies ran while one was open for 0% -> 0% of each run, Pallas kernels for 19% -> 13%
where the time goes in v9:
time: 50.2 us; the launch traced here: 50 us
  starting transfers between devices  24.4 us (49%)
  Pallas kernels  13.5 us (27%)
  waiting for transfers between devices  8.38 us (17%)
  local copies, waits for them, and re-layouts  2.19 us (4%)
  other arithmetic  0.77 us (2%)
  between operations  0.75 us (1%)
    ppermute x15, starting transfers between devices, swapped(): out[step] = lax.ppermute(values[step], 'ctx', pairs_of(step))  23.9 us
    pallas_call x7, Pallas kernels, call(): pl.pallas_call(kernel, out_shape=out_shape, in_specs=in_specs or [vmem] *...  13.5 us
    ppermute x15, waiting for transfers between devices, swapped(): out[step] = lax.ppermute(values[step], 'ctx', pairs_of(step))  6.86 us
    unnamed x6, local copies, waits for them, and re-layouts  2.19 us
    ppermute x1, waiting for transfers between devices, body(): return kept + lax.ppermute(away, 'head', [(0, 1), (1, 0)])  1.52 us
  transfers between devices with their start and end apart: 17, of which 6 were waited for; matrix products, arithmetic and copies ran while one was open for 0% of the time, Pallas kernels for 13%

profile of v9, /device:TPU:0, one launch (start us, length us, event | category | flops | bytes accessed | tf_op | source)
XLA Modules:
  0.0 50.0 jit_solution(12221184629126052017)
XLA Ops:
  1.1 1.5 %shard_map.109 = (bf16[2048,384]{1,0:T(8,128)(2,1)S(1)}, bf16[1,2048]{1,0:T(2,128)(2,1)S(1)}, f32[1,128]{1,0:T(1,128)S(1)}, f32[1,128]{1,0:T(1,128)S(1)}, bf16[64,2048]{1,0:T(8,128)(2,1)S(1)}) custom-call(bf16[2048,128]{1,0:T(8,128)(2,1)} %key_hbm.1, bf16[2048,128]{1,0:T(8,128)(2,1)} %dir_hbm.1, bf16[2048,128]{1,0:T(8,128)(2,1)} %value_hbm.1, ...), custom_call_target="tpu_custom_call" | custom-call | bytes 3145728 | tf_op jit(solution)/shard_map/pallas_call | solution.py:21
  2.7 2.4 %shard_map.110 = (bf16[128,2048]{1,0:T(8,128)(2,1)S(1)}, f32[128,128]{1,0:T(8,128)S(1)}, bf16[128,128]{1,0:T(8,128)(2,1)S(1)}, f32[128,128]{1,0:T(8,128)S(1)}, f...) custom-call(s32[1]{0:T(128)} %bitcast.1.core_ref, ...), custom_call_target="tpu_custom_call" | custom-call | flops 201326592 | bytes 2097152 | tf_op jit(solution)/shard_map/pallas_call | solution.py:21
  5.1 3.5 %collective-permute-start.1 = (bf16[384,128]{1,0:T(8,128)(2,1)S(1)}, bf16[384,128]{1,0:T(8,128)(2,1)S(1)}, u32[]{:S(2)}, u32[]{:S(2)}) collective-permute-start(bf16[384,128]{1,0:T(8,128)(2,1)S(1)} %get-tuple-element.41.refs_3_.refs_11_), channel_id=1, source_target_pairs={{0,6},{2,4},{4,2},{6,0},{8,14},{10,12},{12,10},{14,8},{16,22},{18,... | collective-permute-start | bytes 294920 | tf_op jit(solution)/shard_map/ppermute | solution.py:371
  8.6 0.5 %collective-permute-start.2 = (bf16[384,128]{1,0:T(8,128)(2,1)S(1)}, bf16[384,128]{1,0:T(8,128)(2,1)S(1)}, u32[]{:S(2)}, u32[]{:S(2)}) collective-permute-start(bf16[384,128]{1,0:T(8,128)(2,1)S(1)} %get-tuple-element.41.refs_3_.refs_11_), channel_id=1, source_target_pairs={{0,4},{2,6},{4,0},{6,2},{8,12},{10,14},{12,8},{14,10},{16,20},{18,... | collective-permute-start | bytes 294920 | tf_op jit(solution)/shard_map/ppermute | solution.py:371
  9.3 4.0 %collective-permute-start.4 = (bf16[128,128]{1,0:T(8,128)(2,1)S(1)}, bf16[128,128]{1,0:T(8,128)(2,1)S(1)}, u32[]{:S(2)}, u32[]{:S(2)}) collective-permute-start(bf16[128,128]{1,0:T(8,128)(2,1)S(1)} %get-tuple-element.43.val_ref), channel_id=1, source_target_pairs={{0,24},{2,26},{4,28},{6,30},{8,16},{10,18},{12,20},{14,22},{16,8},... | collective-permute-start | bytes 98312 | tf_op jit(solution)/shard_map/ppermute | solution.py:371
  13.3 0.9 %collective-permute-done.2.refs_1_.refs_9_ = bf16[384,128]{1,0:T(8,128)(2,1)S(1)} collective-permute-done((bf16[384,128]{1,0:T(8,128)(2,1)S(1)}, bf16[384,128]{1,0:T(8,128)(2,1)S(1)}, u32[]{:S(2)}, u32[]{:S(2)}) %collective-permute-start.2) | collective-permute-done | bytes 98336 | tf_op jit(solution)/shard_map/ppermute | solution.py:371
  15.0 3.7 %collective-permute-start.7 = (bf16[384,128]{1,0:T(8,128)(2,1)S(1)}, bf16[384,128]{1,0:T(8,128)(2,1)S(1)}, u32[]{:S(2)}, u32[]{:S(2)}) collective-permute-start(bf16[384,128]{1,0:T(8,128)(2,1)S(1)} %get-tuple-element.45.refs_3_), channel_id=1, source_target_pairs={{0,24},{2,26},{4,28},{6,30},{8,16},{10,18},{12,20},{14,22},{16,8},... | collective-permute-start | bytes 294920 | tf_op jit(solution)/shard_map/ppermute | solution.py:371
  18.6 0.8 %collective-permute-start.9 = (bf16[384,128]{1,0:T(8,128)(2,1)S(1)}, bf16[384,128]{1,0:T(8,128)(2,1)S(1)}, u32[]{:S(2)}, u32[]{:S(2)}) collective-permute-start(bf16[384,128]{1,0:T(8,128)(2,1)S(1)} %get-tuple-element.45.refs_3_), channel_id=1, source_target_pairs={{0,8},{2,10},{4,12},{6,14},{8,0},{10,2},{12,4},{14,6},{16,24},{18,... | collective-permute-start | bytes 294920 | tf_op jit(solution)/shard_map/ppermute | solution.py:371
  19.4 2.1 %collective-permute-start.5 = (bf16[128,128]{1,0:T(8,128)(2,1)S(1)}, bf16[128,128]{1,0:T(8,128)(2,1)S(1)}, u32[]{:S(2)}, u32[]{:S(2)}) collective-permute-start(bf16[128,128]{1,0:T(8,128)(2,1)S(1)} %get-tuple-element.43.val_ref), channel_id=1, source_target_pairs={{0,16},{2,18},{4,20},{6,22},{8,24},{10,26},{12,28},{14,30},{16,0},... | collective-permute-start | bytes 98312 | tf_op jit(solution)/shard_map/ppermute | solution.py:371
  21.6 2.0 %collective-permute-start.6 = (bf16[128,128]{1,0:T(8,128)(2,1)S(1)}, bf16[128,128]{1,0:T(8,128)(2,1)S(1)}, u32[]{:S(2)}, u32[]{:S(2)}) collective-permute-start(bf16[128,128]{1,0:T(8,128)(2,1)S(1)} %get-tuple-element.43.val_ref), channel_id=1, source_target_pairs={{0,8},{2,10},{4,12},{6,14},{8,0},{10,2},{12,4},{14,6},{16,24},{18,... | collective-permute-start | bytes 98312 | tf_op jit(solution)/shard_map/ppermute | solution.py:371
  23.6 4.9 %collective-permute-done.5.refs_1_ = bf16[128,128]{1,0:T(8,128)(2,1)S(1)} collective-permute-done((bf16[128,128]{1,0:T(8,128)(2,1)S(1)}, bf16[128,128]{1,0:T(8,128)(2,1)S(1)}, u32[]{:S(2)}, u32[]{:S(2)}) %collective-permute-start.5) | collective-permute-done | bytes 32800 | tf_op jit(solution)/shard_map/ppermute | solution.py:371
  28.5 1.3 %shard_map.112 = (bf16[384,128]{1,0:T(8,128)(2,1)S(1)}, s32[1]{0:T(128)}) custom-call(s32[1]{0:T(128)} %bitcast.place_ref, s32[16]{0:T(128)S(1)} %bitcast.5, f32[4,128,128]{2,1,0:T(8,128)S(1)} %get-tuple-element.42.after_ref.refs_4_, bf16[128,128]{1,0:T(8,128)(2,1)S(1)} %collective-permute-done.4.refs_0_, ...), custom_call_target="tpu_custom_call" | custom-call | bytes 1000000 | tf_op jit(solution)/shard_map/pallas_call | solution.py:21
  29.8 1.2 %collective-permute-start.13 = (bf16[384,128]{1,0:T(8,128)(2,1)S(1)}, bf16[384,128]{1,0:T(8,128)(2,1)S(1)}, u32[]{:S(2)}, u32[]{:S(2)}) collective-permute-start(bf16[384,128]{1,0:T(8,128)(2,1)S(1)} %get-tuple-element.54.refs_7_), channel_id=1, source_target_pairs={{0,6},{2,4},{4,2},{6,0},{8,14},{10,12},{12,10},{14,8},{16,22},{18,... | collective-permute-start | bytes 294920 | tf_op jit(solution)/shard_map/ppermute | solution.py:371
  31.0 0.8 %shard_map.113 = (bf16[512,128]{1,0:T(8,128)(2,1)S(1)}, bf16[512,128]{1,0:T(8,128)(2,1)S(1)}, bf16[512,128]{1,0:T(8,128)(2,1)S(1)}, bf16[512,128]{1,0:T(8,128)(2,1)S(1)}) custom-call(s32[1]{0:T(128)} %bitcast.place_ref, bf16[384,128]{1,0:T(8,128)(2,1)S(1)} %collective-permute-done.7.refs_0_, bf16[384,128]{1,0:T(8,128)(2,1)S(1)} %collective-permute-done.8.refs_1_, ...), custom_call_target="tpu_custom_call" | custom-call | flops 201326592 | bytes 1000000 | tf_op jit(solution)/shard_map/pallas_call | solution.py:21
  31.8 1.9 %collective-permute-start.10 = (bf16[512,128]{1,0:T(8,128)(2,1)S(1)}, bf16[512,128]{1,0:T(8,128)(2,1)S(1)}, u32[]{:S(2)}, u32[]{:S(2)}) collective-permute-start(bf16[512,128]{1,0:T(8,128)(2,1)S(1)} %get-tuple-element.50), channel_id=1, source_target_pairs={{0,6},{2,4},{4,2},{6,0},{8,14},{10,12},{12,10},{14,8},{16,22},{18,... | collective-permute-start | bytes 393224 | tf_op jit(solution)/shard_map/ppermute | solution.py:371
  33.7 1.5 %collective-permute-start.11 = (bf16[512,128]{1,0:T(8,128)(2,1)S(1)}, bf16[512,128]{1,0:T(8,128)(2,1)S(1)}, u32[]{:S(2)}, u32[]{:S(2)}) collective-permute-start(bf16[512,128]{1,0:T(8,128)(2,1)S(1)} %get-tuple-element.51), channel_id=1, source_target_pairs={{0,4},{2,6},{4,0},{6,2},{8,12},{10,14},{12,8},{14,10},{16,20},{18,... | collective-permute-start | bytes 393224 | tf_op jit(solution)/shard_map/ppermute | solution.py:371
  35.4 1.8 %collective-permute-start.14 = (bf16[384,128]{1,0:T(8,128)(2,1)S(1)}, bf16[384,128]{1,0:T(8,128)(2,1)S(1)}, u32[]{:S(2)}, u32[]{:S(2)}) collective-permute-start(bf16[384,128]{1,0:T(8,128)(2,1)S(1)} %get-tuple-element.54.refs_7_), channel_id=1, source_target_pairs={{0,4},{2,6},{4,0},{6,2},{8,12},{10,14},{12,8},{14,10},{16,20},{18,... | collective-permute-start | bytes 294920 | tf_op jit(solution)/shard_map/ppermute | solution.py:371
  37.2 0.5 %collective-permute-start.15 = (bf16[384,128]{1,0:T(8,128)(2,1)S(1)}, bf16[384,128]{1,0:T(8,128)(2,1)S(1)}, u32[]{:S(2)}, u32[]{:S(2)}) collective-permute-start(bf16[384,128]{1,0:T(8,128)(2,1)S(1)} %get-tuple-element.54.refs_7_), channel_id=1, source_target_pairs={{0,2},{2,0},{4,6},{6,4},{8,10},{10,8},{12,14},{14,12},{16,18},{18,... | collective-permute-start | bytes 294920 | tf_op jit(solution)/shard_map/ppermute | solution.py:371
  37.8 2.2 %copy-done = bf16[2048,1024]{1,0:T(8,128)(2,1)S(1)} copy-done((bf16[2048,1024]{1,0:T(8,128)(2,1)S(1)}, bf16[2048,1024]{1,0:T(8,128)(2,1)}, u32[]{:S(2)}) %copy-start) | copy-done | bytes 4194328
  40.0 2.4 %shard_map.114 = (bf16[8,128,128]{2,1,0:T(8,128)(2,1)S(1)}, f32[8,128,128]{2,1,0:T(8,128)S(1)}, f32[8,128,1]{2,1,0:T(8,128)S(1)}, f32[8,128,1]{2,1,0:T(8,128)S(1)}) custom-call(bf16[128,2048]{1,0:T(8,128)(2,1)S(1)} %get-tuple-element.55.rows_ref, bf16[2048,1024]{1,0:T(8,128)(2,1)S(1)} %copy-done, f32[1,128]{1,0:T(1,128)S(1)} %get-tuple-element.56.gain_ref, ...), custom_call_target="tpu_custom_call" | custom-call | flops 1073741824 | bytes 16777216 | tf_op jit(solution)/shard_map/pallas_call | solution.py:21
  42.4 0.7 %collective-permute-done.14.refs_5_ = bf16[384,128]{1,0:T(8,128)(2,1)S(1)} collective-permute-done((bf16[384,128]{1,0:T(8,128)(2,1)S(1)}, bf16[384,128]{1,0:T(8,128)(2,1)S(1)}, u32[]{:S(2)}, u32[]{:S(2)}) %collective-permute-start.14) | collective-permute-done | bytes 98336 | tf_op jit(solution)/shard_map/ppermute | solution.py:371
  43.2 4.4 %shard_map.115 = (bf16[64,2048]{1,0:T(8,128)(2,1)S(1)}, bf16[64,2048]{1,0:T(8,128)(2,1)S(1)}) custom-call(s32[1]{0:T(128)} %bitcast.place_ref, s32[1]{0:T(128)} %bitcast.1.core_ref, s32[1]{0:T(128)} %get-tuple-element.44.table_ref, bf16[512,128]{1,0:T(8,128)(2,1)S(1)} %collective-permute-done.10.refs_0_, ...), custom_call_target="tpu_custom_call" | custom-call | flops 536870912 | bytes 4000000 | tf_op jit(solution)/shard_map/pallas_call | solution.py:21
  47.7 1.5 %collective-permute-done.16 = bf16[64,2048]{1,0:T(8,128)(2,1)S(1)} collective-permute-done((bf16[64,2048]{1,0:T(8,128)(2,1)S(1)}, bf16[64,2048]{1,0:T(8,128)(2,1)S(1)}, u32[]{:S(2)}, u32[]{:S(2)}) %collective-permute-start.16) | collective-permute-done | bytes 262176 | tf_op jit(solution)/shard_map/ppermute | solution.py:503
  49.3 0.8 %add.3 = bf16[64,2048]{1,0:T(8,128)(2,1)} add(bf16[64,2048]{1,0:T(8,128)(2,1)S(1)} %get-tuple-element.65, bf16[64,2048]{1,0:T(8,128)(2,1)S(1)} %collective-permute-done.16) | non-fusion elementwise | flops 131072 | bytes 786432 | tf_op jit(solution)/shard_map/add | solution.py:503
  (24 shorter events, 1.7 us)
Async XLA Ops:
  0.0 28.5 %copy-start.2 = (s32[1,16]{1,0:T(1,128)S(1)}, s32[1,16]{1,0:T(1,128)}, u32[]{:S(2)}) copy-start(s32[1,16]{1,0:T(1,128)} %param.21) | copy-start | bytes 196
  0.0 2.6 %collective-permute-start = (bf16[64,2048]{1,0:T(8,128)(2,1)}, bf16[64,2048]{1,0:T(8,128)(2,1)S(1)}, u32[]{:S(2)}, u32[]{:S(2)}) collective-permute-start(bf16[64,2048]{1,0:T(8,128)(2,1)} %mine_hbm.1), channel_id=1, source_target_pairs={{0,1},{1,0},{2,3},{3,2},{4,5},{5,4},{6,7},{7,6},{8,9},{9,8},{10,11... | collective-permute-start | bytes 786440 | tf_op jit(solution)/shard_map/ppermute | solution.py:357
  5.1 8.2 %collective-permute-start.1 = (bf16[384,128]{1,0:T(8,128)(2,1)S(1)}, bf16[384,128]{1,0:T(8,128)(2,1)S(1)}, u32[]{:S(2)}, u32[]{:S(2)}) collective-permute-start(bf16[384,128]{1,0:T(8,128)(2,1)S(1)} %get-tuple-element.41.refs_3_.refs_11_), channel_id=1, source_target_pairs={{0,6},{2,4},{4,2},{6,0},{8,14},{10,12},{12,10},{14,8},{16,22},{18,... | collective-permute-start | bytes 294920 | tf_op jit(solution)/shard_map/ppermute | solution.py:371
  8.6 5.6 %collective-permute-start.2 = (bf16[384,128]{1,0:T(8,128)(2,1)S(1)}, bf16[384,128]{1,0:T(8,128)(2,1)S(1)}, u32[]{:S(2)}, u32[]{:S(2)}) collective-permute-start(bf16[384,128]{1,0:T(8,128)(2,1)S(1)} %get-tuple-element.41.refs_3_.refs_11_), channel_id=1, source_target_pairs={{0,4},{2,6},{4,0},{6,2},{8,12},{10,14},{12,8},{14,10},{16,20},{18,... | collective-permute-start | bytes 294920 | tf_op jit(solution)/shard_map/ppermute | solution.py:371
  9.1 5.3 %collective-permute-start.3 = (bf16[384,128]{1,0:T(8,128)(2,1)S(1)}, bf16[384,128]{1,0:T(8,128)(2,1)S(1)}, u32[]{:S(2)}, u32[]{:S(2)}) collective-permute-start(bf16[384,128]{1,0:T(8,128)(2,1)S(1)} %get-tuple-element.41.refs_3_.refs_11_), channel_id=1, source_target_pairs={{0,2},{2,0},{4,6},{6,4},{8,10},{10,8},{12,14},{14,12},{16,18},{18,... | collective-permute-start | bytes 294920 | tf_op jit(solution)/shard_map/ppermute | solution.py:371
  9.3 12.3 %collective-permute-start.4 = (bf16[128,128]{1,0:T(8,128)(2,1)S(1)}, bf16[128,128]{1,0:T(8,128)(2,1)S(1)}, u32[]{:S(2)}, u32[]{:S(2)}) collective-permute-start(bf16[128,128]{1,0:T(8,128)(2,1)S(1)} %get-tuple-element.43.val_ref), channel_id=1, source_target_pairs={{0,24},{2,26},{4,28},{6,30},{8,16},{10,18},{12,20},{14,22},{16,8},... | collective-permute-start | bytes 98312 | tf_op jit(solution)/shard_map/ppermute | solution.py:371
  15.0 16.0 %collective-permute-start.7 = (bf16[384,128]{1,0:T(8,128)(2,1)S(1)}, bf16[384,128]{1,0:T(8,128)(2,1)S(1)}, u32[]{:S(2)}, u32[]{:S(2)}) collective-permute-start(bf16[384,128]{1,0:T(8,128)(2,1)S(1)} %get-tuple-element.45.refs_3_), channel_id=1, source_target_pairs={{0,24},{2,26},{4,28},{6,30},{8,16},{10,18},{12,20},{14,22},{16,8},... | collective-permute-start | bytes 294920 | tf_op jit(solution)/shard_map/ppermute | solution.py:371
  18.6 12.4 %collective-permute-start.8 = (bf16[384,128]{1,0:T(8,128)(2,1)S(1)}, bf16[384,128]{1,0:T(8,128)(2,1)S(1)}, u32[]{:S(2)}, u32[]{:S(2)}) collective-permute-start(bf16[384,128]{1,0:T(8,128)(2,1)S(1)} %get-tuple-element.45.refs_3_), channel_id=1, source_target_pairs={{0,16},{2,18},{4,20},{6,22},{8,24},{10,26},{12,28},{14,30},{16,0},... | collective-permute-start | bytes 294920 | tf_op jit(solution)/shard_map/ppermute | solution.py:371
  18.6 12.4 %collective-permute-start.9 = (bf16[384,128]{1,0:T(8,128)(2,1)S(1)}, bf16[384,128]{1,0:T(8,128)(2,1)S(1)}, u32[]{:S(2)}, u32[]{:S(2)}) collective-permute-start(bf16[384,128]{1,0:T(8,128)(2,1)S(1)} %get-tuple-element.45.refs_3_), channel_id=1, source_target_pairs={{0,8},{2,10},{4,12},{6,14},{8,0},{10,2},{12,4},{14,6},{16,24},{18,... | collective-permute-start | bytes 294920 | tf_op jit(solution)/shard_map/ppermute | solution.py:371
  19.4 9.0 %collective-permute-start.5 = (bf16[128,128]{1,0:T(8,128)(2,1)S(1)}, bf16[128,128]{1,0:T(8,128)(2,1)S(1)}, u32[]{:S(2)}, u32[]{:S(2)}) collective-permute-start(bf16[128,128]{1,0:T(8,128)(2,1)S(1)} %get-tuple-element.43.val_ref), channel_id=1, source_target_pairs={{0,16},{2,18},{4,20},{6,22},{8,24},{10,26},{12,28},{14,30},{16,0},... | collective-permute-start | bytes 98312 | tf_op jit(solution)/shard_map/ppermute | solution.py:371
  21.6 6.9 %collective-permute-start.6 = (bf16[128,128]{1,0:T(8,128)(2,1)S(1)}, bf16[128,128]{1,0:T(8,128)(2,1)S(1)}, u32[]{:S(2)}, u32[]{:S(2)}) collective-permute-start(bf16[128,128]{1,0:T(8,128)(2,1)S(1)} %get-tuple-element.43.val_ref), channel_id=1, source_target_pairs={{0,8},{2,10},{4,12},{6,14},{8,0},{10,2},{12,4},{14,6},{16,24},{18,... | collective-permute-start | bytes 98312 | tf_op jit(solution)/shard_map/ppermute | solution.py:371
  29.8 7.4 %collective-permute-start.13 = (bf16[384,128]{1,0:T(8,128)(2,1)S(1)}, bf16[384,128]{1,0:T(8,128)(2,1)S(1)}, u32[]{:S(2)}, u32[]{:S(2)}) collective-permute-start(bf16[384,128]{1,0:T(8,128)(2,1)S(1)} %get-tuple-element.54.refs_7_), channel_id=1, source_target_pairs={{0,6},{2,4},{4,2},{6,0},{8,14},{10,12},{12,10},{14,8},{16,22},{18,... | collective-permute-start | bytes 294920 | tf_op jit(solution)/shard_map/ppermute | solution.py:371
  31.8 11.4 %collective-permute-start.10 = (bf16[512,128]{1,0:T(8,128)(2,1)S(1)}, bf16[512,128]{1,0:T(8,128)(2,1)S(1)}, u32[]{:S(2)}, u32[]{:S(2)}) collective-permute-start(bf16[512,128]{1,0:T(8,128)(2,1)S(1)} %get-tuple-element.50), channel_id=1, source_target_pairs={{0,6},{2,4},{4,2},{6,0},{8,14},{10,12},{12,10},{14,8},{16,22},{18,... | collective-permute-start | bytes 393224 | tf_op jit(solution)/shard_map/ppermute | solution.py:371
  33.7 9.5 %collective-permute-start.11 = (bf16[512,128]{1,0:T(8,128)(2,1)S(1)}, bf16[512,128]{1,0:T(8,128)(2,1)S(1)}, u32[]{:S(2)}, u32[]{:S(2)}) collective-permute-start(bf16[512,128]{1,0:T(8,128)(2,1)S(1)} %get-tuple-element.51), channel_id=1, source_target_pairs={{0,4},{2,6},{4,0},{6,2},{8,12},{10,14},{12,8},{14,10},{16,20},{18,... | collective-permute-start | bytes 393224 | tf_op jit(solution)/shard_map/ppermute | solution.py:371
  35.2 8.0 %collective-permute-start.12 = (bf16[512,128]{1,0:T(8,128)(2,1)S(1)}, bf16[512,128]{1,0:T(8,128)(2,1)S(1)}, u32[]{:S(2)}, u32[]{:S(2)}) collective-permute-start(bf16[512,128]{1,0:T(8,128)(2,1)S(1)} %get-tuple-element.52), channel_id=1, source_target_pairs={{0,2},{2,0},{4,6},{6,4},{8,10},{10,8},{12,14},{14,12},{16,18},{18,... | collective-permute-start | bytes 393224 | tf_op jit(solution)/shard_map/ppermute | solution.py:371
  35.4 7.7 %collective-permute-start.14 = (bf16[384,128]{1,0:T(8,128)(2,1)S(1)}, bf16[384,128]{1,0:T(8,128)(2,1)S(1)}, u32[]{:S(2)}, u32[]{:S(2)}) collective-permute-start(bf16[384,128]{1,0:T(8,128)(2,1)S(1)} %get-tuple-element.54.refs_7_), channel_id=1, source_target_pairs={{0,4},{2,6},{4,0},{6,2},{8,12},{10,14},{12,8},{14,10},{16,20},{18,... | collective-permute-start | bytes 294920 | tf_op jit(solution)/shard_map/ppermute | solution.py:371
  37.2 6.0 %collective-permute-start.15 = (bf16[384,128]{1,0:T(8,128)(2,1)S(1)}, bf16[384,128]{1,0:T(8,128)(2,1)S(1)}, u32[]{:S(2)}, u32[]{:S(2)}) collective-permute-start(bf16[384,128]{1,0:T(8,128)(2,1)S(1)} %get-tuple-element.54.refs_7_), channel_id=1, source_target_pairs={{0,2},{2,0},{4,6},{6,4},{8,10},{10,8},{12,14},{14,12},{16,18},{18,... | collective-permute-start | bytes 294920 | tf_op jit(solution)/shard_map/ppermute | solution.py:371
  37.8 2.2 %copy-start = (bf16[2048,1024]{1,0:T(8,128)(2,1)S(1)}, bf16[2048,1024]{1,0:T(8,128)(2,1)}, u32[]{:S(2)}) copy-start(bf16[2048,1024]{1,0:T(8,128)(2,1)} %weight_ref.1) | copy-start | bytes 12582916
  40.0 3.3 %copy-start.1 = (bf16[1024,2048]{1,0:T(8,128)(2,1)S(1)}, bf16[1024,2048]{1,0:T(8,128)(2,1)}, u32[]{:S(2)}) copy-start(bf16[1024,2048]{1,0:T(8,128)(2,1)} %refs_16_.1) | copy-start | bytes 12582916
  47.7 1.6 %collective-permute-start.16 = (bf16[64,2048]{1,0:T(8,128)(2,1)S(1)}, bf16[64,2048]{1,0:T(8,128)(2,1)S(1)}, u32[]{:S(2)}, u32[]{:S(2)}) collective-permute-start(bf16[64,2048]{1,0:T(8,128)(2,1)S(1)} %get-tuple-element.66), channel_id=1, source_target_pairs={{0,1},{1,0},{2,3},{3,2},{4,5},{5,4},{6,7},{7,6},{8,9},{9,8},{10,11... | collective-permute-start | bytes 786440 | tf_op jit(solution)/shard_map/ppermute | solution.py:503

commit v10 on v9

--- a/solution.py
+++ b/solution.py
@@ -107,7 +107,10 @@
 
 
 def prepare_kernel(core_ref, mine_ref, other_ref, weight_ref, rate_ref, bias_ref, gain_ref,
-                   rows_ref, kn_ref, val_ref, dirs_ref, coeff_ref, solved_ref, exit_ref, turn_ref):
+                   query_hbm, rows_ref, kn_ref, val_ref, dirs_ref, coeff_ref, solved_ref, exit_ref,
+                   turn_ref, query_ref, sem):
+    query_copy = pltpu.make_async_copy(query_hbm, query_ref, sem)
+    query_copy.start()
     core = core_ref[0]
     half = mine_ref.shape[0]
     rows_ref[pl.ds(pl.multiple_of(core * half, half), half), :] = mine_ref[...]
@@ -141,11 +144,13 @@
     turn_ref[:size] = high
     turn_ref[size : 2 * size] = low
     turn_ref[2 * size :] = vals.astype(BF16)
-
-
-def leave_kernel(group, place_ref, exit_ref, *refs):
-    turn_refs, (leave_ref, starts_ref) = refs[:group], refs[group : group + 2]
-    near_refs, (turns_ref, seen_ref) = refs[group + 2 : -2], refs[-2:]
+    query_copy.wait()
+
+
+def leave_kernel(group, after, place_ref, exit_ref, *refs):
+    turn_refs, refs = refs[after : after + group], refs[after + group :]
+    leave_ref, starts_ref = refs[:2]
+    near_refs, (turns_ref, seen_ref) = refs[2:-2], refs[-2:]
     member = place_ref[0] % group
     tokens, size = exit_ref.shape
     for step in range(group):
@@ -398,28 +403,31 @@
         scratch=(pltpu.SemaphoreType.DMA((7,)),),
         moved=12 * width * size,
     )
-    rows, kn, val, dirs, coeff, solved, exit_keys, turn = call(
+    rows, kn, val, dirs, coeff, solved, exit_keys, turn, query_weights = call(
         prepare_kernel,
         (
             shaped((tokens, width), BF16), square, shaped((tokens, size), BF16), square, square,
             square, square, shaped((2 * size + tokens, size), BF16),
+            shaped(w_query.shape, BF16),
         ),
-        (core, mine, other, weights, rate_row, rate_bias, key_gain),
-        in_specs=[smem] + [vmem] * 4 + [smem, vmem],
+        (core, mine, other, weights, rate_row, rate_bias, key_gain, in_hbm(w_query)),
+        in_specs=[smem] + [vmem] * 4 + [smem, vmem, hbm],
+        scratch=(pltpu.SemaphoreType.DMA,),
+        limit=12,
         flops=6 * tokens * width * size,
         moved=8 * width * size,
     )
     turns = within_group([turn] * group)
     line = along_line([val] * groups)
     leaving, starts, *near = call(
-        functools.partial(leave_kernel, group),
+        functools.partial(leave_kernel, group, groups - 1),
         [
             shaped((2 * tokens + size, size), BF16),
             shaped((group, size, size), F32),
         ]
         + [shaped((tokens, size), BF16)] * group,
-        (place, exit_keys, *turns[::-1]),
-        in_specs=[smem] + [vmem] * (1 + group),
+        (place, exit_keys, *line[1:], *turns[::-1]),
+        in_specs=[smem, vmem] + [anywhere] * (groups - 1) + [vmem] * group,
         scratch=(
             pltpu.VMEM((group, size, size), F32),
             pltpu.VMEM((group, tokens, size), BF16),
@@ -450,7 +458,7 @@
             shaped((heads, tokens, 1), F32),
             shaped((heads, tokens, 1), F32),
         ),
-        (rows, w_query, query_gain, kn, dirs, coeff, solved, val),
+        (rows, query_weights, query_gain, kn, dirs, coeff, solved, val),
         flops=4 * tokens * width * heads * size,
         moved=8 * width * heads * size,
         limit=14,

time: 50.2 us -> 50.9 us (1.014)
  waiting for transfers between devices: 8.38 us -> 5.28 us
  local copies, waits for them, and re-layouts: 2.19 us -> 4.14 us
  starting transfers between devices: 24.4 us -> 26.2 us
    ppermute x15, waiting for transfers between devices: 6.86 us -> 3.76 us  [swapped(): out[step] = lax.ppermute(values[step], 'ctx', pairs_of(step))]
    unnamed x6 -> x8, local copies, waits for them, and re-layouts: 2.19 us -> 4.14 us
    ppermute x15, starting transfers between devices: 23.9 us -> 25.6 us  [swapped(): out[step] = lax.ppermute(values[step], 'ctx', pairs_of(step))]
  transfers between devices with their start and end apart: 17 -> 17, of which waited for: 6 -> 3; matrix products, arithmetic and copies ran while one was open for 0% -> 0% of each run, Pallas kernels for 13% -> 12%
where the time goes in v10:
time: 50.9 us; the launch traced here: 50.7 us
  starting transfers between devices  26.2 us (51%)
  Pallas kernels  13.5 us (27%)
  waiting for transfers between devices  5.28 us (10%)
  local copies, waits for them, and re-layouts  4.14 us (8%)
  between operations  0.8 us (2%)
  other arithmetic  0.77 us (2%)
    ppermute x15, starting transfers between devices, swapped(): out[step] = lax.ppermute(values[step], 'ctx', pairs_of(step))  25.6 us
    pallas_call x7, Pallas kernels, call(): pl.pallas_call(kernel, out_shape=out_shape, in_specs=in_specs or [vmem] *...  13.5 us
    unnamed x8, local copies, waits for them, and re-layouts  4.14 us
    ppermute x15, waiting for transfers between devices, swapped(): out[step] = lax.ppermute(values[step], 'ctx', pairs_of(step))  3.76 us
    ppermute x1, waiting for transfers between devices, body(): return kept + lax.ppermute(away, 'head', [(0, 1), (1, 0)])  1.52 us
  transfers between devices with their start and end apart: 17, of which 3 were waited for; matrix products, arithmetic and copies ran while one was open for 0% of the time, Pallas kernels for 12%

profile of v10, /device:TPU:0, one launch (start us, length us, event | category | flops | bytes accessed | tf_op | source)
XLA Modules:
  0.0 50.7 jit_solution(3229125724406863433)
XLA Ops:
  1.1 1.5 %shard_map.109 = (bf16[2048,384]{1,0:T(8,128)(2,1)S(1)}, bf16[1,2048]{1,0:T(2,128)(2,1)S(1)}, f32[1,128]{1,0:T(1,128)S(1)}, f32[1,128]{1,0:T(1,128)S(1)}, bf16[64,2048]{1,0:T(8,128)(2,1)S(1)}) custom-call(bf16[2048,128]{1,0:T(8,128)(2,1)} %key_hbm.1, bf16[2048,128]{1,0:T(8,128)(2,1)} %dir_hbm.1, bf16[2048,128]{1,0:T(8,128)(2,1)} %value_hbm.1, ...), custom_call_target="tpu_custom_call" | custom-call | bytes 3145728 | tf_op jit(solution)/shard_map/pallas_call | solution.py:21
  2.7 2.5 %shard_map.110 = (bf16[128,2048]{1,0:T(8,128)(2,1)S(1)}, f32[128,128]{1,0:T(8,128)S(1)}, bf16[128,128]{1,0:T(8,128)(2,1)S(1)}, f32[128,128]{1,0:T(8,128)S(1)}, f...) custom-call(s32[1]{0:T(128)} %bitcast.1.core_ref, ...), custom_call_target="tpu_custom_call" | custom-call | flops 201326592 | bytes 2097152 | tf_op jit(solution)/shard_map/pallas_call | solution.py:21
  5.2 1.9 %copy-done.1 = bf16[2048,1024]{1,0:T(8,128)(2,1)} copy-done((bf16[2048,1024]{1,0:T(8,128)(2,1)}, bf16[2048,1024]{1,0:T(8,128)(2,1)S(1)}, u32[]{:S(2)}) %copy-start.1) | copy-done | bytes 4194328
  7.1 3.4 %collective-permute-start.4 = (bf16[384,128]{1,0:T(8,128)(2,1)S(1)}, bf16[384,128]{1,0:T(8,128)(2,1)S(1)}, u32[]{:S(2)}, u32[]{:S(2)}) collective-permute-start(bf16[384,128]{1,0:T(8,128)(2,1)S(1)} %get-tuple-element.43.refs_6_.refs_11_), channel_id=1, source_target_pairs={{0,6},{2,4},{4,2},{6,0},{8,14},{10,12},{12,10},{14,8},{16,22},{18,... | collective-permute-start | bytes 294920 | tf_op jit(solution)/shard_map/ppermute | solution.py:376
  11.1 2.0 %collective-permute-start.1 = (bf16[128,128]{1,0:T(8,128)(2,1)S(1)}, bf16[128,128]{1,0:T(8,128)(2,1)S(1)}, u32[]{:S(2)}, u32[]{:S(2)}) collective-permute-start(bf16[128,128]{1,0:T(8,128)(2,1)S(1)} %get-tuple-element.42.val_ref), channel_id=1, source_target_pairs={{0,8},{2,10},{4,12},{6,14},{8,0},{10,2},{12,4},{14,6},{16,24},{18,... | collective-permute-start | bytes 98312 | tf_op jit(solution)/shard_map/ppermute | solution.py:376
  13.2 2.6 %collective-permute-start.2 = (bf16[128,128]{1,0:T(8,128)(2,1)S(1)}, bf16[128,128]{1,0:T(8,128)(2,1)S(1)}, u32[]{:S(2)}, u32[]{:S(2)}) collective-permute-start(bf16[128,128]{1,0:T(8,128)(2,1)S(1)} %get-tuple-element.42.val_ref), channel_id=1, source_target_pairs={{0,16},{2,18},{4,20},{6,22},{8,24},{10,26},{12,28},{14,30},{16,0},... | collective-permute-start | bytes 98312 | tf_op jit(solution)/shard_map/ppermute | solution.py:376
  15.8 3.5 %collective-permute-start.3 = (bf16[128,128]{1,0:T(8,128)(2,1)S(1)}, bf16[128,128]{1,0:T(8,128)(2,1)S(1)}, u32[]{:S(2)}, u32[]{:S(2)}) collective-permute-start(bf16[128,128]{1,0:T(8,128)(2,1)S(1)} %get-tuple-element.42.val_ref), channel_id=1, source_target_pairs={{0,24},{2,26},{4,28},{6,30},{8,16},{10,18},{12,20},{14,22},{16,8},... | collective-permute-start | bytes 98312 | tf_op jit(solution)/shard_map/ppermute | solution.py:376
  19.2 2.2 %collective-permute-done.3.refs_2_.refs_0_ = bf16[128,128]{1,0:T(8,128)(2,1)S(1)} collective-permute-done((bf16[128,128]{1,0:T(8,128)(2,1)S(1)}, bf16[128,128]{1,0:T(8,128)(2,1)S(1)}, u32[]{:S(2)}, u32[]{:S(2)}) %collective-permute-start.3) | collective-permute-done | bytes 32800 | tf_op jit(solution)/shard_map/ppermute | solution.py:376
  22.0 3.6 %collective-permute-start.7 = (bf16[384,128]{1,0:T(8,128)(2,1)S(1)}, bf16[384,128]{1,0:T(8,128)(2,1)S(1)}, u32[]{:S(2)}, u32[]{:S(2)}) collective-permute-start(bf16[384,128]{1,0:T(8,128)(2,1)S(1)} %get-tuple-element.46.refs_3_), channel_id=1, source_target_pairs={{0,24},{2,26},{4,28},{6,30},{8,16},{10,18},{12,20},{14,22},{16,8},... | collective-permute-start | bytes 294920 | tf_op jit(solution)/shard_map/ppermute | solution.py:376
  25.6 0.8 %collective-permute-start.9 = (bf16[384,128]{1,0:T(8,128)(2,1)S(1)}, bf16[384,128]{1,0:T(8,128)(2,1)S(1)}, u32[]{:S(2)}, u32[]{:S(2)}) collective-permute-start(bf16[384,128]{1,0:T(8,128)(2,1)S(1)} %get-tuple-element.46.refs_3_), channel_id=1, source_target_pairs={{0,8},{2,10},{4,12},{6,14},{8,0},{10,2},{12,4},{14,6},{16,24},{18,... | collective-permute-start | bytes 294920 | tf_op jit(solution)/shard_map/ppermute | solution.py:376
  26.5 1.3 %shard_map.112 = (bf16[384,128]{1,0:T(8,128)(2,1)S(1)}, s32[1]{0:T(128)}) custom-call(s32[1]{0:T(128)} %bitcast.place_ref, s32[16]{0:T(128)S(1)} %bitcast.5, f32[4,128,128]{2,1,0:T(8,128)S(1)} %get-tuple-element.44.after_ref.refs_4_, bf16[128,128]{1,0:T(8,128)(2,1)S(1)} %collective-permute-done.3.refs_2_.refs_0_, ...), custom_call_target="tpu_custom_call" | custom-call | bytes 1000000 | tf_op jit(solution)/shard_map/pallas_call | solution.py:21
  27.8 2.5 %collective-permute-start.13 = (bf16[384,128]{1,0:T(8,128)(2,1)S(1)}, bf16[384,128]{1,0:T(8,128)(2,1)S(1)}, u32[]{:S(2)}, u32[]{:S(2)}) collective-permute-start(bf16[384,128]{1,0:T(8,128)(2,1)S(1)} %get-tuple-element.55.refs_7_), channel_id=1, source_target_pairs={{0,6},{2,4},{4,2},{6,0},{8,14},{10,12},{12,10},{14,8},{16,22},{18,... | collective-permute-start | bytes 294920 | tf_op jit(solution)/shard_map/ppermute | solution.py:376
  30.3 1.5 %collective-permute-done.8.refs_1_ = bf16[384,128]{1,0:T(8,128)(2,1)S(1)} collective-permute-done((bf16[384,128]{1,0:T(8,128)(2,1)S(1)}, bf16[384,128]{1,0:T(8,128)(2,1)S(1)}, u32[]{:S(2)}, u32[]{:S(2)}) %collective-permute-start.8) | collective-permute-done | bytes 98336 | tf_op jit(solution)/shard_map/ppermute | solution.py:376
  31.8 0.8 %shard_map.113 = (bf16[512,128]{1,0:T(8,128)(2,1)S(1)}, bf16[512,128]{1,0:T(8,128)(2,1)S(1)}, bf16[512,128]{1,0:T(8,128)(2,1)S(1)}, bf16[512,128]{1,0:T(8,128)(2,1)S(1)}) custom-call(s32[1]{0:T(128)} %bitcast.place_ref, bf16[384,128]{1,0:T(8,128)(2,1)S(1)} %collective-permute-done.7.refs_0_, bf16[384,128]{1,0:T(8,128)(2,1)S(1)} %collective-permute-done.8.refs_1_, ...), custom_call_target="tpu_custom_call" | custom-call | flops 201326592 | bytes 1000000 | tf_op jit(solution)/shard_map/pallas_call | solution.py:21
  32.6 2.5 %collective-permute-start.10 = (bf16[512,128]{1,0:T(8,128)(2,1)S(1)}, bf16[512,128]{1,0:T(8,128)(2,1)S(1)}, u32[]{:S(2)}, u32[]{:S(2)}) collective-permute-start(bf16[512,128]{1,0:T(8,128)(2,1)S(1)} %get-tuple-element.51), channel_id=1, source_target_pairs={{0,6},{2,4},{4,2},{6,0},{8,14},{10,12},{12,10},{14,8},{16,22},{18,... | collective-permute-start | bytes 393224 | tf_op jit(solution)/shard_map/ppermute | solution.py:376
  35.1 0.5 %collective-permute-start.11 = (bf16[512,128]{1,0:T(8,128)(2,1)S(1)}, bf16[512,128]{1,0:T(8,128)(2,1)S(1)}, u32[]{:S(2)}, u32[]{:S(2)}) collective-permute-start(bf16[512,128]{1,0:T(8,128)(2,1)S(1)} %get-tuple-element.52), channel_id=1, source_target_pairs={{0,4},{2,6},{4,0},{6,2},{8,12},{10,14},{12,8},{14,10},{16,20},{18,... | collective-permute-start | bytes 393224 | tf_op jit(solution)/shard_map/ppermute | solution.py:376
  35.7 0.5 %collective-permute-start.12 = (bf16[512,128]{1,0:T(8,128)(2,1)S(1)}, bf16[512,128]{1,0:T(8,128)(2,1)S(1)}, u32[]{:S(2)}, u32[]{:S(2)}) collective-permute-start(bf16[512,128]{1,0:T(8,128)(2,1)S(1)} %get-tuple-element.53), channel_id=1, source_target_pairs={{0,2},{2,0},{4,6},{6,4},{8,10},{10,8},{12,14},{14,12},{16,18},{18,... | collective-permute-start | bytes 393224 | tf_op jit(solution)/shard_map/ppermute | solution.py:376
  36.2 1.5 %collective-permute-start.14 = (bf16[384,128]{1,0:T(8,128)(2,1)S(1)}, bf16[384,128]{1,0:T(8,128)(2,1)S(1)}, u32[]{:S(2)}, u32[]{:S(2)}) collective-permute-start(bf16[384,128]{1,0:T(8,128)(2,1)S(1)} %get-tuple-element.55.refs_7_), channel_id=1, source_target_pairs={{0,4},{2,6},{4,0},{6,2},{8,12},{10,14},{12,8},{14,10},{16,20},{18,... | collective-permute-start | bytes 294920 | tf_op jit(solution)/shard_map/ppermute | solution.py:376
  37.7 1.5 %collective-permute-start.15 = (bf16[384,128]{1,0:T(8,128)(2,1)S(1)}, bf16[384,128]{1,0:T(8,128)(2,1)S(1)}, u32[]{:S(2)}, u32[]{:S(2)}) collective-permute-start(bf16[384,128]{1,0:T(8,128)(2,1)S(1)} %get-tuple-element.55.refs_7_), channel_id=1, source_target_pairs={{0,2},{2,0},{4,6},{6,4},{8,10},{10,8},{12,14},{14,12},{16,18},{18,... | collective-permute-start | bytes 294920 | tf_op jit(solution)/shard_map/ppermute | solution.py:376
  39.2 2.2 %copy-done.2 = bf16[2048,1024]{1,0:T(8,128)(2,1)S(1)} copy-done((bf16[2048,1024]{1,0:T(8,128)(2,1)S(1)}, bf16[2048,1024]{1,0:T(8,128)(2,1)}, u32[]{:S(2)}) %copy-start.2) | copy-done | bytes 4194328
  41.4 2.4 %shard_map.114 = (bf16[8,128,128]{2,1,0:T(8,128)(2,1)S(1)}, f32[8,128,128]{2,1,0:T(8,128)S(1)}, f32[8,128,1]{2,1,0:T(8,128)S(1)}, f32[8,128,1]{2,1,0:T(8,128)S(1)}) custom-call(bf16[128,2048]{1,0:T(8,128)(2,1)S(1)} %get-tuple-element.56.rows_ref, bf16[2048,1024]{1,0:T(8,128)(2,1)S(1)} %copy-done.2, f32[1,128]{1,0:T(1,128)S(1)} %get-tuple-element.58.gain_ref, ...), custom_call_target="tpu_custom_call" | custom-call | flops 1073741824 | bytes 16777216 | tf_op jit(solution)/shard_map/pallas_call | solution.py:21
  43.9 4.4 %shard_map.115 = (bf16[64,2048]{1,0:T(8,128)(2,1)S(1)}, bf16[64,2048]{1,0:T(8,128)(2,1)S(1)}) custom-call(s32[1]{0:T(128)} %bitcast.place_ref, s32[1]{0:T(128)} %bitcast.1.core_ref, s32[1]{0:T(128)} %get-tuple-element.45.table_ref, bf16[512,128]{1,0:T(8,128)(2,1)S(1)} %collective-permute-done.10.refs_0_, ...), custom_call_target="tpu_custom_call" | custom-call | flops 536870912 | bytes 4000000 | tf_op jit(solution)/shard_map/pallas_call | solution.py:21
  48.4 1.5 %collective-permute-done.16 = bf16[64,2048]{1,0:T(8,128)(2,1)S(1)} collective-permute-done((bf16[64,2048]{1,0:T(8,128)(2,1)S(1)}, bf16[64,2048]{1,0:T(8,128)(2,1)S(1)}, u32[]{:S(2)}, u32[]{:S(2)}) %collective-permute-start.16) | collective-permute-done | bytes 262176 | tf_op jit(solution)/shard_map/ppermute | solution.py:511
  49.9 0.8 %add.3 = bf16[64,2048]{1,0:T(8,128)(2,1)} add(bf16[64,2048]{1,0:T(8,128)(2,1)S(1)} %get-tuple-element.67, bf16[64,2048]{1,0:T(8,128)(2,1)S(1)} %collective-permute-done.16) | non-fusion elementwise | flops 131072 | bytes 786432 | tf_op jit(solution)/shard_map/add | solution.py:511
  (26 shorter events, 1.7 us)
Async XLA Ops:
  0.0 2.7 %collective-permute-start = (bf16[64,2048]{1,0:T(8,128)(2,1)}, bf16[64,2048]{1,0:T(8,128)(2,1)S(1)}, u32[]{:S(2)}, u32[]{:S(2)}) collective-permute-start(bf16[64,2048]{1,0:T(8,128)(2,1)} %mine_hbm.1), channel_id=1, source_target_pairs={{0,1},{1,0},{2,3},{3,2},{4,5},{5,4},{6,7},{7,6},{8,9},{9,8},{10,11... | collective-permute-start | bytes 786440 | tf_op jit(solution)/shard_map/ppermute | solution.py:362
  1.1 25.3 %copy-start.3 = (s32[1,16]{1,0:T(1,128)S(1)}, s32[1,16]{1,0:T(1,128)}, u32[]{:S(2)}) copy-start(s32[1,16]{1,0:T(1,128)} %param.21) | copy-start | bytes 196
  5.1 2.0 %copy-start.1 = (bf16[2048,1024]{1,0:T(8,128)(2,1)}, bf16[2048,1024]{1,0:T(8,128)(2,1)S(1)}, u32[]{:S(2)}) copy-start(bf16[2048,1024]{1,0:T(8,128)(2,1)S(1)} %get-tuple-element.57.weight_ref) | copy-start | bytes 12582916
  7.1 14.4 %collective-permute-start.4 = (bf16[384,128]{1,0:T(8,128)(2,1)S(1)}, bf16[384,128]{1,0:T(8,128)(2,1)S(1)}, u32[]{:S(2)}, u32[]{:S(2)}) collective-permute-start(bf16[384,128]{1,0:T(8,128)(2,1)S(1)} %get-tuple-element.43.refs_6_.refs_11_), channel_id=1, source_target_pairs={{0,6},{2,4},{4,2},{6,0},{8,14},{10,12},{12,10},{14,8},{16,22},{18,... | collective-permute-start | bytes 294920 | tf_op jit(solution)/shard_map/ppermute | solution.py:376
  10.5 10.9 %collective-permute-start.5 = (bf16[384,128]{1,0:T(8,128)(2,1)S(1)}, bf16[384,128]{1,0:T(8,128)(2,1)S(1)}, u32[]{:S(2)}, u32[]{:S(2)}) collective-permute-start(bf16[384,128]{1,0:T(8,128)(2,1)S(1)} %get-tuple-element.43.refs_6_.refs_11_), channel_id=1, source_target_pairs={{0,4},{2,6},{4,0},{6,2},{8,12},{10,14},{12,8},{14,10},{16,20},{18,... | collective-permute-start | bytes 294920 | tf_op jit(solution)/shard_map/ppermute | solution.py:376
  11.1 10.4 %collective-permute-start.6 = (bf16[384,128]{1,0:T(8,128)(2,1)S(1)}, bf16[384,128]{1,0:T(8,128)(2,1)S(1)}, u32[]{:S(2)}, u32[]{:S(2)}) collective-permute-start(bf16[384,128]{1,0:T(8,128)(2,1)S(1)} %get-tuple-element.43.refs_6_.refs_11_), channel_id=1, source_target_pairs={{0,2},{2,0},{4,6},{6,4},{8,10},{10,8},{12,14},{14,12},{16,18},{18,... | collective-permute-start | bytes 294920 | tf_op jit(solution)/shard_map/ppermute | solution.py:376
  11.1 4.6 %collective-permute-start.1 = (bf16[128,128]{1,0:T(8,128)(2,1)S(1)}, bf16[128,128]{1,0:T(8,128)(2,1)S(1)}, u32[]{:S(2)}, u32[]{:S(2)}) collective-permute-start(bf16[128,128]{1,0:T(8,128)(2,1)S(1)} %get-tuple-element.42.val_ref), channel_id=1, source_target_pairs={{0,8},{2,10},{4,12},{6,14},{8,0},{10,2},{12,4},{14,6},{16,24},{18,... | collective-permute-start | bytes 98312 | tf_op jit(solution)/shard_map/ppermute | solution.py:376
  13.2 6.1 %collective-permute-start.2 = (bf16[128,128]{1,0:T(8,128)(2,1)S(1)}, bf16[128,128]{1,0:T(8,128)(2,1)S(1)}, u32[]{:S(2)}, u32[]{:S(2)}) collective-permute-start(bf16[128,128]{1,0:T(8,128)(2,1)S(1)} %get-tuple-element.42.val_ref), channel_id=1, source_target_pairs={{0,16},{2,18},{4,20},{6,22},{8,24},{10,26},{12,28},{14,30},{16,0},... | collective-permute-start | bytes 98312 | tf_op jit(solution)/shard_map/ppermute | solution.py:376
  15.8 5.7 %collective-permute-start.3 = (bf16[128,128]{1,0:T(8,128)(2,1)S(1)}, bf16[128,128]{1,0:T(8,128)(2,1)S(1)}, u32[]{:S(2)}, u32[]{:S(2)}) collective-permute-start(bf16[128,128]{1,0:T(8,128)(2,1)S(1)} %get-tuple-element.42.val_ref), channel_id=1, source_target_pairs={{0,24},{2,26},{4,28},{6,30},{8,16},{10,18},{12,20},{14,22},{16,8},... | collective-permute-start | bytes 98312 | tf_op jit(solution)/shard_map/ppermute | solution.py:376
  19.2 24.7 %copy-start = (bf16[1024,2048]{1,0:T(8,128)(2,1)S(1)}, bf16[1024,2048]{1,0:T(8,128)(2,1)}, u32[]{:S(2)}) copy-start(bf16[1024,2048]{1,0:T(8,128)(2,1)} %refs_16_.1) | copy-start | bytes 12582916
  22.0 8.3 %collective-permute-start.7 = (bf16[384,128]{1,0:T(8,128)(2,1)S(1)}, bf16[384,128]{1,0:T(8,128)(2,1)S(1)}, u32[]{:S(2)}, u32[]{:S(2)}) collective-permute-start(bf16[384,128]{1,0:T(8,128)(2,1)S(1)} %get-tuple-element.46.refs_3_), channel_id=1, source_target_pairs={{0,24},{2,26},{4,28},{6,30},{8,16},{10,18},{12,20},{14,22},{16,8},... | collective-permute-start | bytes 294920 | tf_op jit(solution)/shard_map/ppermute | solution.py:376
  25.6 6.2 %collective-permute-start.8 = (bf16[384,128]{1,0:T(8,128)(2,1)S(1)}, bf16[384,128]{1,0:T(8,128)(2,1)S(1)}, u32[]{:S(2)}, u32[]{:S(2)}) collective-permute-start(bf16[384,128]{1,0:T(8,128)(2,1)S(1)} %get-tuple-element.46.refs_3_), channel_id=1, source_target_pairs={{0,16},{2,18},{4,20},{6,22},{8,24},{10,26},{12,28},{14,30},{16,0},... | collective-permute-start | bytes 294920 | tf_op jit(solution)/shard_map/ppermute | solution.py:376
  25.6 6.2 %collective-permute-start.9 = (bf16[384,128]{1,0:T(8,128)(2,1)S(1)}, bf16[384,128]{1,0:T(8,128)(2,1)S(1)}, u32[]{:S(2)}, u32[]{:S(2)}) collective-permute-start(bf16[384,128]{1,0:T(8,128)(2,1)S(1)} %get-tuple-element.46.refs_3_), channel_id=1, source_target_pairs={{0,8},{2,10},{4,12},{6,14},{8,0},{10,2},{12,4},{14,6},{16,24},{18,... | collective-permute-start | bytes 294920 | tf_op jit(solution)/shard_map/ppermute | solution.py:376
  27.8 9.9 %collective-permute-start.13 = (bf16[384,128]{1,0:T(8,128)(2,1)S(1)}, bf16[384,128]{1,0:T(8,128)(2,1)S(1)}, u32[]{:S(2)}, u32[]{:S(2)}) collective-permute-start(bf16[384,128]{1,0:T(8,128)(2,1)S(1)} %get-tuple-element.55.refs_7_), channel_id=1, source_target_pairs={{0,6},{2,4},{4,2},{6,0},{8,14},{10,12},{12,10},{14,8},{16,22},{18,... | collective-permute-start | bytes 294920 | tf_op jit(solution)/shard_map/ppermute | solution.py:376
  32.6 11.2 %collective-permute-start.10 = (bf16[512,128]{1,0:T(8,128)(2,1)S(1)}, bf16[512,128]{1,0:T(8,128)(2,1)S(1)}, u32[]{:S(2)}, u32[]{:S(2)}) collective-permute-start(bf16[512,128]{1,0:T(8,128)(2,1)S(1)} %get-tuple-element.51), channel_id=1, source_target_pairs={{0,6},{2,4},{4,2},{6,0},{8,14},{10,12},{12,10},{14,8},{16,22},{18,... | collective-permute-start | bytes 393224 | tf_op jit(solution)/shard_map/ppermute | solution.py:376
  35.1 8.7 %collective-permute-start.11 = (bf16[512,128]{1,0:T(8,128)(2,1)S(1)}, bf16[512,128]{1,0:T(8,128)(2,1)S(1)}, u32[]{:S(2)}, u32[]{:S(2)}) collective-permute-start(bf16[512,128]{1,0:T(8,128)(2,1)S(1)} %get-tuple-element.52), channel_id=1, source_target_pairs={{0,4},{2,6},{4,0},{6,2},{8,12},{10,14},{12,8},{14,10},{16,20},{18,... | collective-permute-start | bytes 393224 | tf_op jit(solution)/shard_map/ppermute | solution.py:376
  35.7 8.2 %collective-permute-start.12 = (bf16[512,128]{1,0:T(8,128)(2,1)S(1)}, bf16[512,128]{1,0:T(8,128)(2,1)S(1)}, u32[]{:S(2)}, u32[]{:S(2)}) collective-permute-start(bf16[512,128]{1,0:T(8,128)(2,1)S(1)} %get-tuple-element.53), channel_id=1, source_target_pairs={{0,2},{2,0},{4,6},{6,4},{8,10},{10,8},{12,14},{14,12},{16,18},{18,... | collective-permute-start | bytes 393224 | tf_op jit(solution)/shard_map/ppermute | solution.py:376
  36.2 7.7 %collective-permute-start.14 = (bf16[384,128]{1,0:T(8,128)(2,1)S(1)}, bf16[384,128]{1,0:T(8,128)(2,1)S(1)}, u32[]{:S(2)}, u32[]{:S(2)}) collective-permute-start(bf16[384,128]{1,0:T(8,128)(2,1)S(1)} %get-tuple-element.55.refs_7_), channel_id=1, source_target_pairs={{0,4},{2,6},{4,0},{6,2},{8,12},{10,14},{12,8},{14,10},{16,20},{18,... | collective-permute-start | bytes 294920 | tf_op jit(solution)/shard_map/ppermute | solution.py:376
  37.7 6.1 %collective-permute-start.15 = (bf16[384,128]{1,0:T(8,128)(2,1)S(1)}, bf16[384,128]{1,0:T(8,128)(2,1)S(1)}, u32[]{:S(2)}, u32[]{:S(2)}) collective-permute-start(bf16[384,128]{1,0:T(8,128)(2,1)S(1)} %get-tuple-element.55.refs_7_), channel_id=1, source_target_pairs={{0,2},{2,0},{4,6},{6,4},{8,10},{10,8},{12,14},{14,12},{16,18},{18,... | collective-permute-start | bytes 294920 | tf_op jit(solution)/shard_map/ppermute | solution.py:376
  39.2 2.2 %copy-start.2 = (bf16[2048,1024]{1,0:T(8,128)(2,1)S(1)}, bf16[2048,1024]{1,0:T(8,128)(2,1)}, u32[]{:S(2)}) copy-start(bf16[2048,1024]{1,0:T(8,128)(2,1)} %copy-done.1) | copy-start | bytes 12582916
  48.3 1.6 %collective-permute-start.16 = (bf16[64,2048]{1,0:T(8,128)(2,1)S(1)}, bf16[64,2048]{1,0:T(8,128)(2,1)S(1)}, u32[]{:S(2)}, u32[]{:S(2)}) collective-permute-start(bf16[64,2048]{1,0:T(8,128)(2,1)S(1)} %get-tuple-element.68), channel_id=1, source_target_pairs={{0,1},{1,0},{2,3},{3,2},{4,5},{5,4},{6,7},{7,6},{8,9},{9,8},{10,11... | collective-permute-start | bytes 786440 | tf_op jit(solution)/shard_map/ppermute | solution.py:511

commit v11 on v9

--- a/solution.py
+++ b/solution.py
@@ -203,16 +203,26 @@
         line_ref[(way - 1) * tokens : way * tokens] = val_refs[groups - 1 - way][...]
 
 
-def query_kernel(rows_ref, weight_ref, gain_ref, kn_ref, dirs_ref, coeff_ref, solved_ref, val_ref,
-                 moved_ref, weighted_ref, peak_ref, total_ref):
+def query_kernel(rows_ref, weight_hbm, gain_ref, kn_ref, dirs_ref, coeff_ref, solved_ref, val_ref,
+                 moved_ref, weighted_ref, peak_ref, total_ref, weight_ref, sems):
     tokens, size = kn_ref.shape
     heads = moved_ref.shape[0]
     across = jnp.concatenate([kn_ref[...], dirs_ref[...]], axis=0)
     into = jnp.concatenate([coeff_ref[...], solved_ref[...]], axis=1)
-    count = math.gcd(heads, 4)
-    for turn in range(heads // count):
-        wide = slice(turn * count * size, (turn + 1) * count * size)
-        raw = jnp.dot(rows_ref[...], weight_ref[:, wide], preferred_element_type=F32)
+    turns, _, wide = weight_ref.shape
+    count = heads // turns
+    copies = [
+        pltpu.make_async_copy(
+            weight_hbm.at[:, turn * wide : (turn + 1) * wide], weight_ref.at[turn], sems.at[turn]
+        )
+        for turn in range(turns)
+    ]
+    copies[0].start()
+    for turn in range(turns):
+        copies[turn].wait()
+        if turn + 1 < turns:
+            copies[turn + 1].start()
+        raw = jnp.dot(rows_ref[...], weight_ref[turn], preferred_element_type=F32)
         parts = [raw[:, at : at + size] for at in range(0, count * size, size)]
         raw = jnp.concatenate(parts, axis=0)
         queries = (
@@ -240,10 +250,8 @@
 
 
 def arrive_kernel(groups, group, tokens, place_ref, *refs):
-    arrived, starts_ref, near_refs = refs[:groups], refs[groups], refs[groups + 1 :]
-    far_refs, (keys_ref, whole_ref) = refs[-group - 2 : -2], refs[-2:]
-    mine, member = place_ref[0] // group, place_ref[0] % group
-    size = starts_ref.shape[1]
+    arrived, (brought_ref, keys_ref, whole_ref) = refs[:groups], refs[groups:]
+    mine = place_ref[0] // group
     for step in range(groups):
         index = source_of(mine, step, groups)
         ref = arrived[groups - 1 - step]
@@ -257,11 +265,19 @@
             whole = jnp.where(index + 2 < mine, dot3(whole, product), whole)
         product = whole
         brought.append(jnp.where(index + 1 < mine, dot3(keys, product), keys))
-    keys = jnp.concatenate(brought[::-1], axis=0)
+    brought_ref[...] = jnp.concatenate(brought[::-1], axis=0)
+
+
+def spread_kernel(group, place_ref, *refs):
+    brought_ref, starts_ref, near_refs = refs[0], refs[1], refs[2 : 2 + group]
+    far_refs = refs[-group:]
+    member = place_ref[0] % group
+    keys = brought_ref[...]
+    brought = keys.shape[0]
     for step in range(group):
         start = starts_ref[target_of(member, step, group)]
-        far_refs[step][: (groups - 1) * tokens] = dot3(keys, start).astype(BF16)
-        far_refs[step][(groups - 1) * tokens :] = near_refs[step][...]
+        far_refs[step][:brought] = dot3(keys, start).astype(BF16)
+        far_refs[step][brought:] = near_refs[step][...]
 
 
 def attend_kernel(group, segments, most, place_ref, core_ref, table_ref, *refs):
@@ -442,6 +458,7 @@
         limit=8 + group * groups // 4,
     )
     values = within_group([values] * group)
+    turns_of = heads // math.gcd(heads, 4)
     own = call(
         query_kernel,
         (
@@ -450,7 +467,12 @@
             shaped((heads, tokens, 1), F32),
             shaped((heads, tokens, 1), F32),
         ),
-        (rows, w_query, query_gain, kn, dirs, coeff, solved, val),
+        (rows, in_hbm(w_query), query_gain, kn, dirs, coeff, solved, val),
+        in_specs=[vmem, hbm] + [vmem] * 6,
+        scratch=(
+            pltpu.VMEM((turns_of, width, w_query.shape[1] // turns_of), BF16),
+            pltpu.SemaphoreType.DMA((turns_of,)),
+        ),
         flops=4 * tokens * width * heads * size,
         moved=8 * width * heads * size,
         limit=14,
@@ -469,15 +491,24 @@
         limit=8 + group * groups // 4,
     )
     values = within_group([values] * group)
-    far = call(
+    (brought,) = call(
         functools.partial(arrive_kernel, groups, group, tokens),
-        [shaped((groups * tokens, size), BF16)] * group,
-        (place, *arrived[::-1], starts, *near),
-        in_specs=[smem] + [vmem] * (groups + 1 + group),
+        [shaped(((groups - 1) * tokens, size), F32)],
+        (place, *arrived[::-1]),
+        in_specs=[smem] + [vmem] * groups,
         scratch=(
             pltpu.VMEM((groups, tokens, size), F32),
             pltpu.VMEM((groups, size, size), F32),
         ),
+        flops=6 * groups * size**3,
+        moved=10**6,
+        limit=8 + group * groups // 4,
+    )
+    far = call(
+        functools.partial(spread_kernel, group),
+        [shaped((groups * tokens, size), BF16)] * group,
+        (place, brought, starts, *near, *values[1:]),
+        in_specs=[smem] + [vmem] * (2 + group) + [anywhere] * (group - 1),
         flops=6 * groups * group * size**3,
         moved=10**6,
         limit=8 + group * groups // 4,

time: 50.2 us -> 52.2 us (1.040)
  waiting for transfers between devices: 8.38 us -> 11.8 us
  local copies, waits for them, and re-layouts: 2.19 us -> 0.01 us
  Pallas kernels: 13.5 us -> 15.6 us
  starting transfers between devices: 24.4 us -> 23.1 us
    ppermute x15, waiting for transfers between devices: 6.86 us -> 10.3 us  [swapped(): out[step] = lax.ppermute(values[step], 'ctx', pairs_of(step))]
    unnamed x6 -> x4, local copies, waits for them, and re-layouts: 2.19 us -> 0.01 us
    pallas_call x7 -> x8, Pallas kernels: 13.5 us -> 15.6 us  [call(): pl.pallas_call(kernel, out_shape=out_shape, in_specs=in_specs or [vmem] *...]
    ppermute x15, starting transfers between devices: 23.9 us -> 22.5 us  [swapped(): out[step] = lax.ppermute(values[step], 'ctx', pairs_of(step))]
  transfers between devices with their start and end apart: 17 -> 17, of which waited for: 6 -> 9; matrix products, arithmetic and copies ran while one was open for 0% -> 0% of each run, Pallas kernels for 13% -> 15%
where the time goes in v11:
time: 52.2 us; the launch traced here: 52 us
  starting transfers between devices  23.1 us (44%)
  Pallas kernels  15.6 us (30%)
  waiting for transfers between devices  11.8 us (23%)
  other arithmetic  0.77 us (1%)
  between operations  0.77 us (1%)
    ppermute x15, starting transfers between devices, swapped(): out[step] = lax.ppermute(values[step], 'ctx', pairs_of(step))  22.5 us
    pallas_call x8, Pallas kernels, call(): pl.pallas_call(kernel, out_shape=out_shape, in_specs=in_specs or [vmem] *...  15.6 us
    ppermute x15, waiting for transfers between devices, swapped(): out[step] = lax.ppermute(values[step], 'ctx', pairs_of(step))  10.3 us
    ppermute x1, waiting for transfers between devices, body(): return kept + lax.ppermute(away, 'head', [(0, 1), (1, 0)])  1.52 us
  transfers between devices with their start and end apart: 17, of which 9 were waited for; matrix products, arithmetic and copies ran while one was open for 0% of the time, Pallas kernels for 15%

profile of v11, /device:TPU:0, one launch (start us, length us, event | category | flops | bytes accessed | tf_op | source)
XLA Modules:
  0.0 52.0 jit_solution(10480349945456385499)
XLA Ops:
  1.1 1.5 %shard_map.109 = (bf16[2048,384]{1,0:T(8,128)(2,1)S(1)}, bf16[1,2048]{1,0:T(2,128)(2,1)S(1)}, f32[1,128]{1,0:T(1,128)S(1)}, f32[1,128]{1,0:T(1,128)S(1)}, bf16[64,2048]{1,0:T(8,128)(2,1)S(1)}) custom-call(bf16[2048,128]{1,0:T(8,128)(2,1)} %key_hbm.1, bf16[2048,128]{1,0:T(8,128)(2,1)} %dir_hbm.1, bf16[2048,128]{1,0:T(8,128)(2,1)} %value_hbm.1, ...), custom_call_target="tpu_custom_call" | custom-call | bytes 3145728 | tf_op jit(solution)/shard_map/pallas_call | solution.py:21
  2.7 2.4 %shard_map.110 = (bf16[128,2048]{1,0:T(8,128)(2,1)S(1)}, f32[128,128]{1,0:T(8,128)S(1)}, bf16[128,128]{1,0:T(8,128)(2,1)S(1)}, f32[128,128]{1,0:T(8,128)S(1)}, f...) custom-call(s32[1]{0:T(128)} %bitcast.1.core_ref, ...), custom_call_target="tpu_custom_call" | custom-call | flops 201326592 | bytes 2097152 | tf_op jit(solution)/shard_map/pallas_call | solution.py:21
  5.1 3.5 %collective-permute-start.1 = (bf16[384,128]{1,0:T(8,128)(2,1)S(1)}, bf16[384,128]{1,0:T(8,128)(2,1)S(1)}, u32[]{:S(2)}, u32[]{:S(2)}) collective-permute-start(bf16[384,128]{1,0:T(8,128)(2,1)S(1)} %get-tuple-element.41.refs_3_.refs_11_), channel_id=1, source_target_pairs={{0,6},{2,4},{4,2},{6,0},{8,14},{10,12},{12,10},{14,8},{16,22},{18,... | collective-permute-start | bytes 294920 | tf_op jit(solution)/shard_map/ppermute | solution.py:387
  8.6 0.5 collective-permute-start.2
  9.3 2.9 %collective-permute-done.1.refs_0_.refs_8_ = bf16[384,128]{1,0:T(8,128)(2,1)S(1)} collective-permute-done((bf16[384,128]{1,0:T(8,128)(2,1)S(1)}, bf16[384,128]{1,0:T(8,128)(2,1)S(1)}, u32[]{:S(2)}, u32[]{:S(2)}) %collective-permute-start.1) | collective-permute-done | bytes 98336 | tf_op jit(solution)/shard_map/ppermute | solution.py:387
  12.2 2.0 %collective-permute-done.2.refs_1_.refs_9_ = bf16[384,128]{1,0:T(8,128)(2,1)S(1)} collective-permute-done((bf16[384,128]{1,0:T(8,128)(2,1)S(1)}, bf16[384,128]{1,0:T(8,128)(2,1)S(1)}, u32[]{:S(2)}, u32[]{:S(2)}) %collective-permute-start.2) | collective-permute-done | bytes 98336 | tf_op jit(solution)/shard_map/ppermute | solution.py:387
  15.0 3.7 %collective-permute-start.7 = (bf16[384,128]{1,0:T(8,128)(2,1)S(1)}, bf16[384,128]{1,0:T(8,128)(2,1)S(1)}, u32[]{:S(2)}, u32[]{:S(2)}) collective-permute-start(bf16[384,128]{1,0:T(8,128)(2,1)S(1)} %get-tuple-element.45.refs_3_), channel_id=1, source_target_pairs={{0,24},{2,26},{4,28},{6,30},{8,16},{10,18},{12,20},{14,22},{16,8},... | collective-permute-start | bytes 294920 | tf_op jit(solution)/shard_map/ppermute | solution.py:387
  18.9 0.8 %collective-permute-start.5 = (bf16[128,128]{1,0:T(8,128)(2,1)S(1)}, bf16[128,128]{1,0:T(8,128)(2,1)S(1)}, u32[]{:S(2)}, u32[]{:S(2)}) collective-permute-start(bf16[128,128]{1,0:T(8,128)(2,1)S(1)} %get-tuple-element.43.val_ref), channel_id=1, source_target_pairs={{0,16},{2,18},{4,20},{6,22},{8,24},{10,26},{12,28},{14,30},{16,0},... | collective-permute-start | bytes 98312 | tf_op jit(solution)/shard_map/ppermute | solution.py:387
  19.6 3.4 %collective-permute-start.6 = (bf16[128,128]{1,0:T(8,128)(2,1)S(1)}, bf16[128,128]{1,0:T(8,128)(2,1)S(1)}, u32[]{:S(2)}, u32[]{:S(2)}) collective-permute-start(bf16[128,128]{1,0:T(8,128)(2,1)S(1)} %get-tuple-element.43.val_ref), channel_id=1, source_target_pairs={{0,8},{2,10},{4,12},{6,14},{8,0},{10,2},{12,4},{14,6},{16,24},{18,... | collective-permute-start | bytes 98312 | tf_op jit(solution)/shard_map/ppermute | solution.py:387
  23.0 1.4 %collective-permute-done.4.refs_0_ = bf16[128,128]{1,0:T(8,128)(2,1)S(1)} collective-permute-done((bf16[128,128]{1,0:T(8,128)(2,1)S(1)}, bf16[128,128]{1,0:T(8,128)(2,1)S(1)}, u32[]{:S(2)}, u32[]{:S(2)}) %collective-permute-start.4) | collective-permute-done | bytes 32800 | tf_op jit(solution)/shard_map/ppermute | solution.py:387
  24.4 2.5 %collective-permute-start.9 = (bf16[384,128]{1,0:T(8,128)(2,1)S(1)}, bf16[384,128]{1,0:T(8,128)(2,1)S(1)}, u32[]{:S(2)}, u32[]{:S(2)}) collective-permute-start(bf16[384,128]{1,0:T(8,128)(2,1)S(1)} %get-tuple-element.45.refs_3_), channel_id=1, source_target_pairs={{0,8},{2,10},{4,12},{6,14},{8,0},{10,2},{12,4},{14,6},{16,24},{18,... | collective-permute-start | bytes 294920 | tf_op jit(solution)/shard_map/ppermute | solution.py:387
  27.4 1.3 %shard_map.112 = (bf16[384,128]{1,0:T(8,128)(2,1)S(1)}, s32[1]{0:T(128)}) custom-call(s32[1]{0:T(128)} %bitcast.place_ref, s32[16]{0:T(128)S(1)} %bitcast.5, f32[4,128,128]{2,1,0:T(8,128)S(1)} %get-tuple-element.42.after_ref.refs_1_, bf16[128,128]{1,0:T(8,128)(2,1)S(1)} %collective-permute-done.4.refs_0_, ...), custom_call_target="tpu_custom_call" | custom-call | bytes 1000000 | tf_op jit(solution)/shard_map/pallas_call | solution.py:21
  28.8 1.4 %collective-permute-start.10 = (bf16[384,128]{1,0:T(8,128)(2,1)S(1)}, bf16[384,128]{1,0:T(8,128)(2,1)S(1)}, u32[]{:S(2)}, u32[]{:S(2)}) collective-permute-start(bf16[384,128]{1,0:T(8,128)(2,1)S(1)} %get-tuple-element.50.refs_7_), channel_id=1, source_target_pairs={{0,2},{2,0},{4,6},{6,4},{8,10},{10,8},{12,14},{14,12},{16,18},{18,... | collective-permute-start | bytes 294920 | tf_op jit(solution)/shard_map/ppermute | solution.py:387
  30.3 2.0 %collective-permute-start.12 = (bf16[384,128]{1,0:T(8,128)(2,1)S(1)}, bf16[384,128]{1,0:T(8,128)(2,1)S(1)}, u32[]{:S(2)}, u32[]{:S(2)}) collective-permute-start(bf16[384,128]{1,0:T(8,128)(2,1)S(1)} %get-tuple-element.50.refs_7_), channel_id=1, source_target_pairs={{0,6},{2,4},{4,2},{6,0},{8,14},{10,12},{12,10},{14,8},{16,22},{18,... | collective-permute-start | bytes 294920 | tf_op jit(solution)/shard_map/ppermute | solution.py:387
  32.7 0.7 %collective-permute-done.10.refs_6_ = bf16[384,128]{1,0:T(8,128)(2,1)S(1)} collective-permute-done((bf16[384,128]{1,0:T(8,128)(2,1)S(1)}, bf16[384,128]{1,0:T(8,128)(2,1)S(1)}, u32[]{:S(2)}, u32[]{:S(2)}) %collective-permute-start.10) | collective-permute-done | bytes 98336 | tf_op jit(solution)/shard_map/ppermute | solution.py:387
  33.5 1.4 %collective-permute-done.11.refs_7_.refs_5_ = bf16[384,128]{1,0:T(8,128)(2,1)S(1)} collective-permute-done((bf16[384,128]{1,0:T(8,128)(2,1)S(1)}, bf16[384,128]{1,0:T(8,128)(2,1)S(1)}, u32[]{:S(2)}, u32[]{:S(2)}) %collective-permute-start.11) | collective-permute-done | bytes 98336 | tf_op jit(solution)/shard_map/ppermute | solution.py:387
  34.8 1.2 %collective-permute-done.12.refs_8_.refs_4_ = bf16[384,128]{1,0:T(8,128)(2,1)S(1)} collective-permute-done((bf16[384,128]{1,0:T(8,128)(2,1)S(1)}, bf16[384,128]{1,0:T(8,128)(2,1)S(1)}, u32[]{:S(2)}, u32[]{:S(2)}) %collective-permute-start.12) | collective-permute-done | bytes 98336 | tf_op jit(solution)/shard_map/ppermute | solution.py:387
  36.5 2.3 %collective-permute-start.13 = (bf16[512,128]{1,0:T(8,128)(2,1)S(1)}, bf16[512,128]{1,0:T(8,128)(2,1)S(1)}, u32[]{:S(2)}, u32[]{:S(2)}) collective-permute-start(bf16[512,128]{1,0:T(8,128)(2,1)S(1)} %get-tuple-element.51), channel_id=1, source_target_pairs={{0,6},{2,4},{4,2},{6,0},{8,14},{10,12},{12,10},{14,8},{16,22},{18,... | collective-permute-start | bytes 393224 | tf_op jit(solution)/shard_map/ppermute | solution.py:387
  38.8 1.1 %collective-permute-start.14 = (bf16[512,128]{1,0:T(8,128)(2,1)S(1)}, bf16[512,128]{1,0:T(8,128)(2,1)S(1)}, u32[]{:S(2)}, u32[]{:S(2)}) collective-permute-start(bf16[512,128]{1,0:T(8,128)(2,1)S(1)} %get-tuple-element.52), channel_id=1, source_target_pairs={{0,4},{2,6},{4,0},{6,2},{8,12},{10,14},{12,8},{14,10},{16,20},{18,... | collective-permute-start | bytes 393224 | tf_op jit(solution)/shard_map/ppermute | solution.py:387
  39.9 0.8 %collective-permute-start.15 = (bf16[512,128]{1,0:T(8,128)(2,1)S(1)}, bf16[512,128]{1,0:T(8,128)(2,1)S(1)}, u32[]{:S(2)}, u32[]{:S(2)}) collective-permute-start(bf16[512,128]{1,0:T(8,128)(2,1)S(1)} %get-tuple-element.53), channel_id=1, source_target_pairs={{0,2},{2,0},{4,6},{6,4},{8,10},{10,8},{12,14},{14,12},{16,18},{18,... | collective-permute-start | bytes 393224 | tf_op jit(solution)/shard_map/ppermute | solution.py:387
  40.7 4.6 %shard_map.115 = (bf16[8,128,128]{2,1,0:T(8,128)(2,1)S(1)}, f32[8,128,128]{2,1,0:T(8,128)S(1)}, f32[8,128,1]{2,1,0:T(8,128)S(1)}, f32[8,128,1]{2,1,0:T(8,128)S(1)}) custom-call(bf16[128,2048]{1,0:T(8,128)(2,1)S(1)} %get-tuple-element.55.rows_ref, bf16[2048,1024]{1,0:T(8,128)(2,1)} %weight_hbm.1, f32[1,128]{1,0:T(1,128)S(1)} %get-tuple-element.56.gain_ref, ...), custom_call_target="tpu_custom_call" | custom-call | flops 1073741824 | bytes 16777216 | tf_op jit(solution)/shard_map/pallas_call | solution.py:21
  45.3 4.3 %shard_map.116 = (bf16[64,2048]{1,0:T(8,128)(2,1)S(1)}, bf16[64,2048]{1,0:T(8,128)(2,1)S(1)}) custom-call(s32[1]{0:T(128)} %bitcast.place_ref, s32[1]{0:T(128)} %bitcast.1.core_ref, s32[1]{0:T(128)} %get-tuple-element.44.table_ref, bf16[512,128]{1,0:T(8,128)(2,1)S(1)} %collective-permute-done.13.refs_0_, ...), custom_call_target="tpu_custom_call" | custom-call | flops 536870912 | bytes 4000000 | tf_op jit(solution)/shard_map/pallas_call | solution.py:21
  49.7 1.5 %collective-permute-done.16 = bf16[64,2048]{1,0:T(8,128)(2,1)S(1)} collective-permute-done((bf16[64,2048]{1,0:T(8,128)(2,1)S(1)}, bf16[64,2048]{1,0:T(8,128)(2,1)S(1)}, u32[]{:S(2)}, u32[]{:S(2)}) %collective-permute-start.16) | collective-permute-done | bytes 262176 | tf_op jit(solution)/shard_map/ppermute | solution.py:534
  51.2 0.8 %add.3 = bf16[64,2048]{1,0:T(8,128)(2,1)} add(bf16[64,2048]{1,0:T(8,128)(2,1)S(1)} %get-tuple-element.65, bf16[64,2048]{1,0:T(8,128)(2,1)S(1)} %collective-permute-done.16) | non-fusion elementwise | flops 131072 | bytes 786432 | tf_op jit(solution)/shard_map/add | solution.py:534
  (23 shorter events, 3.1 us)
Async XLA Ops:
  0.0 27.4 %copy-start.1 = (s32[1,16]{1,0:T(1,128)S(1)}, s32[1,16]{1,0:T(1,128)}, u32[]{:S(2)}) copy-start(s32[1,16]{1,0:T(1,128)} %param.21) | copy-start | bytes 196
  0.0 2.6 %collective-permute-start = (bf16[64,2048]{1,0:T(8,128)(2,1)}, bf16[64,2048]{1,0:T(8,128)(2,1)S(1)}, u32[]{:S(2)}, u32[]{:S(2)}) collective-permute-start(bf16[64,2048]{1,0:T(8,128)(2,1)} %mine_hbm.1), channel_id=1, source_target_pairs={{0,1},{1,0},{2,3},{3,2},{4,5},{5,4},{6,7},{7,6},{8,9},{9,8},{10,11... | collective-permute-start | bytes 786440 | tf_op jit(solution)/shard_map/ppermute | solution.py:373
  5.1 7.0 %collective-permute-start.1 = (bf16[384,128]{1,0:T(8,128)(2,1)S(1)}, bf16[384,128]{1,0:T(8,128)(2,1)S(1)}, u32[]{:S(2)}, u32[]{:S(2)}) collective-permute-start(bf16[384,128]{1,0:T(8,128)(2,1)S(1)} %get-tuple-element.41.refs_3_.refs_11_), channel_id=1, source_target_pairs={{0,6},{2,4},{4,2},{6,0},{8,14},{10,12},{12,10},{14,8},{16,22},{18,... | collective-permute-start | bytes 294920 | tf_op jit(solution)/shard_map/ppermute | solution.py:387
  8.6 5.6 %collective-permute-start.2 = (bf16[384,128]{1,0:T(8,128)(2,1)S(1)}, bf16[384,128]{1,0:T(8,128)(2,1)S(1)}, u32[]{:S(2)}, u32[]{:S(2)}) collective-permute-start(bf16[384,128]{1,0:T(8,128)(2,1)S(1)} %get-tuple-element.41.refs_3_.refs_11_), channel_id=1, source_target_pairs={{0,4},{2,6},{4,0},{6,2},{8,12},{10,14},{12,8},{14,10},{16,20},{18,... | collective-permute-start | bytes 294920 | tf_op jit(solution)/shard_map/ppermute | solution.py:387
  9.1 5.3 %collective-permute-start.3 = (bf16[384,128]{1,0:T(8,128)(2,1)S(1)}, bf16[384,128]{1,0:T(8,128)(2,1)S(1)}, u32[]{:S(2)}, u32[]{:S(2)}) collective-permute-start(bf16[384,128]{1,0:T(8,128)(2,1)S(1)} %get-tuple-element.41.refs_3_.refs_11_), channel_id=1, source_target_pairs={{0,2},{2,0},{4,6},{6,4},{8,10},{10,8},{12,14},{14,12},{16,18},{18,... | collective-permute-start | bytes 294920 | tf_op jit(solution)/shard_map/ppermute | solution.py:387
  9.3 36.0 %copy-start = (bf16[1024,2048]{1,0:T(8,128)(2,1)S(1)}, bf16[1024,2048]{1,0:T(8,128)(2,1)}, u32[]{:S(2)}) copy-start(bf16[1024,2048]{1,0:T(8,128)(2,1)} %refs_16_.1) | copy-start | bytes 12582916
  15.0 15.3 %collective-permute-start.7 = (bf16[384,128]{1,0:T(8,128)(2,1)S(1)}, bf16[384,128]{1,0:T(8,128)(2,1)S(1)}, u32[]{:S(2)}, u32[]{:S(2)}) collective-permute-start(bf16[384,128]{1,0:T(8,128)(2,1)S(1)} %get-tuple-element.45.refs_3_), channel_id=1, source_target_pairs={{0,24},{2,26},{4,28},{6,30},{8,16},{10,18},{12,20},{14,22},{16,8},... | collective-permute-start | bytes 294920 | tf_op jit(solution)/shard_map/ppermute | solution.py:387
  18.6 5.8 %collective-permute-start.4 = (bf16[128,128]{1,0:T(8,128)(2,1)S(1)}, bf16[128,128]{1,0:T(8,128)(2,1)S(1)}, u32[]{:S(2)}, u32[]{:S(2)}) collective-permute-start(bf16[128,128]{1,0:T(8,128)(2,1)S(1)} %get-tuple-element.43.val_ref), channel_id=1, source_target_pairs={{0,24},{2,26},{4,28},{6,30},{8,16},{10,18},{12,20},{14,22},{16,8},... | collective-permute-start | bytes 98312 | tf_op jit(solution)/shard_map/ppermute | solution.py:387
  18.9 8.6 %collective-permute-start.5 = (bf16[128,128]{1,0:T(8,128)(2,1)S(1)}, bf16[128,128]{1,0:T(8,128)(2,1)S(1)}, u32[]{:S(2)}, u32[]{:S(2)}) collective-permute-start(bf16[128,128]{1,0:T(8,128)(2,1)S(1)} %get-tuple-element.43.val_ref), channel_id=1, source_target_pairs={{0,16},{2,18},{4,20},{6,22},{8,24},{10,26},{12,28},{14,30},{16,0},... | collective-permute-start | bytes 98312 | tf_op jit(solution)/shard_map/ppermute | solution.py:387
  19.6 7.8 %collective-permute-start.6 = (bf16[128,128]{1,0:T(8,128)(2,1)S(1)}, bf16[128,128]{1,0:T(8,128)(2,1)S(1)}, u32[]{:S(2)}, u32[]{:S(2)}) collective-permute-start(bf16[128,128]{1,0:T(8,128)(2,1)S(1)} %get-tuple-element.43.val_ref), channel_id=1, source_target_pairs={{0,8},{2,10},{4,12},{6,14},{8,0},{10,2},{12,4},{14,6},{16,24},{18,... | collective-permute-start | bytes 98312 | tf_op jit(solution)/shard_map/ppermute | solution.py:387
  23.0 9.3 %collective-permute-start.8 = (bf16[384,128]{1,0:T(8,128)(2,1)S(1)}, bf16[384,128]{1,0:T(8,128)(2,1)S(1)}, u32[]{:S(2)}, u32[]{:S(2)}) collective-permute-start(bf16[384,128]{1,0:T(8,128)(2,1)S(1)} %get-tuple-element.45.refs_3_), channel_id=1, source_target_pairs={{0,16},{2,18},{4,20},{6,22},{8,24},{10,26},{12,28},{14,30},{16,0},... | collective-permute-start | bytes 294920 | tf_op jit(solution)/shard_map/ppermute | solution.py:387
  24.4 7.9 %collective-permute-start.9 = (bf16[384,128]{1,0:T(8,128)(2,1)S(1)}, bf16[384,128]{1,0:T(8,128)(2,1)S(1)}, u32[]{:S(2)}, u32[]{:S(2)}) collective-permute-start(bf16[384,128]{1,0:T(8,128)(2,1)S(1)} %get-tuple-element.45.refs_3_), channel_id=1, source_target_pairs={{0,8},{2,10},{4,12},{6,14},{8,0},{10,2},{12,4},{14,6},{16,24},{18,... | collective-permute-start | bytes 294920 | tf_op jit(solution)/shard_map/ppermute | solution.py:387
  28.8 4.7 %collective-permute-start.10 = (bf16[384,128]{1,0:T(8,128)(2,1)S(1)}, bf16[384,128]{1,0:T(8,128)(2,1)S(1)}, u32[]{:S(2)}, u32[]{:S(2)}) collective-permute-start(bf16[384,128]{1,0:T(8,128)(2,1)S(1)} %get-tuple-element.50.refs_7_), channel_id=1, source_target_pairs={{0,2},{2,0},{4,6},{6,4},{8,10},{10,8},{12,14},{14,12},{16,18},{18,... | collective-permute-start | bytes 294920 | tf_op jit(solution)/shard_map/ppermute | solution.py:387
  30.2 4.6 %collective-permute-start.11 = (bf16[384,128]{1,0:T(8,128)(2,1)S(1)}, bf16[384,128]{1,0:T(8,128)(2,1)S(1)}, u32[]{:S(2)}, u32[]{:S(2)}) collective-permute-start(bf16[384,128]{1,0:T(8,128)(2,1)S(1)} %get-tuple-element.50.refs_7_), channel_id=1, source_target_pairs={{0,4},{2,6},{4,0},{6,2},{8,12},{10,14},{12,8},{14,10},{16,20},{18,... | collective-permute-start | bytes 294920 | tf_op jit(solution)/shard_map/ppermute | solution.py:387
  30.3 5.7 %collective-permute-start.12 = (bf16[384,128]{1,0:T(8,128)(2,1)S(1)}, bf16[384,128]{1,0:T(8,128)(2,1)S(1)}, u32[]{:S(2)}, u32[]{:S(2)}) collective-permute-start(bf16[384,128]{1,0:T(8,128)(2,1)S(1)} %get-tuple-element.50.refs_7_), channel_id=1, source_target_pairs={{0,6},{2,4},{4,2},{6,0},{8,14},{10,12},{12,10},{14,8},{16,22},{18,... | collective-permute-start | bytes 294920 | tf_op jit(solution)/shard_map/ppermute | solution.py:387
  36.5 8.8 %collective-permute-start.13 = (bf16[512,128]{1,0:T(8,128)(2,1)S(1)}, bf16[512,128]{1,0:T(8,128)(2,1)S(1)}, u32[]{:S(2)}, u32[]{:S(2)}) collective-permute-start(bf16[512,128]{1,0:T(8,128)(2,1)S(1)} %get-tuple-element.51), channel_id=1, source_target_pairs={{0,6},{2,4},{4,2},{6,0},{8,14},{10,12},{12,10},{14,8},{16,22},{18,... | collective-permute-start | bytes 393224 | tf_op jit(solution)/shard_map/ppermute | solution.py:387
  38.8 6.5 %collective-permute-start.14 = (bf16[512,128]{1,0:T(8,128)(2,1)S(1)}, bf16[512,128]{1,0:T(8,128)(2,1)S(1)}, u32[]{:S(2)}, u32[]{:S(2)}) collective-permute-start(bf16[512,128]{1,0:T(8,128)(2,1)S(1)} %get-tuple-element.52), channel_id=1, source_target_pairs={{0,4},{2,6},{4,0},{6,2},{8,12},{10,14},{12,8},{14,10},{16,20},{18,... | collective-permute-start | bytes 393224 | tf_op jit(solution)/shard_map/ppermute | solution.py:387
  39.9 5.4 %collective-permute-start.15 = (bf16[512,128]{1,0:T(8,128)(2,1)S(1)}, bf16[512,128]{1,0:T(8,128)(2,1)S(1)}, u32[]{:S(2)}, u32[]{:S(2)}) collective-permute-start(bf16[512,128]{1,0:T(8,128)(2,1)S(1)} %get-tuple-element.53), channel_id=1, source_target_pairs={{0,2},{2,0},{4,6},{6,4},{8,10},{10,8},{12,14},{14,12},{16,18},{18,... | collective-permute-start | bytes 393224 | tf_op jit(solution)/shard_map/ppermute | solution.py:387
  49.6 1.6 %collective-permute-start.16 = (bf16[64,2048]{1,0:T(8,128)(2,1)S(1)}, bf16[64,2048]{1,0:T(8,128)(2,1)S(1)}, u32[]{:S(2)}, u32[]{:S(2)}) collective-permute-start(bf16[64,2048]{1,0:T(8,128)(2,1)S(1)} %get-tuple-element.66), channel_id=1, source_target_pairs={{0,1},{1,0},{2,3},{3,2},{4,5},{5,4},{6,7},{7,6},{8,9},{9,8},{10,11... | collective-permute-start | bytes 786440 | tf_op jit(solution)/shard_map/ppermute | solution.py:534

commit v12 on v9

--- a/solution.py
+++ b/solution.py
@@ -39,10 +39,6 @@
 
 def in_hbm(array):
     return pltpu.with_memory_space_constraint(array, pltpu.HBM)
-
-
-def step_between(member, source, group):
-    return member ^ source if group & (group - 1) == 0 else (member + group - source) % group
 
 
 def shaped(shape, dtype):
@@ -113,7 +109,7 @@
     rows_ref[pl.ds(pl.multiple_of(core * half, half), half), :] = mine_ref[...]
     rows_ref[pl.ds(pl.multiple_of((1 - core) * half, half), half), :] = other_ref[...]
     seg = rows_ref[...]
-    size = turn_ref.shape[1]
+    size = turn_ref.shape[0]
     raw = jnp.dot(seg, weight_ref[...], preferred_element_type=F32)
     keys, raw, vals = raw[:, :size], raw[:, size : 2 * size], raw[:, 2 * size :]
     kn = keys * lax.rsqrt(jnp.mean(keys * keys, axis=-1, keepdims=True) + EPSILON) * gain_ref[...]
@@ -137,10 +133,7 @@
     crossed = dot3(both, dirs, 0, 0)
     exit_ref[...] = kn - crossed[:tokens]
     heads, lanes = iota2((size, size))
-    high, low = split(jnp.where(heads == lanes, 1.0, 0.0) - crossed[tokens:])
-    turn_ref[:size] = high
-    turn_ref[size : 2 * size] = low
-    turn_ref[2 * size :] = vals.astype(BF16)
+    turn_ref[...] = jnp.where(heads == lanes, 1.0, 0.0) - crossed[tokens:]
 
 
 def leave_kernel(group, place_ref, exit_ref, *refs):
@@ -149,10 +142,7 @@
     member = place_ref[0] % group
     tokens, size = exit_ref.shape
     for step in range(group):
-        ref = turn_refs[group - 1 - step]
-        turns_ref[source_of(member, step, group)] = ref[:size].astype(F32) + ref[
-            size : 2 * size
-        ].astype(F32)
+        turns_ref[source_of(member, step, group)] = turn_refs[group - 1 - step][...]
     own = exit_ref[...]
     keys = own
     product = None
@@ -169,7 +159,9 @@
     high, low = split(keys)
     leave_ref[:tokens] = high
     leave_ref[tokens : 2 * tokens] = low
-    leave_ref[2 * tokens :] = product.astype(BF16)
+    high, low = split(product)
+    leave_ref[2 * tokens : 2 * tokens + size] = high
+    leave_ref[2 * tokens + size :] = low
     for step in range(group):
         near_refs[step][...] = seen_ref[target_of(member, step, group)]
 
@@ -181,8 +173,9 @@
 
 
 def bundle_kernel(group, groups, most, place_ref, mask_ref, after_ref, *refs):
-    val_refs, (line_ref, table_ref) = refs[: groups - 1], refs[groups - 1 :]
+    val_refs, (line_ref, table_ref) = refs[:groups], refs[groups:]
     place = place_ref[0]
+    mine = place // group
     segments = mask_ref.shape[0]
     for word in range(table_ref.shape[0]):
         table_ref[word] = 0
@@ -199,22 +192,41 @@
 
     lax.fori_loop(0, segments, pick, jnp.int32(0))
     tokens = val_refs[0].shape[0]
-    for way in range(1, groups):
-        line_ref[(way - 1) * tokens : way * tokens] = val_refs[groups - 1 - way][...]
-
-
-def query_kernel(rows_ref, weight_ref, gain_ref, kn_ref, dirs_ref, coeff_ref, solved_ref, val_ref,
-                 moved_ref, weighted_ref, peak_ref, total_ref):
+    for way in range(groups):
+        at = pl.multiple_of(source_of(mine, way, groups) * tokens, tokens)
+        line_ref[pl.ds(at, tokens), :] = val_refs[groups - 1 - way][...]
+
+
+def query_kernel(rows_ref, weight_hbm, gain_ref, kn_ref, dirs_ref, coeff_ref, solved_ref, val_ref,
+                 moved_ref, weighted_ref, peak_ref, total_ref, weight_ref, raw_ref, sems):
     tokens, size = kn_ref.shape
     heads = moved_ref.shape[0]
+    pieces, deep, _ = weight_ref.shape
+    copies = [
+        pltpu.make_async_copy(
+            weight_hbm.at[n * deep : (n + 1) * deep, :], weight_ref.at[n], sems.at[n]
+        )
+        for n in range(pieces)
+    ]
+    for copy in copies:
+        copy.start()
     across = jnp.concatenate([kn_ref[...], dirs_ref[...]], axis=0)
     into = jnp.concatenate([coeff_ref[...], solved_ref[...]], axis=1)
+    for n in range(pieces):
+        copies[n].wait()
+        part = jnp.dot(
+            rows_ref[:, n * deep : (n + 1) * deep], weight_ref[n], preferred_element_type=F32
+        )
+        raw_ref[...] = raw_ref[...] + part if n else part
     count = math.gcd(heads, 4)
     for turn in range(heads // count):
-        wide = slice(turn * count * size, (turn + 1) * count * size)
-        raw = jnp.dot(rows_ref[...], weight_ref[:, wide], preferred_element_type=F32)
-        parts = [raw[:, at : at + size] for at in range(0, count * size, size)]
-        raw = jnp.concatenate(parts, axis=0)
+        raw = jnp.concatenate(
+            [
+                raw_ref[:, head * size : (head + 1) * size]
+                for head in range(turn * count, (turn + 1) * count)
+            ],
+            axis=0,
+        )
         queries = (
             raw * lax.rsqrt(jnp.mean(raw * raw, axis=-1, keepdims=True) + EPSILON) * gain_ref[...]
         )
@@ -248,7 +260,8 @@
         index = source_of(mine, step, groups)
         ref = arrived[groups - 1 - step]
         keys_ref[index] = ref[:tokens].astype(F32) + ref[tokens : 2 * tokens].astype(F32)
-        whole_ref[index] = ref[2 * tokens :].astype(F32)
+        whole = ref[2 * tokens : 2 * tokens + size].astype(F32)
+        whole_ref[index] = whole + ref[2 * tokens + size :].astype(F32)
     brought = [keys_ref[groups - 2]]
     product = None
     for index in range(groups - 3, -1, -1):
@@ -266,9 +279,8 @@
 
 def attend_kernel(group, segments, most, place_ref, core_ref, table_ref, *refs):
     far_refs, line_refs = refs[:group][::-1], refs[group : 2 * group][::-1]
-    turn_refs = refs[2 * group : 3 * group][::-1]
     (moved_ref, weighted_ref, peak_ref, total_ref, out_ref, away_ref, kept_ref, keys_ref, vals_ref,
-     attended_ref) = refs[3 * group :]
+     attended_ref) = refs[2 * group :]
     core = core_ref[0]
     mine, member = place_ref[0] // group, place_ref[0] % group
     heads, tokens, size = moved_ref.shape
@@ -288,17 +300,12 @@
             whose, source = segment % group, segment // group
             before = jnp.where(source < mine, source, groups - 1)
             before = pl.multiple_of(before * tokens, tokens)
-            after = jnp.maximum(step_between(mine, source, groups) - 1, 0)
-            after = pl.multiple_of(after * tokens, tokens)
+            after = pl.multiple_of(source * tokens, tokens)
             for number in range(group):
 
                 @pl.when(whose == source_of(member, number, group))
                 def _():
-                    vals_ref[part, :] = jnp.where(
-                        source < mine,
-                        line_refs[number][pl.ds(after, tokens), :],
-                        turn_refs[number][2 * size :],
-                    )
+                    vals_ref[part, :] = line_refs[number][pl.ds(after, tokens), :]
                     keys_ref[part, :] = far_refs[number][pl.ds(before, tokens), :]
 
         return jnp.where(lanes < found * tokens, 0.0, NEGATIVE)
@@ -402,7 +409,7 @@
         prepare_kernel,
         (
             shaped((tokens, width), BF16), square, shaped((tokens, size), BF16), square, square,
-            square, square, shaped((2 * size + tokens, size), BF16),
+            square, square, shaped((size, size), F32),
         ),
         (core, mine, other, weights, rate_row, rate_bias, key_gain),
         in_specs=[smem] + [vmem] * 4 + [smem, vmem],
@@ -414,7 +421,7 @@
     leaving, starts, *near = call(
         functools.partial(leave_kernel, group),
         [
-            shaped((2 * tokens + size, size), BF16),
+            shaped((2 * tokens + 2 * size, size), BF16),
             shaped((group, size, size), F32),
         ]
         + [shaped((tokens, size), BF16)] * group,
@@ -432,11 +439,11 @@
     values, table = call(
         functools.partial(bundle_kernel, group, groups, most),
         [
-            shaped(((groups - 1) * tokens, size), BF16),
+            shaped((groups * tokens, size), BF16),
             shaped((word_of(most - 1, segments)[0] + 1,), jnp.int32),
         ],
-        (place, block_mask[0], starts, *line[:0:-1]),
-        in_specs=[smem, smem, anywhere] + [vmem] * (groups - 1),
+        (place, block_mask[0], starts, *line[::-1]),
+        in_specs=[smem, smem, anywhere] + [vmem] * groups,
         out_specs=[vmem, smem],
         moved=10**6,
         limit=8 + group * groups // 4,
@@ -450,25 +457,17 @@
             shaped((heads, tokens, 1), F32),
             shaped((heads, tokens, 1), F32),
         ),
-        (rows, w_query, query_gain, kn, dirs, coeff, solved, val),
+        (rows, in_hbm(w_query), query_gain, kn, dirs, coeff, solved, val),
+        in_specs=[vmem, hbm] + [vmem] * 6,
+        scratch=(
+            pltpu.VMEM((2, width // 2, w_query.shape[1]), BF16),
+            pltpu.VMEM((tokens, w_query.shape[1]), F32),
+            pltpu.SemaphoreType.DMA((2,)),
+        ),
         flops=4 * tokens * width * heads * size,
         moved=8 * width * heads * size,
-        limit=14,
-    )
-    most = segments // 4
-    values, table = call(
-        functools.partial(bundle_kernel, group, groups, most),
-        [
-            shaped(((groups - 1) * tokens, size), BF16),
-            shaped((word_of(most - 1, segments)[0] + 1,), jnp.int32),
-        ],
-        (place, block_mask[0], starts, *line[:0:-1]),
-        in_specs=[smem, smem, anywhere] + [vmem] * (groups - 1),
-        out_specs=[vmem, smem],
-        moved=10**6,
-        limit=8 + group * groups // 4,
-    )
-    values = within_group([values] * group)
+        limit=16,
+    )
     far = call(
         functools.partial(arrive_kernel, groups, group, tokens),
         [shaped((groups * tokens, size), BF16)] * group,
@@ -485,17 +484,16 @@
     far = within_group(far)
     chunk = math.gcd(most, 4)
     width_out = w_out.shape[1]
-    scratch = [
-        pltpu.VMEM((chunk * tokens, size), BF16),
-        pltpu.VMEM((chunk * tokens, size), BF16),
-        pltpu.VMEM((tokens, heads * size), BF16),
-    ]
     away, kept = call(
         functools.partial(attend_kernel, group, segments, most),
         [shaped((half, width_out), BF16)] * 2,
-        (place, core, table, *far[::-1], *values[::-1], *turns[::-1], *own, w_out),
-        in_specs=[smem] * 3 + [vmem] * (3 * group + 5),
-        scratch=scratch,
+        (place, core, table, *far[::-1], *values[::-1], *own, w_out),
+        in_specs=[smem] * 3 + [vmem] * (2 * group + 5),
+        scratch=[
+            pltpu.VMEM((chunk * tokens, size), BF16),
+            pltpu.VMEM((chunk * tokens, size), BF16),
+            pltpu.VMEM((tokens, heads * size), BF16),
+        ],
         flops=2 * tokens * width_out * heads * size,
         moved=4 * 10**6,
         limit=14 + group * groups // 4,

time: 50.2 us -> 45.1 us (0.90)
  starting transfers between devices: 24.4 us -> 20.9 us
  local copies, waits for them, and re-layouts: 2.19 us -> 0.01 us
  Pallas kernels: 13.5 us -> 14.9 us
  waiting for transfers between devices: 8.38 us -> 7.59 us
    ppermute x15, starting transfers between devices: 23.9 us -> 20.4 us  [swapped(): out[step] = lax.ppermute(values[step], 'ctx', pairs_of(step))]
    unnamed x6 -> x4, local copies, waits for them, and re-layouts: 2.19 us -> 0.01 us
    pallas_call x7, Pallas kernels: 13.5 us -> 14.9 us  [call(): pl.pallas_call(kernel, out_shape=out_shape, in_specs=in_specs or [vmem] *...]
    ppermute x15, waiting for transfers between devices: 6.86 us -> 6.07 us  [swapped(): out[step] = lax.ppermute(values[step], 'ctx', pairs_of(step))]
  transfers between devices with their start and end apart: 17 -> 17, of which waited for: 6 -> 4; matrix products, arithmetic and copies ran while one was open for 0% -> 0% of each run, Pallas kernels for 13% -> 18%
where the time goes in v12:
time: 45.1 us; the launch traced here: 44.9 us
  starting transfers between devices  20.9 us (46%)
  Pallas kernels  14.9 us (33%)
  waiting for transfers between devices  7.59 us (17%)
  other arithmetic  0.77 us (2%)
  between operations  0.77 us (2%)
    ppermute x15, starting transfers between devices, swapped(): out[step] = lax.ppermute(values[step], 'ctx', pairs_of(step))  20.4 us
    pallas_call x7, Pallas kernels, call(): pl.pallas_call(kernel, out_shape=out_shape, in_specs=in_specs or [vmem] *...  14.9 us
    ppermute x15, waiting for transfers between devices, swapped(): out[step] = lax.ppermute(values[step], 'ctx', pairs_of(step))  6.07 us
    ppermute x1, waiting for transfers between devices, body(): return kept + lax.ppermute(away, 'head', [(0, 1), (1, 0)])  1.52 us
  transfers between devices with their start and end apart: 17, of which 4 were waited for; matrix products, arithmetic and copies ran while one was open for 0% of the time, Pallas kernels for 18%

profile of v12, /device:TPU:0, one launch (start us, length us, event | category | flops | bytes accessed | tf_op | source)
XLA Modules:
  0.0 44.9 jit_solution(6956315140386927667)
XLA Ops:
  0.0 0.5 %collective-permute-start = (bf16[64,2048]{1,0:T(8,128)(2,1)}, bf16[64,2048]{1,0:T(8,128)(2,1)S(1)}, u32[]{:S(2)}, u32[]{:S(2)}) collective-permute-start(bf16[64,2048]{1,0:T(8,128)(2,1)} %mine_hbm.1), channel_id=1, source_target_pairs={{0,1},{1,0},{2,3},{3,2},{4,5},{5,4},{6,7},{7,6},{8,9},{9,8},{10,11... | collective-permute-start | bytes 786440 | tf_op jit(solution)/shard_map/ppermute | solution.py:364
  1.1 1.5 %shard_map.109 = (bf16[2048,384]{1,0:T(8,128)(2,1)S(1)}, bf16[1,2048]{1,0:T(2,128)(2,1)S(1)}, f32[1,128]{1,0:T(1,128)S(1)}, f32[1,128]{1,0:T(1,128)S(1)}, bf16[64,2048]{1,0:T(8,128)(2,1)S(1)}) custom-call(bf16[2048,128]{1,0:T(8,128)(2,1)} %key_hbm.1, bf16[2048,128]{1,0:T(8,128)(2,1)} %dir_hbm.1, bf16[2048,128]{1,0:T(8,128)(2,1)} %value_hbm.1, ...), custom_call_target="tpu_custom_call" | custom-call | bytes 3145728 | tf_op jit(solution)/shard_map/pallas_call | solution.py:21
  2.7 2.4 %shard_map.110 = (bf16[128,2048]{1,0:T(8,128)(2,1)S(1)}, f32[128,128]{1,0:T(8,128)S(1)}, bf16[128,128]{1,0:T(8,128)(2,1)S(1)}, f32[128,128]{1,0:T(8,128)S(1)}, f...) custom-call(s32[1]{0:T(128)} %bitcast.1.core_ref, ...), custom_call_target="tpu_custom_call" | custom-call | flops 201326592 | bytes 2097152 | tf_op jit(solution)/shard_map/pallas_call | solution.py:21
  5.1 3.5 %collective-permute-start.1 = (f32[128,128]{1,0:T(8,128)S(1)}, f32[128,128]{1,0:T(8,128)S(1)}, u32[]{:S(2)}, u32[]{:S(2)}) collective-permute-start(f32[128,128]{1,0:T(8,128)S(1)} %get-tuple-element.41.refs_3_), channel_id=1, source_target_pairs={{0,6},{2,4},{4,2},{6,0},{8,14},{10,12},{12,10},{14,8},{16,22},{18,... | collective-permute-start | bytes 196616 | tf_op jit(solution)/shard_map/ppermute | solution.py:378
  8.6 0.5 %collective-permute-start.2 = (f32[128,128]{1,0:T(8,128)S(1)}, f32[128,128]{1,0:T(8,128)S(1)}, u32[]{:S(2)}, u32[]{:S(2)}) collective-permute-start(f32[128,128]{1,0:T(8,128)S(1)} %get-tuple-element.41.refs_3_), channel_id=1, source_target_pairs={{0,4},{2,6},{4,0},{6,2},{8,12},{10,14},{12,8},{14,10},{16,20},{18,... | collective-permute-start | bytes 196616 | tf_op jit(solution)/shard_map/ppermute | solution.py:378
  9.3 4.0 %collective-permute-start.4 = (bf16[128,128]{1,0:T(8,128)(2,1)S(1)}, bf16[128,128]{1,0:T(8,128)(2,1)S(1)}, u32[]{:S(2)}, u32[]{:S(2)}) collective-permute-start(bf16[128,128]{1,0:T(8,128)(2,1)S(1)} %get-tuple-element.43.refs_3_.val_ref), channel_id=1, source_target_pairs={{0,24},{2,26},{4,28},{6,30},{8,16},{10,18},{12,20},{14,22},{16,8},... | collective-permute-start | bytes 98312 | tf_op jit(solution)/shard_map/ppermute | solution.py:378
  13.3 0.6 %collective-permute-start.6 = (bf16[128,128]{1,0:T(8,128)(2,1)S(1)}, bf16[128,128]{1,0:T(8,128)(2,1)S(1)}, u32[]{:S(2)}, u32[]{:S(2)}) collective-permute-start(bf16[128,128]{1,0:T(8,128)(2,1)S(1)} %get-tuple-element.43.refs_3_.val_ref), channel_id=1, source_target_pairs={{0,8},{2,10},{4,12},{6,14},{8,0},{10,2},{12,4},{14,6},{16,24},{18,... | collective-permute-start | bytes 98312 | tf_op jit(solution)/shard_map/ppermute | solution.py:378
  13.9 0.5 %shard_map.111 = (bf16[512,128]{1,0:T(8,128)(2,1)S(1)}, f32[4,128,128]{2,1,0:T(8,128)S(1)}, bf16[128,128]{1,0:T(8,128)(2,1)S(1)}, bf16[128,128]{1,0:T(8,128)(2,1...) custom-call(s32[1]{0:T(128)} %bitcast.place_ref, f32[128,128]{1,0:T(8,128)S(1)} %get-tuple-element.40.exit_ref, ...), custom_call_target="tpu_custom_call" | custom-call | flops 100663296 | bytes 1000000 | tf_op jit(solution)/shard_map/pallas_call | solution.py:21
  14.4 3.9 %collective-permute-start.7 = (bf16[512,128]{1,0:T(8,128)(2,1)S(1)}, bf16[512,128]{1,0:T(8,128)(2,1)S(1)}, u32[]{:S(2)}, u32[]{:S(2)}) collective-permute-start(bf16[512,128]{1,0:T(8,128)(2,1)S(1)} %get-tuple-element.45.refs_3_), channel_id=1, source_target_pairs={{0,24},{2,26},{4,28},{6,30},{8,16},{10,18},{12,20},{14,22},{16,8},... | collective-permute-start | bytes 393224 | tf_op jit(solution)/shard_map/ppermute | solution.py:378
  18.3 0.6 %collective-permute-start.9 = (bf16[512,128]{1,0:T(8,128)(2,1)S(1)}, bf16[512,128]{1,0:T(8,128)(2,1)S(1)}, u32[]{:S(2)}, u32[]{:S(2)}) collective-permute-start(bf16[512,128]{1,0:T(8,128)(2,1)S(1)} %get-tuple-element.45.refs_3_), channel_id=1, source_target_pairs={{0,8},{2,10},{4,12},{6,14},{8,0},{10,2},{12,4},{14,6},{16,24},{18,... | collective-permute-start | bytes 393224 | tf_op jit(solution)/shard_map/ppermute | solution.py:378
  18.9 3.5 %collective-permute-done.5.refs_1_ = bf16[128,128]{1,0:T(8,128)(2,1)S(1)} collective-permute-done((bf16[128,128]{1,0:T(8,128)(2,1)S(1)}, bf16[128,128]{1,0:T(8,128)(2,1)S(1)}, u32[]{:S(2)}, u32[]{:S(2)}) %collective-permute-start.5) | collective-permute-done | bytes 32800 | tf_op jit(solution)/shard_map/ppermute | solution.py:378
  22.5 1.3 %shard_map.112 = (bf16[512,128]{1,0:T(8,128)(2,1)S(1)}, s32[1]{0:T(128)}) custom-call(s32[1]{0:T(128)} %bitcast.place_ref, s32[16]{0:T(128)S(1)} %bitcast.5, f32[4,128,128]{2,1,0:T(8,128)S(1)} %get-tuple-element.42.after_ref.refs_4_, bf16[128,128]{1,0:T(8,128)(2,1)S(1)} %collective-permute-done.4.refs_0_, ...), custom_call_target="tpu_custom_call" | custom-call | bytes 1000000 | tf_op jit(solution)/shard_map/pallas_call | solution.py:21
  23.8 2.4 %collective-permute-start.13 = (bf16[512,128]{1,0:T(8,128)(2,1)S(1)}, bf16[512,128]{1,0:T(8,128)(2,1)S(1)}, u32[]{:S(2)}, u32[]{:S(2)}) collective-permute-start(bf16[512,128]{1,0:T(8,128)(2,1)S(1)} %get-tuple-element.54.refs_7_), channel_id=1, source_target_pairs={{0,6},{2,4},{4,2},{6,0},{8,14},{10,12},{12,10},{14,8},{16,22},{18,... | collective-permute-start | bytes 393224 | tf_op jit(solution)/shard_map/ppermute | solution.py:378
  26.2 1.2 %collective-permute-start.15 = (bf16[512,128]{1,0:T(8,128)(2,1)S(1)}, bf16[512,128]{1,0:T(8,128)(2,1)S(1)}, u32[]{:S(2)}, u32[]{:S(2)}) collective-permute-start(bf16[512,128]{1,0:T(8,128)(2,1)S(1)} %get-tuple-element.54.refs_7_), channel_id=1, source_target_pairs={{0,2},{2,0},{4,6},{6,4},{8,10},{10,8},{12,14},{14,12},{16,18},{18,... | collective-permute-start | bytes 393224 | tf_op jit(solution)/shard_map/ppermute | solution.py:378
  27.4 1.3 %collective-permute-done.8.refs_1_ = bf16[512,128]{1,0:T(8,128)(2,1)S(1)} collective-permute-done((bf16[512,128]{1,0:T(8,128)(2,1)S(1)}, bf16[512,128]{1,0:T(8,128)(2,1)S(1)}, u32[]{:S(2)}, u32[]{:S(2)}) %collective-permute-start.8) | collective-permute-done | bytes 131104 | tf_op jit(solution)/shard_map/ppermute | solution.py:378
  28.7 0.8 %shard_map.113 = (bf16[512,128]{1,0:T(8,128)(2,1)S(1)}, bf16[512,128]{1,0:T(8,128)(2,1)S(1)}, bf16[512,128]{1,0:T(8,128)(2,1)S(1)}, bf16[512,128]{1,0:T(8,128)(2,1)S(1)}) custom-call(s32[1]{0:T(128)} %bitcast.place_ref, bf16[512,128]{1,0:T(8,128)(2,1)S(1)} %collective-permute-done.7.refs_0_, bf16[512,128]{1,0:T(8,128)(2,1)S(1)} %collective-permute-done.8.refs_1_, ...), custom_call_target="tpu_custom_call" | custom-call | flops 201326592 | bytes 1000000 | tf_op jit(solution)/shard_map/pallas_call | solution.py:21
  29.5 2.5 %collective-permute-start.10 = (bf16[512,128]{1,0:T(8,128)(2,1)S(1)}, bf16[512,128]{1,0:T(8,128)(2,1)S(1)}, u32[]{:S(2)}, u32[]{:S(2)}) collective-permute-start(bf16[512,128]{1,0:T(8,128)(2,1)S(1)} %get-tuple-element.50), channel_id=1, source_target_pairs={{0,6},{2,4},{4,2},{6,0},{8,14},{10,12},{12,10},{14,8},{16,22},{18,... | collective-permute-start | bytes 393224 | tf_op jit(solution)/shard_map/ppermute | solution.py:378
  32.0 0.6 %collective-permute-start.11 = (bf16[512,128]{1,0:T(8,128)(2,1)S(1)}, bf16[512,128]{1,0:T(8,128)(2,1)S(1)}, u32[]{:S(2)}, u32[]{:S(2)}) collective-permute-start(bf16[512,128]{1,0:T(8,128)(2,1)S(1)} %get-tuple-element.51), channel_id=1, source_target_pairs={{0,4},{2,6},{4,0},{6,2},{8,12},{10,14},{12,8},{14,10},{16,20},{18,... | collective-permute-start | bytes 393224 | tf_op jit(solution)/shard_map/ppermute | solution.py:378
  32.7 0.4 collective-permute-start.12
  33.1 3.9 %shard_map.114 = (bf16[8,128,128]{2,1,0:T(8,128)(2,1)S(1)}, f32[8,128,128]{2,1,0:T(8,128)S(1)}, f32[8,128,1]{2,1,0:T(8,128)S(1)}, f32[8,128,1]{2,1,0:T(8,128)S(1)}) custom-call(bf16[128,2048]{1,0:T(8,128)(2,1)S(1)} %get-tuple-element.55.rows_ref, bf16[2048,1024]{1,0:T(8,128)(2,1)} %weight_hbm.1, f32[1,128]{1,0:T(1,128)S(1)} %get-tuple-element.56.gain_ref, ...), custom_call_target="tpu_custom_call" | custom-call | flops 1073741824 | bytes 16777216 | tf_op jit(solution)/shard_map/pallas_call | solution.py:21
  37.0 1.2 %collective-permute-done.11.refs_1_ = bf16[512,128]{1,0:T(8,128)(2,1)S(1)} collective-permute-done((bf16[512,128]{1,0:T(8,128)(2,1)S(1)}, bf16[512,128]{1,0:T(8,128)(2,1)S(1)}, u32[]{:S(2)}, u32[]{:S(2)}) %collective-permute-start.11) | collective-permute-done | bytes 131104 | tf_op jit(solution)/shard_map/ppermute | solution.py:378
  38.2 4.3 %shard_map.115 = (bf16[64,2048]{1,0:T(8,128)(2,1)S(1)}, bf16[64,2048]{1,0:T(8,128)(2,1)S(1)}) custom-call(s32[1]{0:T(128)} %bitcast.place_ref, s32[1]{0:T(128)} %bitcast.1.core_ref, s32[1]{0:T(128)} %get-tuple-element.44.table_ref, bf16[512,128]{1,0:T(8,128)(2,1)S(1)} %collective-permute-done.10.refs_0_, ...), custom_call_target="tpu_custom_call" | custom-call | flops 536870912 | bytes 4000000 | tf_op jit(solution)/shard_map/pallas_call | solution.py:21
  42.6 1.5 %collective-permute-done.16 = bf16[64,2048]{1,0:T(8,128)(2,1)S(1)} collective-permute-done((bf16[64,2048]{1,0:T(8,128)(2,1)S(1)}, bf16[64,2048]{1,0:T(8,128)(2,1)S(1)}, u32[]{:S(2)}, u32[]{:S(2)}) %collective-permute-start.16) | collective-permute-done | bytes 262176 | tf_op jit(solution)/shard_map/ppermute | solution.py:501
  44.1 0.8 %add.3 = bf16[64,2048]{1,0:T(8,128)(2,1)} add(bf16[64,2048]{1,0:T(8,128)(2,1)S(1)} %get-tuple-element.65, bf16[64,2048]{1,0:T(8,128)(2,1)S(1)} %collective-permute-done.16) | non-fusion elementwise | flops 131072 | bytes 786432 | tf_op jit(solution)/shard_map/add | solution.py:501
  (22 shorter events, 0.3 us)
Async XLA Ops:
  0.0 22.5 %copy-start.1 = (s32[1,16]{1,0:T(1,128)S(1)}, s32[1,16]{1,0:T(1,128)}, u32[]{:S(2)}) copy-start(s32[1,16]{1,0:T(1,128)} %param.21) | copy-start | bytes 196
  0.0 2.6 %collective-permute-start = (bf16[64,2048]{1,0:T(8,128)(2,1)}, bf16[64,2048]{1,0:T(8,128)(2,1)S(1)}, u32[]{:S(2)}, u32[]{:S(2)}) collective-permute-start(bf16[64,2048]{1,0:T(8,128)(2,1)} %mine_hbm.1), channel_id=1, source_target_pairs={{0,1},{1,0},{2,3},{3,2},{4,5},{5,4},{6,7},{7,6},{8,9},{9,8},{10,11... | collective-permute-start | bytes 786440 | tf_op jit(solution)/shard_map/ppermute | solution.py:364
  5.1 8.2 %collective-permute-start.1 = (f32[128,128]{1,0:T(8,128)S(1)}, f32[128,128]{1,0:T(8,128)S(1)}, u32[]{:S(2)}, u32[]{:S(2)}) collective-permute-start(f32[128,128]{1,0:T(8,128)S(1)} %get-tuple-element.41.refs_3_), channel_id=1, source_target_pairs={{0,6},{2,4},{4,2},{6,0},{8,14},{10,12},{12,10},{14,8},{16,22},{18,... | collective-permute-start | bytes 196616 | tf_op jit(solution)/shard_map/ppermute | solution.py:378
  8.6 5.2 %collective-permute-start.2 = (f32[128,128]{1,0:T(8,128)S(1)}, f32[128,128]{1,0:T(8,128)S(1)}, u32[]{:S(2)}, u32[]{:S(2)}) collective-permute-start(f32[128,128]{1,0:T(8,128)S(1)} %get-tuple-element.41.refs_3_), channel_id=1, source_target_pairs={{0,4},{2,6},{4,0},{6,2},{8,12},{10,14},{12,8},{14,10},{16,20},{18,... | collective-permute-start | bytes 196616 | tf_op jit(solution)/shard_map/ppermute | solution.py:378
  9.1 4.7 %collective-permute-start.3 = (f32[128,128]{1,0:T(8,128)S(1)}, f32[128,128]{1,0:T(8,128)S(1)}, u32[]{:S(2)}, u32[]{:S(2)}) collective-permute-start(f32[128,128]{1,0:T(8,128)S(1)} %get-tuple-element.41.refs_3_), channel_id=1, source_target_pairs={{0,2},{2,0},{4,6},{6,4},{8,10},{10,8},{12,14},{14,12},{16,18},{18,... | collective-permute-start | bytes 196616 | tf_op jit(solution)/shard_map/ppermute | solution.py:378
  9.3 9.0 %collective-permute-start.4 = (bf16[128,128]{1,0:T(8,128)(2,1)S(1)}, bf16[128,128]{1,0:T(8,128)(2,1)S(1)}, u32[]{:S(2)}, u32[]{:S(2)}) collective-permute-start(bf16[128,128]{1,0:T(8,128)(2,1)S(1)} %get-tuple-element.43.refs_3_.val_ref), channel_id=1, source_target_pairs={{0,24},{2,26},{4,28},{6,30},{8,16},{10,18},{12,20},{14,22},{16,8},... | collective-permute-start | bytes 98312 | tf_op jit(solution)/shard_map/ppermute | solution.py:378
  13.3 9.2 %collective-permute-start.5 = (bf16[128,128]{1,0:T(8,128)(2,1)S(1)}, bf16[128,128]{1,0:T(8,128)(2,1)S(1)}, u32[]{:S(2)}, u32[]{:S(2)}) collective-permute-start(bf16[128,128]{1,0:T(8,128)(2,1)S(1)} %get-tuple-element.43.refs_3_.val_ref), channel_id=1, source_target_pairs={{0,16},{2,18},{4,20},{6,22},{8,24},{10,26},{12,28},{14,30},{16,0},... | collective-permute-start | bytes 98312 | tf_op jit(solution)/shard_map/ppermute | solution.py:378
  13.3 9.2 %collective-permute-start.6 = (bf16[128,128]{1,0:T(8,128)(2,1)S(1)}, bf16[128,128]{1,0:T(8,128)(2,1)S(1)}, u32[]{:S(2)}, u32[]{:S(2)}) collective-permute-start(bf16[128,128]{1,0:T(8,128)(2,1)S(1)} %get-tuple-element.43.refs_3_.val_ref), channel_id=1, source_target_pairs={{0,8},{2,10},{4,12},{6,14},{8,0},{10,2},{12,4},{14,6},{16,24},{18,... | collective-permute-start | bytes 98312 | tf_op jit(solution)/shard_map/ppermute | solution.py:378
  13.8 24.4 %copy-start = (bf16[1024,2048]{1,0:T(8,128)(2,1)S(1)}, bf16[1024,2048]{1,0:T(8,128)(2,1)}, u32[]{:S(2)}) copy-start(bf16[1024,2048]{1,0:T(8,128)(2,1)} %refs_12_.1) | copy-start | bytes 12582916
  14.4 11.8 %collective-permute-start.7 = (bf16[512,128]{1,0:T(8,128)(2,1)S(1)}, bf16[512,128]{1,0:T(8,128)(2,1)S(1)}, u32[]{:S(2)}, u32[]{:S(2)}) collective-permute-start(bf16[512,128]{1,0:T(8,128)(2,1)S(1)} %get-tuple-element.45.refs_3_), channel_id=1, source_target_pairs={{0,24},{2,26},{4,28},{6,30},{8,16},{10,18},{12,20},{14,22},{16,8},... | collective-permute-start | bytes 393224 | tf_op jit(solution)/shard_map/ppermute | solution.py:378
  18.3 10.4 %collective-permute-start.8 = (bf16[512,128]{1,0:T(8,128)(2,1)S(1)}, bf16[512,128]{1,0:T(8,128)(2,1)S(1)}, u32[]{:S(2)}, u32[]{:S(2)}) collective-permute-start(bf16[512,128]{1,0:T(8,128)(2,1)S(1)} %get-tuple-element.45.refs_3_), channel_id=1, source_target_pairs={{0,16},{2,18},{4,20},{6,22},{8,24},{10,26},{12,28},{14,30},{16,0},... | collective-permute-start | bytes 393224 | tf_op jit(solution)/shard_map/ppermute | solution.py:378
  18.3 10.4 %collective-permute-start.9 = (bf16[512,128]{1,0:T(8,128)(2,1)S(1)}, bf16[512,128]{1,0:T(8,128)(2,1)S(1)}, u32[]{:S(2)}, u32[]{:S(2)}) collective-permute-start(bf16[512,128]{1,0:T(8,128)(2,1)S(1)} %get-tuple-element.45.refs_3_), channel_id=1, source_target_pairs={{0,8},{2,10},{4,12},{6,14},{8,0},{10,2},{12,4},{14,6},{16,24},{18,... | collective-permute-start | bytes 393224 | tf_op jit(solution)/shard_map/ppermute | solution.py:378
  23.8 8.9 %collective-permute-start.13 = (bf16[512,128]{1,0:T(8,128)(2,1)S(1)}, bf16[512,128]{1,0:T(8,128)(2,1)S(1)}, u32[]{:S(2)}, u32[]{:S(2)}) collective-permute-start(bf16[512,128]{1,0:T(8,128)(2,1)S(1)} %get-tuple-element.54.refs_7_), channel_id=1, source_target_pairs={{0,6},{2,4},{4,2},{6,0},{8,14},{10,12},{12,10},{14,8},{16,22},{18,... | collective-permute-start | bytes 393224 | tf_op jit(solution)/shard_map/ppermute | solution.py:378
  26.2 10.8 %collective-permute-start.14 = (bf16[512,128]{1,0:T(8,128)(2,1)S(1)}, bf16[512,128]{1,0:T(8,128)(2,1)S(1)}, u32[]{:S(2)}, u32[]{:S(2)}) collective-permute-start(bf16[512,128]{1,0:T(8,128)(2,1)S(1)} %get-tuple-element.54.refs_7_), channel_id=1, source_target_pairs={{0,4},{2,6},{4,0},{6,2},{8,12},{10,14},{12,8},{14,10},{16,20},{18,... | collective-permute-start | bytes 393224 | tf_op jit(solution)/shard_map/ppermute | solution.py:378
  26.2 10.8 %collective-permute-start.15 = (bf16[512,128]{1,0:T(8,128)(2,1)S(1)}, bf16[512,128]{1,0:T(8,128)(2,1)S(1)}, u32[]{:S(2)}, u32[]{:S(2)}) collective-permute-start(bf16[512,128]{1,0:T(8,128)(2,1)S(1)} %get-tuple-element.54.refs_7_), channel_id=1, source_target_pairs={{0,2},{2,0},{4,6},{6,4},{8,10},{10,8},{12,14},{14,12},{16,18},{18,... | collective-permute-start | bytes 393224 | tf_op jit(solution)/shard_map/ppermute | solution.py:378
  29.5 7.5 %collective-permute-start.10 = (bf16[512,128]{1,0:T(8,128)(2,1)S(1)}, bf16[512,128]{1,0:T(8,128)(2,1)S(1)}, u32[]{:S(2)}, u32[]{:S(2)}) collective-permute-start(bf16[512,128]{1,0:T(8,128)(2,1)S(1)} %get-tuple-element.50), channel_id=1, source_target_pairs={{0,6},{2,4},{4,2},{6,0},{8,14},{10,12},{12,10},{14,8},{16,22},{18,... | collective-permute-start | bytes 393224 | tf_op jit(solution)/shard_map/ppermute | solution.py:378
  32.0 6.2 %collective-permute-start.11 = (bf16[512,128]{1,0:T(8,128)(2,1)S(1)}, bf16[512,128]{1,0:T(8,128)(2,1)S(1)}, u32[]{:S(2)}, u32[]{:S(2)}) collective-permute-start(bf16[512,128]{1,0:T(8,128)(2,1)S(1)} %get-tuple-element.51), channel_id=1, source_target_pairs={{0,4},{2,6},{4,0},{6,2},{8,12},{10,14},{12,8},{14,10},{16,20},{18,... | collective-permute-start | bytes 393224 | tf_op jit(solution)/shard_map/ppermute | solution.py:378
  32.7 5.6 %collective-permute-start.12 = (bf16[512,128]{1,0:T(8,128)(2,1)S(1)}, bf16[512,128]{1,0:T(8,128)(2,1)S(1)}, u32[]{:S(2)}, u32[]{:S(2)}) collective-permute-start(bf16[512,128]{1,0:T(8,128)(2,1)S(1)} %get-tuple-element.52), channel_id=1, source_target_pairs={{0,2},{2,0},{4,6},{6,4},{8,10},{10,8},{12,14},{14,12},{16,18},{18,... | collective-permute-start | bytes 393224 | tf_op jit(solution)/shard_map/ppermute | solution.py:378
  42.5 1.6 %collective-permute-start.16 = (bf16[64,2048]{1,0:T(8,128)(2,1)S(1)}, bf16[64,2048]{1,0:T(8,128)(2,1)S(1)}, u32[]{:S(2)}, u32[]{:S(2)}) collective-permute-start(bf16[64,2048]{1,0:T(8,128)(2,1)S(1)} %get-tuple-element.66), channel_id=1, source_target_pairs={{0,1},{1,0},{2,3},{3,2},{4,5},{5,4},{6,7},{7,6},{8,9},{9,8},{10,11... | collective-permute-start | bytes 786440 | tf_op jit(solution)/shard_map/ppermute | solution.py:501

commit v13 on v12

--- a/solution.py
+++ b/solution.py
@@ -136,7 +136,7 @@
     turn_ref[...] = jnp.where(heads == lanes, 1.0, 0.0) - crossed[tokens:]
 
 
-def leave_kernel(group, place_ref, exit_ref, *refs):
+def leave_kernel(group, place_ref, exit_ref, val_ref, *refs):
     turn_refs, (leave_ref, starts_ref) = refs[:group], refs[group : group + 2]
     near_refs, (turns_ref, seen_ref) = refs[group + 2 : -2], refs[-2:]
     member = place_ref[0] % group
@@ -156,14 +156,12 @@
             keys = jnp.where(index > member, dot3(keys, turn), own)
         if index < group - 1:
             starts_ref[index + 1] = product
-    high, low = split(keys)
-    leave_ref[:tokens] = high
-    leave_ref[tokens : 2 * tokens] = low
-    high, low = split(product)
-    leave_ref[2 * tokens : 2 * tokens + size] = high
-    leave_ref[2 * tokens + size :] = low
+    leave_ref[:tokens] = keys.astype(BF16)
+    leave_ref[tokens : 2 * tokens] = val_ref[...]
+    leave_ref[2 * tokens :] = product.astype(BF16)
     for step in range(group):
-        near_refs[step][...] = seen_ref[target_of(member, step, group)]
+        near_refs[step][:tokens] = seen_ref[target_of(member, step, group)]
+        near_refs[step][tokens:] = val_ref[...]
 
 
 def word_of(slot, segments):
@@ -172,10 +170,7 @@
     return slot // per_word, bits * (slot % per_word), (1 << bits) - 1
 
 
-def bundle_kernel(group, groups, most, place_ref, mask_ref, after_ref, *refs):
-    val_refs, (line_ref, table_ref) = refs[:groups], refs[groups:]
-    place = place_ref[0]
-    mine = place // group
+def pack_table(most, place, mask_ref, table_ref):
     segments = mask_ref.shape[0]
     for word in range(table_ref.shape[0]):
         table_ref[word] = 0
@@ -191,14 +186,11 @@
         return count + wanted.astype(jnp.int32)
 
     lax.fori_loop(0, segments, pick, jnp.int32(0))
-    tokens = val_refs[0].shape[0]
-    for way in range(groups):
-        at = pl.multiple_of(source_of(mine, way, groups) * tokens, tokens)
-        line_ref[pl.ds(at, tokens), :] = val_refs[groups - 1 - way][...]
-
-
-def query_kernel(rows_ref, weight_hbm, gain_ref, kn_ref, dirs_ref, coeff_ref, solved_ref, val_ref,
-                 moved_ref, weighted_ref, peak_ref, total_ref, weight_ref, raw_ref, sems):
+
+
+def query_kernel(most, place_ref, mask_ref, rows_ref, weight_hbm, gain_ref, kn_ref, dirs_ref,
+                 coeff_ref, solved_ref, val_ref, moved_ref, weighted_ref, peak_ref, total_ref,
+                 table_ref, weight_ref, raw_ref, sems):
     tokens, size = kn_ref.shape
     heads = moved_ref.shape[0]
     pieces, deep, _ = weight_ref.shape
@@ -210,6 +202,7 @@
     ]
     for copy in copies:
         copy.start()
+    pack_table(most, place_ref[0], mask_ref, table_ref)
     across = jnp.concatenate([kn_ref[...], dirs_ref[...]], axis=0)
     into = jnp.concatenate([coeff_ref[...], solved_ref[...]], axis=1)
     for n in range(pieces):
@@ -252,16 +245,15 @@
 
 
 def arrive_kernel(groups, group, tokens, place_ref, *refs):
-    arrived, starts_ref, near_refs = refs[:groups], refs[groups], refs[groups + 1 :]
-    far_refs, (keys_ref, whole_ref) = refs[-group - 2 : -2], refs[-2:]
+    arrived, starts_ref = refs[:groups], refs[groups]
+    far_refs, (keys_ref, vals_ref, whole_ref) = refs[-group - 3 : -3], refs[-3:]
     mine, member = place_ref[0] // group, place_ref[0] % group
-    size = starts_ref.shape[1]
     for step in range(groups):
         index = source_of(mine, step, groups)
         ref = arrived[groups - 1 - step]
-        keys_ref[index] = ref[:tokens].astype(F32) + ref[tokens : 2 * tokens].astype(F32)
-        whole = ref[2 * tokens : 2 * tokens + size].astype(F32)
-        whole_ref[index] = whole + ref[2 * tokens + size :].astype(F32)
+        keys_ref[index] = ref[:tokens].astype(F32)
+        vals_ref[index] = ref[tokens : 2 * tokens]
+        whole_ref[index] = ref[2 * tokens :].astype(F32)
     brought = [keys_ref[groups - 2]]
     product = None
     for index in range(groups - 3, -1, -1):
@@ -271,20 +263,23 @@
         product = whole
         brought.append(jnp.where(index + 1 < mine, dot3(keys, product), keys))
     keys = jnp.concatenate(brought[::-1], axis=0)
+    count = (groups - 1) * tokens
     for step in range(group):
         start = starts_ref[target_of(member, step, group)]
-        far_refs[step][: (groups - 1) * tokens] = dot3(keys, start).astype(BF16)
-        far_refs[step][(groups - 1) * tokens :] = near_refs[step][...]
+        far_refs[step][:count] = dot3(keys, start).astype(BF16)
+        for index in range(groups - 1):
+            at = count + index * tokens
+            far_refs[step][at : at + tokens] = vals_ref[index]
 
 
 def attend_kernel(group, segments, most, place_ref, core_ref, table_ref, *refs):
-    far_refs, line_refs = refs[:group][::-1], refs[group : 2 * group][::-1]
+    far_refs, near_refs = refs[:group][::-1], refs[group : 2 * group][::-1]
     (moved_ref, weighted_ref, peak_ref, total_ref, out_ref, away_ref, kept_ref, keys_ref, vals_ref,
      attended_ref) = refs[2 * group :]
     core = core_ref[0]
     mine, member = place_ref[0] // group, place_ref[0] % group
     heads, tokens, size = moved_ref.shape
-    groups = far_refs[0].shape[0] // tokens
+    earlier = far_refs[0].shape[0] // (2 * tokens)
     scaling = LOG2E / math.sqrt(size)
     chunk = keys_ref.shape[0] // tokens
     lanes = lax.broadcasted_iota(jnp.int32, (1, chunk * tokens), 1)
@@ -298,15 +293,19 @@
             found = found + (code > 0).astype(jnp.int32)
             segment = jnp.maximum(code - 1, 0)
             whose, source = segment % group, segment // group
-            before = jnp.where(source < mine, source, groups - 1)
-            before = pl.multiple_of(before * tokens, tokens)
-            after = pl.multiple_of(source * tokens, tokens)
+            before = pl.multiple_of(jnp.minimum(source, earlier - 1) * tokens, tokens)
+            after = pl.multiple_of(before + earlier * tokens, tokens)
             for number in range(group):
 
-                @pl.when(whose == source_of(member, number, group))
+                @pl.when((whose == source_of(member, number, group)) & (source < mine))
                 def _():
-                    vals_ref[part, :] = line_refs[number][pl.ds(after, tokens), :]
                     keys_ref[part, :] = far_refs[number][pl.ds(before, tokens), :]
+                    vals_ref[part, :] = far_refs[number][pl.ds(after, tokens), :]
+
+                @pl.when((whose == source_of(member, number, group)) & (source >= mine))
+                def _():
+                    keys_ref[part, :] = near_refs[number][:tokens]
+                    vals_ref[part, :] = near_refs[number][tokens:]
 
         return jnp.where(lanes < found * tokens, 0.0, NEGATIVE)
 
@@ -417,16 +416,15 @@
         moved=8 * width * size,
     )
     turns = within_group([turn] * group)
-    line = along_line([val] * groups)
     leaving, starts, *near = call(
         functools.partial(leave_kernel, group),
         [
-            shaped((2 * tokens + 2 * size, size), BF16),
+            shaped((2 * tokens + size, size), BF16),
             shaped((group, size, size), F32),
         ]
-        + [shaped((tokens, size), BF16)] * group,
-        (place, exit_keys, *turns[::-1]),
-        in_specs=[smem] + [vmem] * (1 + group),
+        + [shaped((2 * tokens, size), BF16)] * group,
+        (place, exit_keys, val, *turns[::-1]),
+        in_specs=[smem] + [vmem] * (2 + group),
         scratch=(
             pltpu.VMEM((group, size, size), F32),
             pltpu.VMEM((group, tokens, size), BF16),
@@ -435,30 +433,22 @@
         moved=10**6,
     )
     arrived = along_line([leaving] * groups)
+    near = within_group(near)
     most = segments // 4
-    values, table = call(
-        functools.partial(bundle_kernel, group, groups, most),
-        [
-            shaped((groups * tokens, size), BF16),
-            shaped((word_of(most - 1, segments)[0] + 1,), jnp.int32),
-        ],
-        (place, block_mask[0], starts, *line[::-1]),
-        in_specs=[smem, smem, anywhere] + [vmem] * groups,
-        out_specs=[vmem, smem],
-        moved=10**6,
-        limit=8 + group * groups // 4,
-    )
-    values = within_group([values] * group)
-    own = call(
-        query_kernel,
+    *own, table = call(
+        functools.partial(query_kernel, most),
         (
             shaped((heads, tokens, size), BF16),
             shaped((heads, tokens, size), F32),
             shaped((heads, tokens, 1), F32),
             shaped((heads, tokens, 1), F32),
-        ),
-        (rows, in_hbm(w_query), query_gain, kn, dirs, coeff, solved, val),
-        in_specs=[vmem, hbm] + [vmem] * 6,
+            shaped((word_of(most - 1, segments)[0] + 1,), jnp.int32),
+        ),
+        (
+            place, block_mask[0], rows, in_hbm(w_query), query_gain, kn, dirs, coeff, solved, val,
+        ),
+        in_specs=[smem, smem, vmem, hbm] + [vmem] * 6,
+        out_specs=(vmem, vmem, vmem, vmem, smem),
         scratch=(
             pltpu.VMEM((2, width // 2, w_query.shape[1]), BF16),
             pltpu.VMEM((tokens, w_query.shape[1]), F32),
@@ -470,11 +460,12 @@
     )
     far = call(
         functools.partial(arrive_kernel, groups, group, tokens),
-        [shaped((groups * tokens, size), BF16)] * group,
-        (place, *arrived[::-1], starts, *near),
-        in_specs=[smem] + [vmem] * (groups + 1 + group),
+        [shaped((2 * (groups - 1) * tokens, size), BF16)] * group,
+        (place, *arrived[::-1], starts, *near[1:]),
+        in_specs=[smem] + [vmem] * (groups + 1) + [anywhere] * (group - 1),
         scratch=(
             pltpu.VMEM((groups, tokens, size), F32),
+            pltpu.VMEM((groups, tokens, size), BF16),
             pltpu.VMEM((groups, size, size), F32),
         ),
         flops=6 * groups * group * size**3,
@@ -487,7 +478,7 @@
     away, kept = call(
         functools.partial(attend_kernel, group, segments, most),
         [shaped((half, width_out), BF16)] * 2,
-        (place, core, table, *far[::-1], *values[::-1], *own, w_out),
+        (place, core, table, *far[::-1], *near[::-1], *own, w_out),
         in_specs=[smem] * 3 + [vmem] * (2 * group + 5),
         scratch=[
             pltpu.VMEM((chunk * tokens, size), BF16),

time: 45.1 us -> 45.8 us (1.016)
  waiting for transfers between devices: 7.59 us -> 13.7 us
  starting transfers between devices: 20.9 us -> 16.2 us
  Pallas kernels: 14.9 us -> 14.3 us
    ppermute x15 -> x12, waiting for transfers between devices: 6.07 us -> 12.2 us  [swapped(): out[step] = lax.ppermute(values[step], 'ctx', pairs_of(step))]
    ppermute x15 -> x12, starting transfers between devices: 20.4 us -> 15.7 us  [swapped(): out[step] = lax.ppermute(values[step], 'ctx', pairs_of(step))]
    pallas_call x7 -> x6, Pallas kernels: 14.9 us -> 14.3 us  [call(): pl.pallas_call(kernel, out_shape=out_shape, in_specs=in_specs or [vmem] *...]
  transfers between devices with their start and end apart: 17 -> 14, of which waited for: 4 -> 9; matrix products, arithmetic and copies ran while one was open for 0% -> 0% of each run, Pallas kernels for 18% -> 13%
where the time goes in v13:
time: 45.8 us; the launch traced here: 45.7 us
  starting transfers between devices  16.2 us (35%)
  Pallas kernels  14.3 us (31%)
  waiting for transfers between devices  13.7 us (30%)
  other arithmetic  0.77 us (2%)
  between operations  0.72 us (2%)
    ppermute x12, starting transfers between devices, swapped(): out[step] = lax.ppermute(values[step], 'ctx', pairs_of(step))  15.7 us
    pallas_call x6, Pallas kernels, call(): pl.pallas_call(kernel, out_shape=out_shape, in_specs=in_specs or [vmem] *...  14.3 us
    ppermute x12, waiting for transfers between devices, swapped(): out[step] = lax.ppermute(values[step], 'ctx', pairs_of(step))  12.2 us
    ppermute x1, waiting for transfers between devices, body(): return kept + lax.ppermute(away, 'head', [(0, 1), (1, 0)])  1.51 us
  transfers between devices with their start and end apart: 14, of which 9 were waited for; matrix products, arithmetic and copies ran while one was open for 0% of the time, Pallas kernels for 13%

profile of v13, /device:TPU:0, one launch (start us, length us, event | category | flops | bytes accessed | tf_op | source)
XLA Modules:
  0.0 45.7 jit_solution(8325518277675477527)
XLA Ops:
  1.1 1.5 %shard_map.109 = (bf16[2048,384]{1,0:T(8,128)(2,1)S(1)}, bf16[1,2048]{1,0:T(2,128)(2,1)S(1)}, f32[1,128]{1,0:T(1,128)S(1)}, f32[1,128]{1,0:T(1,128)S(1)}, bf16[64,2048]{1,0:T(8,128)(2,1)S(1)}) custom-call(bf16[2048,128]{1,0:T(8,128)(2,1)} %key_hbm.1, bf16[2048,128]{1,0:T(8,128)(2,1)} %dir_hbm.1, bf16[2048,128]{1,0:T(8,128)(2,1)} %value_hbm.1, ...), custom_call_target="tpu_custom_call" | custom-call | bytes 3145728 | tf_op jit(solution)/shard_map/pallas_call | solution.py:21
  2.7 2.4 %shard_map.110 = (bf16[128,2048]{1,0:T(8,128)(2,1)S(1)}, f32[128,128]{1,0:T(8,128)S(1)}, bf16[128,128]{1,0:T(8,128)(2,1)S(1)}, f32[128,128]{1,0:T(8,128)S(1)}, f...) custom-call(s32[1]{0:T(128)} %bitcast.1.core_ref, ...), custom_call_target="tpu_custom_call" | custom-call | flops 201326592 | bytes 2097152 | tf_op jit(solution)/shard_map/pallas_call | solution.py:21
  5.1 3.5 %collective-permute-start.1 = (f32[128,128]{1,0:T(8,128)S(1)}, f32[128,128]{1,0:T(8,128)S(1)}, u32[]{:S(2)}, u32[]{:S(2)}) collective-permute-start(f32[128,128]{1,0:T(8,128)S(1)} %get-tuple-element.48.refs_3_), channel_id=1, source_target_pairs={{0,6},{2,4},{4,2},{6,0},{8,14},{10,12},{12,10},{14,8},{16,22},{18,... | collective-permute-start | bytes 196616 | tf_op jit(solution)/shard_map/ppermute | solution.py:377
  8.6 0.5 %collective-permute-start.2 = (f32[128,128]{1,0:T(8,128)S(1)}, f32[128,128]{1,0:T(8,128)S(1)}, u32[]{:S(2)}, u32[]{:S(2)}) collective-permute-start(f32[128,128]{1,0:T(8,128)S(1)} %get-tuple-element.48.refs_3_), channel_id=1, source_target_pairs={{0,4},{2,6},{4,0},{6,2},{8,12},{10,14},{12,8},{14,10},{16,20},{18,... | collective-permute-start | bytes 196616 | tf_op jit(solution)/shard_map/ppermute | solution.py:377
  9.3 2.1 %collective-permute-done.1.refs_0_ = f32[128,128]{1,0:T(8,128)S(1)} collective-permute-done((f32[128,128]{1,0:T(8,128)S(1)}, f32[128,128]{1,0:T(8,128)S(1)}, u32[]{:S(2)}, u32[]{:S(2)}) %collective-permute-start.1) | collective-permute-done | bytes 65568 | tf_op jit(solution)/shard_map/ppermute | solution.py:377
  11.4 1.5 %collective-permute-done.2.refs_1_ = f32[128,128]{1,0:T(8,128)S(1)} collective-permute-done((f32[128,128]{1,0:T(8,128)S(1)}, f32[128,128]{1,0:T(8,128)S(1)}, u32[]{:S(2)}, u32[]{:S(2)}) %collective-permute-start.2) | collective-permute-done | bytes 65568 | tf_op jit(solution)/shard_map/ppermute | solution.py:377
  12.9 0.5 %collective-permute-done.3.refs_2_ = f32[128,128]{1,0:T(8,128)S(1)} collective-permute-done((f32[128,128]{1,0:T(8,128)S(1)}, f32[128,128]{1,0:T(8,128)S(1)}, u32[]{:S(2)}, u32[]{:S(2)}) %collective-permute-start.3) | collective-permute-done | bytes 65568 | tf_op jit(solution)/shard_map/ppermute | solution.py:377
  13.9 1.2 %collective-permute-start.7 = (bf16[256,128]{1,0:T(8,128)(2,1)S(1)}, bf16[256,128]{1,0:T(8,128)(2,1)S(1)}, u32[]{:S(2)}, u32[]{:S(2)}) collective-permute-start(bf16[256,128]{1,0:T(8,128)(2,1)S(1)} %get-tuple-element.51), channel_id=1, source_target_pairs={{0,2},{2,0},{4,6},{6,4},{8,10},{10,8},{12,14},{14,12},{16,18},{18,... | collective-permute-start | bytes 196616 | tf_op jit(solution)/shard_map/ppermute | solution.py:377
  15.2 3.6 %collective-permute-start.4 = (bf16[384,128]{1,0:T(8,128)(2,1)S(1)}, bf16[384,128]{1,0:T(8,128)(2,1)S(1)}, u32[]{:S(2)}, u32[]{:S(2)}) collective-permute-start(bf16[384,128]{1,0:T(8,128)(2,1)S(1)} %get-tuple-element.49.refs_3_), channel_id=1, source_target_pairs={{0,24},{2,26},{4,28},{6,30},{8,16},{10,18},{12,20},{14,22},{16,8},... | collective-permute-start | bytes 294920 | tf_op jit(solution)/shard_map/ppermute | solution.py:377
  18.7 0.8 %collective-permute-start.6 = (bf16[384,128]{1,0:T(8,128)(2,1)S(1)}, bf16[384,128]{1,0:T(8,128)(2,1)S(1)}, u32[]{:S(2)}, u32[]{:S(2)}) collective-permute-start(bf16[384,128]{1,0:T(8,128)(2,1)S(1)} %get-tuple-element.49.refs_3_), channel_id=1, source_target_pairs={{0,8},{2,10},{4,12},{6,14},{8,0},{10,2},{12,4},{14,6},{16,24},{18,... | collective-permute-start | bytes 294920 | tf_op jit(solution)/shard_map/ppermute | solution.py:377
  19.5 0.9 %collective-permute-start.8 = (bf16[256,128]{1,0:T(8,128)(2,1)S(1)}, bf16[256,128]{1,0:T(8,128)(2,1)S(1)}, u32[]{:S(2)}, u32[]{:S(2)}) collective-permute-start(bf16[256,128]{1,0:T(8,128)(2,1)S(1)} %get-tuple-element.52), channel_id=1, source_target_pairs={{0,4},{2,6},{4,0},{6,2},{8,12},{10,14},{12,8},{14,10},{16,20},{18,... | collective-permute-start | bytes 196616 | tf_op jit(solution)/shard_map/ppermute | solution.py:377
  20.4 1.4 %collective-permute-start.9 = (bf16[256,128]{1,0:T(8,128)(2,1)S(1)}, bf16[256,128]{1,0:T(8,128)(2,1)S(1)}, u32[]{:S(2)}, u32[]{:S(2)}) collective-permute-start(bf16[256,128]{1,0:T(8,128)(2,1)S(1)} %get-tuple-element.53), channel_id=1, source_target_pairs={{0,6},{2,4},{4,2},{6,0},{8,14},{10,12},{12,10},{14,8},{16,22},{18,... | collective-permute-start | bytes 196616 | tf_op jit(solution)/shard_map/ppermute | solution.py:377
  21.9 1.9 %collective-permute-done.8.refs_6_.refs_5_ = bf16[256,128]{1,0:T(8,128)(2,1)S(1)} collective-permute-done((bf16[256,128]{1,0:T(8,128)(2,1)S(1)}, bf16[256,128]{1,0:T(8,128)(2,1)S(1)}, u32[]{:S(2)}, u32[]{:S(2)}) %collective-permute-start.8) | collective-permute-done | bytes 65568 | tf_op jit(solution)/shard_map/ppermute | solution.py:377
  23.8 1.8 %collective-permute-done.9.refs_7_.refs_4_ = bf16[256,128]{1,0:T(8,128)(2,1)S(1)} collective-permute-done((bf16[256,128]{1,0:T(8,128)(2,1)S(1)}, bf16[256,128]{1,0:T(8,128)(2,1)S(1)}, u32[]{:S(2)}, u32[]{:S(2)}) %collective-permute-start.9) | collective-permute-done | bytes 65568 | tf_op jit(solution)/shard_map/ppermute | solution.py:377
  25.6 1.3 %collective-permute-done.5.refs_1_ = bf16[384,128]{1,0:T(8,128)(2,1)S(1)} collective-permute-done((bf16[384,128]{1,0:T(8,128)(2,1)S(1)}, bf16[384,128]{1,0:T(8,128)(2,1)S(1)}, u32[]{:S(2)}, u32[]{:S(2)}) %collective-permute-start.5) | collective-permute-done | bytes 98336 | tf_op jit(solution)/shard_map/ppermute | solution.py:377
  26.9 0.9 %shard_map.113 = (bf16[768,128]{1,0:T(8,128)(2,1)S(1)}, bf16[768,128]{1,0:T(8,128)(2,1)S(1)}, bf16[768,128]{1,0:T(8,128)(2,1)S(1)}, bf16[768,128]{1,0:T(8,128)(2,1)S(1)}) custom-call(s32[1]{0:T(128)} %bitcast.place_ref, bf16[384,128]{1,0:T(8,128)(2,1)S(1)} %collective-permute-done.4.refs_0_, bf16[384,128]{1,0:T(8,128)(2,1)S(1)} %collective-permute-done.5.refs_1_, ...), custom_call_target="tpu_custom_call" | custom-call | flops 201326592 | bytes 1000000 | tf_op jit(solution)/shard_map/pallas_call | solution.py:21
  27.7 1.6 %collective-permute-start.10 = (bf16[768,128]{1,0:T(8,128)(2,1)S(1)}, bf16[768,128]{1,0:T(8,128)(2,1)S(1)}, u32[]{:S(2)}, u32[]{:S(2)}) collective-permute-start(bf16[768,128]{1,0:T(8,128)(2,1)S(1)} %get-tuple-element.54), channel_id=1, source_target_pairs={{0,6},{2,4},{4,2},{6,0},{8,14},{10,12},{12,10},{14,8},{16,22},{18,... | collective-permute-start | bytes 589832 | tf_op jit(solution)/shard_map/ppermute | solution.py:377
  29.6 1.7 %collective-permute-start.12 = (bf16[768,128]{1,0:T(8,128)(2,1)S(1)}, bf16[768,128]{1,0:T(8,128)(2,1)S(1)}, u32[]{:S(2)}, u32[]{:S(2)}) collective-permute-start(bf16[768,128]{1,0:T(8,128)(2,1)S(1)} %get-tuple-element.56), channel_id=1, source_target_pairs={{0,2},{2,0},{4,6},{6,4},{8,10},{10,8},{12,14},{14,12},{16,18},{18,... | collective-permute-start | bytes 589832 | tf_op jit(solution)/shard_map/ppermute | solution.py:377
  31.3 4.5 %shard_map.111 = (bf16[8,128,128]{2,1,0:T(8,128)(2,1)S(1)}, f32[8,128,128]{2,1,0:T(8,128)S(1)}, f32[8,128,1]{2,1,0:T(8,128)S(1)}, f32[8,128,1]{2,1,0:T(8,128)S(1)}, s32[1]{0:T(128)}) custom-call(s32[1]{0:T(128)} %bitcast.place_ref, s32[16]{0:T(128)S(1)} %bitcast.5, bf16[128,2048]{1,0:T(8,128)(2,1)S(1)} %get-tuple-element.39.rows_ref, ...), custom_call_target="tpu_custom_call" | custom-call | flops 1073741824 | bytes 16777216 | tf_op jit(solution)/shard_map/pallas_call | solution.py:21
  35.8 0.8 %collective-permute-done.10.refs_0_ = bf16[768,128]{1,0:T(8,128)(2,1)S(1)} collective-permute-done((bf16[768,128]{1,0:T(8,128)(2,1)S(1)}, bf16[768,128]{1,0:T(8,128)(2,1)S(1)}, u32[]{:S(2)}, u32[]{:S(2)}) %collective-permute-start.10) | collective-permute-done | bytes 196640 | tf_op jit(solution)/shard_map/ppermute | solution.py:377
  36.6 2.3 %collective-permute-done.11.refs_1_ = bf16[768,128]{1,0:T(8,128)(2,1)S(1)} collective-permute-done((bf16[768,128]{1,0:T(8,128)(2,1)S(1)}, bf16[768,128]{1,0:T(8,128)(2,1)S(1)}, u32[]{:S(2)}, u32[]{:S(2)}) %collective-permute-start.11) | collective-permute-done | bytes 196640 | tf_op jit(solution)/shard_map/ppermute | solution.py:377
  38.9 4.4 %shard_map.114 = (bf16[64,2048]{1,0:T(8,128)(2,1)S(1)}, bf16[64,2048]{1,0:T(8,128)(2,1)S(1)}) custom-call(s32[1]{0:T(128)} %bitcast.place_ref, s32[1]{0:T(128)} %bitcast.1.core_ref, s32[1]{0:T(128)} %get-tuple-element.46.table_ref, bf16[768,128]{1,0:T(8,128)(2,1)S(1)} %collective-permute-done.10.refs_0_, ...), custom_call_target="tpu_custom_call" | custom-call | flops 536870912 | bytes 4000000 | tf_op jit(solution)/shard_map/pallas_call | solution.py:21
  43.4 1.5 %collective-permute-done.13 = bf16[64,2048]{1,0:T(8,128)(2,1)S(1)} collective-permute-done((bf16[64,2048]{1,0:T(8,128)(2,1)S(1)}, bf16[64,2048]{1,0:T(8,128)(2,1)S(1)}, u32[]{:S(2)}, u32[]{:S(2)}) %collective-permute-start.13) | collective-permute-done | bytes 262176 | tf_op jit(solution)/shard_map/ppermute | solution.py:492
  44.9 0.8 %add.3 = bf16[64,2048]{1,0:T(8,128)(2,1)} add(bf16[64,2048]{1,0:T(8,128)(2,1)S(1)} %get-tuple-element.63, bf16[64,2048]{1,0:T(8,128)(2,1)S(1)} %collective-permute-done.13) | non-fusion elementwise | flops 131072 | bytes 786432 | tf_op jit(solution)/shard_map/add | solution.py:492
  (15 shorter events, 1.5 us)
Async XLA Ops:
  0.0 31.3 %copy-start.1 = (s32[1,16]{1,0:T(1,128)S(1)}, s32[1,16]{1,0:T(1,128)}, u32[]{:S(2)}) copy-start(s32[1,16]{1,0:T(1,128)} %param.21) | copy-start | bytes 196
  0.0 2.6 %collective-permute-start = (bf16[64,2048]{1,0:T(8,128)(2,1)}, bf16[64,2048]{1,0:T(8,128)(2,1)S(1)}, u32[]{:S(2)}, u32[]{:S(2)}) collective-permute-start(bf16[64,2048]{1,0:T(8,128)(2,1)} %mine_hbm.1), channel_id=1, source_target_pairs={{0,1},{1,0},{2,3},{3,2},{4,5},{5,4},{6,7},{7,6},{8,9},{9,8},{10,11... | collective-permute-start | bytes 786440 | tf_op jit(solution)/shard_map/ppermute | solution.py:363
  5.1 6.3 %collective-permute-start.1 = (f32[128,128]{1,0:T(8,128)S(1)}, f32[128,128]{1,0:T(8,128)S(1)}, u32[]{:S(2)}, u32[]{:S(2)}) collective-permute-start(f32[128,128]{1,0:T(8,128)S(1)} %get-tuple-element.48.refs_3_), channel_id=1, source_target_pairs={{0,6},{2,4},{4,2},{6,0},{8,14},{10,12},{12,10},{14,8},{16,22},{18,... | collective-permute-start | bytes 196616 | tf_op jit(solution)/shard_map/ppermute | solution.py:377
  8.6 4.3 %collective-permute-start.2 = (f32[128,128]{1,0:T(8,128)S(1)}, f32[128,128]{1,0:T(8,128)S(1)}, u32[]{:S(2)}, u32[]{:S(2)}) collective-permute-start(f32[128,128]{1,0:T(8,128)S(1)} %get-tuple-element.48.refs_3_), channel_id=1, source_target_pairs={{0,4},{2,6},{4,0},{6,2},{8,12},{10,14},{12,8},{14,10},{16,20},{18,... | collective-permute-start | bytes 196616 | tf_op jit(solution)/shard_map/ppermute | solution.py:377
  9.1 4.3 %collective-permute-start.3 = (f32[128,128]{1,0:T(8,128)S(1)}, f32[128,128]{1,0:T(8,128)S(1)}, u32[]{:S(2)}, u32[]{:S(2)}) collective-permute-start(f32[128,128]{1,0:T(8,128)S(1)} %get-tuple-element.48.refs_3_), channel_id=1, source_target_pairs={{0,2},{2,0},{4,6},{6,4},{8,10},{10,8},{12,14},{14,12},{16,18},{18,... | collective-permute-start | bytes 196616 | tf_op jit(solution)/shard_map/ppermute | solution.py:377
  9.3 29.6 %copy-start = (bf16[1024,2048]{1,0:T(8,128)(2,1)S(1)}, bf16[1024,2048]{1,0:T(8,128)(2,1)}, u32[]{:S(2)}) copy-start(bf16[1024,2048]{1,0:T(8,128)(2,1)} %refs_12_.1) | copy-start | bytes 12582916
  13.9 6.5 %collective-permute-start.7 = (bf16[256,128]{1,0:T(8,128)(2,1)S(1)}, bf16[256,128]{1,0:T(8,128)(2,1)S(1)}, u32[]{:S(2)}, u32[]{:S(2)}) collective-permute-start(bf16[256,128]{1,0:T(8,128)(2,1)S(1)} %get-tuple-element.51), channel_id=1, source_target_pairs={{0,2},{2,0},{4,6},{6,4},{8,10},{10,8},{12,14},{14,12},{16,18},{18,... | collective-permute-start | bytes 196616 | tf_op jit(solution)/shard_map/ppermute | solution.py:377
  15.2 10.4 %collective-permute-start.4 = (bf16[384,128]{1,0:T(8,128)(2,1)S(1)}, bf16[384,128]{1,0:T(8,128)(2,1)S(1)}, u32[]{:S(2)}, u32[]{:S(2)}) collective-permute-start(bf16[384,128]{1,0:T(8,128)(2,1)S(1)} %get-tuple-element.49.refs_3_), channel_id=1, source_target_pairs={{0,24},{2,26},{4,28},{6,30},{8,16},{10,18},{12,20},{14,22},{16,8},... | collective-permute-start | bytes 294920 | tf_op jit(solution)/shard_map/ppermute | solution.py:377
  18.7 8.1 %collective-permute-start.5 = (bf16[384,128]{1,0:T(8,128)(2,1)S(1)}, bf16[384,128]{1,0:T(8,128)(2,1)S(1)}, u32[]{:S(2)}, u32[]{:S(2)}) collective-permute-start(bf16[384,128]{1,0:T(8,128)(2,1)S(1)} %get-tuple-element.49.refs_3_), channel_id=1, source_target_pairs={{0,16},{2,18},{4,20},{6,22},{8,24},{10,26},{12,28},{14,30},{16,0},... | collective-permute-start | bytes 294920 | tf_op jit(solution)/shard_map/ppermute | solution.py:377
  18.7 8.1 %collective-permute-start.6 = (bf16[384,128]{1,0:T(8,128)(2,1)S(1)}, bf16[384,128]{1,0:T(8,128)(2,1)S(1)}, u32[]{:S(2)}, u32[]{:S(2)}) collective-permute-start(bf16[384,128]{1,0:T(8,128)(2,1)S(1)} %get-tuple-element.49.refs_3_), channel_id=1, source_target_pairs={{0,8},{2,10},{4,12},{6,14},{8,0},{10,2},{12,4},{14,6},{16,24},{18,... | collective-permute-start | bytes 294920 | tf_op jit(solution)/shard_map/ppermute | solution.py:377
  19.5 4.3 %collective-permute-start.8 = (bf16[256,128]{1,0:T(8,128)(2,1)S(1)}, bf16[256,128]{1,0:T(8,128)(2,1)S(1)}, u32[]{:S(2)}, u32[]{:S(2)}) collective-permute-start(bf16[256,128]{1,0:T(8,128)(2,1)S(1)} %get-tuple-element.52), channel_id=1, source_target_pairs={{0,4},{2,6},{4,0},{6,2},{8,12},{10,14},{12,8},{14,10},{16,20},{18,... | collective-permute-start | bytes 196616 | tf_op jit(solution)/shard_map/ppermute | solution.py:377
  20.4 5.2 %collective-permute-start.9 = (bf16[256,128]{1,0:T(8,128)(2,1)S(1)}, bf16[256,128]{1,0:T(8,128)(2,1)S(1)}, u32[]{:S(2)}, u32[]{:S(2)}) collective-permute-start(bf16[256,128]{1,0:T(8,128)(2,1)S(1)} %get-tuple-element.53), channel_id=1, source_target_pairs={{0,6},{2,4},{4,2},{6,0},{8,14},{10,12},{12,10},{14,8},{16,22},{18,... | collective-permute-start | bytes 196616 | tf_op jit(solution)/shard_map/ppermute | solution.py:377
  27.7 8.8 %collective-permute-start.10 = (bf16[768,128]{1,0:T(8,128)(2,1)S(1)}, bf16[768,128]{1,0:T(8,128)(2,1)S(1)}, u32[]{:S(2)}, u32[]{:S(2)}) collective-permute-start(bf16[768,128]{1,0:T(8,128)(2,1)S(1)} %get-tuple-element.54), channel_id=1, source_target_pairs={{0,6},{2,4},{4,2},{6,0},{8,14},{10,12},{12,10},{14,8},{16,22},{18,... | collective-permute-start | bytes 589832 | tf_op jit(solution)/shard_map/ppermute | solution.py:377
  29.3 9.6 %collective-permute-start.11 = (bf16[768,128]{1,0:T(8,128)(2,1)S(1)}, bf16[768,128]{1,0:T(8,128)(2,1)S(1)}, u32[]{:S(2)}, u32[]{:S(2)}) collective-permute-start(bf16[768,128]{1,0:T(8,128)(2,1)S(1)} %get-tuple-element.55), channel_id=1, source_target_pairs={{0,4},{2,6},{4,0},{6,2},{8,12},{10,14},{12,8},{14,10},{16,20},{18,... | collective-permute-start | bytes 589832 | tf_op jit(solution)/shard_map/ppermute | solution.py:377
  29.6 9.2 %collective-permute-start.12 = (bf16[768,128]{1,0:T(8,128)(2,1)S(1)}, bf16[768,128]{1,0:T(8,128)(2,1)S(1)}, u32[]{:S(2)}, u32[]{:S(2)}) collective-permute-start(bf16[768,128]{1,0:T(8,128)(2,1)S(1)} %get-tuple-element.56), channel_id=1, source_target_pairs={{0,2},{2,0},{4,6},{6,4},{8,10},{10,8},{12,14},{14,12},{16,18},{18,... | collective-permute-start | bytes 589832 | tf_op jit(solution)/shard_map/ppermute | solution.py:377
  43.3 1.6 %collective-permute-start.13 = (bf16[64,2048]{1,0:T(8,128)(2,1)S(1)}, bf16[64,2048]{1,0:T(8,128)(2,1)S(1)}, u32[]{:S(2)}, u32[]{:S(2)}) collective-permute-start(bf16[64,2048]{1,0:T(8,128)(2,1)S(1)} %get-tuple-element.64), channel_id=1, source_target_pairs={{0,1},{1,0},{2,3},{3,2},{4,5},{5,4},{6,7},{7,6},{8,9},{9,8},{10,11... | collective-permute-start | bytes 786440 | tf_op jit(solution)/shard_map/ppermute | solution.py:492

commit v14 on v12

--- a/solution.py
+++ b/solution.py
@@ -67,7 +67,7 @@
 
 def merge_inverse(lower, rows, cols):
     tokens = lower.shape[0]
-    block = 8
+    block = 16
     inverse = jnp.where(rows == cols, 1.0, 0.0).astype(F32)
     first = rows - rows % block
     for step in range(block - 1):
@@ -328,22 +328,31 @@
     turns = most // chunk
     if turns == 1:
         bias = collect(0)
-    for head in range(heads):
-        state = (peak_ref[head], total_ref[head], weighted_ref[head])
+    stack = math.gcd(heads, 2)
+    for first in range(0, heads, stack):
+        some = slice(first, first + stack)
+        moved = moved_ref[some].reshape(stack * tokens, size)
+        state = (
+            peak_ref[some].reshape(stack * tokens, 1),
+            total_ref[some].reshape(stack * tokens, 1),
+            weighted_ref[some].reshape(stack * tokens, size),
+        )
         if turns == 1:
-            _, total, weighted = advance(moved_ref[head], bias, *state)
+            _, total, weighted = advance(moved, bias, *state)
         else:
 
-            def step_of(turn, state, head=head):
-                return advance(moved_ref[head], collect(turn), *state)
+            def step_of(turn, state, moved=moved):
+                return advance(moved, collect(turn), *state)
 
             _, total, weighted = lax.fori_loop(0, turns, step_of, state)
         done = (weighted * (1.0 / total)).astype(BF16)
-        for index in range(tokens // half):
-            at = pl.multiple_of(jnp.where(index == core, half, 0), half)
-            attended_ref[pl.ds(at, half), head * size : (head + 1) * size] = done[
-                index * half : (index + 1) * half
-            ]
+        for head in range(first, first + stack):
+            for index in range(tokens // half):
+                at = pl.multiple_of(jnp.where(index == core, half, 0), half)
+                row = (head - first) * tokens + index * half
+                attended_ref[pl.ds(at, half), head * size : (head + 1) * size] = done[
+                    row : row + half
+                ]
     wide = math.gcd(out_ref.shape[1], 4 * size)
     for at in range(0, out_ref.shape[1], wide):
         part = slice(at, at + wide)

time: 45.1 us -> 44 us (0.976)
  Pallas kernels: 14.9 us -> 13.8 us
    pallas_call x7, Pallas kernels: 14.9 us -> 13.8 us  [call(): pl.pallas_call(kernel, out_shape=out_shape, in_specs=in_specs or [vmem] *...]
  transfers between devices with their start and end apart: 17 -> 17, of which waited for: 4 -> 4; matrix products, arithmetic and copies ran while one was open for 0% -> 0% of each run, Pallas kernels for 18% -> 19%
where the time goes in v14:
time: 44 us; the launch traced here: 43.9 us
  starting transfers between devices  20.9 us (48%)
  Pallas kernels  13.8 us (31%)
  waiting for transfers between devices  7.59 us (17%)
  other arithmetic  0.77 us (2%)
  between operations  0.77 us (2%)
    ppermute x15, starting transfers between devices, swapped(): out[step] = lax.ppermute(values[step], 'ctx', pairs_of(step))  20.4 us
    pallas_call x7, Pallas kernels, call(): pl.pallas_call(kernel, out_shape=out_shape, in_specs=in_specs or [vmem] *...  13.8 us
    ppermute x15, waiting for transfers between devices, swapped(): out[step] = lax.ppermute(values[step], 'ctx', pairs_of(step))  6.07 us
    ppermute x1, waiting for transfers between devices, body(): return kept + lax.ppermute(away, 'head', [(0, 1), (1, 0)])  1.52 us
  transfers between devices with their start and end apart: 17, of which 4 were waited for; matrix products, arithmetic and copies ran while one was open for 0% of the time, Pallas kernels for 19%

profile of v14, /device:TPU:0, one launch (start us, length us, event | category | flops | bytes accessed | tf_op | source)
XLA Modules:
  0.0 43.9 jit_solution(6993484109601206464)
XLA Ops:
  0.0 0.5 %collective-permute-start = (bf16[64,2048]{1,0:T(8,128)(2,1)}, bf16[64,2048]{1,0:T(8,128)(2,1)S(1)}, u32[]{:S(2)}, u32[]{:S(2)}) collective-permute-start(bf16[64,2048]{1,0:T(8,128)(2,1)} %mine_hbm.1), channel_id=1, source_target_pairs={{0,1},{1,0},{2,3},{3,2},{4,5},{5,4},{6,7},{7,6},{8,9},{9,8},{10,11... | collective-permute-start | bytes 786440 | tf_op jit(solution)/shard_map/ppermute | solution.py:373
  1.1 1.5 %shard_map.109 = (bf16[2048,384]{1,0:T(8,128)(2,1)S(1)}, bf16[1,2048]{1,0:T(2,128)(2,1)S(1)}, f32[1,128]{1,0:T(1,128)S(1)}, f32[1,128]{1,0:T(1,128)S(1)}, bf16[64,2048]{1,0:T(8,128)(2,1)S(1)}) custom-call(bf16[2048,128]{1,0:T(8,128)(2,1)} %key_hbm.1, bf16[2048,128]{1,0:T(8,128)(2,1)} %dir_hbm.1, bf16[2048,128]{1,0:T(8,128)(2,1)} %value_hbm.1, ...), custom_call_target="tpu_custom_call" | custom-call | bytes 3145728 | tf_op jit(solution)/shard_map/pallas_call | solution.py:21
  2.7 2.3 %shard_map.110 = (bf16[128,2048]{1,0:T(8,128)(2,1)S(1)}, f32[128,128]{1,0:T(8,128)S(1)}, bf16[128,128]{1,0:T(8,128)(2,1)S(1)}, f32[128,128]{1,0:T(8,128)S(1)}, f...) custom-call(s32[1]{0:T(128)} %bitcast.1.core_ref, ...), custom_call_target="tpu_custom_call" | custom-call | flops 201326592 | bytes 2097152 | tf_op jit(solution)/shard_map/pallas_call | solution.py:21
  5.0 3.5 %collective-permute-start.1 = (f32[128,128]{1,0:T(8,128)S(1)}, f32[128,128]{1,0:T(8,128)S(1)}, u32[]{:S(2)}, u32[]{:S(2)}) collective-permute-start(f32[128,128]{1,0:T(8,128)S(1)} %get-tuple-element.41.refs_3_), channel_id=1, source_target_pairs={{0,6},{2,4},{4,2},{6,0},{8,14},{10,12},{12,10},{14,8},{16,22},{18,... | collective-permute-start | bytes 196616 | tf_op jit(solution)/shard_map/ppermute | solution.py:387
  8.5 0.5 %collective-permute-start.2 = (f32[128,128]{1,0:T(8,128)S(1)}, f32[128,128]{1,0:T(8,128)S(1)}, u32[]{:S(2)}, u32[]{:S(2)}) collective-permute-start(f32[128,128]{1,0:T(8,128)S(1)} %get-tuple-element.41.refs_3_), channel_id=1, source_target_pairs={{0,4},{2,6},{4,0},{6,2},{8,12},{10,14},{12,8},{14,10},{16,20},{18,... | collective-permute-start | bytes 196616 | tf_op jit(solution)/shard_map/ppermute | solution.py:387
  9.1 4.0 %collective-permute-start.4 = (bf16[128,128]{1,0:T(8,128)(2,1)S(1)}, bf16[128,128]{1,0:T(8,128)(2,1)S(1)}, u32[]{:S(2)}, u32[]{:S(2)}) collective-permute-start(bf16[128,128]{1,0:T(8,128)(2,1)S(1)} %get-tuple-element.43.refs_3_.val_ref), channel_id=1, source_target_pairs={{0,24},{2,26},{4,28},{6,30},{8,16},{10,18},{12,20},{14,22},{16,8},... | collective-permute-start | bytes 98312 | tf_op jit(solution)/shard_map/ppermute | solution.py:387
  13.2 0.6 %collective-permute-start.6 = (bf16[128,128]{1,0:T(8,128)(2,1)S(1)}, bf16[128,128]{1,0:T(8,128)(2,1)S(1)}, u32[]{:S(2)}, u32[]{:S(2)}) collective-permute-start(bf16[128,128]{1,0:T(8,128)(2,1)S(1)} %get-tuple-element.43.refs_3_.val_ref), channel_id=1, source_target_pairs={{0,8},{2,10},{4,12},{6,14},{8,0},{10,2},{12,4},{14,6},{16,24},{18,... | collective-permute-start | bytes 98312 | tf_op jit(solution)/shard_map/ppermute | solution.py:387
  13.7 0.5 %shard_map.111 = (bf16[512,128]{1,0:T(8,128)(2,1)S(1)}, f32[4,128,128]{2,1,0:T(8,128)S(1)}, bf16[128,128]{1,0:T(8,128)(2,1)S(1)}, bf16[128,128]{1,0:T(8,128)(2,1...) custom-call(s32[1]{0:T(128)} %bitcast.place_ref, f32[128,128]{1,0:T(8,128)S(1)} %get-tuple-element.40.exit_ref, ...), custom_call_target="tpu_custom_call" | custom-call | flops 100663296 | bytes 1000000 | tf_op jit(solution)/shard_map/pallas_call | solution.py:21
  14.2 3.9 %collective-permute-start.7 = (bf16[512,128]{1,0:T(8,128)(2,1)S(1)}, bf16[512,128]{1,0:T(8,128)(2,1)S(1)}, u32[]{:S(2)}, u32[]{:S(2)}) collective-permute-start(bf16[512,128]{1,0:T(8,128)(2,1)S(1)} %get-tuple-element.45.refs_3_), channel_id=1, source_target_pairs={{0,24},{2,26},{4,28},{6,30},{8,16},{10,18},{12,20},{14,22},{16,8},... | collective-permute-start | bytes 393224 | tf_op jit(solution)/shard_map/ppermute | solution.py:387
  18.1 0.6 %collective-permute-start.9 = (bf16[512,128]{1,0:T(8,128)(2,1)S(1)}, bf16[512,128]{1,0:T(8,128)(2,1)S(1)}, u32[]{:S(2)}, u32[]{:S(2)}) collective-permute-start(bf16[512,128]{1,0:T(8,128)(2,1)S(1)} %get-tuple-element.45.refs_3_), channel_id=1, source_target_pairs={{0,8},{2,10},{4,12},{6,14},{8,0},{10,2},{12,4},{14,6},{16,24},{18,... | collective-permute-start | bytes 393224 | tf_op jit(solution)/shard_map/ppermute | solution.py:387
  18.8 3.6 %collective-permute-done.5.refs_1_ = bf16[128,128]{1,0:T(8,128)(2,1)S(1)} collective-permute-done((bf16[128,128]{1,0:T(8,128)(2,1)S(1)}, bf16[128,128]{1,0:T(8,128)(2,1)S(1)}, u32[]{:S(2)}, u32[]{:S(2)}) %collective-permute-start.5) | collective-permute-done | bytes 32800 | tf_op jit(solution)/shard_map/ppermute | solution.py:387
  22.3 1.3 %shard_map.112 = (bf16[512,128]{1,0:T(8,128)(2,1)S(1)}, s32[1]{0:T(128)}) custom-call(s32[1]{0:T(128)} %bitcast.place_ref, s32[16]{0:T(128)S(1)} %bitcast.5, f32[4,128,128]{2,1,0:T(8,128)S(1)} %get-tuple-element.42.after_ref.refs_4_, bf16[128,128]{1,0:T(8,128)(2,1)S(1)} %collective-permute-done.4.refs_0_, ...), custom_call_target="tpu_custom_call" | custom-call | bytes 1000000 | tf_op jit(solution)/shard_map/pallas_call | solution.py:21
  23.7 2.4 %collective-permute-start.13 = (bf16[512,128]{1,0:T(8,128)(2,1)S(1)}, bf16[512,128]{1,0:T(8,128)(2,1)S(1)}, u32[]{:S(2)}, u32[]{:S(2)}) collective-permute-start(bf16[512,128]{1,0:T(8,128)(2,1)S(1)} %get-tuple-element.54.refs_7_), channel_id=1, source_target_pairs={{0,6},{2,4},{4,2},{6,0},{8,14},{10,12},{12,10},{14,8},{16,22},{18,... | collective-permute-start | bytes 393224 | tf_op jit(solution)/shard_map/ppermute | solution.py:387
  26.1 1.2 %collective-permute-start.15 = (bf16[512,128]{1,0:T(8,128)(2,1)S(1)}, bf16[512,128]{1,0:T(8,128)(2,1)S(1)}, u32[]{:S(2)}, u32[]{:S(2)}) collective-permute-start(bf16[512,128]{1,0:T(8,128)(2,1)S(1)} %get-tuple-element.54.refs_7_), channel_id=1, source_target_pairs={{0,2},{2,0},{4,6},{6,4},{8,10},{10,8},{12,14},{14,12},{16,18},{18,... | collective-permute-start | bytes 393224 | tf_op jit(solution)/shard_map/ppermute | solution.py:387
  27.2 1.3 %collective-permute-done.8.refs_1_ = bf16[512,128]{1,0:T(8,128)(2,1)S(1)} collective-permute-done((bf16[512,128]{1,0:T(8,128)(2,1)S(1)}, bf16[512,128]{1,0:T(8,128)(2,1)S(1)}, u32[]{:S(2)}, u32[]{:S(2)}) %collective-permute-start.8) | collective-permute-done | bytes 131104 | tf_op jit(solution)/shard_map/ppermute | solution.py:387
  28.5 0.8 %shard_map.113 = (bf16[512,128]{1,0:T(8,128)(2,1)S(1)}, bf16[512,128]{1,0:T(8,128)(2,1)S(1)}, bf16[512,128]{1,0:T(8,128)(2,1)S(1)}, bf16[512,128]{1,0:T(8,128)(2,1)S(1)}) custom-call(s32[1]{0:T(128)} %bitcast.place_ref, bf16[512,128]{1,0:T(8,128)(2,1)S(1)} %collective-permute-done.7.refs_0_, bf16[512,128]{1,0:T(8,128)(2,1)S(1)} %collective-permute-done.8.refs_1_, ...), custom_call_target="tpu_custom_call" | custom-call | flops 201326592 | bytes 1000000 | tf_op jit(solution)/shard_map/pallas_call | solution.py:21
  29.4 2.5 %collective-permute-start.10 = (bf16[512,128]{1,0:T(8,128)(2,1)S(1)}, bf16[512,128]{1,0:T(8,128)(2,1)S(1)}, u32[]{:S(2)}, u32[]{:S(2)}) collective-permute-start(bf16[512,128]{1,0:T(8,128)(2,1)S(1)} %get-tuple-element.50), channel_id=1, source_target_pairs={{0,6},{2,4},{4,2},{6,0},{8,14},{10,12},{12,10},{14,8},{16,22},{18,... | collective-permute-start | bytes 393224 | tf_op jit(solution)/shard_map/ppermute | solution.py:387
  31.9 0.6 %collective-permute-start.11 = (bf16[512,128]{1,0:T(8,128)(2,1)S(1)}, bf16[512,128]{1,0:T(8,128)(2,1)S(1)}, u32[]{:S(2)}, u32[]{:S(2)}) collective-permute-start(bf16[512,128]{1,0:T(8,128)(2,1)S(1)} %get-tuple-element.51), channel_id=1, source_target_pairs={{0,4},{2,6},{4,0},{6,2},{8,12},{10,14},{12,8},{14,10},{16,20},{18,... | collective-permute-start | bytes 393224 | tf_op jit(solution)/shard_map/ppermute | solution.py:387
  32.5 0.4 collective-permute-start.12
  32.9 3.9 %shard_map.114 = (bf16[8,128,128]{2,1,0:T(8,128)(2,1)S(1)}, f32[8,128,128]{2,1,0:T(8,128)S(1)}, f32[8,128,1]{2,1,0:T(8,128)S(1)}, f32[8,128,1]{2,1,0:T(8,128)S(1)}) custom-call(bf16[128,2048]{1,0:T(8,128)(2,1)S(1)} %get-tuple-element.55.rows_ref, bf16[2048,1024]{1,0:T(8,128)(2,1)} %weight_hbm.1, f32[1,128]{1,0:T(1,128)S(1)} %get-tuple-element.56.gain_ref, ...), custom_call_target="tpu_custom_call" | custom-call | flops 1073741824 | bytes 16777216 | tf_op jit(solution)/shard_map/pallas_call | solution.py:21
  36.9 1.2 %collective-permute-done.11.refs_1_ = bf16[512,128]{1,0:T(8,128)(2,1)S(1)} collective-permute-done((bf16[512,128]{1,0:T(8,128)(2,1)S(1)}, bf16[512,128]{1,0:T(8,128)(2,1)S(1)}, u32[]{:S(2)}, u32[]{:S(2)}) %collective-permute-start.11) | collective-permute-done | bytes 131104 | tf_op jit(solution)/shard_map/ppermute | solution.py:387
  38.1 3.4 %shard_map.115 = (bf16[64,2048]{1,0:T(8,128)(2,1)S(1)}, bf16[64,2048]{1,0:T(8,128)(2,1)S(1)}) custom-call(s32[1]{0:T(128)} %bitcast.place_ref, s32[1]{0:T(128)} %bitcast.1.core_ref, s32[1]{0:T(128)} %get-tuple-element.44.table_ref, bf16[512,128]{1,0:T(8,128)(2,1)S(1)} %collective-permute-done.10.refs_0_, ...), custom_call_target="tpu_custom_call" | custom-call | flops 536870912 | bytes 4000000 | tf_op jit(solution)/shard_map/pallas_call | solution.py:21
  41.6 1.5 %collective-permute-done.16 = bf16[64,2048]{1,0:T(8,128)(2,1)S(1)} collective-permute-done((bf16[64,2048]{1,0:T(8,128)(2,1)S(1)}, bf16[64,2048]{1,0:T(8,128)(2,1)S(1)}, u32[]{:S(2)}, u32[]{:S(2)}) %collective-permute-start.16) | collective-permute-done | bytes 262176 | tf_op jit(solution)/shard_map/ppermute | solution.py:510
  43.1 0.8 %add.3 = bf16[64,2048]{1,0:T(8,128)(2,1)} add(bf16[64,2048]{1,0:T(8,128)(2,1)S(1)} %get-tuple-element.65, bf16[64,2048]{1,0:T(8,128)(2,1)S(1)} %collective-permute-done.16) | non-fusion elementwise | flops 131072 | bytes 786432 | tf_op jit(solution)/shard_map/add | solution.py:510
  (22 shorter events, 0.3 us)
Async XLA Ops:
  0.0 22.3 %copy-start.1 = (s32[1,16]{1,0:T(1,128)S(1)}, s32[1,16]{1,0:T(1,128)}, u32[]{:S(2)}) copy-start(s32[1,16]{1,0:T(1,128)} %param.21) | copy-start | bytes 196
  0.0 2.6 %collective-permute-start = (bf16[64,2048]{1,0:T(8,128)(2,1)}, bf16[64,2048]{1,0:T(8,128)(2,1)S(1)}, u32[]{:S(2)}, u32[]{:S(2)}) collective-permute-start(bf16[64,2048]{1,0:T(8,128)(2,1)} %mine_hbm.1), channel_id=1, source_target_pairs={{0,1},{1,0},{2,3},{3,2},{4,5},{5,4},{6,7},{7,6},{8,9},{9,8},{10,11... | collective-permute-start | bytes 786440 | tf_op jit(solution)/shard_map/ppermute | solution.py:373
  5.0 8.2 %collective-permute-start.1 = (f32[128,128]{1,0:T(8,128)S(1)}, f32[128,128]{1,0:T(8,128)S(1)}, u32[]{:S(2)}, u32[]{:S(2)}) collective-permute-start(f32[128,128]{1,0:T(8,128)S(1)} %get-tuple-element.41.refs_3_), channel_id=1, source_target_pairs={{0,6},{2,4},{4,2},{6,0},{8,14},{10,12},{12,10},{14,8},{16,22},{18,... | collective-permute-start | bytes 196616 | tf_op jit(solution)/shard_map/ppermute | solution.py:387
  8.5 5.2 %collective-permute-start.2 = (f32[128,128]{1,0:T(8,128)S(1)}, f32[128,128]{1,0:T(8,128)S(1)}, u32[]{:S(2)}, u32[]{:S(2)}) collective-permute-start(f32[128,128]{1,0:T(8,128)S(1)} %get-tuple-element.41.refs_3_), channel_id=1, source_target_pairs={{0,4},{2,6},{4,0},{6,2},{8,12},{10,14},{12,8},{14,10},{16,20},{18,... | collective-permute-start | bytes 196616 | tf_op jit(solution)/shard_map/ppermute | solution.py:387
  9.0 4.7 %collective-permute-start.3 = (f32[128,128]{1,0:T(8,128)S(1)}, f32[128,128]{1,0:T(8,128)S(1)}, u32[]{:S(2)}, u32[]{:S(2)}) collective-permute-start(f32[128,128]{1,0:T(8,128)S(1)} %get-tuple-element.41.refs_3_), channel_id=1, source_target_pairs={{0,2},{2,0},{4,6},{6,4},{8,10},{10,8},{12,14},{14,12},{16,18},{18,... | collective-permute-start | bytes 196616 | tf_op jit(solution)/shard_map/ppermute | solution.py:387
  9.1 9.0 %collective-permute-start.4 = (bf16[128,128]{1,0:T(8,128)(2,1)S(1)}, bf16[128,128]{1,0:T(8,128)(2,1)S(1)}, u32[]{:S(2)}, u32[]{:S(2)}) collective-permute-start(bf16[128,128]{1,0:T(8,128)(2,1)S(1)} %get-tuple-element.43.refs_3_.val_ref), channel_id=1, source_target_pairs={{0,24},{2,26},{4,28},{6,30},{8,16},{10,18},{12,20},{14,22},{16,8},... | collective-permute-start | bytes 98312 | tf_op jit(solution)/shard_map/ppermute | solution.py:387
  13.1 9.2 %collective-permute-start.5 = (bf16[128,128]{1,0:T(8,128)(2,1)S(1)}, bf16[128,128]{1,0:T(8,128)(2,1)S(1)}, u32[]{:S(2)}, u32[]{:S(2)}) collective-permute-start(bf16[128,128]{1,0:T(8,128)(2,1)S(1)} %get-tuple-element.43.refs_3_.val_ref), channel_id=1, source_target_pairs={{0,16},{2,18},{4,20},{6,22},{8,24},{10,26},{12,28},{14,30},{16,0},... | collective-permute-start | bytes 98312 | tf_op jit(solution)/shard_map/ppermute | solution.py:387
  13.2 9.2 %collective-permute-start.6 = (bf16[128,128]{1,0:T(8,128)(2,1)S(1)}, bf16[128,128]{1,0:T(8,128)(2,1)S(1)}, u32[]{:S(2)}, u32[]{:S(2)}) collective-permute-start(bf16[128,128]{1,0:T(8,128)(2,1)S(1)} %get-tuple-element.43.refs_3_.val_ref), channel_id=1, source_target_pairs={{0,8},{2,10},{4,12},{6,14},{8,0},{10,2},{12,4},{14,6},{16,24},{18,... | collective-permute-start | bytes 98312 | tf_op jit(solution)/shard_map/ppermute | solution.py:387
  13.7 24.4 %copy-start = (bf16[1024,2048]{1,0:T(8,128)(2,1)S(1)}, bf16[1024,2048]{1,0:T(8,128)(2,1)}, u32[]{:S(2)}) copy-start(bf16[1024,2048]{1,0:T(8,128)(2,1)} %refs_12_.1) | copy-start | bytes 12582916
  14.2 11.8 %collective-permute-start.7 = (bf16[512,128]{1,0:T(8,128)(2,1)S(1)}, bf16[512,128]{1,0:T(8,128)(2,1)S(1)}, u32[]{:S(2)}, u32[]{:S(2)}) collective-permute-start(bf16[512,128]{1,0:T(8,128)(2,1)S(1)} %get-tuple-element.45.refs_3_), channel_id=1, source_target_pairs={{0,24},{2,26},{4,28},{6,30},{8,16},{10,18},{12,20},{14,22},{16,8},... | collective-permute-start | bytes 393224 | tf_op jit(solution)/shard_map/ppermute | solution.py:387
  18.1 10.4 %collective-permute-start.8 = (bf16[512,128]{1,0:T(8,128)(2,1)S(1)}, bf16[512,128]{1,0:T(8,128)(2,1)S(1)}, u32[]{:S(2)}, u32[]{:S(2)}) collective-permute-start(bf16[512,128]{1,0:T(8,128)(2,1)S(1)} %get-tuple-element.45.refs_3_), channel_id=1, source_target_pairs={{0,16},{2,18},{4,20},{6,22},{8,24},{10,26},{12,28},{14,30},{16,0},... | collective-permute-start | bytes 393224 | tf_op jit(solution)/shard_map/ppermute | solution.py:387
  18.1 10.4 %collective-permute-start.9 = (bf16[512,128]{1,0:T(8,128)(2,1)S(1)}, bf16[512,128]{1,0:T(8,128)(2,1)S(1)}, u32[]{:S(2)}, u32[]{:S(2)}) collective-permute-start(bf16[512,128]{1,0:T(8,128)(2,1)S(1)} %get-tuple-element.45.refs_3_), channel_id=1, source_target_pairs={{0,8},{2,10},{4,12},{6,14},{8,0},{10,2},{12,4},{14,6},{16,24},{18,... | collective-permute-start | bytes 393224 | tf_op jit(solution)/shard_map/ppermute | solution.py:387
  23.7 8.8 %collective-permute-start.13 = (bf16[512,128]{1,0:T(8,128)(2,1)S(1)}, bf16[512,128]{1,0:T(8,128)(2,1)S(1)}, u32[]{:S(2)}, u32[]{:S(2)}) collective-permute-start(bf16[512,128]{1,0:T(8,128)(2,1)S(1)} %get-tuple-element.54.refs_7_), channel_id=1, source_target_pairs={{0,6},{2,4},{4,2},{6,0},{8,14},{10,12},{12,10},{14,8},{16,22},{18,... | collective-permute-start | bytes 393224 | tf_op jit(solution)/shard_map/ppermute | solution.py:387
  26.1 10.8 %collective-permute-start.14 = (bf16[512,128]{1,0:T(8,128)(2,1)S(1)}, bf16[512,128]{1,0:T(8,128)(2,1)S(1)}, u32[]{:S(2)}, u32[]{:S(2)}) collective-permute-start(bf16[512,128]{1,0:T(8,128)(2,1)S(1)} %get-tuple-element.54.refs_7_), channel_id=1, source_target_pairs={{0,4},{2,6},{4,0},{6,2},{8,12},{10,14},{12,8},{14,10},{16,20},{18,... | collective-permute-start | bytes 393224 | tf_op jit(solution)/shard_map/ppermute | solution.py:387
  26.1 10.8 %collective-permute-start.15 = (bf16[512,128]{1,0:T(8,128)(2,1)S(1)}, bf16[512,128]{1,0:T(8,128)(2,1)S(1)}, u32[]{:S(2)}, u32[]{:S(2)}) collective-permute-start(bf16[512,128]{1,0:T(8,128)(2,1)S(1)} %get-tuple-element.54.refs_7_), channel_id=1, source_target_pairs={{0,2},{2,0},{4,6},{6,4},{8,10},{10,8},{12,14},{14,12},{16,18},{18,... | collective-permute-start | bytes 393224 | tf_op jit(solution)/shard_map/ppermute | solution.py:387
  29.4 7.5 %collective-permute-start.10 = (bf16[512,128]{1,0:T(8,128)(2,1)S(1)}, bf16[512,128]{1,0:T(8,128)(2,1)S(1)}, u32[]{:S(2)}, u32[]{:S(2)}) collective-permute-start(bf16[512,128]{1,0:T(8,128)(2,1)S(1)} %get-tuple-element.50), channel_id=1, source_target_pairs={{0,6},{2,4},{4,2},{6,0},{8,14},{10,12},{12,10},{14,8},{16,22},{18,... | collective-permute-start | bytes 393224 | tf_op jit(solution)/shard_map/ppermute | solution.py:387
  31.9 6.2 %collective-permute-start.11 = (bf16[512,128]{1,0:T(8,128)(2,1)S(1)}, bf16[512,128]{1,0:T(8,128)(2,1)S(1)}, u32[]{:S(2)}, u32[]{:S(2)}) collective-permute-start(bf16[512,128]{1,0:T(8,128)(2,1)S(1)} %get-tuple-element.51), channel_id=1, source_target_pairs={{0,4},{2,6},{4,0},{6,2},{8,12},{10,14},{12,8},{14,10},{16,20},{18,... | collective-permute-start | bytes 393224 | tf_op jit(solution)/shard_map/ppermute | solution.py:387
  32.5 5.6 %collective-permute-start.12 = (bf16[512,128]{1,0:T(8,128)(2,1)S(1)}, bf16[512,128]{1,0:T(8,128)(2,1)S(1)}, u32[]{:S(2)}, u32[]{:S(2)}) collective-permute-start(bf16[512,128]{1,0:T(8,128)(2,1)S(1)} %get-tuple-element.52), channel_id=1, source_target_pairs={{0,2},{2,0},{4,6},{6,4},{8,10},{10,8},{12,14},{14,12},{16,18},{18,... | collective-permute-start | bytes 393224 | tf_op jit(solution)/shard_map/ppermute | solution.py:387
  41.5 1.6 %collective-permute-start.16 = (bf16[64,2048]{1,0:T(8,128)(2,1)S(1)}, bf16[64,2048]{1,0:T(8,128)(2,1)S(1)}, u32[]{:S(2)}, u32[]{:S(2)}) collective-permute-start(bf16[64,2048]{1,0:T(8,128)(2,1)S(1)} %get-tuple-element.66), channel_id=1, source_target_pairs={{0,1},{1,0},{2,3},{3,2},{4,5},{5,4},{6,7},{7,6},{8,9},{9,8},{10,11... | collective-permute-start | bytes 786440 | tf_op jit(solution)/shard_map/ppermute | solution.py:510

commit v15 on v14

--- a/solution.py
+++ b/solution.py
@@ -271,10 +271,12 @@
         product = whole
         brought.append(jnp.where(index + 1 < mine, dot3(keys, product), keys))
     keys = jnp.concatenate(brought[::-1], axis=0)
+    count, size = keys.shape
+    ways = [starts_ref[target_of(member, step, group)] for step in range(group)]
+    spread = dot3(keys, jnp.concatenate(ways, axis=1)).astype(BF16)
     for step in range(group):
-        start = starts_ref[target_of(member, step, group)]
-        far_refs[step][: (groups - 1) * tokens] = dot3(keys, start).astype(BF16)
-        far_refs[step][(groups - 1) * tokens :] = near_refs[step][...]
+        far_refs[step][:count] = spread[:, step * size : (step + 1) * size]
+        far_refs[step][count:] = near_refs[step][...]
 
 
 def attend_kernel(group, segments, most, place_ref, core_ref, table_ref, *refs):
@@ -328,7 +330,7 @@
     turns = most // chunk
     if turns == 1:
         bias = collect(0)
-    stack = math.gcd(heads, 2)
+    stack = math.gcd(heads, 4)
     for first in range(0, heads, stack):
         some = slice(first, first + stack)
         moved = moved_ref[some].reshape(stack * tokens, size)

time: 44 us -> 43.6 us (level)
  Pallas kernels: 13.8 us -> 13.3 us
    pallas_call x7, Pallas kernels: 13.8 us -> 13.3 us  [call(): pl.pallas_call(kernel, out_shape=out_shape, in_specs=in_specs or [vmem] *...]
where the time goes in v15:
time: 43.6 us; the launch traced here: 43.4 us
  starting transfers between devices  20.9 us (48%)
  Pallas kernels  13.3 us (31%)
  waiting for transfers between devices  7.7 us (18%)
  other arithmetic  0.77 us (2%)
  between operations  0.76 us (2%)
    ppermute x15, starting transfers between devices, swapped(): out[step] = lax.ppermute(values[step], 'ctx', pairs_of(step))  20.4 us
    pallas_call x7, Pallas kernels, call(): pl.pallas_call(kernel, out_shape=out_shape, in_specs=in_specs or [vmem] *...  13.3 us
    ppermute x15, waiting for transfers between devices, swapped(): out[step] = lax.ppermute(values[step], 'ctx', pairs_of(step))  6.18 us
    ppermute x1, waiting for transfers between devices, body(): return kept + lax.ppermute(away, 'head', [(0, 1), (1, 0)])  1.52 us
  transfers between devices with their start and end apart: 17, of which 4 were waited for; matrix products, arithmetic and copies ran while one was open for 0% of the time, Pallas kernels for 19%

profile of v15, /device:TPU:0, one launch (start us, length us, event | category | flops | bytes accessed | tf_op | source)
XLA Modules:
  0.0 43.4 jit_solution(12862177424871920480)
XLA Ops:
  0.0 0.5 %collective-permute-start = (bf16[64,2048]{1,0:T(8,128)(2,1)}, bf16[64,2048]{1,0:T(8,128)(2,1)S(1)}, u32[]{:S(2)}, u32[]{:S(2)}) collective-permute-start(bf16[64,2048]{1,0:T(8,128)(2,1)} %mine_hbm.1), channel_id=1, source_target_pairs={{0,1},{1,0},{2,3},{3,2},{4,5},{5,4},{6,7},{7,6},{8,9},{9,8},{10,11... | collective-permute-start | bytes 786440 | tf_op jit(solution)/shard_map/ppermute | solution.py:375
  1.1 1.5 %shard_map.109 = (bf16[2048,384]{1,0:T(8,128)(2,1)S(1)}, bf16[1,2048]{1,0:T(2,128)(2,1)S(1)}, f32[1,128]{1,0:T(1,128)S(1)}, f32[1,128]{1,0:T(1,128)S(1)}, bf16[64,2048]{1,0:T(8,128)(2,1)S(1)}) custom-call(bf16[2048,128]{1,0:T(8,128)(2,1)} %key_hbm.1, bf16[2048,128]{1,0:T(8,128)(2,1)} %dir_hbm.1, bf16[2048,128]{1,0:T(8,128)(2,1)} %value_hbm.1, ...), custom_call_target="tpu_custom_call" | custom-call | bytes 3145728 | tf_op jit(solution)/shard_map/pallas_call | solution.py:21
  2.7 2.3 %shard_map.110 = (bf16[128,2048]{1,0:T(8,128)(2,1)S(1)}, f32[128,128]{1,0:T(8,128)S(1)}, bf16[128,128]{1,0:T(8,128)(2,1)S(1)}, f32[128,128]{1,0:T(8,128)S(1)}, f...) custom-call(s32[1]{0:T(128)} %bitcast.1.core_ref, ...), custom_call_target="tpu_custom_call" | custom-call | flops 201326592 | bytes 2097152 | tf_op jit(solution)/shard_map/pallas_call | solution.py:21
  5.0 3.5 %collective-permute-start.1 = (f32[128,128]{1,0:T(8,128)S(1)}, f32[128,128]{1,0:T(8,128)S(1)}, u32[]{:S(2)}, u32[]{:S(2)}) collective-permute-start(f32[128,128]{1,0:T(8,128)S(1)} %get-tuple-element.41.refs_3_), channel_id=1, source_target_pairs={{0,6},{2,4},{4,2},{6,0},{8,14},{10,12},{12,10},{14,8},{16,22},{18,... | collective-permute-start | bytes 196616 | tf_op jit(solution)/shard_map/ppermute | solution.py:389
  8.5 0.5 %collective-permute-start.2 = (f32[128,128]{1,0:T(8,128)S(1)}, f32[128,128]{1,0:T(8,128)S(1)}, u32[]{:S(2)}, u32[]{:S(2)}) collective-permute-start(f32[128,128]{1,0:T(8,128)S(1)} %get-tuple-element.41.refs_3_), channel_id=1, source_target_pairs={{0,4},{2,6},{4,0},{6,2},{8,12},{10,14},{12,8},{14,10},{16,20},{18,... | collective-permute-start | bytes 196616 | tf_op jit(solution)/shard_map/ppermute | solution.py:389
  9.1 4.0 %collective-permute-start.4 = (bf16[128,128]{1,0:T(8,128)(2,1)S(1)}, bf16[128,128]{1,0:T(8,128)(2,1)S(1)}, u32[]{:S(2)}, u32[]{:S(2)}) collective-permute-start(bf16[128,128]{1,0:T(8,128)(2,1)S(1)} %get-tuple-element.43.refs_3_.val_ref), channel_id=1, source_target_pairs={{0,24},{2,26},{4,28},{6,30},{8,16},{10,18},{12,20},{14,22},{16,8},... | collective-permute-start | bytes 98312 | tf_op jit(solution)/shard_map/ppermute | solution.py:389
  13.2 0.6 %collective-permute-start.6 = (bf16[128,128]{1,0:T(8,128)(2,1)S(1)}, bf16[128,128]{1,0:T(8,128)(2,1)S(1)}, u32[]{:S(2)}, u32[]{:S(2)}) collective-permute-start(bf16[128,128]{1,0:T(8,128)(2,1)S(1)} %get-tuple-element.43.refs_3_.val_ref), channel_id=1, source_target_pairs={{0,8},{2,10},{4,12},{6,14},{8,0},{10,2},{12,4},{14,6},{16,24},{18,... | collective-permute-start | bytes 98312 | tf_op jit(solution)/shard_map/ppermute | solution.py:389
  13.7 0.5 %shard_map.111 = (bf16[512,128]{1,0:T(8,128)(2,1)S(1)}, f32[4,128,128]{2,1,0:T(8,128)S(1)}, bf16[128,128]{1,0:T(8,128)(2,1)S(1)}, bf16[128,128]{1,0:T(8,128)(2,1...) custom-call(s32[1]{0:T(128)} %bitcast.place_ref, f32[128,128]{1,0:T(8,128)S(1)} %get-tuple-element.40.exit_ref, ...), custom_call_target="tpu_custom_call" | custom-call | flops 100663296 | bytes 1000000 | tf_op jit(solution)/shard_map/pallas_call | solution.py:21
  14.2 3.9 %collective-permute-start.7 = (bf16[512,128]{1,0:T(8,128)(2,1)S(1)}, bf16[512,128]{1,0:T(8,128)(2,1)S(1)}, u32[]{:S(2)}, u32[]{:S(2)}) collective-permute-start(bf16[512,128]{1,0:T(8,128)(2,1)S(1)} %get-tuple-element.45.refs_3_), channel_id=1, source_target_pairs={{0,24},{2,26},{4,28},{6,30},{8,16},{10,18},{12,20},{14,22},{16,8},... | collective-permute-start | bytes 393224 | tf_op jit(solution)/shard_map/ppermute | solution.py:389
  18.1 0.6 %collective-permute-start.9 = (bf16[512,128]{1,0:T(8,128)(2,1)S(1)}, bf16[512,128]{1,0:T(8,128)(2,1)S(1)}, u32[]{:S(2)}, u32[]{:S(2)}) collective-permute-start(bf16[512,128]{1,0:T(8,128)(2,1)S(1)} %get-tuple-element.45.refs_3_), channel_id=1, source_target_pairs={{0,8},{2,10},{4,12},{6,14},{8,0},{10,2},{12,4},{14,6},{16,24},{18,... | collective-permute-start | bytes 393224 | tf_op jit(solution)/shard_map/ppermute | solution.py:389
  18.8 3.6 %collective-permute-done.5.refs_1_ = bf16[128,128]{1,0:T(8,128)(2,1)S(1)} collective-permute-done((bf16[128,128]{1,0:T(8,128)(2,1)S(1)}, bf16[128,128]{1,0:T(8,128)(2,1)S(1)}, u32[]{:S(2)}, u32[]{:S(2)}) %collective-permute-start.5) | collective-permute-done | bytes 32800 | tf_op jit(solution)/shard_map/ppermute | solution.py:389
  22.3 1.3 %shard_map.112 = (bf16[512,128]{1,0:T(8,128)(2,1)S(1)}, s32[1]{0:T(128)}) custom-call(s32[1]{0:T(128)} %bitcast.place_ref, s32[16]{0:T(128)S(1)} %bitcast.5, f32[4,128,128]{2,1,0:T(8,128)S(1)} %get-tuple-element.42.after_ref.refs_4_, bf16[128,128]{1,0:T(8,128)(2,1)S(1)} %collective-permute-done.4.refs_0_, ...), custom_call_target="tpu_custom_call" | custom-call | bytes 1000000 | tf_op jit(solution)/shard_map/pallas_call | solution.py:21
  23.7 2.4 %collective-permute-start.13 = (bf16[512,128]{1,0:T(8,128)(2,1)S(1)}, bf16[512,128]{1,0:T(8,128)(2,1)S(1)}, u32[]{:S(2)}, u32[]{:S(2)}) collective-permute-start(bf16[512,128]{1,0:T(8,128)(2,1)S(1)} %get-tuple-element.54.refs_7_), channel_id=1, source_target_pairs={{0,6},{2,4},{4,2},{6,0},{8,14},{10,12},{12,10},{14,8},{16,22},{18,... | collective-permute-start | bytes 393224 | tf_op jit(solution)/shard_map/ppermute | solution.py:389
  26.1 1.2 %collective-permute-start.15 = (bf16[512,128]{1,0:T(8,128)(2,1)S(1)}, bf16[512,128]{1,0:T(8,128)(2,1)S(1)}, u32[]{:S(2)}, u32[]{:S(2)}) collective-permute-start(bf16[512,128]{1,0:T(8,128)(2,1)S(1)} %get-tuple-element.54.refs_7_), channel_id=1, source_target_pairs={{0,2},{2,0},{4,6},{6,4},{8,10},{10,8},{12,14},{14,12},{16,18},{18,... | collective-permute-start | bytes 393224 | tf_op jit(solution)/shard_map/ppermute | solution.py:389
  27.2 1.3 %collective-permute-done.8.refs_1_ = bf16[512,128]{1,0:T(8,128)(2,1)S(1)} collective-permute-done((bf16[512,128]{1,0:T(8,128)(2,1)S(1)}, bf16[512,128]{1,0:T(8,128)(2,1)S(1)}, u32[]{:S(2)}, u32[]{:S(2)}) %collective-permute-start.8) | collective-permute-done | bytes 131104 | tf_op jit(solution)/shard_map/ppermute | solution.py:389
  28.5 0.7 %shard_map.113 = (bf16[512,128]{1,0:T(8,128)(2,1)S(1)}, bf16[512,128]{1,0:T(8,128)(2,1)S(1)}, bf16[512,128]{1,0:T(8,128)(2,1)S(1)}, bf16[512,128]{1,0:T(8,128)(2,1)S(1)}) custom-call(s32[1]{0:T(128)} %bitcast.place_ref, bf16[512,128]{1,0:T(8,128)(2,1)S(1)} %collective-permute-done.7.refs_0_, bf16[512,128]{1,0:T(8,128)(2,1)S(1)} %collective-permute-done.8.refs_1_, ...), custom_call_target="tpu_custom_call" | custom-call | flops 201326592 | bytes 1000000 | tf_op jit(solution)/shard_map/pallas_call | solution.py:21
  29.3 2.5 %collective-permute-start.10 = (bf16[512,128]{1,0:T(8,128)(2,1)S(1)}, bf16[512,128]{1,0:T(8,128)(2,1)S(1)}, u32[]{:S(2)}, u32[]{:S(2)}) collective-permute-start(bf16[512,128]{1,0:T(8,128)(2,1)S(1)} %get-tuple-element.50), channel_id=1, source_target_pairs={{0,6},{2,4},{4,2},{6,0},{8,14},{10,12},{12,10},{14,8},{16,22},{18,... | collective-permute-start | bytes 393224 | tf_op jit(solution)/shard_map/ppermute | solution.py:389
  31.8 0.6 %collective-permute-start.11 = (bf16[512,128]{1,0:T(8,128)(2,1)S(1)}, bf16[512,128]{1,0:T(8,128)(2,1)S(1)}, u32[]{:S(2)}, u32[]{:S(2)}) collective-permute-start(bf16[512,128]{1,0:T(8,128)(2,1)S(1)} %get-tuple-element.51), channel_id=1, source_target_pairs={{0,4},{2,6},{4,0},{6,2},{8,12},{10,14},{12,8},{14,10},{16,20},{18,... | collective-permute-start | bytes 393224 | tf_op jit(solution)/shard_map/ppermute | solution.py:389
  32.4 0.4 collective-permute-start.12
  32.8 3.9 %shard_map.114 = (bf16[8,128,128]{2,1,0:T(8,128)(2,1)S(1)}, f32[8,128,128]{2,1,0:T(8,128)S(1)}, f32[8,128,1]{2,1,0:T(8,128)S(1)}, f32[8,128,1]{2,1,0:T(8,128)S(1)}) custom-call(bf16[128,2048]{1,0:T(8,128)(2,1)S(1)} %get-tuple-element.55.rows_ref, bf16[2048,1024]{1,0:T(8,128)(2,1)} %weight_hbm.1, f32[1,128]{1,0:T(1,128)S(1)} %get-tuple-element.56.gain_ref, ...), custom_call_target="tpu_custom_call" | custom-call | flops 1073741824 | bytes 16777216 | tf_op jit(solution)/shard_map/pallas_call | solution.py:21
  36.8 1.3 %collective-permute-done.11.refs_1_ = bf16[512,128]{1,0:T(8,128)(2,1)S(1)} collective-permute-done((bf16[512,128]{1,0:T(8,128)(2,1)S(1)}, bf16[512,128]{1,0:T(8,128)(2,1)S(1)}, u32[]{:S(2)}, u32[]{:S(2)}) %collective-permute-start.11) | collective-permute-done | bytes 131104 | tf_op jit(solution)/shard_map/ppermute | solution.py:389
  38.1 2.9 %shard_map.115 = (bf16[64,2048]{1,0:T(8,128)(2,1)S(1)}, bf16[64,2048]{1,0:T(8,128)(2,1)S(1)}) custom-call(s32[1]{0:T(128)} %bitcast.place_ref, s32[1]{0:T(128)} %bitcast.1.core_ref, s32[1]{0:T(128)} %get-tuple-element.44.table_ref, bf16[512,128]{1,0:T(8,128)(2,1)S(1)} %collective-permute-done.10.refs_0_, ...), custom_call_target="tpu_custom_call" | custom-call | flops 536870912 | bytes 4000000 | tf_op jit(solution)/shard_map/pallas_call | solution.py:21
  41.1 1.5 %collective-permute-done.16 = bf16[64,2048]{1,0:T(8,128)(2,1)S(1)} collective-permute-done((bf16[64,2048]{1,0:T(8,128)(2,1)S(1)}, bf16[64,2048]{1,0:T(8,128)(2,1)S(1)}, u32[]{:S(2)}, u32[]{:S(2)}) %collective-permute-start.16) | collective-permute-done | bytes 262176 | tf_op jit(solution)/shard_map/ppermute | solution.py:512
  42.6 0.8 %add.3 = bf16[64,2048]{1,0:T(8,128)(2,1)} add(bf16[64,2048]{1,0:T(8,128)(2,1)S(1)} %get-tuple-element.65, bf16[64,2048]{1,0:T(8,128)(2,1)S(1)} %collective-permute-done.16) | non-fusion elementwise | flops 131072 | bytes 786432 | tf_op jit(solution)/shard_map/add | solution.py:512
  (22 shorter events, 0.3 us)
Async XLA Ops:
  0.0 22.3 %copy-start.1 = (s32[1,16]{1,0:T(1,128)S(1)}, s32[1,16]{1,0:T(1,128)}, u32[]{:S(2)}) copy-start(s32[1,16]{1,0:T(1,128)} %param.21) | copy-start | bytes 196
  0.0 2.6 %collective-permute-start = (bf16[64,2048]{1,0:T(8,128)(2,1)}, bf16[64,2048]{1,0:T(8,128)(2,1)S(1)}, u32[]{:S(2)}, u32[]{:S(2)}) collective-permute-start(bf16[64,2048]{1,0:T(8,128)(2,1)} %mine_hbm.1), channel_id=1, source_target_pairs={{0,1},{1,0},{2,3},{3,2},{4,5},{5,4},{6,7},{7,6},{8,9},{9,8},{10,11... | collective-permute-start | bytes 786440 | tf_op jit(solution)/shard_map/ppermute | solution.py:375
  5.0 8.2 %collective-permute-start.1 = (f32[128,128]{1,0:T(8,128)S(1)}, f32[128,128]{1,0:T(8,128)S(1)}, u32[]{:S(2)}, u32[]{:S(2)}) collective-permute-start(f32[128,128]{1,0:T(8,128)S(1)} %get-tuple-element.41.refs_3_), channel_id=1, source_target_pairs={{0,6},{2,4},{4,2},{6,0},{8,14},{10,12},{12,10},{14,8},{16,22},{18,... | collective-permute-start | bytes 196616 | tf_op jit(solution)/shard_map/ppermute | solution.py:389
  8.5 5.2 %collective-permute-start.2 = (f32[128,128]{1,0:T(8,128)S(1)}, f32[128,128]{1,0:T(8,128)S(1)}, u32[]{:S(2)}, u32[]{:S(2)}) collective-permute-start(f32[128,128]{1,0:T(8,128)S(1)} %get-tuple-element.41.refs_3_), channel_id=1, source_target_pairs={{0,4},{2,6},{4,0},{6,2},{8,12},{10,14},{12,8},{14,10},{16,20},{18,... | collective-permute-start | bytes 196616 | tf_op jit(solution)/shard_map/ppermute | solution.py:389
  9.0 4.7 %collective-permute-start.3 = (f32[128,128]{1,0:T(8,128)S(1)}, f32[128,128]{1,0:T(8,128)S(1)}, u32[]{:S(2)}, u32[]{:S(2)}) collective-permute-start(f32[128,128]{1,0:T(8,128)S(1)} %get-tuple-element.41.refs_3_), channel_id=1, source_target_pairs={{0,2},{2,0},{4,6},{6,4},{8,10},{10,8},{12,14},{14,12},{16,18},{18,... | collective-permute-start | bytes 196616 | tf_op jit(solution)/shard_map/ppermute | solution.py:389
  9.1 9.0 %collective-permute-start.4 = (bf16[128,128]{1,0:T(8,128)(2,1)S(1)}, bf16[128,128]{1,0:T(8,128)(2,1)S(1)}, u32[]{:S(2)}, u32[]{:S(2)}) collective-permute-start(bf16[128,128]{1,0:T(8,128)(2,1)S(1)} %get-tuple-element.43.refs_3_.val_ref), channel_id=1, source_target_pairs={{0,24},{2,26},{4,28},{6,30},{8,16},{10,18},{12,20},{14,22},{16,8},... | collective-permute-start | bytes 98312 | tf_op jit(solution)/shard_map/ppermute | solution.py:389
  13.1 9.2 %collective-permute-start.5 = (bf16[128,128]{1,0:T(8,128)(2,1)S(1)}, bf16[128,128]{1,0:T(8,128)(2,1)S(1)}, u32[]{:S(2)}, u32[]{:S(2)}) collective-permute-start(bf16[128,128]{1,0:T(8,128)(2,1)S(1)} %get-tuple-element.43.refs_3_.val_ref), channel_id=1, source_target_pairs={{0,16},{2,18},{4,20},{6,22},{8,24},{10,26},{12,28},{14,30},{16,0},... | collective-permute-start | bytes 98312 | tf_op jit(solution)/shard_map/ppermute | solution.py:389
  13.2 9.2 %collective-permute-start.6 = (bf16[128,128]{1,0:T(8,128)(2,1)S(1)}, bf16[128,128]{1,0:T(8,128)(2,1)S(1)}, u32[]{:S(2)}, u32[]{:S(2)}) collective-permute-start(bf16[128,128]{1,0:T(8,128)(2,1)S(1)} %get-tuple-element.43.refs_3_.val_ref), channel_id=1, source_target_pairs={{0,8},{2,10},{4,12},{6,14},{8,0},{10,2},{12,4},{14,6},{16,24},{18,... | collective-permute-start | bytes 98312 | tf_op jit(solution)/shard_map/ppermute | solution.py:389
  13.7 24.4 %copy-start = (bf16[1024,2048]{1,0:T(8,128)(2,1)S(1)}, bf16[1024,2048]{1,0:T(8,128)(2,1)}, u32[]{:S(2)}) copy-start(bf16[1024,2048]{1,0:T(8,128)(2,1)} %refs_12_.1) | copy-start | bytes 12582916
  14.2 11.8 %collective-permute-start.7 = (bf16[512,128]{1,0:T(8,128)(2,1)S(1)}, bf16[512,128]{1,0:T(8,128)(2,1)S(1)}, u32[]{:S(2)}, u32[]{:S(2)}) collective-permute-start(bf16[512,128]{1,0:T(8,128)(2,1)S(1)} %get-tuple-element.45.refs_3_), channel_id=1, source_target_pairs={{0,24},{2,26},{4,28},{6,30},{8,16},{10,18},{12,20},{14,22},{16,8},... | collective-permute-start | bytes 393224 | tf_op jit(solution)/shard_map/ppermute | solution.py:389
  18.1 10.4 %collective-permute-start.8 = (bf16[512,128]{1,0:T(8,128)(2,1)S(1)}, bf16[512,128]{1,0:T(8,128)(2,1)S(1)}, u32[]{:S(2)}, u32[]{:S(2)}) collective-permute-start(bf16[512,128]{1,0:T(8,128)(2,1)S(1)} %get-tuple-element.45.refs_3_), channel_id=1, source_target_pairs={{0,16},{2,18},{4,20},{6,22},{8,24},{10,26},{12,28},{14,30},{16,0},... | collective-permute-start | bytes 393224 | tf_op jit(solution)/shard_map/ppermute | solution.py:389
  18.1 10.4 %collective-permute-start.9 = (bf16[512,128]{1,0:T(8,128)(2,1)S(1)}, bf16[512,128]{1,0:T(8,128)(2,1)S(1)}, u32[]{:S(2)}, u32[]{:S(2)}) collective-permute-start(bf16[512,128]{1,0:T(8,128)(2,1)S(1)} %get-tuple-element.45.refs_3_), channel_id=1, source_target_pairs={{0,8},{2,10},{4,12},{6,14},{8,0},{10,2},{12,4},{14,6},{16,24},{18,... | collective-permute-start | bytes 393224 | tf_op jit(solution)/shard_map/ppermute | solution.py:389
  23.7 8.7 %collective-permute-start.13 = (bf16[512,128]{1,0:T(8,128)(2,1)S(1)}, bf16[512,128]{1,0:T(8,128)(2,1)S(1)}, u32[]{:S(2)}, u32[]{:S(2)}) collective-permute-start(bf16[512,128]{1,0:T(8,128)(2,1)S(1)} %get-tuple-element.54.refs_7_), channel_id=1, source_target_pairs={{0,6},{2,4},{4,2},{6,0},{8,14},{10,12},{12,10},{14,8},{16,22},{18,... | collective-permute-start | bytes 393224 | tf_op jit(solution)/shard_map/ppermute | solution.py:389
  26.1 10.7 %collective-permute-start.14 = (bf16[512,128]{1,0:T(8,128)(2,1)S(1)}, bf16[512,128]{1,0:T(8,128)(2,1)S(1)}, u32[]{:S(2)}, u32[]{:S(2)}) collective-permute-start(bf16[512,128]{1,0:T(8,128)(2,1)S(1)} %get-tuple-element.54.refs_7_), channel_id=1, source_target_pairs={{0,4},{2,6},{4,0},{6,2},{8,12},{10,14},{12,8},{14,10},{16,20},{18,... | collective-permute-start | bytes 393224 | tf_op jit(solution)/shard_map/ppermute | solution.py:389
  26.1 10.7 %collective-permute-start.15 = (bf16[512,128]{1,0:T(8,128)(2,1)S(1)}, bf16[512,128]{1,0:T(8,128)(2,1)S(1)}, u32[]{:S(2)}, u32[]{:S(2)}) collective-permute-start(bf16[512,128]{1,0:T(8,128)(2,1)S(1)} %get-tuple-element.54.refs_7_), channel_id=1, source_target_pairs={{0,2},{2,0},{4,6},{6,4},{8,10},{10,8},{12,14},{14,12},{16,18},{18,... | collective-permute-start | bytes 393224 | tf_op jit(solution)/shard_map/ppermute | solution.py:389
  29.3 7.5 %collective-permute-start.10 = (bf16[512,128]{1,0:T(8,128)(2,1)S(1)}, bf16[512,128]{1,0:T(8,128)(2,1)S(1)}, u32[]{:S(2)}, u32[]{:S(2)}) collective-permute-start(bf16[512,128]{1,0:T(8,128)(2,1)S(1)} %get-tuple-element.50), channel_id=1, source_target_pairs={{0,6},{2,4},{4,2},{6,0},{8,14},{10,12},{12,10},{14,8},{16,22},{18,... | collective-permute-start | bytes 393224 | tf_op jit(solution)/shard_map/ppermute | solution.py:389
  31.8 6.3 %collective-permute-start.11 = (bf16[512,128]{1,0:T(8,128)(2,1)S(1)}, bf16[512,128]{1,0:T(8,128)(2,1)S(1)}, u32[]{:S(2)}, u32[]{:S(2)}) collective-permute-start(bf16[512,128]{1,0:T(8,128)(2,1)S(1)} %get-tuple-element.51), channel_id=1, source_target_pairs={{0,4},{2,6},{4,0},{6,2},{8,12},{10,14},{12,8},{14,10},{16,20},{18,... | collective-permute-start | bytes 393224 | tf_op jit(solution)/shard_map/ppermute | solution.py:389
  32.4 5.7 %collective-permute-start.12 = (bf16[512,128]{1,0:T(8,128)(2,1)S(1)}, bf16[512,128]{1,0:T(8,128)(2,1)S(1)}, u32[]{:S(2)}, u32[]{:S(2)}) collective-permute-start(bf16[512,128]{1,0:T(8,128)(2,1)S(1)} %get-tuple-element.52), channel_id=1, source_target_pairs={{0,2},{2,0},{4,6},{6,4},{8,10},{10,8},{12,14},{14,12},{16,18},{18,... | collective-permute-start | bytes 393224 | tf_op jit(solution)/shard_map/ppermute | solution.py:389
  41.0 1.6 %collective-permute-start.16 = (bf16[64,2048]{1,0:T(8,128)(2,1)S(1)}, bf16[64,2048]{1,0:T(8,128)(2,1)S(1)}, u32[]{:S(2)}, u32[]{:S(2)}) collective-permute-start(bf16[64,2048]{1,0:T(8,128)(2,1)S(1)} %get-tuple-element.66), channel_id=1, source_target_pairs={{0,1},{1,0},{2,3},{3,2},{4,5},{5,4},{6,7},{7,6},{8,9},{9,8},{10,11... | collective-permute-start | bytes 786440 | tf_op jit(solution)/shard_map/ppermute | solution.py:512

commit v16 on v15

--- a/solution.py
+++ b/solution.py
@@ -39,6 +39,10 @@
 
 def in_hbm(array):
     return pltpu.with_memory_space_constraint(array, pltpu.HBM)
+
+
+def line_order(groups):
+    return [groups // 2] + [step for step in range(groups - 1, 0, -1) if step != groups // 2] + [0]
 
 
 def shaped(shape, dtype):
@@ -256,9 +260,8 @@
     far_refs, (keys_ref, whole_ref) = refs[-group - 2 : -2], refs[-2:]
     mine, member = place_ref[0] // group, place_ref[0] % group
     size = starts_ref.shape[1]
-    for step in range(groups):
+    for ref, step in zip(arrived, line_order(groups)):
         index = source_of(mine, step, groups)
-        ref = arrived[groups - 1 - step]
         keys_ref[index] = ref[:tokens].astype(F32) + ref[tokens : 2 * tokens].astype(F32)
         whole = ref[2 * tokens : 2 * tokens + size].astype(F32)
         whole_ref[index] = whole + ref[2 * tokens + size :].astype(F32)
@@ -330,7 +333,7 @@
     turns = most // chunk
     if turns == 1:
         bias = collect(0)
-    stack = math.gcd(heads, 4)
+    stack = math.gcd(heads, 8)
     for first in range(0, heads, stack):
         some = slice(first, first + stack)
         moved = moved_ref[some].reshape(stack * tokens, size)
@@ -482,7 +485,7 @@
     far = call(
         functools.partial(arrive_kernel, groups, group, tokens),
         [shaped((groups * tokens, size), BF16)] * group,
-        (place, *arrived[::-1], starts, *near),
+        (place, *(arrived[step] for step in line_order(groups)), starts, *near),
         in_specs=[smem] + [vmem] * (groups + 1 + group),
         scratch=(
             pltpu.VMEM((groups, tokens, size), F32),

time: 43.6 us -> 43.3 us (level)
  waiting for transfers between devices: 7.7 us -> 5.94 us
  starting transfers between devices: 20.9 us -> 21.7 us
  Pallas kernels: 13.3 us -> 14 us
    ppermute x15, waiting for transfers between devices: 6.18 us -> 4.42 us  [swapped(): out[step] = lax.ppermute(values[step], 'ctx', pairs_of(step))]
    ppermute x15, starting transfers between devices: 20.4 us -> 21.2 us  [swapped(): out[step] = lax.ppermute(values[step], 'ctx', pairs_of(step))]
    pallas_call x7, Pallas kernels: 13.3 us -> 14 us  [call(): pl.pallas_call(kernel, out_shape=out_shape, in_specs=in_specs or [vmem] *...]
  transfers between devices with their start and end apart: 17 -> 17, of which waited for: 4 -> 5; matrix products, arithmetic and copies ran while one was open for 0% -> 0% of each run, Pallas kernels for 19% -> 19%
where the time goes in v16:
time: 43.3 us; the launch traced here: 43.2 us
  starting transfers between devices  21.7 us (50%)
  Pallas kernels  14 us (32%)
  waiting for transfers between devices  5.94 us (14%)
  other arithmetic  0.77 us (2%)
  between operations  0.76 us (2%)
    ppermute x15, starting transfers between devices, swapped(): out[step] = lax.ppermute(values[step], 'ctx', pairs_of(step))  21.2 us
    pallas_call x7, Pallas kernels, call(): pl.pallas_call(kernel, out_shape=out_shape, in_specs=in_specs or [vmem] *...  14 us
    ppermute x15, waiting for transfers between devices, swapped(): out[step] = lax.ppermute(values[step], 'ctx', pairs_of(step))  4.42 us
    ppermute x1, waiting for transfers between devices, body(): return kept + lax.ppermute(away, 'head', [(0, 1), (1, 0)])  1.52 us
  transfers between devices with their start and end apart: 17, of which 5 were waited for; matrix products, arithmetic and copies ran while one was open for 0% of the time, Pallas kernels for 19%

profile of v16, /device:TPU:0, one launch (start us, length us, event | category | flops | bytes accessed | tf_op | source)
XLA Modules:
  0.0 43.2 jit_solution(5177235826752953311)
XLA Ops:
  0.0 0.5 %collective-permute-start = (bf16[64,2048]{1,0:T(8,128)(2,1)}, bf16[64,2048]{1,0:T(8,128)(2,1)S(1)}, u32[]{:S(2)}, u32[]{:S(2)}) collective-permute-start(bf16[64,2048]{1,0:T(8,128)(2,1)} %mine_hbm.1), channel_id=1, source_target_pairs={{0,1},{1,0},{2,3},{3,2},{4,5},{5,4},{6,7},{7,6},{8,9},{9,8},{10,11... | collective-permute-start | bytes 786440 | tf_op jit(solution)/shard_map/ppermute | solution.py:378
  1.1 1.5 %shard_map.109 = (bf16[2048,384]{1,0:T(8,128)(2,1)S(1)}, bf16[1,2048]{1,0:T(2,128)(2,1)S(1)}, f32[1,128]{1,0:T(1,128)S(1)}, f32[1,128]{1,0:T(1,128)S(1)}, bf16[64,2048]{1,0:T(8,128)(2,1)S(1)}) custom-call(bf16[2048,128]{1,0:T(8,128)(2,1)} %key_hbm.1, bf16[2048,128]{1,0:T(8,128)(2,1)} %dir_hbm.1, bf16[2048,128]{1,0:T(8,128)(2,1)} %value_hbm.1, ...), custom_call_target="tpu_custom_call" | custom-call | bytes 3145728 | tf_op jit(solution)/shard_map/pallas_call | solution.py:21
  2.7 2.3 %shard_map.110 = (bf16[128,2048]{1,0:T(8,128)(2,1)S(1)}, f32[128,128]{1,0:T(8,128)S(1)}, bf16[128,128]{1,0:T(8,128)(2,1)S(1)}, f32[128,128]{1,0:T(8,128)S(1)}, f...) custom-call(s32[1]{0:T(128)} %bitcast.1.core_ref, ...), custom_call_target="tpu_custom_call" | custom-call | flops 201326592 | bytes 2097152 | tf_op jit(solution)/shard_map/pallas_call | solution.py:21
  5.0 3.5 %collective-permute-start.1 = (f32[128,128]{1,0:T(8,128)S(1)}, f32[128,128]{1,0:T(8,128)S(1)}, u32[]{:S(2)}, u32[]{:S(2)}) collective-permute-start(f32[128,128]{1,0:T(8,128)S(1)} %get-tuple-element.41.refs_3_), channel_id=1, source_target_pairs={{0,6},{2,4},{4,2},{6,0},{8,14},{10,12},{12,10},{14,8},{16,22},{18,... | collective-permute-start | bytes 196616 | tf_op jit(solution)/shard_map/ppermute | solution.py:392
  8.5 0.5 %collective-permute-start.2 = (f32[128,128]{1,0:T(8,128)S(1)}, f32[128,128]{1,0:T(8,128)S(1)}, u32[]{:S(2)}, u32[]{:S(2)}) collective-permute-start(f32[128,128]{1,0:T(8,128)S(1)} %get-tuple-element.41.refs_3_), channel_id=1, source_target_pairs={{0,4},{2,6},{4,0},{6,2},{8,12},{10,14},{12,8},{14,10},{16,20},{18,... | collective-permute-start | bytes 196616 | tf_op jit(solution)/shard_map/ppermute | solution.py:392
  9.1 4.0 %collective-permute-start.4 = (bf16[128,128]{1,0:T(8,128)(2,1)S(1)}, bf16[128,128]{1,0:T(8,128)(2,1)S(1)}, u32[]{:S(2)}, u32[]{:S(2)}) collective-permute-start(bf16[128,128]{1,0:T(8,128)(2,1)S(1)} %get-tuple-element.43.refs_3_.val_ref), channel_id=1, source_target_pairs={{0,24},{2,26},{4,28},{6,30},{8,16},{10,18},{12,20},{14,22},{16,8},... | collective-permute-start | bytes 98312 | tf_op jit(solution)/shard_map/ppermute | solution.py:392
  13.2 0.6 %collective-permute-start.6 = (bf16[128,128]{1,0:T(8,128)(2,1)S(1)}, bf16[128,128]{1,0:T(8,128)(2,1)S(1)}, u32[]{:S(2)}, u32[]{:S(2)}) collective-permute-start(bf16[128,128]{1,0:T(8,128)(2,1)S(1)} %get-tuple-element.43.refs_3_.val_ref), channel_id=1, source_target_pairs={{0,8},{2,10},{4,12},{6,14},{8,0},{10,2},{12,4},{14,6},{16,24},{18,... | collective-permute-start | bytes 98312 | tf_op jit(solution)/shard_map/ppermute | solution.py:392
  13.7 0.5 %shard_map.111 = (bf16[512,128]{1,0:T(8,128)(2,1)S(1)}, f32[4,128,128]{2,1,0:T(8,128)S(1)}, bf16[128,128]{1,0:T(8,128)(2,1)S(1)}, bf16[128,128]{1,0:T(8,128)(2,1...) custom-call(s32[1]{0:T(128)} %bitcast.place_ref, f32[128,128]{1,0:T(8,128)S(1)} %get-tuple-element.40.exit_ref, ...), custom_call_target="tpu_custom_call" | custom-call | flops 100663296 | bytes 1000000 | tf_op jit(solution)/shard_map/pallas_call | solution.py:21
  14.2 2.4 %collective-permute-start.7 = (bf16[512,128]{1,0:T(8,128)(2,1)S(1)}, bf16[512,128]{1,0:T(8,128)(2,1)S(1)}, u32[]{:S(2)}, u32[]{:S(2)}) collective-permute-start(bf16[512,128]{1,0:T(8,128)(2,1)S(1)} %get-tuple-element.45.refs_3_), channel_id=1, source_target_pairs={{0,16},{2,18},{4,20},{6,22},{8,24},{10,26},{12,28},{14,30},{16,0},... | collective-permute-start | bytes 393224 | tf_op jit(solution)/shard_map/ppermute | solution.py:392
  16.7 1.5 %collective-permute-start.8 = (bf16[512,128]{1,0:T(8,128)(2,1)S(1)}, bf16[512,128]{1,0:T(8,128)(2,1)S(1)}, u32[]{:S(2)}, u32[]{:S(2)}) collective-permute-start(bf16[512,128]{1,0:T(8,128)(2,1)S(1)} %get-tuple-element.45.refs_3_), channel_id=1, source_target_pairs={{0,24},{2,26},{4,28},{6,30},{8,16},{10,18},{12,20},{14,22},{16,8},... | collective-permute-start | bytes 393224 | tf_op jit(solution)/shard_map/ppermute | solution.py:392
  18.2 0.5 %collective-permute-start.9 = (bf16[512,128]{1,0:T(8,128)(2,1)S(1)}, bf16[512,128]{1,0:T(8,128)(2,1)S(1)}, u32[]{:S(2)}, u32[]{:S(2)}) collective-permute-start(bf16[512,128]{1,0:T(8,128)(2,1)S(1)} %get-tuple-element.45.refs_3_), channel_id=1, source_target_pairs={{0,8},{2,10},{4,12},{6,14},{8,0},{10,2},{12,4},{14,6},{16,24},{18,... | collective-permute-start | bytes 393224 | tf_op jit(solution)/shard_map/ppermute | solution.py:392
  18.7 1.1 %collective-permute-done.5.refs_1_ = bf16[128,128]{1,0:T(8,128)(2,1)S(1)} collective-permute-done((bf16[128,128]{1,0:T(8,128)(2,1)S(1)}, bf16[128,128]{1,0:T(8,128)(2,1)S(1)}, u32[]{:S(2)}, u32[]{:S(2)}) %collective-permute-start.5) | collective-permute-done | bytes 32800 | tf_op jit(solution)/shard_map/ppermute | solution.py:392
  19.8 1.3 %shard_map.112 = (bf16[512,128]{1,0:T(8,128)(2,1)S(1)}, s32[1]{0:T(128)}) custom-call(s32[1]{0:T(128)} %bitcast.place_ref, s32[16]{0:T(128)S(1)} %bitcast.5, f32[4,128,128]{2,1,0:T(8,128)S(1)} %get-tuple-element.42.after_ref.refs_4_, bf16[128,128]{1,0:T(8,128)(2,1)S(1)} %collective-permute-done.4.refs_0_, ...), custom_call_target="tpu_custom_call" | custom-call | bytes 1000000 | tf_op jit(solution)/shard_map/pallas_call | solution.py:21
  21.1 2.5 %collective-permute-start.13 = (bf16[512,128]{1,0:T(8,128)(2,1)S(1)}, bf16[512,128]{1,0:T(8,128)(2,1)S(1)}, u32[]{:S(2)}, u32[]{:S(2)}) collective-permute-start(bf16[512,128]{1,0:T(8,128)(2,1)S(1)} %get-tuple-element.54.refs_7_), channel_id=1, source_target_pairs={{0,6},{2,4},{4,2},{6,0},{8,14},{10,12},{12,10},{14,8},{16,22},{18,... | collective-permute-start | bytes 393224 | tf_op jit(solution)/shard_map/ppermute | solution.py:392
  24.0 2.7 %collective-permute-done.7.refs_0_ = bf16[512,128]{1,0:T(8,128)(2,1)S(1)} collective-permute-done((bf16[512,128]{1,0:T(8,128)(2,1)S(1)}, bf16[512,128]{1,0:T(8,128)(2,1)S(1)}, u32[]{:S(2)}, u32[]{:S(2)}) %collective-permute-start.7) | collective-permute-done | bytes 131104 | tf_op jit(solution)/shard_map/ppermute | solution.py:392
  26.7 1.5 %collective-permute-start.15 = (bf16[512,128]{1,0:T(8,128)(2,1)S(1)}, bf16[512,128]{1,0:T(8,128)(2,1)S(1)}, u32[]{:S(2)}, u32[]{:S(2)}) collective-permute-start(bf16[512,128]{1,0:T(8,128)(2,1)S(1)} %get-tuple-element.54.refs_7_), channel_id=1, source_target_pairs={{0,2},{2,0},{4,6},{6,4},{8,10},{10,8},{12,14},{14,12},{16,18},{18,... | collective-permute-start | bytes 393224 | tf_op jit(solution)/shard_map/ppermute | solution.py:392
  28.2 0.7 %shard_map.113 = (bf16[512,128]{1,0:T(8,128)(2,1)S(1)}, bf16[512,128]{1,0:T(8,128)(2,1)S(1)}, bf16[512,128]{1,0:T(8,128)(2,1)S(1)}, bf16[512,128]{1,0:T(8,128)(2,1)S(1)}) custom-call(s32[1]{0:T(128)} %bitcast.place_ref, bf16[512,128]{1,0:T(8,128)(2,1)S(1)} %collective-permute-done.7.refs_0_, bf16[512,128]{1,0:T(8,128)(2,1)S(1)} %collective-permute-done.8.refs_1_, ...), custom_call_target="tpu_custom_call" | custom-call | flops 201326592 | bytes 1000000 | tf_op jit(solution)/shard_map/pallas_call | solution.py:21
  29.0 1.6 %collective-permute-start.10 = (bf16[512,128]{1,0:T(8,128)(2,1)S(1)}, bf16[512,128]{1,0:T(8,128)(2,1)S(1)}, u32[]{:S(2)}, u32[]{:S(2)}) collective-permute-start(bf16[512,128]{1,0:T(8,128)(2,1)S(1)} %get-tuple-element.50), channel_id=1, source_target_pairs={{0,6},{2,4},{4,2},{6,0},{8,14},{10,12},{12,10},{14,8},{16,22},{18,... | collective-permute-start | bytes 393224 | tf_op jit(solution)/shard_map/ppermute | solution.py:392
  30.5 0.5 %collective-permute-start.11 = (bf16[512,128]{1,0:T(8,128)(2,1)S(1)}, bf16[512,128]{1,0:T(8,128)(2,1)S(1)}, u32[]{:S(2)}, u32[]{:S(2)}) collective-permute-start(bf16[512,128]{1,0:T(8,128)(2,1)S(1)} %get-tuple-element.51), channel_id=1, source_target_pairs={{0,4},{2,6},{4,0},{6,2},{8,12},{10,14},{12,8},{14,10},{16,20},{18,... | collective-permute-start | bytes 393224 | tf_op jit(solution)/shard_map/ppermute | solution.py:392
  31.0 1.5 %collective-permute-start.12 = (bf16[512,128]{1,0:T(8,128)(2,1)S(1)}, bf16[512,128]{1,0:T(8,128)(2,1)S(1)}, u32[]{:S(2)}, u32[]{:S(2)}) collective-permute-start(bf16[512,128]{1,0:T(8,128)(2,1)S(1)} %get-tuple-element.52), channel_id=1, source_target_pairs={{0,2},{2,0},{4,6},{6,4},{8,10},{10,8},{12,14},{14,12},{16,18},{18,... | collective-permute-start | bytes 393224 | tf_op jit(solution)/shard_map/ppermute | solution.py:392
  32.5 3.9 %shard_map.114 = (bf16[8,128,128]{2,1,0:T(8,128)(2,1)S(1)}, f32[8,128,128]{2,1,0:T(8,128)S(1)}, f32[8,128,1]{2,1,0:T(8,128)S(1)}, f32[8,128,1]{2,1,0:T(8,128)S(1)}) custom-call(bf16[128,2048]{1,0:T(8,128)(2,1)S(1)} %get-tuple-element.55.rows_ref, bf16[2048,1024]{1,0:T(8,128)(2,1)} %weight_hbm.1, f32[1,128]{1,0:T(1,128)S(1)} %get-tuple-element.56.gain_ref, ...), custom_call_target="tpu_custom_call" | custom-call | flops 1073741824 | bytes 16777216 | tf_op jit(solution)/shard_map/pallas_call | solution.py:21
  37.1 3.7 %shard_map.115 = (bf16[64,2048]{1,0:T(8,128)(2,1)S(1)}, bf16[64,2048]{1,0:T(8,128)(2,1)S(1)}) custom-call(s32[1]{0:T(128)} %bitcast.place_ref, s32[1]{0:T(128)} %bitcast.1.core_ref, s32[1]{0:T(128)} %get-tuple-element.44.table_ref, bf16[512,128]{1,0:T(8,128)(2,1)S(1)} %collective-permute-done.10.refs_0_, ...), custom_call_target="tpu_custom_call" | custom-call | flops 536870912 | bytes 4000000 | tf_op jit(solution)/shard_map/pallas_call | solution.py:21
  40.9 1.5 %collective-permute-done.16 = bf16[64,2048]{1,0:T(8,128)(2,1)S(1)} collective-permute-done((bf16[64,2048]{1,0:T(8,128)(2,1)S(1)}, bf16[64,2048]{1,0:T(8,128)(2,1)S(1)}, u32[]{:S(2)}, u32[]{:S(2)}) %collective-permute-start.16) | collective-permute-done | bytes 262176 | tf_op jit(solution)/shard_map/ppermute | solution.py:515
  42.4 0.8 %add.3 = bf16[64,2048]{1,0:T(8,128)(2,1)} add(bf16[64,2048]{1,0:T(8,128)(2,1)S(1)} %get-tuple-element.65, bf16[64,2048]{1,0:T(8,128)(2,1)S(1)} %collective-permute-done.16) | non-fusion elementwise | flops 131072 | bytes 786432 | tf_op jit(solution)/shard_map/add | solution.py:515
  (22 shorter events, 1.3 us)
Async XLA Ops:
  0.0 19.8 %copy-start.1 = (s32[1,16]{1,0:T(1,128)S(1)}, s32[1,16]{1,0:T(1,128)}, u32[]{:S(2)}) copy-start(s32[1,16]{1,0:T(1,128)} %param.21) | copy-start | bytes 196
  0.0 2.6 %collective-permute-start = (bf16[64,2048]{1,0:T(8,128)(2,1)}, bf16[64,2048]{1,0:T(8,128)(2,1)S(1)}, u32[]{:S(2)}, u32[]{:S(2)}) collective-permute-start(bf16[64,2048]{1,0:T(8,128)(2,1)} %mine_hbm.1), channel_id=1, source_target_pairs={{0,1},{1,0},{2,3},{3,2},{4,5},{5,4},{6,7},{7,6},{8,9},{9,8},{10,11... | collective-permute-start | bytes 786440 | tf_op jit(solution)/shard_map/ppermute | solution.py:378
  5.0 8.2 %collective-permute-start.1 = (f32[128,128]{1,0:T(8,128)S(1)}, f32[128,128]{1,0:T(8,128)S(1)}, u32[]{:S(2)}, u32[]{:S(2)}) collective-permute-start(f32[128,128]{1,0:T(8,128)S(1)} %get-tuple-element.41.refs_3_), channel_id=1, source_target_pairs={{0,6},{2,4},{4,2},{6,0},{8,14},{10,12},{12,10},{14,8},{16,22},{18,... | collective-permute-start | bytes 196616 | tf_op jit(solution)/shard_map/ppermute | solution.py:392
  8.5 5.2 %collective-permute-start.2 = (f32[128,128]{1,0:T(8,128)S(1)}, f32[128,128]{1,0:T(8,128)S(1)}, u32[]{:S(2)}, u32[]{:S(2)}) collective-permute-start(f32[128,128]{1,0:T(8,128)S(1)} %get-tuple-element.41.refs_3_), channel_id=1, source_target_pairs={{0,4},{2,6},{4,0},{6,2},{8,12},{10,14},{12,8},{14,10},{16,20},{18,... | collective-permute-start | bytes 196616 | tf_op jit(solution)/shard_map/ppermute | solution.py:392
  9.0 4.7 %collective-permute-start.3 = (f32[128,128]{1,0:T(8,128)S(1)}, f32[128,128]{1,0:T(8,128)S(1)}, u32[]{:S(2)}, u32[]{:S(2)}) collective-permute-start(f32[128,128]{1,0:T(8,128)S(1)} %get-tuple-element.41.refs_3_), channel_id=1, source_target_pairs={{0,2},{2,0},{4,6},{6,4},{8,10},{10,8},{12,14},{14,12},{16,18},{18,... | collective-permute-start | bytes 196616 | tf_op jit(solution)/shard_map/ppermute | solution.py:392
  9.1 9.1 %collective-permute-start.4 = (bf16[128,128]{1,0:T(8,128)(2,1)S(1)}, bf16[128,128]{1,0:T(8,128)(2,1)S(1)}, u32[]{:S(2)}, u32[]{:S(2)}) collective-permute-start(bf16[128,128]{1,0:T(8,128)(2,1)S(1)} %get-tuple-element.43.refs_3_.val_ref), channel_id=1, source_target_pairs={{0,24},{2,26},{4,28},{6,30},{8,16},{10,18},{12,20},{14,22},{16,8},... | collective-permute-start | bytes 98312 | tf_op jit(solution)/shard_map/ppermute | solution.py:392
  13.1 6.6 %collective-permute-start.5 = (bf16[128,128]{1,0:T(8,128)(2,1)S(1)}, bf16[128,128]{1,0:T(8,128)(2,1)S(1)}, u32[]{:S(2)}, u32[]{:S(2)}) collective-permute-start(bf16[128,128]{1,0:T(8,128)(2,1)S(1)} %get-tuple-element.43.refs_3_.val_ref), channel_id=1, source_target_pairs={{0,16},{2,18},{4,20},{6,22},{8,24},{10,26},{12,28},{14,30},{16,0},... | collective-permute-start | bytes 98312 | tf_op jit(solution)/shard_map/ppermute | solution.py:392
  13.2 6.6 %collective-permute-start.6 = (bf16[128,128]{1,0:T(8,128)(2,1)S(1)}, bf16[128,128]{1,0:T(8,128)(2,1)S(1)}, u32[]{:S(2)}, u32[]{:S(2)}) collective-permute-start(bf16[128,128]{1,0:T(8,128)(2,1)S(1)} %get-tuple-element.43.refs_3_.val_ref), channel_id=1, source_target_pairs={{0,8},{2,10},{4,12},{6,14},{8,0},{10,2},{12,4},{14,6},{16,24},{18,... | collective-permute-start | bytes 98312 | tf_op jit(solution)/shard_map/ppermute | solution.py:392
  13.7 23.4 %copy-start = (bf16[1024,2048]{1,0:T(8,128)(2,1)S(1)}, bf16[1024,2048]{1,0:T(8,128)(2,1)}, u32[]{:S(2)}) copy-start(bf16[1024,2048]{1,0:T(8,128)(2,1)} %refs_12_.1) | copy-start | bytes 12582916
  14.2 12.5 %collective-permute-start.7 = (bf16[512,128]{1,0:T(8,128)(2,1)S(1)}, bf16[512,128]{1,0:T(8,128)(2,1)S(1)}, u32[]{:S(2)}, u32[]{:S(2)}) collective-permute-start(bf16[512,128]{1,0:T(8,128)(2,1)S(1)} %get-tuple-element.45.refs_3_), channel_id=1, source_target_pairs={{0,16},{2,18},{4,20},{6,22},{8,24},{10,26},{12,28},{14,30},{16,0},... | collective-permute-start | bytes 393224 | tf_op jit(solution)/shard_map/ppermute | solution.py:392
  16.7 11.5 %collective-permute-start.8 = (bf16[512,128]{1,0:T(8,128)(2,1)S(1)}, bf16[512,128]{1,0:T(8,128)(2,1)S(1)}, u32[]{:S(2)}, u32[]{:S(2)}) collective-permute-start(bf16[512,128]{1,0:T(8,128)(2,1)S(1)} %get-tuple-element.45.refs_3_), channel_id=1, source_target_pairs={{0,24},{2,26},{4,28},{6,30},{8,16},{10,18},{12,20},{14,22},{16,8},... | collective-permute-start | bytes 393224 | tf_op jit(solution)/shard_map/ppermute | solution.py:392
  18.2 10.0 %collective-permute-start.9 = (bf16[512,128]{1,0:T(8,128)(2,1)S(1)}, bf16[512,128]{1,0:T(8,128)(2,1)S(1)}, u32[]{:S(2)}, u32[]{:S(2)}) collective-permute-start(bf16[512,128]{1,0:T(8,128)(2,1)S(1)} %get-tuple-element.45.refs_3_), channel_id=1, source_target_pairs={{0,8},{2,10},{4,12},{6,14},{8,0},{10,2},{12,4},{14,6},{16,24},{18,... | collective-permute-start | bytes 393224 | tf_op jit(solution)/shard_map/ppermute | solution.py:392
  21.1 9.9 %collective-permute-start.13 = (bf16[512,128]{1,0:T(8,128)(2,1)S(1)}, bf16[512,128]{1,0:T(8,128)(2,1)S(1)}, u32[]{:S(2)}, u32[]{:S(2)}) collective-permute-start(bf16[512,128]{1,0:T(8,128)(2,1)S(1)} %get-tuple-element.54.refs_7_), channel_id=1, source_target_pairs={{0,6},{2,4},{4,2},{6,0},{8,14},{10,12},{12,10},{14,8},{16,22},{18,... | collective-permute-start | bytes 393224 | tf_op jit(solution)/shard_map/ppermute | solution.py:392
  23.6 12.8 %collective-permute-start.14 = (bf16[512,128]{1,0:T(8,128)(2,1)S(1)}, bf16[512,128]{1,0:T(8,128)(2,1)S(1)}, u32[]{:S(2)}, u32[]{:S(2)}) collective-permute-start(bf16[512,128]{1,0:T(8,128)(2,1)S(1)} %get-tuple-element.54.refs_7_), channel_id=1, source_target_pairs={{0,4},{2,6},{4,0},{6,2},{8,12},{10,14},{12,8},{14,10},{16,20},{18,... | collective-permute-start | bytes 393224 | tf_op jit(solution)/shard_map/ppermute | solution.py:392
  26.7 9.8 %collective-permute-start.15 = (bf16[512,128]{1,0:T(8,128)(2,1)S(1)}, bf16[512,128]{1,0:T(8,128)(2,1)S(1)}, u32[]{:S(2)}, u32[]{:S(2)}) collective-permute-start(bf16[512,128]{1,0:T(8,128)(2,1)S(1)} %get-tuple-element.54.refs_7_), channel_id=1, source_target_pairs={{0,2},{2,0},{4,6},{6,4},{8,10},{10,8},{12,14},{14,12},{16,18},{18,... | collective-permute-start | bytes 393224 | tf_op jit(solution)/shard_map/ppermute | solution.py:392
  29.0 7.5 %collective-permute-start.10 = (bf16[512,128]{1,0:T(8,128)(2,1)S(1)}, bf16[512,128]{1,0:T(8,128)(2,1)S(1)}, u32[]{:S(2)}, u32[]{:S(2)}) collective-permute-start(bf16[512,128]{1,0:T(8,128)(2,1)S(1)} %get-tuple-element.50), channel_id=1, source_target_pairs={{0,6},{2,4},{4,2},{6,0},{8,14},{10,12},{12,10},{14,8},{16,22},{18,... | collective-permute-start | bytes 393224 | tf_op jit(solution)/shard_map/ppermute | solution.py:392
  30.5 6.4 %collective-permute-start.11 = (bf16[512,128]{1,0:T(8,128)(2,1)S(1)}, bf16[512,128]{1,0:T(8,128)(2,1)S(1)}, u32[]{:S(2)}, u32[]{:S(2)}) collective-permute-start(bf16[512,128]{1,0:T(8,128)(2,1)S(1)} %get-tuple-element.51), channel_id=1, source_target_pairs={{0,4},{2,6},{4,0},{6,2},{8,12},{10,14},{12,8},{14,10},{16,20},{18,... | collective-permute-start | bytes 393224 | tf_op jit(solution)/shard_map/ppermute | solution.py:392
  31.0 6.1 %collective-permute-start.12 = (bf16[512,128]{1,0:T(8,128)(2,1)S(1)}, bf16[512,128]{1,0:T(8,128)(2,1)S(1)}, u32[]{:S(2)}, u32[]{:S(2)}) collective-permute-start(bf16[512,128]{1,0:T(8,128)(2,1)S(1)} %get-tuple-element.52), channel_id=1, source_target_pairs={{0,2},{2,0},{4,6},{6,4},{8,10},{10,8},{12,14},{14,12},{16,18},{18,... | collective-permute-start | bytes 393224 | tf_op jit(solution)/shard_map/ppermute | solution.py:392
  40.8 1.6 %collective-permute-start.16 = (bf16[64,2048]{1,0:T(8,128)(2,1)S(1)}, bf16[64,2048]{1,0:T(8,128)(2,1)S(1)}, u32[]{:S(2)}, u32[]{:S(2)}) collective-permute-start(bf16[64,2048]{1,0:T(8,128)(2,1)S(1)} %get-tuple-element.66), channel_id=1, source_target_pairs={{0,1},{1,0},{2,3},{3,2},{4,5},{5,4},{6,7},{7,6},{8,9},{9,8},{10,11... | collective-permute-start | bytes 786440 | tf_op jit(solution)/shard_map/ppermute | solution.py:515

commit v17 on v16

--- a/solution.py
+++ b/solution.py
@@ -285,7 +285,7 @@
 def attend_kernel(group, segments, most, place_ref, core_ref, table_ref, *refs):
     far_refs, line_refs = refs[:group][::-1], refs[group : 2 * group][::-1]
     (moved_ref, weighted_ref, peak_ref, total_ref, out_ref, away_ref, kept_ref, keys_ref, vals_ref,
-     attended_ref) = refs[2 * group :]
+     summed_ref) = refs[2 * group :]
     core = core_ref[0]
     mine, member = place_ref[0] // group, place_ref[0] % group
     heads, tokens, size = moved_ref.shape
@@ -333,7 +333,8 @@
     turns = most // chunk
     if turns == 1:
         bias = collect(0)
-    stack = math.gcd(heads, 8)
+    stack = math.gcd(heads, 4)
+    wide = math.gcd(out_ref.shape[1], 4 * size)
     for first in range(0, heads, stack):
         some = slice(first, first + stack)
         moved = moved_ref[some].reshape(stack * tokens, size)
@@ -351,20 +352,20 @@
 
             _, total, weighted = lax.fori_loop(0, turns, step_of, state)
         done = (weighted * (1.0 / total)).astype(BF16)
-        for head in range(first, first + stack):
-            for index in range(tokens // half):
-                at = pl.multiple_of(jnp.where(index == core, half, 0), half)
-                row = (head - first) * tokens + index * half
-                attended_ref[pl.ds(at, half), head * size : (head + 1) * size] = done[
-                    row : row + half
-                ]
-    wide = math.gcd(out_ref.shape[1], 4 * size)
-    for at in range(0, out_ref.shape[1], wide):
-        part = slice(at, at + wide)
-        result = jnp.dot(attended_ref[...], out_ref[:, part], preferred_element_type=F32)
-        result = result.astype(BF16)
-        away_ref[:, part] = result[:half]
-        kept_ref[:, part] = result[half:]
+        done = jnp.concatenate(
+            [done[n * tokens : (n + 1) * tokens] for n in range(stack)], axis=1
+        )
+        deep = slice(first * size, (first + stack) * size)
+        for at in range(0, out_ref.shape[1], wide):
+            part = slice(at, at + wide)
+            result = jnp.dot(done, out_ref[deep, part], preferred_element_type=F32)
+            if first:
+                result = result + summed_ref[:, part]
+            if first + stack < heads:
+                summed_ref[:, part] = result
+            else:
+                away_ref[:, part] = jnp.where(core == 0, result[half:], result[:half]).astype(BF16)
+                kept_ref[:, part] = jnp.where(core == 0, result[:half], result[half:]).astype(BF16)
 
 
 def body(
@@ -506,7 +507,7 @@
         scratch=[
             pltpu.VMEM((chunk * tokens, size), BF16),
             pltpu.VMEM((chunk * tokens, size), BF16),
-            pltpu.VMEM((tokens, heads * size), BF16),
+            pltpu.VMEM((tokens, width_out), F32),
         ],
         flops=2 * tokens * width_out * heads * size,
         moved=4 * 10**6,

time: 43.3 us -> 42.5 us (0.982)
  Pallas kernels: 14 us -> 13.2 us
    pallas_call x7, Pallas kernels: 14 us -> 13.2 us  [call(): pl.pallas_call(kernel, out_shape=out_shape, in_specs=in_specs or [vmem] *...]
where the time goes in v17:
time: 42.5 us; the launch traced here: 42.4 us
  starting transfers between devices  21.7 us (51%)
  Pallas kernels  13.2 us (31%)
  waiting for transfers between devices  5.94 us (14%)
  other arithmetic  0.77 us (2%)
  between operations  0.76 us (2%)
    ppermute x15, starting transfers between devices, swapped(): out[step] = lax.ppermute(values[step], 'ctx', pairs_of(step))  21.2 us
    pallas_call x7, Pallas kernels, call(): pl.pallas_call(kernel, out_shape=out_shape, in_specs=in_specs or [vmem] *...  13.2 us
    ppermute x15, waiting for transfers between devices, swapped(): out[step] = lax.ppermute(values[step], 'ctx', pairs_of(step))  4.42 us
    ppermute x1, waiting for transfers between devices, body(): return kept + lax.ppermute(away, 'head', [(0, 1), (1, 0)])  1.52 us
  transfers between devices with their start and end apart: 17, of which 5 were waited for; matrix products, arithmetic and copies ran while one was open for 0% of the time, Pallas kernels for 19%

profile of v17, /device:TPU:0, one launch (start us, length us, event | category | flops | bytes accessed | tf_op | source)
XLA Modules:
  0.0 42.4 jit_solution(6537864262777643110)
XLA Ops:
  0.0 0.5 %collective-permute-start = (bf16[64,2048]{1,0:T(8,128)(2,1)}, bf16[64,2048]{1,0:T(8,128)(2,1)S(1)}, u32[]{:S(2)}, u32[]{:S(2)}) collective-permute-start(bf16[64,2048]{1,0:T(8,128)(2,1)} %mine_hbm.1), channel_id=1, source_target_pairs={{0,1},{1,0},{2,3},{3,2},{4,5},{5,4},{6,7},{7,6},{8,9},{9,8},{10,11... | collective-permute-start | bytes 786440 | tf_op jit(solution)/shard_map/ppermute | solution.py:379
  1.1 1.5 %shard_map.109 = (bf16[2048,384]{1,0:T(8,128)(2,1)S(1)}, bf16[1,2048]{1,0:T(2,128)(2,1)S(1)}, f32[1,128]{1,0:T(1,128)S(1)}, f32[1,128]{1,0:T(1,128)S(1)}, bf16[64,2048]{1,0:T(8,128)(2,1)S(1)}) custom-call(bf16[2048,128]{1,0:T(8,128)(2,1)} %key_hbm.1, bf16[2048,128]{1,0:T(8,128)(2,1)} %dir_hbm.1, bf16[2048,128]{1,0:T(8,128)(2,1)} %value_hbm.1, ...), custom_call_target="tpu_custom_call" | custom-call | bytes 3145728 | tf_op jit(solution)/shard_map/pallas_call | solution.py:21
  2.7 2.3 %shard_map.110 = (bf16[128,2048]{1,0:T(8,128)(2,1)S(1)}, f32[128,128]{1,0:T(8,128)S(1)}, bf16[128,128]{1,0:T(8,128)(2,1)S(1)}, f32[128,128]{1,0:T(8,128)S(1)}, f...) custom-call(s32[1]{0:T(128)} %bitcast.1.core_ref, ...), custom_call_target="tpu_custom_call" | custom-call | flops 201326592 | bytes 2097152 | tf_op jit(solution)/shard_map/pallas_call | solution.py:21
  5.0 3.5 %collective-permute-start.1 = (f32[128,128]{1,0:T(8,128)S(1)}, f32[128,128]{1,0:T(8,128)S(1)}, u32[]{:S(2)}, u32[]{:S(2)}) collective-permute-start(f32[128,128]{1,0:T(8,128)S(1)} %get-tuple-element.41.refs_3_), channel_id=1, source_target_pairs={{0,6},{2,4},{4,2},{6,0},{8,14},{10,12},{12,10},{14,8},{16,22},{18,... | collective-permute-start | bytes 196616 | tf_op jit(solution)/shard_map/ppermute | solution.py:393
  8.5 0.5 %collective-permute-start.2 = (f32[128,128]{1,0:T(8,128)S(1)}, f32[128,128]{1,0:T(8,128)S(1)}, u32[]{:S(2)}, u32[]{:S(2)}) collective-permute-start(f32[128,128]{1,0:T(8,128)S(1)} %get-tuple-element.41.refs_3_), channel_id=1, source_target_pairs={{0,4},{2,6},{4,0},{6,2},{8,12},{10,14},{12,8},{14,10},{16,20},{18,... | collective-permute-start | bytes 196616 | tf_op jit(solution)/shard_map/ppermute | solution.py:393
  9.1 4.0 %collective-permute-start.4 = (bf16[128,128]{1,0:T(8,128)(2,1)S(1)}, bf16[128,128]{1,0:T(8,128)(2,1)S(1)}, u32[]{:S(2)}, u32[]{:S(2)}) collective-permute-start(bf16[128,128]{1,0:T(8,128)(2,1)S(1)} %get-tuple-element.43.refs_3_.val_ref), channel_id=1, source_target_pairs={{0,24},{2,26},{4,28},{6,30},{8,16},{10,18},{12,20},{14,22},{16,8},... | collective-permute-start | bytes 98312 | tf_op jit(solution)/shard_map/ppermute | solution.py:393
  13.2 0.6 %collective-permute-start.6 = (bf16[128,128]{1,0:T(8,128)(2,1)S(1)}, bf16[128,128]{1,0:T(8,128)(2,1)S(1)}, u32[]{:S(2)}, u32[]{:S(2)}) collective-permute-start(bf16[128,128]{1,0:T(8,128)(2,1)S(1)} %get-tuple-element.43.refs_3_.val_ref), channel_id=1, source_target_pairs={{0,8},{2,10},{4,12},{6,14},{8,0},{10,2},{12,4},{14,6},{16,24},{18,... | collective-permute-start | bytes 98312 | tf_op jit(solution)/shard_map/ppermute | solution.py:393
  13.7 0.5 %shard_map.111 = (bf16[512,128]{1,0:T(8,128)(2,1)S(1)}, f32[4,128,128]{2,1,0:T(8,128)S(1)}, bf16[128,128]{1,0:T(8,128)(2,1)S(1)}, bf16[128,128]{1,0:T(8,128)(2,1...) custom-call(s32[1]{0:T(128)} %bitcast.place_ref, f32[128,128]{1,0:T(8,128)S(1)} %get-tuple-element.40.exit_ref, ...), custom_call_target="tpu_custom_call" | custom-call | flops 100663296 | bytes 1000000 | tf_op jit(solution)/shard_map/pallas_call | solution.py:21
  14.2 2.4 %collective-permute-start.7 = (bf16[512,128]{1,0:T(8,128)(2,1)S(1)}, bf16[512,128]{1,0:T(8,128)(2,1)S(1)}, u32[]{:S(2)}, u32[]{:S(2)}) collective-permute-start(bf16[512,128]{1,0:T(8,128)(2,1)S(1)} %get-tuple-element.45.refs_3_), channel_id=1, source_target_pairs={{0,16},{2,18},{4,20},{6,22},{8,24},{10,26},{12,28},{14,30},{16,0},... | collective-permute-start | bytes 393224 | tf_op jit(solution)/shard_map/ppermute | solution.py:393
  16.7 1.5 %collective-permute-start.8 = (bf16[512,128]{1,0:T(8,128)(2,1)S(1)}, bf16[512,128]{1,0:T(8,128)(2,1)S(1)}, u32[]{:S(2)}, u32[]{:S(2)}) collective-permute-start(bf16[512,128]{1,0:T(8,128)(2,1)S(1)} %get-tuple-element.45.refs_3_), channel_id=1, source_target_pairs={{0,24},{2,26},{4,28},{6,30},{8,16},{10,18},{12,20},{14,22},{16,8},... | collective-permute-start | bytes 393224 | tf_op jit(solution)/shard_map/ppermute | solution.py:393
  18.2 0.5 %collective-permute-start.9 = (bf16[512,128]{1,0:T(8,128)(2,1)S(1)}, bf16[512,128]{1,0:T(8,128)(2,1)S(1)}, u32[]{:S(2)}, u32[]{:S(2)}) collective-permute-start(bf16[512,128]{1,0:T(8,128)(2,1)S(1)} %get-tuple-element.45.refs_3_), channel_id=1, source_target_pairs={{0,8},{2,10},{4,12},{6,14},{8,0},{10,2},{12,4},{14,6},{16,24},{18,... | collective-permute-start | bytes 393224 | tf_op jit(solution)/shard_map/ppermute | solution.py:393
  18.7 1.1 %collective-permute-done.5.refs_1_ = bf16[128,128]{1,0:T(8,128)(2,1)S(1)} collective-permute-done((bf16[128,128]{1,0:T(8,128)(2,1)S(1)}, bf16[128,128]{1,0:T(8,128)(2,1)S(1)}, u32[]{:S(2)}, u32[]{:S(2)}) %collective-permute-start.5) | collective-permute-done | bytes 32800 | tf_op jit(solution)/shard_map/ppermute | solution.py:393
  19.8 1.3 %shard_map.112 = (bf16[512,128]{1,0:T(8,128)(2,1)S(1)}, s32[1]{0:T(128)}) custom-call(s32[1]{0:T(128)} %bitcast.place_ref, s32[16]{0:T(128)S(1)} %bitcast.5, f32[4,128,128]{2,1,0:T(8,128)S(1)} %get-tuple-element.42.after_ref.refs_4_, bf16[128,128]{1,0:T(8,128)(2,1)S(1)} %collective-permute-done.4.refs_0_, ...), custom_call_target="tpu_custom_call" | custom-call | bytes 1000000 | tf_op jit(solution)/shard_map/pallas_call | solution.py:21
  21.1 2.5 %collective-permute-start.13 = (bf16[512,128]{1,0:T(8,128)(2,1)S(1)}, bf16[512,128]{1,0:T(8,128)(2,1)S(1)}, u32[]{:S(2)}, u32[]{:S(2)}) collective-permute-start(bf16[512,128]{1,0:T(8,128)(2,1)S(1)} %get-tuple-element.54.refs_7_), channel_id=1, source_target_pairs={{0,6},{2,4},{4,2},{6,0},{8,14},{10,12},{12,10},{14,8},{16,22},{18,... | collective-permute-start | bytes 393224 | tf_op jit(solution)/shard_map/ppermute | solution.py:393
  24.0 2.7 %collective-permute-done.7.refs_0_ = bf16[512,128]{1,0:T(8,128)(2,1)S(1)} collective-permute-done((bf16[512,128]{1,0:T(8,128)(2,1)S(1)}, bf16[512,128]{1,0:T(8,128)(2,1)S(1)}, u32[]{:S(2)}, u32[]{:S(2)}) %collective-permute-start.7) | collective-permute-done | bytes 131104 | tf_op jit(solution)/shard_map/ppermute | solution.py:393
  26.7 1.5 %collective-permute-start.15 = (bf16[512,128]{1,0:T(8,128)(2,1)S(1)}, bf16[512,128]{1,0:T(8,128)(2,1)S(1)}, u32[]{:S(2)}, u32[]{:S(2)}) collective-permute-start(bf16[512,128]{1,0:T(8,128)(2,1)S(1)} %get-tuple-element.54.refs_7_), channel_id=1, source_target_pairs={{0,2},{2,0},{4,6},{6,4},{8,10},{10,8},{12,14},{14,12},{16,18},{18,... | collective-permute-start | bytes 393224 | tf_op jit(solution)/shard_map/ppermute | solution.py:393
  28.2 0.7 %shard_map.113 = (bf16[512,128]{1,0:T(8,128)(2,1)S(1)}, bf16[512,128]{1,0:T(8,128)(2,1)S(1)}, bf16[512,128]{1,0:T(8,128)(2,1)S(1)}, bf16[512,128]{1,0:T(8,128)(2,1)S(1)}) custom-call(s32[1]{0:T(128)} %bitcast.place_ref, bf16[512,128]{1,0:T(8,128)(2,1)S(1)} %collective-permute-done.7.refs_0_, bf16[512,128]{1,0:T(8,128)(2,1)S(1)} %collective-permute-done.8.refs_1_, ...), custom_call_target="tpu_custom_call" | custom-call | flops 201326592 | bytes 1000000 | tf_op jit(solution)/shard_map/pallas_call | solution.py:21
  29.0 1.6 %collective-permute-start.10 = (bf16[512,128]{1,0:T(8,128)(2,1)S(1)}, bf16[512,128]{1,0:T(8,128)(2,1)S(1)}, u32[]{:S(2)}, u32[]{:S(2)}) collective-permute-start(bf16[512,128]{1,0:T(8,128)(2,1)S(1)} %get-tuple-element.50), channel_id=1, source_target_pairs={{0,6},{2,4},{4,2},{6,0},{8,14},{10,12},{12,10},{14,8},{16,22},{18,... | collective-permute-start | bytes 393224 | tf_op jit(solution)/shard_map/ppermute | solution.py:393
  30.5 0.5 %collective-permute-start.11 = (bf16[512,128]{1,0:T(8,128)(2,1)S(1)}, bf16[512,128]{1,0:T(8,128)(2,1)S(1)}, u32[]{:S(2)}, u32[]{:S(2)}) collective-permute-start(bf16[512,128]{1,0:T(8,128)(2,1)S(1)} %get-tuple-element.51), channel_id=1, source_target_pairs={{0,4},{2,6},{4,0},{6,2},{8,12},{10,14},{12,8},{14,10},{16,20},{18,... | collective-permute-start | bytes 393224 | tf_op jit(solution)/shard_map/ppermute | solution.py:393
  31.0 1.5 %collective-permute-start.12 = (bf16[512,128]{1,0:T(8,128)(2,1)S(1)}, bf16[512,128]{1,0:T(8,128)(2,1)S(1)}, u32[]{:S(2)}, u32[]{:S(2)}) collective-permute-start(bf16[512,128]{1,0:T(8,128)(2,1)S(1)} %get-tuple-element.52), channel_id=1, source_target_pairs={{0,2},{2,0},{4,6},{6,4},{8,10},{10,8},{12,14},{14,12},{16,18},{18,... | collective-permute-start | bytes 393224 | tf_op jit(solution)/shard_map/ppermute | solution.py:393
  32.5 3.9 %shard_map.114 = (bf16[8,128,128]{2,1,0:T(8,128)(2,1)S(1)}, f32[8,128,128]{2,1,0:T(8,128)S(1)}, f32[8,128,1]{2,1,0:T(8,128)S(1)}, f32[8,128,1]{2,1,0:T(8,128)S(1)}) custom-call(bf16[128,2048]{1,0:T(8,128)(2,1)S(1)} %get-tuple-element.55.rows_ref, bf16[2048,1024]{1,0:T(8,128)(2,1)} %weight_hbm.1, f32[1,128]{1,0:T(1,128)S(1)} %get-tuple-element.56.gain_ref, ...), custom_call_target="tpu_custom_call" | custom-call | flops 1073741824 | bytes 16777216 | tf_op jit(solution)/shard_map/pallas_call | solution.py:21
  37.1 2.9 %shard_map.115 = (bf16[64,2048]{1,0:T(8,128)(2,1)S(1)}, bf16[64,2048]{1,0:T(8,128)(2,1)S(1)}) custom-call(s32[1]{0:T(128)} %bitcast.place_ref, s32[1]{0:T(128)} %bitcast.1.core_ref, s32[1]{0:T(128)} %get-tuple-element.44.table_ref, bf16[512,128]{1,0:T(8,128)(2,1)S(1)} %collective-permute-done.10.refs_0_, ...), custom_call_target="tpu_custom_call" | custom-call | flops 536870912 | bytes 4000000 | tf_op jit(solution)/shard_map/pallas_call | solution.py:21
  40.1 1.5 %collective-permute-done.16 = bf16[64,2048]{1,0:T(8,128)(2,1)S(1)} collective-permute-done((bf16[64,2048]{1,0:T(8,128)(2,1)S(1)}, bf16[64,2048]{1,0:T(8,128)(2,1)S(1)}, u32[]{:S(2)}, u32[]{:S(2)}) %collective-permute-start.16) | collective-permute-done | bytes 262176 | tf_op jit(solution)/shard_map/ppermute | solution.py:516
  41.6 0.8 %add.3 = bf16[64,2048]{1,0:T(8,128)(2,1)} add(bf16[64,2048]{1,0:T(8,128)(2,1)S(1)} %get-tuple-element.65, bf16[64,2048]{1,0:T(8,128)(2,1)S(1)} %collective-permute-done.16) | non-fusion elementwise | flops 131072 | bytes 786432 | tf_op jit(solution)/shard_map/add | solution.py:516
  (22 shorter events, 1.3 us)
Async XLA Ops:
  0.0 19.8 %copy-start.1 = (s32[1,16]{1,0:T(1,128)S(1)}, s32[1,16]{1,0:T(1,128)}, u32[]{:S(2)}) copy-start(s32[1,16]{1,0:T(1,128)} %param.21) | copy-start | bytes 196
  0.0 2.6 %collective-permute-start = (bf16[64,2048]{1,0:T(8,128)(2,1)}, bf16[64,2048]{1,0:T(8,128)(2,1)S(1)}, u32[]{:S(2)}, u32[]{:S(2)}) collective-permute-start(bf16[64,2048]{1,0:T(8,128)(2,1)} %mine_hbm.1), channel_id=1, source_target_pairs={{0,1},{1,0},{2,3},{3,2},{4,5},{5,4},{6,7},{7,6},{8,9},{9,8},{10,11... | collective-permute-start | bytes 786440 | tf_op jit(solution)/shard_map/ppermute | solution.py:379
  5.0 8.2 %collective-permute-start.1 = (f32[128,128]{1,0:T(8,128)S(1)}, f32[128,128]{1,0:T(8,128)S(1)}, u32[]{:S(2)}, u32[]{:S(2)}) collective-permute-start(f32[128,128]{1,0:T(8,128)S(1)} %get-tuple-element.41.refs_3_), channel_id=1, source_target_pairs={{0,6},{2,4},{4,2},{6,0},{8,14},{10,12},{12,10},{14,8},{16,22},{18,... | collective-permute-start | bytes 196616 | tf_op jit(solution)/shard_map/ppermute | solution.py:393
  8.5 5.2 %collective-permute-start.2 = (f32[128,128]{1,0:T(8,128)S(1)}, f32[128,128]{1,0:T(8,128)S(1)}, u32[]{:S(2)}, u32[]{:S(2)}) collective-permute-start(f32[128,128]{1,0:T(8,128)S(1)} %get-tuple-element.41.refs_3_), channel_id=1, source_target_pairs={{0,4},{2,6},{4,0},{6,2},{8,12},{10,14},{12,8},{14,10},{16,20},{18,... | collective-permute-start | bytes 196616 | tf_op jit(solution)/shard_map/ppermute | solution.py:393
  9.0 4.7 %collective-permute-start.3 = (f32[128,128]{1,0:T(8,128)S(1)}, f32[128,128]{1,0:T(8,128)S(1)}, u32[]{:S(2)}, u32[]{:S(2)}) collective-permute-start(f32[128,128]{1,0:T(8,128)S(1)} %get-tuple-element.41.refs_3_), channel_id=1, source_target_pairs={{0,2},{2,0},{4,6},{6,4},{8,10},{10,8},{12,14},{14,12},{16,18},{18,... | collective-permute-start | bytes 196616 | tf_op jit(solution)/shard_map/ppermute | solution.py:393
  9.1 9.1 %collective-permute-start.4 = (bf16[128,128]{1,0:T(8,128)(2,1)S(1)}, bf16[128,128]{1,0:T(8,128)(2,1)S(1)}, u32[]{:S(2)}, u32[]{:S(2)}) collective-permute-start(bf16[128,128]{1,0:T(8,128)(2,1)S(1)} %get-tuple-element.43.refs_3_.val_ref), channel_id=1, source_target_pairs={{0,24},{2,26},{4,28},{6,30},{8,16},{10,18},{12,20},{14,22},{16,8},... | collective-permute-start | bytes 98312 | tf_op jit(solution)/shard_map/ppermute | solution.py:393
  13.1 6.6 %collective-permute-start.5 = (bf16[128,128]{1,0:T(8,128)(2,1)S(1)}, bf16[128,128]{1,0:T(8,128)(2,1)S(1)}, u32[]{:S(2)}, u32[]{:S(2)}) collective-permute-start(bf16[128,128]{1,0:T(8,128)(2,1)S(1)} %get-tuple-element.43.refs_3_.val_ref), channel_id=1, source_target_pairs={{0,16},{2,18},{4,20},{6,22},{8,24},{10,26},{12,28},{14,30},{16,0},... | collective-permute-start | bytes 98312 | tf_op jit(solution)/shard_map/ppermute | solution.py:393
  13.2 6.6 %collective-permute-start.6 = (bf16[128,128]{1,0:T(8,128)(2,1)S(1)}, bf16[128,128]{1,0:T(8,128)(2,1)S(1)}, u32[]{:S(2)}, u32[]{:S(2)}) collective-permute-start(bf16[128,128]{1,0:T(8,128)(2,1)S(1)} %get-tuple-element.43.refs_3_.val_ref), channel_id=1, source_target_pairs={{0,8},{2,10},{4,12},{6,14},{8,0},{10,2},{12,4},{14,6},{16,24},{18,... | collective-permute-start | bytes 98312 | tf_op jit(solution)/shard_map/ppermute | solution.py:393
  13.7 23.4 %copy-start = (bf16[1024,2048]{1,0:T(8,128)(2,1)S(1)}, bf16[1024,2048]{1,0:T(8,128)(2,1)}, u32[]{:S(2)}) copy-start(bf16[1024,2048]{1,0:T(8,128)(2,1)} %refs_12_.1) | copy-start | bytes 12582916
  14.2 12.5 %collective-permute-start.7 = (bf16[512,128]{1,0:T(8,128)(2,1)S(1)}, bf16[512,128]{1,0:T(8,128)(2,1)S(1)}, u32[]{:S(2)}, u32[]{:S(2)}) collective-permute-start(bf16[512,128]{1,0:T(8,128)(2,1)S(1)} %get-tuple-element.45.refs_3_), channel_id=1, source_target_pairs={{0,16},{2,18},{4,20},{6,22},{8,24},{10,26},{12,28},{14,30},{16,0},... | collective-permute-start | bytes 393224 | tf_op jit(solution)/shard_map/ppermute | solution.py:393
  16.7 11.5 %collective-permute-start.8 = (bf16[512,128]{1,0:T(8,128)(2,1)S(1)}, bf16[512,128]{1,0:T(8,128)(2,1)S(1)}, u32[]{:S(2)}, u32[]{:S(2)}) collective-permute-start(bf16[512,128]{1,0:T(8,128)(2,1)S(1)} %get-tuple-element.45.refs_3_), channel_id=1, source_target_pairs={{0,24},{2,26},{4,28},{6,30},{8,16},{10,18},{12,20},{14,22},{16,8},... | collective-permute-start | bytes 393224 | tf_op jit(solution)/shard_map/ppermute | solution.py:393
  18.2 10.0 %collective-permute-start.9 = (bf16[512,128]{1,0:T(8,128)(2,1)S(1)}, bf16[512,128]{1,0:T(8,128)(2,1)S(1)}, u32[]{:S(2)}, u32[]{:S(2)}) collective-permute-start(bf16[512,128]{1,0:T(8,128)(2,1)S(1)} %get-tuple-element.45.refs_3_), channel_id=1, source_target_pairs={{0,8},{2,10},{4,12},{6,14},{8,0},{10,2},{12,4},{14,6},{16,24},{18,... | collective-permute-start | bytes 393224 | tf_op jit(solution)/shard_map/ppermute | solution.py:393
  21.1 9.9 %collective-permute-start.13 = (bf16[512,128]{1,0:T(8,128)(2,1)S(1)}, bf16[512,128]{1,0:T(8,128)(2,1)S(1)}, u32[]{:S(2)}, u32[]{:S(2)}) collective-permute-start(bf16[512,128]{1,0:T(8,128)(2,1)S(1)} %get-tuple-element.54.refs_7_), channel_id=1, source_target_pairs={{0,6},{2,4},{4,2},{6,0},{8,14},{10,12},{12,10},{14,8},{16,22},{18,... | collective-permute-start | bytes 393224 | tf_op jit(solution)/shard_map/ppermute | solution.py:393
  23.6 12.8 %collective-permute-start.14 = (bf16[512,128]{1,0:T(8,128)(2,1)S(1)}, bf16[512,128]{1,0:T(8,128)(2,1)S(1)}, u32[]{:S(2)}, u32[]{:S(2)}) collective-permute-start(bf16[512,128]{1,0:T(8,128)(2,1)S(1)} %get-tuple-element.54.refs_7_), channel_id=1, source_target_pairs={{0,4},{2,6},{4,0},{6,2},{8,12},{10,14},{12,8},{14,10},{16,20},{18,... | collective-permute-start | bytes 393224 | tf_op jit(solution)/shard_map/ppermute | solution.py:393
  26.7 9.8 %collective-permute-start.15 = (bf16[512,128]{1,0:T(8,128)(2,1)S(1)}, bf16[512,128]{1,0:T(8,128)(2,1)S(1)}, u32[]{:S(2)}, u32[]{:S(2)}) collective-permute-start(bf16[512,128]{1,0:T(8,128)(2,1)S(1)} %get-tuple-element.54.refs_7_), channel_id=1, source_target_pairs={{0,2},{2,0},{4,6},{6,4},{8,10},{10,8},{12,14},{14,12},{16,18},{18,... | collective-permute-start | bytes 393224 | tf_op jit(solution)/shard_map/ppermute | solution.py:393
  29.0 7.5 %collective-permute-start.10 = (bf16[512,128]{1,0:T(8,128)(2,1)S(1)}, bf16[512,128]{1,0:T(8,128)(2,1)S(1)}, u32[]{:S(2)}, u32[]{:S(2)}) collective-permute-start(bf16[512,128]{1,0:T(8,128)(2,1)S(1)} %get-tuple-element.50), channel_id=1, source_target_pairs={{0,6},{2,4},{4,2},{6,0},{8,14},{10,12},{12,10},{14,8},{16,22},{18,... | collective-permute-start | bytes 393224 | tf_op jit(solution)/shard_map/ppermute | solution.py:393
  30.5 6.4 %collective-permute-start.11 = (bf16[512,128]{1,0:T(8,128)(2,1)S(1)}, bf16[512,128]{1,0:T(8,128)(2,1)S(1)}, u32[]{:S(2)}, u32[]{:S(2)}) collective-permute-start(bf16[512,128]{1,0:T(8,128)(2,1)S(1)} %get-tuple-element.51), channel_id=1, source_target_pairs={{0,4},{2,6},{4,0},{6,2},{8,12},{10,14},{12,8},{14,10},{16,20},{18,... | collective-permute-start | bytes 393224 | tf_op jit(solution)/shard_map/ppermute | solution.py:393
  31.0 6.1 %collective-permute-start.12 = (bf16[512,128]{1,0:T(8,128)(2,1)S(1)}, bf16[512,128]{1,0:T(8,128)(2,1)S(1)}, u32[]{:S(2)}, u32[]{:S(2)}) collective-permute-start(bf16[512,128]{1,0:T(8,128)(2,1)S(1)} %get-tuple-element.52), channel_id=1, source_target_pairs={{0,2},{2,0},{4,6},{6,4},{8,10},{10,8},{12,14},{14,12},{16,18},{18,... | collective-permute-start | bytes 393224 | tf_op jit(solution)/shard_map/ppermute | solution.py:393
  40.0 1.6 %collective-permute-start.16 = (bf16[64,2048]{1,0:T(8,128)(2,1)S(1)}, bf16[64,2048]{1,0:T(8,128)(2,1)S(1)}, u32[]{:S(2)}, u32[]{:S(2)}) collective-permute-start(bf16[64,2048]{1,0:T(8,128)(2,1)S(1)} %get-tuple-element.66), channel_id=1, source_target_pairs={{0,1},{1,0},{2,3},{3,2},{4,5},{5,4},{6,7},{7,6},{8,9},{9,8},{10,11... | collective-permute-start | bytes 786440 | tf_op jit(solution)/shard_map/ppermute | solution.py:516

commit v18 on v17

--- a/solution.py
+++ b/solution.py
@@ -90,12 +90,12 @@
     return inverse
 
 
-def load_kernel(size, key_hbm, dir_hbm, value_hbm, rate_hbm, key_gain_hbm,
+def load_kernel(size, key_hbm, dir_hbm, rate_hbm, key_gain_hbm,
                 query_gain_hbm, mine_hbm, weight_ref, rate_ref, key_gain_ref, query_gain_ref,
                 mine_ref, sems):
     pairs = [
         (hbm, weight_ref.at[:, index * size : (index + 1) * size])
-        for index, hbm in enumerate((key_hbm, dir_hbm, value_hbm))
+        for index, hbm in enumerate((key_hbm, dir_hbm))
     ]
     pairs += [(rate_hbm, rate_ref), (key_gain_hbm, key_gain_ref)]
     pairs += [(query_gain_hbm, query_gain_ref), (mine_hbm, mine_ref)]
@@ -107,7 +107,10 @@
 
 
 def prepare_kernel(core_ref, mine_ref, other_ref, weight_ref, rate_ref, bias_ref, gain_ref,
-                   rows_ref, kn_ref, val_ref, dirs_ref, coeff_ref, solved_ref, exit_ref, turn_ref):
+                   value_hbm, rows_ref, kn_ref, val_ref, dirs_ref, coeff_ref, solved_ref, exit_ref,
+                   turn_ref, value_ref, value_sem):
+    value_copy = pltpu.make_async_copy(value_hbm, value_ref, value_sem)
+    value_copy.start()
     core = core_ref[0]
     half = mine_ref.shape[0]
     rows_ref[pl.ds(pl.multiple_of(core * half, half), half), :] = mine_ref[...]
@@ -115,13 +118,12 @@
     seg = rows_ref[...]
     size = turn_ref.shape[0]
     raw = jnp.dot(seg, weight_ref[...], preferred_element_type=F32)
-    keys, raw, vals = raw[:, :size], raw[:, size : 2 * size], raw[:, 2 * size :]
+    keys, raw = raw[:, :size], raw[:, size:]
     kn = keys * lax.rsqrt(jnp.mean(keys * keys, axis=-1, keepdims=True) + EPSILON) * gain_ref[...]
     dirs = raw * lax.rsqrt(jnp.sum(raw * raw, axis=-1, keepdims=True) + EPSILON)
     vector = jnp.broadcast_to(rate_ref[...], (16, seg.shape[1]))
     logits = lax.dot_general(seg, vector, (((1,), (1,)), ((), ())), preferred_element_type=F32)
     rates = 2.0 * jax.nn.sigmoid(logits[:, :1] + bias_ref[0])
-    val_ref[...] = vals.astype(BF16)
     kn_ref[...] = kn
     dirs_ref[...] = dirs
     tokens, size = dirs.shape
@@ -131,6 +133,8 @@
     lower = jnp.where(below, rates * grams[:, :tokens], 0.0)
     crossing = jnp.where(below, rates * grams[:, tokens:], 0.0)
     inverse = merge_inverse(lower, rows, cols)
+    value_copy.wait()
+    val_ref[...] = jnp.dot(seg, value_ref[...], preferred_element_type=F32).astype(BF16)
     both = dot3(inverse, jnp.concatenate([crossing, rates * dirs], axis=1))
     coeff_ref[...] = both[:, :tokens]
     solved_ref[...] = both[:, tokens:]
@@ -406,18 +410,18 @@
     weights, rate_row, key_gain, query_gain, mine = call(
         functools.partial(load_kernel, size),
         (
-            shaped((width, 3 * size), BF16), shaped((1, width), BF16), shaped((1, size), F32),
+            shaped((width, 2 * size), BF16), shaped((1, width), BF16), shaped((1, size), F32),
             shaped((1, size), F32), shaped((half, width), BF16),
         ),
         tuple(
             in_hbm(array)
             for array in (
-                w_key, w_dir, w_value, u_rate, k_gain.reshape(1, size), q_gain.reshape(1, size),
+                w_key, w_dir, u_rate, k_gain.reshape(1, size), q_gain.reshape(1, size),
                 hidden,
             )
         ),
-        in_specs=[hbm] * 7,
-        scratch=(pltpu.SemaphoreType.DMA((7,)),),
+        in_specs=[hbm] * 6,
+        scratch=(pltpu.SemaphoreType.DMA((6,)),),
         moved=12 * width * size,
     )
     rows, kn, val, dirs, coeff, solved, exit_keys, turn = call(
@@ -426,8 +430,9 @@
             shaped((tokens, width), BF16), square, shaped((tokens, size), BF16), square, square,
             square, square, shaped((size, size), F32),
         ),
-        (core, mine, other, weights, rate_row, rate_bias, key_gain),
-        in_specs=[smem] + [vmem] * 4 + [smem, vmem],
+        (core, mine, other, weights, rate_row, rate_bias, key_gain, in_hbm(w_value)),
+        in_specs=[smem] + [vmem] * 4 + [smem, vmem, hbm],
+        scratch=(pltpu.VMEM(w_value.shape, BF16), pltpu.SemaphoreType.DMA),
         flops=6 * tokens * width * size,
         moved=8 * width * size,
     )

time: 42.5 us -> 42.5 us (level)
  local copies, waits for them, and re-layouts: 0.01 us -> 0.66 us
  waiting for transfers between devices: 5.94 us -> 5.34 us
    unnamed x4, local copies, waits for them, and re-layouts: 0.01 us -> 0.66 us
    ppermute x15, waiting for transfers between devices: 4.42 us -> 3.81 us  [swapped(): out[step] = lax.ppermute(values[step], 'ctx', pairs_of(step))]
where the time goes in v18:
time: 42.5 us; the launch traced here: 42.3 us
  starting transfers between devices  21.6 us (51%)
  Pallas kernels  13.2 us (31%)
  waiting for transfers between devices  5.34 us (13%)
  other arithmetic  0.77 us (2%)
  between operations  0.76 us (2%)
  local copies, waits for them, and re-layouts  0.66 us (2%)
    ppermute x15, starting transfers between devices, swapped(): out[step] = lax.ppermute(values[step], 'ctx', pairs_of(step))  21.1 us
    pallas_call x7, Pallas kernels, call(): pl.pallas_call(kernel, out_shape=out_shape, in_specs=in_specs or [vmem] *...  13.2 us
    ppermute x15, waiting for transfers between devices, swapped(): out[step] = lax.ppermute(values[step], 'ctx', pairs_of(step))  3.81 us
    ppermute x1, waiting for transfers between devices, body(): return kept + lax.ppermute(away, 'head', [(0, 1), (1, 0)])  1.52 us
  transfers between devices with their start and end apart: 17, of which 5 were waited for; matrix products, arithmetic and copies ran while one was open for 0% of the time, Pallas kernels for 19%

profile of v18, /device:TPU:0, one launch (start us, length us, event | category | flops | bytes accessed | tf_op | source)
XLA Modules:
  0.0 42.3 jit_solution(13743617607317630850)
XLA Ops:
  0.0 0.5 %collective-permute-start = (bf16[64,2048]{1,0:T(8,128)(2,1)}, bf16[64,2048]{1,0:T(8,128)(2,1)S(1)}, u32[]{:S(2)}, u32[]{:S(2)}) collective-permute-start(bf16[64,2048]{1,0:T(8,128)(2,1)} %mine_hbm.1), channel_id=1, source_target_pairs={{0,1},{1,0},{2,3},{3,2},{4,5},{5,4},{6,7},{7,6},{8,9},{9,8},{10,11... | collective-permute-start | bytes 786440 | tf_op jit(solution)/shard_map/ppermute | solution.py:383
  1.1 1.4 %shard_map.109 = (bf16[2048,256]{1,0:T(8,128)(2,1)S(1)}, bf16[1,2048]{1,0:T(2,128)(2,1)S(1)}, f32[1,128]{1,0:T(1,128)S(1)}, f32[1,128]{1,0:T(1,128)S(1)}, bf16[64,2048]{1,0:T(8,128)(2,1)S(1)}) custom-call(bf16[2048,128]{1,0:T(8,128)(2,1)} %key_hbm.1, bf16[2048,128]{1,0:T(8,128)(2,1)} %dir_hbm.1, bf16[1,2048]{1,0:T(2,128)(2,1)} %rate_hbm.1, ...), custom_call_target="tpu_custom_call" | custom-call | bytes 3145728 | tf_op jit(solution)/shard_map/pallas_call | solution.py:21
  2.5 2.4 %shard_map.110 = (bf16[128,2048]{1,0:T(8,128)(2,1)S(1)}, f32[128,128]{1,0:T(8,128)S(1)}, bf16[128,128]{1,0:T(8,128)(2,1)S(1)}, f32[128,128]{1,0:T(8,128)S(1)}, f...) custom-call(s32[1]{0:T(128)} %bitcast.1.core_ref, ...), custom_call_target="tpu_custom_call" | custom-call | flops 201326592 | bytes 2097152 | tf_op jit(solution)/shard_map/pallas_call | solution.py:21
  4.9 3.5 %collective-permute-start.1 = (f32[128,128]{1,0:T(8,128)S(1)}, f32[128,128]{1,0:T(8,128)S(1)}, u32[]{:S(2)}, u32[]{:S(2)}) collective-permute-start(f32[128,128]{1,0:T(8,128)S(1)} %get-tuple-element.41.refs_3_), channel_id=1, source_target_pairs={{0,6},{2,4},{4,2},{6,0},{8,14},{10,12},{12,10},{14,8},{16,22},{18,... | collective-permute-start | bytes 196616 | tf_op jit(solution)/shard_map/ppermute | solution.py:397
  8.4 0.5 %collective-permute-start.2 = (f32[128,128]{1,0:T(8,128)S(1)}, f32[128,128]{1,0:T(8,128)S(1)}, u32[]{:S(2)}, u32[]{:S(2)}) collective-permute-start(f32[128,128]{1,0:T(8,128)S(1)} %get-tuple-element.41.refs_3_), channel_id=1, source_target_pairs={{0,4},{2,6},{4,0},{6,2},{8,12},{10,14},{12,8},{14,10},{16,20},{18,... | collective-permute-start | bytes 196616 | tf_op jit(solution)/shard_map/ppermute | solution.py:397
  9.1 4.0 %collective-permute-start.4 = (bf16[128,128]{1,0:T(8,128)(2,1)S(1)}, bf16[128,128]{1,0:T(8,128)(2,1)S(1)}, u32[]{:S(2)}, u32[]{:S(2)}) collective-permute-start(bf16[128,128]{1,0:T(8,128)(2,1)S(1)} %get-tuple-element.43.refs_3_.val_ref), channel_id=1, source_target_pairs={{0,24},{2,26},{4,28},{6,30},{8,16},{10,18},{12,20},{14,22},{16,8},... | collective-permute-start | bytes 98312 | tf_op jit(solution)/shard_map/ppermute | solution.py:397
  13.1 0.6 %collective-permute-start.6 = (bf16[128,128]{1,0:T(8,128)(2,1)S(1)}, bf16[128,128]{1,0:T(8,128)(2,1)S(1)}, u32[]{:S(2)}, u32[]{:S(2)}) collective-permute-start(bf16[128,128]{1,0:T(8,128)(2,1)S(1)} %get-tuple-element.43.refs_3_.val_ref), channel_id=1, source_target_pairs={{0,8},{2,10},{4,12},{6,14},{8,0},{10,2},{12,4},{14,6},{16,24},{18,... | collective-permute-start | bytes 98312 | tf_op jit(solution)/shard_map/ppermute | solution.py:397
  13.7 0.5 %shard_map.111 = (bf16[512,128]{1,0:T(8,128)(2,1)S(1)}, f32[4,128,128]{2,1,0:T(8,128)S(1)}, bf16[128,128]{1,0:T(8,128)(2,1)S(1)}, bf16[128,128]{1,0:T(8,128)(2,1...) custom-call(s32[1]{0:T(128)} %bitcast.place_ref, f32[128,128]{1,0:T(8,128)S(1)} %get-tuple-element.40.exit_ref, ...), custom_call_target="tpu_custom_call" | custom-call | flops 100663296 | bytes 1000000 | tf_op jit(solution)/shard_map/pallas_call | solution.py:21
  14.2 2.4 %collective-permute-start.7 = (bf16[512,128]{1,0:T(8,128)(2,1)S(1)}, bf16[512,128]{1,0:T(8,128)(2,1)S(1)}, u32[]{:S(2)}, u32[]{:S(2)}) collective-permute-start(bf16[512,128]{1,0:T(8,128)(2,1)S(1)} %get-tuple-element.45.refs_3_), channel_id=1, source_target_pairs={{0,16},{2,18},{4,20},{6,22},{8,24},{10,26},{12,28},{14,30},{16,0},... | collective-permute-start | bytes 393224 | tf_op jit(solution)/shard_map/ppermute | solution.py:397
  16.6 1.5 %collective-permute-start.8 = (bf16[512,128]{1,0:T(8,128)(2,1)S(1)}, bf16[512,128]{1,0:T(8,128)(2,1)S(1)}, u32[]{:S(2)}, u32[]{:S(2)}) collective-permute-start(bf16[512,128]{1,0:T(8,128)(2,1)S(1)} %get-tuple-element.45.refs_3_), channel_id=1, source_target_pairs={{0,24},{2,26},{4,28},{6,30},{8,16},{10,18},{12,20},{14,22},{16,8},... | collective-permute-start | bytes 393224 | tf_op jit(solution)/shard_map/ppermute | solution.py:397
  18.1 0.5 %collective-permute-start.9 = (bf16[512,128]{1,0:T(8,128)(2,1)S(1)}, bf16[512,128]{1,0:T(8,128)(2,1)S(1)}, u32[]{:S(2)}, u32[]{:S(2)}) collective-permute-start(bf16[512,128]{1,0:T(8,128)(2,1)S(1)} %get-tuple-element.45.refs_3_), channel_id=1, source_target_pairs={{0,8},{2,10},{4,12},{6,14},{8,0},{10,2},{12,4},{14,6},{16,24},{18,... | collective-permute-start | bytes 393224 | tf_op jit(solution)/shard_map/ppermute | solution.py:397
  18.6 1.1 %collective-permute-done.5.refs_1_ = bf16[128,128]{1,0:T(8,128)(2,1)S(1)} collective-permute-done((bf16[128,128]{1,0:T(8,128)(2,1)S(1)}, bf16[128,128]{1,0:T(8,128)(2,1)S(1)}, u32[]{:S(2)}, u32[]{:S(2)}) %collective-permute-start.5) | collective-permute-done | bytes 32800 | tf_op jit(solution)/shard_map/ppermute | solution.py:397
  19.7 0.7 %copy-done.1 = s32[1,16]{1,0:T(1,128)S(1)} copy-done((s32[1,16]{1,0:T(1,128)S(1)}, s32[1,16]{1,0:T(1,128)}, u32[]{:S(2)}) %copy-start.1) | copy-done | bytes 88
  20.4 1.3 %shard_map.112 = (bf16[512,128]{1,0:T(8,128)(2,1)S(1)}, s32[1]{0:T(128)}) custom-call(s32[1]{0:T(128)} %bitcast.place_ref, s32[16]{0:T(128)S(1)} %bitcast.5, f32[4,128,128]{2,1,0:T(8,128)S(1)} %get-tuple-element.42.after_ref.refs_4_, bf16[128,128]{1,0:T(8,128)(2,1)S(1)} %collective-permute-done.4.refs_0_, ...), custom_call_target="tpu_custom_call" | custom-call | bytes 1000000 | tf_op jit(solution)/shard_map/pallas_call | solution.py:21
  21.7 2.5 %collective-permute-start.13 = (bf16[512,128]{1,0:T(8,128)(2,1)S(1)}, bf16[512,128]{1,0:T(8,128)(2,1)S(1)}, u32[]{:S(2)}, u32[]{:S(2)}) collective-permute-start(bf16[512,128]{1,0:T(8,128)(2,1)S(1)} %get-tuple-element.54.refs_7_), channel_id=1, source_target_pairs={{0,6},{2,4},{4,2},{6,0},{8,14},{10,12},{12,10},{14,8},{16,22},{18,... | collective-permute-start | bytes 393224 | tf_op jit(solution)/shard_map/ppermute | solution.py:397
  24.5 2.1 %collective-permute-done.7.refs_0_ = bf16[512,128]{1,0:T(8,128)(2,1)S(1)} collective-permute-done((bf16[512,128]{1,0:T(8,128)(2,1)S(1)}, bf16[512,128]{1,0:T(8,128)(2,1)S(1)}, u32[]{:S(2)}, u32[]{:S(2)}) %collective-permute-start.7) | collective-permute-done | bytes 131104 | tf_op jit(solution)/shard_map/ppermute | solution.py:397
  26.6 1.6 %collective-permute-start.15 = (bf16[512,128]{1,0:T(8,128)(2,1)S(1)}, bf16[512,128]{1,0:T(8,128)(2,1)S(1)}, u32[]{:S(2)}, u32[]{:S(2)}) collective-permute-start(bf16[512,128]{1,0:T(8,128)(2,1)S(1)} %get-tuple-element.54.refs_7_), channel_id=1, source_target_pairs={{0,2},{2,0},{4,6},{6,4},{8,10},{10,8},{12,14},{14,12},{16,18},{18,... | collective-permute-start | bytes 393224 | tf_op jit(solution)/shard_map/ppermute | solution.py:397
  28.2 0.7 %shard_map.113 = (bf16[512,128]{1,0:T(8,128)(2,1)S(1)}, bf16[512,128]{1,0:T(8,128)(2,1)S(1)}, bf16[512,128]{1,0:T(8,128)(2,1)S(1)}, bf16[512,128]{1,0:T(8,128)(2,1)S(1)}) custom-call(s32[1]{0:T(128)} %bitcast.place_ref, bf16[512,128]{1,0:T(8,128)(2,1)S(1)} %collective-permute-done.7.refs_0_, bf16[512,128]{1,0:T(8,128)(2,1)S(1)} %collective-permute-done.8.refs_1_, ...), custom_call_target="tpu_custom_call" | custom-call | flops 201326592 | bytes 1000000 | tf_op jit(solution)/shard_map/pallas_call | solution.py:21
  28.9 1.6 %collective-permute-start.10 = (bf16[512,128]{1,0:T(8,128)(2,1)S(1)}, bf16[512,128]{1,0:T(8,128)(2,1)S(1)}, u32[]{:S(2)}, u32[]{:S(2)}) collective-permute-start(bf16[512,128]{1,0:T(8,128)(2,1)S(1)} %get-tuple-element.50), channel_id=1, source_target_pairs={{0,6},{2,4},{4,2},{6,0},{8,14},{10,12},{12,10},{14,8},{16,22},{18,... | collective-permute-start | bytes 393224 | tf_op jit(solution)/shard_map/ppermute | solution.py:397
  30.9 1.6 %collective-permute-start.12 = (bf16[512,128]{1,0:T(8,128)(2,1)S(1)}, bf16[512,128]{1,0:T(8,128)(2,1)S(1)}, u32[]{:S(2)}, u32[]{:S(2)}) collective-permute-start(bf16[512,128]{1,0:T(8,128)(2,1)S(1)} %get-tuple-element.52), channel_id=1, source_target_pairs={{0,2},{2,0},{4,6},{6,4},{8,10},{10,8},{12,14},{14,12},{16,18},{18,... | collective-permute-start | bytes 393224 | tf_op jit(solution)/shard_map/ppermute | solution.py:397
  32.5 3.9 %shard_map.114 = (bf16[8,128,128]{2,1,0:T(8,128)(2,1)S(1)}, f32[8,128,128]{2,1,0:T(8,128)S(1)}, f32[8,128,1]{2,1,0:T(8,128)S(1)}, f32[8,128,1]{2,1,0:T(8,128)S(1)}) custom-call(bf16[128,2048]{1,0:T(8,128)(2,1)S(1)} %get-tuple-element.55.rows_ref, bf16[2048,1024]{1,0:T(8,128)(2,1)} %weight_hbm.1, f32[1,128]{1,0:T(1,128)S(1)} %get-tuple-element.56.gain_ref, ...), custom_call_target="tpu_custom_call" | custom-call | flops 1073741824 | bytes 16777216 | tf_op jit(solution)/shard_map/pallas_call | solution.py:21
  37.1 2.9 %shard_map.115 = (bf16[64,2048]{1,0:T(8,128)(2,1)S(1)}, bf16[64,2048]{1,0:T(8,128)(2,1)S(1)}) custom-call(s32[1]{0:T(128)} %bitcast.place_ref, s32[1]{0:T(128)} %bitcast.1.core_ref, s32[1]{0:T(128)} %get-tuple-element.44.table_ref, bf16[512,128]{1,0:T(8,128)(2,1)S(1)} %collective-permute-done.10.refs_0_, ...), custom_call_target="tpu_custom_call" | custom-call | flops 536870912 | bytes 4000000 | tf_op jit(solution)/shard_map/pallas_call | solution.py:21
  40.1 1.5 %collective-permute-done.16 = bf16[64,2048]{1,0:T(8,128)(2,1)S(1)} collective-permute-done((bf16[64,2048]{1,0:T(8,128)(2,1)S(1)}, bf16[64,2048]{1,0:T(8,128)(2,1)S(1)}, u32[]{:S(2)}, u32[]{:S(2)}) %collective-permute-start.16) | collective-permute-done | bytes 262176 | tf_op jit(solution)/shard_map/ppermute | solution.py:521
  41.6 0.8 %add.3 = bf16[64,2048]{1,0:T(8,128)(2,1)} add(bf16[64,2048]{1,0:T(8,128)(2,1)S(1)} %get-tuple-element.65, bf16[64,2048]{1,0:T(8,128)(2,1)S(1)} %collective-permute-done.16) | non-fusion elementwise | flops 131072 | bytes 786432 | tf_op jit(solution)/shard_map/add | solution.py:521
  (22 shorter events, 1.6 us)
Async XLA Ops:
  0.0 2.5 %collective-permute-start = (bf16[64,2048]{1,0:T(8,128)(2,1)}, bf16[64,2048]{1,0:T(8,128)(2,1)S(1)}, u32[]{:S(2)}, u32[]{:S(2)}) collective-permute-start(bf16[64,2048]{1,0:T(8,128)(2,1)} %mine_hbm.1), channel_id=1, source_target_pairs={{0,1},{1,0},{2,3},{3,2},{4,5},{5,4},{6,7},{7,6},{8,9},{9,8},{10,11... | collective-permute-start | bytes 786440 | tf_op jit(solution)/shard_map/ppermute | solution.py:383
  4.9 8.2 %collective-permute-start.1 = (f32[128,128]{1,0:T(8,128)S(1)}, f32[128,128]{1,0:T(8,128)S(1)}, u32[]{:S(2)}, u32[]{:S(2)}) collective-permute-start(f32[128,128]{1,0:T(8,128)S(1)} %get-tuple-element.41.refs_3_), channel_id=1, source_target_pairs={{0,6},{2,4},{4,2},{6,0},{8,14},{10,12},{12,10},{14,8},{16,22},{18,... | collective-permute-start | bytes 196616 | tf_op jit(solution)/shard_map/ppermute | solution.py:397
  8.4 5.2 %collective-permute-start.2 = (f32[128,128]{1,0:T(8,128)S(1)}, f32[128,128]{1,0:T(8,128)S(1)}, u32[]{:S(2)}, u32[]{:S(2)}) collective-permute-start(f32[128,128]{1,0:T(8,128)S(1)} %get-tuple-element.41.refs_3_), channel_id=1, source_target_pairs={{0,4},{2,6},{4,0},{6,2},{8,12},{10,14},{12,8},{14,10},{16,20},{18,... | collective-permute-start | bytes 196616 | tf_op jit(solution)/shard_map/ppermute | solution.py:397
  8.9 4.7 %collective-permute-start.3 = (f32[128,128]{1,0:T(8,128)S(1)}, f32[128,128]{1,0:T(8,128)S(1)}, u32[]{:S(2)}, u32[]{:S(2)}) collective-permute-start(f32[128,128]{1,0:T(8,128)S(1)} %get-tuple-element.41.refs_3_), channel_id=1, source_target_pairs={{0,2},{2,0},{4,6},{6,4},{8,10},{10,8},{12,14},{14,12},{16,18},{18,... | collective-permute-start | bytes 196616 | tf_op jit(solution)/shard_map/ppermute | solution.py:397
  9.1 9.1 %collective-permute-start.4 = (bf16[128,128]{1,0:T(8,128)(2,1)S(1)}, bf16[128,128]{1,0:T(8,128)(2,1)S(1)}, u32[]{:S(2)}, u32[]{:S(2)}) collective-permute-start(bf16[128,128]{1,0:T(8,128)(2,1)S(1)} %get-tuple-element.43.refs_3_.val_ref), channel_id=1, source_target_pairs={{0,24},{2,26},{4,28},{6,30},{8,16},{10,18},{12,20},{14,22},{16,8},... | collective-permute-start | bytes 98312 | tf_op jit(solution)/shard_map/ppermute | solution.py:397
  13.1 6.6 %collective-permute-start.5 = (bf16[128,128]{1,0:T(8,128)(2,1)S(1)}, bf16[128,128]{1,0:T(8,128)(2,1)S(1)}, u32[]{:S(2)}, u32[]{:S(2)}) collective-permute-start(bf16[128,128]{1,0:T(8,128)(2,1)S(1)} %get-tuple-element.43.refs_3_.val_ref), channel_id=1, source_target_pairs={{0,16},{2,18},{4,20},{6,22},{8,24},{10,26},{12,28},{14,30},{16,0},... | collective-permute-start | bytes 98312 | tf_op jit(solution)/shard_map/ppermute | solution.py:397
  13.1 6.6 %collective-permute-start.6 = (bf16[128,128]{1,0:T(8,128)(2,1)S(1)}, bf16[128,128]{1,0:T(8,128)(2,1)S(1)}, u32[]{:S(2)}, u32[]{:S(2)}) collective-permute-start(bf16[128,128]{1,0:T(8,128)(2,1)S(1)} %get-tuple-element.43.refs_3_.val_ref), channel_id=1, source_target_pairs={{0,8},{2,10},{4,12},{6,14},{8,0},{10,2},{12,4},{14,6},{16,24},{18,... | collective-permute-start | bytes 98312 | tf_op jit(solution)/shard_map/ppermute | solution.py:397
  13.7 23.4 %copy-start = (bf16[1024,2048]{1,0:T(8,128)(2,1)S(1)}, bf16[1024,2048]{1,0:T(8,128)(2,1)}, u32[]{:S(2)}) copy-start(bf16[1024,2048]{1,0:T(8,128)(2,1)} %refs_12_.1) | copy-start | bytes 12582916
  14.2 12.4 %collective-permute-start.7 = (bf16[512,128]{1,0:T(8,128)(2,1)S(1)}, bf16[512,128]{1,0:T(8,128)(2,1)S(1)}, u32[]{:S(2)}, u32[]{:S(2)}) collective-permute-start(bf16[512,128]{1,0:T(8,128)(2,1)S(1)} %get-tuple-element.45.refs_3_), channel_id=1, source_target_pairs={{0,16},{2,18},{4,20},{6,22},{8,24},{10,26},{12,28},{14,30},{16,0},... | collective-permute-start | bytes 393224 | tf_op jit(solution)/shard_map/ppermute | solution.py:397
  16.6 11.6 %collective-permute-start.8 = (bf16[512,128]{1,0:T(8,128)(2,1)S(1)}, bf16[512,128]{1,0:T(8,128)(2,1)S(1)}, u32[]{:S(2)}, u32[]{:S(2)}) collective-permute-start(bf16[512,128]{1,0:T(8,128)(2,1)S(1)} %get-tuple-element.45.refs_3_), channel_id=1, source_target_pairs={{0,24},{2,26},{4,28},{6,30},{8,16},{10,18},{12,20},{14,22},{16,8},... | collective-permute-start | bytes 393224 | tf_op jit(solution)/shard_map/ppermute | solution.py:397
  18.1 10.0 %collective-permute-start.9 = (bf16[512,128]{1,0:T(8,128)(2,1)S(1)}, bf16[512,128]{1,0:T(8,128)(2,1)S(1)}, u32[]{:S(2)}, u32[]{:S(2)}) collective-permute-start(bf16[512,128]{1,0:T(8,128)(2,1)S(1)} %get-tuple-element.45.refs_3_), channel_id=1, source_target_pairs={{0,8},{2,10},{4,12},{6,14},{8,0},{10,2},{12,4},{14,6},{16,24},{18,... | collective-permute-start | bytes 393224 | tf_op jit(solution)/shard_map/ppermute | solution.py:397
  19.7 0.7 %copy-start.1 = (s32[1,16]{1,0:T(1,128)S(1)}, s32[1,16]{1,0:T(1,128)}, u32[]{:S(2)}) copy-start(s32[1,16]{1,0:T(1,128)} %param.21) | copy-start | bytes 196
  21.7 9.2 %collective-permute-start.13 = (bf16[512,128]{1,0:T(8,128)(2,1)S(1)}, bf16[512,128]{1,0:T(8,128)(2,1)S(1)}, u32[]{:S(2)}, u32[]{:S(2)}) collective-permute-start(bf16[512,128]{1,0:T(8,128)(2,1)S(1)} %get-tuple-element.54.refs_7_), channel_id=1, source_target_pairs={{0,6},{2,4},{4,2},{6,0},{8,14},{10,12},{12,10},{14,8},{16,22},{18,... | collective-permute-start | bytes 393224 | tf_op jit(solution)/shard_map/ppermute | solution.py:397
  24.2 12.2 %collective-permute-start.14 = (bf16[512,128]{1,0:T(8,128)(2,1)S(1)}, bf16[512,128]{1,0:T(8,128)(2,1)S(1)}, u32[]{:S(2)}, u32[]{:S(2)}) collective-permute-start(bf16[512,128]{1,0:T(8,128)(2,1)S(1)} %get-tuple-element.54.refs_7_), channel_id=1, source_target_pairs={{0,4},{2,6},{4,0},{6,2},{8,12},{10,14},{12,8},{14,10},{16,20},{18,... | collective-permute-start | bytes 393224 | tf_op jit(solution)/shard_map/ppermute | solution.py:397
  26.6 9.8 %collective-permute-start.15 = (bf16[512,128]{1,0:T(8,128)(2,1)S(1)}, bf16[512,128]{1,0:T(8,128)(2,1)S(1)}, u32[]{:S(2)}, u32[]{:S(2)}) collective-permute-start(bf16[512,128]{1,0:T(8,128)(2,1)S(1)} %get-tuple-element.54.refs_7_), channel_id=1, source_target_pairs={{0,2},{2,0},{4,6},{6,4},{8,10},{10,8},{12,14},{14,12},{16,18},{18,... | collective-permute-start | bytes 393224 | tf_op jit(solution)/shard_map/ppermute | solution.py:397
  28.9 7.5 %collective-permute-start.10 = (bf16[512,128]{1,0:T(8,128)(2,1)S(1)}, bf16[512,128]{1,0:T(8,128)(2,1)S(1)}, u32[]{:S(2)}, u32[]{:S(2)}) collective-permute-start(bf16[512,128]{1,0:T(8,128)(2,1)S(1)} %get-tuple-element.50), channel_id=1, source_target_pairs={{0,6},{2,4},{4,2},{6,0},{8,14},{10,12},{12,10},{14,8},{16,22},{18,... | collective-permute-start | bytes 393224 | tf_op jit(solution)/shard_map/ppermute | solution.py:397
  30.5 6.4 %collective-permute-start.11 = (bf16[512,128]{1,0:T(8,128)(2,1)S(1)}, bf16[512,128]{1,0:T(8,128)(2,1)S(1)}, u32[]{:S(2)}, u32[]{:S(2)}) collective-permute-start(bf16[512,128]{1,0:T(8,128)(2,1)S(1)} %get-tuple-element.51), channel_id=1, source_target_pairs={{0,4},{2,6},{4,0},{6,2},{8,12},{10,14},{12,8},{14,10},{16,20},{18,... | collective-permute-start | bytes 393224 | tf_op jit(solution)/shard_map/ppermute | solution.py:397
  30.9 6.2 %collective-permute-start.12 = (bf16[512,128]{1,0:T(8,128)(2,1)S(1)}, bf16[512,128]{1,0:T(8,128)(2,1)S(1)}, u32[]{:S(2)}, u32[]{:S(2)}) collective-permute-start(bf16[512,128]{1,0:T(8,128)(2,1)S(1)} %get-tuple-element.52), channel_id=1, source_target_pairs={{0,2},{2,0},{4,6},{6,4},{8,10},{10,8},{12,14},{14,12},{16,18},{18,... | collective-permute-start | bytes 393224 | tf_op jit(solution)/shard_map/ppermute | solution.py:397
  40.0 1.6 %collective-permute-start.16 = (bf16[64,2048]{1,0:T(8,128)(2,1)S(1)}, bf16[64,2048]{1,0:T(8,128)(2,1)S(1)}, u32[]{:S(2)}, u32[]{:S(2)}) collective-permute-start(bf16[64,2048]{1,0:T(8,128)(2,1)S(1)} %get-tuple-element.66), channel_id=1, source_target_pairs={{0,1},{1,0},{2,3},{3,2},{4,5},{5,4},{6,7},{7,6},{8,9},{9,8},{10,11... | collective-permute-start | bytes 786440 | tf_op jit(solution)/shard_map/ppermute | solution.py:521

commit v19 on v18

--- a/solution.py
+++ b/solution.py
@@ -41,7 +41,7 @@
     return pltpu.with_memory_space_constraint(array, pltpu.HBM)
 
 
-def line_order(groups):
+def swap_order(groups):
     return [groups // 2] + [step for step in range(groups - 1, 0, -1) if step != groups // 2] + [0]
 
 
@@ -149,8 +149,8 @@
     near_refs, (turns_ref, seen_ref) = refs[group + 2 : -2], refs[-2:]
     member = place_ref[0] % group
     tokens, size = exit_ref.shape
-    for step in range(group):
-        turns_ref[source_of(member, step, group)] = turn_refs[group - 1 - step][...]
+    for ref, step in zip(turn_refs, swap_order(group)):
+        turns_ref[source_of(member, step, group)] = ref[...]
     own = exit_ref[...]
     keys = own
     product = None
@@ -264,7 +264,7 @@
     far_refs, (keys_ref, whole_ref) = refs[-group - 2 : -2], refs[-2:]
     mine, member = place_ref[0] // group, place_ref[0] % group
     size = starts_ref.shape[1]
-    for ref, step in zip(arrived, line_order(groups)):
+    for ref, step in zip(arrived, swap_order(groups)):
         index = source_of(mine, step, groups)
         keys_ref[index] = ref[:tokens].astype(F32) + ref[tokens : 2 * tokens].astype(F32)
         whole = ref[2 * tokens : 2 * tokens + size].astype(F32)
@@ -287,7 +287,9 @@
 
 
 def attend_kernel(group, segments, most, place_ref, core_ref, table_ref, *refs):
-    far_refs, line_refs = refs[:group][::-1], refs[group : 2 * group][::-1]
+    order = swap_order(group)
+    far_refs = [refs[order.index(step)] for step in range(group)]
+    line_refs = refs[group : 2 * group][::-1]
     (moved_ref, weighted_ref, peak_ref, total_ref, out_ref, away_ref, kept_ref, keys_ref, vals_ref,
      summed_ref) = refs[2 * group :]
     core = core_ref[0]
@@ -445,7 +447,7 @@
             shaped((group, size, size), F32),
         ]
         + [shaped((tokens, size), BF16)] * group,
-        (place, exit_keys, *turns[::-1]),
+        (place, exit_keys, *(turns[step] for step in swap_order(group))),
         in_specs=[smem] + [vmem] * (1 + group),
         scratch=(
             pltpu.VMEM((group, size, size), F32),
@@ -491,7 +493,7 @@
     far = call(
         functools.partial(arrive_kernel, groups, group, tokens),
         [shaped((groups * tokens, size), BF16)] * group,
-        (place, *(arrived[step] for step in line_order(groups)), starts, *near),
+        (place, *(arrived[step] for step in swap_order(groups)), starts, *near),
         in_specs=[smem] + [vmem] * (groups + 1 + group),
         scratch=(
             pltpu.VMEM((groups, tokens, size), F32),
@@ -507,7 +509,10 @@
     away, kept = call(
         functools.partial(attend_kernel, group, segments, most),
         [shaped((half, width_out), BF16)] * 2,
-        (place, core, table, *far[::-1], *values[::-1], *own, w_out),
+        (
+            place, core, table, *(far[step] for step in swap_order(group)), *values[::-1], *own,
+            w_out,
+        ),
         in_specs=[smem] * 3 + [vmem] * (2 * group + 5),
         scratch=[
             pltpu.VMEM((chunk * tokens, size), BF16),

time: 42.5 us -> 42.6 us (level)
  no operation moved by 1% of the time
where the time goes in v19:
time: 42.6 us; the launch traced here: 42.5 us
  starting transfers between devices  21.8 us (51%)
  Pallas kernels  13.2 us (31%)
  waiting for transfers between devices  5.34 us (13%)
  other arithmetic  0.77 us (2%)
  between operations  0.76 us (2%)
  local copies, waits for them, and re-layouts  0.66 us (2%)
    ppermute x15, starting transfers between devices, swapped(): out[step] = lax.ppermute(values[step], 'ctx', pairs_of(step))  21.2 us
    pallas_call x7, Pallas kernels, call(): pl.pallas_call(kernel, out_shape=out_shape, in_specs=in_specs or [vmem] *...  13.2 us
    ppermute x15, waiting for transfers between devices, swapped(): out[step] = lax.ppermute(values[step], 'ctx', pairs_of(step))  3.82 us
    ppermute x1, waiting for transfers between devices, body(): return kept + lax.ppermute(away, 'head', [(0, 1), (1, 0)])  1.52 us
  transfers between devices with their start and end apart: 17, of which 5 were waited for; matrix products, arithmetic and copies ran while one was open for 0% of the time, Pallas kernels for 19%

profile of v19, /device:TPU:0, one launch (start us, length us, event | category | flops | bytes accessed | tf_op | source)
XLA Modules:
  0.0 42.5 jit_solution(7891120406076002830)
XLA Ops:
  1.1 1.4 %shard_map.109 = (bf16[2048,256]{1,0:T(8,128)(2,1)S(1)}, bf16[1,2048]{1,0:T(2,128)(2,1)S(1)}, f32[1,128]{1,0:T(1,128)S(1)}, f32[1,128]{1,0:T(1,128)S(1)}, bf16[64,2048]{1,0:T(8,128)(2,1)S(1)}) custom-call(bf16[2048,128]{1,0:T(8,128)(2,1)} %key_hbm.1, bf16[2048,128]{1,0:T(8,128)(2,1)} %dir_hbm.1, bf16[1,2048]{1,0:T(2,128)(2,1)} %rate_hbm.1, ...), custom_call_target="tpu_custom_call" | custom-call | bytes 3145728 | tf_op jit(solution)/shard_map/pallas_call | solution.py:21
  2.5 2.4 %shard_map.110 = (bf16[128,2048]{1,0:T(8,128)(2,1)S(1)}, f32[128,128]{1,0:T(8,128)S(1)}, bf16[128,128]{1,0:T(8,128)(2,1)S(1)}, f32[128,128]{1,0:T(8,128)S(1)}, f...) custom-call(s32[1]{0:T(128)} %bitcast.1.core_ref, ...), custom_call_target="tpu_custom_call" | custom-call | flops 201326592 | bytes 2097152 | tf_op jit(solution)/shard_map/pallas_call | solution.py:21
  4.9 2.6 %collective-permute-start.1 = (f32[128,128]{1,0:T(8,128)S(1)}, f32[128,128]{1,0:T(8,128)S(1)}, u32[]{:S(2)}, u32[]{:S(2)}) collective-permute-start(f32[128,128]{1,0:T(8,128)S(1)} %get-tuple-element.41.refs_3_), channel_id=1, source_target_pairs={{0,4},{2,6},{4,0},{6,2},{8,12},{10,14},{12,8},{14,10},{16,20},{18,... | collective-permute-start | bytes 196616 | tf_op jit(solution)/shard_map/ppermute | solution.py:399
  7.5 1.4 %collective-permute-start.2 = (f32[128,128]{1,0:T(8,128)S(1)}, f32[128,128]{1,0:T(8,128)S(1)}, u32[]{:S(2)}, u32[]{:S(2)}) collective-permute-start(f32[128,128]{1,0:T(8,128)S(1)} %get-tuple-element.41.refs_3_), channel_id=1, source_target_pairs={{0,6},{2,4},{4,2},{6,0},{8,14},{10,12},{12,10},{14,8},{16,22},{18,... | collective-permute-start | bytes 196616 | tf_op jit(solution)/shard_map/ppermute | solution.py:399
  9.1 4.0 %collective-permute-start.4 = (bf16[128,128]{1,0:T(8,128)(2,1)S(1)}, bf16[128,128]{1,0:T(8,128)(2,1)S(1)}, u32[]{:S(2)}, u32[]{:S(2)}) collective-permute-start(bf16[128,128]{1,0:T(8,128)(2,1)S(1)} %get-tuple-element.43.refs_3_.val_ref), channel_id=1, source_target_pairs={{0,24},{2,26},{4,28},{6,30},{8,16},{10,18},{12,20},{14,22},{16,8},... | collective-permute-start | bytes 98312 | tf_op jit(solution)/shard_map/ppermute | solution.py:399
  13.1 0.6 %collective-permute-start.6 = (bf16[128,128]{1,0:T(8,128)(2,1)S(1)}, bf16[128,128]{1,0:T(8,128)(2,1)S(1)}, u32[]{:S(2)}, u32[]{:S(2)}) collective-permute-start(bf16[128,128]{1,0:T(8,128)(2,1)S(1)} %get-tuple-element.43.refs_3_.val_ref), channel_id=1, source_target_pairs={{0,8},{2,10},{4,12},{6,14},{8,0},{10,2},{12,4},{14,6},{16,24},{18,... | collective-permute-start | bytes 98312 | tf_op jit(solution)/shard_map/ppermute | solution.py:399
  13.7 0.5 %shard_map.111 = (bf16[512,128]{1,0:T(8,128)(2,1)S(1)}, f32[4,128,128]{2,1,0:T(8,128)S(1)}, bf16[128,128]{1,0:T(8,128)(2,1)S(1)}, bf16[128,128]{1,0:T(8,128)(2,1...) custom-call(s32[1]{0:T(128)} %bitcast.place_ref, f32[128,128]{1,0:T(8,128)S(1)} %get-tuple-element.40.exit_ref, ...), custom_call_target="tpu_custom_call" | custom-call | flops 100663296 | bytes 1000000 | tf_op jit(solution)/shard_map/pallas_call | solution.py:21
  14.2 2.4 %collective-permute-start.7 = (bf16[512,128]{1,0:T(8,128)(2,1)S(1)}, bf16[512,128]{1,0:T(8,128)(2,1)S(1)}, u32[]{:S(2)}, u32[]{:S(2)}) collective-permute-start(bf16[512,128]{1,0:T(8,128)(2,1)S(1)} %get-tuple-element.45.refs_3_), channel_id=1, source_target_pairs={{0,16},{2,18},{4,20},{6,22},{8,24},{10,26},{12,28},{14,30},{16,0},... | collective-permute-start | bytes 393224 | tf_op jit(solution)/shard_map/ppermute | solution.py:399
  16.6 1.5 %collective-permute-start.8 = (bf16[512,128]{1,0:T(8,128)(2,1)S(1)}, bf16[512,128]{1,0:T(8,128)(2,1)S(1)}, u32[]{:S(2)}, u32[]{:S(2)}) collective-permute-start(bf16[512,128]{1,0:T(8,128)(2,1)S(1)} %get-tuple-element.45.refs_3_), channel_id=1, source_target_pairs={{0,24},{2,26},{4,28},{6,30},{8,16},{10,18},{12,20},{14,22},{16,8},... | collective-permute-start | bytes 393224 | tf_op jit(solution)/shard_map/ppermute | solution.py:399
  18.1 0.5 %collective-permute-start.9 = (bf16[512,128]{1,0:T(8,128)(2,1)S(1)}, bf16[512,128]{1,0:T(8,128)(2,1)S(1)}, u32[]{:S(2)}, u32[]{:S(2)}) collective-permute-start(bf16[512,128]{1,0:T(8,128)(2,1)S(1)} %get-tuple-element.45.refs_3_), channel_id=1, source_target_pairs={{0,8},{2,10},{4,12},{6,14},{8,0},{10,2},{12,4},{14,6},{16,24},{18,... | collective-permute-start | bytes 393224 | tf_op jit(solution)/shard_map/ppermute | solution.py:399
  18.6 1.1 %collective-permute-done.5.refs_1_ = bf16[128,128]{1,0:T(8,128)(2,1)S(1)} collective-permute-done((bf16[128,128]{1,0:T(8,128)(2,1)S(1)}, bf16[128,128]{1,0:T(8,128)(2,1)S(1)}, u32[]{:S(2)}, u32[]{:S(2)}) %collective-permute-start.5) | collective-permute-done | bytes 32800 | tf_op jit(solution)/shard_map/ppermute | solution.py:399
  19.7 0.7 %copy-done.1 = s32[1,16]{1,0:T(1,128)S(1)} copy-done((s32[1,16]{1,0:T(1,128)S(1)}, s32[1,16]{1,0:T(1,128)}, u32[]{:S(2)}) %copy-start.1) | copy-done | bytes 88
  20.4 1.3 %shard_map.112 = (bf16[512,128]{1,0:T(8,128)(2,1)S(1)}, s32[1]{0:T(128)}) custom-call(s32[1]{0:T(128)} %bitcast.place_ref, s32[16]{0:T(128)S(1)} %bitcast.5, f32[4,128,128]{2,1,0:T(8,128)S(1)} %get-tuple-element.42.after_ref.refs_4_, bf16[128,128]{1,0:T(8,128)(2,1)S(1)} %collective-permute-done.4.refs_0_, ...), custom_call_target="tpu_custom_call" | custom-call | bytes 1000000 | tf_op jit(solution)/shard_map/pallas_call | solution.py:21
  21.7 2.5 %collective-permute-start.13 = (bf16[512,128]{1,0:T(8,128)(2,1)S(1)}, bf16[512,128]{1,0:T(8,128)(2,1)S(1)}, u32[]{:S(2)}, u32[]{:S(2)}) collective-permute-start(bf16[512,128]{1,0:T(8,128)(2,1)S(1)} %get-tuple-element.54.refs_7_), channel_id=1, source_target_pairs={{0,6},{2,4},{4,2},{6,0},{8,14},{10,12},{12,10},{14,8},{16,22},{18,... | collective-permute-start | bytes 393224 | tf_op jit(solution)/shard_map/ppermute | solution.py:399
  24.2 0.5 %collective-permute-start.14 = (bf16[512,128]{1,0:T(8,128)(2,1)S(1)}, bf16[512,128]{1,0:T(8,128)(2,1)S(1)}, u32[]{:S(2)}, u32[]{:S(2)}) collective-permute-start(bf16[512,128]{1,0:T(8,128)(2,1)S(1)} %get-tuple-element.54.refs_7_), channel_id=1, source_target_pairs={{0,4},{2,6},{4,0},{6,2},{8,12},{10,14},{12,8},{14,10},{16,20},{18,... | collective-permute-start | bytes 393224 | tf_op jit(solution)/shard_map/ppermute | solution.py:399
  24.7 1.9 %collective-permute-done.7.refs_0_ = bf16[512,128]{1,0:T(8,128)(2,1)S(1)} collective-permute-done((bf16[512,128]{1,0:T(8,128)(2,1)S(1)}, bf16[512,128]{1,0:T(8,128)(2,1)S(1)}, u32[]{:S(2)}, u32[]{:S(2)}) %collective-permute-start.7) | collective-permute-done | bytes 131104 | tf_op jit(solution)/shard_map/ppermute | solution.py:399
  26.6 1.5 %collective-permute-start.15 = (bf16[512,128]{1,0:T(8,128)(2,1)S(1)}, bf16[512,128]{1,0:T(8,128)(2,1)S(1)}, u32[]{:S(2)}, u32[]{:S(2)}) collective-permute-start(bf16[512,128]{1,0:T(8,128)(2,1)S(1)} %get-tuple-element.54.refs_7_), channel_id=1, source_target_pairs={{0,2},{2,0},{4,6},{6,4},{8,10},{10,8},{12,14},{14,12},{16,18},{18,... | collective-permute-start | bytes 393224 | tf_op jit(solution)/shard_map/ppermute | solution.py:399
  28.1 0.7 %shard_map.113 = (bf16[512,128]{1,0:T(8,128)(2,1)S(1)}, bf16[512,128]{1,0:T(8,128)(2,1)S(1)}, bf16[512,128]{1,0:T(8,128)(2,1)S(1)}, bf16[512,128]{1,0:T(8,128)(2,1)S(1)}) custom-call(s32[1]{0:T(128)} %bitcast.place_ref, bf16[512,128]{1,0:T(8,128)(2,1)S(1)} %collective-permute-done.7.refs_0_, bf16[512,128]{1,0:T(8,128)(2,1)S(1)} %collective-permute-done.8.refs_1_, ...), custom_call_target="tpu_custom_call" | custom-call | flops 201326592 | bytes 1000000 | tf_op jit(solution)/shard_map/pallas_call | solution.py:21
  28.9 1.6 %collective-permute-start.10 = (bf16[512,128]{1,0:T(8,128)(2,1)S(1)}, bf16[512,128]{1,0:T(8,128)(2,1)S(1)}, u32[]{:S(2)}, u32[]{:S(2)}) collective-permute-start(bf16[512,128]{1,0:T(8,128)(2,1)S(1)} %get-tuple-element.50), channel_id=1, source_target_pairs={{0,4},{2,6},{4,0},{6,2},{8,12},{10,14},{12,8},{14,10},{16,20},{18,... | collective-permute-start | bytes 393224 | tf_op jit(solution)/shard_map/ppermute | solution.py:399
  30.9 1.5 %collective-permute-start.12 = (bf16[512,128]{1,0:T(8,128)(2,1)S(1)}, bf16[512,128]{1,0:T(8,128)(2,1)S(1)}, u32[]{:S(2)}, u32[]{:S(2)}) collective-permute-start(bf16[512,128]{1,0:T(8,128)(2,1)S(1)} %get-tuple-element.52), channel_id=1, source_target_pairs={{0,2},{2,0},{4,6},{6,4},{8,10},{10,8},{12,14},{14,12},{16,18},{18,... | collective-permute-start | bytes 393224 | tf_op jit(solution)/shard_map/ppermute | solution.py:399
  32.4 3.9 %shard_map.114 = (bf16[8,128,128]{2,1,0:T(8,128)(2,1)S(1)}, f32[8,128,128]{2,1,0:T(8,128)S(1)}, f32[8,128,1]{2,1,0:T(8,128)S(1)}, f32[8,128,1]{2,1,0:T(8,128)S(1)}) custom-call(bf16[128,2048]{1,0:T(8,128)(2,1)S(1)} %get-tuple-element.55.rows_ref, bf16[2048,1024]{1,0:T(8,128)(2,1)} %weight_hbm.1, f32[1,128]{1,0:T(1,128)S(1)} %get-tuple-element.56.gain_ref, ...), custom_call_target="tpu_custom_call" | custom-call | flops 1073741824 | bytes 16777216 | tf_op jit(solution)/shard_map/pallas_call | solution.py:21
  37.2 2.9 %shard_map.115 = (bf16[64,2048]{1,0:T(8,128)(2,1)S(1)}, bf16[64,2048]{1,0:T(8,128)(2,1)S(1)}) custom-call(s32[1]{0:T(128)} %bitcast.place_ref, s32[1]{0:T(128)} %bitcast.1.core_ref, s32[1]{0:T(128)} %get-tuple-element.44.table_ref, bf16[512,128]{1,0:T(8,128)(2,1)S(1)} %collective-permute-done.10.refs_0_, ...), custom_call_target="tpu_custom_call" | custom-call | flops 536870912 | bytes 4000000 | tf_op jit(solution)/shard_map/pallas_call | solution.py:21
  40.2 1.5 %collective-permute-done.16 = bf16[64,2048]{1,0:T(8,128)(2,1)S(1)} collective-permute-done((bf16[64,2048]{1,0:T(8,128)(2,1)S(1)}, bf16[64,2048]{1,0:T(8,128)(2,1)S(1)}, u32[]{:S(2)}, u32[]{:S(2)}) %collective-permute-start.16) | collective-permute-done | bytes 262176 | tf_op jit(solution)/shard_map/ppermute | solution.py:526
  41.7 0.8 %add.3 = bf16[64,2048]{1,0:T(8,128)(2,1)} add(bf16[64,2048]{1,0:T(8,128)(2,1)S(1)} %get-tuple-element.65, bf16[64,2048]{1,0:T(8,128)(2,1)S(1)} %collective-permute-done.16) | non-fusion elementwise | flops 131072 | bytes 786432 | tf_op jit(solution)/shard_map/add | solution.py:526
  (22 shorter events, 2.0 us)
Async XLA Ops:
  0.0 2.5 %collective-permute-start = (bf16[64,2048]{1,0:T(8,128)(2,1)}, bf16[64,2048]{1,0:T(8,128)(2,1)S(1)}, u32[]{:S(2)}, u32[]{:S(2)}) collective-permute-start(bf16[64,2048]{1,0:T(8,128)(2,1)} %mine_hbm.1), channel_id=1, source_target_pairs={{0,1},{1,0},{2,3},{3,2},{4,5},{5,4},{6,7},{7,6},{8,9},{9,8},{10,11... | collective-permute-start | bytes 786440 | tf_op jit(solution)/shard_map/ppermute | solution.py:385
  4.9 8.2 %collective-permute-start.1 = (f32[128,128]{1,0:T(8,128)S(1)}, f32[128,128]{1,0:T(8,128)S(1)}, u32[]{:S(2)}, u32[]{:S(2)}) collective-permute-start(f32[128,128]{1,0:T(8,128)S(1)} %get-tuple-element.41.refs_3_), channel_id=1, source_target_pairs={{0,4},{2,6},{4,0},{6,2},{8,12},{10,14},{12,8},{14,10},{16,20},{18,... | collective-permute-start | bytes 196616 | tf_op jit(solution)/shard_map/ppermute | solution.py:399
  7.5 6.1 %collective-permute-start.2 = (f32[128,128]{1,0:T(8,128)S(1)}, f32[128,128]{1,0:T(8,128)S(1)}, u32[]{:S(2)}, u32[]{:S(2)}) collective-permute-start(f32[128,128]{1,0:T(8,128)S(1)} %get-tuple-element.41.refs_3_), channel_id=1, source_target_pairs={{0,6},{2,4},{4,2},{6,0},{8,14},{10,12},{12,10},{14,8},{16,22},{18,... | collective-permute-start | bytes 196616 | tf_op jit(solution)/shard_map/ppermute | solution.py:399
  8.9 4.7 %collective-permute-start.3 = (f32[128,128]{1,0:T(8,128)S(1)}, f32[128,128]{1,0:T(8,128)S(1)}, u32[]{:S(2)}, u32[]{:S(2)}) collective-permute-start(f32[128,128]{1,0:T(8,128)S(1)} %get-tuple-element.41.refs_3_), channel_id=1, source_target_pairs={{0,2},{2,0},{4,6},{6,4},{8,10},{10,8},{12,14},{14,12},{16,18},{18,... | collective-permute-start | bytes 196616 | tf_op jit(solution)/shard_map/ppermute | solution.py:399
  9.1 9.1 %collective-permute-start.4 = (bf16[128,128]{1,0:T(8,128)(2,1)S(1)}, bf16[128,128]{1,0:T(8,128)(2,1)S(1)}, u32[]{:S(2)}, u32[]{:S(2)}) collective-permute-start(bf16[128,128]{1,0:T(8,128)(2,1)S(1)} %get-tuple-element.43.refs_3_.val_ref), channel_id=1, source_target_pairs={{0,24},{2,26},{4,28},{6,30},{8,16},{10,18},{12,20},{14,22},{16,8},... | collective-permute-start | bytes 98312 | tf_op jit(solution)/shard_map/ppermute | solution.py:399
  13.1 6.6 %collective-permute-start.5 = (bf16[128,128]{1,0:T(8,128)(2,1)S(1)}, bf16[128,128]{1,0:T(8,128)(2,1)S(1)}, u32[]{:S(2)}, u32[]{:S(2)}) collective-permute-start(bf16[128,128]{1,0:T(8,128)(2,1)S(1)} %get-tuple-element.43.refs_3_.val_ref), channel_id=1, source_target_pairs={{0,16},{2,18},{4,20},{6,22},{8,24},{10,26},{12,28},{14,30},{16,0},... | collective-permute-start | bytes 98312 | tf_op jit(solution)/shard_map/ppermute | solution.py:399
  13.1 6.6 %collective-permute-start.6 = (bf16[128,128]{1,0:T(8,128)(2,1)S(1)}, bf16[128,128]{1,0:T(8,128)(2,1)S(1)}, u32[]{:S(2)}, u32[]{:S(2)}) collective-permute-start(bf16[128,128]{1,0:T(8,128)(2,1)S(1)} %get-tuple-element.43.refs_3_.val_ref), channel_id=1, source_target_pairs={{0,8},{2,10},{4,12},{6,14},{8,0},{10,2},{12,4},{14,6},{16,24},{18,... | collective-permute-start | bytes 98312 | tf_op jit(solution)/shard_map/ppermute | solution.py:399
  13.7 23.6 %copy-start = (bf16[1024,2048]{1,0:T(8,128)(2,1)S(1)}, bf16[1024,2048]{1,0:T(8,128)(2,1)}, u32[]{:S(2)}) copy-start(bf16[1024,2048]{1,0:T(8,128)(2,1)} %refs_12_.1) | copy-start | bytes 12582916
  14.2 12.5 %collective-permute-start.7 = (bf16[512,128]{1,0:T(8,128)(2,1)S(1)}, bf16[512,128]{1,0:T(8,128)(2,1)S(1)}, u32[]{:S(2)}, u32[]{:S(2)}) collective-permute-start(bf16[512,128]{1,0:T(8,128)(2,1)S(1)} %get-tuple-element.45.refs_3_), channel_id=1, source_target_pairs={{0,16},{2,18},{4,20},{6,22},{8,24},{10,26},{12,28},{14,30},{16,0},... | collective-permute-start | bytes 393224 | tf_op jit(solution)/shard_map/ppermute | solution.py:399
  16.6 11.5 %collective-permute-start.8 = (bf16[512,128]{1,0:T(8,128)(2,1)S(1)}, bf16[512,128]{1,0:T(8,128)(2,1)S(1)}, u32[]{:S(2)}, u32[]{:S(2)}) collective-permute-start(bf16[512,128]{1,0:T(8,128)(2,1)S(1)} %get-tuple-element.45.refs_3_), channel_id=1, source_target_pairs={{0,24},{2,26},{4,28},{6,30},{8,16},{10,18},{12,20},{14,22},{16,8},... | collective-permute-start | bytes 393224 | tf_op jit(solution)/shard_map/ppermute | solution.py:399
  18.1 10.0 %collective-permute-start.9 = (bf16[512,128]{1,0:T(8,128)(2,1)S(1)}, bf16[512,128]{1,0:T(8,128)(2,1)S(1)}, u32[]{:S(2)}, u32[]{:S(2)}) collective-permute-start(bf16[512,128]{1,0:T(8,128)(2,1)S(1)} %get-tuple-element.45.refs_3_), channel_id=1, source_target_pairs={{0,8},{2,10},{4,12},{6,14},{8,0},{10,2},{12,4},{14,6},{16,24},{18,... | collective-permute-start | bytes 393224 | tf_op jit(solution)/shard_map/ppermute | solution.py:399
  19.7 0.7 %copy-start.1 = (s32[1,16]{1,0:T(1,128)S(1)}, s32[1,16]{1,0:T(1,128)}, u32[]{:S(2)}) copy-start(s32[1,16]{1,0:T(1,128)} %param.21) | copy-start | bytes 196
  21.7 9.2 %collective-permute-start.13 = (bf16[512,128]{1,0:T(8,128)(2,1)S(1)}, bf16[512,128]{1,0:T(8,128)(2,1)S(1)}, u32[]{:S(2)}, u32[]{:S(2)}) collective-permute-start(bf16[512,128]{1,0:T(8,128)(2,1)S(1)} %get-tuple-element.54.refs_7_), channel_id=1, source_target_pairs={{0,6},{2,4},{4,2},{6,0},{8,14},{10,12},{12,10},{14,8},{16,22},{18,... | collective-permute-start | bytes 393224 | tf_op jit(solution)/shard_map/ppermute | solution.py:399
  24.2 12.1 %collective-permute-start.14 = (bf16[512,128]{1,0:T(8,128)(2,1)S(1)}, bf16[512,128]{1,0:T(8,128)(2,1)S(1)}, u32[]{:S(2)}, u32[]{:S(2)}) collective-permute-start(bf16[512,128]{1,0:T(8,128)(2,1)S(1)} %get-tuple-element.54.refs_7_), channel_id=1, source_target_pairs={{0,4},{2,6},{4,0},{6,2},{8,12},{10,14},{12,8},{14,10},{16,20},{18,... | collective-permute-start | bytes 393224 | tf_op jit(solution)/shard_map/ppermute | solution.py:399
  26.6 9.7 %collective-permute-start.15 = (bf16[512,128]{1,0:T(8,128)(2,1)S(1)}, bf16[512,128]{1,0:T(8,128)(2,1)S(1)}, u32[]{:S(2)}, u32[]{:S(2)}) collective-permute-start(bf16[512,128]{1,0:T(8,128)(2,1)S(1)} %get-tuple-element.54.refs_7_), channel_id=1, source_target_pairs={{0,2},{2,0},{4,6},{6,4},{8,10},{10,8},{12,14},{14,12},{16,18},{18,... | collective-permute-start | bytes 393224 | tf_op jit(solution)/shard_map/ppermute | solution.py:399
  28.9 7.5 %collective-permute-start.10 = (bf16[512,128]{1,0:T(8,128)(2,1)S(1)}, bf16[512,128]{1,0:T(8,128)(2,1)S(1)}, u32[]{:S(2)}, u32[]{:S(2)}) collective-permute-start(bf16[512,128]{1,0:T(8,128)(2,1)S(1)} %get-tuple-element.50), channel_id=1, source_target_pairs={{0,4},{2,6},{4,0},{6,2},{8,12},{10,14},{12,8},{14,10},{16,20},{18,... | collective-permute-start | bytes 393224 | tf_op jit(solution)/shard_map/ppermute | solution.py:399
  30.4 6.3 %collective-permute-start.11 = (bf16[512,128]{1,0:T(8,128)(2,1)S(1)}, bf16[512,128]{1,0:T(8,128)(2,1)S(1)}, u32[]{:S(2)}, u32[]{:S(2)}) collective-permute-start(bf16[512,128]{1,0:T(8,128)(2,1)S(1)} %get-tuple-element.51), channel_id=1, source_target_pairs={{0,6},{2,4},{4,2},{6,0},{8,14},{10,12},{12,10},{14,8},{16,22},{18,... | collective-permute-start | bytes 393224 | tf_op jit(solution)/shard_map/ppermute | solution.py:399
  30.9 6.3 %collective-permute-start.12 = (bf16[512,128]{1,0:T(8,128)(2,1)S(1)}, bf16[512,128]{1,0:T(8,128)(2,1)S(1)}, u32[]{:S(2)}, u32[]{:S(2)}) collective-permute-start(bf16[512,128]{1,0:T(8,128)(2,1)S(1)} %get-tuple-element.52), channel_id=1, source_target_pairs={{0,2},{2,0},{4,6},{6,4},{8,10},{10,8},{12,14},{14,12},{16,18},{18,... | collective-permute-start | bytes 393224 | tf_op jit(solution)/shard_map/ppermute | solution.py:399
  40.1 1.6 %collective-permute-start.16 = (bf16[64,2048]{1,0:T(8,128)(2,1)S(1)}, bf16[64,2048]{1,0:T(8,128)(2,1)S(1)}, u32[]{:S(2)}, u32[]{:S(2)}) collective-permute-start(bf16[64,2048]{1,0:T(8,128)(2,1)S(1)} %get-tuple-element.66), channel_id=1, source_target_pairs={{0,1},{1,0},{2,3},{3,2},{4,5},{5,4},{6,7},{7,6},{8,9},{9,8},{10,11... | collective-permute-start | bytes 786440 | tf_op jit(solution)/shard_map/ppermute | solution.py:526

commit v20 on v18

--- a/solution.py
+++ b/solution.py
@@ -404,7 +404,8 @@
 
     def along_line(values):
         return swapped(values, groups, lambda step: [
-            (s, s % group + group * target_of(s // group, step, groups)) for s in range(segments)
+            (s, s % group + group * target_of(s // group, step, groups))
+            for s in reversed(range(segments))
         ])
 
     weights, rate_row, key_gain, query_gain, mine = call(

time: 42.5 us -> 42.5 us (level)
  no operation moved by 1% of the time
where the time goes in v20:
time: 42.5 us; the launch traced here: 42.3 us
  starting transfers between devices  21.6 us (51%)
  Pallas kernels  13.2 us (31%)
  waiting for transfers between devices  5.34 us (13%)
  other arithmetic  0.77 us (2%)
  between operations  0.76 us (2%)
  local copies, waits for them, and re-layouts  0.66 us (2%)
    ppermute x15, starting transfers between devices, swapped(): out[step] = lax.ppermute(values[step], 'ctx', pairs_of(step))  21.1 us
    pallas_call x7, Pallas kernels, call(): pl.pallas_call(kernel, out_shape=out_shape, in_specs=in_specs or [vmem] *...  13.2 us
    ppermute x15, waiting for transfers between devices, swapped(): out[step] = lax.ppermute(values[step], 'ctx', pairs_of(step))  3.81 us
    ppermute x1, waiting for transfers between devices, body(): return kept + lax.ppermute(away, 'head', [(0, 1), (1, 0)])  1.52 us
  transfers between devices with their start and end apart: 17, of which 5 were waited for; matrix products, arithmetic and copies ran while one was open for 0% of the time, Pallas kernels for 19%

profile of v20, /device:TPU:0, one launch (start us, length us, event | category | flops | bytes accessed | tf_op | source)
XLA Modules:
  0.0 42.3 jit_solution(13743617607317630850)
XLA Ops:
  0.0 0.5 %collective-permute-start = (bf16[64,2048]{1,0:T(8,128)(2,1)}, bf16[64,2048]{1,0:T(8,128)(2,1)S(1)}, u32[]{:S(2)}, u32[]{:S(2)}) collective-permute-start(bf16[64,2048]{1,0:T(8,128)(2,1)} %mine_hbm.1), channel_id=1, source_target_pairs={{0,1},{1,0},{2,3},{3,2},{4,5},{5,4},{6,7},{7,6},{8,9},{9,8},{10,11... | collective-permute-start | bytes 786440 | tf_op jit(solution)/shard_map/ppermute | solution.py:383
  1.1 1.4 %shard_map.109 = (bf16[2048,256]{1,0:T(8,128)(2,1)S(1)}, bf16[1,2048]{1,0:T(2,128)(2,1)S(1)}, f32[1,128]{1,0:T(1,128)S(1)}, f32[1,128]{1,0:T(1,128)S(1)}, bf16[64,2048]{1,0:T(8,128)(2,1)S(1)}) custom-call(bf16[2048,128]{1,0:T(8,128)(2,1)} %key_hbm.1, bf16[2048,128]{1,0:T(8,128)(2,1)} %dir_hbm.1, bf16[1,2048]{1,0:T(2,128)(2,1)} %rate_hbm.1, ...), custom_call_target="tpu_custom_call" | custom-call | bytes 3145728 | tf_op jit(solution)/shard_map/pallas_call | solution.py:21
  2.5 2.4 %shard_map.110 = (bf16[128,2048]{1,0:T(8,128)(2,1)S(1)}, f32[128,128]{1,0:T(8,128)S(1)}, bf16[128,128]{1,0:T(8,128)(2,1)S(1)}, f32[128,128]{1,0:T(8,128)S(1)}, f...) custom-call(s32[1]{0:T(128)} %bitcast.1.core_ref, ...), custom_call_target="tpu_custom_call" | custom-call | flops 201326592 | bytes 2097152 | tf_op jit(solution)/shard_map/pallas_call | solution.py:21
  4.9 3.5 %collective-permute-start.1 = (f32[128,128]{1,0:T(8,128)S(1)}, f32[128,128]{1,0:T(8,128)S(1)}, u32[]{:S(2)}, u32[]{:S(2)}) collective-permute-start(f32[128,128]{1,0:T(8,128)S(1)} %get-tuple-element.41.refs_3_), channel_id=1, source_target_pairs={{0,6},{2,4},{4,2},{6,0},{8,14},{10,12},{12,10},{14,8},{16,22},{18,... | collective-permute-start | bytes 196616 | tf_op jit(solution)/shard_map/ppermute | solution.py:397
  8.4 0.5 %collective-permute-start.2 = (f32[128,128]{1,0:T(8,128)S(1)}, f32[128,128]{1,0:T(8,128)S(1)}, u32[]{:S(2)}, u32[]{:S(2)}) collective-permute-start(f32[128,128]{1,0:T(8,128)S(1)} %get-tuple-element.41.refs_3_), channel_id=1, source_target_pairs={{0,4},{2,6},{4,0},{6,2},{8,12},{10,14},{12,8},{14,10},{16,20},{18,... | collective-permute-start | bytes 196616 | tf_op jit(solution)/shard_map/ppermute | solution.py:397
  9.1 4.0 %collective-permute-start.4 = (bf16[128,128]{1,0:T(8,128)(2,1)S(1)}, bf16[128,128]{1,0:T(8,128)(2,1)S(1)}, u32[]{:S(2)}, u32[]{:S(2)}) collective-permute-start(bf16[128,128]{1,0:T(8,128)(2,1)S(1)} %get-tuple-element.43.refs_3_.val_ref), channel_id=1, source_target_pairs={{30,6},{28,4},{26,2},{24,0},{22,14},{20,12},{18,10},{16,8},{14,22}... | collective-permute-start | bytes 98312 | tf_op jit(solution)/shard_map/ppermute | solution.py:397
  13.1 0.6 %collective-permute-start.6 = (bf16[128,128]{1,0:T(8,128)(2,1)S(1)}, bf16[128,128]{1,0:T(8,128)(2,1)S(1)}, u32[]{:S(2)}, u32[]{:S(2)}) collective-permute-start(bf16[128,128]{1,0:T(8,128)(2,1)S(1)} %get-tuple-element.43.refs_3_.val_ref), channel_id=1, source_target_pairs={{30,22},{28,20},{26,18},{24,16},{22,30},{20,28},{18,26},{16,24},{1... | collective-permute-start | bytes 98312 | tf_op jit(solution)/shard_map/ppermute | solution.py:397
  13.7 0.5 %shard_map.111 = (bf16[512,128]{1,0:T(8,128)(2,1)S(1)}, f32[4,128,128]{2,1,0:T(8,128)S(1)}, bf16[128,128]{1,0:T(8,128)(2,1)S(1)}, bf16[128,128]{1,0:T(8,128)(2,1...) custom-call(s32[1]{0:T(128)} %bitcast.place_ref, f32[128,128]{1,0:T(8,128)S(1)} %get-tuple-element.40.exit_ref, ...), custom_call_target="tpu_custom_call" | custom-call | flops 100663296 | bytes 1000000 | tf_op jit(solution)/shard_map/pallas_call | solution.py:21
  14.2 2.4 %collective-permute-start.7 = (bf16[512,128]{1,0:T(8,128)(2,1)S(1)}, bf16[512,128]{1,0:T(8,128)(2,1)S(1)}, u32[]{:S(2)}, u32[]{:S(2)}) collective-permute-start(bf16[512,128]{1,0:T(8,128)(2,1)S(1)} %get-tuple-element.45.refs_3_), channel_id=1, source_target_pairs={{30,14},{28,12},{26,10},{24,8},{22,6},{20,4},{18,2},{16,0},{14,30}... | collective-permute-start | bytes 393224 | tf_op jit(solution)/shard_map/ppermute | solution.py:397
  16.6 1.5 %collective-permute-start.8 = (bf16[512,128]{1,0:T(8,128)(2,1)S(1)}, bf16[512,128]{1,0:T(8,128)(2,1)S(1)}, u32[]{:S(2)}, u32[]{:S(2)}) collective-permute-start(bf16[512,128]{1,0:T(8,128)(2,1)S(1)} %get-tuple-element.45.refs_3_), channel_id=1, source_target_pairs={{30,6},{28,4},{26,2},{24,0},{22,14},{20,12},{18,10},{16,8},{14,22}... | collective-permute-start | bytes 393224 | tf_op jit(solution)/shard_map/ppermute | solution.py:397
  18.1 0.5 %collective-permute-start.9 = (bf16[512,128]{1,0:T(8,128)(2,1)S(1)}, bf16[512,128]{1,0:T(8,128)(2,1)S(1)}, u32[]{:S(2)}, u32[]{:S(2)}) collective-permute-start(bf16[512,128]{1,0:T(8,128)(2,1)S(1)} %get-tuple-element.45.refs_3_), channel_id=1, source_target_pairs={{30,22},{28,20},{26,18},{24,16},{22,30},{20,28},{18,26},{16,24},{1... | collective-permute-start | bytes 393224 | tf_op jit(solution)/shard_map/ppermute | solution.py:397
  18.6 1.1 %collective-permute-done.5.refs_1_ = bf16[128,128]{1,0:T(8,128)(2,1)S(1)} collective-permute-done((bf16[128,128]{1,0:T(8,128)(2,1)S(1)}, bf16[128,128]{1,0:T(8,128)(2,1)S(1)}, u32[]{:S(2)}, u32[]{:S(2)}) %collective-permute-start.5) | collective-permute-done | bytes 32800 | tf_op jit(solution)/shard_map/ppermute | solution.py:397
  19.7 0.7 %copy-done.1 = s32[1,16]{1,0:T(1,128)S(1)} copy-done((s32[1,16]{1,0:T(1,128)S(1)}, s32[1,16]{1,0:T(1,128)}, u32[]{:S(2)}) %copy-start.1) | copy-done | bytes 88
  20.4 1.3 %shard_map.112 = (bf16[512,128]{1,0:T(8,128)(2,1)S(1)}, s32[1]{0:T(128)}) custom-call(s32[1]{0:T(128)} %bitcast.place_ref, s32[16]{0:T(128)S(1)} %bitcast.5, f32[4,128,128]{2,1,0:T(8,128)S(1)} %get-tuple-element.42.after_ref.refs_4_, bf16[128,128]{1,0:T(8,128)(2,1)S(1)} %collective-permute-done.4.refs_0_, ...), custom_call_target="tpu_custom_call" | custom-call | bytes 1000000 | tf_op jit(solution)/shard_map/pallas_call | solution.py:21
  21.7 2.5 %collective-permute-start.13 = (bf16[512,128]{1,0:T(8,128)(2,1)S(1)}, bf16[512,128]{1,0:T(8,128)(2,1)S(1)}, u32[]{:S(2)}, u32[]{:S(2)}) collective-permute-start(bf16[512,128]{1,0:T(8,128)(2,1)S(1)} %get-tuple-element.54.refs_7_), channel_id=1, source_target_pairs={{0,6},{2,4},{4,2},{6,0},{8,14},{10,12},{12,10},{14,8},{16,22},{18,... | collective-permute-start | bytes 393224 | tf_op jit(solution)/shard_map/ppermute | solution.py:397
  24.5 2.1 %collective-permute-done.7.refs_0_ = bf16[512,128]{1,0:T(8,128)(2,1)S(1)} collective-permute-done((bf16[512,128]{1,0:T(8,128)(2,1)S(1)}, bf16[512,128]{1,0:T(8,128)(2,1)S(1)}, u32[]{:S(2)}, u32[]{:S(2)}) %collective-permute-start.7) | collective-permute-done | bytes 131104 | tf_op jit(solution)/shard_map/ppermute | solution.py:397
  26.6 1.6 %collective-permute-start.15 = (bf16[512,128]{1,0:T(8,128)(2,1)S(1)}, bf16[512,128]{1,0:T(8,128)(2,1)S(1)}, u32[]{:S(2)}, u32[]{:S(2)}) collective-permute-start(bf16[512,128]{1,0:T(8,128)(2,1)S(1)} %get-tuple-element.54.refs_7_), channel_id=1, source_target_pairs={{0,2},{2,0},{4,6},{6,4},{8,10},{10,8},{12,14},{14,12},{16,18},{18,... | collective-permute-start | bytes 393224 | tf_op jit(solution)/shard_map/ppermute | solution.py:397
  28.2 0.7 %shard_map.113 = (bf16[512,128]{1,0:T(8,128)(2,1)S(1)}, bf16[512,128]{1,0:T(8,128)(2,1)S(1)}, bf16[512,128]{1,0:T(8,128)(2,1)S(1)}, bf16[512,128]{1,0:T(8,128)(2,1)S(1)}) custom-call(s32[1]{0:T(128)} %bitcast.place_ref, bf16[512,128]{1,0:T(8,128)(2,1)S(1)} %collective-permute-done.7.refs_0_, bf16[512,128]{1,0:T(8,128)(2,1)S(1)} %collective-permute-done.8.refs_1_, ...), custom_call_target="tpu_custom_call" | custom-call | flops 201326592 | bytes 1000000 | tf_op jit(solution)/shard_map/pallas_call | solution.py:21
  28.9 1.6 %collective-permute-start.10 = (bf16[512,128]{1,0:T(8,128)(2,1)S(1)}, bf16[512,128]{1,0:T(8,128)(2,1)S(1)}, u32[]{:S(2)}, u32[]{:S(2)}) collective-permute-start(bf16[512,128]{1,0:T(8,128)(2,1)S(1)} %get-tuple-element.50), channel_id=1, source_target_pairs={{0,6},{2,4},{4,2},{6,0},{8,14},{10,12},{12,10},{14,8},{16,22},{18,... | collective-permute-start | bytes 393224 | tf_op jit(solution)/shard_map/ppermute | solution.py:397
  30.9 1.6 %collective-permute-start.12 = (bf16[512,128]{1,0:T(8,128)(2,1)S(1)}, bf16[512,128]{1,0:T(8,128)(2,1)S(1)}, u32[]{:S(2)}, u32[]{:S(2)}) collective-permute-start(bf16[512,128]{1,0:T(8,128)(2,1)S(1)} %get-tuple-element.52), channel_id=1, source_target_pairs={{0,2},{2,0},{4,6},{6,4},{8,10},{10,8},{12,14},{14,12},{16,18},{18,... | collective-permute-start | bytes 393224 | tf_op jit(solution)/shard_map/ppermute | solution.py:397
  32.5 3.9 %shard_map.114 = (bf16[8,128,128]{2,1,0:T(8,128)(2,1)S(1)}, f32[8,128,128]{2,1,0:T(8,128)S(1)}, f32[8,128,1]{2,1,0:T(8,128)S(1)}, f32[8,128,1]{2,1,0:T(8,128)S(1)}) custom-call(bf16[128,2048]{1,0:T(8,128)(2,1)S(1)} %get-tuple-element.55.rows_ref, bf16[2048,1024]{1,0:T(8,128)(2,1)} %weight_hbm.1, f32[1,128]{1,0:T(1,128)S(1)} %get-tuple-element.56.gain_ref, ...), custom_call_target="tpu_custom_call" | custom-call | flops 1073741824 | bytes 16777216 | tf_op jit(solution)/shard_map/pallas_call | solution.py:21
  37.1 2.9 %shard_map.115 = (bf16[64,2048]{1,0:T(8,128)(2,1)S(1)}, bf16[64,2048]{1,0:T(8,128)(2,1)S(1)}) custom-call(s32[1]{0:T(128)} %bitcast.place_ref, s32[1]{0:T(128)} %bitcast.1.core_ref, s32[1]{0:T(128)} %get-tuple-element.44.table_ref, bf16[512,128]{1,0:T(8,128)(2,1)S(1)} %collective-permute-done.10.refs_0_, ...), custom_call_target="tpu_custom_call" | custom-call | flops 536870912 | bytes 4000000 | tf_op jit(solution)/shard_map/pallas_call | solution.py:21
  40.1 1.5 %collective-permute-done.16 = bf16[64,2048]{1,0:T(8,128)(2,1)S(1)} collective-permute-done((bf16[64,2048]{1,0:T(8,128)(2,1)S(1)}, bf16[64,2048]{1,0:T(8,128)(2,1)S(1)}, u32[]{:S(2)}, u32[]{:S(2)}) %collective-permute-start.16) | collective-permute-done | bytes 262176 | tf_op jit(solution)/shard_map/ppermute | solution.py:522
  41.6 0.8 %add.3 = bf16[64,2048]{1,0:T(8,128)(2,1)} add(bf16[64,2048]{1,0:T(8,128)(2,1)S(1)} %get-tuple-element.65, bf16[64,2048]{1,0:T(8,128)(2,1)S(1)} %collective-permute-done.16) | non-fusion elementwise | flops 131072 | bytes 786432 | tf_op jit(solution)/shard_map/add | solution.py:522
  (22 shorter events, 1.6 us)
Async XLA Ops:
  0.0 2.5 %collective-permute-start = (bf16[64,2048]{1,0:T(8,128)(2,1)}, bf16[64,2048]{1,0:T(8,128)(2,1)S(1)}, u32[]{:S(2)}, u32[]{:S(2)}) collective-permute-start(bf16[64,2048]{1,0:T(8,128)(2,1)} %mine_hbm.1), channel_id=1, source_target_pairs={{0,1},{1,0},{2,3},{3,2},{4,5},{5,4},{6,7},{7,6},{8,9},{9,8},{10,11... | collective-permute-start | bytes 786440 | tf_op jit(solution)/shard_map/ppermute | solution.py:383
  4.9 8.2 %collective-permute-start.1 = (f32[128,128]{1,0:T(8,128)S(1)}, f32[128,128]{1,0:T(8,128)S(1)}, u32[]{:S(2)}, u32[]{:S(2)}) collective-permute-start(f32[128,128]{1,0:T(8,128)S(1)} %get-tuple-element.41.refs_3_), channel_id=1, source_target_pairs={{0,6},{2,4},{4,2},{6,0},{8,14},{10,12},{12,10},{14,8},{16,22},{18,... | collective-permute-start | bytes 196616 | tf_op jit(solution)/shard_map/ppermute | solution.py:397
  8.4 5.2 %collective-permute-start.2 = (f32[128,128]{1,0:T(8,128)S(1)}, f32[128,128]{1,0:T(8,128)S(1)}, u32[]{:S(2)}, u32[]{:S(2)}) collective-permute-start(f32[128,128]{1,0:T(8,128)S(1)} %get-tuple-element.41.refs_3_), channel_id=1, source_target_pairs={{0,4},{2,6},{4,0},{6,2},{8,12},{10,14},{12,8},{14,10},{16,20},{18,... | collective-permute-start | bytes 196616 | tf_op jit(solution)/shard_map/ppermute | solution.py:397
  8.9 4.7 %collective-permute-start.3 = (f32[128,128]{1,0:T(8,128)S(1)}, f32[128,128]{1,0:T(8,128)S(1)}, u32[]{:S(2)}, u32[]{:S(2)}) collective-permute-start(f32[128,128]{1,0:T(8,128)S(1)} %get-tuple-element.41.refs_3_), channel_id=1, source_target_pairs={{0,2},{2,0},{4,6},{6,4},{8,10},{10,8},{12,14},{14,12},{16,18},{18,... | collective-permute-start | bytes 196616 | tf_op jit(solution)/shard_map/ppermute | solution.py:397
  9.1 9.1 %collective-permute-start.4 = (bf16[128,128]{1,0:T(8,128)(2,1)S(1)}, bf16[128,128]{1,0:T(8,128)(2,1)S(1)}, u32[]{:S(2)}, u32[]{:S(2)}) collective-permute-start(bf16[128,128]{1,0:T(8,128)(2,1)S(1)} %get-tuple-element.43.refs_3_.val_ref), channel_id=1, source_target_pairs={{30,6},{28,4},{26,2},{24,0},{22,14},{20,12},{18,10},{16,8},{14,22}... | collective-permute-start | bytes 98312 | tf_op jit(solution)/shard_map/ppermute | solution.py:397
  13.1 6.6 %collective-permute-start.5 = (bf16[128,128]{1,0:T(8,128)(2,1)S(1)}, bf16[128,128]{1,0:T(8,128)(2,1)S(1)}, u32[]{:S(2)}, u32[]{:S(2)}) collective-permute-start(bf16[128,128]{1,0:T(8,128)(2,1)S(1)} %get-tuple-element.43.refs_3_.val_ref), channel_id=1, source_target_pairs={{30,14},{28,12},{26,10},{24,8},{22,6},{20,4},{18,2},{16,0},{14,30}... | collective-permute-start | bytes 98312 | tf_op jit(solution)/shard_map/ppermute | solution.py:397
  13.1 6.6 %collective-permute-start.6 = (bf16[128,128]{1,0:T(8,128)(2,1)S(1)}, bf16[128,128]{1,0:T(8,128)(2,1)S(1)}, u32[]{:S(2)}, u32[]{:S(2)}) collective-permute-start(bf16[128,128]{1,0:T(8,128)(2,1)S(1)} %get-tuple-element.43.refs_3_.val_ref), channel_id=1, source_target_pairs={{30,22},{28,20},{26,18},{24,16},{22,30},{20,28},{18,26},{16,24},{1... | collective-permute-start | bytes 98312 | tf_op jit(solution)/shard_map/ppermute | solution.py:397
  13.7 23.4 %copy-start = (bf16[1024,2048]{1,0:T(8,128)(2,1)S(1)}, bf16[1024,2048]{1,0:T(8,128)(2,1)}, u32[]{:S(2)}) copy-start(bf16[1024,2048]{1,0:T(8,128)(2,1)} %refs_12_.1) | copy-start | bytes 12582916
  14.2 12.4 %collective-permute-start.7 = (bf16[512,128]{1,0:T(8,128)(2,1)S(1)}, bf16[512,128]{1,0:T(8,128)(2,1)S(1)}, u32[]{:S(2)}, u32[]{:S(2)}) collective-permute-start(bf16[512,128]{1,0:T(8,128)(2,1)S(1)} %get-tuple-element.45.refs_3_), channel_id=1, source_target_pairs={{30,14},{28,12},{26,10},{24,8},{22,6},{20,4},{18,2},{16,0},{14,30}... | collective-permute-start | bytes 393224 | tf_op jit(solution)/shard_map/ppermute | solution.py:397
  16.6 11.6 %collective-permute-start.8 = (bf16[512,128]{1,0:T(8,128)(2,1)S(1)}, bf16[512,128]{1,0:T(8,128)(2,1)S(1)}, u32[]{:S(2)}, u32[]{:S(2)}) collective-permute-start(bf16[512,128]{1,0:T(8,128)(2,1)S(1)} %get-tuple-element.45.refs_3_), channel_id=1, source_target_pairs={{30,6},{28,4},{26,2},{24,0},{22,14},{20,12},{18,10},{16,8},{14,22}... | collective-permute-start | bytes 393224 | tf_op jit(solution)/shard_map/ppermute | solution.py:397
  18.1 10.0 %collective-permute-start.9 = (bf16[512,128]{1,0:T(8,128)(2,1)S(1)}, bf16[512,128]{1,0:T(8,128)(2,1)S(1)}, u32[]{:S(2)}, u32[]{:S(2)}) collective-permute-start(bf16[512,128]{1,0:T(8,128)(2,1)S(1)} %get-tuple-element.45.refs_3_), channel_id=1, source_target_pairs={{30,22},{28,20},{26,18},{24,16},{22,30},{20,28},{18,26},{16,24},{1... | collective-permute-start | bytes 393224 | tf_op jit(solution)/shard_map/ppermute | solution.py:397
  19.7 0.7 %copy-start.1 = (s32[1,16]{1,0:T(1,128)S(1)}, s32[1,16]{1,0:T(1,128)}, u32[]{:S(2)}) copy-start(s32[1,16]{1,0:T(1,128)} %param.21) | copy-start | bytes 196
  21.7 9.2 %collective-permute-start.13 = (bf16[512,128]{1,0:T(8,128)(2,1)S(1)}, bf16[512,128]{1,0:T(8,128)(2,1)S(1)}, u32[]{:S(2)}, u32[]{:S(2)}) collective-permute-start(bf16[512,128]{1,0:T(8,128)(2,1)S(1)} %get-tuple-element.54.refs_7_), channel_id=1, source_target_pairs={{0,6},{2,4},{4,2},{6,0},{8,14},{10,12},{12,10},{14,8},{16,22},{18,... | collective-permute-start | bytes 393224 | tf_op jit(solution)/shard_map/ppermute | solution.py:397
  24.2 12.2 %collective-permute-start.14 = (bf16[512,128]{1,0:T(8,128)(2,1)S(1)}, bf16[512,128]{1,0:T(8,128)(2,1)S(1)}, u32[]{:S(2)}, u32[]{:S(2)}) collective-permute-start(bf16[512,128]{1,0:T(8,128)(2,1)S(1)} %get-tuple-element.54.refs_7_), channel_id=1, source_target_pairs={{0,4},{2,6},{4,0},{6,2},{8,12},{10,14},{12,8},{14,10},{16,20},{18,... | collective-permute-start | bytes 393224 | tf_op jit(solution)/shard_map/ppermute | solution.py:397
  26.6 9.8 %collective-permute-start.15 = (bf16[512,128]{1,0:T(8,128)(2,1)S(1)}, bf16[512,128]{1,0:T(8,128)(2,1)S(1)}, u32[]{:S(2)}, u32[]{:S(2)}) collective-permute-start(bf16[512,128]{1,0:T(8,128)(2,1)S(1)} %get-tuple-element.54.refs_7_), channel_id=1, source_target_pairs={{0,2},{2,0},{4,6},{6,4},{8,10},{10,8},{12,14},{14,12},{16,18},{18,... | collective-permute-start | bytes 393224 | tf_op jit(solution)/shard_map/ppermute | solution.py:397
  28.9 7.5 %collective-permute-start.10 = (bf16[512,128]{1,0:T(8,128)(2,1)S(1)}, bf16[512,128]{1,0:T(8,128)(2,1)S(1)}, u32[]{:S(2)}, u32[]{:S(2)}) collective-permute-start(bf16[512,128]{1,0:T(8,128)(2,1)S(1)} %get-tuple-element.50), channel_id=1, source_target_pairs={{0,6},{2,4},{4,2},{6,0},{8,14},{10,12},{12,10},{14,8},{16,22},{18,... | collective-permute-start | bytes 393224 | tf_op jit(solution)/shard_map/ppermute | solution.py:397
  30.5 6.4 %collective-permute-start.11 = (bf16[512,128]{1,0:T(8,128)(2,1)S(1)}, bf16[512,128]{1,0:T(8,128)(2,1)S(1)}, u32[]{:S(2)}, u32[]{:S(2)}) collective-permute-start(bf16[512,128]{1,0:T(8,128)(2,1)S(1)} %get-tuple-element.51), channel_id=1, source_target_pairs={{0,4},{2,6},{4,0},{6,2},{8,12},{10,14},{12,8},{14,10},{16,20},{18,... | collective-permute-start | bytes 393224 | tf_op jit(solution)/shard_map/ppermute | solution.py:397
  30.9 6.2 %collective-permute-start.12 = (bf16[512,128]{1,0:T(8,128)(2,1)S(1)}, bf16[512,128]{1,0:T(8,128)(2,1)S(1)}, u32[]{:S(2)}, u32[]{:S(2)}) collective-permute-start(bf16[512,128]{1,0:T(8,128)(2,1)S(1)} %get-tuple-element.52), channel_id=1, source_target_pairs={{0,2},{2,0},{4,6},{6,4},{8,10},{10,8},{12,14},{14,12},{16,18},{18,... | collective-permute-start | bytes 393224 | tf_op jit(solution)/shard_map/ppermute | solution.py:397
  40.0 1.6 %collective-permute-start.16 = (bf16[64,2048]{1,0:T(8,128)(2,1)S(1)}, bf16[64,2048]{1,0:T(8,128)(2,1)S(1)}, u32[]{:S(2)}, u32[]{:S(2)}) collective-permute-start(bf16[64,2048]{1,0:T(8,128)(2,1)S(1)} %get-tuple-element.66), channel_id=1, source_target_pairs={{0,1},{1,0},{2,3},{3,2},{4,5},{5,4},{6,7},{7,6},{8,9},{9,8},{10,11... | collective-permute-start | bytes 786440 | tf_op jit(solution)/shard_map/ppermute | solution.py:522

commit v21 on v18

--- a/solution.py
+++ b/solution.py
@@ -42,7 +42,7 @@
 
 
 def line_order(groups):
-    return [groups // 2] + [step for step in range(groups - 1, 0, -1) if step != groups // 2] + [0]
+    return [groups // 2] + [step for step in range(1, groups) if step != groups // 2] + [0]
 
 
 def shaped(shape, dtype):

time: 42.5 us -> 42 us (0.988)
  transfers between devices with their start and end apart: 17 -> 17, of which waited for: 5 -> 4; matrix products, arithmetic and copies ran while one was open for 0% -> 0% of each run, Pallas kernels for 19% -> 19%
where the time goes in v21:
time: 42 us; the launch traced here: 41.8 us
  starting transfers between devices  21.2 us (50%)
  Pallas kernels  13.2 us (31%)
  waiting for transfers between devices  5.23 us (12%)
  between operations  0.78 us (2%)
  other arithmetic  0.77 us (2%)
  local copies, waits for them, and re-layouts  0.66 us (2%)
    ppermute x15, starting transfers between devices, swapped(): out[step] = lax.ppermute(values[step], 'ctx', pairs_of(step))  20.7 us
    pallas_call x7, Pallas kernels, call(): pl.pallas_call(kernel, out_shape=out_shape, in_specs=in_specs or [vmem] *...  13.2 us
    ppermute x15, waiting for transfers between devices, swapped(): out[step] = lax.ppermute(values[step], 'ctx', pairs_of(step))  3.71 us
    ppermute x1, waiting for transfers between devices, body(): return kept + lax.ppermute(away, 'head', [(0, 1), (1, 0)])  1.52 us
  transfers between devices with their start and end apart: 17, of which 4 were waited for; matrix products, arithmetic and copies ran while one was open for 0% of the time, Pallas kernels for 19%

profile of v21, /device:TPU:0, one launch (start us, length us, event | category | flops | bytes accessed | tf_op | source)
XLA Modules:
  0.0 41.8 jit_solution(14356676185551691830)
XLA Ops:
  0.0 0.5 %collective-permute-start = (bf16[64,2048]{1,0:T(8,128)(2,1)}, bf16[64,2048]{1,0:T(8,128)(2,1)S(1)}, u32[]{:S(2)}, u32[]{:S(2)}) collective-permute-start(bf16[64,2048]{1,0:T(8,128)(2,1)} %mine_hbm.1), channel_id=1, source_target_pairs={{0,1},{1,0},{2,3},{3,2},{4,5},{5,4},{6,7},{7,6},{8,9},{9,8},{10,11... | collective-permute-start | bytes 786440 | tf_op jit(solution)/shard_map/ppermute | solution.py:383
  1.1 1.4 %shard_map.109 = (bf16[2048,256]{1,0:T(8,128)(2,1)S(1)}, bf16[1,2048]{1,0:T(2,128)(2,1)S(1)}, f32[1,128]{1,0:T(1,128)S(1)}, f32[1,128]{1,0:T(1,128)S(1)}, bf16[64,2048]{1,0:T(8,128)(2,1)S(1)}) custom-call(bf16[2048,128]{1,0:T(8,128)(2,1)} %key_hbm.1, bf16[2048,128]{1,0:T(8,128)(2,1)} %dir_hbm.1, bf16[1,2048]{1,0:T(2,128)(2,1)} %rate_hbm.1, ...), custom_call_target="tpu_custom_call" | custom-call | bytes 3145728 | tf_op jit(solution)/shard_map/pallas_call | solution.py:21
  2.5 2.4 %shard_map.110 = (bf16[128,2048]{1,0:T(8,128)(2,1)S(1)}, f32[128,128]{1,0:T(8,128)S(1)}, bf16[128,128]{1,0:T(8,128)(2,1)S(1)}, f32[128,128]{1,0:T(8,128)S(1)}, f...) custom-call(s32[1]{0:T(128)} %bitcast.1.core_ref, ...), custom_call_target="tpu_custom_call" | custom-call | flops 201326592 | bytes 2097152 | tf_op jit(solution)/shard_map/pallas_call | solution.py:21
  4.9 3.5 %collective-permute-start.1 = (f32[128,128]{1,0:T(8,128)S(1)}, f32[128,128]{1,0:T(8,128)S(1)}, u32[]{:S(2)}, u32[]{:S(2)}) collective-permute-start(f32[128,128]{1,0:T(8,128)S(1)} %get-tuple-element.41.refs_3_), channel_id=1, source_target_pairs={{0,6},{2,4},{4,2},{6,0},{8,14},{10,12},{12,10},{14,8},{16,22},{18,... | collective-permute-start | bytes 196616 | tf_op jit(solution)/shard_map/ppermute | solution.py:397
  8.4 0.5 %collective-permute-start.2 = (f32[128,128]{1,0:T(8,128)S(1)}, f32[128,128]{1,0:T(8,128)S(1)}, u32[]{:S(2)}, u32[]{:S(2)}) collective-permute-start(f32[128,128]{1,0:T(8,128)S(1)} %get-tuple-element.41.refs_3_), channel_id=1, source_target_pairs={{0,4},{2,6},{4,0},{6,2},{8,12},{10,14},{12,8},{14,10},{16,20},{18,... | collective-permute-start | bytes 196616 | tf_op jit(solution)/shard_map/ppermute | solution.py:397
  9.1 4.0 %collective-permute-start.4 = (bf16[128,128]{1,0:T(8,128)(2,1)S(1)}, bf16[128,128]{1,0:T(8,128)(2,1)S(1)}, u32[]{:S(2)}, u32[]{:S(2)}) collective-permute-start(bf16[128,128]{1,0:T(8,128)(2,1)S(1)} %get-tuple-element.43.refs_3_.val_ref), channel_id=1, source_target_pairs={{0,24},{2,26},{4,28},{6,30},{8,16},{10,18},{12,20},{14,22},{16,8},... | collective-permute-start | bytes 98312 | tf_op jit(solution)/shard_map/ppermute | solution.py:397
  13.1 0.6 %collective-permute-start.6 = (bf16[128,128]{1,0:T(8,128)(2,1)S(1)}, bf16[128,128]{1,0:T(8,128)(2,1)S(1)}, u32[]{:S(2)}, u32[]{:S(2)}) collective-permute-start(bf16[128,128]{1,0:T(8,128)(2,1)S(1)} %get-tuple-element.43.refs_3_.val_ref), channel_id=1, source_target_pairs={{0,8},{2,10},{4,12},{6,14},{8,0},{10,2},{12,4},{14,6},{16,24},{18,... | collective-permute-start | bytes 98312 | tf_op jit(solution)/shard_map/ppermute | solution.py:397
  13.7 0.5 %shard_map.111 = (bf16[512,128]{1,0:T(8,128)(2,1)S(1)}, f32[4,128,128]{2,1,0:T(8,128)S(1)}, bf16[128,128]{1,0:T(8,128)(2,1)S(1)}, bf16[128,128]{1,0:T(8,128)(2,1...) custom-call(s32[1]{0:T(128)} %bitcast.place_ref, f32[128,128]{1,0:T(8,128)S(1)} %get-tuple-element.40.exit_ref, ...), custom_call_target="tpu_custom_call" | custom-call | flops 100663296 | bytes 1000000 | tf_op jit(solution)/shard_map/pallas_call | solution.py:21
  14.2 2.4 %collective-permute-start.7 = (bf16[512,128]{1,0:T(8,128)(2,1)S(1)}, bf16[512,128]{1,0:T(8,128)(2,1)S(1)}, u32[]{:S(2)}, u32[]{:S(2)}) collective-permute-start(bf16[512,128]{1,0:T(8,128)(2,1)S(1)} %get-tuple-element.45.refs_3_), channel_id=1, source_target_pairs={{0,16},{2,18},{4,20},{6,22},{8,24},{10,26},{12,28},{14,30},{16,0},... | collective-permute-start | bytes 393224 | tf_op jit(solution)/shard_map/ppermute | solution.py:397
  16.6 2.0 %collective-permute-start.8 = (bf16[512,128]{1,0:T(8,128)(2,1)S(1)}, bf16[512,128]{1,0:T(8,128)(2,1)S(1)}, u32[]{:S(2)}, u32[]{:S(2)}) collective-permute-start(bf16[512,128]{1,0:T(8,128)(2,1)S(1)} %get-tuple-element.45.refs_3_), channel_id=1, source_target_pairs={{0,8},{2,10},{4,12},{6,14},{8,0},{10,2},{12,4},{14,6},{16,24},{18,... | collective-permute-start | bytes 393224 | tf_op jit(solution)/shard_map/ppermute | solution.py:397
  18.8 0.9 %collective-permute-done.5.refs_1_ = bf16[128,128]{1,0:T(8,128)(2,1)S(1)} collective-permute-done((bf16[128,128]{1,0:T(8,128)(2,1)S(1)}, bf16[128,128]{1,0:T(8,128)(2,1)S(1)}, u32[]{:S(2)}, u32[]{:S(2)}) %collective-permute-start.5) | collective-permute-done | bytes 32800 | tf_op jit(solution)/shard_map/ppermute | solution.py:397
  19.7 0.7 %copy-done.1 = s32[1,16]{1,0:T(1,128)S(1)} copy-done((s32[1,16]{1,0:T(1,128)S(1)}, s32[1,16]{1,0:T(1,128)}, u32[]{:S(2)}) %copy-start.1) | copy-done | bytes 88
  20.4 1.3 %shard_map.112 = (bf16[512,128]{1,0:T(8,128)(2,1)S(1)}, s32[1]{0:T(128)}) custom-call(s32[1]{0:T(128)} %bitcast.place_ref, s32[16]{0:T(128)S(1)} %bitcast.5, f32[4,128,128]{2,1,0:T(8,128)S(1)} %get-tuple-element.42.after_ref.refs_4_, bf16[128,128]{1,0:T(8,128)(2,1)S(1)} %collective-permute-done.4.refs_0_, ...), custom_call_target="tpu_custom_call" | custom-call | bytes 1000000 | tf_op jit(solution)/shard_map/pallas_call | solution.py:21
  21.7 2.5 %collective-permute-start.13 = (bf16[512,128]{1,0:T(8,128)(2,1)S(1)}, bf16[512,128]{1,0:T(8,128)(2,1)S(1)}, u32[]{:S(2)}, u32[]{:S(2)}) collective-permute-start(bf16[512,128]{1,0:T(8,128)(2,1)S(1)} %get-tuple-element.54.refs_7_), channel_id=1, source_target_pairs={{0,6},{2,4},{4,2},{6,0},{8,14},{10,12},{12,10},{14,8},{16,22},{18,... | collective-permute-start | bytes 393224 | tf_op jit(solution)/shard_map/ppermute | solution.py:397
  24.5 2.1 %collective-permute-done.7.refs_0_ = bf16[512,128]{1,0:T(8,128)(2,1)S(1)} collective-permute-done((bf16[512,128]{1,0:T(8,128)(2,1)S(1)}, bf16[512,128]{1,0:T(8,128)(2,1)S(1)}, u32[]{:S(2)}, u32[]{:S(2)}) %collective-permute-start.7) | collective-permute-done | bytes 131104 | tf_op jit(solution)/shard_map/ppermute | solution.py:397
  26.6 0.7 %shard_map.113 = (bf16[512,128]{1,0:T(8,128)(2,1)S(1)}, bf16[512,128]{1,0:T(8,128)(2,1)S(1)}, bf16[512,128]{1,0:T(8,128)(2,1)S(1)}, bf16[512,128]{1,0:T(8,128)(2,1)S(1)}) custom-call(s32[1]{0:T(128)} %bitcast.place_ref, bf16[512,128]{1,0:T(8,128)(2,1)S(1)} %collective-permute-done.7.refs_0_, bf16[512,128]{1,0:T(8,128)(2,1)S(1)} %collective-permute-done.8.refs_1_, ...), custom_call_target="tpu_custom_call" | custom-call | flops 201326592 | bytes 1000000 | tf_op jit(solution)/shard_map/pallas_call | solution.py:21
  27.4 2.5 %collective-permute-start.10 = (bf16[512,128]{1,0:T(8,128)(2,1)S(1)}, bf16[512,128]{1,0:T(8,128)(2,1)S(1)}, u32[]{:S(2)}, u32[]{:S(2)}) collective-permute-start(bf16[512,128]{1,0:T(8,128)(2,1)S(1)} %get-tuple-element.50), channel_id=1, source_target_pairs={{0,6},{2,4},{4,2},{6,0},{8,14},{10,12},{12,10},{14,8},{16,22},{18,... | collective-permute-start | bytes 393224 | tf_op jit(solution)/shard_map/ppermute | solution.py:397
  29.9 1.0 %collective-permute-start.11 = (bf16[512,128]{1,0:T(8,128)(2,1)S(1)}, bf16[512,128]{1,0:T(8,128)(2,1)S(1)}, u32[]{:S(2)}, u32[]{:S(2)}) collective-permute-start(bf16[512,128]{1,0:T(8,128)(2,1)S(1)} %get-tuple-element.51), channel_id=1, source_target_pairs={{0,4},{2,6},{4,0},{6,2},{8,12},{10,14},{12,8},{14,10},{16,20},{18,... | collective-permute-start | bytes 393224 | tf_op jit(solution)/shard_map/ppermute | solution.py:397
  30.9 1.0 %collective-permute-start.12 = (bf16[512,128]{1,0:T(8,128)(2,1)S(1)}, bf16[512,128]{1,0:T(8,128)(2,1)S(1)}, u32[]{:S(2)}, u32[]{:S(2)}) collective-permute-start(bf16[512,128]{1,0:T(8,128)(2,1)S(1)} %get-tuple-element.52), channel_id=1, source_target_pairs={{0,2},{2,0},{4,6},{6,4},{8,10},{10,8},{12,14},{14,12},{16,18},{18,... | collective-permute-start | bytes 393224 | tf_op jit(solution)/shard_map/ppermute | solution.py:397
  31.9 3.9 %shard_map.114 = (bf16[8,128,128]{2,1,0:T(8,128)(2,1)S(1)}, f32[8,128,128]{2,1,0:T(8,128)S(1)}, f32[8,128,1]{2,1,0:T(8,128)S(1)}, f32[8,128,1]{2,1,0:T(8,128)S(1)}) custom-call(bf16[128,2048]{1,0:T(8,128)(2,1)S(1)} %get-tuple-element.55.rows_ref, bf16[2048,1024]{1,0:T(8,128)(2,1)} %weight_hbm.1, f32[1,128]{1,0:T(1,128)S(1)} %get-tuple-element.56.gain_ref, ...), custom_call_target="tpu_custom_call" | custom-call | flops 1073741824 | bytes 16777216 | tf_op jit(solution)/shard_map/pallas_call | solution.py:21
  35.9 0.7 %collective-permute-done.12.refs_2_ = bf16[512,128]{1,0:T(8,128)(2,1)S(1)} collective-permute-done((bf16[512,128]{1,0:T(8,128)(2,1)S(1)}, bf16[512,128]{1,0:T(8,128)(2,1)S(1)}, u32[]{:S(2)}, u32[]{:S(2)}) %collective-permute-start.12) | collective-permute-done | bytes 131104 | tf_op jit(solution)/shard_map/ppermute | solution.py:397
  36.6 2.9 %shard_map.115 = (bf16[64,2048]{1,0:T(8,128)(2,1)S(1)}, bf16[64,2048]{1,0:T(8,128)(2,1)S(1)}) custom-call(s32[1]{0:T(128)} %bitcast.place_ref, s32[1]{0:T(128)} %bitcast.1.core_ref, s32[1]{0:T(128)} %get-tuple-element.44.table_ref, bf16[512,128]{1,0:T(8,128)(2,1)S(1)} %collective-permute-done.10.refs_0_, ...), custom_call_target="tpu_custom_call" | custom-call | flops 536870912 | bytes 4000000 | tf_op jit(solution)/shard_map/pallas_call | solution.py:21
  39.5 1.5 %collective-permute-done.16 = bf16[64,2048]{1,0:T(8,128)(2,1)S(1)} collective-permute-done((bf16[64,2048]{1,0:T(8,128)(2,1)S(1)}, bf16[64,2048]{1,0:T(8,128)(2,1)S(1)}, u32[]{:S(2)}, u32[]{:S(2)}) %collective-permute-start.16) | collective-permute-done | bytes 262176 | tf_op jit(solution)/shard_map/ppermute | solution.py:521
  41.1 0.8 %add.3 = bf16[64,2048]{1,0:T(8,128)(2,1)} add(bf16[64,2048]{1,0:T(8,128)(2,1)S(1)} %get-tuple-element.65, bf16[64,2048]{1,0:T(8,128)(2,1)S(1)} %collective-permute-done.16) | non-fusion elementwise | flops 131072 | bytes 786432 | tf_op jit(solution)/shard_map/add | solution.py:521
  (22 shorter events, 0.7 us)
Async XLA Ops:
  0.0 2.5 %collective-permute-start = (bf16[64,2048]{1,0:T(8,128)(2,1)}, bf16[64,2048]{1,0:T(8,128)(2,1)S(1)}, u32[]{:S(2)}, u32[]{:S(2)}) collective-permute-start(bf16[64,2048]{1,0:T(8,128)(2,1)} %mine_hbm.1), channel_id=1, source_target_pairs={{0,1},{1,0},{2,3},{3,2},{4,5},{5,4},{6,7},{7,6},{8,9},{9,8},{10,11... | collective-permute-start | bytes 786440 | tf_op jit(solution)/shard_map/ppermute | solution.py:383
  4.9 8.2 %collective-permute-start.1 = (f32[128,128]{1,0:T(8,128)S(1)}, f32[128,128]{1,0:T(8,128)S(1)}, u32[]{:S(2)}, u32[]{:S(2)}) collective-permute-start(f32[128,128]{1,0:T(8,128)S(1)} %get-tuple-element.41.refs_3_), channel_id=1, source_target_pairs={{0,6},{2,4},{4,2},{6,0},{8,14},{10,12},{12,10},{14,8},{16,22},{18,... | collective-permute-start | bytes 196616 | tf_op jit(solution)/shard_map/ppermute | solution.py:397
  8.4 5.2 %collective-permute-start.2 = (f32[128,128]{1,0:T(8,128)S(1)}, f32[128,128]{1,0:T(8,128)S(1)}, u32[]{:S(2)}, u32[]{:S(2)}) collective-permute-start(f32[128,128]{1,0:T(8,128)S(1)} %get-tuple-element.41.refs_3_), channel_id=1, source_target_pairs={{0,4},{2,6},{4,0},{6,2},{8,12},{10,14},{12,8},{14,10},{16,20},{18,... | collective-permute-start | bytes 196616 | tf_op jit(solution)/shard_map/ppermute | solution.py:397
  8.9 4.7 %collective-permute-start.3 = (f32[128,128]{1,0:T(8,128)S(1)}, f32[128,128]{1,0:T(8,128)S(1)}, u32[]{:S(2)}, u32[]{:S(2)}) collective-permute-start(f32[128,128]{1,0:T(8,128)S(1)} %get-tuple-element.41.refs_3_), channel_id=1, source_target_pairs={{0,2},{2,0},{4,6},{6,4},{8,10},{10,8},{12,14},{14,12},{16,18},{18,... | collective-permute-start | bytes 196616 | tf_op jit(solution)/shard_map/ppermute | solution.py:397
  9.1 9.6 %collective-permute-start.4 = (bf16[128,128]{1,0:T(8,128)(2,1)S(1)}, bf16[128,128]{1,0:T(8,128)(2,1)S(1)}, u32[]{:S(2)}, u32[]{:S(2)}) collective-permute-start(bf16[128,128]{1,0:T(8,128)(2,1)S(1)} %get-tuple-element.43.refs_3_.val_ref), channel_id=1, source_target_pairs={{0,24},{2,26},{4,28},{6,30},{8,16},{10,18},{12,20},{14,22},{16,8},... | collective-permute-start | bytes 98312 | tf_op jit(solution)/shard_map/ppermute | solution.py:397
  13.1 6.6 %collective-permute-start.5 = (bf16[128,128]{1,0:T(8,128)(2,1)S(1)}, bf16[128,128]{1,0:T(8,128)(2,1)S(1)}, u32[]{:S(2)}, u32[]{:S(2)}) collective-permute-start(bf16[128,128]{1,0:T(8,128)(2,1)S(1)} %get-tuple-element.43.refs_3_.val_ref), channel_id=1, source_target_pairs={{0,16},{2,18},{4,20},{6,22},{8,24},{10,26},{12,28},{14,30},{16,0},... | collective-permute-start | bytes 98312 | tf_op jit(solution)/shard_map/ppermute | solution.py:397
  13.1 6.6 %collective-permute-start.6 = (bf16[128,128]{1,0:T(8,128)(2,1)S(1)}, bf16[128,128]{1,0:T(8,128)(2,1)S(1)}, u32[]{:S(2)}, u32[]{:S(2)}) collective-permute-start(bf16[128,128]{1,0:T(8,128)(2,1)S(1)} %get-tuple-element.43.refs_3_.val_ref), channel_id=1, source_target_pairs={{0,8},{2,10},{4,12},{6,14},{8,0},{10,2},{12,4},{14,6},{16,24},{18,... | collective-permute-start | bytes 98312 | tf_op jit(solution)/shard_map/ppermute | solution.py:397
  13.7 22.9 %copy-start = (bf16[1024,2048]{1,0:T(8,128)(2,1)S(1)}, bf16[1024,2048]{1,0:T(8,128)(2,1)}, u32[]{:S(2)}) copy-start(bf16[1024,2048]{1,0:T(8,128)(2,1)} %refs_12_.1) | copy-start | bytes 12582916
  14.2 12.4 %collective-permute-start.7 = (bf16[512,128]{1,0:T(8,128)(2,1)S(1)}, bf16[512,128]{1,0:T(8,128)(2,1)S(1)}, u32[]{:S(2)}, u32[]{:S(2)}) collective-permute-start(bf16[512,128]{1,0:T(8,128)(2,1)S(1)} %get-tuple-element.45.refs_3_), channel_id=1, source_target_pairs={{0,16},{2,18},{4,20},{6,22},{8,24},{10,26},{12,28},{14,30},{16,0},... | collective-permute-start | bytes 393224 | tf_op jit(solution)/shard_map/ppermute | solution.py:397
  16.6 10.0 %collective-permute-start.8 = (bf16[512,128]{1,0:T(8,128)(2,1)S(1)}, bf16[512,128]{1,0:T(8,128)(2,1)S(1)}, u32[]{:S(2)}, u32[]{:S(2)}) collective-permute-start(bf16[512,128]{1,0:T(8,128)(2,1)S(1)} %get-tuple-element.45.refs_3_), channel_id=1, source_target_pairs={{0,8},{2,10},{4,12},{6,14},{8,0},{10,2},{12,4},{14,6},{16,24},{18,... | collective-permute-start | bytes 393224 | tf_op jit(solution)/shard_map/ppermute | solution.py:397
  18.6 8.0 %collective-permute-start.9 = (bf16[512,128]{1,0:T(8,128)(2,1)S(1)}, bf16[512,128]{1,0:T(8,128)(2,1)S(1)}, u32[]{:S(2)}, u32[]{:S(2)}) collective-permute-start(bf16[512,128]{1,0:T(8,128)(2,1)S(1)} %get-tuple-element.45.refs_3_), channel_id=1, source_target_pairs={{0,24},{2,26},{4,28},{6,30},{8,16},{10,18},{12,20},{14,22},{16,8},... | collective-permute-start | bytes 393224 | tf_op jit(solution)/shard_map/ppermute | solution.py:397
  19.7 0.7 %copy-start.1 = (s32[1,16]{1,0:T(1,128)S(1)}, s32[1,16]{1,0:T(1,128)}, u32[]{:S(2)}) copy-start(s32[1,16]{1,0:T(1,128)} %param.21) | copy-start | bytes 196
  21.7 9.2 %collective-permute-start.13 = (bf16[512,128]{1,0:T(8,128)(2,1)S(1)}, bf16[512,128]{1,0:T(8,128)(2,1)S(1)}, u32[]{:S(2)}, u32[]{:S(2)}) collective-permute-start(bf16[512,128]{1,0:T(8,128)(2,1)S(1)} %get-tuple-element.54.refs_7_), channel_id=1, source_target_pairs={{0,6},{2,4},{4,2},{6,0},{8,14},{10,12},{12,10},{14,8},{16,22},{18,... | collective-permute-start | bytes 393224 | tf_op jit(solution)/shard_map/ppermute | solution.py:397
  24.2 11.6 %collective-permute-start.14 = (bf16[512,128]{1,0:T(8,128)(2,1)S(1)}, bf16[512,128]{1,0:T(8,128)(2,1)S(1)}, u32[]{:S(2)}, u32[]{:S(2)}) collective-permute-start(bf16[512,128]{1,0:T(8,128)(2,1)S(1)} %get-tuple-element.54.refs_7_), channel_id=1, source_target_pairs={{0,4},{2,6},{4,0},{6,2},{8,12},{10,14},{12,8},{14,10},{16,20},{18,... | collective-permute-start | bytes 393224 | tf_op jit(solution)/shard_map/ppermute | solution.py:397
  26.6 9.2 %collective-permute-start.15 = (bf16[512,128]{1,0:T(8,128)(2,1)S(1)}, bf16[512,128]{1,0:T(8,128)(2,1)S(1)}, u32[]{:S(2)}, u32[]{:S(2)}) collective-permute-start(bf16[512,128]{1,0:T(8,128)(2,1)S(1)} %get-tuple-element.54.refs_7_), channel_id=1, source_target_pairs={{0,2},{2,0},{4,6},{6,4},{8,10},{10,8},{12,14},{14,12},{16,18},{18,... | collective-permute-start | bytes 393224 | tf_op jit(solution)/shard_map/ppermute | solution.py:397
  27.4 8.5 %collective-permute-start.10 = (bf16[512,128]{1,0:T(8,128)(2,1)S(1)}, bf16[512,128]{1,0:T(8,128)(2,1)S(1)}, u32[]{:S(2)}, u32[]{:S(2)}) collective-permute-start(bf16[512,128]{1,0:T(8,128)(2,1)S(1)} %get-tuple-element.50), channel_id=1, source_target_pairs={{0,6},{2,4},{4,2},{6,0},{8,14},{10,12},{12,10},{14,8},{16,22},{18,... | collective-permute-start | bytes 393224 | tf_op jit(solution)/shard_map/ppermute | solution.py:397
  29.9 6.0 %collective-permute-start.11 = (bf16[512,128]{1,0:T(8,128)(2,1)S(1)}, bf16[512,128]{1,0:T(8,128)(2,1)S(1)}, u32[]{:S(2)}, u32[]{:S(2)}) collective-permute-start(bf16[512,128]{1,0:T(8,128)(2,1)S(1)} %get-tuple-element.51), channel_id=1, source_target_pairs={{0,4},{2,6},{4,0},{6,2},{8,12},{10,14},{12,8},{14,10},{16,20},{18,... | collective-permute-start | bytes 393224 | tf_op jit(solution)/shard_map/ppermute | solution.py:397
  30.9 5.7 %collective-permute-start.12 = (bf16[512,128]{1,0:T(8,128)(2,1)S(1)}, bf16[512,128]{1,0:T(8,128)(2,1)S(1)}, u32[]{:S(2)}, u32[]{:S(2)}) collective-permute-start(bf16[512,128]{1,0:T(8,128)(2,1)S(1)} %get-tuple-element.52), channel_id=1, source_target_pairs={{0,2},{2,0},{4,6},{6,4},{8,10},{10,8},{12,14},{14,12},{16,18},{18,... | collective-permute-start | bytes 393224 | tf_op jit(solution)/shard_map/ppermute | solution.py:397
  39.5 1.6 %collective-permute-start.16 = (bf16[64,2048]{1,0:T(8,128)(2,1)S(1)}, bf16[64,2048]{1,0:T(8,128)(2,1)S(1)}, u32[]{:S(2)}, u32[]{:S(2)}) collective-permute-start(bf16[64,2048]{1,0:T(8,128)(2,1)S(1)} %get-tuple-element.66), channel_id=1, source_target_pairs={{0,1},{1,0},{2,3},{3,2},{4,5},{5,4},{6,7},{7,6},{8,9},{9,8},{10,11... | collective-permute-start | bytes 786440 | tf_op jit(solution)/shard_map/ppermute | solution.py:521

commit v22 on v21

--- a/solution.py
+++ b/solution.py
@@ -42,7 +42,7 @@
 
 
 def line_order(groups):
-    return [groups // 2] + [step for step in range(1, groups) if step != groups // 2] + [0]
+    return [*range(1, groups), 0]
 
 
 def shaped(shape, dtype):

time: 42 us -> 42.2 us (level)
  waiting for transfers between devices: 5.23 us -> 5.68 us
    ppermute x15, waiting for transfers between devices: 3.71 us -> 4.16 us  [swapped(): out[step] = lax.ppermute(values[step], 'ctx', pairs_of(step))]
  transfers between devices with their start and end apart: 17 -> 17, of which waited for: 4 -> 3; matrix products, arithmetic and copies ran while one was open for 0% -> 0% of each run, Pallas kernels for 19% -> 19%
where the time goes in v22:
time: 42.2 us; the launch traced here: 42 us
  starting transfers between devices  21 us (50%)
  Pallas kernels  13.2 us (31%)
  waiting for transfers between devices  5.68 us (13%)
  other arithmetic  0.77 us (2%)
  between operations  0.77 us (2%)
  local copies, waits for them, and re-layouts  0.66 us (2%)
    ppermute x15, starting transfers between devices, swapped(): out[step] = lax.ppermute(values[step], 'ctx', pairs_of(step))  20.4 us
    pallas_call x7, Pallas kernels, call(): pl.pallas_call(kernel, out_shape=out_shape, in_specs=in_specs or [vmem] *...  13.2 us
    ppermute x15, waiting for transfers between devices, swapped(): out[step] = lax.ppermute(values[step], 'ctx', pairs_of(step))  4.16 us
    ppermute x1, waiting for transfers between devices, body(): return kept + lax.ppermute(away, 'head', [(0, 1), (1, 0)])  1.52 us
  transfers between devices with their start and end apart: 17, of which 3 were waited for; matrix products, arithmetic and copies ran while one was open for 0% of the time, Pallas kernels for 19%

profile of v22, /device:TPU:0, one launch (start us, length us, event | category | flops | bytes accessed | tf_op | source)
XLA Modules:
  0.0 42.0 jit_solution(4236350276510415940)
XLA Ops:
  0.0 0.5 %collective-permute-start = (bf16[64,2048]{1,0:T(8,128)(2,1)}, bf16[64,2048]{1,0:T(8,128)(2,1)S(1)}, u32[]{:S(2)}, u32[]{:S(2)}) collective-permute-start(bf16[64,2048]{1,0:T(8,128)(2,1)} %mine_hbm.1), channel_id=1, source_target_pairs={{0,1},{1,0},{2,3},{3,2},{4,5},{5,4},{6,7},{7,6},{8,9},{9,8},{10,11... | collective-permute-start | bytes 786440 | tf_op jit(solution)/shard_map/ppermute | solution.py:383
  1.1 1.4 %shard_map.109 = (bf16[2048,256]{1,0:T(8,128)(2,1)S(1)}, bf16[1,2048]{1,0:T(2,128)(2,1)S(1)}, f32[1,128]{1,0:T(1,128)S(1)}, f32[1,128]{1,0:T(1,128)S(1)}, bf16[64,2048]{1,0:T(8,128)(2,1)S(1)}) custom-call(bf16[2048,128]{1,0:T(8,128)(2,1)} %key_hbm.1, bf16[2048,128]{1,0:T(8,128)(2,1)} %dir_hbm.1, bf16[1,2048]{1,0:T(2,128)(2,1)} %rate_hbm.1, ...), custom_call_target="tpu_custom_call" | custom-call | bytes 3145728 | tf_op jit(solution)/shard_map/pallas_call | solution.py:21
  2.5 2.4 %shard_map.110 = (bf16[128,2048]{1,0:T(8,128)(2,1)S(1)}, f32[128,128]{1,0:T(8,128)S(1)}, bf16[128,128]{1,0:T(8,128)(2,1)S(1)}, f32[128,128]{1,0:T(8,128)S(1)}, f...) custom-call(s32[1]{0:T(128)} %bitcast.1.core_ref, ...), custom_call_target="tpu_custom_call" | custom-call | flops 201326592 | bytes 2097152 | tf_op jit(solution)/shard_map/pallas_call | solution.py:21
  4.9 3.5 %collective-permute-start.1 = (f32[128,128]{1,0:T(8,128)S(1)}, f32[128,128]{1,0:T(8,128)S(1)}, u32[]{:S(2)}, u32[]{:S(2)}) collective-permute-start(f32[128,128]{1,0:T(8,128)S(1)} %get-tuple-element.41.refs_3_), channel_id=1, source_target_pairs={{0,6},{2,4},{4,2},{6,0},{8,14},{10,12},{12,10},{14,8},{16,22},{18,... | collective-permute-start | bytes 196616 | tf_op jit(solution)/shard_map/ppermute | solution.py:397
  8.4 0.5 %collective-permute-start.2 = (f32[128,128]{1,0:T(8,128)S(1)}, f32[128,128]{1,0:T(8,128)S(1)}, u32[]{:S(2)}, u32[]{:S(2)}) collective-permute-start(f32[128,128]{1,0:T(8,128)S(1)} %get-tuple-element.41.refs_3_), channel_id=1, source_target_pairs={{0,4},{2,6},{4,0},{6,2},{8,12},{10,14},{12,8},{14,10},{16,20},{18,... | collective-permute-start | bytes 196616 | tf_op jit(solution)/shard_map/ppermute | solution.py:397
  9.1 4.0 %collective-permute-start.4 = (bf16[128,128]{1,0:T(8,128)(2,1)S(1)}, bf16[128,128]{1,0:T(8,128)(2,1)S(1)}, u32[]{:S(2)}, u32[]{:S(2)}) collective-permute-start(bf16[128,128]{1,0:T(8,128)(2,1)S(1)} %get-tuple-element.43.refs_3_.val_ref), channel_id=1, source_target_pairs={{0,24},{2,26},{4,28},{6,30},{8,16},{10,18},{12,20},{14,22},{16,8},... | collective-permute-start | bytes 98312 | tf_op jit(solution)/shard_map/ppermute | solution.py:397
  13.1 0.6 %collective-permute-start.6 = (bf16[128,128]{1,0:T(8,128)(2,1)S(1)}, bf16[128,128]{1,0:T(8,128)(2,1)S(1)}, u32[]{:S(2)}, u32[]{:S(2)}) collective-permute-start(bf16[128,128]{1,0:T(8,128)(2,1)S(1)} %get-tuple-element.43.refs_3_.val_ref), channel_id=1, source_target_pairs={{0,8},{2,10},{4,12},{6,14},{8,0},{10,2},{12,4},{14,6},{16,24},{18,... | collective-permute-start | bytes 98312 | tf_op jit(solution)/shard_map/ppermute | solution.py:397
  13.7 0.5 %shard_map.111 = (bf16[512,128]{1,0:T(8,128)(2,1)S(1)}, f32[4,128,128]{2,1,0:T(8,128)S(1)}, bf16[128,128]{1,0:T(8,128)(2,1)S(1)}, bf16[128,128]{1,0:T(8,128)(2,1...) custom-call(s32[1]{0:T(128)} %bitcast.place_ref, f32[128,128]{1,0:T(8,128)S(1)} %get-tuple-element.40.exit_ref, ...), custom_call_target="tpu_custom_call" | custom-call | flops 100663296 | bytes 1000000 | tf_op jit(solution)/shard_map/pallas_call | solution.py:21
  14.2 1.5 %collective-permute-start.7 = (bf16[512,128]{1,0:T(8,128)(2,1)S(1)}, bf16[512,128]{1,0:T(8,128)(2,1)S(1)}, u32[]{:S(2)}, u32[]{:S(2)}) collective-permute-start(bf16[512,128]{1,0:T(8,128)(2,1)S(1)} %get-tuple-element.45.refs_3_), channel_id=1, source_target_pairs={{0,8},{2,10},{4,12},{6,14},{8,0},{10,2},{12,4},{14,6},{16,24},{18,... | collective-permute-start | bytes 393224 | tf_op jit(solution)/shard_map/ppermute | solution.py:397
  15.7 2.9 %collective-permute-start.8 = (bf16[512,128]{1,0:T(8,128)(2,1)S(1)}, bf16[512,128]{1,0:T(8,128)(2,1)S(1)}, u32[]{:S(2)}, u32[]{:S(2)}) collective-permute-start(bf16[512,128]{1,0:T(8,128)(2,1)S(1)} %get-tuple-element.45.refs_3_), channel_id=1, source_target_pairs={{0,16},{2,18},{4,20},{6,22},{8,24},{10,26},{12,28},{14,30},{16,0},... | collective-permute-start | bytes 393224 | tf_op jit(solution)/shard_map/ppermute | solution.py:397
  18.8 0.7 %copy-done.1 = s32[1,16]{1,0:T(1,128)S(1)} copy-done((s32[1,16]{1,0:T(1,128)S(1)}, s32[1,16]{1,0:T(1,128)}, u32[]{:S(2)}) %copy-start.1) | copy-done | bytes 88
  19.5 1.3 %shard_map.112 = (bf16[512,128]{1,0:T(8,128)(2,1)S(1)}, s32[1]{0:T(128)}) custom-call(s32[1]{0:T(128)} %bitcast.place_ref, s32[16]{0:T(128)S(1)} %bitcast.5, f32[4,128,128]{2,1,0:T(8,128)S(1)} %get-tuple-element.42.after_ref.refs_4_, bf16[128,128]{1,0:T(8,128)(2,1)S(1)} %collective-permute-done.4.refs_0_, ...), custom_call_target="tpu_custom_call" | custom-call | bytes 1000000 | tf_op jit(solution)/shard_map/pallas_call | solution.py:21
  20.8 2.6 %collective-permute-start.13 = (bf16[512,128]{1,0:T(8,128)(2,1)S(1)}, bf16[512,128]{1,0:T(8,128)(2,1)S(1)}, u32[]{:S(2)}, u32[]{:S(2)}) collective-permute-start(bf16[512,128]{1,0:T(8,128)(2,1)S(1)} %get-tuple-element.54.refs_7_), channel_id=1, source_target_pairs={{0,6},{2,4},{4,2},{6,0},{8,14},{10,12},{12,10},{14,8},{16,22},{18,... | collective-permute-start | bytes 393224 | tf_op jit(solution)/shard_map/ppermute | solution.py:397
  23.4 0.5 %collective-permute-start.14 = (bf16[512,128]{1,0:T(8,128)(2,1)S(1)}, bf16[512,128]{1,0:T(8,128)(2,1)S(1)}, u32[]{:S(2)}, u32[]{:S(2)}) collective-permute-start(bf16[512,128]{1,0:T(8,128)(2,1)S(1)} %get-tuple-element.54.refs_7_), channel_id=1, source_target_pairs={{0,4},{2,6},{4,0},{6,2},{8,12},{10,14},{12,8},{14,10},{16,20},{18,... | collective-permute-start | bytes 393224 | tf_op jit(solution)/shard_map/ppermute | solution.py:397
  23.9 0.5 %collective-permute-start.15 = (bf16[512,128]{1,0:T(8,128)(2,1)S(1)}, bf16[512,128]{1,0:T(8,128)(2,1)S(1)}, u32[]{:S(2)}, u32[]{:S(2)}) collective-permute-start(bf16[512,128]{1,0:T(8,128)(2,1)S(1)} %get-tuple-element.54.refs_7_), channel_id=1, source_target_pairs={{0,2},{2,0},{4,6},{6,4},{8,10},{10,8},{12,14},{14,12},{16,18},{18,... | collective-permute-start | bytes 393224 | tf_op jit(solution)/shard_map/ppermute | solution.py:397
  24.4 3.5 %collective-permute-done.8.refs_1_ = bf16[512,128]{1,0:T(8,128)(2,1)S(1)} collective-permute-done((bf16[512,128]{1,0:T(8,128)(2,1)S(1)}, bf16[512,128]{1,0:T(8,128)(2,1)S(1)}, u32[]{:S(2)}, u32[]{:S(2)}) %collective-permute-start.8) | collective-permute-done | bytes 131104 | tf_op jit(solution)/shard_map/ppermute | solution.py:397
  27.9 0.7 %shard_map.113 = (bf16[512,128]{1,0:T(8,128)(2,1)S(1)}, bf16[512,128]{1,0:T(8,128)(2,1)S(1)}, bf16[512,128]{1,0:T(8,128)(2,1)S(1)}, bf16[512,128]{1,0:T(8,128)(2,1)S(1)}) custom-call(s32[1]{0:T(128)} %bitcast.place_ref, bf16[512,128]{1,0:T(8,128)(2,1)S(1)} %collective-permute-done.7.refs_0_, bf16[512,128]{1,0:T(8,128)(2,1)S(1)} %collective-permute-done.8.refs_1_, ...), custom_call_target="tpu_custom_call" | custom-call | flops 201326592 | bytes 1000000 | tf_op jit(solution)/shard_map/pallas_call | solution.py:21
  28.6 2.5 %collective-permute-start.10 = (bf16[512,128]{1,0:T(8,128)(2,1)S(1)}, bf16[512,128]{1,0:T(8,128)(2,1)S(1)}, u32[]{:S(2)}, u32[]{:S(2)}) collective-permute-start(bf16[512,128]{1,0:T(8,128)(2,1)S(1)} %get-tuple-element.50), channel_id=1, source_target_pairs={{0,6},{2,4},{4,2},{6,0},{8,14},{10,12},{12,10},{14,8},{16,22},{18,... | collective-permute-start | bytes 393224 | tf_op jit(solution)/shard_map/ppermute | solution.py:397
  31.1 0.7 %collective-permute-start.11 = (bf16[512,128]{1,0:T(8,128)(2,1)S(1)}, bf16[512,128]{1,0:T(8,128)(2,1)S(1)}, u32[]{:S(2)}, u32[]{:S(2)}) collective-permute-start(bf16[512,128]{1,0:T(8,128)(2,1)S(1)} %get-tuple-element.51), channel_id=1, source_target_pairs={{0,4},{2,6},{4,0},{6,2},{8,12},{10,14},{12,8},{14,10},{16,20},{18,... | collective-permute-start | bytes 393224 | tf_op jit(solution)/shard_map/ppermute | solution.py:397
  32.1 3.9 %shard_map.114 = (bf16[8,128,128]{2,1,0:T(8,128)(2,1)S(1)}, f32[8,128,128]{2,1,0:T(8,128)S(1)}, f32[8,128,1]{2,1,0:T(8,128)S(1)}, f32[8,128,1]{2,1,0:T(8,128)S(1)}) custom-call(bf16[128,2048]{1,0:T(8,128)(2,1)S(1)} %get-tuple-element.55.rows_ref, bf16[2048,1024]{1,0:T(8,128)(2,1)} %weight_hbm.1, f32[1,128]{1,0:T(1,128)S(1)} %get-tuple-element.56.gain_ref, ...), custom_call_target="tpu_custom_call" | custom-call | flops 1073741824 | bytes 16777216 | tf_op jit(solution)/shard_map/pallas_call | solution.py:21
  36.1 0.6 %collective-permute-done.12.refs_2_ = bf16[512,128]{1,0:T(8,128)(2,1)S(1)} collective-permute-done((bf16[512,128]{1,0:T(8,128)(2,1)S(1)}, bf16[512,128]{1,0:T(8,128)(2,1)S(1)}, u32[]{:S(2)}, u32[]{:S(2)}) %collective-permute-start.12) | collective-permute-done | bytes 131104 | tf_op jit(solution)/shard_map/ppermute | solution.py:397
  36.8 2.9 %shard_map.115 = (bf16[64,2048]{1,0:T(8,128)(2,1)S(1)}, bf16[64,2048]{1,0:T(8,128)(2,1)S(1)}) custom-call(s32[1]{0:T(128)} %bitcast.place_ref, s32[1]{0:T(128)} %bitcast.1.core_ref, s32[1]{0:T(128)} %get-tuple-element.44.table_ref, bf16[512,128]{1,0:T(8,128)(2,1)S(1)} %collective-permute-done.10.refs_0_, ...), custom_call_target="tpu_custom_call" | custom-call | flops 536870912 | bytes 4000000 | tf_op jit(solution)/shard_map/pallas_call | solution.py:21
  39.7 1.5 %collective-permute-done.16 = bf16[64,2048]{1,0:T(8,128)(2,1)S(1)} collective-permute-done((bf16[64,2048]{1,0:T(8,128)(2,1)S(1)}, bf16[64,2048]{1,0:T(8,128)(2,1)S(1)}, u32[]{:S(2)}, u32[]{:S(2)}) %collective-permute-start.16) | collective-permute-done | bytes 262176 | tf_op jit(solution)/shard_map/ppermute | solution.py:521
  41.3 0.8 %add.3 = bf16[64,2048]{1,0:T(8,128)(2,1)} add(bf16[64,2048]{1,0:T(8,128)(2,1)S(1)} %get-tuple-element.65, bf16[64,2048]{1,0:T(8,128)(2,1)S(1)} %collective-permute-done.16) | non-fusion elementwise | flops 131072 | bytes 786432 | tf_op jit(solution)/shard_map/add | solution.py:521
  (22 shorter events, 0.8 us)
Async XLA Ops:
  0.0 2.5 %collective-permute-start = (bf16[64,2048]{1,0:T(8,128)(2,1)}, bf16[64,2048]{1,0:T(8,128)(2,1)S(1)}, u32[]{:S(2)}, u32[]{:S(2)}) collective-permute-start(bf16[64,2048]{1,0:T(8,128)(2,1)} %mine_hbm.1), channel_id=1, source_target_pairs={{0,1},{1,0},{2,3},{3,2},{4,5},{5,4},{6,7},{7,6},{8,9},{9,8},{10,11... | collective-permute-start | bytes 786440 | tf_op jit(solution)/shard_map/ppermute | solution.py:383
  4.9 8.2 %collective-permute-start.1 = (f32[128,128]{1,0:T(8,128)S(1)}, f32[128,128]{1,0:T(8,128)S(1)}, u32[]{:S(2)}, u32[]{:S(2)}) collective-permute-start(f32[128,128]{1,0:T(8,128)S(1)} %get-tuple-element.41.refs_3_), channel_id=1, source_target_pairs={{0,6},{2,4},{4,2},{6,0},{8,14},{10,12},{12,10},{14,8},{16,22},{18,... | collective-permute-start | bytes 196616 | tf_op jit(solution)/shard_map/ppermute | solution.py:397
  8.4 5.2 %collective-permute-start.2 = (f32[128,128]{1,0:T(8,128)S(1)}, f32[128,128]{1,0:T(8,128)S(1)}, u32[]{:S(2)}, u32[]{:S(2)}) collective-permute-start(f32[128,128]{1,0:T(8,128)S(1)} %get-tuple-element.41.refs_3_), channel_id=1, source_target_pairs={{0,4},{2,6},{4,0},{6,2},{8,12},{10,14},{12,8},{14,10},{16,20},{18,... | collective-permute-start | bytes 196616 | tf_op jit(solution)/shard_map/ppermute | solution.py:397
  8.9 4.7 %collective-permute-start.3 = (f32[128,128]{1,0:T(8,128)S(1)}, f32[128,128]{1,0:T(8,128)S(1)}, u32[]{:S(2)}, u32[]{:S(2)}) collective-permute-start(f32[128,128]{1,0:T(8,128)S(1)} %get-tuple-element.41.refs_3_), channel_id=1, source_target_pairs={{0,2},{2,0},{4,6},{6,4},{8,10},{10,8},{12,14},{14,12},{16,18},{18,... | collective-permute-start | bytes 196616 | tf_op jit(solution)/shard_map/ppermute | solution.py:397
  9.1 9.6 %collective-permute-start.4 = (bf16[128,128]{1,0:T(8,128)(2,1)S(1)}, bf16[128,128]{1,0:T(8,128)(2,1)S(1)}, u32[]{:S(2)}, u32[]{:S(2)}) collective-permute-start(bf16[128,128]{1,0:T(8,128)(2,1)S(1)} %get-tuple-element.43.refs_3_.val_ref), channel_id=1, source_target_pairs={{0,24},{2,26},{4,28},{6,30},{8,16},{10,18},{12,20},{14,22},{16,8},... | collective-permute-start | bytes 98312 | tf_op jit(solution)/shard_map/ppermute | solution.py:397
  13.1 5.7 %collective-permute-start.5 = (bf16[128,128]{1,0:T(8,128)(2,1)S(1)}, bf16[128,128]{1,0:T(8,128)(2,1)S(1)}, u32[]{:S(2)}, u32[]{:S(2)}) collective-permute-start(bf16[128,128]{1,0:T(8,128)(2,1)S(1)} %get-tuple-element.43.refs_3_.val_ref), channel_id=1, source_target_pairs={{0,16},{2,18},{4,20},{6,22},{8,24},{10,26},{12,28},{14,30},{16,0},... | collective-permute-start | bytes 98312 | tf_op jit(solution)/shard_map/ppermute | solution.py:397
  13.1 5.7 %collective-permute-start.6 = (bf16[128,128]{1,0:T(8,128)(2,1)S(1)}, bf16[128,128]{1,0:T(8,128)(2,1)S(1)}, u32[]{:S(2)}, u32[]{:S(2)}) collective-permute-start(bf16[128,128]{1,0:T(8,128)(2,1)S(1)} %get-tuple-element.43.refs_3_.val_ref), channel_id=1, source_target_pairs={{0,8},{2,10},{4,12},{6,14},{8,0},{10,2},{12,4},{14,6},{16,24},{18,... | collective-permute-start | bytes 98312 | tf_op jit(solution)/shard_map/ppermute | solution.py:397
  13.7 23.1 %copy-start = (bf16[1024,2048]{1,0:T(8,128)(2,1)S(1)}, bf16[1024,2048]{1,0:T(8,128)(2,1)}, u32[]{:S(2)}) copy-start(bf16[1024,2048]{1,0:T(8,128)(2,1)} %refs_12_.1) | copy-start | bytes 12582916
  14.2 9.7 %collective-permute-start.7 = (bf16[512,128]{1,0:T(8,128)(2,1)S(1)}, bf16[512,128]{1,0:T(8,128)(2,1)S(1)}, u32[]{:S(2)}, u32[]{:S(2)}) collective-permute-start(bf16[512,128]{1,0:T(8,128)(2,1)S(1)} %get-tuple-element.45.refs_3_), channel_id=1, source_target_pairs={{0,8},{2,10},{4,12},{6,14},{8,0},{10,2},{12,4},{14,6},{16,24},{18,... | collective-permute-start | bytes 393224 | tf_op jit(solution)/shard_map/ppermute | solution.py:397
  15.7 12.1 %collective-permute-start.8 = (bf16[512,128]{1,0:T(8,128)(2,1)S(1)}, bf16[512,128]{1,0:T(8,128)(2,1)S(1)}, u32[]{:S(2)}, u32[]{:S(2)}) collective-permute-start(bf16[512,128]{1,0:T(8,128)(2,1)S(1)} %get-tuple-element.45.refs_3_), channel_id=1, source_target_pairs={{0,16},{2,18},{4,20},{6,22},{8,24},{10,26},{12,28},{14,30},{16,0},... | collective-permute-start | bytes 393224 | tf_op jit(solution)/shard_map/ppermute | solution.py:397
  18.6 9.2 %collective-permute-start.9 = (bf16[512,128]{1,0:T(8,128)(2,1)S(1)}, bf16[512,128]{1,0:T(8,128)(2,1)S(1)}, u32[]{:S(2)}, u32[]{:S(2)}) collective-permute-start(bf16[512,128]{1,0:T(8,128)(2,1)S(1)} %get-tuple-element.45.refs_3_), channel_id=1, source_target_pairs={{0,24},{2,26},{4,28},{6,30},{8,16},{10,18},{12,20},{14,22},{16,8},... | collective-permute-start | bytes 393224 | tf_op jit(solution)/shard_map/ppermute | solution.py:397
  18.8 0.7 %copy-start.1 = (s32[1,16]{1,0:T(1,128)S(1)}, s32[1,16]{1,0:T(1,128)}, u32[]{:S(2)}) copy-start(s32[1,16]{1,0:T(1,128)} %param.21) | copy-start | bytes 196
  20.8 11.0 %collective-permute-start.13 = (bf16[512,128]{1,0:T(8,128)(2,1)S(1)}, bf16[512,128]{1,0:T(8,128)(2,1)S(1)}, u32[]{:S(2)}, u32[]{:S(2)}) collective-permute-start(bf16[512,128]{1,0:T(8,128)(2,1)S(1)} %get-tuple-element.54.refs_7_), channel_id=1, source_target_pairs={{0,6},{2,4},{4,2},{6,0},{8,14},{10,12},{12,10},{14,8},{16,22},{18,... | collective-permute-start | bytes 393224 | tf_op jit(solution)/shard_map/ppermute | solution.py:397
  23.4 12.7 %collective-permute-start.14 = (bf16[512,128]{1,0:T(8,128)(2,1)S(1)}, bf16[512,128]{1,0:T(8,128)(2,1)S(1)}, u32[]{:S(2)}, u32[]{:S(2)}) collective-permute-start(bf16[512,128]{1,0:T(8,128)(2,1)S(1)} %get-tuple-element.54.refs_7_), channel_id=1, source_target_pairs={{0,4},{2,6},{4,0},{6,2},{8,12},{10,14},{12,8},{14,10},{16,20},{18,... | collective-permute-start | bytes 393224 | tf_op jit(solution)/shard_map/ppermute | solution.py:397
  23.9 12.2 %collective-permute-start.15 = (bf16[512,128]{1,0:T(8,128)(2,1)S(1)}, bf16[512,128]{1,0:T(8,128)(2,1)S(1)}, u32[]{:S(2)}, u32[]{:S(2)}) collective-permute-start(bf16[512,128]{1,0:T(8,128)(2,1)S(1)} %get-tuple-element.54.refs_7_), channel_id=1, source_target_pairs={{0,2},{2,0},{4,6},{6,4},{8,10},{10,8},{12,14},{14,12},{16,18},{18,... | collective-permute-start | bytes 393224 | tf_op jit(solution)/shard_map/ppermute | solution.py:397
  28.6 7.5 %collective-permute-start.10 = (bf16[512,128]{1,0:T(8,128)(2,1)S(1)}, bf16[512,128]{1,0:T(8,128)(2,1)S(1)}, u32[]{:S(2)}, u32[]{:S(2)}) collective-permute-start(bf16[512,128]{1,0:T(8,128)(2,1)S(1)} %get-tuple-element.50), channel_id=1, source_target_pairs={{0,6},{2,4},{4,2},{6,0},{8,14},{10,12},{12,10},{14,8},{16,22},{18,... | collective-permute-start | bytes 393224 | tf_op jit(solution)/shard_map/ppermute | solution.py:397
  31.1 5.0 %collective-permute-start.11 = (bf16[512,128]{1,0:T(8,128)(2,1)S(1)}, bf16[512,128]{1,0:T(8,128)(2,1)S(1)}, u32[]{:S(2)}, u32[]{:S(2)}) collective-permute-start(bf16[512,128]{1,0:T(8,128)(2,1)S(1)} %get-tuple-element.51), channel_id=1, source_target_pairs={{0,4},{2,6},{4,0},{6,2},{8,12},{10,14},{12,8},{14,10},{16,20},{18,... | collective-permute-start | bytes 393224 | tf_op jit(solution)/shard_map/ppermute | solution.py:397
  31.8 5.0 %collective-permute-start.12 = (bf16[512,128]{1,0:T(8,128)(2,1)S(1)}, bf16[512,128]{1,0:T(8,128)(2,1)S(1)}, u32[]{:S(2)}, u32[]{:S(2)}) collective-permute-start(bf16[512,128]{1,0:T(8,128)(2,1)S(1)} %get-tuple-element.52), channel_id=1, source_target_pairs={{0,2},{2,0},{4,6},{6,4},{8,10},{10,8},{12,14},{14,12},{16,18},{18,... | collective-permute-start | bytes 393224 | tf_op jit(solution)/shard_map/ppermute | solution.py:397
  39.7 1.6 %collective-permute-start.16 = (bf16[64,2048]{1,0:T(8,128)(2,1)S(1)}, bf16[64,2048]{1,0:T(8,128)(2,1)S(1)}, u32[]{:S(2)}, u32[]{:S(2)}) collective-permute-start(bf16[64,2048]{1,0:T(8,128)(2,1)S(1)} %get-tuple-element.66), channel_id=1, source_target_pairs={{0,1},{1,0},{2,3},{3,2},{4,5},{5,4},{6,7},{7,6},{8,9},{9,8},{10,11... | collective-permute-start | bytes 786440 | tf_op jit(solution)/shard_map/ppermute | solution.py:521

commit v23 on v21

--- a/solution.py
+++ b/solution.py
@@ -200,9 +200,9 @@
 
     lax.fori_loop(0, segments, pick, jnp.int32(0))
     tokens = val_refs[0].shape[0]
-    for way in range(groups):
+    for ref, way in zip(val_refs, line_order(groups)):
         at = pl.multiple_of(source_of(mine, way, groups) * tokens, tokens)
-        line_ref[pl.ds(at, tokens), :] = val_refs[groups - 1 - way][...]
+        line_ref[pl.ds(at, tokens), :] = ref[...]
 
 
 def query_kernel(rows_ref, weight_hbm, gain_ref, kn_ref, dirs_ref, coeff_ref, solved_ref, val_ref,
@@ -462,7 +462,7 @@
             shaped((groups * tokens, size), BF16),
             shaped((word_of(most - 1, segments)[0] + 1,), jnp.int32),
         ],
-        (place, block_mask[0], starts, *line[::-1]),
+        (place, block_mask[0], starts, *(line[way] for way in line_order(groups))),
         in_specs=[smem, smem, anywhere] + [vmem] * groups,
         out_specs=[vmem, smem],
         moved=10**6,

time: 42 us -> 42.8 us (1.019)
  starting transfers between devices: 21.2 us -> 23.3 us
  waiting for transfers between devices: 5.23 us -> 3.64 us
    ppermute x15, starting transfers between devices: 20.7 us -> 22.8 us  [swapped(): out[step] = lax.ppermute(values[step], 'ctx', pairs_of(step))]
    ppermute x15, waiting for transfers between devices: 3.71 us -> 2.11 us  [swapped(): out[step] = lax.ppermute(values[step], 'ctx', pairs_of(step))]
  transfers between devices with their start and end apart: 17 -> 17, of which waited for: 4 -> 3; matrix products, arithmetic and copies ran while one was open for 0% -> 0% of each run, Pallas kernels for 19% -> 19%
where the time goes in v23:
time: 42.8 us; the launch traced here: 42.4 us
  starting transfers between devices  23.3 us (54%)
  Pallas kernels  13.2 us (31%)
  waiting for transfers between devices  3.64 us (9%)
  other arithmetic  0.77 us (2%)
  between operations  0.77 us (2%)
  local copies, waits for them, and re-layouts  0.66 us (2%)
    ppermute x15, starting transfers between devices, swapped(): out[step] = lax.ppermute(values[step], 'ctx', pairs_of(step))  22.8 us
    pallas_call x7, Pallas kernels, call(): pl.pallas_call(kernel, out_shape=out_shape, in_specs=in_specs or [vmem] *...  13.2 us
    ppermute x15, waiting for transfers between devices, swapped(): out[step] = lax.ppermute(values[step], 'ctx', pairs_of(step))  2.11 us
    ppermute x1, waiting for transfers between devices, body(): return kept + lax.ppermute(away, 'head', [(0, 1), (1, 0)])  1.52 us
  transfers between devices with their start and end apart: 17, of which 3 were waited for; matrix products, arithmetic and copies ran while one was open for 0% of the time, Pallas kernels for 19%

profile of v23, /device:TPU:0, one launch (start us, length us, event | category | flops | bytes accessed | tf_op | source)
XLA Modules:
  0.0 42.4 jit_solution(597140936192408562)
XLA Ops:
  0.0 0.5 %collective-permute-start = (bf16[64,2048]{1,0:T(8,128)(2,1)}, bf16[64,2048]{1,0:T(8,128)(2,1)S(1)}, u32[]{:S(2)}, u32[]{:S(2)}) collective-permute-start(bf16[64,2048]{1,0:T(8,128)(2,1)} %mine_hbm.1), channel_id=1, source_target_pairs={{0,1},{1,0},{2,3},{3,2},{4,5},{5,4},{6,7},{7,6},{8,9},{9,8},{10,11... | collective-permute-start | bytes 786440 | tf_op jit(solution)/shard_map/ppermute | solution.py:383
  1.1 1.4 %shard_map.109 = (bf16[2048,256]{1,0:T(8,128)(2,1)S(1)}, bf16[1,2048]{1,0:T(2,128)(2,1)S(1)}, f32[1,128]{1,0:T(1,128)S(1)}, f32[1,128]{1,0:T(1,128)S(1)}, bf16[64,2048]{1,0:T(8,128)(2,1)S(1)}) custom-call(bf16[2048,128]{1,0:T(8,128)(2,1)} %key_hbm.1, bf16[2048,128]{1,0:T(8,128)(2,1)} %dir_hbm.1, bf16[1,2048]{1,0:T(2,128)(2,1)} %rate_hbm.1, ...), custom_call_target="tpu_custom_call" | custom-call | bytes 3145728 | tf_op jit(solution)/shard_map/pallas_call | solution.py:21
  2.5 2.4 %shard_map.110 = (bf16[128,2048]{1,0:T(8,128)(2,1)S(1)}, f32[128,128]{1,0:T(8,128)S(1)}, bf16[128,128]{1,0:T(8,128)(2,1)S(1)}, f32[128,128]{1,0:T(8,128)S(1)}, f...) custom-call(s32[1]{0:T(128)} %bitcast.1.core_ref, ...), custom_call_target="tpu_custom_call" | custom-call | flops 201326592 | bytes 2097152 | tf_op jit(solution)/shard_map/pallas_call | solution.py:21
  4.9 3.5 %collective-permute-start.1 = (f32[128,128]{1,0:T(8,128)S(1)}, f32[128,128]{1,0:T(8,128)S(1)}, u32[]{:S(2)}, u32[]{:S(2)}) collective-permute-start(f32[128,128]{1,0:T(8,128)S(1)} %get-tuple-element.41.refs_3_), channel_id=1, source_target_pairs={{0,6},{2,4},{4,2},{6,0},{8,14},{10,12},{12,10},{14,8},{16,22},{18,... | collective-permute-start | bytes 196616 | tf_op jit(solution)/shard_map/ppermute | solution.py:397
  8.4 0.5 %collective-permute-start.2 = (f32[128,128]{1,0:T(8,128)S(1)}, f32[128,128]{1,0:T(8,128)S(1)}, u32[]{:S(2)}, u32[]{:S(2)}) collective-permute-start(f32[128,128]{1,0:T(8,128)S(1)} %get-tuple-element.41.refs_3_), channel_id=1, source_target_pairs={{0,4},{2,6},{4,0},{6,2},{8,12},{10,14},{12,8},{14,10},{16,20},{18,... | collective-permute-start | bytes 196616 | tf_op jit(solution)/shard_map/ppermute | solution.py:397
  9.1 3.0 %collective-permute-start.4 = (bf16[128,128]{1,0:T(8,128)(2,1)S(1)}, bf16[128,128]{1,0:T(8,128)(2,1)S(1)}, u32[]{:S(2)}, u32[]{:S(2)}) collective-permute-start(bf16[128,128]{1,0:T(8,128)(2,1)S(1)} %get-tuple-element.43.refs_3_.val_ref), channel_id=1, source_target_pairs={{0,16},{2,18},{4,20},{6,22},{8,24},{10,26},{12,28},{14,30},{16,0},... | collective-permute-start | bytes 98312 | tf_op jit(solution)/shard_map/ppermute | solution.py:397
  12.1 1.6 %collective-permute-start.5 = (bf16[128,128]{1,0:T(8,128)(2,1)S(1)}, bf16[128,128]{1,0:T(8,128)(2,1)S(1)}, u32[]{:S(2)}, u32[]{:S(2)}) collective-permute-start(bf16[128,128]{1,0:T(8,128)(2,1)S(1)} %get-tuple-element.43.refs_3_.val_ref), channel_id=1, source_target_pairs={{0,8},{2,10},{4,12},{6,14},{8,0},{10,2},{12,4},{14,6},{16,24},{18,... | collective-permute-start | bytes 98312 | tf_op jit(solution)/shard_map/ppermute | solution.py:397
  13.6 1.4 %collective-permute-start.6 = (bf16[128,128]{1,0:T(8,128)(2,1)S(1)}, bf16[128,128]{1,0:T(8,128)(2,1)S(1)}, u32[]{:S(2)}, u32[]{:S(2)}) collective-permute-start(bf16[128,128]{1,0:T(8,128)(2,1)S(1)} %get-tuple-element.43.refs_3_.val_ref), channel_id=1, source_target_pairs={{0,24},{2,26},{4,28},{6,30},{8,16},{10,18},{12,20},{14,22},{16,8},... | collective-permute-start | bytes 98312 | tf_op jit(solution)/shard_map/ppermute | solution.py:397
  15.0 0.5 %shard_map.111 = (bf16[512,128]{1,0:T(8,128)(2,1)S(1)}, f32[4,128,128]{2,1,0:T(8,128)S(1)}, bf16[128,128]{1,0:T(8,128)(2,1)S(1)}, bf16[128,128]{1,0:T(8,128)(2,1...) custom-call(s32[1]{0:T(128)} %bitcast.place_ref, f32[128,128]{1,0:T(8,128)S(1)} %get-tuple-element.40.exit_ref, ...), custom_call_target="tpu_custom_call" | custom-call | flops 100663296 | bytes 1000000 | tf_op jit(solution)/shard_map/pallas_call | solution.py:21
  15.5 0.8 %collective-permute-start.7 = (bf16[512,128]{1,0:T(8,128)(2,1)S(1)}, bf16[512,128]{1,0:T(8,128)(2,1)S(1)}, u32[]{:S(2)}, u32[]{:S(2)}) collective-permute-start(bf16[512,128]{1,0:T(8,128)(2,1)S(1)} %get-tuple-element.45.refs_3_), channel_id=1, source_target_pairs={{0,16},{2,18},{4,20},{6,22},{8,24},{10,26},{12,28},{14,30},{16,0},... | collective-permute-start | bytes 393224 | tf_op jit(solution)/shard_map/ppermute | solution.py:397
  16.4 2.3 %collective-permute-start.8 = (bf16[512,128]{1,0:T(8,128)(2,1)S(1)}, bf16[512,128]{1,0:T(8,128)(2,1)S(1)}, u32[]{:S(2)}, u32[]{:S(2)}) collective-permute-start(bf16[512,128]{1,0:T(8,128)(2,1)S(1)} %get-tuple-element.45.refs_3_), channel_id=1, source_target_pairs={{0,8},{2,10},{4,12},{6,14},{8,0},{10,2},{12,4},{14,6},{16,24},{18,... | collective-permute-start | bytes 393224 | tf_op jit(solution)/shard_map/ppermute | solution.py:397
  18.6 1.4 %collective-permute-start.9 = (bf16[512,128]{1,0:T(8,128)(2,1)S(1)}, bf16[512,128]{1,0:T(8,128)(2,1)S(1)}, u32[]{:S(2)}, u32[]{:S(2)}) collective-permute-start(bf16[512,128]{1,0:T(8,128)(2,1)S(1)} %get-tuple-element.45.refs_3_), channel_id=1, source_target_pairs={{0,24},{2,26},{4,28},{6,30},{8,16},{10,18},{12,20},{14,22},{16,8},... | collective-permute-start | bytes 393224 | tf_op jit(solution)/shard_map/ppermute | solution.py:397
  20.0 0.7 %copy-done.1 = s32[1,16]{1,0:T(1,128)S(1)} copy-done((s32[1,16]{1,0:T(1,128)S(1)}, s32[1,16]{1,0:T(1,128)}, u32[]{:S(2)}) %copy-start.1) | copy-done | bytes 88
  20.6 1.3 %shard_map.112 = (bf16[512,128]{1,0:T(8,128)(2,1)S(1)}, s32[1]{0:T(128)}) custom-call(s32[1]{0:T(128)} %bitcast.place_ref, s32[16]{0:T(128)S(1)} %bitcast.5, f32[4,128,128]{2,1,0:T(8,128)S(1)} %get-tuple-element.42.after_ref.refs_4_, bf16[128,128]{1,0:T(8,128)(2,1)S(1)} %collective-permute-done.4.refs_0_, ...), custom_call_target="tpu_custom_call" | custom-call | bytes 1000000 | tf_op jit(solution)/shard_map/pallas_call | solution.py:21
  22.0 2.9 %collective-permute-start.13 = (bf16[512,128]{1,0:T(8,128)(2,1)S(1)}, bf16[512,128]{1,0:T(8,128)(2,1)S(1)}, u32[]{:S(2)}, u32[]{:S(2)}) collective-permute-start(bf16[512,128]{1,0:T(8,128)(2,1)S(1)} %get-tuple-element.54.refs_7_), channel_id=1, source_target_pairs={{0,6},{2,4},{4,2},{6,0},{8,14},{10,12},{12,10},{14,8},{16,22},{18,... | collective-permute-start | bytes 393224 | tf_op jit(solution)/shard_map/ppermute | solution.py:397
  25.1 1.7 %collective-permute-done.7.refs_0_ = bf16[512,128]{1,0:T(8,128)(2,1)S(1)} collective-permute-done((bf16[512,128]{1,0:T(8,128)(2,1)S(1)}, bf16[512,128]{1,0:T(8,128)(2,1)S(1)}, u32[]{:S(2)}, u32[]{:S(2)}) %collective-permute-start.7) | collective-permute-done | bytes 131104 | tf_op jit(solution)/shard_map/ppermute | solution.py:397
  26.8 1.6 %collective-permute-start.15 = (bf16[512,128]{1,0:T(8,128)(2,1)S(1)}, bf16[512,128]{1,0:T(8,128)(2,1)S(1)}, u32[]{:S(2)}, u32[]{:S(2)}) collective-permute-start(bf16[512,128]{1,0:T(8,128)(2,1)S(1)} %get-tuple-element.54.refs_7_), channel_id=1, source_target_pairs={{0,2},{2,0},{4,6},{6,4},{8,10},{10,8},{12,14},{14,12},{16,18},{18,... | collective-permute-start | bytes 393224 | tf_op jit(solution)/shard_map/ppermute | solution.py:397
  28.4 0.7 %shard_map.113 = (bf16[512,128]{1,0:T(8,128)(2,1)S(1)}, bf16[512,128]{1,0:T(8,128)(2,1)S(1)}, bf16[512,128]{1,0:T(8,128)(2,1)S(1)}, bf16[512,128]{1,0:T(8,128)(2,1)S(1)}) custom-call(s32[1]{0:T(128)} %bitcast.place_ref, bf16[512,128]{1,0:T(8,128)(2,1)S(1)} %collective-permute-done.7.refs_0_, bf16[512,128]{1,0:T(8,128)(2,1)S(1)} %collective-permute-done.8.refs_1_, ...), custom_call_target="tpu_custom_call" | custom-call | flops 201326592 | bytes 1000000 | tf_op jit(solution)/shard_map/pallas_call | solution.py:21
  29.2 1.6 %collective-permute-start.10 = (bf16[512,128]{1,0:T(8,128)(2,1)S(1)}, bf16[512,128]{1,0:T(8,128)(2,1)S(1)}, u32[]{:S(2)}, u32[]{:S(2)}) collective-permute-start(bf16[512,128]{1,0:T(8,128)(2,1)S(1)} %get-tuple-element.50), channel_id=1, source_target_pairs={{0,6},{2,4},{4,2},{6,0},{8,14},{10,12},{12,10},{14,8},{16,22},{18,... | collective-permute-start | bytes 393224 | tf_op jit(solution)/shard_map/ppermute | solution.py:397
  31.1 1.6 %collective-permute-start.12 = (bf16[512,128]{1,0:T(8,128)(2,1)S(1)}, bf16[512,128]{1,0:T(8,128)(2,1)S(1)}, u32[]{:S(2)}, u32[]{:S(2)}) collective-permute-start(bf16[512,128]{1,0:T(8,128)(2,1)S(1)} %get-tuple-element.52), channel_id=1, source_target_pairs={{0,2},{2,0},{4,6},{6,4},{8,10},{10,8},{12,14},{14,12},{16,18},{18,... | collective-permute-start | bytes 393224 | tf_op jit(solution)/shard_map/ppermute | solution.py:397
  32.7 3.9 %shard_map.114 = (bf16[8,128,128]{2,1,0:T(8,128)(2,1)S(1)}, f32[8,128,128]{2,1,0:T(8,128)S(1)}, f32[8,128,1]{2,1,0:T(8,128)S(1)}, f32[8,128,1]{2,1,0:T(8,128)S(1)}) custom-call(bf16[128,2048]{1,0:T(8,128)(2,1)S(1)} %get-tuple-element.55.rows_ref, bf16[2048,1024]{1,0:T(8,128)(2,1)} %weight_hbm.1, f32[1,128]{1,0:T(1,128)S(1)} %get-tuple-element.56.gain_ref, ...), custom_call_target="tpu_custom_call" | custom-call | flops 1073741824 | bytes 16777216 | tf_op jit(solution)/shard_map/pallas_call | solution.py:21
  37.1 2.9 %shard_map.115 = (bf16[64,2048]{1,0:T(8,128)(2,1)S(1)}, bf16[64,2048]{1,0:T(8,128)(2,1)S(1)}) custom-call(s32[1]{0:T(128)} %bitcast.place_ref, s32[1]{0:T(128)} %bitcast.1.core_ref, s32[1]{0:T(128)} %get-tuple-element.44.table_ref, bf16[512,128]{1,0:T(8,128)(2,1)S(1)} %collective-permute-done.10.refs_0_, ...), custom_call_target="tpu_custom_call" | custom-call | flops 536870912 | bytes 4000000 | tf_op jit(solution)/shard_map/pallas_call | solution.py:21
  40.1 1.5 %collective-permute-done.16 = bf16[64,2048]{1,0:T(8,128)(2,1)S(1)} collective-permute-done((bf16[64,2048]{1,0:T(8,128)(2,1)S(1)}, bf16[64,2048]{1,0:T(8,128)(2,1)S(1)}, u32[]{:S(2)}, u32[]{:S(2)}) %collective-permute-start.16) | collective-permute-done | bytes 262176 | tf_op jit(solution)/shard_map/ppermute | solution.py:521
  41.6 0.8 %add.3 = bf16[64,2048]{1,0:T(8,128)(2,1)} add(bf16[64,2048]{1,0:T(8,128)(2,1)S(1)} %get-tuple-element.65, bf16[64,2048]{1,0:T(8,128)(2,1)S(1)} %collective-permute-done.16) | non-fusion elementwise | flops 131072 | bytes 786432 | tf_op jit(solution)/shard_map/add | solution.py:521
  (22 shorter events, 1.2 us)
Async XLA Ops:
  0.0 2.5 %collective-permute-start = (bf16[64,2048]{1,0:T(8,128)(2,1)}, bf16[64,2048]{1,0:T(8,128)(2,1)S(1)}, u32[]{:S(2)}, u32[]{:S(2)}) collective-permute-start(bf16[64,2048]{1,0:T(8,128)(2,1)} %mine_hbm.1), channel_id=1, source_target_pairs={{0,1},{1,0},{2,3},{3,2},{4,5},{5,4},{6,7},{7,6},{8,9},{9,8},{10,11... | collective-permute-start | bytes 786440 | tf_op jit(solution)/shard_map/ppermute | solution.py:383
  4.9 8.7 %collective-permute-start.1 = (f32[128,128]{1,0:T(8,128)S(1)}, f32[128,128]{1,0:T(8,128)S(1)}, u32[]{:S(2)}, u32[]{:S(2)}) collective-permute-start(f32[128,128]{1,0:T(8,128)S(1)} %get-tuple-element.41.refs_3_), channel_id=1, source_target_pairs={{0,6},{2,4},{4,2},{6,0},{8,14},{10,12},{12,10},{14,8},{16,22},{18,... | collective-permute-start | bytes 196616 | tf_op jit(solution)/shard_map/ppermute | solution.py:397
  8.4 6.6 %collective-permute-start.2 = (f32[128,128]{1,0:T(8,128)S(1)}, f32[128,128]{1,0:T(8,128)S(1)}, u32[]{:S(2)}, u32[]{:S(2)}) collective-permute-start(f32[128,128]{1,0:T(8,128)S(1)} %get-tuple-element.41.refs_3_), channel_id=1, source_target_pairs={{0,4},{2,6},{4,0},{6,2},{8,12},{10,14},{12,8},{14,10},{16,20},{18,... | collective-permute-start | bytes 196616 | tf_op jit(solution)/shard_map/ppermute | solution.py:397
  8.9 6.1 %collective-permute-start.3 = (f32[128,128]{1,0:T(8,128)S(1)}, f32[128,128]{1,0:T(8,128)S(1)}, u32[]{:S(2)}, u32[]{:S(2)}) collective-permute-start(f32[128,128]{1,0:T(8,128)S(1)} %get-tuple-element.41.refs_3_), channel_id=1, source_target_pairs={{0,2},{2,0},{4,6},{6,4},{8,10},{10,8},{12,14},{14,12},{16,18},{18,... | collective-permute-start | bytes 196616 | tf_op jit(solution)/shard_map/ppermute | solution.py:397
  9.1 9.6 %collective-permute-start.4 = (bf16[128,128]{1,0:T(8,128)(2,1)S(1)}, bf16[128,128]{1,0:T(8,128)(2,1)S(1)}, u32[]{:S(2)}, u32[]{:S(2)}) collective-permute-start(bf16[128,128]{1,0:T(8,128)(2,1)S(1)} %get-tuple-element.43.refs_3_.val_ref), channel_id=1, source_target_pairs={{0,16},{2,18},{4,20},{6,22},{8,24},{10,26},{12,28},{14,30},{16,0},... | collective-permute-start | bytes 98312 | tf_op jit(solution)/shard_map/ppermute | solution.py:397
  12.1 7.9 %collective-permute-start.5 = (bf16[128,128]{1,0:T(8,128)(2,1)S(1)}, bf16[128,128]{1,0:T(8,128)(2,1)S(1)}, u32[]{:S(2)}, u32[]{:S(2)}) collective-permute-start(bf16[128,128]{1,0:T(8,128)(2,1)S(1)} %get-tuple-element.43.refs_3_.val_ref), channel_id=1, source_target_pairs={{0,8},{2,10},{4,12},{6,14},{8,0},{10,2},{12,4},{14,6},{16,24},{18,... | collective-permute-start | bytes 98312 | tf_op jit(solution)/shard_map/ppermute | solution.py:397
  13.6 6.3 %collective-permute-start.6 = (bf16[128,128]{1,0:T(8,128)(2,1)S(1)}, bf16[128,128]{1,0:T(8,128)(2,1)S(1)}, u32[]{:S(2)}, u32[]{:S(2)}) collective-permute-start(bf16[128,128]{1,0:T(8,128)(2,1)S(1)} %get-tuple-element.43.refs_3_.val_ref), channel_id=1, source_target_pairs={{0,24},{2,26},{4,28},{6,30},{8,16},{10,18},{12,20},{14,22},{16,8},... | collective-permute-start | bytes 98312 | tf_op jit(solution)/shard_map/ppermute | solution.py:397
  15.0 22.1 %copy-start = (bf16[1024,2048]{1,0:T(8,128)(2,1)S(1)}, bf16[1024,2048]{1,0:T(8,128)(2,1)}, u32[]{:S(2)}) copy-start(bf16[1024,2048]{1,0:T(8,128)(2,1)} %refs_12_.1) | copy-start | bytes 12582916
  15.5 11.3 %collective-permute-start.7 = (bf16[512,128]{1,0:T(8,128)(2,1)S(1)}, bf16[512,128]{1,0:T(8,128)(2,1)S(1)}, u32[]{:S(2)}, u32[]{:S(2)}) collective-permute-start(bf16[512,128]{1,0:T(8,128)(2,1)S(1)} %get-tuple-element.45.refs_3_), channel_id=1, source_target_pairs={{0,16},{2,18},{4,20},{6,22},{8,24},{10,26},{12,28},{14,30},{16,0},... | collective-permute-start | bytes 393224 | tf_op jit(solution)/shard_map/ppermute | solution.py:397
  16.4 12.1 %collective-permute-start.8 = (bf16[512,128]{1,0:T(8,128)(2,1)S(1)}, bf16[512,128]{1,0:T(8,128)(2,1)S(1)}, u32[]{:S(2)}, u32[]{:S(2)}) collective-permute-start(bf16[512,128]{1,0:T(8,128)(2,1)S(1)} %get-tuple-element.45.refs_3_), channel_id=1, source_target_pairs={{0,8},{2,10},{4,12},{6,14},{8,0},{10,2},{12,4},{14,6},{16,24},{18,... | collective-permute-start | bytes 393224 | tf_op jit(solution)/shard_map/ppermute | solution.py:397
  18.6 9.8 %collective-permute-start.9 = (bf16[512,128]{1,0:T(8,128)(2,1)S(1)}, bf16[512,128]{1,0:T(8,128)(2,1)S(1)}, u32[]{:S(2)}, u32[]{:S(2)}) collective-permute-start(bf16[512,128]{1,0:T(8,128)(2,1)S(1)} %get-tuple-element.45.refs_3_), channel_id=1, source_target_pairs={{0,24},{2,26},{4,28},{6,30},{8,16},{10,18},{12,20},{14,22},{16,8},... | collective-permute-start | bytes 393224 | tf_op jit(solution)/shard_map/ppermute | solution.py:397
  20.0 0.7 %copy-start.1 = (s32[1,16]{1,0:T(1,128)S(1)}, s32[1,16]{1,0:T(1,128)}, u32[]{:S(2)}) copy-start(s32[1,16]{1,0:T(1,128)} %param.21) | copy-start | bytes 196
  22.0 9.1 %collective-permute-start.13 = (bf16[512,128]{1,0:T(8,128)(2,1)S(1)}, bf16[512,128]{1,0:T(8,128)(2,1)S(1)}, u32[]{:S(2)}, u32[]{:S(2)}) collective-permute-start(bf16[512,128]{1,0:T(8,128)(2,1)S(1)} %get-tuple-element.54.refs_7_), channel_id=1, source_target_pairs={{0,6},{2,4},{4,2},{6,0},{8,14},{10,12},{12,10},{14,8},{16,22},{18,... | collective-permute-start | bytes 393224 | tf_op jit(solution)/shard_map/ppermute | solution.py:397
  24.9 11.8 %collective-permute-start.14 = (bf16[512,128]{1,0:T(8,128)(2,1)S(1)}, bf16[512,128]{1,0:T(8,128)(2,1)S(1)}, u32[]{:S(2)}, u32[]{:S(2)}) collective-permute-start(bf16[512,128]{1,0:T(8,128)(2,1)S(1)} %get-tuple-element.54.refs_7_), channel_id=1, source_target_pairs={{0,4},{2,6},{4,0},{6,2},{8,12},{10,14},{12,8},{14,10},{16,20},{18,... | collective-permute-start | bytes 393224 | tf_op jit(solution)/shard_map/ppermute | solution.py:397
  26.8 9.9 %collective-permute-start.15 = (bf16[512,128]{1,0:T(8,128)(2,1)S(1)}, bf16[512,128]{1,0:T(8,128)(2,1)S(1)}, u32[]{:S(2)}, u32[]{:S(2)}) collective-permute-start(bf16[512,128]{1,0:T(8,128)(2,1)S(1)} %get-tuple-element.54.refs_7_), channel_id=1, source_target_pairs={{0,2},{2,0},{4,6},{6,4},{8,10},{10,8},{12,14},{14,12},{16,18},{18,... | collective-permute-start | bytes 393224 | tf_op jit(solution)/shard_map/ppermute | solution.py:397
  29.2 7.5 %collective-permute-start.10 = (bf16[512,128]{1,0:T(8,128)(2,1)S(1)}, bf16[512,128]{1,0:T(8,128)(2,1)S(1)}, u32[]{:S(2)}, u32[]{:S(2)}) collective-permute-start(bf16[512,128]{1,0:T(8,128)(2,1)S(1)} %get-tuple-element.50), channel_id=1, source_target_pairs={{0,6},{2,4},{4,2},{6,0},{8,14},{10,12},{12,10},{14,8},{16,22},{18,... | collective-permute-start | bytes 393224 | tf_op jit(solution)/shard_map/ppermute | solution.py:397
  30.7 6.4 %collective-permute-start.11 = (bf16[512,128]{1,0:T(8,128)(2,1)S(1)}, bf16[512,128]{1,0:T(8,128)(2,1)S(1)}, u32[]{:S(2)}, u32[]{:S(2)}) collective-permute-start(bf16[512,128]{1,0:T(8,128)(2,1)S(1)} %get-tuple-element.51), channel_id=1, source_target_pairs={{0,4},{2,6},{4,0},{6,2},{8,12},{10,14},{12,8},{14,10},{16,20},{18,... | collective-permute-start | bytes 393224 | tf_op jit(solution)/shard_map/ppermute | solution.py:397
  31.1 6.0 %collective-permute-start.12 = (bf16[512,128]{1,0:T(8,128)(2,1)S(1)}, bf16[512,128]{1,0:T(8,128)(2,1)S(1)}, u32[]{:S(2)}, u32[]{:S(2)}) collective-permute-start(bf16[512,128]{1,0:T(8,128)(2,1)S(1)} %get-tuple-element.52), channel_id=1, source_target_pairs={{0,2},{2,0},{4,6},{6,4},{8,10},{10,8},{12,14},{14,12},{16,18},{18,... | collective-permute-start | bytes 393224 | tf_op jit(solution)/shard_map/ppermute | solution.py:397
  40.0 1.6 %collective-permute-start.16 = (bf16[64,2048]{1,0:T(8,128)(2,1)S(1)}, bf16[64,2048]{1,0:T(8,128)(2,1)S(1)}, u32[]{:S(2)}, u32[]{:S(2)}) collective-permute-start(bf16[64,2048]{1,0:T(8,128)(2,1)S(1)} %get-tuple-element.66), channel_id=1, source_target_pairs={{0,1},{1,0},{2,3},{3,2},{4,5},{5,4},{6,7},{7,6},{8,9},{9,8},{10,11... | collective-permute-start | bytes 786440 | tf_op jit(solution)/shard_map/ppermute | solution.py:521

commit v24 on v17

--- a/solution.py
+++ b/solution.py
@@ -42,7 +42,7 @@
 
 
 def line_order(groups):
-    return [groups // 2] + [step for step in range(groups - 1, 0, -1) if step != groups // 2] + [0]
+    return [groups // 2] + [step for step in range(1, groups) if step != groups // 2] + [0]
 
 
 def shaped(shape, dtype):

time: 42.5 us -> 42 us (0.988)
  transfers between devices with their start and end apart: 17 -> 17, of which waited for: 5 -> 4; matrix products, arithmetic and copies ran while one was open for 0% -> 0% of each run, Pallas kernels for 19% -> 19%
where the time goes in v24:
time: 42 us; the launch traced here: 41.9 us
  starting transfers between devices  21.3 us (51%)
  Pallas kernels  13.2 us (31%)
  waiting for transfers between devices  5.81 us (14%)
  other arithmetic  0.77 us (2%)
  between operations  0.77 us (2%)
    ppermute x15, starting transfers between devices, swapped(): out[step] = lax.ppermute(values[step], 'ctx', pairs_of(step))  20.8 us
    pallas_call x7, Pallas kernels, call(): pl.pallas_call(kernel, out_shape=out_shape, in_specs=in_specs or [vmem] *...  13.2 us
    ppermute x15, waiting for transfers between devices, swapped(): out[step] = lax.ppermute(values[step], 'ctx', pairs_of(step))  4.29 us
    ppermute x1, waiting for transfers between devices, body(): return kept + lax.ppermute(away, 'head', [(0, 1), (1, 0)])  1.52 us
  transfers between devices with their start and end apart: 17, of which 4 were waited for; matrix products, arithmetic and copies ran while one was open for 0% of the time, Pallas kernels for 19%

profile of v24, /device:TPU:0, one launch (start us, length us, event | category | flops | bytes accessed | tf_op | source)
XLA Modules:
  0.0 41.9 jit_solution(9397701768294208655)
XLA Ops:
  0.0 0.5 %collective-permute-start = (bf16[64,2048]{1,0:T(8,128)(2,1)}, bf16[64,2048]{1,0:T(8,128)(2,1)S(1)}, u32[]{:S(2)}, u32[]{:S(2)}) collective-permute-start(bf16[64,2048]{1,0:T(8,128)(2,1)} %mine_hbm.1), channel_id=1, source_target_pairs={{0,1},{1,0},{2,3},{3,2},{4,5},{5,4},{6,7},{7,6},{8,9},{9,8},{10,11... | collective-permute-start | bytes 786440 | tf_op jit(solution)/shard_map/ppermute | solution.py:379
  1.1 1.5 %shard_map.109 = (bf16[2048,384]{1,0:T(8,128)(2,1)S(1)}, bf16[1,2048]{1,0:T(2,128)(2,1)S(1)}, f32[1,128]{1,0:T(1,128)S(1)}, f32[1,128]{1,0:T(1,128)S(1)}, bf16[64,2048]{1,0:T(8,128)(2,1)S(1)}) custom-call(bf16[2048,128]{1,0:T(8,128)(2,1)} %key_hbm.1, bf16[2048,128]{1,0:T(8,128)(2,1)} %dir_hbm.1, bf16[2048,128]{1,0:T(8,128)(2,1)} %value_hbm.1, ...), custom_call_target="tpu_custom_call" | custom-call | bytes 3145728 | tf_op jit(solution)/shard_map/pallas_call | solution.py:21
  2.7 2.3 %shard_map.110 = (bf16[128,2048]{1,0:T(8,128)(2,1)S(1)}, f32[128,128]{1,0:T(8,128)S(1)}, bf16[128,128]{1,0:T(8,128)(2,1)S(1)}, f32[128,128]{1,0:T(8,128)S(1)}, f...) custom-call(s32[1]{0:T(128)} %bitcast.1.core_ref, ...), custom_call_target="tpu_custom_call" | custom-call | flops 201326592 | bytes 2097152 | tf_op jit(solution)/shard_map/pallas_call | solution.py:21
  5.0 3.5 %collective-permute-start.1 = (f32[128,128]{1,0:T(8,128)S(1)}, f32[128,128]{1,0:T(8,128)S(1)}, u32[]{:S(2)}, u32[]{:S(2)}) collective-permute-start(f32[128,128]{1,0:T(8,128)S(1)} %get-tuple-element.41.refs_3_), channel_id=1, source_target_pairs={{0,6},{2,4},{4,2},{6,0},{8,14},{10,12},{12,10},{14,8},{16,22},{18,... | collective-permute-start | bytes 196616 | tf_op jit(solution)/shard_map/ppermute | solution.py:393
  8.5 0.5 %collective-permute-start.2 = (f32[128,128]{1,0:T(8,128)S(1)}, f32[128,128]{1,0:T(8,128)S(1)}, u32[]{:S(2)}, u32[]{:S(2)}) collective-permute-start(f32[128,128]{1,0:T(8,128)S(1)} %get-tuple-element.41.refs_3_), channel_id=1, source_target_pairs={{0,4},{2,6},{4,0},{6,2},{8,12},{10,14},{12,8},{14,10},{16,20},{18,... | collective-permute-start | bytes 196616 | tf_op jit(solution)/shard_map/ppermute | solution.py:393
  9.1 4.0 %collective-permute-start.4 = (bf16[128,128]{1,0:T(8,128)(2,1)S(1)}, bf16[128,128]{1,0:T(8,128)(2,1)S(1)}, u32[]{:S(2)}, u32[]{:S(2)}) collective-permute-start(bf16[128,128]{1,0:T(8,128)(2,1)S(1)} %get-tuple-element.43.refs_3_.val_ref), channel_id=1, source_target_pairs={{0,24},{2,26},{4,28},{6,30},{8,16},{10,18},{12,20},{14,22},{16,8},... | collective-permute-start | bytes 98312 | tf_op jit(solution)/shard_map/ppermute | solution.py:393
  13.2 0.6 %collective-permute-start.6 = (bf16[128,128]{1,0:T(8,128)(2,1)S(1)}, bf16[128,128]{1,0:T(8,128)(2,1)S(1)}, u32[]{:S(2)}, u32[]{:S(2)}) collective-permute-start(bf16[128,128]{1,0:T(8,128)(2,1)S(1)} %get-tuple-element.43.refs_3_.val_ref), channel_id=1, source_target_pairs={{0,8},{2,10},{4,12},{6,14},{8,0},{10,2},{12,4},{14,6},{16,24},{18,... | collective-permute-start | bytes 98312 | tf_op jit(solution)/shard_map/ppermute | solution.py:393
  13.7 0.5 %shard_map.111 = (bf16[512,128]{1,0:T(8,128)(2,1)S(1)}, f32[4,128,128]{2,1,0:T(8,128)S(1)}, bf16[128,128]{1,0:T(8,128)(2,1)S(1)}, bf16[128,128]{1,0:T(8,128)(2,1...) custom-call(s32[1]{0:T(128)} %bitcast.place_ref, f32[128,128]{1,0:T(8,128)S(1)} %get-tuple-element.40.exit_ref, ...), custom_call_target="tpu_custom_call" | custom-call | flops 100663296 | bytes 1000000 | tf_op jit(solution)/shard_map/pallas_call | solution.py:21
  14.2 2.4 %collective-permute-start.7 = (bf16[512,128]{1,0:T(8,128)(2,1)S(1)}, bf16[512,128]{1,0:T(8,128)(2,1)S(1)}, u32[]{:S(2)}, u32[]{:S(2)}) collective-permute-start(bf16[512,128]{1,0:T(8,128)(2,1)S(1)} %get-tuple-element.45.refs_3_), channel_id=1, source_target_pairs={{0,16},{2,18},{4,20},{6,22},{8,24},{10,26},{12,28},{14,30},{16,0},... | collective-permute-start | bytes 393224 | tf_op jit(solution)/shard_map/ppermute | solution.py:393
  16.7 2.0 %collective-permute-start.8 = (bf16[512,128]{1,0:T(8,128)(2,1)S(1)}, bf16[512,128]{1,0:T(8,128)(2,1)S(1)}, u32[]{:S(2)}, u32[]{:S(2)}) collective-permute-start(bf16[512,128]{1,0:T(8,128)(2,1)S(1)} %get-tuple-element.45.refs_3_), channel_id=1, source_target_pairs={{0,8},{2,10},{4,12},{6,14},{8,0},{10,2},{12,4},{14,6},{16,24},{18,... | collective-permute-start | bytes 393224 | tf_op jit(solution)/shard_map/ppermute | solution.py:393
  18.9 0.9 %collective-permute-done.5.refs_1_ = bf16[128,128]{1,0:T(8,128)(2,1)S(1)} collective-permute-done((bf16[128,128]{1,0:T(8,128)(2,1)S(1)}, bf16[128,128]{1,0:T(8,128)(2,1)S(1)}, u32[]{:S(2)}, u32[]{:S(2)}) %collective-permute-start.5) | collective-permute-done | bytes 32800 | tf_op jit(solution)/shard_map/ppermute | solution.py:393
  19.8 1.3 %shard_map.112 = (bf16[512,128]{1,0:T(8,128)(2,1)S(1)}, s32[1]{0:T(128)}) custom-call(s32[1]{0:T(128)} %bitcast.place_ref, s32[16]{0:T(128)S(1)} %bitcast.5, f32[4,128,128]{2,1,0:T(8,128)S(1)} %get-tuple-element.42.after_ref.refs_4_, bf16[128,128]{1,0:T(8,128)(2,1)S(1)} %collective-permute-done.4.refs_0_, ...), custom_call_target="tpu_custom_call" | custom-call | bytes 1000000 | tf_op jit(solution)/shard_map/pallas_call | solution.py:21
  21.1 2.5 %collective-permute-start.13 = (bf16[512,128]{1,0:T(8,128)(2,1)S(1)}, bf16[512,128]{1,0:T(8,128)(2,1)S(1)}, u32[]{:S(2)}, u32[]{:S(2)}) collective-permute-start(bf16[512,128]{1,0:T(8,128)(2,1)S(1)} %get-tuple-element.54.refs_7_), channel_id=1, source_target_pairs={{0,6},{2,4},{4,2},{6,0},{8,14},{10,12},{12,10},{14,8},{16,22},{18,... | collective-permute-start | bytes 393224 | tf_op jit(solution)/shard_map/ppermute | solution.py:393
  23.6 0.4 collective-permute-start.14
  24.0 2.7 %collective-permute-done.7.refs_0_ = bf16[512,128]{1,0:T(8,128)(2,1)S(1)} collective-permute-done((bf16[512,128]{1,0:T(8,128)(2,1)S(1)}, bf16[512,128]{1,0:T(8,128)(2,1)S(1)}, u32[]{:S(2)}, u32[]{:S(2)}) %collective-permute-start.7) | collective-permute-done | bytes 131104 | tf_op jit(solution)/shard_map/ppermute | solution.py:393
  26.8 0.7 %shard_map.113 = (bf16[512,128]{1,0:T(8,128)(2,1)S(1)}, bf16[512,128]{1,0:T(8,128)(2,1)S(1)}, bf16[512,128]{1,0:T(8,128)(2,1)S(1)}, bf16[512,128]{1,0:T(8,128)(2,1)S(1)}) custom-call(s32[1]{0:T(128)} %bitcast.place_ref, bf16[512,128]{1,0:T(8,128)(2,1)S(1)} %collective-permute-done.7.refs_0_, bf16[512,128]{1,0:T(8,128)(2,1)S(1)} %collective-permute-done.8.refs_1_, ...), custom_call_target="tpu_custom_call" | custom-call | flops 201326592 | bytes 1000000 | tf_op jit(solution)/shard_map/pallas_call | solution.py:21
  27.5 2.5 %collective-permute-start.10 = (bf16[512,128]{1,0:T(8,128)(2,1)S(1)}, bf16[512,128]{1,0:T(8,128)(2,1)S(1)}, u32[]{:S(2)}, u32[]{:S(2)}) collective-permute-start(bf16[512,128]{1,0:T(8,128)(2,1)S(1)} %get-tuple-element.50), channel_id=1, source_target_pairs={{0,6},{2,4},{4,2},{6,0},{8,14},{10,12},{12,10},{14,8},{16,22},{18,... | collective-permute-start | bytes 393224 | tf_op jit(solution)/shard_map/ppermute | solution.py:393
  29.9 1.0 %collective-permute-start.11 = (bf16[512,128]{1,0:T(8,128)(2,1)S(1)}, bf16[512,128]{1,0:T(8,128)(2,1)S(1)}, u32[]{:S(2)}, u32[]{:S(2)}) collective-permute-start(bf16[512,128]{1,0:T(8,128)(2,1)S(1)} %get-tuple-element.51), channel_id=1, source_target_pairs={{0,4},{2,6},{4,0},{6,2},{8,12},{10,14},{12,8},{14,10},{16,20},{18,... | collective-permute-start | bytes 393224 | tf_op jit(solution)/shard_map/ppermute | solution.py:393
  31.0 1.0 %collective-permute-start.12 = (bf16[512,128]{1,0:T(8,128)(2,1)S(1)}, bf16[512,128]{1,0:T(8,128)(2,1)S(1)}, u32[]{:S(2)}, u32[]{:S(2)}) collective-permute-start(bf16[512,128]{1,0:T(8,128)(2,1)S(1)} %get-tuple-element.52), channel_id=1, source_target_pairs={{0,2},{2,0},{4,6},{6,4},{8,10},{10,8},{12,14},{14,12},{16,18},{18,... | collective-permute-start | bytes 393224 | tf_op jit(solution)/shard_map/ppermute | solution.py:393
  32.0 3.9 %shard_map.114 = (bf16[8,128,128]{2,1,0:T(8,128)(2,1)S(1)}, f32[8,128,128]{2,1,0:T(8,128)S(1)}, f32[8,128,1]{2,1,0:T(8,128)S(1)}, f32[8,128,1]{2,1,0:T(8,128)S(1)}) custom-call(bf16[128,2048]{1,0:T(8,128)(2,1)S(1)} %get-tuple-element.55.rows_ref, bf16[2048,1024]{1,0:T(8,128)(2,1)} %weight_hbm.1, f32[1,128]{1,0:T(1,128)S(1)} %get-tuple-element.56.gain_ref, ...), custom_call_target="tpu_custom_call" | custom-call | flops 1073741824 | bytes 16777216 | tf_op jit(solution)/shard_map/pallas_call | solution.py:21
  36.0 0.7 %collective-permute-done.12.refs_2_ = bf16[512,128]{1,0:T(8,128)(2,1)S(1)} collective-permute-done((bf16[512,128]{1,0:T(8,128)(2,1)S(1)}, bf16[512,128]{1,0:T(8,128)(2,1)S(1)}, u32[]{:S(2)}, u32[]{:S(2)}) %collective-permute-start.12) | collective-permute-done | bytes 131104 | tf_op jit(solution)/shard_map/ppermute | solution.py:393
  36.6 2.9 %shard_map.115 = (bf16[64,2048]{1,0:T(8,128)(2,1)S(1)}, bf16[64,2048]{1,0:T(8,128)(2,1)S(1)}) custom-call(s32[1]{0:T(128)} %bitcast.place_ref, s32[1]{0:T(128)} %bitcast.1.core_ref, s32[1]{0:T(128)} %get-tuple-element.44.table_ref, bf16[512,128]{1,0:T(8,128)(2,1)S(1)} %collective-permute-done.10.refs_0_, ...), custom_call_target="tpu_custom_call" | custom-call | flops 536870912 | bytes 4000000 | tf_op jit(solution)/shard_map/pallas_call | solution.py:21
  39.6 1.5 %collective-permute-done.16 = bf16[64,2048]{1,0:T(8,128)(2,1)S(1)} collective-permute-done((bf16[64,2048]{1,0:T(8,128)(2,1)S(1)}, bf16[64,2048]{1,0:T(8,128)(2,1)S(1)}, u32[]{:S(2)}, u32[]{:S(2)}) %collective-permute-start.16) | collective-permute-done | bytes 262176 | tf_op jit(solution)/shard_map/ppermute | solution.py:516
  41.1 0.8 %add.3 = bf16[64,2048]{1,0:T(8,128)(2,1)} add(bf16[64,2048]{1,0:T(8,128)(2,1)S(1)} %get-tuple-element.65, bf16[64,2048]{1,0:T(8,128)(2,1)S(1)} %collective-permute-done.16) | non-fusion elementwise | flops 131072 | bytes 786432 | tf_op jit(solution)/shard_map/add | solution.py:516
  (22 shorter events, 0.5 us)
Async XLA Ops:
  0.0 19.8 %copy-start.1 = (s32[1,16]{1,0:T(1,128)S(1)}, s32[1,16]{1,0:T(1,128)}, u32[]{:S(2)}) copy-start(s32[1,16]{1,0:T(1,128)} %param.21) | copy-start | bytes 196
  0.0 2.6 %collective-permute-start = (bf16[64,2048]{1,0:T(8,128)(2,1)}, bf16[64,2048]{1,0:T(8,128)(2,1)S(1)}, u32[]{:S(2)}, u32[]{:S(2)}) collective-permute-start(bf16[64,2048]{1,0:T(8,128)(2,1)} %mine_hbm.1), channel_id=1, source_target_pairs={{0,1},{1,0},{2,3},{3,2},{4,5},{5,4},{6,7},{7,6},{8,9},{9,8},{10,11... | collective-permute-start | bytes 786440 | tf_op jit(solution)/shard_map/ppermute | solution.py:379
  5.0 8.2 %collective-permute-start.1 = (f32[128,128]{1,0:T(8,128)S(1)}, f32[128,128]{1,0:T(8,128)S(1)}, u32[]{:S(2)}, u32[]{:S(2)}) collective-permute-start(f32[128,128]{1,0:T(8,128)S(1)} %get-tuple-element.41.refs_3_), channel_id=1, source_target_pairs={{0,6},{2,4},{4,2},{6,0},{8,14},{10,12},{12,10},{14,8},{16,22},{18,... | collective-permute-start | bytes 196616 | tf_op jit(solution)/shard_map/ppermute | solution.py:393
  8.5 5.2 %collective-permute-start.2 = (f32[128,128]{1,0:T(8,128)S(1)}, f32[128,128]{1,0:T(8,128)S(1)}, u32[]{:S(2)}, u32[]{:S(2)}) collective-permute-start(f32[128,128]{1,0:T(8,128)S(1)} %get-tuple-element.41.refs_3_), channel_id=1, source_target_pairs={{0,4},{2,6},{4,0},{6,2},{8,12},{10,14},{12,8},{14,10},{16,20},{18,... | collective-permute-start | bytes 196616 | tf_op jit(solution)/shard_map/ppermute | solution.py:393
  9.0 4.7 %collective-permute-start.3 = (f32[128,128]{1,0:T(8,128)S(1)}, f32[128,128]{1,0:T(8,128)S(1)}, u32[]{:S(2)}, u32[]{:S(2)}) collective-permute-start(f32[128,128]{1,0:T(8,128)S(1)} %get-tuple-element.41.refs_3_), channel_id=1, source_target_pairs={{0,2},{2,0},{4,6},{6,4},{8,10},{10,8},{12,14},{14,12},{16,18},{18,... | collective-permute-start | bytes 196616 | tf_op jit(solution)/shard_map/ppermute | solution.py:393
  9.1 9.5 %collective-permute-start.4 = (bf16[128,128]{1,0:T(8,128)(2,1)S(1)}, bf16[128,128]{1,0:T(8,128)(2,1)S(1)}, u32[]{:S(2)}, u32[]{:S(2)}) collective-permute-start(bf16[128,128]{1,0:T(8,128)(2,1)S(1)} %get-tuple-element.43.refs_3_.val_ref), channel_id=1, source_target_pairs={{0,24},{2,26},{4,28},{6,30},{8,16},{10,18},{12,20},{14,22},{16,8},... | collective-permute-start | bytes 98312 | tf_op jit(solution)/shard_map/ppermute | solution.py:393
  13.1 6.6 %collective-permute-start.5 = (bf16[128,128]{1,0:T(8,128)(2,1)S(1)}, bf16[128,128]{1,0:T(8,128)(2,1)S(1)}, u32[]{:S(2)}, u32[]{:S(2)}) collective-permute-start(bf16[128,128]{1,0:T(8,128)(2,1)S(1)} %get-tuple-element.43.refs_3_.val_ref), channel_id=1, source_target_pairs={{0,16},{2,18},{4,20},{6,22},{8,24},{10,26},{12,28},{14,30},{16,0},... | collective-permute-start | bytes 98312 | tf_op jit(solution)/shard_map/ppermute | solution.py:393
  13.2 6.6 %collective-permute-start.6 = (bf16[128,128]{1,0:T(8,128)(2,1)S(1)}, bf16[128,128]{1,0:T(8,128)(2,1)S(1)}, u32[]{:S(2)}, u32[]{:S(2)}) collective-permute-start(bf16[128,128]{1,0:T(8,128)(2,1)S(1)} %get-tuple-element.43.refs_3_.val_ref), channel_id=1, source_target_pairs={{0,8},{2,10},{4,12},{6,14},{8,0},{10,2},{12,4},{14,6},{16,24},{18,... | collective-permute-start | bytes 98312 | tf_op jit(solution)/shard_map/ppermute | solution.py:393
  13.7 22.9 %copy-start = (bf16[1024,2048]{1,0:T(8,128)(2,1)S(1)}, bf16[1024,2048]{1,0:T(8,128)(2,1)}, u32[]{:S(2)}) copy-start(bf16[1024,2048]{1,0:T(8,128)(2,1)} %refs_12_.1) | copy-start | bytes 12582916
  14.2 12.5 %collective-permute-start.7 = (bf16[512,128]{1,0:T(8,128)(2,1)S(1)}, bf16[512,128]{1,0:T(8,128)(2,1)S(1)}, u32[]{:S(2)}, u32[]{:S(2)}) collective-permute-start(bf16[512,128]{1,0:T(8,128)(2,1)S(1)} %get-tuple-element.45.refs_3_), channel_id=1, source_target_pairs={{0,16},{2,18},{4,20},{6,22},{8,24},{10,26},{12,28},{14,30},{16,0},... | collective-permute-start | bytes 393224 | tf_op jit(solution)/shard_map/ppermute | solution.py:393
  16.7 10.1 %collective-permute-start.8 = (bf16[512,128]{1,0:T(8,128)(2,1)S(1)}, bf16[512,128]{1,0:T(8,128)(2,1)S(1)}, u32[]{:S(2)}, u32[]{:S(2)}) collective-permute-start(bf16[512,128]{1,0:T(8,128)(2,1)S(1)} %get-tuple-element.45.refs_3_), channel_id=1, source_target_pairs={{0,8},{2,10},{4,12},{6,14},{8,0},{10,2},{12,4},{14,6},{16,24},{18,... | collective-permute-start | bytes 393224 | tf_op jit(solution)/shard_map/ppermute | solution.py:393
  18.7 8.1 %collective-permute-start.9 = (bf16[512,128]{1,0:T(8,128)(2,1)S(1)}, bf16[512,128]{1,0:T(8,128)(2,1)S(1)}, u32[]{:S(2)}, u32[]{:S(2)}) collective-permute-start(bf16[512,128]{1,0:T(8,128)(2,1)S(1)} %get-tuple-element.45.refs_3_), channel_id=1, source_target_pairs={{0,24},{2,26},{4,28},{6,30},{8,16},{10,18},{12,20},{14,22},{16,8},... | collective-permute-start | bytes 393224 | tf_op jit(solution)/shard_map/ppermute | solution.py:393
  21.1 9.9 %collective-permute-start.13 = (bf16[512,128]{1,0:T(8,128)(2,1)S(1)}, bf16[512,128]{1,0:T(8,128)(2,1)S(1)}, u32[]{:S(2)}, u32[]{:S(2)}) collective-permute-start(bf16[512,128]{1,0:T(8,128)(2,1)S(1)} %get-tuple-element.54.refs_7_), channel_id=1, source_target_pairs={{0,6},{2,4},{4,2},{6,0},{8,14},{10,12},{12,10},{14,8},{16,22},{18,... | collective-permute-start | bytes 393224 | tf_op jit(solution)/shard_map/ppermute | solution.py:393
  23.6 12.3 %collective-permute-start.14 = (bf16[512,128]{1,0:T(8,128)(2,1)S(1)}, bf16[512,128]{1,0:T(8,128)(2,1)S(1)}, u32[]{:S(2)}, u32[]{:S(2)}) collective-permute-start(bf16[512,128]{1,0:T(8,128)(2,1)S(1)} %get-tuple-element.54.refs_7_), channel_id=1, source_target_pairs={{0,4},{2,6},{4,0},{6,2},{8,12},{10,14},{12,8},{14,10},{16,20},{18,... | collective-permute-start | bytes 393224 | tf_op jit(solution)/shard_map/ppermute | solution.py:393
  26.7 9.2 %collective-permute-start.15 = (bf16[512,128]{1,0:T(8,128)(2,1)S(1)}, bf16[512,128]{1,0:T(8,128)(2,1)S(1)}, u32[]{:S(2)}, u32[]{:S(2)}) collective-permute-start(bf16[512,128]{1,0:T(8,128)(2,1)S(1)} %get-tuple-element.54.refs_7_), channel_id=1, source_target_pairs={{0,2},{2,0},{4,6},{6,4},{8,10},{10,8},{12,14},{14,12},{16,18},{18,... | collective-permute-start | bytes 393224 | tf_op jit(solution)/shard_map/ppermute | solution.py:393
  27.5 8.5 %collective-permute-start.10 = (bf16[512,128]{1,0:T(8,128)(2,1)S(1)}, bf16[512,128]{1,0:T(8,128)(2,1)S(1)}, u32[]{:S(2)}, u32[]{:S(2)}) collective-permute-start(bf16[512,128]{1,0:T(8,128)(2,1)S(1)} %get-tuple-element.50), channel_id=1, source_target_pairs={{0,6},{2,4},{4,2},{6,0},{8,14},{10,12},{12,10},{14,8},{16,22},{18,... | collective-permute-start | bytes 393224 | tf_op jit(solution)/shard_map/ppermute | solution.py:393
  29.9 6.0 %collective-permute-start.11 = (bf16[512,128]{1,0:T(8,128)(2,1)S(1)}, bf16[512,128]{1,0:T(8,128)(2,1)S(1)}, u32[]{:S(2)}, u32[]{:S(2)}) collective-permute-start(bf16[512,128]{1,0:T(8,128)(2,1)S(1)} %get-tuple-element.51), channel_id=1, source_target_pairs={{0,4},{2,6},{4,0},{6,2},{8,12},{10,14},{12,8},{14,10},{16,20},{18,... | collective-permute-start | bytes 393224 | tf_op jit(solution)/shard_map/ppermute | solution.py:393
  31.0 5.6 %collective-permute-start.12 = (bf16[512,128]{1,0:T(8,128)(2,1)S(1)}, bf16[512,128]{1,0:T(8,128)(2,1)S(1)}, u32[]{:S(2)}, u32[]{:S(2)}) collective-permute-start(bf16[512,128]{1,0:T(8,128)(2,1)S(1)} %get-tuple-element.52), channel_id=1, source_target_pairs={{0,2},{2,0},{4,6},{6,4},{8,10},{10,8},{12,14},{14,12},{16,18},{18,... | collective-permute-start | bytes 393224 | tf_op jit(solution)/shard_map/ppermute | solution.py:393
  39.5 1.6 %collective-permute-start.16 = (bf16[64,2048]{1,0:T(8,128)(2,1)S(1)}, bf16[64,2048]{1,0:T(8,128)(2,1)S(1)}, u32[]{:S(2)}, u32[]{:S(2)}) collective-permute-start(bf16[64,2048]{1,0:T(8,128)(2,1)S(1)} %get-tuple-element.66), channel_id=1, source_target_pairs={{0,1},{1,0},{2,3},{3,2},{4,5},{5,4},{6,7},{7,6},{8,9},{9,8},{10,11... | collective-permute-start | bytes 786440 | tf_op jit(solution)/shard_map/ppermute | solution.py:516

commit v25 on v21

--- a/solution.py
+++ b/solution.py
@@ -338,7 +338,7 @@
     if turns == 1:
         bias = collect(0)
     stack = math.gcd(heads, 4)
-    wide = math.gcd(out_ref.shape[1], 4 * size)
+    wide = math.gcd(out_ref.shape[1], 8 * size)
     for first in range(0, heads, stack):
         some = slice(first, first + stack)
         moved = moved_ref[some].reshape(stack * tokens, size)

time: 42 us -> 42 us (level)
  no operation moved by 1% of the time
where the time goes in v25:
time: 42 us; the launch traced here: 41.8 us
  starting transfers between devices  21.2 us (50%)
  Pallas kernels  13.2 us (31%)
  waiting for transfers between devices  5.23 us (12%)
  between operations  0.78 us (2%)
  other arithmetic  0.77 us (2%)
  local copies, waits for them, and re-layouts  0.66 us (2%)
    ppermute x15, starting transfers between devices, swapped(): out[step] = lax.ppermute(values[step], 'ctx', pairs_of(step))  20.7 us
    pallas_call x7, Pallas kernels, call(): pl.pallas_call(kernel, out_shape=out_shape, in_specs=in_specs or [vmem] *...  13.2 us
    ppermute x15, waiting for transfers between devices, swapped(): out[step] = lax.ppermute(values[step], 'ctx', pairs_of(step))  3.71 us
    ppermute x1, waiting for transfers between devices, body(): return kept + lax.ppermute(away, 'head', [(0, 1), (1, 0)])  1.52 us
  transfers between devices with their start and end apart: 17, of which 4 were waited for; matrix products, arithmetic and copies ran while one was open for 0% of the time, Pallas kernels for 19%

profile of v25, /device:TPU:0, one launch (start us, length us, event | category | flops | bytes accessed | tf_op | source)
XLA Modules:
  0.0 41.8 jit_solution(14356676185551691830)
XLA Ops:
  0.0 0.5 %collective-permute-start = (bf16[64,2048]{1,0:T(8,128)(2,1)}, bf16[64,2048]{1,0:T(8,128)(2,1)S(1)}, u32[]{:S(2)}, u32[]{:S(2)}) collective-permute-start(bf16[64,2048]{1,0:T(8,128)(2,1)} %mine_hbm.1), channel_id=1, source_target_pairs={{0,1},{1,0},{2,3},{3,2},{4,5},{5,4},{6,7},{7,6},{8,9},{9,8},{10,11... | collective-permute-start | bytes 786440 | tf_op jit(solution)/shard_map/ppermute | solution.py:383
  1.1 1.4 %shard_map.109 = (bf16[2048,256]{1,0:T(8,128)(2,1)S(1)}, bf16[1,2048]{1,0:T(2,128)(2,1)S(1)}, f32[1,128]{1,0:T(1,128)S(1)}, f32[1,128]{1,0:T(1,128)S(1)}, bf16[64,2048]{1,0:T(8,128)(2,1)S(1)}) custom-call(bf16[2048,128]{1,0:T(8,128)(2,1)} %key_hbm.1, bf16[2048,128]{1,0:T(8,128)(2,1)} %dir_hbm.1, bf16[1,2048]{1,0:T(2,128)(2,1)} %rate_hbm.1, ...), custom_call_target="tpu_custom_call" | custom-call | bytes 3145728 | tf_op jit(solution)/shard_map/pallas_call | solution.py:21
  2.5 2.4 %shard_map.110 = (bf16[128,2048]{1,0:T(8,128)(2,1)S(1)}, f32[128,128]{1,0:T(8,128)S(1)}, bf16[128,128]{1,0:T(8,128)(2,1)S(1)}, f32[128,128]{1,0:T(8,128)S(1)}, f...) custom-call(s32[1]{0:T(128)} %bitcast.1.core_ref, ...), custom_call_target="tpu_custom_call" | custom-call | flops 201326592 | bytes 2097152 | tf_op jit(solution)/shard_map/pallas_call | solution.py:21
  4.9 3.5 %collective-permute-start.1 = (f32[128,128]{1,0:T(8,128)S(1)}, f32[128,128]{1,0:T(8,128)S(1)}, u32[]{:S(2)}, u32[]{:S(2)}) collective-permute-start(f32[128,128]{1,0:T(8,128)S(1)} %get-tuple-element.41.refs_3_), channel_id=1, source_target_pairs={{0,6},{2,4},{4,2},{6,0},{8,14},{10,12},{12,10},{14,8},{16,22},{18,... | collective-permute-start | bytes 196616 | tf_op jit(solution)/shard_map/ppermute | solution.py:397
  8.4 0.5 %collective-permute-start.2 = (f32[128,128]{1,0:T(8,128)S(1)}, f32[128,128]{1,0:T(8,128)S(1)}, u32[]{:S(2)}, u32[]{:S(2)}) collective-permute-start(f32[128,128]{1,0:T(8,128)S(1)} %get-tuple-element.41.refs_3_), channel_id=1, source_target_pairs={{0,4},{2,6},{4,0},{6,2},{8,12},{10,14},{12,8},{14,10},{16,20},{18,... | collective-permute-start | bytes 196616 | tf_op jit(solution)/shard_map/ppermute | solution.py:397
  9.1 4.0 %collective-permute-start.4 = (bf16[128,128]{1,0:T(8,128)(2,1)S(1)}, bf16[128,128]{1,0:T(8,128)(2,1)S(1)}, u32[]{:S(2)}, u32[]{:S(2)}) collective-permute-start(bf16[128,128]{1,0:T(8,128)(2,1)S(1)} %get-tuple-element.43.refs_3_.val_ref), channel_id=1, source_target_pairs={{0,24},{2,26},{4,28},{6,30},{8,16},{10,18},{12,20},{14,22},{16,8},... | collective-permute-start | bytes 98312 | tf_op jit(solution)/shard_map/ppermute | solution.py:397
  13.1 0.6 %collective-permute-start.6 = (bf16[128,128]{1,0:T(8,128)(2,1)S(1)}, bf16[128,128]{1,0:T(8,128)(2,1)S(1)}, u32[]{:S(2)}, u32[]{:S(2)}) collective-permute-start(bf16[128,128]{1,0:T(8,128)(2,1)S(1)} %get-tuple-element.43.refs_3_.val_ref), channel_id=1, source_target_pairs={{0,8},{2,10},{4,12},{6,14},{8,0},{10,2},{12,4},{14,6},{16,24},{18,... | collective-permute-start | bytes 98312 | tf_op jit(solution)/shard_map/ppermute | solution.py:397
  13.7 0.5 %shard_map.111 = (bf16[512,128]{1,0:T(8,128)(2,1)S(1)}, f32[4,128,128]{2,1,0:T(8,128)S(1)}, bf16[128,128]{1,0:T(8,128)(2,1)S(1)}, bf16[128,128]{1,0:T(8,128)(2,1...) custom-call(s32[1]{0:T(128)} %bitcast.place_ref, f32[128,128]{1,0:T(8,128)S(1)} %get-tuple-element.40.exit_ref, ...), custom_call_target="tpu_custom_call" | custom-call | flops 100663296 | bytes 1000000 | tf_op jit(solution)/shard_map/pallas_call | solution.py:21
  14.2 2.4 %collective-permute-start.7 = (bf16[512,128]{1,0:T(8,128)(2,1)S(1)}, bf16[512,128]{1,0:T(8,128)(2,1)S(1)}, u32[]{:S(2)}, u32[]{:S(2)}) collective-permute-start(bf16[512,128]{1,0:T(8,128)(2,1)S(1)} %get-tuple-element.45.refs_3_), channel_id=1, source_target_pairs={{0,16},{2,18},{4,20},{6,22},{8,24},{10,26},{12,28},{14,30},{16,0},... | collective-permute-start | bytes 393224 | tf_op jit(solution)/shard_map/ppermute | solution.py:397
  16.6 2.0 %collective-permute-start.8 = (bf16[512,128]{1,0:T(8,128)(2,1)S(1)}, bf16[512,128]{1,0:T(8,128)(2,1)S(1)}, u32[]{:S(2)}, u32[]{:S(2)}) collective-permute-start(bf16[512,128]{1,0:T(8,128)(2,1)S(1)} %get-tuple-element.45.refs_3_), channel_id=1, source_target_pairs={{0,8},{2,10},{4,12},{6,14},{8,0},{10,2},{12,4},{14,6},{16,24},{18,... | collective-permute-start | bytes 393224 | tf_op jit(solution)/shard_map/ppermute | solution.py:397
  18.8 0.9 %collective-permute-done.5.refs_1_ = bf16[128,128]{1,0:T(8,128)(2,1)S(1)} collective-permute-done((bf16[128,128]{1,0:T(8,128)(2,1)S(1)}, bf16[128,128]{1,0:T(8,128)(2,1)S(1)}, u32[]{:S(2)}, u32[]{:S(2)}) %collective-permute-start.5) | collective-permute-done | bytes 32800 | tf_op jit(solution)/shard_map/ppermute | solution.py:397
  19.7 0.7 %copy-done.1 = s32[1,16]{1,0:T(1,128)S(1)} copy-done((s32[1,16]{1,0:T(1,128)S(1)}, s32[1,16]{1,0:T(1,128)}, u32[]{:S(2)}) %copy-start.1) | copy-done | bytes 88
  20.4 1.3 %shard_map.112 = (bf16[512,128]{1,0:T(8,128)(2,1)S(1)}, s32[1]{0:T(128)}) custom-call(s32[1]{0:T(128)} %bitcast.place_ref, s32[16]{0:T(128)S(1)} %bitcast.5, f32[4,128,128]{2,1,0:T(8,128)S(1)} %get-tuple-element.42.after_ref.refs_4_, bf16[128,128]{1,0:T(8,128)(2,1)S(1)} %collective-permute-done.4.refs_0_, ...), custom_call_target="tpu_custom_call" | custom-call | bytes 1000000 | tf_op jit(solution)/shard_map/pallas_call | solution.py:21
  21.7 2.5 %collective-permute-start.13 = (bf16[512,128]{1,0:T(8,128)(2,1)S(1)}, bf16[512,128]{1,0:T(8,128)(2,1)S(1)}, u32[]{:S(2)}, u32[]{:S(2)}) collective-permute-start(bf16[512,128]{1,0:T(8,128)(2,1)S(1)} %get-tuple-element.54.refs_7_), channel_id=1, source_target_pairs={{0,6},{2,4},{4,2},{6,0},{8,14},{10,12},{12,10},{14,8},{16,22},{18,... | collective-permute-start | bytes 393224 | tf_op jit(solution)/shard_map/ppermute | solution.py:397
  24.5 2.1 %collective-permute-done.7.refs_0_ = bf16[512,128]{1,0:T(8,128)(2,1)S(1)} collective-permute-done((bf16[512,128]{1,0:T(8,128)(2,1)S(1)}, bf16[512,128]{1,0:T(8,128)(2,1)S(1)}, u32[]{:S(2)}, u32[]{:S(2)}) %collective-permute-start.7) | collective-permute-done | bytes 131104 | tf_op jit(solution)/shard_map/ppermute | solution.py:397
  26.6 0.7 %shard_map.113 = (bf16[512,128]{1,0:T(8,128)(2,1)S(1)}, bf16[512,128]{1,0:T(8,128)(2,1)S(1)}, bf16[512,128]{1,0:T(8,128)(2,1)S(1)}, bf16[512,128]{1,0:T(8,128)(2,1)S(1)}) custom-call(s32[1]{0:T(128)} %bitcast.place_ref, bf16[512,128]{1,0:T(8,128)(2,1)S(1)} %collective-permute-done.7.refs_0_, bf16[512,128]{1,0:T(8,128)(2,1)S(1)} %collective-permute-done.8.refs_1_, ...), custom_call_target="tpu_custom_call" | custom-call | flops 201326592 | bytes 1000000 | tf_op jit(solution)/shard_map/pallas_call | solution.py:21
  27.4 2.5 %collective-permute-start.10 = (bf16[512,128]{1,0:T(8,128)(2,1)S(1)}, bf16[512,128]{1,0:T(8,128)(2,1)S(1)}, u32[]{:S(2)}, u32[]{:S(2)}) collective-permute-start(bf16[512,128]{1,0:T(8,128)(2,1)S(1)} %get-tuple-element.50), channel_id=1, source_target_pairs={{0,6},{2,4},{4,2},{6,0},{8,14},{10,12},{12,10},{14,8},{16,22},{18,... | collective-permute-start | bytes 393224 | tf_op jit(solution)/shard_map/ppermute | solution.py:397
  29.9 1.0 %collective-permute-start.11 = (bf16[512,128]{1,0:T(8,128)(2,1)S(1)}, bf16[512,128]{1,0:T(8,128)(2,1)S(1)}, u32[]{:S(2)}, u32[]{:S(2)}) collective-permute-start(bf16[512,128]{1,0:T(8,128)(2,1)S(1)} %get-tuple-element.51), channel_id=1, source_target_pairs={{0,4},{2,6},{4,0},{6,2},{8,12},{10,14},{12,8},{14,10},{16,20},{18,... | collective-permute-start | bytes 393224 | tf_op jit(solution)/shard_map/ppermute | solution.py:397
  30.9 1.0 %collective-permute-start.12 = (bf16[512,128]{1,0:T(8,128)(2,1)S(1)}, bf16[512,128]{1,0:T(8,128)(2,1)S(1)}, u32[]{:S(2)}, u32[]{:S(2)}) collective-permute-start(bf16[512,128]{1,0:T(8,128)(2,1)S(1)} %get-tuple-element.52), channel_id=1, source_target_pairs={{0,2},{2,0},{4,6},{6,4},{8,10},{10,8},{12,14},{14,12},{16,18},{18,... | collective-permute-start | bytes 393224 | tf_op jit(solution)/shard_map/ppermute | solution.py:397
  31.9 3.9 %shard_map.114 = (bf16[8,128,128]{2,1,0:T(8,128)(2,1)S(1)}, f32[8,128,128]{2,1,0:T(8,128)S(1)}, f32[8,128,1]{2,1,0:T(8,128)S(1)}, f32[8,128,1]{2,1,0:T(8,128)S(1)}) custom-call(bf16[128,2048]{1,0:T(8,128)(2,1)S(1)} %get-tuple-element.55.rows_ref, bf16[2048,1024]{1,0:T(8,128)(2,1)} %weight_hbm.1, f32[1,128]{1,0:T(1,128)S(1)} %get-tuple-element.56.gain_ref, ...), custom_call_target="tpu_custom_call" | custom-call | flops 1073741824 | bytes 16777216 | tf_op jit(solution)/shard_map/pallas_call | solution.py:21
  35.9 0.7 %collective-permute-done.12.refs_2_ = bf16[512,128]{1,0:T(8,128)(2,1)S(1)} collective-permute-done((bf16[512,128]{1,0:T(8,128)(2,1)S(1)}, bf16[512,128]{1,0:T(8,128)(2,1)S(1)}, u32[]{:S(2)}, u32[]{:S(2)}) %collective-permute-start.12) | collective-permute-done | bytes 131104 | tf_op jit(solution)/shard_map/ppermute | solution.py:397
  36.6 2.9 %shard_map.115 = (bf16[64,2048]{1,0:T(8,128)(2,1)S(1)}, bf16[64,2048]{1,0:T(8,128)(2,1)S(1)}) custom-call(s32[1]{0:T(128)} %bitcast.place_ref, s32[1]{0:T(128)} %bitcast.1.core_ref, s32[1]{0:T(128)} %get-tuple-element.44.table_ref, bf16[512,128]{1,0:T(8,128)(2,1)S(1)} %collective-permute-done.10.refs_0_, ...), custom_call_target="tpu_custom_call" | custom-call | flops 536870912 | bytes 4000000 | tf_op jit(solution)/shard_map/pallas_call | solution.py:21
  39.5 1.5 %collective-permute-done.16 = bf16[64,2048]{1,0:T(8,128)(2,1)S(1)} collective-permute-done((bf16[64,2048]{1,0:T(8,128)(2,1)S(1)}, bf16[64,2048]{1,0:T(8,128)(2,1)S(1)}, u32[]{:S(2)}, u32[]{:S(2)}) %collective-permute-start.16) | collective-permute-done | bytes 262176 | tf_op jit(solution)/shard_map/ppermute | solution.py:521
  41.1 0.8 %add.3 = bf16[64,2048]{1,0:T(8,128)(2,1)} add(bf16[64,2048]{1,0:T(8,128)(2,1)S(1)} %get-tuple-element.65, bf16[64,2048]{1,0:T(8,128)(2,1)S(1)} %collective-permute-done.16) | non-fusion elementwise | flops 131072 | bytes 786432 | tf_op jit(solution)/shard_map/add | solution.py:521
  (22 shorter events, 0.7 us)
Async XLA Ops:
  0.0 2.5 %collective-permute-start = (bf16[64,2048]{1,0:T(8,128)(2,1)}, bf16[64,2048]{1,0:T(8,128)(2,1)S(1)}, u32[]{:S(2)}, u32[]{:S(2)}) collective-permute-start(bf16[64,2048]{1,0:T(8,128)(2,1)} %mine_hbm.1), channel_id=1, source_target_pairs={{0,1},{1,0},{2,3},{3,2},{4,5},{5,4},{6,7},{7,6},{8,9},{9,8},{10,11... | collective-permute-start | bytes 786440 | tf_op jit(solution)/shard_map/ppermute | solution.py:383
  4.9 8.2 %collective-permute-start.1 = (f32[128,128]{1,0:T(8,128)S(1)}, f32[128,128]{1,0:T(8,128)S(1)}, u32[]{:S(2)}, u32[]{:S(2)}) collective-permute-start(f32[128,128]{1,0:T(8,128)S(1)} %get-tuple-element.41.refs_3_), channel_id=1, source_target_pairs={{0,6},{2,4},{4,2},{6,0},{8,14},{10,12},{12,10},{14,8},{16,22},{18,... | collective-permute-start | bytes 196616 | tf_op jit(solution)/shard_map/ppermute | solution.py:397
  8.4 5.2 %collective-permute-start.2 = (f32[128,128]{1,0:T(8,128)S(1)}, f32[128,128]{1,0:T(8,128)S(1)}, u32[]{:S(2)}, u32[]{:S(2)}) collective-permute-start(f32[128,128]{1,0:T(8,128)S(1)} %get-tuple-element.41.refs_3_), channel_id=1, source_target_pairs={{0,4},{2,6},{4,0},{6,2},{8,12},{10,14},{12,8},{14,10},{16,20},{18,... | collective-permute-start | bytes 196616 | tf_op jit(solution)/shard_map/ppermute | solution.py:397
  8.9 4.7 %collective-permute-start.3 = (f32[128,128]{1,0:T(8,128)S(1)}, f32[128,128]{1,0:T(8,128)S(1)}, u32[]{:S(2)}, u32[]{:S(2)}) collective-permute-start(f32[128,128]{1,0:T(8,128)S(1)} %get-tuple-element.41.refs_3_), channel_id=1, source_target_pairs={{0,2},{2,0},{4,6},{6,4},{8,10},{10,8},{12,14},{14,12},{16,18},{18,... | collective-permute-start | bytes 196616 | tf_op jit(solution)/shard_map/ppermute | solution.py:397
  9.1 9.6 %collective-permute-start.4 = (bf16[128,128]{1,0:T(8,128)(2,1)S(1)}, bf16[128,128]{1,0:T(8,128)(2,1)S(1)}, u32[]{:S(2)}, u32[]{:S(2)}) collective-permute-start(bf16[128,128]{1,0:T(8,128)(2,1)S(1)} %get-tuple-element.43.refs_3_.val_ref), channel_id=1, source_target_pairs={{0,24},{2,26},{4,28},{6,30},{8,16},{10,18},{12,20},{14,22},{16,8},... | collective-permute-start | bytes 98312 | tf_op jit(solution)/shard_map/ppermute | solution.py:397
  13.1 6.6 %collective-permute-start.5 = (bf16[128,128]{1,0:T(8,128)(2,1)S(1)}, bf16[128,128]{1,0:T(8,128)(2,1)S(1)}, u32[]{:S(2)}, u32[]{:S(2)}) collective-permute-start(bf16[128,128]{1,0:T(8,128)(2,1)S(1)} %get-tuple-element.43.refs_3_.val_ref), channel_id=1, source_target_pairs={{0,16},{2,18},{4,20},{6,22},{8,24},{10,26},{12,28},{14,30},{16,0},... | collective-permute-start | bytes 98312 | tf_op jit(solution)/shard_map/ppermute | solution.py:397
  13.1 6.6 %collective-permute-start.6 = (bf16[128,128]{1,0:T(8,128)(2,1)S(1)}, bf16[128,128]{1,0:T(8,128)(2,1)S(1)}, u32[]{:S(2)}, u32[]{:S(2)}) collective-permute-start(bf16[128,128]{1,0:T(8,128)(2,1)S(1)} %get-tuple-element.43.refs_3_.val_ref), channel_id=1, source_target_pairs={{0,8},{2,10},{4,12},{6,14},{8,0},{10,2},{12,4},{14,6},{16,24},{18,... | collective-permute-start | bytes 98312 | tf_op jit(solution)/shard_map/ppermute | solution.py:397
  13.7 22.9 %copy-start = (bf16[1024,2048]{1,0:T(8,128)(2,1)S(1)}, bf16[1024,2048]{1,0:T(8,128)(2,1)}, u32[]{:S(2)}) copy-start(bf16[1024,2048]{1,0:T(8,128)(2,1)} %refs_12_.1) | copy-start | bytes 12582916
  14.2 12.4 %collective-permute-start.7 = (bf16[512,128]{1,0:T(8,128)(2,1)S(1)}, bf16[512,128]{1,0:T(8,128)(2,1)S(1)}, u32[]{:S(2)}, u32[]{:S(2)}) collective-permute-start(bf16[512,128]{1,0:T(8,128)(2,1)S(1)} %get-tuple-element.45.refs_3_), channel_id=1, source_target_pairs={{0,16},{2,18},{4,20},{6,22},{8,24},{10,26},{12,28},{14,30},{16,0},... | collective-permute-start | bytes 393224 | tf_op jit(solution)/shard_map/ppermute | solution.py:397
  16.6 10.0 %collective-permute-start.8 = (bf16[512,128]{1,0:T(8,128)(2,1)S(1)}, bf16[512,128]{1,0:T(8,128)(2,1)S(1)}, u32[]{:S(2)}, u32[]{:S(2)}) collective-permute-start(bf16[512,128]{1,0:T(8,128)(2,1)S(1)} %get-tuple-element.45.refs_3_), channel_id=1, source_target_pairs={{0,8},{2,10},{4,12},{6,14},{8,0},{10,2},{12,4},{14,6},{16,24},{18,... | collective-permute-start | bytes 393224 | tf_op jit(solution)/shard_map/ppermute | solution.py:397
  18.6 8.0 %collective-permute-start.9 = (bf16[512,128]{1,0:T(8,128)(2,1)S(1)}, bf16[512,128]{1,0:T(8,128)(2,1)S(1)}, u32[]{:S(2)}, u32[]{:S(2)}) collective-permute-start(bf16[512,128]{1,0:T(8,128)(2,1)S(1)} %get-tuple-element.45.refs_3_), channel_id=1, source_target_pairs={{0,24},{2,26},{4,28},{6,30},{8,16},{10,18},{12,20},{14,22},{16,8},... | collective-permute-start | bytes 393224 | tf_op jit(solution)/shard_map/ppermute | solution.py:397
  19.7 0.7 %copy-start.1 = (s32[1,16]{1,0:T(1,128)S(1)}, s32[1,16]{1,0:T(1,128)}, u32[]{:S(2)}) copy-start(s32[1,16]{1,0:T(1,128)} %param.21) | copy-start | bytes 196
  21.7 9.2 %collective-permute-start.13 = (bf16[512,128]{1,0:T(8,128)(2,1)S(1)}, bf16[512,128]{1,0:T(8,128)(2,1)S(1)}, u32[]{:S(2)}, u32[]{:S(2)}) collective-permute-start(bf16[512,128]{1,0:T(8,128)(2,1)S(1)} %get-tuple-element.54.refs_7_), channel_id=1, source_target_pairs={{0,6},{2,4},{4,2},{6,0},{8,14},{10,12},{12,10},{14,8},{16,22},{18,... | collective-permute-start | bytes 393224 | tf_op jit(solution)/shard_map/ppermute | solution.py:397
  24.2 11.6 %collective-permute-start.14 = (bf16[512,128]{1,0:T(8,128)(2,1)S(1)}, bf16[512,128]{1,0:T(8,128)(2,1)S(1)}, u32[]{:S(2)}, u32[]{:S(2)}) collective-permute-start(bf16[512,128]{1,0:T(8,128)(2,1)S(1)} %get-tuple-element.54.refs_7_), channel_id=1, source_target_pairs={{0,4},{2,6},{4,0},{6,2},{8,12},{10,14},{12,8},{14,10},{16,20},{18,... | collective-permute-start | bytes 393224 | tf_op jit(solution)/shard_map/ppermute | solution.py:397
  26.6 9.2 %collective-permute-start.15 = (bf16[512,128]{1,0:T(8,128)(2,1)S(1)}, bf16[512,128]{1,0:T(8,128)(2,1)S(1)}, u32[]{:S(2)}, u32[]{:S(2)}) collective-permute-start(bf16[512,128]{1,0:T(8,128)(2,1)S(1)} %get-tuple-element.54.refs_7_), channel_id=1, source_target_pairs={{0,2},{2,0},{4,6},{6,4},{8,10},{10,8},{12,14},{14,12},{16,18},{18,... | collective-permute-start | bytes 393224 | tf_op jit(solution)/shard_map/ppermute | solution.py:397
  27.4 8.5 %collective-permute-start.10 = (bf16[512,128]{1,0:T(8,128)(2,1)S(1)}, bf16[512,128]{1,0:T(8,128)(2,1)S(1)}, u32[]{:S(2)}, u32[]{:S(2)}) collective-permute-start(bf16[512,128]{1,0:T(8,128)(2,1)S(1)} %get-tuple-element.50), channel_id=1, source_target_pairs={{0,6},{2,4},{4,2},{6,0},{8,14},{10,12},{12,10},{14,8},{16,22},{18,... | collective-permute-start | bytes 393224 | tf_op jit(solution)/shard_map/ppermute | solution.py:397
  29.9 6.0 %collective-permute-start.11 = (bf16[512,128]{1,0:T(8,128)(2,1)S(1)}, bf16[512,128]{1,0:T(8,128)(2,1)S(1)}, u32[]{:S(2)}, u32[]{:S(2)}) collective-permute-start(bf16[512,128]{1,0:T(8,128)(2,1)S(1)} %get-tuple-element.51), channel_id=1, source_target_pairs={{0,4},{2,6},{4,0},{6,2},{8,12},{10,14},{12,8},{14,10},{16,20},{18,... | collective-permute-start | bytes 393224 | tf_op jit(solution)/shard_map/ppermute | solution.py:397
  30.9 5.7 %collective-permute-start.12 = (bf16[512,128]{1,0:T(8,128)(2,1)S(1)}, bf16[512,128]{1,0:T(8,128)(2,1)S(1)}, u32[]{:S(2)}, u32[]{:S(2)}) collective-permute-start(bf16[512,128]{1,0:T(8,128)(2,1)S(1)} %get-tuple-element.52), channel_id=1, source_target_pairs={{0,2},{2,0},{4,6},{6,4},{8,10},{10,8},{12,14},{14,12},{16,18},{18,... | collective-permute-start | bytes 393224 | tf_op jit(solution)/shard_map/ppermute | solution.py:397
  39.5 1.6 %collective-permute-start.16 = (bf16[64,2048]{1,0:T(8,128)(2,1)S(1)}, bf16[64,2048]{1,0:T(8,128)(2,1)S(1)}, u32[]{:S(2)}, u32[]{:S(2)}) collective-permute-start(bf16[64,2048]{1,0:T(8,128)(2,1)S(1)} %get-tuple-element.66), channel_id=1, source_target_pairs={{0,1},{1,0},{2,3},{3,2},{4,5},{5,4},{6,7},{7,6},{8,9},{9,8},{10,11... | collective-permute-start | bytes 786440 | tf_op jit(solution)/shard_map/ppermute | solution.py:521
